TPU v7x, 128 devices: a whole 4x4x4 slice. The times are simulated.
128 devices in a mesh: wide: 16 (over y, x_lo, core), narrow: 8 (over z, x_hi).
Axes of the slice: x: 4 (x_hi: 2, x_lo: 2; x = x_hi * 2 + x_lo), y: 4, z: 4, core: 2. Of those that a mesh axis runs over, the one named last changes fastest.
Arguments:
- tokens: bfloat16 [2, 2048, 768], P(None, 'wide'), may hold values from -6 to 6
- scene_of_block: int32 [2, 32], replicated, may hold values from 0 to 3, as said below
- ln1_gain: float32 [768], replicated, may hold values from 0.1 to 1.9
- ln1_shift: float32 [768], replicated, may hold values from -3 to 3
- w_qkv: bfloat16 [768, 2304], replicated, may hold values from -0.21875 to 0.21875
- w_out: bfloat16 [768, 768], replicated, may hold values from -6 to 6
- ln2_gain: float32 [768], replicated, may hold values from 0.1 to 1.9
- ln2_shift: float32 [768], replicated, may hold values from -3 to 3
- w_up: bfloat16 [768, 3072], P(None, 'narrow'), may hold values from -0.21875 to 0.21875
- w_down: bfloat16 [3072, 768], P('narrow'), may hold values from -0.109375 to 0.109375
- out_grad: bfloat16 [2, 2048, 768], P(None, 'wide'), may hold values from -6 to 6
Outputs:
- result: bfloat16 [2, 2048, 768], P(None, 'wide')
- input_grad: float32 [2, 2048, 768], P(None, 'wide')
- qkv_grad: float32 [768, 2304], replicated
- out_proj_grad: float32 [768, 768], replicated
- ln1_gain_grad: float32 [768], replicated
- ln1_shift_grad: float32 [768], replicated
- ln2_gain_grad: float32 [768], replicated
- ln2_shift_grad: float32 [768], replicated
- up_grad: float32 [768, 3072], P(None, 'narrow')
- down_grad: float32 [3072, 768], P('narrow')
Inputs may be any that keep to these rules, and one draw needn't show every extreme that they name: `scene_of_block`: in each micro-batch the scene ids never fall along the blocks, so each scene is one contiguous span of blocks. One scene, drawn from the seed, holds 32 - 3 * (4) blocks; each of the others holds 4 blocks.
All inputs are finite; a program needn't handle non-finite values.
Results may differ from a plain program's by a relative error of at most 0.023.
Values may be sent and summed in bfloat16 or wider, within the bound.
No kernel may reach another device: no remote copies, remote signals or barrier semaphores. Data moves between devices by JAX's collectives and lax.ppermute only.
A program may use at most 128 MiB of HBM per device.

v0:
```python
from functools import partial

import jax
import jax.numpy as jnp
from jax import lax
from jax.sharding import PartitionSpec as P

HEADS = 12
HD = 64
SCENE_BLOCK = 64


EPS = 1e-05
NEGATIVE = -1e30


def from_everyone(value, axis):
    length = lax.axis_size(axis)
    return lax.all_to_all(
        jnp.broadcast_to(value[None], (length, *value.shape)), axis, 0, 0, tiled=True
    )


def of_everyone(value, axis):
    return from_everyone(value, axis).astype(jnp.float32).sum(axis=0)


def shortened(value):

    def short(part):
        return part.astype(jnp.bfloat16) if part.dtype == jnp.float32 else part

    return jax.tree.map(short, value)


def layer_norm(values, gain, shift):
    center = values - jnp.mean(values, axis=-1, keepdims=True)
    spread = jnp.mean(center * center, axis=-1, keepdims=True)
    return center * lax.rsqrt(spread + EPS) * gain + shift


def contract_rows(left, right):
    return lax.dot_general(
        left, right, (((0,), (0,)), ((), ())), preferred_element_type=jnp.float32
    )


def contract_cols(left, right):
    return lax.dot_general(
        left, right, (((1,), (1,)), ((), ())), preferred_element_type=jnp.float32
    )


def split_heads(matrix):
    return matrix.reshape(matrix.shape[0], HEADS, HD)


def key_piece(kv_all, block_scene, index, rows, width):
    piece = lax.dynamic_slice_in_dim(kv_all, index * rows, rows, 0)
    scenes = lax.dynamic_slice_in_dim(block_scene, index * rows, rows, 0)
    return (split_heads(piece[:, :width]), split_heads(piece[:, width:]), scenes)


def scene_range(own_scene, block_scene, rows):
    lower = jnp.sum((block_scene < own_scene[0]).astype(jnp.int32))
    upper = jnp.sum((block_scene <= own_scene[-1]).astype(jnp.int32))
    return (lower // rows, (upper + rows - 1) // rows)


def attend(query, kv_all, own_scene, block_scene, first, last):
    rows, width = query.shape
    scale = HD ** (-0.5)
    q_heads = split_heads(query)

    def scores_of(index):
        keys, values, scenes = key_piece(kv_all, block_scene, index, rows, width)
        same = (own_scene[:, None] == scenes[None, :])[None]
        scores = (
            jnp.einsum("qhd,khd->hqk", q_heads, keys, preferred_element_type=jnp.float32) * scale
        )
        return (jnp.where(same, scores, NEGATIVE), same, values)

    def stats_step(index, carry):
        top, total = carry
        scores, same, unused = scores_of(index)
        new_top = jnp.maximum(top, jnp.max(scores, axis=-1))
        weights = jnp.where(same, jnp.exp(scores - new_top[:, :, None]), 0.0)
        total = total * jnp.exp(top - new_top) + jnp.sum(weights, axis=-1)
        return (new_top, total)

    start_stats = (
        jnp.full((HEADS, rows), NEGATIVE, jnp.float32),
        jnp.zeros((HEADS, rows), jnp.float32),
    )
    top, total = lax.fori_loop(first, last, stats_step, start_stats)

    def output_step(index, mixed):
        scores, same, values = scores_of(index)
        probs = jnp.where(same, jnp.exp(scores - top[:, :, None]) / total[:, :, None], 0.0).astype(
            jnp.bfloat16
        )
        return mixed + jnp.einsum("hqk,khd->qhd", probs, values, preferred_element_type=jnp.float32)

    mixed = lax.fori_loop(first, last, output_step, jnp.zeros((rows, HEADS, HD), jnp.float32))
    return (mixed.reshape(rows, width), top, total)


def attend_back(query, kv_all, own_scene, block_scene, top, total, grad_mixed, first, last):
    rows, width = query.shape
    scale = HD ** (-0.5)
    q_heads = split_heads(query)
    g_heads = split_heads(grad_mixed)

    def parts_of(index):
        keys, values, scenes = key_piece(kv_all, block_scene, index, rows, width)
        same = (own_scene[:, None] == scenes[None, :])[None]
        scores = (
            jnp.einsum("qhd,khd->hqk", q_heads, keys, preferred_element_type=jnp.float32) * scale
        )
        probs = jnp.where(same, jnp.exp(scores - top[:, :, None]) / total[:, :, None], 0.0)
        grad_probs = jnp.einsum("qhd,khd->hqk", g_heads, values, preferred_element_type=jnp.float32)
        return (probs, grad_probs, keys)

    def delta_step(index, delta):
        probs, grad_probs, unused = parts_of(index)
        return delta + jnp.sum(probs * grad_probs, axis=-1)

    delta = lax.fori_loop(first, last, delta_step, jnp.zeros((HEADS, rows), jnp.float32))

    def grads_of(index):
        probs, grad_probs, keys = parts_of(index)
        grad_scores = (probs * (grad_probs - delta[:, :, None])).astype(jnp.bfloat16)
        grad_q = (
            jnp.einsum("hqk,khd->qhd", grad_scores, keys, preferred_element_type=jnp.float32)
            * scale
        )
        return (probs, grad_scores, grad_q)

    grad_start = jnp.zeros((rows, HEADS, HD), jnp.float32)

    def full_step(index, carry):
        grad_query, terms = carry
        probs, grad_scores, grad_q = grads_of(index)
        grad_k = (
            jnp.einsum("hqk,qhd->khd", grad_scores, q_heads, preferred_element_type=jnp.float32)
            * scale
        )
        grad_v = jnp.einsum(
            "hqk,qhd->khd", probs.astype(jnp.bfloat16), g_heads, preferred_element_type=jnp.float32
        )
        block = jnp.concatenate([grad_k.reshape(rows, width), grad_v.reshape(rows, width)], axis=1)
        terms = lax.dynamic_update_slice_in_dim(terms, block, index * rows, 0)
        return (grad_query + grad_q, terms)

    terms_start = jnp.zeros((kv_all.shape[0], 2 * width), jnp.float32)
    grad_query, terms = lax.fori_loop(first, last, full_step, (grad_start, terms_start))
    return (grad_query.reshape(rows, width), delta, terms)


def shards(
    tokens,
    scene_of_block,
    ln1_gain,
    ln1_shift,
    w_qkv,
    w_out,
    ln2_gain,
    ln2_shift,
    w_up,
    w_down,
    out_grad,
):
    rows = tokens.shape[1]
    width = tokens.shape[2]
    offset = lax.axis_index("wide") * rows
    totals = (
        jnp.zeros(w_qkv.shape, jnp.float32),
        jnp.zeros(w_out.shape, jnp.float32),
        jnp.zeros(w_up.shape, jnp.float32),
        jnp.zeros(w_down.shape, jnp.float32),
        jnp.zeros((width,), jnp.float32),
        jnp.zeros((width,), jnp.float32),
        jnp.zeros((width,), jnp.float32),
        jnp.zeros((width,), jnp.float32),
    )
    results = []
    input_grads = []
    for micro in range(tokens.shape[0]):
        block_scene = jnp.repeat(scene_of_block[micro], SCENE_BLOCK)
        own_scene = lax.dynamic_slice_in_dim(block_scene, offset, rows, 0)
        first, last = scene_range(own_scene, block_scene, rows)
        inputs = tokens[micro].astype(jnp.float32)
        normed = layer_norm(inputs, ln1_gain, ln1_shift).astype(jnp.bfloat16)
        qkv = jnp.dot(normed, w_qkv, preferred_element_type=jnp.float32).astype(jnp.bfloat16)
        query = qkv[:, :width]
        own_kv = qkv[:, width:]
        kv_all = lax.all_gather(own_kv, "wide", axis=0, tiled=True)
        mixed, top_all, total_all = attend(query, kv_all, own_scene, block_scene, first, last)
        mixed_low = mixed.astype(jnp.bfloat16)
        middle = inputs + jnp.dot(mixed_low, w_out, preferred_element_type=jnp.float32)
        normed2 = layer_norm(middle, ln2_gain, ln2_shift).astype(jnp.bfloat16)
        pre = jnp.dot(normed2, w_up, preferred_element_type=jnp.float32)
        act_low = jax.nn.gelu(pre, approximate=False).astype(jnp.bfloat16)
        branch = of_everyone(
            jnp.dot(act_low, w_down, preferred_element_type=jnp.float32).astype(jnp.bfloat16),
            "narrow",
        ).astype(jnp.float32)
        results.append((middle + branch).astype(jnp.bfloat16))
        grad_out = out_grad[micro]
        grad_down = contract_rows(act_low, grad_out)
        grad_act = contract_cols(grad_out, w_down)
        unused_act, gelu_back = jax.vjp(partial(jax.nn.gelu, approximate=False), pre)
        grad_pre = gelu_back(grad_act)[0].astype(jnp.bfloat16)
        grad_up = contract_rows(normed2, grad_pre)
        grad_normed2 = of_everyone(
            contract_cols(grad_pre, w_up).astype(jnp.bfloat16), "narrow"
        ).astype(jnp.float32)
        unused_mid, second_back = jax.vjp(layer_norm, middle, ln2_gain, ln2_shift)
        grad_mid, grad_gain2, grad_shift2 = second_back(grad_normed2)
        grad_mid = grad_mid + grad_out.astype(jnp.float32)
        grad_mid_low = grad_mid.astype(jnp.bfloat16)
        grad_wout = contract_rows(mixed_low, grad_mid_low)
        grad_mixed = contract_cols(grad_mid_low, w_out).astype(jnp.bfloat16)
        grad_query, deltas, terms = attend_back(
            query, kv_all, own_scene, block_scene, top_all, total_all, grad_mixed, first, last
        )
        grad_kv = lax.psum_scatter(
            terms.astype(jnp.bfloat16), "wide", scatter_dimension=0, tiled=True
        ).astype(jnp.float32)
        grad_qkv = jnp.concatenate([grad_query, grad_kv], axis=1).astype(jnp.bfloat16)
        grad_wqkv = contract_rows(normed, grad_qkv)
        grad_normed = contract_cols(grad_qkv, w_qkv)
        unused_in, first_back = jax.vjp(layer_norm, inputs, ln1_gain, ln1_shift)
        grad_in, grad_gain1, grad_shift1 = first_back(grad_normed)
        input_grads.append(grad_in + grad_mid)
        local = (
            grad_wqkv,
            grad_wout,
            grad_up,
            grad_down,
            grad_gain1,
            grad_shift1,
            grad_gain2,
            grad_shift2,
        )
        totals = tuple((before + term for before, term in zip(totals, local)))
    totals = jax.tree.map(
        lambda part: part.astype(jnp.float32), lax.psum(shortened(totals), "wide")
    )
    grad_wqkv, grad_wout, grad_up, grad_down, grad_gain1, grad_shift1, grad_gain2, grad_shift2 = (
        totals
    )
    return (
        jnp.stack(results),
        jnp.stack(input_grads),
        grad_wqkv,
        grad_wout,
        grad_gain1,
        grad_shift1,
        grad_gain2,
        grad_shift2,
        grad_up,
        grad_down,
    )


def solution(mesh):
    placed = (
        P(None, "wide", None),
        P(),
        P(),
        P(),
        P(),
        P(),
        P(),
        P(),
        P(None, "narrow"),
        P("narrow", None),
        P(None, "wide", None),
    )
    return jax.shard_map(
        shards,
        mesh=mesh,
        in_specs=placed,
        out_specs=(
            P(None, "wide", None),
            P(None, "wide", None),
            P(),
            P(),
            P(),
            P(),
            P(),
            P(),
            P(None, "narrow"),
            P("narrow", None),
        ),
        check_vma=False,
    )
```

profile of v0, /device:TPU:1, one launch (start us, length us, event | category | flops | bytes accessed | tf_op | source)
XLA Modules:
  0.0 894.4 jit_solution(11852014119683795070)
XLA Ops:
  22.9 3.3 compare_convert_fusion.2
  40.9 19.3 %all-gather.3.cloned.1.call-done = bf16[2048,1536]{1,0:T(8,128)(2,1)} async-done(((bf16[128,1536]{1,0:T(8,128)(2,1)}), bf16[2048,1536]{1,0:T(8,128)(2,1)}) %all-gather.3.cloned.1.call-update) | async-done | bytes 6291472 | tf_op jit(solution)/shard_map/all_gather | solution.py:197
  60.2 8.6 copy.95
  68.8 7.8 while.88
  77.5 13.1 %while.89 = (s32[]{:T(128)}, f32[128,12,64]{0,2,1:T(8,128)}, s32[]{:T(128)}, bf16[2048,1536]{0,1:T(8,128)(2,1)}, s32[128]{0:T(128)}, /*index=5*/s32[2048]{0:T(10...) while((s32[]{:T(128)}, f32[128,12,64]{0,2,1:T(8,128)}, ...), condition=%wide.region_9.10_spmd, body=%wide.region_8.9_spmd.sunk | while | flops 51625992 | bytes 2210003 | solution.py:104
  87.9 2.7 fusion.294
  98.2 6.5 all-to-all-start.2
  105.7 8.7 copy.98
  114.5 39.3 %while.90 = (s32[]{:T(128)}, f32[12,128]{1,0:T(8,128)S(1)}, f32[12,128]{1,0:T(8,128)S(1)}, s32[]{:T(128)}, s32[128]{0:T(128)}, /*index=5*/s32[2048]{0:T(1024)}, ...) while((s32[]{:T(128)}, f32[12,128]{1,0:T(8,128)S(1)}, ...), condition=%wide.region_20.21_spmd, body=%wide.region_17.20_spmd.sunk | while | flops 26364932 | bytes 2490547 | solution.py:95
  154.6 65.2 %while.91 = (s32[]{:T(128)}, f32[128,12,64]{0,2,1:T(8,128)}, s32[]{:T(128)}, bf16[2048,1536]{0,1:T(8,128)(2,1)}, s32[128]{0:T(128)}, /*index=5*/s32[2048]{0:T(10...) while((s32[]{:T(128)}, f32[128,12,64]{0,2,1:T(8,128)}, ...), condition=%wide.region_22.23_spmd, body=%wide.region_21.22_spmd.sunk | while | flops 51625992 | bytes 2210003 | solution.py:104
  228.9 6.5 all-to-all-start.3
  238.0 20.0 %all-to-all-done.3 = bf16[8,128,768]{2,1,0:T(8,128)(2,1)} async-done(((bf16[8,128,768]{2,1,0:T(8,128)(2,1)}), bf16[8,128,768]{2,1,0:T(8,128)(2,1)}, u32[]{:S(2)}, u32[]{:S(2)}) %all-to-all-start.3) | async-done | bytes 1572896 | tf_op jit(solution)/shard_map/all_to_all | solution.py:19
  260.1 4.3 all-to-all-start
  266.9 18.9 %all-to-all-done = bf16[8,128,768]{2,1,0:T(8,128)(2,1)} async-done(((bf16[8,128,768]{2,1,0:T(8,128)(2,1)}), bf16[8,128,768]{2,1,0:T(8,128)(2,1)}, u32[]{:S(2)}, u32[]{:S(2)}) %all-to-all-start) | async-done | bytes 1572896 | tf_op jit(solution)/shard_map/all_to_all | solution.py:19
  288.0 4.3 all-to-all-start.1
  297.6 2.7 convert_reduce_fusion
  302.4 10.3 %all-to-all-done.1 = bf16[8,128,768]{2,1,0:T(8,128)(2,1)} async-done(((bf16[8,128,768]{2,1,0:T(8,128)(2,1)}), bf16[8,128,768]{2,1,0:T(8,128)(2,1)}, u32[]{:S(2)}, u32[]{:S(2)}) %all-to-all-start.1) | async-done | bytes 1572896 | tf_op jit(solution)/shard_map/all_to_all | solution.py:19
  322.3 8.6 while.92
  331.6 3.4 broadcast.539.clone.1
  335.0 12.5 %while.93 = (s32[]{:T(128)}, f32[128,12,64]{0,2,1:T(8,128)}, bf16[2048,1536]{0,1:T(8,128)(2,1)}, s32[]{:T(128)}, bf16[2048,1536]{0,1:T(8,128)(2,1)}, /*index=5*/...) while((s32[]{:T(128)}, f32[128,12,64]{0,2,1:T(8,128)}, ...), condition=%wide.region_33.34_spmd, body=%wide.region_32.33_spmd.sunk | while | flops 128598024 | bytes 12439903 | solution.py:156
  347.5 8.7 copy.113
  360.6 43.1 %while.94 = (s32[]{:T(128)}, f32[12,128]{1,0:T(8,128)S(1)}, s32[]{:T(128)}, s32[128]{0:T(128)}, s32[2048]{0:T(1024)}, /*index=5*/bf16[2048,1536]{0,1:T(8,128)(2,...) while((s32[]{:T(128)}, f32[12,128]{1,0:T(8,128)S(1)}, ...), condition=%wide.region_42.43_spmd, body=%wide.region_40.42_spmd.sunk | while | flops 51527688 | bytes 4004087 | solution.py:128
  404.5 3.5 broadcast.539.clone
  407.9 61.4 %while.95 = (s32[]{:T(128)}, f32[128,12,64]{0,2,1:T(8,128)}, bf16[2048,1536]{0,1:T(8,128)(2,1)}, s32[]{:T(128)}, bf16[2048,1536]{0,1:T(8,128)(2,1)}, /*index=5*/...) while((s32[]{:T(128)}, f32[128,12,64]{0,2,1:T(8,128)}, ...), condition=%wide.region_44.45_spmd, body=%wide.region_43.44_spmd.sunk | while | flops 128598024 | bytes 12439903 | solution.py:156
  469.3 8.6 copy.115
  487.0 110.3 %reduce-scatter.7.cloned.1.call-done = bf16[128,1536]{1,0:T(8,128)(2,1)} async-done(((bf16[2048,1536]{1,0:T(8,128)(2,1)}), bf16[128,1536]{1,0:T(8,128)(2,1)}) %reduce-scatter.7.cloned.1.call-update) | async-done | bytes 393232
  599.2 5.3 fusion.103
  604.5 114.8 %reduce-scatter.9.cloned.1.call-done = bf16[128,1536]{1,0:T(8,128)(2,1)} async-done(((bf16[2048,1536]{1,0:T(8,128)(2,1)}), bf16[128,1536]{1,0:T(8,128)(2,1)}) %reduce-scatter.9.cloned.1.call-update) | async-done | bytes 393232
  721.2 6.4 add_convert_fusion
  737.6 31.8 %all-reduce = (bf16[768]{0:T(1024)(128)(2,1)}, bf16[768]{0:T(1024)(128)(2,1)}, bf16[768]{0:T(1024)(128)(2,1)}, bf16[768]{0:T(1024)(128)(2,1)}) all-reduce(bf16[768]{0:T(1024)(128)(2,1)} %add_convert_fusion.11, bf16[768]{0:T(1024)(128)(2,1)S(1)} %add_convert_fusion.10, ...), channel_id=1, replica_groups=mesh['wide'=16,'narrow'=8] {'wide'}, use_global_device_ids=true, to_apply=%region_52.53 | all-reduce | flops 3072 | bytes 12288 | tf_op jit(solution)/shard_map/psum | solution.py:248
  778.8 99.8 %all-reduce.4.cloned.1.call-done = (bf16[768,2304]{1,0:T(8,128)(2,1)}, bf16[768,768]{1,0:T(8,128)(2,1)}, bf16[768,384]{1,0:T(8,128)(2,1)}, bf16[384,768]{1,0:T(8,128)(2,1)}) async-done(((bf16[768,2304]{1,0:T(8,128)(2,1)}, bf16[768,768]{1,0:T(8,128)(2,1)}, bf16[768,384]{1,0:T(8,128)(2,1)}, bf16[384,768]{1,0:T(8,128)(2,1)}), (bf16[768,2304]{1,0:T(8,128)(2,1)}, bf16[768,768]{1,0:T(8,128)(2,1)}, ...) | async-done | bytes 5898256 | tf_op jit(solution)/shard_map/psum | solution.py:248
  878.6 5.6 convert_element_type.239
  (748 shorter events, 356.2 us)
Async XLA Ops:
  7.2 53.0 %all-gather.3.cloned.1.call-start = ((), (), s32[]{:S(2)}) async-start(), calls=%async_computation.6 | async-start | bytes 6684672 | tf_op jit(solution)/shard_map/all_gather | solution.py:197
  8.6 5.7 copy-start.72
  14.2 91.5 %all-gather.5.cloned.1.call-start = ((), (), s32[]{:S(2)}) async-start(), calls=%async_computation.7 | async-start | bytes 6684672 | tf_op jit(solution)/shard_map/all_gather | solution.py:197
  90.6 5.3 copy-start.44
  90.6 5.3 copy-start.54
  98.2 128.6 %all-to-all-start.2 = ((bf16[8,128,768]{2,1,0:T(8,128)(2,1)}), bf16[8,128,768]{2,1,0:T(8,128)(2,1)}, u32[]{:S(2)}, u32[]{:S(2)}) async-start(bf16[8,128,768]{2,1,0:T(8,128)(2,1)} %broadcast_in_dim.230), calls=%async_computation.2 | async-start | bytes 3145728 | tf_op jit(solution)/shard_map/all_to_all | solution.py:19
  219.8 5.3 copy-start.55
  228.9 29.0 %all-to-all-start.3 = ((bf16[8,128,768]{2,1,0:T(8,128)(2,1)}), bf16[8,128,768]{2,1,0:T(8,128)(2,1)}, u32[]{:S(2)}, u32[]{:S(2)}) async-start(bf16[8,128,768]{2,1,0:T(8,128)(2,1)} %broadcast_in_dim.235), calls=%async_computation.3 | async-start | bytes 3145728 | tf_op jit(solution)/shard_map/all_to_all | solution.py:19
  260.1 25.7 %all-to-all-start = ((bf16[8,128,768]{2,1,0:T(8,128)(2,1)}), bf16[8,128,768]{2,1,0:T(8,128)(2,1)}, u32[]{:S(2)}, u32[]{:S(2)}) async-start(bf16[8,128,768]{2,1,0:T(8,128)(2,1)} %broadcast_in_dim.225), calls=%async_computation | async-start | bytes 3145728 | tf_op jit(solution)/shard_map/all_to_all | solution.py:19
  288.0 24.6 %all-to-all-start.1 = ((bf16[8,128,768]{2,1,0:T(8,128)(2,1)}), bf16[8,128,768]{2,1,0:T(8,128)(2,1)}, u32[]{:S(2)}, u32[]{:S(2)}) async-start(bf16[8,128,768]{2,1,0:T(8,128)(2,1)} %broadcast_in_dim.229), calls=%async_computation.1 | async-start | bytes 3145728 | tf_op jit(solution)/shard_map/all_to_all | solution.py:19
  292.3 304.9 %reduce-scatter.7.cloned.1.call-start = ((), (), s32[]{:S(2)}) async-start(), calls=%async_computation.8 | async-start | bytes 6684672
  294.9 5.4 copy-start.16
  294.9 5.4 copy-start.19
  295.0 5.4 copy-start.65
  295.0 5.4 copy-start.76
  295.0 5.4 copy-start.79
  295.0 5.4 copy-start.86
  295.0 5.4 copy-start.89
  295.0 6.3 copy-start.101
  295.0 6.9 copy-start.103
  312.7 5.1 copy-start.39
  314.4 4.9 copy-start.14
  356.2 363.1 %reduce-scatter.9.cloned.1.call-start = ((), (), s32[]{:S(2)}) async-start(), calls=%async_computation.9 | async-start | bytes 6684672
  478.0 400.5 %all-reduce.4.cloned.1.call-start = ((), (), s32[]{:S(2)}) async-start(), calls=%async_computation.10 | async-start | bytes 11796480 | tf_op jit(solution)/shard_map/psum | solution.py:248
  485.5 113.7 %copy-start.53 = (f32[768]{0:T(1024)S(1)}, f32[768]{0:T(1024)}, u32[]{:S(2)}) copy-start(f32[768]{0:T(1024)} %param.29) | copy-start | bytes 9220
  485.5 113.7 %copy-start.59 = (f32[768]{0:T(1024)S(1)}, f32[768]{0:T(1024)}, u32[]{:S(2)}) copy-start(f32[768]{0:T(1024)} %param.30) | copy-start | bytes 9220
  485.5 113.7 %copy-start.71 = (f32[128]{0:T(128)S(1)}, f32[128]{0:T(128)}, u32[]{:S(2)}) copy-start(f32[128]{0:T(128)} %copy-done.70) | copy-start | bytes 1540
  599.2 122.0 %copy-start.73 = (f32[128]{0:T(128)S(1)}, f32[128]{0:T(128)}, u32[]{:S(2)}) copy-start(f32[128]{0:T(128)} %copy-done.72) | copy-start | bytes 1540
  729.4 5.0 copy-start.7
  729.4 5.0 copy-start.42
  729.4 5.0 copy-start.45
  878.6 5.6 copy-start.43
  (133 other events, 305.2 us)
Sparse Core Ops, SparseCore 0:
  14.3 45.8 all-gather.2
  62.5 43.1 all-gather.4
  356.3 240.9 reduce-scatter.6
  599.5 119.7 reduce-scatter.8
  727.7 150.7 all-reduce.3
where the time goes:
time: 904 us; the launch traced here: 894 us
  waiting for transfers between devices  394 us (44%)
  local copies, waits for them, and re-layouts  177 us (20%)
  matrix products  140 us (15%)
  other arithmetic  106 us (12%)
  blocking collectives  31.8 us (4%)
  starting transfers between devices  22.2 us (2%)
  between operations  21.4 us (2%)
    unnamed x7, waiting for transfers between devices  225 us
    psum x1, waiting for transfers between devices, shards(): lax.psum(shortened(totals), 'wide')  99.8 us
    all_to_all x4, waiting for transfers between devices, from_everyone(): lax.all_to_all(jnp.broadcast_to(value[None], (length, *value.shape)), axi...  49.2 us
    dynamic_slice x48, local copies, waits for them, and re-layouts, key_piece(): scenes = lax.dynamic_slice_in_dim(block_scene, index * rows, rows, 0)  36 us
    slice x24, local copies, waits for them, and re-layouts, key_piece(): piece[:, :width]  32.9 us
    dot_general x24, matrix products, parts_of(): jnp.einsum('qhd,khd->hqk', q_heads, keys, preferred_element_type=jnp.floa...  32 us
    psum x1, blocking collectives, shards(): lax.psum(shortened(totals), 'wide')  31.8 us
    dot_general x12, matrix products, output_step(): jnp.einsum('hqk,khd->qhd', probs, values, preferred_element_type=jnp.floa...  31.6 us
  transfers between devices with their start and end apart: 9, of which 8 were waited for; matrix products, arithmetic and copies ran while one was open for 38% of the time, Pallas kernels for 0%

commit v1 on v0

v1 whole, which is shorter than its diff:
```python
import functools

import jax
import jax.numpy as jnp
from jax import lax
from jax.experimental import pallas as pl
from jax.experimental.pallas import tpu as pltpu
from jax.sharding import Mesh
from jax.sharding import PartitionSpec as P

D = 768
HD = 64
FFL = 384
TOK = 128
BLK = 32
EPS = 1e-05
BF = jnp.bfloat16
F32 = jnp.float32

CHIP = ("y", "xl")
CORE = "c"
MICRO = "zh"
GROUP = ("zl", "xh")
NARROW = (MICRO, *GROUP)
WIDE = (*CHIP, CORE)


def chip_index():
    return lax.axis_index("y") * 2 + lax.axis_index("xl")


def group_index():
    return lax.axis_index("zl") * 2 + lax.axis_index("xh")


def mm(left, right):
    return lax.dot_general(left, right, (((1,), (0,)), ((), ())), preferred_element_type=F32)


def mm_nt(left, right):
    return lax.dot_general(left, right, (((1,), (1,)), ((), ())), preferred_element_type=F32)


def mm_tn(left, right):
    return lax.dot_general(left, right, (((0,), (0,)), ((), ())), preferred_element_type=F32)


def normalized(values):
    center = values - jnp.mean(values, axis=-1, keepdims=True)
    spread = jnp.mean(center * center, axis=-1, keepdims=True)
    inverse = lax.rsqrt(spread + EPS)
    return center * inverse, inverse


def norm_back(grad, unit, inverse, gain):
    scaled = grad * gain
    first = jnp.mean(scaled, axis=-1, keepdims=True)
    second = jnp.mean(scaled * unit, axis=-1, keepdims=True)
    return inverse * (scaled - first - unit * second)


def halves(block):
    lane = lax.broadcasted_iota(jnp.int32, block.shape, 1)
    zero = jnp.zeros_like(block)
    return jnp.where(lane < HD, block, zero), jnp.where(lane < HD, zero, block)


def join(low, high):
    lane = lax.broadcasted_iota(jnp.int32, low.shape, 1)
    return jnp.where(lane < HD, low, high)


def span(scene_ref):
    micro = lax.axis_index(MICRO)
    own = scene_ref[micro, chip_index() * 4]
    first = jnp.int32(0)
    count = jnp.int32(0)
    for index in range(8):
        other = scene_ref[micro, index * 4]
        first += (other < own).astype(jnp.int32)
        count += (other == own).astype(jnp.int32)
    return first, count > 1


def three(value):
    a = value.astype(BF).astype(F32)
    b = (value - a).astype(BF).astype(F32)
    c = value - a - b
    return a, b, c


def put_columns(width, rows, start, columns):
    lane = lax.broadcasted_iota(jnp.int32, (rows, width), 1)
    out = jnp.zeros((rows, width), F32)
    for offset, column in enumerate(columns):
        out = jnp.where(lane == start + offset, column, out)
    return out


def call(kernel, outs, ins, cost, scratch=(), smem=0):
    specs = [pl.BlockSpec(memory_space=pltpu.SMEM)] * smem + [
        pl.BlockSpec(memory_space=pl.ANY) if any_space else pl.BlockSpec(memory_space=pltpu.VMEM)
        for any_space in [isinstance(value, tuple) for value in ins[smem:]]
    ]
    values = [value[0] if isinstance(value, tuple) else value for value in ins]
    return pl.pallas_call(
        kernel,
        out_shape=[jax.ShapeDtypeStruct(shape, dtype) for shape, dtype in outs],
        in_specs=specs,
        out_specs=[pl.BlockSpec(memory_space=pltpu.VMEM)] * len(outs),
        scratch_shapes=list(scratch),
        cost_estimate=pl.CostEstimate(flops=cost, bytes_accessed=2000000, transcendentals=0),
        compiler_params=pltpu.CompilerParams(vmem_limit_bytes=40 * 2**20),
    )(*values)


def project_kernel(tok_ref, gain_ref, shift_ref, w_ref, kv_ref, q_ref, normed_ref, x_buf, w_buf, x_sem, w_sem):
    micro = lax.axis_index(MICRO)
    group = group_index()
    copy_x = pltpu.make_async_copy(tok_ref.at[micro], x_buf, x_sem)
    copy_x.start()
    copies = []
    for slot, part in enumerate((1, 2, 0)):
        column = pl.multiple_of(part * D + (group // 2) * 384, 128)
        copy = pltpu.make_async_copy(w_ref.at[:, pl.ds(column, 384)], w_buf.at[slot], w_sem.at[slot])
        copy.start()
        copies.append(copy)
    copy_x.wait()
    unit, _ = normalized(x_buf[...].astype(F32))
    normed = (unit * gain_ref[...] + shift_ref[...]).astype(BF)
    normed_ref[...] = normed
    odd = (group % 2) == 1
    parts = []
    for slot in range(3):
        copies[slot].wait()
        full = mm(normed, w_buf[slot])
        parts.append(jnp.where(odd, full[:, 192:], full[:, :192]).astype(BF))
    kv = jnp.concatenate(parts[:2], axis=1)
    query = jnp.concatenate([parts[2], jnp.zeros((TOK, 64), BF)], axis=1)
    for chip in range(8):
        kv_ref[chip] = kv
        q_ref[chip] = query


def attend_kernel(scene_ref, q_ref, same_ref, other_ref, out_ref):
    first, big = span(scene_ref)

    def run(count):
        rows = count * TOK
        keys = jnp.concatenate(
            [ref[pl.ds(first, count)].reshape(rows, 384) for ref in (same_ref, other_ref)], axis=0
        )
        query = q_ref[0]
        q0, q1 = halves(query[:, :128])
        blocks = [keys[:, :128], keys[:, 128:256], keys[:, 256:]]
        mixed = []
        columns = []
        for qh, kb, vb in ((q0, 0, 1), (q1, 0, 2), (query[:, 128:], 1, 2)):
            scores = mm_nt(qh, blocks[kb]) * (HD**-0.5)
            top = jnp.max(scores, axis=-1, keepdims=True)
            weights = jnp.exp(scores - top)
            total = jnp.sum(weights, axis=-1, keepdims=True)
            probs = (weights * (1.0 / total)).astype(BF)
            mixed.append(mm(probs, blocks[vb]))
            columns += three(top + jnp.log(total))
        stats = put_columns(128, TOK, 0, columns)
        packed = jnp.concatenate([join(stats, mixed[0]), join(mixed[1], mixed[2])], axis=1).astype(BF)
        for index in range(8):
            out_ref[index] = packed

    @pl.when(big)
    def _():
        run(5)

    @pl.when(jnp.logical_not(big))
    def _():
        run(1)


def forward_kernel(
    mixed_ref, tok_ref, og_ref, wo_ref, gain_ref, shift_ref, up_ref, down_ref,
    out_ref, middle_ref, normed_ref, act_ref, gpre_ref,
):
    x = tok_ref[...].reshape(2 * TOK, D).astype(F32)
    total = x
    for group in range(4):
        rows = jnp.concatenate([mixed_ref[group], mixed_ref[4 + group]], axis=0)
        total = total + mm(rows, wo_ref[group])
    middle_ref[...] = total.reshape(8, BLK, D)
    unit, _ = normalized(total)
    normed = (unit * gain_ref[...] + shift_ref[...]).astype(BF)
    normed_ref[...] = normed
    pre = mm(normed, up_ref[...])
    cdf = 0.5 * (1.0 + lax.erf(pre * (0.5**0.5)))
    act = (pre * cdf).astype(BF)
    act_ref[...] = act
    slope = cdf + pre * jnp.exp(-0.5 * pre * pre) * 0.3989422804014327
    grad_out = og_ref[...].reshape(2 * TOK, D)
    gpre = (mm_nt(grad_out, down_ref[...]) * slope).astype(BF)
    gpre_ref[...] = gpre
    grad = mm_nt(gpre, up_ref[...]).astype(BF).reshape(8, BLK, D)
    branch = mm(act, down_ref[...]).astype(BF).reshape(8, BLK, D)
    out_ref[:, :BLK] = branch
    out_ref[:, BLK:] = grad


def ff_grads_kernel(normed_ref, act_ref, gpre_ref, og_ref, out_ref):
    up = mm_tn(normed_ref[...], gpre_ref[...]).astype(BF)
    grad_out = og_ref[...].reshape(2 * TOK, D)
    down = mm_tn(act_ref[...], grad_out).astype(BF)
    for tile in range(16):
        half = (tile % 2) * 384
        out_ref[tile, :, :384] = up[tile * 48:(tile + 1) * 48]
        out_ref[tile, :, 384:] = down[(tile // 2) * 48:(tile // 2 + 1) * 48, half:half + 384]


def middle_kernel(
    sums_ref, middle_ref, og_ref, mixed_ref, wo_ref, gain_ref, out_ref, rest_ref
):
    micro = lax.axis_index(MICRO)
    group = group_index()
    start = pl.multiple_of(group * BLK, BLK)
    total = sums_ref[0].astype(F32)
    for index in range(1, 8):
        total = total + sums_ref[index].astype(F32)
    branch, grad = total[:BLK], total[BLK:]
    middle = middle_ref[micro * 4 + group]
    unit, inverse = normalized(middle)
    grad_mid = og_ref[micro, pl.ds(start, BLK)].astype(F32) + norm_back(grad, unit, inverse, gain_ref[...])
    low = grad_mid.astype(BF)
    for head_group in range(4):
        mixed = mixed_ref[micro * 4 + head_group, pl.ds(start, BLK)].astype(F32)
        back = mm_nt(low, wo_ref[head_group]).astype(BF).astype(F32)
        lane = lax.broadcasted_iota(jnp.int32, (BLK, 256), 1)
        product = mixed * back
        columns = []
        for head in range(3):
            inside = (lane >= (head + 1) * HD) & (lane < (head + 2) * HD)
            columns += three(jnp.sum(jnp.where(inside, product, 0.0), axis=-1, keepdims=True))
        stats = put_columns(256, BLK, 9, columns)
        packed = jnp.where(lane < 9, mixed, jnp.where(lane < HD, stats, back)).astype(BF)
        for chip in range(8):
            out_ref[chip * 4 + head_group] = packed
    result = (middle + branch).astype(BF)
    gain_grad = jnp.sum(grad * unit, axis=0, keepdims=True)
    shift_grad = jnp.sum(grad, axis=0, keepdims=True)
    vectors = jnp.concatenate([gain_grad, shift_grad, jnp.zeros((14, D), F32)], axis=0).astype(BF)
    for index in range(8):
        rest_ref[index, :BLK] = result
        rest_ref[index, BLK:2 * BLK] = low
        rest_ref[index, 2 * BLK:] = vectors


def attend_back_kernel(
    scene_ref, kvs_ref, kvo_ref, qs_ref, qo_ref, gs_ref, go_ref, out_ref
):
    first, big = span(scene_ref)
    chip = chip_index()
    scale = HD**-0.5

    def run(count):
        rows = count * TOK

        def gathered(one, two, width):
            return jnp.concatenate(
                [ref[pl.ds(first, count)].reshape(rows, width) for ref in (one, two)], axis=0
            )

        def cut(value):
            return [value[:, at:at + 128] for at in range(0, value.shape[1], 128)]

        kv = cut(gathered(kvs_ref, kvo_ref, 384))
        query = cut(gathered(qs_ref, qo_ref, 256))
        grad = cut(gathered(gs_ref, go_ref, 256))
        kv_own = cut(kvs_ref[chip])
        q_own = cut(qs_ref[chip])
        g_own = cut(gs_ref[chip])
        q_heads = [*halves(q_own[0]), q_own[1]]
        g_heads = [halves(g_own[0])[1], *halves(g_own[1])]
        k_heads = [*halves(kv_own[0]), halves(kv_own[1])[0]]
        v_heads = [halves(kv_own[1])[1], *halves(kv_own[2])]
        own_stats = g_own[0].astype(F32)
        all_stats = grad[0].astype(F32).T

        def column(at):
            return own_stats[:, at:at + 1] + own_stats[:, at + 1:at + 2] + own_stats[:, at + 2:at + 3]

        def row(at):
            return all_stats[at:at + 1] + all_stats[at + 1:at + 2] + all_stats[at + 2:at + 3]

        dq, dk, dv = [], [], []
        for head, (kb, vb) in enumerate(((0, 1), (0, 2), (1, 2))):
            qb, gb = (0, 0, 1)[head], (0, 1, 1)[head]
            probs = jnp.exp(mm_nt(q_heads[head], kv[kb]) * scale - column(3 * head))
            gap = mm_nt(g_heads[head], kv[vb]) - column(9 + 3 * head)
            dq.append(mm((probs * gap).astype(BF), kv[kb]) * scale)
            probs = jnp.exp(mm_nt(k_heads[head], query[qb]) * scale - row(3 * head))
            gap = mm_nt(v_heads[head], grad[gb]) - row(9 + 3 * head)
            dv.append(mm(probs.astype(BF), grad[gb]))
            dk.append(mm((probs * gap).astype(BF), query[qb]) * scale)
        packed = jnp.concatenate(
            [join(dk[0], dk[1]), join(dk[2], dv[0]), join(dv[1], dv[2]), join(dq[0], dq[1]), dq[2][:, :HD]],
            axis=1,
        ).astype(BF)
        for index in range(8):
            out_ref[index] = packed

    @pl.when(big)
    def _():
        run(5)

    @pl.when(jnp.logical_not(big))
    def _():
        run(1)


def weight_grads_kernel(gqkv_ref, normed_ref, mixed_ref, rest_ref, out_ref):
    index = lax.axis_index(MICRO) * 4 + group_index()
    grad = mm_tn(normed_ref[...], gqkv_ref[0])
    low = jnp.concatenate([rest_ref[lax.axis_index(MICRO) * 4 + b, BLK:2 * BLK] for b in range(4)], axis=0)
    out = mm_tn(mixed_ref[index], low)[HD:]
    for tile in range(16):
        rows = grad[tile * 48:(tile + 1) * 48]
        at, column = (tile // 4) * 48, (tile % 4) * 192
        out_ref[2 * tile] = rows[:, :384].astype(BF)
        out_ref[2 * tile + 1] = jnp.concatenate(
            [rows[:, 384:], out[at:at + 48, column:column + 192]], axis=1
        ).astype(BF)


def sum_kernel(parts, copies, in_ref, out_ref):
    total = in_ref[0].astype(F32)
    for index in range(1, parts):
        total = total + in_ref[index].astype(F32)
    total = total.astype(BF)
    for index in range(copies):
        out_ref[index] = total


def spread_kernel(same_ref, other_ref, qkv_ref, out_ref):
    swapped = lax.axis_index(CORE) == 1
    same, other = same_ref[0], other_ref[0]
    for core in range(2):
        block = jnp.where(swapped, other, same) if core == 0 else jnp.where(swapped, same, other)
        block = block.astype(F32)
        rows = slice(core * 48, (core + 1) * 48)
        for part, half, at in ((1, 0, 0), (2, 0, 192), (0, 1, 0)):
            qkv_ref[rows, part * D:(part + 1) * D] = jnp.concatenate(
                [block[half * 4 + group][:, at:at + 192] for group in range(4)], axis=1
            )
        for group in range(4):
            out_ref[group, 0, :, core * 192:(core + 1) * 192] = block[4 + group][:, 192:]


def spread_ff_kernel(same_ref, other_ref, up_ref, down_ref):
    swapped = lax.axis_index(CORE) == 1
    for chip in range(8):
        same, other = same_ref[chip], other_ref[chip]
        for core in range(2):
            block = jnp.where(swapped, other, same) if core == 0 else jnp.where(swapped, same, other)
            block = block.astype(F32)
            tile = chip * 2 + core
            up_ref[tile * 48:(tile + 1) * 48] = block[:, :384]
            down_ref[chip * 48:(chip + 1) * 48, core * 384:(core + 1) * 384] = block[:, 384:]


def input_kernel(gqkv_ref, rest_ref, tok_ref, w_ref, gain_ref, grad_ref, result_ref, vec_ref):
    total = jnp.zeros((2 * TOK, D), F32)
    for part, at in ((1, 0), (2, 192), (0, 384)):
        for pair in range(2):
            rows = jnp.concatenate(
                [
                    jnp.concatenate(
                        [gqkv_ref[micro * 4 + pair * 2 + k][:, at:at + 192] for k in range(2)], axis=1
                    )
                    for micro in range(2)
                ],
                axis=0,
            )
            column = part * D + pair * 384
            total = total + mm_nt(rows, w_ref[:, column:column + 384])
    unit, inverse = normalized(tok_ref[...].reshape(2 * TOK, D).astype(F32))
    grad_mid = rest_ref[:, BLK:2 * BLK].reshape(2 * TOK, D).astype(F32)
    grad_ref[...] = (grad_mid + norm_back(total, unit, inverse, gain_ref[...])).reshape(2, TOK, D)
    result_ref[...] = rest_ref[:, :BLK].reshape(2, TOK, D)
    gain1 = jnp.sum(total * unit, axis=0, keepdims=True)
    shift1 = jnp.sum(total, axis=0, keepdims=True)
    second = rest_ref[:, 2 * BLK:].astype(F32)
    sums = second[0]
    for index in range(1, 8):
        sums = sums + second[index]
    vectors = jnp.concatenate([gain1, shift1, sums[:2], jnp.zeros((4, D), F32)], axis=0)
    for index in range(16):
        vec_ref[index] = vectors


def vectors_kernel(in_ref, a_ref, b_ref, c_ref, d_ref):
    total = in_ref[0]
    for index in range(1, 16):
        total = total + in_ref[index]
    for row, ref in enumerate((a_ref, b_ref, c_ref, d_ref)):
        ref[...] = total[row:row + 1]


def exchange(value, axes):
    return lax.all_to_all(value, axes, 0, 0, tiled=True)


def swap(value):
    return lax.ppermute(value, CORE, [(0, 1), (1, 0)])


def shards(
    tokens, scene_of_block, ln1_gain, ln1_shift, w_qkv, w_out, ln2_gain, ln2_shift, w_up, w_down, out_grad
):
    ln1_gain, ln1_shift, ln2_gain, ln2_shift = (
        value.reshape(1, D) for value in (ln1_gain, ln1_shift, ln2_gain, ln2_shift)
    )
    w_out_pad = jnp.pad(w_out.reshape(4, 192, D), ((0, 0), (HD, 0), (0, 0)))
    kv_send, q_send, normed = call(
        project_kernel,
        [((8, TOK, 384), BF), ((8, TOK, 256), BF), ((TOK, D), BF)],
        [(tokens,), ln1_gain, ln1_shift, (w_qkv,)],
        10**9,
        [
            pltpu.VMEM((TOK, D), BF),
            pltpu.VMEM((3, D, 384), BF),
            pltpu.SemaphoreType.DMA,
            pltpu.SemaphoreType.DMA((3,)),
        ],
    )
    kv_same = exchange(kv_send, CHIP)
    kv_other = swap(kv_same)
    (mixed_send,) = call(
        attend_kernel,
        [((8, TOK, 256), BF)],
        [scene_of_block, q_send, kv_same, kv_other],
        2 * 10**9,
        smem=1,
    )
    mixed = exchange(mixed_send, NARROW)
    q_send, _ = lax.optimization_barrier((q_send, mixed_send))
    q_same = exchange(q_send, CHIP)
    q_other = swap(q_same)
    ff_send, middle, normed2, act, grad_pre = call(
        forward_kernel,
        [
            ((8, 2 * BLK, D), BF),
            ((8, BLK, D), F32),
            ((2 * TOK, D), BF),
            ((2 * TOK, FFL), BF),
            ((2 * TOK, FFL), BF),
        ],
        [mixed, tokens, out_grad, w_out_pad, ln2_gain, ln2_shift, w_up, w_down],
        4 * 10**9,
    )
    ff_sums = exchange(ff_send, NARROW)
    (ff_grads,) = call(
        ff_grads_kernel, [((16, 48, D), BF)], [normed2, act, grad_pre, out_grad], 2 * 10**9
    )
    ff_grads = exchange(ff_grads, WIDE)
    grad_send, rest_send = call(
        middle_kernel,
        [((32, BLK, 256), BF), ((8, 80, D), BF)],
        [ff_sums, middle, out_grad, mixed, w_out_pad, ln2_gain],
        10**9,
    )
    grad_same = exchange(grad_send, (*CHIP, *GROUP)).reshape(8, TOK, 256)
    grad_other = swap(grad_same)
    rest_send, _ = lax.optimization_barrier((rest_send, grad_same))
    rest = exchange(rest_send, NARROW)
    (ff_total,) = call(functools.partial(sum_kernel, 16, 8), [((8, 48, D), BF)], [ff_grads], 10**8)
    ff_total, _ = lax.optimization_barrier((ff_total, grad_same))
    ff_same = exchange(ff_total, CHIP)
    ff_other = swap(ff_same)
    (gqkv_send,) = call(
        attend_back_kernel,
        [((8, TOK, 576), BF)],
        [scene_of_block, kv_same, kv_other, q_same, q_other, grad_same, grad_other],
        8 * 10**9,
        smem=1,
    )
    (weight_send,) = call(
        weight_grads_kernel, [((32, 48, 384), BF)], [gqkv_send, normed, mixed, rest], 10**9
    )
    weight_parts = exchange(weight_send, (*CHIP, CORE, MICRO))
    gqkv_send, _ = lax.optimization_barrier((gqkv_send, weight_send))
    gqkv = exchange(gqkv_send, NARROW)
    (weight_total,) = call(
        functools.partial(sum_kernel, 32, 64), [((64, 48, 384), BF)], [weight_parts], 10**8
    )
    weight_same = exchange(weight_total, (*CHIP, *NARROW)).reshape(8, 8, 48, 384)
    weight_other = swap(weight_same)
    input_grad, result, vector_send = call(
        input_kernel,
        [((2, TOK, D), F32), ((2, TOK, D), BF), ((16, 8, D), F32)],
        [gqkv, rest, tokens, w_qkv, ln1_gain],
        2 * 10**9,
    )
    vectors = exchange(vector_send, WIDE)
    gain1, shift1, gain2, shift2 = call(vectors_kernel, [((1, D), F32)] * 4, [vectors], 10**6)
    up_grad, down_grad = call(
        spread_ff_kernel, [((D, FFL), F32), ((FFL, D), F32)], [ff_same, ff_other], 10**7
    )
    qkv_grad, out_proj_grad = pl.pallas_call(
        spread_kernel,
        out_shape=[
            jax.ShapeDtypeStruct((D, 3 * D), F32),
            jax.ShapeDtypeStruct((4, 4, 48, D), F32),
        ],
        grid=(8,),
        in_specs=[pl.BlockSpec((1, 8, 48, 384), lambda p: (p, 0, 0, 0))] * 2,
        out_specs=[
            pl.BlockSpec((96, 3 * D), lambda p: (p, 0)),
            pl.BlockSpec((4, 1, 48, 384), lambda p: (0, p // 2, 0, p % 2)),
        ],
        cost_estimate=pl.CostEstimate(flops=10**7, bytes_accessed=15000000, transcendentals=0),
        compiler_params=pltpu.CompilerParams(vmem_limit_bytes=40 * 2**20),
    )(weight_same, weight_other)
    return (
        result,
        input_grad,
        qkv_grad,
        out_proj_grad.reshape(D, D),
        gain1.reshape(D),
        shift1.reshape(D),
        gain2.reshape(D),
        shift2.reshape(D),
        up_grad,
        down_grad,
    )


def solution(mesh):
    names = ("y", "xl", "c", "zh", "zl", "xh")
    fine = Mesh(mesh.devices.reshape(4, 2, 2, 2, 2, 2), names)
    tokens = P(None, WIDE, None)
    placed = (
        tokens, P(), P(), P(), P(), P(), P(), P(), P(None, NARROW), P(NARROW, None), tokens
    )
    return jax.shard_map(
        shards,
        mesh=fine,
        in_specs=placed,
        out_specs=(
            tokens, tokens, P(), P(), P(), P(), P(), P(), P(None, NARROW), P(NARROW, None)
        ),
        check_vma=False,
    )
```

time: 904 us -> 284 us (0.31)
  waiting for transfers between devices: 394 us -> 114 us
  matrix products: 140 us -> 0 us
  local copies, waits for them, and re-layouts: 177 us -> 37.9 us
  other arithmetic: 106 us -> 2.42 us
  starting transfers between devices: 22.2 us -> 60.5 us
  Pallas kernels: 0 us -> 24.8 us
  between operations: 21.4 us -> 1.01 us
  blocking collectives: 31.8 us -> 41.7 us
    unnamed x7 -> x0, waiting for transfers between devices: 225 us -> none
    dot_general x132 -> x0, matrix products: 140 us -> none  [the longest x24 32 us: parts_of(): jnp.einsum('qhd,khd->hqk', q_heads, keys, preferred_element_type=jnp.floa...]
    psum x1 -> x0, waiting for transfers between devices: 99.8 us -> none  [shards(): lax.psum(shortened(totals), 'wide')]
    slice x56 -> x0, local copies, waits for them, and re-layouts: 68.6 us -> none  [the longest x24 32.9 us: key_piece(): piece[:, :width]]
    all_to_all x4 -> x10, waiting for transfers between devices: 49.2 us -> 112 us  [exchange(): return lax.all_to_all(value, axes, 0, 0, tiled=True)]
    eq x48 -> x0, other arithmetic: 43 us -> none  [the longest x24 25.1 us: scores_of(): same = (own_scene[:, None] == scenes[None, :])[None]]
    all_to_all x0 -> x2, blocking collectives: none -> 41.7 us  [exchange(): return lax.all_to_all(value, axes, 0, 0, tiled=True)]
    dynamic_slice x50 -> x0, local copies, waits for them, and re-layouts: 37.5 us -> none  [the longest x48 36 us: key_piece(): scenes = lax.dynamic_slice_in_dim(block_scene, index * rows, rows, 0)]
  transfers between devices with their start and end apart: 9 -> 15, of which waited for: 8 -> 11; matrix products, arithmetic and copies ran while one was open for 38% -> 3% of each run, Pallas kernels for 0% -> 3%
where the time goes in v1:
time: 284 us; the launch traced here: 282 us
  waiting for transfers between devices  114 us (40%)
  starting transfers between devices  60.5 us (21%)
  blocking collectives  41.7 us (15%)
  local copies, waits for them, and re-layouts  37.9 us (13%)
  Pallas kernels  24.8 us (9%)
    all_to_all x10, waiting for transfers between devices, exchange(): return lax.all_to_all(value, axes, 0, 0, tiled=True)  112 us
    all_to_all x10, starting transfers between devices, exchange(): return lax.all_to_all(value, axes, 0, 0, tiled=True)  47.5 us
    all_to_all x2, blocking collectives, exchange(): return lax.all_to_all(value, axes, 0, 0, tiled=True)  41.7 us
    unnamed x88, local copies, waits for them, and re-layouts  30.3 us
    pallas_call x12, Pallas kernels, call(): pl.pallas_call(kernel, out_shape=[jax.ShapeDtypeStruct(shape, dtype) for...  17.5 us
    ppermute x5, starting transfers between devices, swap(): return lax.ppermute(value, CORE, [(0, 1), (1, 0)])  13 us
    pallas_call x1, Pallas kernels, shards(): pl.pallas_call(spread_kernel, out_shape=[jax.ShapeDtypeStruct((D, 3 * D),...  7.35 us
  transfers between devices with their start and end apart: 15, of which 11 were waited for; matrix products, arithmetic and copies ran while one was open for 3% of the time, Pallas kernels for 3%

profile of v1, /device:TPU:1, one launch (start us, length us, event | category | flops | bytes accessed | tf_op | source)
XLA Modules:
  0.0 282.0 jit_solution(15488874679918877273)
XLA Ops:
  5.0 2.6 shard_map.186
  7.6 17.9 %all_to_all.60.same_ref.kvs_ref = bf16[8,128,384]{2,1,0:T(8,128)(2,1)S(1)} all-to-all(bf16[8,128,384]{2,1,0:T(8,128)(2,1)S(1)} %get-tuple-element.35), channel_id=1, replica_groups=mesh['y'=4,'xl'=2,'c'=2,'zh'=2,'zl'=2,'xh'=2] {'y','xl'}, dimensions={0} | all-to-all | bytes 1572864 | tf_op jit(solution)/shard_map/all_to_all | solution.py:406
  29.4 2.8 shard_map.187
  33.9 7.2 %all-to-all-start.2 = ((bf16[8,128,256]{2,1,0:T(8,128)(2,1)}), bf16[8,128,256]{2,1,0:T(8,128)(2,1)S(1)}, u32[]{:S(2)}, u32[]{:S(2)}) async-start(bf16[8,128,256]{2,1,0:T(8,128)(2,1)} %shard_map.187), calls=%async_computation.2 | async-start | bytes 1048576 | tf_op jit(solution)/shard_map/all_to_all | solution.py:406
  42.6 9.2 %all-to-all-done.2.mixed_ref = bf16[8,128,256]{2,1,0:T(8,128)(2,1)S(1)} async-done(((bf16[8,128,256]{2,1,0:T(8,128)(2,1)}), bf16[8,128,256]{2,1,0:T(8,128)(2,1)S(1)}, u32[]{:S(2)}, u32[]{:S(2)}) %all-to-all-start.2) | async-done | bytes 524320 | tf_op jit(solution)/shard_map/all_to_all | solution.py:406
  59.1 3.5 %all-to-all-start.3 = ((bf16[8,64,768]{2,1,0:T(8,128)(2,1)}), bf16[8,64,768]{2,1,0:T(8,128)(2,1)S(1)}, u32[]{:S(2)}, u32[]{:S(2)}) async-start(bf16[8,64,768]{2,1,0:T(8,128)(2,1)} %copy-done.16), calls=%async_computation.3 | async-start | bytes 1572864 | tf_op jit(solution)/shard_map/all_to_all | solution.py:406
  62.7 12.6 %all-to-all-done.3.sums_ref = bf16[8,64,768]{2,1,0:T(8,128)(2,1)S(1)} async-done(((bf16[8,64,768]{2,1,0:T(8,128)(2,1)}), bf16[8,64,768]{2,1,0:T(8,128)(2,1)S(1)}, u32[]{:S(2)}, u32[]{:S(2)}) %all-to-all-start.3) | async-done | bytes 786464 | tf_op jit(solution)/shard_map/all_to_all | solution.py:406
  75.2 3.5 %all-to-all-start.1 = ((bf16[8,128,256]{2,1,0:T(8,128)(2,1)}), bf16[8,128,256]{2,1,0:T(8,128)(2,1)S(1)}, u32[]{:S(2)}, u32[]{:S(2)}) async-start(bf16[8,128,256]{2,1,0:T(8,128)(2,1)} %get-tuple-element.37.q_ref), calls=%async_computation.1 | async-start | bytes 1048576 | tf_op jit(solution)/shard_map/all_to_all | solution.py:406
  83.5 2.7 all-to-all-done.1.qs_ref
  86.3 3.9 %all-to-all-start.4 = ((bf16[32,32,256]{2,1,0:T(8,128)(2,1)}), bf16[32,32,256]{2,1,0:T(8,128)(2,1)S(1)}, u32[]{:S(2)}, u32[]{:S(2)}) async-start(bf16[32,32,256]{2,1,0:T(8,128)(2,1)} %copy-done.19), calls=%async_computation.4 | async-start | bytes 1048576 | tf_op jit(solution)/shard_map/all_to_all | solution.py:406
  90.2 3.9 %collective-permute-start.1 = (bf16[8,128,256]{2,1,0:T(8,128)(2,1)S(1)}, bf16[8,128,256]{2,1,0:T(8,128)(2,1)S(1)}, u32[]{:S(2)}, u32[]{:S(2)}) collective-permute-start(bf16[8,128,256]{2,1,0:T(8,128)(2,1)S(1)} %all-to-all-done.1.qs_ref), channel_id=1, source_target_pairs={{0,8},{8,0},{1,9},{9,1},{2,10},{10,2},{3,11},{11,3},{4,12},{12,4},... | collective-permute-start | bytes 1572872 | tf_op jit(solution)/shard_map/ppermute | solution.py:410
  94.0 5.7 %all-to-all-done.4 = bf16[32,32,256]{2,1,0:T(8,128)(2,1)S(1)} async-done(((bf16[32,32,256]{2,1,0:T(8,128)(2,1)}), bf16[32,32,256]{2,1,0:T(8,128)(2,1)S(1)}, u32[]{:S(2)}, u32[]{:S(2)}) %all-to-all-start.4) | async-done | bytes 524320 | tf_op jit(solution)/shard_map/all_to_all | solution.py:406
  99.7 5.0 %collective-permute-start.2 = (bf16[8,128,256]{2,1,0:T(8,128)(2,1)S(1)}, bf16[8,128,256]{2,1,0:T(8,128)(2,1)}, u32[]{:S(2)}, u32[]{:S(2)}) collective-permute-start(bf16[8,128,256]{2,1,0:T(8,128)(2,1)S(1)} %bitcast.6), channel_id=1, source_target_pairs={{0,8},{8,0},{1,9},{9,1},{2,10},{10,2},{3,11},{11,3},{4,12},{12,4},... | collective-permute-start | bytes 1572872 | tf_op jit(solution)/shard_map/ppermute | solution.py:410
  104.7 3.6 %all-to-all-start.5 = ((bf16[8,80,768]{2,1,0:T(8,128)(2,1)}), bf16[8,80,768]{2,1,0:T(8,128)(2,1)S(1)}, u32[]{:S(2)}, u32[]{:S(2)}) async-start(bf16[8,80,768]{2,1,0:T(8,128)(2,1)} %copy-done.11), calls=%async_computation.5 | async-start | bytes 1966080 | tf_op jit(solution)/shard_map/all_to_all | solution.py:406
  113.4 2.2 shard_map.190.gqkv_ref
  115.6 9.2 %all-to-all-done.5.rest_ref = bf16[8,80,768]{2,1,0:T(8,128)(2,1)S(1)} async-done(((bf16[8,80,768]{2,1,0:T(8,128)(2,1)}), bf16[8,80,768]{2,1,0:T(8,128)(2,1)S(1)}, u32[]{:S(2)}, u32[]{:S(2)}) %all-to-all-start.5) | async-done | bytes 983072 | tf_op jit(solution)/shard_map/all_to_all | solution.py:406
  126.6 23.7 %all_to_all.61.in_ref = bf16[32,48,384]{2,1,0:T(8,128)(2,1)S(1)} all-to-all(bf16[32,48,384]{2,1,0:T(8,128)(2,1)S(1)} %shard_map.191), channel_id=1, replica_groups=mesh['y'=4,'xl'=2,'c'=2,'zh'=2,'zl'=2,'xh'=2] {'y','xl','c','zh'}, dimensions={0} | all-to-all | bytes 2359296 | tf_op jit(solution)/shard_map/all_to_all | solution.py:406
  152.0 4.9 %all-to-all-start.8 = ((bf16[64,48,384]{2,1,0:T(8,128)(2,1)}), bf16[64,48,384]{2,1,0:T(8,128)(2,1)S(1)}, u32[]{:S(2)}, u32[]{:S(2)}) async-start(bf16[64,48,384]{2,1,0:T(8,128)(2,1)} %copy-done), calls=%async_computation.8 | async-start | bytes 4718592 | tf_op jit(solution)/shard_map/all_to_all | solution.py:406
  158.5 28.7 %all-to-all-done.8 = bf16[64,48,384]{2,1,0:T(8,128)(2,1)S(1)} async-done(((bf16[64,48,384]{2,1,0:T(8,128)(2,1)}), bf16[64,48,384]{2,1,0:T(8,128)(2,1)S(1)}, u32[]{:S(2)}, u32[]{:S(2)}) %all-to-all-start.8) | async-done | bytes 2359328 | tf_op jit(solution)/shard_map/all_to_all | solution.py:406
  187.2 6.4 %all-to-all-start.10 = ((bf16[16,48,768]{2,1,0:T(8,128)(2,1)}), bf16[16,48,768]{2,1,0:T(8,128)(2,1)S(1)}, u32[]{:S(2)}, u32[]{:S(2)}) async-start(bf16[16,48,768]{2,1,0:T(8,128)(2,1)} %copy-done.10), calls=%async_computation.10 | async-start | bytes 2359296 | tf_op jit(solution)/shard_map/all_to_all | solution.py:406
  193.9 17.1 %all-to-all-done.10.in_ref = bf16[16,48,768]{2,1,0:T(8,128)(2,1)S(1)} async-done(((bf16[16,48,768]{2,1,0:T(8,128)(2,1)}), bf16[16,48,768]{2,1,0:T(8,128)(2,1)S(1)}, u32[]{:S(2)}, u32[]{:S(2)}) %all-to-all-start.10) | async-done | bytes 1179680 | tf_op jit(solution)/shard_map/all_to_all | solution.py:406
  211.9 3.5 %all-to-all-start.11 = ((bf16[8,48,768]{2,1,0:T(8,128)(2,1)}), bf16[8,48,768]{2,1,0:T(8,128)(2,1)S(1)}, u32[]{:S(2)}, u32[]{:S(2)}) async-start(bf16[8,48,768]{2,1,0:T(8,128)(2,1)} %copy-done.6), calls=%async_computation.11 | async-start | bytes 1179648 | tf_op jit(solution)/shard_map/all_to_all | solution.py:406
  215.5 2.4 copy.21
  217.9 7.4 %all-to-all-done.11.same_ref = bf16[8,48,768]{2,1,0:T(8,128)(2,1)S(1)} async-done(((bf16[8,48,768]{2,1,0:T(8,128)(2,1)}), bf16[8,48,768]{2,1,0:T(8,128)(2,1)S(1)}, u32[]{:S(2)}, u32[]{:S(2)}) %all-to-all-start.11) | async-done | bytes 589856 | tf_op jit(solution)/shard_map/all_to_all | solution.py:406
  226.1 4.3 %all-to-all-start.6 = ((bf16[8,128,576]{1,2,0:T(8,128)(2,1)}), bf16[8,128,576]{1,2,0:T(8,128)(2,1)}, u32[]{:S(2)}, u32[]{:S(2)}) async-start(bf16[8,128,576]{1,2,0:T(8,128)(2,1)} %copy.21), calls=%async_computation.6 | async-start | bytes 2359296 | tf_op jit(solution)/shard_map/all_to_all | solution.py:406
  232.3 14.5 %all-to-all-done.6 = bf16[8,128,576]{1,2,0:T(8,128)(2,1)} async-done(((bf16[8,128,576]{1,2,0:T(8,128)(2,1)}), bf16[8,128,576]{1,2,0:T(8,128)(2,1)}, u32[]{:S(2)}, u32[]{:S(2)}) %all-to-all-start.6) | async-done | bytes 1179680 | tf_op jit(solution)/shard_map/all_to_all | solution.py:406
  246.8 2.4 copy.22.gqkv_ref
  253.5 2.7 shard_map.192
  257.0 6.8 %all-to-all-start.9 = ((f32[16,8,768]{2,1,0:T(8,128)}), f32[16,8,768]{2,1,0:T(8,128)S(1)}, u32[]{:S(2)}, u32[]{:S(2)}) async-start(f32[16,8,768]{2,1,0:T(8,128)} %copy-done.26), calls=%async_computation.9 | async-start | bytes 786432 | tf_op jit(solution)/shard_map/all_to_all | solution.py:406
  264.9 2.6 shard_map.198
  267.5 4.7 %all-to-all-done.9.in_ref = f32[16,8,768]{2,1,0:T(8,128)S(1)} async-done(((f32[16,8,768]{2,1,0:T(8,128)}), f32[16,8,768]{2,1,0:T(8,128)S(1)}, u32[]{:S(2)}, u32[]{:S(2)}) %all-to-all-start.9) | async-done | bytes 393248 | tf_op jit(solution)/shard_map/all_to_all | solution.py:406
  274.7 7.4 %shard_map.194 = (f32[768,2304]{1,0:T(8,128)}, f32[4,4,48,768]{3,2,1,0:T(8,128)}) custom-call(bf16[8,8,48,384]{3,2,1,0:T(8,128)(2,1)S(1)} %bitcast.5, bf16[8,8,48,384]{3,2,1,0:T(8,128)(2,1)} %collective-permute-done.3.other_ref), custom_call_target="tpu_custom_call" | custom-call | flops 10000000 | bytes 15000000 | tf_op jit(solution)/shard_map/pallas_call | solution.py:505
  (112 shorter events, 46.2 us)
Async XLA Ops:
  2.0 2.0 copy-start.4
  7.6 21.7 %copy-start.27 = (bf16[128,768]{1,0:T(8,128)(2,1)}, bf16[128,768]{1,0:T(8,128)(2,1)S(1)}, u32[]{:S(2)}) copy-start(bf16[128,768]{1,0:T(8,128)(2,1)S(1)} %get-tuple-element.41.normed_ref) | copy-start | bytes 589828
  7.6 21.7 %copy-start.35 = (s32[2,32]{1,0:T(2,128)S(1)}, s32[2,32]{1,0:T(2,128)}, u32[]{:S(2)}) copy-start(s32[2,32]{1,0:T(2,128)} %scene_ref.3) | copy-start | bytes 772
  25.6 3.8 %collective-permute-start = (bf16[8,128,384]{2,1,0:T(8,128)(2,1)S(1)}, bf16[8,128,384]{2,1,0:T(8,128)(2,1)S(1)}, u32[]{:S(2)}, u32[]{:S(2)}) collective-permute-start(bf16[8,128,384]{2,1,0:T(8,128)(2,1)S(1)} %all_to_all.60.same_ref.kvs_ref), channel_id=1, source_target_pairs={{0,8},{8,0},{1,9},{9,1},{2,10},{10,2},{3,11},{11,3},{4,12},{12,4},... | collective-permute-start | bytes 2359304 | tf_op jit(solution)/shard_map/ppermute | solution.py:410
  29.4 11.7 %copy-start.42 = (f32[768]{0:T(1024)S(1)}, f32[768]{0:T(1024)}, u32[]{:S(2)}) copy-start(f32[768]{0:T(1024)} %param.17) | copy-start | bytes 9220
  29.4 11.8 %copy-start.43 = (f32[768]{0:T(1024)S(1)}, f32[768]{0:T(1024)}, u32[]{:S(2)}) copy-start(f32[768]{0:T(1024)} %param.18) | copy-start | bytes 9220
  33.9 18.0 %all-to-all-start.2 = ((bf16[8,128,256]{2,1,0:T(8,128)(2,1)}), bf16[8,128,256]{2,1,0:T(8,128)(2,1)S(1)}, u32[]{:S(2)}, u32[]{:S(2)}) async-start(bf16[8,128,256]{2,1,0:T(8,128)(2,1)} %shard_map.187), calls=%async_computation.2 | async-start | bytes 1048576 | tf_op jit(solution)/shard_map/all_to_all | solution.py:406
  41.1 10.7 %copy-start.20 = (bf16[2,128,768]{2,1,0:T(8,128)(2,1)S(1)}, bf16[2,128,768]{2,1,0:T(8,128)(2,1)}, u32[]{:S(2)}) copy-start(bf16[2,128,768]{2,1,0:T(8,128)(2,1)} %og_ref.5) | copy-start | bytes 1179652
  41.1 10.7 %copy-start.24 = (bf16[2,128,768]{2,1,0:T(8,128)(2,1)S(1)}, bf16[2,128,768]{2,1,0:T(8,128)(2,1)}, u32[]{:S(2)}) copy-start(bf16[2,128,768]{2,1,0:T(8,128)(2,1)} %tok_ref.5) | copy-start | bytes 1179652
  59.1 16.1 %copy-start.36 = (bf16[256,768]{1,0:T(8,128)(2,1)}, bf16[256,768]{1,0:T(8,128)(2,1)S(1)}, u32[]{:S(2)}) copy-start(bf16[256,768]{1,0:T(8,128)(2,1)S(1)} %get-tuple-element.54.normed_ref) | copy-start | bytes 1179652
  59.1 16.1 %all-to-all-start.3 = ((bf16[8,64,768]{2,1,0:T(8,128)(2,1)}), bf16[8,64,768]{2,1,0:T(8,128)(2,1)S(1)}, u32[]{:S(2)}, u32[]{:S(2)}) async-start(bf16[8,64,768]{2,1,0:T(8,128)(2,1)} %copy-done.16), calls=%async_computation.3 | async-start | bytes 1572864 | tf_op jit(solution)/shard_map/all_to_all | solution.py:406
  75.2 11.0 %all-to-all-start.1 = ((bf16[8,128,256]{2,1,0:T(8,128)(2,1)}), bf16[8,128,256]{2,1,0:T(8,128)(2,1)S(1)}, u32[]{:S(2)}, u32[]{:S(2)}) async-start(bf16[8,128,256]{2,1,0:T(8,128)(2,1)} %get-tuple-element.37.q_ref), calls=%async_computation.1 | async-start | bytes 1048576 | tf_op jit(solution)/shard_map/all_to_all | solution.py:406
  86.3 13.5 %all-to-all-start.4 = ((bf16[32,32,256]{2,1,0:T(8,128)(2,1)}), bf16[32,32,256]{2,1,0:T(8,128)(2,1)S(1)}, u32[]{:S(2)}, u32[]{:S(2)}) async-start(bf16[32,32,256]{2,1,0:T(8,128)(2,1)} %copy-done.19), calls=%async_computation.4 | async-start | bytes 1048576 | tf_op jit(solution)/shard_map/all_to_all | solution.py:406
  90.2 18.1 %collective-permute-start.1 = (bf16[8,128,256]{2,1,0:T(8,128)(2,1)S(1)}, bf16[8,128,256]{2,1,0:T(8,128)(2,1)S(1)}, u32[]{:S(2)}, u32[]{:S(2)}) collective-permute-start(bf16[8,128,256]{2,1,0:T(8,128)(2,1)S(1)} %all-to-all-done.1.qs_ref), channel_id=1, source_target_pairs={{0,8},{8,0},{1,9},{9,1},{2,10},{10,2},{3,11},{11,3},{4,12},{12,4},... | collective-permute-start | bytes 1572872 | tf_op jit(solution)/shard_map/ppermute | solution.py:410
  99.7 8.5 %copy-start.17 = (bf16[32,32,256]{2,1,0:T(8,128)(2,1)}, bf16[32,32,256]{2,1,0:T(8,128)(2,1)S(1)}, u32[]{:S(2)}) copy-start(bf16[32,32,256]{2,1,0:T(8,128)(2,1)S(1)} %all-to-all-done.4) | copy-start | bytes 1572868
  99.7 9.3 %collective-permute-start.2 = (bf16[8,128,256]{2,1,0:T(8,128)(2,1)S(1)}, bf16[8,128,256]{2,1,0:T(8,128)(2,1)}, u32[]{:S(2)}, u32[]{:S(2)}) collective-permute-start(bf16[8,128,256]{2,1,0:T(8,128)(2,1)S(1)} %bitcast.6), channel_id=1, source_target_pairs={{0,8},{8,0},{1,9},{9,1},{2,10},{10,2},{3,11},{11,3},{4,12},{12,4},... | collective-permute-start | bytes 1572872 | tf_op jit(solution)/shard_map/ppermute | solution.py:410
  104.7 20.2 %all-to-all-start.5 = ((bf16[8,80,768]{2,1,0:T(8,128)(2,1)}), bf16[8,80,768]{2,1,0:T(8,128)(2,1)S(1)}, u32[]{:S(2)}, u32[]{:S(2)}) async-start(bf16[8,80,768]{2,1,0:T(8,128)(2,1)} %copy-done.11), calls=%async_computation.5 | async-start | bytes 1966080 | tf_op jit(solution)/shard_map/all_to_all | solution.py:406
  115.6 11.0 %copy-start.1 = (bf16[8,128,576]{2,1,0:T(8,128)(2,1)}, bf16[8,128,576]{2,1,0:T(8,128)(2,1)S(1)}, u32[]{:S(2)}) copy-start(bf16[8,128,576]{2,1,0:T(8,128)(2,1)S(1)} %shard_map.190.gqkv_ref) | copy-start | bytes 3538948
  124.8 1.8 copy-start.2
  152.0 4.9 %copy-start.22 = (bf16[2,128,768]{2,1,0:T(8,128)(2,1)S(1)}, bf16[2,128,768]{2,1,0:T(8,128)(2,1)}, u32[]{:S(2)}) copy-start(bf16[2,128,768]{2,1,0:T(8,128)(2,1)} %og_ref.5) | copy-start | bytes 1179652
  152.0 4.9 %copy-start.37 = (bf16[256,768]{1,0:T(8,128)(2,1)S(1)}, bf16[256,768]{1,0:T(8,128)(2,1)}, u32[]{:S(2)}) copy-start(bf16[256,768]{1,0:T(8,128)(2,1)} %copy-done.36) | copy-start | bytes 1179652
  152.0 4.9 %copy-start.39 = (bf16[256,384]{1,0:T(8,128)(2,1)S(1)}, bf16[256,384]{1,0:T(8,128)(2,1)}, u32[]{:S(2)}) copy-start(bf16[256,384]{1,0:T(8,128)(2,1)} %copy-done.38) | copy-start | bytes 589828
  152.0 4.9 %copy-start.41 = (bf16[256,384]{1,0:T(8,128)(2,1)S(1)}, bf16[256,384]{1,0:T(8,128)(2,1)}, u32[]{:S(2)}) copy-start(bf16[256,384]{1,0:T(8,128)(2,1)} %copy-done.40) | copy-start | bytes 589828
  152.0 35.2 %all-to-all-start.8 = ((bf16[64,48,384]{2,1,0:T(8,128)(2,1)}), bf16[64,48,384]{2,1,0:T(8,128)(2,1)S(1)}, u32[]{:S(2)}, u32[]{:S(2)}) async-start(bf16[64,48,384]{2,1,0:T(8,128)(2,1)} %copy-done), calls=%async_computation.8 | async-start | bytes 4718592 | tf_op jit(solution)/shard_map/all_to_all | solution.py:406
  187.2 23.8 %all-to-all-start.10 = ((bf16[16,48,768]{2,1,0:T(8,128)(2,1)}), bf16[16,48,768]{2,1,0:T(8,128)(2,1)S(1)}, u32[]{:S(2)}, u32[]{:S(2)}) async-start(bf16[16,48,768]{2,1,0:T(8,128)(2,1)} %copy-done.10), calls=%async_computation.10 | async-start | bytes 2359296 | tf_op jit(solution)/shard_map/all_to_all | solution.py:406
  193.6 81.1 %collective-permute-start.3 = (bf16[8,8,48,384]{3,2,1,0:T(8,128)(2,1)S(1)}, bf16[8,8,48,384]{3,2,1,0:T(8,128)(2,1)}, u32[]{:S(2)}, u32[]{:S(2)}) collective-permute-start(bf16[8,8,48,384]{3,2,1,0:T(8,128)(2,1)S(1)} %bitcast.4), channel_id=1, source_target_pairs={{0,8},{8,0},{1,9},{9,1},{2,10},{10,2},{3,11},{11,3},{4,12},{12,4},... | collective-permute-start | bytes 7077896 | tf_op jit(solution)/shard_map/ppermute | solution.py:410
  211.9 13.3 %all-to-all-start.11 = ((bf16[8,48,768]{2,1,0:T(8,128)(2,1)}), bf16[8,48,768]{2,1,0:T(8,128)(2,1)S(1)}, u32[]{:S(2)}, u32[]{:S(2)}) async-start(bf16[8,48,768]{2,1,0:T(8,128)(2,1)} %copy-done.6), calls=%async_computation.11 | async-start | bytes 1179648 | tf_op jit(solution)/shard_map/all_to_all | solution.py:406
  226.1 20.7 %all-to-all-start.6 = ((bf16[8,128,576]{1,2,0:T(8,128)(2,1)}), bf16[8,128,576]{1,2,0:T(8,128)(2,1)}, u32[]{:S(2)}, u32[]{:S(2)}) async-start(bf16[8,128,576]{1,2,0:T(8,128)(2,1)} %copy.21), calls=%async_computation.6 | async-start | bytes 2359296 | tf_op jit(solution)/shard_map/all_to_all | solution.py:406
  230.4 18.9 %copy-start.3 = (bf16[8,80,768]{2,1,0:T(8,128)(2,1)S(1)}, bf16[8,80,768]{2,1,0:T(8,128)(2,1)}, u32[]{:S(2)}) copy-start(bf16[8,80,768]{2,1,0:T(8,128)(2,1)} %copy-done.2) | copy-start | bytes 2949124
  230.4 33.4 %collective-permute-start.4 = (bf16[8,48,768]{2,1,0:T(8,128)(2,1)}, bf16[8,48,768]{2,1,0:T(8,128)(2,1)}, u32[]{:S(2)}, u32[]{:S(2)}) collective-permute-start(bf16[8,48,768]{2,1,0:T(8,128)(2,1)} %copy-done.7), channel_id=1, source_target_pairs={{0,8},{8,0},{1,9},{9,1},{2,10},{10,2},{3,11},{11,3},{4,12},{12,4},... | collective-permute-start | bytes 1769480 | tf_op jit(solution)/shard_map/ppermute | solution.py:410
  249.2 2.0 copy-start.5
  257.0 15.2 %all-to-all-start.9 = ((f32[16,8,768]{2,1,0:T(8,128)}), f32[16,8,768]{2,1,0:T(8,128)S(1)}, u32[]{:S(2)}, u32[]{:S(2)}) async-start(f32[16,8,768]{2,1,0:T(8,128)} %copy-done.26), calls=%async_computation.9 | async-start | bytes 786432 | tf_op jit(solution)/shard_map/all_to_all | solution.py:406
  (27 other events, 26.3 us)

commit v2 on v1

v2 whole, which is shorter than its diff:
```python
import functools

import jax
import jax.numpy as jnp
from jax import lax
from jax.experimental import pallas as pl
from jax.experimental.pallas import tpu as pltpu
from jax.sharding import Mesh
from jax.sharding import PartitionSpec as P

D = 768
HD = 64
FFL = 384
TOK = 128
BLK = 32
EPS = 1e-05
BF = jnp.bfloat16
F32 = jnp.float32

CHIP = ("y", "xl")
CORE = "c"
MICRO = "zh"
GROUP = ("zl", "xh")
NARROW = (MICRO, *GROUP)
WIDE = (*CHIP, CORE)


def chip_index():
    return lax.axis_index("y") * 2 + lax.axis_index("xl")


def group_index():
    return lax.axis_index("zl") * 2 + lax.axis_index("xh")


def mm(left, right):
    return lax.dot_general(left, right, (((1,), (0,)), ((), ())), preferred_element_type=F32)


def mm_nt(left, right):
    return lax.dot_general(left, right, (((1,), (1,)), ((), ())), preferred_element_type=F32)


def mm_tn(left, right):
    return lax.dot_general(left, right, (((0,), (0,)), ((), ())), preferred_element_type=F32)


def normalized(values):
    center = values - jnp.mean(values, axis=-1, keepdims=True)
    spread = jnp.mean(center * center, axis=-1, keepdims=True)
    inverse = lax.rsqrt(spread + EPS)
    return center * inverse, inverse


def norm_back(grad, unit, inverse, gain):
    scaled = grad * gain
    first = jnp.mean(scaled, axis=-1, keepdims=True)
    second = jnp.mean(scaled * unit, axis=-1, keepdims=True)
    return inverse * (scaled - first - unit * second)


def halves(block):
    lane = lax.broadcasted_iota(jnp.int32, block.shape, 1)
    zero = jnp.zeros_like(block)
    return jnp.where(lane < HD, block, zero), jnp.where(lane < HD, zero, block)


def join(low, high):
    lane = lax.broadcasted_iota(jnp.int32, low.shape, 1)
    return jnp.where(lane < HD, low, high)


def span(scene_ref):
    micro = lax.axis_index(MICRO)
    own = scene_ref[micro, chip_index() * 4]
    first = jnp.int32(0)
    count = jnp.int32(0)
    for index in range(8):
        other = scene_ref[micro, index * 4]
        first += (other < own).astype(jnp.int32)
        count += (other == own).astype(jnp.int32)
    return first, count > 1


def three(value):
    a = value.astype(BF).astype(F32)
    b = (value - a).astype(BF).astype(F32)
    c = value - a - b
    return a, b, c


def put_columns(width, rows, start, columns):
    lane = lax.broadcasted_iota(jnp.int32, (rows, width), 1)
    out = jnp.zeros((rows, width), F32)
    for offset, column in enumerate(columns):
        out = jnp.where(lane == start + offset, column, out)
    return out


def call(kernel, outs, ins, cost, scratch=(), vmem=16, aliases=None):
    places = {"V": pltpu.VMEM, "H": pltpu.HBM, "S": pltpu.SMEM}
    return pl.pallas_call(
        kernel,
        out_shape=[jax.ShapeDtypeStruct(shape, dtype) for shape, dtype, _ in outs],
        in_specs=[pl.BlockSpec(memory_space=places[place]) for _, place in ins],
        out_specs=[pl.BlockSpec(memory_space=places[place]) for _, _, place in outs],
        scratch_shapes=list(scratch),
        input_output_aliases=aliases or {},
        cost_estimate=pl.CostEstimate(flops=cost, bytes_accessed=2000000, transcendentals=0),
        compiler_params=pltpu.CompilerParams(vmem_limit_bytes=vmem * 2**20),
    )(*[value for value, _ in ins])


DMA = pltpu.SemaphoreType.DMA


def send_copies(source, target, indices, sem):
    copies = [pltpu.make_async_copy(source, target.at[index], sem.at[index]) for index in indices]
    for copy in copies:
        copy.start()
    return copies


def wait_all(copies):
    for copy in copies:
        copy.wait()


def weight_copies(w_ref, w_buf, w_sem):
    group = group_index()
    copies = []
    for slot, part in enumerate((1, 2, 0)):
        column = pl.multiple_of(part * D + (group // 2) * 384, 128)
        copy = pltpu.make_async_copy(w_ref.at[:, pl.ds(column, 384)], w_buf.at[slot], w_sem.at[slot])
        copy.start()
        copies.append(copy)
    return copies


def project_kernel(
    tok_ref, gain_ref, shift_ref, w_ref, kv_ref, q_ref, normed_ref, x_buf, w_buf, kv_buf, x_sem, w_sem, kv_sem
):
    copy_x = pltpu.make_async_copy(tok_ref.at[lax.axis_index(MICRO)], x_buf, x_sem)
    copy_x.start()
    copies = weight_copies(w_ref, w_buf, w_sem)
    copy_x.wait()
    unit, _ = normalized(x_buf[...].astype(F32))
    normed = (unit * gain_ref[...].reshape(1, D) + shift_ref[...].reshape(1, D)).astype(BF)
    odd = (group_index() % 2) == 1

    def part(slot):
        copies[slot].wait()
        full = mm(normed, w_buf[slot])
        return jnp.where(odd, full[:, 192:], full[:, :192]).astype(BF)

    kv_buf[...] = jnp.concatenate([part(0), part(1)], axis=1)
    sends = send_copies(kv_buf, kv_ref, range(8), kv_sem)
    normed_ref[...] = normed
    q_ref[...] = jnp.concatenate([part(2), jnp.zeros((TOK, HD), BF)], axis=1)
    wait_all(sends)


def attend_kernel(scene_ref, q_ref, same_ref, other_ref, out_ref, buf, sem):
    first, big = span(scene_ref)

    def run(count):
        rows = count * TOK
        keys = jnp.concatenate(
            [ref[pl.ds(first, count)].reshape(rows, 384) for ref in (same_ref, other_ref)], axis=0
        )
        query = q_ref[...]
        q0, q1 = halves(query[:, :128])
        blocks = [keys[:, :128], keys[:, 128:256], keys[:, 256:]]
        mixed = []
        columns = []
        for qh, kb, vb in ((q0, 0, 1), (q1, 0, 2), (query[:, 128:], 1, 2)):
            scores = mm_nt(qh, blocks[kb]) * (HD**-0.5)
            top = jnp.max(scores, axis=-1, keepdims=True)
            weights = jnp.exp(scores - top)
            total = jnp.sum(weights, axis=-1, keepdims=True)
            probs = (weights * (1.0 / total)).astype(BF)
            mixed.append(mm(probs, blocks[vb]))
            columns += three(top + jnp.log(total))
        stats = put_columns(128, TOK, 0, columns)
        buf[...] = jnp.concatenate([join(stats, mixed[0]), join(mixed[1], mixed[2])], axis=1).astype(BF)

    @pl.when(big)
    def _():
        run(5)

    @pl.when(jnp.logical_not(big))
    def _():
        run(1)

    wait_all(send_copies(buf, out_ref, range(8), sem))


def forward_kernel(
    mixed_ref, tok_ref, og_ref, wo_ref, gain_ref, shift_ref, up_ref, down_ref,
    out_ref, middle_ref, normed_ref, act_ref, gpre_ref, grad_buf, branch_buf, sem,
):
    total = tok_ref[...].reshape(2 * TOK, D).astype(F32)
    for group in range(4):
        rows = jnp.concatenate([mixed_ref[group], mixed_ref[4 + group]], axis=0)
        total = total + mm(rows, wo_ref[group])
    middle_ref[...] = total.reshape(8, BLK, D)
    unit, _ = normalized(total)
    normed = (unit * gain_ref[...].reshape(1, D) + shift_ref[...].reshape(1, D)).astype(BF)
    normed_ref[...] = normed
    pre = mm(normed, up_ref[...])
    cdf = 0.5 * (1.0 + lax.erf(pre * (0.5**0.5)))
    slope = cdf + pre * jnp.exp(-0.5 * pre * pre) * 0.3989422804014327
    grad_out = og_ref[...].reshape(2 * TOK, D)
    gpre = (mm_nt(grad_out, down_ref[...]) * slope).astype(BF)
    gpre_ref[...] = gpre
    grad_buf[...] = mm_nt(gpre, up_ref[...]).astype(BF).reshape(8, BLK, D)
    first = pltpu.make_async_copy(grad_buf, out_ref.at[:, pl.ds(BLK, BLK)], sem.at[0])
    first.start()
    act = (pre * cdf).astype(BF)
    act_ref[...] = act
    branch_buf[...] = mm(act, down_ref[...]).astype(BF).reshape(8, BLK, D)
    second = pltpu.make_async_copy(branch_buf, out_ref.at[:, pl.ds(0, BLK)], sem.at[1])
    second.start()
    first.wait()
    second.wait()


def ff_grads_kernel(normed_ref, act_ref, gpre_ref, og_ref, out_ref):
    up = mm_tn(normed_ref[...], gpre_ref[...]).astype(BF)
    grad_out = og_ref[...].reshape(2 * TOK, D)
    down = mm_tn(act_ref[...], grad_out).astype(BF)
    out_ref[:, :384] = up
    for tile in range(16):
        half = (tile % 2) * 384
        out_ref[tile * 48:(tile + 1) * 48, 384:] = down[
            (tile // 2) * 48:(tile // 2 + 1) * 48, half:half + 384
        ]


def middle_kernel(
    sums_ref, middle_ref, og_ref, mixed_ref, wo_ref, gain_ref,
    out_ref, low_ref, grad_ref, result_ref, vec_ref, buf, sem,
):
    micro = lax.axis_index(MICRO)
    group = group_index()
    start = pl.multiple_of(group * BLK, BLK)
    total = sums_ref[0].astype(F32)
    for index in range(1, 8):
        total = total + sums_ref[index].astype(F32)
    branch, grad = total[:BLK], total[BLK:]
    middle = middle_ref[micro * 4 + group]
    unit, inverse = normalized(middle)
    grad_mid = og_ref[micro, pl.ds(start, BLK)].astype(F32) + norm_back(
        grad, unit, inverse, gain_ref[...].reshape(1, D)
    )
    low = grad_mid.astype(BF)
    lane = lax.broadcasted_iota(jnp.int32, (BLK, 256), 1)
    sends = []
    for head_group in range(4):
        mixed = mixed_ref[micro * 4 + head_group, pl.ds(start, BLK)].astype(F32)
        back = mm_nt(low, wo_ref[head_group]).astype(BF).astype(F32)
        product = mixed * back
        columns = []
        for head in range(3):
            inside = (lane >= (head + 1) * HD) & (lane < (head + 2) * HD)
            columns += three(jnp.sum(jnp.where(inside, product, 0.0), axis=-1, keepdims=True))
        stats = put_columns(256, BLK, 9, columns)
        buf[head_group] = jnp.where(lane < 9, mixed, jnp.where(lane < HD, stats, back)).astype(BF)
        sends += send_copies(
            buf.at[head_group], out_ref, [chip * 4 + head_group for chip in range(8)], sem
        )
    low_ref[...] = low
    grad_ref[...] = grad_mid
    result_ref[...] = (middle + branch).astype(BF)
    gain_grad = jnp.sum(grad * unit, axis=0, keepdims=True)
    shift_grad = jnp.sum(grad, axis=0, keepdims=True)
    vec_ref[...] = jnp.concatenate([gain_grad, shift_grad, jnp.zeros((6, D), F32)], axis=0)
    wait_all(sends)


def attend_back_kernel(
    scene_ref, kvs_ref, kvo_ref, q_ref, gs_ref, go_ref, normed_ref, mixed_ref, low0_ref, low1_ref, low2_ref,
    low3_ref, gqkv_ref, keep_ref, send_ref, grad_buf,
):
    first, big = span(scene_ref)
    chip = chip_index()
    core = lax.axis_index(CORE)
    group = group_index()
    scale = HD**-0.5

    def run(count):
        rows = count * TOK

        def cut(value):
            return [value[:, at:at + 128] for at in range(0, value.shape[1], 128)]

        def gathered(one, two, width):
            return cut(jnp.concatenate(
                [ref[pl.ds(first, count)].reshape(rows, width) for ref in (one, two)], axis=0
            ))

        kv = gathered(kvs_ref, kvo_ref, 384)
        grad = gathered(gs_ref, go_ref, 256)
        query = cut(jnp.concatenate(
            [q_ref[pl.ds(first, count), which].reshape(rows, 256) for which in (core, 1 - core)], axis=0
        ))
        kv_own = cut(kvs_ref[chip])
        q_own = cut(q_ref[chip, core])
        g_own = cut(gs_ref[chip])
        q_heads = [*halves(q_own[0]), q_own[1]]
        g_heads = [halves(g_own[0])[1], *halves(g_own[1])]
        k_heads = [*halves(kv_own[0]), halves(kv_own[1])[0]]
        v_heads = [halves(kv_own[1])[1], *halves(kv_own[2])]
        own_stats = g_own[0].astype(F32)
        all_stats = grad[0].astype(F32).T

        def column(at):
            return own_stats[:, at:at + 1] + own_stats[:, at + 1:at + 2] + own_stats[:, at + 2:at + 3]

        def row(at):
            return all_stats[at:at + 1] + all_stats[at + 1:at + 2] + all_stats[at + 2:at + 3]

        dq, dk, dv = [], [], []
        for head, (kb, vb) in enumerate(((0, 1), (0, 2), (1, 2))):
            qb, gb = (0, 0, 1)[head], (0, 1, 1)[head]
            probs = jnp.exp(mm_nt(q_heads[head], kv[kb]) * scale - column(3 * head))
            gap = mm_nt(g_heads[head], kv[vb]) - column(9 + 3 * head)
            dq.append(mm((probs * gap).astype(BF), kv[kb]) * scale)
            probs = jnp.exp(mm_nt(k_heads[head], query[qb]) * scale - row(3 * head))
            gap = mm_nt(v_heads[head], grad[gb]) - row(9 + 3 * head)
            dv.append(mm(probs.astype(BF), grad[gb]))
            dk.append(mm((probs * gap).astype(BF), query[qb]) * scale)
        tail = dq[2]
        gqkv_ref[...] = jnp.concatenate(
            [join(dk[0], dk[1]), join(dk[2], dv[0]), join(dv[1], dv[2]), join(dq[0], dq[1]),
             join(tail, jnp.zeros_like(tail))],
            axis=1,
        ).astype(BF)

    @pl.when(big)
    def _():
        run(5)

    @pl.when(jnp.logical_not(big))
    def _():
        run(1)

    grad_buf[...] = mm_tn(normed_ref[...], gqkv_ref[...])
    index = lax.axis_index(MICRO) * 4 + group
    low = jnp.concatenate([ref[...] for ref in (low0_ref, low1_ref, low2_ref, low3_ref)], axis=0)
    mixed = jnp.concatenate(
        [mixed_ref[index, pl.ds(pl.multiple_of((group ^ k) * BLK, BLK), BLK)] for k in range(4)], axis=0
    )
    out = mm_tn(mixed, low)[HD:]
    for ref, owner in ((keep_ref, core), (send_ref, 1 - core)):
        for tile in range(8):
            rows = grad_buf[pl.ds(pl.multiple_of((2 * tile + owner) * 48, 16), 48)]
            at = (tile // 4) * 96
            pieces = [
                out[at + row * 48:at + (row + 1) * 48, (tile % 4) * 192:(tile % 4 + 1) * 192] for row in range(2)
            ]
            ref[2 * tile] = rows[:, :384].astype(BF)
            ref[2 * tile + 1] = jnp.concatenate(
                [rows[:, 384:576], jnp.where(owner == 1, pieces[1], pieces[0])], axis=1
            ).astype(BF)


def add_kernel(one_ref, two_ref, out_ref, buf, sem):
    buf[...] = (one_ref[...].astype(F32) + two_ref[...].astype(F32)).astype(BF)
    copy = pltpu.make_async_copy(buf, out_ref, sem)
    copy.start()
    copy.wait()


def sum_kernel(in_ref, out_ref, buf, sem):
    total = in_ref[0].astype(F32)
    for index in range(1, 16):
        total = total + in_ref[index].astype(F32)
    buf[...] = total.astype(BF)
    wait_all(send_copies(buf, out_ref, range(64), sem))


def spread_kernel(turn, in_ref, *refs):
    qkv_ref, out_ref, qkv_buf, out_buf, sem, out_sem = refs[-6:]
    owner = lax.axis_index(CORE)
    owner = 1 - owner if turn else owner
    copies = []
    for tile in range(8):
        block = [in_ref[tile, index].astype(F32) for index in range(8)]
        for part, half, at in ((1, 0, 0), (2, 0, 192), (0, 4, 0)):
            qkv_buf[tile, :, part * D:(part + 1) * D] = jnp.concatenate(
                [block[half + group][:, at:at + 192] for group in range(4)], axis=1
            )
        start = pl.multiple_of((2 * tile + owner) * 48, 16)
        copy = pltpu.make_async_copy(qkv_buf.at[tile], qkv_ref.at[pl.ds(start, 48)], sem.at[tile])
        copy.start()
        copies.append(copy)
        for group in range(4):
            out_buf[group, tile // 4, :, (tile % 4) * 192:(tile % 4 + 1) * 192] = block[4 + group][:, 192:]
    for group in range(4):
        for pair in range(2):
            start = pl.multiple_of(group * 192 + (pair * 2 + owner) * 48, 16)
            copy = pltpu.make_async_copy(
                out_buf.at[group, pair], out_ref.at[pl.ds(start, 48)], out_sem.at[group, pair]
            )
            copy.start()
            copies.append(copy)
    wait_all(copies)


def spread_ff_kernel(in_ref, up_ref, down_ref):
    up_ref[...] = in_ref[:, :384].astype(F32)
    for tile in range(16):
        half = (tile % 2) * 384
        down_ref[(tile // 2) * 48:(tile // 2 + 1) * 48, half:half + 384] = in_ref[
            tile * 48:(tile + 1) * 48, 384:
        ].astype(F32)


def normed_grad_kernel(gqkv_ref, w_ref, own_ref, one_ref, two_ref, three_ref, w_buf, buf, w_sem):
    copies = weight_copies(w_ref, w_buf, w_sem)
    group = group_index()
    odd = (group % 2) == 1
    total = jnp.zeros((TOK, D), F32)
    for slot in range(3):
        copies[slot].wait()
        part = gqkv_ref[:, slot * 192:(slot + 1) * 192]
        zero = jnp.zeros_like(part)
        wide = jnp.where(
            odd, jnp.concatenate([zero, part], axis=1), jnp.concatenate([part, zero], axis=1)
        )
        total = total + mm_nt(wide, w_buf[slot])
    buf[...] = total
    own_ref[...] = buf[pl.ds(pl.multiple_of(group * BLK, BLK), BLK)]
    for k, ref in ((1, one_ref), (2, two_ref), (3, three_ref)):
        ref[...] = buf[pl.ds(pl.multiple_of((group ^ k) * BLK, BLK), BLK)].astype(BF)


def input_kernel(
    own_ref, one_ref, two_ref, three_ref, tok_ref, gain_ref, grad_ref, result_ref, vec_ref, out_ref, x_buf, sem
):
    start = pl.multiple_of(group_index() * BLK, BLK)
    copy = pltpu.make_async_copy(tok_ref.at[lax.axis_index(MICRO), pl.ds(start, BLK)], x_buf, sem)
    copy.start()
    total = own_ref[...]
    for ref in (one_ref, two_ref, three_ref):
        total = total + ref[...].astype(F32)
    copy.wait()
    unit, inverse = normalized(x_buf[...].astype(F32))
    grad = grad_ref[...] + norm_back(total, unit, inverse, gain_ref[...].reshape(1, D))
    gain1 = jnp.sum(total * unit, axis=0, keepdims=True)
    shift1 = jnp.sum(total, axis=0, keepdims=True)
    vectors = jnp.concatenate([gain1, shift1, vec_ref[...][:2], jnp.zeros((12, D), F32)], axis=0)
    out_ref[:BLK] = grad.astype(BF)
    out_ref[BLK:2 * BLK] = result_ref[...]
    out_ref[2 * BLK:] = vectors.astype(BF)


def unpack_kernel(*refs):
    parts, (grad_ref, result_ref, vec_ref) = refs[:8], refs[8:]
    micro = lax.axis_index(MICRO)
    group = group_index()
    total = jnp.zeros((16, D), F32)
    for k, ref in enumerate(parts):
        rows = pl.ds(pl.multiple_of((group ^ (k % 4)) * BLK, BLK), BLK)
        where = micro ^ (k // 4)
        grad_ref[where, rows] = ref[:BLK].astype(F32)
        result_ref[where, rows] = ref[BLK:2 * BLK]
        total = total + ref[2 * BLK:].astype(F32)
    vec_ref[...] = total[:8]


def exchange(value, axes):
    return lax.all_to_all(value, axes, 0, 0, tiled=True)


def swap(value):
    return lax.ppermute(value, CORE, [(0, 1), (1, 0)])


def flip(value, axes, count, bits):
    return lax.ppermute(value, axes, [(index, index ^ bits) for index in range(count)])


def shards(
    tokens, scene_of_block, ln1_gain, ln1_shift, w_qkv, w_out, ln2_gain, ln2_shift, w_up, w_down, out_grad
):
    w_out_pad = jnp.pad(w_out.reshape(4, 192, D), ((0, 0), (HD, 0), (0, 0)))
    kv_send, query, normed = call(
        project_kernel,
        [((8, TOK, 384), BF, "H"), ((TOK, 256), BF, "V"), ((TOK, D), BF, "V")],
        [(tokens, "H"), (ln1_gain, "V"), (ln1_shift, "V"), (w_qkv, "H")],
        10**9,
        [
            pltpu.VMEM((TOK, D), BF), pltpu.VMEM((3, D, 384), BF), pltpu.VMEM((TOK, 384), BF),
            DMA, DMA((3,)), DMA((8,)),
        ],
    )
    kv_same = exchange(kv_send, CHIP)
    kv_other = swap(kv_same)
    (mixed_send,) = call(
        attend_kernel,
        [((8, TOK, 256), BF, "H")],
        [(scene_of_block, "S"), (query, "V"), (kv_same, "V"), (kv_other, "V")],
        2 * 10**9,
        [pltpu.VMEM((TOK, 256), BF), DMA((8,))],
    )
    mixed = exchange(mixed_send, NARROW)
    query, _ = lax.optimization_barrier((query, kv_same))
    queries = lax.all_gather(query, WIDE, axis=0, tiled=True).reshape(8, 2, TOK, 256)
    ff_send, middle, normed2, act, grad_pre = call(
        forward_kernel,
        [
            ((8, 2 * BLK, D), BF, "H"), ((8, BLK, D), F32, "V"), ((2 * TOK, D), BF, "V"),
            ((2 * TOK, FFL), BF, "V"), ((2 * TOK, FFL), BF, "V"),
        ],
        [
            (mixed, "V"), (tokens, "V"), (out_grad, "V"), (w_out_pad, "V"), (ln2_gain, "V"), (ln2_shift, "V"),
            (w_up, "V"), (w_down, "V"),
        ],
        4 * 10**9,
        [pltpu.VMEM((8, BLK, D), BF), pltpu.VMEM((8, BLK, D), BF), DMA((2,))],
    )
    ff_sums = exchange(ff_send, NARROW)
    (ff_grads,) = call(
        ff_grads_kernel,
        [((D, D), BF, "V")],
        [(normed2, "V"), (act, "V"), (grad_pre, "V"), (out_grad, "V")],
        2 * 10**9,
    )
    ff_part = lax.psum_scatter(ff_grads, WIDE, scatter_dimension=0, tiled=True)
    ff_all = lax.all_gather(ff_part, WIDE, axis=0, tiled=True)
    grad_send, low, grad_mid, result_part, vec2 = call(
        middle_kernel,
        [
            ((32, BLK, 256), BF, "H"), ((BLK, D), BF, "V"), ((BLK, D), F32, "V"), ((BLK, D), BF, "V"),
            ((8, D), F32, "V"),
        ],
        [(ff_sums, "V"), (middle, "V"), (out_grad, "V"), (mixed, "V"), (w_out_pad, "V"), (ln2_gain, "V")],
        10**9,
        [pltpu.VMEM((4, BLK, 256), BF), DMA((32,))],
    )
    grad_same = exchange(grad_send, (*CHIP, *GROUP)).reshape(8, TOK, 256)
    lows = [low] + [flip(low, GROUP, 4, k) for k in (1, 2, 3)]
    grad_other = swap(grad_same)
    gqkv, keep, send = call(
        attend_back_kernel,
        [((TOK, 640), BF, "V"), ((16, 48, 384), BF, "V"), ((16, 48, 384), BF, "V")],
        [
            (scene_of_block, "S"), (kv_same, "V"), (kv_other, "V"), (queries, "V"), (grad_same, "V"),
            (grad_other, "V"), (normed, "V"), (mixed, "V"), *[(value, "V") for value in lows],
        ],
        8 * 10**9,
        [pltpu.VMEM((D, 640), F32)],
        vmem=24,
    )
    (weight_send,) = call(
        add_kernel,
        [((16, 48, 384), BF, "H")],
        [(keep, "V"), (swap(send), "V")],
        10**8,
        [pltpu.VMEM((16, 48, 384), BF), DMA],
    )
    weight_parts = exchange(weight_send, (*CHIP, MICRO))
    own, *sends = call(
        normed_grad_kernel,
        [((BLK, D), F32, "V")] + [((BLK, D), BF, "V")] * 3,
        [(gqkv, "V"), (w_qkv, "H")],
        10**9,
        [pltpu.VMEM((3, D, 384), BF), pltpu.VMEM((TOK, D), F32), DMA((3,))],
    )
    parts = [flip(value, GROUP, 4, k + 1) for k, value in enumerate(sends)]
    (packed,) = call(
        input_kernel,
        [((80, D), BF, "V")],
        [
            (own, "V"), *[(value, "V") for value in parts], (tokens, "H"), (ln1_gain, "V"), (grad_mid, "V"),
            (result_part, "V"), (vec2, "V"),
        ],
        10**8,
        [pltpu.VMEM((BLK, D), BF), DMA],
    )
    everyone = [packed] + [flip(packed, NARROW, 8, k) for k in range(1, 8)]
    input_grad, result, vectors = call(
        unpack_kernel,
        [((2, TOK, D), F32, "V"), ((2, TOK, D), BF, "V"), ((8, D), F32, "V")],
        [(value, "V") for value in everyone],
        10**8,
    )
    (weight_total,) = call(
        sum_kernel,
        [((64, 48, 384), BF, "H")],
        [(weight_parts, "V")],
        10**8,
        [pltpu.VMEM((48, 384), BF), DMA((64,))],
    )
    weight_same = exchange(weight_total, (*CHIP, *NARROW)).reshape(8, 8, 48, 384)
    weight_other = swap(weight_same)
    vectors = vectors + swap(vectors)
    for bits in (1, 2, 4):
        vectors = vectors + flip(vectors, CHIP, 8, bits)
    up_grad, down_grad = call(
        spread_ff_kernel, [((D, FFL), F32, "V"), ((FFL, D), F32, "V")], [(ff_all, "V")], 10**7
    )
    scratch = [
        pltpu.VMEM((8, 48, 3 * D), F32), pltpu.VMEM((4, 2, 48, D), F32), DMA((8,)), DMA((4, 2)),
    ]
    grads = [((D, 3 * D), F32, "H"), ((D, D), F32, "H")]
    half = call(
        functools.partial(spread_kernel, False), grads, [(weight_same, "V")], 10**8, scratch
    )
    qkv_grad, out_proj_grad = call(
        functools.partial(spread_kernel, True),
        grads,
        [(weight_other, "V"), (half[0], "H"), (half[1], "H")],
        10**8,
        scratch,
        aliases={1: 0, 2: 1},
    )
    return (
        result, input_grad, qkv_grad, out_proj_grad, vectors[0], vectors[1], vectors[2], vectors[3], up_grad,
        down_grad,
    )


def solution(mesh):
    names = ("y", "xl", "c", "zh", "zl", "xh")
    fine = Mesh(mesh.devices.reshape(4, 2, 2, 2, 2, 2), names)
    tokens = P(None, WIDE, None)
    placed = (
        tokens, P(), P(), P(), P(), P(), P(), P(), P(None, NARROW), P(NARROW, None), tokens
    )
    return jax.shard_map(
        shards,
        mesh=fine,
        in_specs=placed,
        out_specs=(
            tokens, tokens, P(), P(), P(), P(), P(), P(), P(None, NARROW), P(NARROW, None)
        ),
        check_vma=False,
    )
```

time: 284 us -> 284 us (level)
  blocking collectives: 41.7 us -> 65.4 us
  waiting for transfers between devices: 114 us -> 95.1 us
  local copies, waits for them, and re-layouts: 37.9 us -> 21.7 us
  between operations: 1.01 us -> 14.1 us
  starting transfers between devices: 60.5 us -> 54.7 us
  Pallas kernels: 24.8 us -> 29.5 us
    all_to_all x10 -> x2, waiting for transfers between devices: 112 us -> 34.6 us  [exchange(): return lax.all_to_all(value, axes, 0, 0, tiled=True)]
    reduce_scatter x0 -> x1, waiting for transfers between devices: none -> 33.9 us  [shards(): ff_part = lax.psum_scatter(ff_grads, WIDE, scatter_dimension=0, tiled=True)]
    all_to_all x10 -> x2, starting transfers between devices: 47.5 us -> 15.7 us  [exchange(): return lax.all_to_all(value, axes, 0, 0, tiled=True)]
    all_to_all x2 -> x4, blocking collectives: 41.7 us -> 65.4 us  [exchange(): return lax.all_to_all(value, axes, 0, 0, tiled=True)]
    ppermute x0 -> x16, waiting for transfers between devices: none -> 22.2 us  [flip(): lax.ppermute(value, axes, [(index, index ^ bits) for index in range(count)])]
    ppermute x0 -> x16, starting transfers between devices: none -> 21.8 us  [flip(): lax.ppermute(value, axes, [(index, index ^ bits) for index in range(count)])]
    pallas_call x12 -> x14, Pallas kernels: 17.5 us -> 29.5 us  [call(): pl.pallas_call(kernel, out_shape=[jax.ShapeDtypeStruct(shape, dtype) for...]
    unnamed x88 -> x72, local copies, waits for them, and re-layouts: 30.3 us -> 19.7 us
  transfers between devices with their start and end apart: 15 -> 26, of which waited for: 11 -> 17; matrix products, arithmetic and copies ran while one was open for 3% -> 1% of each run, Pallas kernels for 3% -> 5%
where the time goes in v2:
time: 284 us; the launch traced here: 281 us
  waiting for transfers between devices  95.1 us (33%)
  blocking collectives  65.4 us (23%)
  starting transfers between devices  54.7 us (19%)
  Pallas kernels  29.5 us (10%)
  local copies, waits for them, and re-layouts  21.7 us (8%)
  between operations  14.1 us (5%)
    all_to_all x4, blocking collectives, exchange(): return lax.all_to_all(value, axes, 0, 0, tiled=True)  65.4 us
    all_to_all x2, waiting for transfers between devices, exchange(): return lax.all_to_all(value, axes, 0, 0, tiled=True)  34.6 us
    reduce_scatter x1, waiting for transfers between devices, shards(): ff_part = lax.psum_scatter(ff_grads, WIDE, scatter_dimension=0, tiled=True)  33.9 us
    pallas_call x14, Pallas kernels, call(): pl.pallas_call(kernel, out_shape=[jax.ShapeDtypeStruct(shape, dtype) for...  29.5 us
    ppermute x16, waiting for transfers between devices, flip(): lax.ppermute(value, axes, [(index, index ^ bits) for index in range(count)])  22.2 us
    ppermute x16, starting transfers between devices, flip(): lax.ppermute(value, axes, [(index, index ^ bits) for index in range(count)])  21.8 us
    unnamed x72, local copies, waits for them, and re-layouts  19.7 us
    ppermute x5, starting transfers between devices, swap(): return lax.ppermute(value, CORE, [(0, 1), (1, 0)])  17.1 us
  transfers between devices with their start and end apart: 26, of which 17 were waited for; matrix products, arithmetic and copies ran while one was open for 1% of the time, Pallas kernels for 5%

profile of v2, /device:TPU:1, one launch (start us, length us, event | category | flops | bytes accessed | tf_op | source)
XLA Modules:
  0.0 280.5 jit_solution(5916792747379575353)
XLA Ops:
  7.2 2.0 copy-done
  11.6 3.5 %shard_map.186 = (bf16[8,128,384]{2,1,0:T(8,128)(2,1)S(1)}, bf16[128,256]{1,0:T(8,128)(2,1)}, bf16[128,768]{1,0:T(8,128)(2,1)S(1)}) custom-call(bf16[2,128,768]{2,1,0:T(8,128)(2,1)S(1)} %copy-done.2, f32[768]{0:T(1024)S(1)} %copy-done.17, f32[768]{0:T(1024)S(1)} %copy-done.20, bf16[768,2304]{1,0:T(8,128)(2,1)S(1)} %copy-done), custom_call_target="tpu_custom_call" | custom-call | flops 1000000000 | bytes 2000000 | tf_op jit(solution)/shard_map/pallas_call | solution.py:102
  15.1 17.8 %all_to_all.30.same_ref.kvs_ref = bf16[8,128,384]{2,1,0:T(8,128)(2,1)S(1)} all-to-all(bf16[8,128,384]{2,1,0:T(8,128)(2,1)S(1)} %get-tuple-element.40), channel_id=1, replica_groups=mesh['y'=4,'xl'=2,'c'=2,'zh'=2,'zl'=2,'xh'=2] {'y','xl'}, dimensions={0} | all-to-all | bytes 1572864 | tf_op jit(solution)/shard_map/all_to_all | solution.py:474
  36.7 2.6 shard_map.187
  40.1 8.2 %all-to-all-start.1 = ((bf16[8,128,256]{2,1,0:T(8,128)(2,1)}), bf16[8,128,256]{2,1,0:T(8,128)(2,1)S(1)}, u32[]{:S(2)}, u32[]{:S(2)}) async-start(bf16[8,128,256]{2,1,0:T(8,128)(2,1)} %shard_map.187), calls=%async_computation.1 | async-start | bytes 1048576 | tf_op jit(solution)/shard_map/all_to_all | solution.py:474
  49.8 9.3 %all-to-all-done.1.mixed_ref = bf16[8,128,256]{2,1,0:T(8,128)(2,1)S(1)} async-done(((bf16[8,128,256]{2,1,0:T(8,128)(2,1)}), bf16[8,128,256]{2,1,0:T(8,128)(2,1)S(1)}, u32[]{:S(2)}, u32[]{:S(2)}) %all-to-all-start.1) | async-done | bytes 524320 | tf_op jit(solution)/shard_map/all_to_all | solution.py:474
  62.3 2.4 shard_map.188
  64.7 18.8 %all_to_all.31.sums_ref = bf16[8,64,768]{2,1,0:T(8,128)(2,1)S(1)} all-to-all(bf16[8,64,768]{2,1,0:T(8,128)(2,1)S(1)} %get-tuple-element.43), channel_id=1, replica_groups=mesh['y'=4,'xl'=2,'c'=2,'zh'=2,'zl'=2,'xh'=2] {'zh','zl','xh'}, dimensions={0} | all-to-all | bytes 1572864 | tf_op jit(solution)/shard_map/all_to_all | solution.py:474
  83.5 3.0 %shard_map.189 = (bf16[32,32,256]{2,1,0:T(8,128)(2,1)S(1)}, bf16[32,768]{1,0:T(8,128)(2,1)S(1)}, f32[32,768]{1,0:T(8,128)S(1)}, bf16[32,768]{1,0:T(8,128)(2,1)S(1)}, f32[8,768]{1,0:T(8,128)S(1)}) custom-call(bf16[8,64,768]{2,1,0:T(8,128)(2,1)S(1)} %all_to_all.31.sums_ref, f32[8,32,768]{2,1,0:T(8,128)S(1)} %get-tuple-element.44.middle_ref, ...), custom_call_target="tpu_custom_call" | custom-call | flops 1000000000 | bytes 2000000 | tf_op jit(solution)/shard_map/pallas_call | solution.py:102
  86.5 12.6 %all_to_all.32 = bf16[32,32,256]{2,1,0:T(8,128)(2,1)S(1)} all-to-all(bf16[32,32,256]{2,1,0:T(8,128)(2,1)S(1)} %get-tuple-element.45), channel_id=1, replica_groups=mesh['y'=4,'xl'=2,'c'=2,'zh'=2,'zl'=2,'xh'=2] {'y','xl','zl','xh'}, dimensions={0} | all-to-all | bytes 1048576 | tf_op jit(solution)/shard_map/all_to_all | solution.py:474
  99.1 3.5 %collective-permute-start.1 = (bf16[8,128,256]{2,1,0:T(8,128)(2,1)S(1)}, bf16[8,128,256]{2,1,0:T(8,128)(2,1)S(1)}, u32[]{:S(2)}, u32[]{:S(2)}) collective-permute-start(bf16[8,128,256]{2,1,0:T(8,128)(2,1)S(1)} %bitcast.4), channel_id=1, source_target_pairs={{0,8},{8,0},{1,9},{9,1},{2,10},{10,2},{3,11},{11,3},{4,12},{12,4},... | collective-permute-start | bytes 1572872 | tf_op jit(solution)/shard_map/ppermute | solution.py:478
  103.5 3.2 %collective-permute-start.4 = (bf16[32,768]{1,0:T(8,128)(2,1)S(1)}, bf16[32,768]{1,0:T(8,128)(2,1)S(1)}, u32[]{:S(2)}, u32[]{:S(2)}) collective-permute-start(bf16[32,768]{1,0:T(8,128)(2,1)S(1)} %get-tuple-element.47.low0_ref), channel_id=1, source_target_pairs={{0,3},{1,2},{2,1},{3,0},{4,7},{5,6},{6,5},{7,4},{8,11},{9,10},{10,... | collective-permute-start | bytes 147464 | tf_op jit(solution)/shard_map/ppermute | solution.py:482
  113.1 2.9 %shard_map.190 = (bf16[128,640]{1,0:T(8,128)(2,1)S(1)}, bf16[16,48,384]{2,1,0:T(8,128)(2,1)S(1)}, bf16[16,48,384]{2,1,0:T(8,128)(2,1)S(1)}) custom-call(s32[2,32]{1,0:T(2,128)S(1)} %copy-done.29, bf16[8,128,384]{2,1,0:T(8,128)(2,1)S(1)} %all_to_all.30.same_ref.kvs_ref, bf16[8,128,384]{2,1,0:T(8,128)(2,1)S(1)} %copy-done.23, ...), custom_call_target="tpu_custom_call" | custom-call | flops 8000000000 | bytes 2000000 | tf_op jit(solution)/shard_map/pallas_call | solution.py:102
  119.7 16.2 %all_to_all.33.in_ref = bf16[16,48,384]{2,1,0:T(8,128)(2,1)S(1)} all-to-all(bf16[16,48,384]{2,1,0:T(8,128)(2,1)S(1)} %shard_map.194), channel_id=1, replica_groups=mesh['y'=4,'xl'=2,'c'=2,'zh'=2,'zl'=2,'xh'=2] {'y','xl','zh'}, dimensions={0} | all-to-all | bytes 1179648 | tf_op jit(solution)/shard_map/all_to_all | solution.py:474
  135.9 2.0 shard_map.195
  138.0 7.4 %all-to-all-start.5 = ((bf16[64,48,384]{2,1,0:T(8,128)(2,1)}), bf16[64,48,384]{2,1,0:T(8,128)(2,1)}, u32[]{:S(2)}, u32[]{:S(2)}) async-start(bf16[64,48,384]{2,1,0:T(8,128)(2,1)} %shard_map.195), calls=%async_computation.5 | async-start | bytes 4718592 | tf_op jit(solution)/shard_map/all_to_all | solution.py:474
  151.0 25.3 %all-to-all-done.5 = bf16[64,48,384]{2,1,0:T(8,128)(2,1)} async-done(((bf16[64,48,384]{2,1,0:T(8,128)(2,1)}), bf16[64,48,384]{2,1,0:T(8,128)(2,1)}, u32[]{:S(2)}, u32[]{:S(2)}) %all-to-all-start.5) | async-done | bytes 2359328 | tf_op jit(solution)/shard_map/all_to_all | solution.py:474
  176.2 3.9 %collective-permute-start.16 = (bf16[8,8,48,384]{3,2,1,0:T(8,128)(2,1)}, bf16[8,8,48,384]{3,2,1,0:T(8,128)(2,1)}, u32[]{:S(2)}, u32[]{:S(2)}) collective-permute-start(bf16[8,8,48,384]{3,2,1,0:T(8,128)(2,1)} %bitcast.3.in_ref), channel_id=1, source_target_pairs={{0,8},{8,0},{1,9},{9,1},{2,10},{10,2},{3,11},{11,3},{4,12},{12,4},... | collective-permute-start | bytes 7077896 | tf_op jit(solution)/shard_map/ppermute | solution.py:478
  180.2 33.9 %reduce-scatter.2.cloned.1.call-done = bf16[48,768]{1,0:T(8,128)(2,1)} async-done(((bf16[768,768]{1,0:T(8,128)(2,1)}), bf16[48,768]{1,0:T(8,128)(2,1)}) %reduce-scatter.2.cloned.1.call-update) | async-done | bytes 73744 | tf_op jit(solution)/shard_map/reduce_scatter | solution.py:531
  216.2 3.8 %collective-permute-start.5 = (bf16[32,768]{1,0:T(8,128)(2,1)S(1)}, bf16[32,768]{1,0:T(8,128)(2,1)S(1)}, u32[]{:S(2)}, u32[]{:S(2)}) collective-permute-start(bf16[32,768]{1,0:T(8,128)(2,1)S(1)} %get-tuple-element.50), channel_id=1, source_target_pairs={{0,1},{1,0},{2,3},{3,2},{4,5},{5,4},{6,7},{7,6},{8,9},{9,8},{10,11... | collective-permute-start | bytes 147464 | tf_op jit(solution)/shard_map/ppermute | solution.py:482
  223.0 2.7 collective-permute-done.7.three_ref
  227.2 2.8 collective-permute-start.11
  229.9 2.8 %collective-permute-start.12 = (bf16[80,768]{1,0:T(8,128)(2,1)S(1)}, bf16[80,768]{1,0:T(8,128)(2,1)S(1)}, u32[]{:S(2)}, u32[]{:S(2)}) collective-permute-start(bf16[80,768]{1,0:T(8,128)(2,1)S(1)} %shard_map.192.refs_0_), channel_id=1, source_target_pairs={{0,5},{1,4},{2,7},{3,6},{4,1},{5,0},{6,3},{7,2},{8,13},{9,12},{10,... | collective-permute-start | bytes 368648 | tf_op jit(solution)/shard_map/ppermute | solution.py:482
  232.8 2.7 collective-permute-start.13
  235.6 2.6 collective-permute-start.8
  239.8 5.1 %collective-permute-done.14.refs_7_ = bf16[80,768]{1,0:T(8,128)(2,1)S(1)} collective-permute-done((bf16[80,768]{1,0:T(8,128)(2,1)S(1)}, bf16[80,768]{1,0:T(8,128)(2,1)S(1)}, u32[]{:S(2)}, u32[]{:S(2)}) %collective-permute-start.14) | collective-permute-done | bytes 122912 | tf_op jit(solution)/shard_map/ppermute | solution.py:482
  246.0 6.0 %collective-permute-start.17 = (f32[8,768]{1,0:T(8,128)S(1)}, f32[8,768]{1,0:T(8,128)S(1)}, u32[]{:S(2)}, u32[]{:S(2)}) collective-permute-start(f32[8,768]{1,0:T(8,128)S(1)} %get-tuple-element.64), channel_id=1, source_target_pairs={{0,8},{8,0},{1,9},{9,1},{2,10},{10,2},{3,11},{11,3},{4,12},{12,4},... | collective-permute-start | bytes 73736 | tf_op jit(solution)/shard_map/ppermute | solution.py:478
  252.8 2.7 collective-permute-done.18
  255.5 2.7 collective-permute-done.19
  258.2 4.2 %collective-permute-done.20 = f32[8,768]{1,0:T(8,128)S(1)} collective-permute-done((f32[8,768]{1,0:T(8,128)S(1)}, f32[8,768]{1,0:T(8,128)S(1)}, u32[]{:S(2)}, u32[]{:S(2)}) %collective-permute-start.20) | collective-permute-done | bytes 24608 | tf_op jit(solution)/shard_map/ppermute | solution.py:482
  265.7 4.1 %shard_map.196 = (f32[768,2304]{1,0:T(8,128)}, f32[768,768]{1,0:T(8,128)}) custom-call(bf16[8,8,48,384]{3,2,1,0:T(8,128)(2,1)} %bitcast.3.in_ref), custom_call_target="tpu_custom_call" | custom-call | flops 100000000 | bytes 2000000 | tf_op jit(solution)/shard_map/pallas_call | solution.py:102
  269.9 4.1 %shard_map.197 = (f32[768,2304]{1,0:T(8,128)}, f32[768,768]{1,0:T(8,128)}) custom-call(bf16[8,8,48,384]{3,2,1,0:T(8,128)(2,1)} %collective-permute-done.16.in_ref, f32[768,2304]{1,0:T(8,128)} %get-tuple-element.60.refs_0_, f32[768,768]{1,0:T(8,128)} %get-tuple-element.61.refs_1_), custom_call_target="tpu_custom_call", output_to_operand_aliasing={{0}: (1, {}), {1}: (2, {})} | custom-call | flops 100000000 | bytes 2000000 | tf_op jit(solution)/shard_map/pallas_call | solution.py:102
  (119 shorter events, 41.6 us)
Async XLA Ops:
  11.6 25.1 %copy-start.29 = (s32[2,32]{1,0:T(2,128)S(1)}, s32[2,32]{1,0:T(2,128)}, u32[]{:S(2)}) copy-start(s32[2,32]{1,0:T(2,128)} %scene_ref.3) | copy-start | bytes 772
  32.9 3.8 %collective-permute-start = (bf16[8,128,384]{2,1,0:T(8,128)(2,1)S(1)}, bf16[8,128,384]{2,1,0:T(8,128)(2,1)S(1)}, u32[]{:S(2)}, u32[]{:S(2)}) collective-permute-start(bf16[8,128,384]{2,1,0:T(8,128)(2,1)S(1)} %all_to_all.30.same_ref.kvs_ref), channel_id=1, source_target_pairs={{0,8},{8,0},{1,9},{9,1},{2,10},{10,2},{3,11},{11,3},{4,12},{12,4},... | collective-permute-start | bytes 2359304 | tf_op jit(solution)/shard_map/ppermute | solution.py:478
  40.1 19.0 %all-to-all-start.1 = ((bf16[8,128,256]{2,1,0:T(8,128)(2,1)}), bf16[8,128,256]{2,1,0:T(8,128)(2,1)S(1)}, u32[]{:S(2)}, u32[]{:S(2)}) async-start(bf16[8,128,256]{2,1,0:T(8,128)(2,1)} %shard_map.187), calls=%async_computation.1 | async-start | bytes 1048576 | tf_op jit(solution)/shard_map/all_to_all | solution.py:474
  48.4 58.4 %all-gather.3.cloned.1.call-start = ((), (), s32[]{:S(2)}) async-start(), calls=%async_computation.7 | async-start | bytes 1114112 | tf_op jit(solution)/shard_map/all_gather | solution.py:510
  64.7 21.8 %copy-start.30 = (bf16[256,768]{1,0:T(8,128)(2,1)}, bf16[256,768]{1,0:T(8,128)(2,1)S(1)}, u32[]{:S(2)}) copy-start(bf16[256,768]{1,0:T(8,128)(2,1)S(1)} %get-tuple-element.65.normed_ref) | copy-start | bytes 1179652
  64.7 21.8 %copy-start.32 = (bf16[256,384]{1,0:T(8,128)(2,1)}, bf16[256,384]{1,0:T(8,128)(2,1)S(1)}, u32[]{:S(2)}) copy-start(bf16[256,384]{1,0:T(8,128)(2,1)S(1)} %get-tuple-element.66.act_ref) | copy-start | bytes 589828
  64.7 21.8 %copy-start.34 = (bf16[256,384]{1,0:T(8,128)(2,1)}, bf16[256,384]{1,0:T(8,128)(2,1)S(1)}, u32[]{:S(2)}) copy-start(bf16[256,384]{1,0:T(8,128)(2,1)S(1)} %get-tuple-element.67.gpre_ref) | copy-start | bytes 589828
  99.1 9.8 %collective-permute-start.1 = (bf16[8,128,256]{2,1,0:T(8,128)(2,1)S(1)}, bf16[8,128,256]{2,1,0:T(8,128)(2,1)S(1)}, u32[]{:S(2)}, u32[]{:S(2)}) collective-permute-start(bf16[8,128,256]{2,1,0:T(8,128)(2,1)S(1)} %bitcast.4), channel_id=1, source_target_pairs={{0,8},{8,0},{1,9},{9,1},{2,10},{10,2},{3,11},{11,3},{4,12},{12,4},... | collective-permute-start | bytes 1572872 | tf_op jit(solution)/shard_map/ppermute | solution.py:478
  102.6 4.5 %collective-permute-start.2 = (bf16[32,768]{1,0:T(8,128)(2,1)S(1)}, bf16[32,768]{1,0:T(8,128)(2,1)S(1)}, u32[]{:S(2)}, u32[]{:S(2)}) collective-permute-start(bf16[32,768]{1,0:T(8,128)(2,1)S(1)} %get-tuple-element.47.low0_ref), channel_id=1, source_target_pairs={{0,1},{1,0},{2,3},{3,2},{4,5},{5,4},{6,7},{7,6},{8,9},{9,8},{10,11... | collective-permute-start | bytes 147464 | tf_op jit(solution)/shard_map/ppermute | solution.py:482
  103.1 3.9 %collective-permute-start.3 = (bf16[32,768]{1,0:T(8,128)(2,1)S(1)}, bf16[32,768]{1,0:T(8,128)(2,1)S(1)}, u32[]{:S(2)}, u32[]{:S(2)}) collective-permute-start(bf16[32,768]{1,0:T(8,128)(2,1)S(1)} %get-tuple-element.47.low0_ref), channel_id=1, source_target_pairs={{0,2},{1,3},{2,0},{3,1},{4,6},{5,7},{6,4},{7,5},{8,10},{9,11},{10,... | collective-permute-start | bytes 147464 | tf_op jit(solution)/shard_map/ppermute | solution.py:482
  103.5 5.3 %collective-permute-start.4 = (bf16[32,768]{1,0:T(8,128)(2,1)S(1)}, bf16[32,768]{1,0:T(8,128)(2,1)S(1)}, u32[]{:S(2)}, u32[]{:S(2)}) collective-permute-start(bf16[32,768]{1,0:T(8,128)(2,1)S(1)} %get-tuple-element.47.low0_ref), channel_id=1, source_target_pairs={{0,3},{1,2},{2,1},{3,0},{4,7},{5,6},{6,5},{7,4},{8,11},{9,10},{10,... | collective-permute-start | bytes 147464 | tf_op jit(solution)/shard_map/ppermute | solution.py:482
  115.9 3.5 %collective-permute-start.15 = (bf16[16,48,384]{2,1,0:T(8,128)(2,1)S(1)}, bf16[16,48,384]{2,1,0:T(8,128)(2,1)S(1)}, u32[]{:S(2)}, u32[]{:S(2)}) collective-permute-start(bf16[16,48,384]{2,1,0:T(8,128)(2,1)S(1)} %get-tuple-element.59), channel_id=1, source_target_pairs={{0,8},{8,0},{1,9},{9,1},{2,10},{10,2},{3,11},{11,3},{4,12},{12,4},... | collective-permute-start | bytes 1769480 | tf_op jit(solution)/shard_map/ppermute | solution.py:478
  138.0 38.3 %all-to-all-start.5 = ((bf16[64,48,384]{2,1,0:T(8,128)(2,1)}), bf16[64,48,384]{2,1,0:T(8,128)(2,1)}, u32[]{:S(2)}, u32[]{:S(2)}) async-start(bf16[64,48,384]{2,1,0:T(8,128)(2,1)} %shard_map.195), calls=%async_computation.5 | async-start | bytes 4718592 | tf_op jit(solution)/shard_map/all_to_all | solution.py:474
  145.4 68.7 %reduce-scatter.2.cloned.1.call-start = ((), (), s32[]{:S(2)}) async-start(), calls=%async_computation.8 | async-start | bytes 1253376 | tf_op jit(solution)/shard_map/reduce_scatter | solution.py:531
  149.3 64.8 %copy-start.1 = (bf16[768,2304]{1,0:T(8,128)(2,1)S(1)}, bf16[768,2304]{1,0:T(8,128)(2,1)}, u32[]{:S(2)}) copy-start(bf16[768,2304]{1,0:T(8,128)(2,1)} %w_ref.3) | copy-start | bytes 10616836
  150.9 74.8 %copy-start.18 = (f32[768]{0:T(1024)S(1)}, f32[768]{0:T(1024)}, u32[]{:S(2)}) copy-start(f32[768]{0:T(1024)} %gain_ref.7) | copy-start | bytes 9220
  150.9 112.1 %all-gather.5.cloned.1.call-start = ((), (), s32[]{:S(2)}) async-start(), calls=%async_computation.9 | async-start | bytes 1253376 | tf_op jit(solution)/shard_map/all_gather | solution.py:532
  176.2 93.6 %collective-permute-start.16 = (bf16[8,8,48,384]{3,2,1,0:T(8,128)(2,1)}, bf16[8,8,48,384]{3,2,1,0:T(8,128)(2,1)}, u32[]{:S(2)}, u32[]{:S(2)}) collective-permute-start(bf16[8,8,48,384]{3,2,1,0:T(8,128)(2,1)} %bitcast.3.in_ref), channel_id=1, source_target_pairs={{0,8},{8,0},{1,9},{9,1},{2,10},{10,2},{3,11},{11,3},{4,12},{12,4},... | collective-permute-start | bytes 7077896 | tf_op jit(solution)/shard_map/ppermute | solution.py:478
  216.2 5.3 %collective-permute-start.5 = (bf16[32,768]{1,0:T(8,128)(2,1)S(1)}, bf16[32,768]{1,0:T(8,128)(2,1)S(1)}, u32[]{:S(2)}, u32[]{:S(2)}) collective-permute-start(bf16[32,768]{1,0:T(8,128)(2,1)S(1)} %get-tuple-element.50), channel_id=1, source_target_pairs={{0,1},{1,0},{2,3},{3,2},{4,5},{5,4},{6,7},{7,6},{8,9},{9,8},{10,11... | collective-permute-start | bytes 147464 | tf_op jit(solution)/shard_map/ppermute | solution.py:482
  220.0 2.9 %collective-permute-start.6 = (bf16[32,768]{1,0:T(8,128)(2,1)S(1)}, bf16[32,768]{1,0:T(8,128)(2,1)S(1)}, u32[]{:S(2)}, u32[]{:S(2)}) collective-permute-start(bf16[32,768]{1,0:T(8,128)(2,1)S(1)} %get-tuple-element.51), channel_id=1, source_target_pairs={{0,2},{1,3},{2,0},{3,1},{4,6},{5,7},{6,4},{7,5},{8,10},{9,11},{10,... | collective-permute-start | bytes 147464 | tf_op jit(solution)/shard_map/ppermute | solution.py:482
  220.0 5.7 %collective-permute-start.7 = (bf16[32,768]{1,0:T(8,128)(2,1)S(1)}, bf16[32,768]{1,0:T(8,128)(2,1)S(1)}, u32[]{:S(2)}, u32[]{:S(2)}) collective-permute-start(bf16[32,768]{1,0:T(8,128)(2,1)S(1)} %get-tuple-element.52), channel_id=1, source_target_pairs={{0,3},{1,2},{2,1},{3,0},{4,7},{5,6},{6,5},{7,4},{8,11},{9,10},{10,... | collective-permute-start | bytes 147464 | tf_op jit(solution)/shard_map/ppermute | solution.py:482
  226.1 9.4 %collective-permute-start.10 = (bf16[80,768]{1,0:T(8,128)(2,1)S(1)}, bf16[80,768]{1,0:T(8,128)(2,1)S(1)}, u32[]{:S(2)}, u32[]{:S(2)}) collective-permute-start(bf16[80,768]{1,0:T(8,128)(2,1)S(1)} %shard_map.192.refs_0_), channel_id=1, source_target_pairs={{0,3},{1,2},{2,1},{3,0},{4,7},{5,6},{6,5},{7,4},{8,11},{9,10},{10,... | collective-permute-start | bytes 368648 | tf_op jit(solution)/shard_map/ppermute | solution.py:482
  227.2 8.4 %collective-permute-start.11 = (bf16[80,768]{1,0:T(8,128)(2,1)S(1)}, bf16[80,768]{1,0:T(8,128)(2,1)S(1)}, u32[]{:S(2)}, u32[]{:S(2)}) collective-permute-start(bf16[80,768]{1,0:T(8,128)(2,1)S(1)} %shard_map.192.refs_0_), channel_id=1, source_target_pairs={{0,4},{1,5},{2,6},{3,7},{4,0},{5,1},{6,2},{7,3},{8,12},{9,13},{10,... | collective-permute-start | bytes 368648 | tf_op jit(solution)/shard_map/ppermute | solution.py:482
  229.9 8.4 %collective-permute-start.12 = (bf16[80,768]{1,0:T(8,128)(2,1)S(1)}, bf16[80,768]{1,0:T(8,128)(2,1)S(1)}, u32[]{:S(2)}, u32[]{:S(2)}) collective-permute-start(bf16[80,768]{1,0:T(8,128)(2,1)S(1)} %shard_map.192.refs_0_), channel_id=1, source_target_pairs={{0,5},{1,4},{2,7},{3,6},{4,1},{5,0},{6,3},{7,2},{8,13},{9,12},{10,... | collective-permute-start | bytes 368648 | tf_op jit(solution)/shard_map/ppermute | solution.py:482
  232.8 7.0 %collective-permute-start.13 = (bf16[80,768]{1,0:T(8,128)(2,1)S(1)}, bf16[80,768]{1,0:T(8,128)(2,1)S(1)}, u32[]{:S(2)}, u32[]{:S(2)}) collective-permute-start(bf16[80,768]{1,0:T(8,128)(2,1)S(1)} %shard_map.192.refs_0_), channel_id=1, source_target_pairs={{0,6},{1,7},{2,4},{3,5},{4,2},{5,3},{6,0},{7,1},{8,14},{9,15},{10,... | collective-permute-start | bytes 368648 | tf_op jit(solution)/shard_map/ppermute | solution.py:482
  235.5 9.4 %collective-permute-start.14 = (bf16[80,768]{1,0:T(8,128)(2,1)S(1)}, bf16[80,768]{1,0:T(8,128)(2,1)S(1)}, u32[]{:S(2)}, u32[]{:S(2)}) collective-permute-start(bf16[80,768]{1,0:T(8,128)(2,1)S(1)} %shard_map.192.refs_0_), channel_id=1, source_target_pairs={{0,7},{1,6},{2,5},{3,4},{4,3},{5,2},{6,1},{7,0},{8,15},{9,14},{10,... | collective-permute-start | bytes 368648 | tf_op jit(solution)/shard_map/ppermute | solution.py:482
  235.6 9.3 %collective-permute-start.8 = (bf16[80,768]{1,0:T(8,128)(2,1)S(1)}, bf16[80,768]{1,0:T(8,128)(2,1)S(1)}, u32[]{:S(2)}, u32[]{:S(2)}) collective-permute-start(bf16[80,768]{1,0:T(8,128)(2,1)S(1)} %shard_map.192.refs_0_), channel_id=1, source_target_pairs={{0,1},{1,0},{2,3},{3,2},{4,5},{5,4},{6,7},{7,6},{8,9},{9,8},{10,11... | collective-permute-start | bytes 368648 | tf_op jit(solution)/shard_map/ppermute | solution.py:482
  238.3 6.5 %collective-permute-start.9 = (bf16[80,768]{1,0:T(8,128)(2,1)S(1)}, bf16[80,768]{1,0:T(8,128)(2,1)S(1)}, u32[]{:S(2)}, u32[]{:S(2)}) collective-permute-start(bf16[80,768]{1,0:T(8,128)(2,1)S(1)} %shard_map.192.refs_0_), channel_id=1, source_target_pairs={{0,2},{1,3},{2,0},{3,1},{4,6},{5,7},{6,4},{7,5},{8,10},{9,11},{10,... | collective-permute-start | bytes 368648 | tf_op jit(solution)/shard_map/ppermute | solution.py:482
  246.0 6.8 %collective-permute-start.17 = (f32[8,768]{1,0:T(8,128)S(1)}, f32[8,768]{1,0:T(8,128)S(1)}, u32[]{:S(2)}, u32[]{:S(2)}) collective-permute-start(f32[8,768]{1,0:T(8,128)S(1)} %get-tuple-element.64), channel_id=1, source_target_pairs={{0,8},{8,0},{1,9},{9,1},{2,10},{10,2},{3,11},{11,3},{4,12},{12,4},... | collective-permute-start | bytes 73736 | tf_op jit(solution)/shard_map/ppermute | solution.py:478
  252.8 2.7 collective-permute-start.18
  255.5 2.7 collective-permute-start.19
  258.2 4.2 %collective-permute-start.20 = (f32[8,768]{1,0:T(8,128)S(1)}, f32[8,768]{1,0:T(8,128)S(1)}, u32[]{:S(2)}, u32[]{:S(2)}) collective-permute-start(f32[8,768]{1,0:T(8,128)S(1)} %add.18), channel_id=1, source_target_pairs={{0,64},{16,80},{32,96},{48,112},{64,0},{80,16},{96,32},{112,48},{1... | collective-permute-start | bytes 73736 | tf_op jit(solution)/shard_map/ppermute | solution.py:482
  (30 other events, 181.4 us)
Sparse Core Ops, SparseCore 0:
  51.5 33.3 all-gather.2
  151.0 62.9 reduce-scatter.1
  215.8 35.8 all-gather.4

commit v3 on v2

--- a/solution.py
+++ b/solution.py
@@ -138,14 +138,19 @@
 
 
 def project_kernel(
-    tok_ref, gain_ref, shift_ref, w_ref, kv_ref, q_ref, normed_ref, x_buf, w_buf, kv_buf, x_sem, w_sem, kv_sem
+    tok_ref, gain_ref, shift_ref, w_ref, kv_ref, q_ref, normed_ref,
+    x_buf, w_buf, kv_buf, gain_buf, shift_buf, x_sem, w_sem, kv_sem, gain_sem, shift_sem,
 ):
     copy_x = pltpu.make_async_copy(tok_ref.at[lax.axis_index(MICRO)], x_buf, x_sem)
     copy_x.start()
+    copy_gain = pltpu.make_async_copy(gain_ref, gain_buf, gain_sem)
+    copy_gain.start()
+    copy_shift = pltpu.make_async_copy(shift_ref, shift_buf, shift_sem)
+    copy_shift.start()
     copies = weight_copies(w_ref, w_buf, w_sem)
-    copy_x.wait()
+    wait_all([copy_x, copy_gain, copy_shift])
     unit, _ = normalized(x_buf[...].astype(F32))
-    normed = (unit * gain_ref[...].reshape(1, D) + shift_ref[...].reshape(1, D)).astype(BF)
+    normed = (unit * gain_buf[...].reshape(1, D) + shift_buf[...].reshape(1, D)).astype(BF)
     odd = (group_index() % 2) == 1
 
     def part(slot):
@@ -225,16 +230,28 @@
     second.wait()
 
 
-def ff_grads_kernel(normed_ref, act_ref, gpre_ref, og_ref, out_ref):
-    up = mm_tn(normed_ref[...], gpre_ref[...]).astype(BF)
-    grad_out = og_ref[...].reshape(2 * TOK, D)
-    down = mm_tn(act_ref[...], grad_out).astype(BF)
-    out_ref[:, :384] = up
-    for tile in range(16):
-        half = (tile % 2) * 384
-        out_ref[tile * 48:(tile + 1) * 48, 384:] = down[
-            (tile // 2) * 48:(tile // 2 + 1) * 48, half:half + 384
-        ]
+def ff_grads_kernel(normed_ref, act_ref, gpre_ref, og_ref, keep_ref, send_ref, up_buf, down_buf):
+    core = lax.axis_index(CORE)
+    up_buf[...] = mm_tn(normed_ref[...], gpre_ref[...])
+    down_buf[...] = mm_tn(act_ref[...], og_ref[...].reshape(2 * TOK, D))
+    for ref, owner in ((keep_ref, core), (send_ref, 1 - core)):
+        column = pl.multiple_of(owner * 384, 128)
+        for tile in range(8):
+            rows = pl.ds(pl.multiple_of((2 * tile + owner) * 48, 16), 48)
+            ref[tile, :, :384] = up_buf[rows].astype(BF)
+            ref[tile, :, 384:] = down_buf[tile * 48:(tile + 1) * 48, pl.ds(column, 384)].astype(BF)
+
+
+def halve_kernel(bit_of, one_ref, two_ref, keep_ref, send_ref):
+    bit = bit_of()
+    for ref, owner in ((keep_ref, bit), (send_ref, 1 - bit)):
+        for index in range(ref.shape[0]):
+            at = 2 * index + owner
+            ref[index] = (one_ref[at].astype(F32) + two_ref[at].astype(F32)).astype(BF)
+
+
+def pair_kernel(one_ref, two_ref, out_ref):
+    out_ref[...] = (one_ref[0].astype(F32) + two_ref[0].astype(F32)).astype(BF)
 
 
 def middle_kernel(
@@ -478,6 +495,18 @@
     return lax.ppermute(value, CORE, [(0, 1), (1, 0)])
 
 
+def after(value, *others):
+    return pl.pallas_call(
+        lambda *refs: None,
+        out_shape=jax.ShapeDtypeStruct(value.shape, value.dtype),
+        in_specs=[pl.BlockSpec(memory_space=pl.ANY)] * (1 + len(others)),
+        out_specs=pl.BlockSpec(memory_space=pl.ANY),
+        input_output_aliases={0: 0},
+        cost_estimate=pl.CostEstimate(flops=1, bytes_accessed=1, transcendentals=0),
+        compiler_params=pltpu.CompilerParams(vmem_limit_bytes=2**20),
+    )(value, *others)
+
+
 def flip(value, axes, count, bits):
     return lax.ppermute(value, axes, [(index, index ^ bits) for index in range(count)])
 
@@ -489,12 +518,13 @@
     kv_send, query, normed = call(
         project_kernel,
         [((8, TOK, 384), BF, "H"), ((TOK, 256), BF, "V"), ((TOK, D), BF, "V")],
-        [(tokens, "H"), (ln1_gain, "V"), (ln1_shift, "V"), (w_qkv, "H")],
+        [(tokens, "H"), (ln1_gain, "H"), (ln1_shift, "H"), (w_qkv, "H")],
         10**9,
         [
             pltpu.VMEM((TOK, D), BF), pltpu.VMEM((3, D, 384), BF), pltpu.VMEM((TOK, 384), BF),
-            DMA, DMA((3,)), DMA((8,)),
+            pltpu.VMEM((D,), F32), pltpu.VMEM((D,), F32), DMA, DMA((3,)), DMA((8,)), DMA, DMA,
         ],
+        vmem=56,
     )
     kv_same = exchange(kv_send, CHIP)
     kv_other = swap(kv_same)
@@ -522,13 +552,33 @@
         [pltpu.VMEM((8, BLK, D), BF), pltpu.VMEM((8, BLK, D), BF), DMA((2,))],
     )
     ff_sums = exchange(ff_send, NARROW)
-    (ff_grads,) = call(
+    keep, send = call(
         ff_grads_kernel,
-        [((D, D), BF, "V")],
+        [((8, 48, D), BF, "V")] * 2,
         [(normed2, "V"), (act, "V"), (grad_pre, "V"), (out_grad, "V")],
         2 * 10**9,
-    )
-    ff_part = lax.psum_scatter(ff_grads, WIDE, scatter_dimension=0, tiled=True)
+        [pltpu.VMEM((D, FFL), F32), pltpu.VMEM((FFL, D), F32)],
+    )
+    pieces = [(keep, send)]
+    for count, bit_of, move in (
+        (4, lambda: lax.axis_index("xl"), swap),
+        (2, lambda: lax.axis_index("y") % 2, lambda value: flip(value, "xl", 2, 1)),
+        (1, lambda: lax.axis_index("y") // 2, lambda value: flip(value, "y", 4, 1)),
+    ):
+        keep, send = pieces[-1]
+        pieces.append(
+            call(
+                functools.partial(halve_kernel, bit_of),
+                [((count, 48, D), BF, "V")] * 2,
+                [(keep, "V"), (move(send), "V")],
+                10**8,
+            )
+        )
+    ff_sums = after(ff_sums, pieces[2][0])
+    keep, send = pieces[3]
+    (ff_part,) = call(
+        pair_kernel, [((48, D), BF, "V")], [(keep, "V"), (flip(send, "y", 4, 2), "V")], 10**7
+    )
     ff_all = lax.all_gather(ff_part, WIDE, axis=0, tiled=True)
     grad_send, low, grad_mid, result_part, vec2 = call(
         middle_kernel,
@@ -542,6 +592,7 @@
     )
     grad_same = exchange(grad_send, (*CHIP, *GROUP)).reshape(8, TOK, 256)
     lows = [low] + [flip(low, GROUP, 4, k) for k in (1, 2, 3)]
+    grad_same = after(grad_same, *lows, ff_part)
     grad_other = swap(grad_same)
     gqkv, keep, send = call(
         attend_back_kernel,
@@ -587,6 +638,7 @@
         [(value, "V") for value in everyone],
         10**8,
     )
+    weight_parts = after(weight_parts, packed)
     (weight_total,) = call(
         sum_kernel,
         [((64, 48, 384), BF, "H")],
@@ -595,13 +647,14 @@
         [pltpu.VMEM((48, 384), BF), DMA((64,))],
     )
     weight_same = exchange(weight_total, (*CHIP, *NARROW)).reshape(8, 8, 48, 384)
-    weight_other = swap(weight_same)
     vectors = vectors + swap(vectors)
     for bits in (1, 2, 4):
         vectors = vectors + flip(vectors, CHIP, 8, bits)
     up_grad, down_grad = call(
         spread_ff_kernel, [((D, FFL), F32, "V"), ((FFL, D), F32, "V")], [(ff_all, "V")], 10**7
     )
+    weight_same = after(weight_same, vectors, input_grad, result, up_grad, down_grad)
+    weight_other = swap(weight_same)
     scratch = [
         pltpu.VMEM((8, 48, 3 * D), F32), pltpu.VMEM((4, 2, 48, D), F32), DMA((8,)), DMA((4, 2)),
     ]

time: 284 us -> 262 us (0.923)
  blocking collectives: 65.4 us -> 18 us
  starting transfers between devices: 54.7 us -> 72.4 us
  local copies, waits for them, and re-layouts: 21.7 us -> 31.5 us
  waiting for transfers between devices: 95.1 us -> 91.2 us
  Pallas kernels: 29.5 us -> 33 us
    ppermute x16 -> x19, waiting for transfers between devices: 22.2 us -> 74.8 us  [flip(): lax.ppermute(value, axes, [(index, index ^ bits) for index in range(count)])]
    all_to_all x4 -> x1, blocking collectives: 65.4 us -> 18 us  [exchange(): return lax.all_to_all(value, axes, 0, 0, tiled=True)]
    reduce_scatter x1 -> x0, waiting for transfers between devices: 33.9 us -> none  [shards(): ff_part = lax.psum_scatter(ff_grads, WIDE, scatter_dimension=0, tiled=True)]
    all_to_all x2 -> x5, waiting for transfers between devices: 34.6 us -> 9.34 us  [exchange(): return lax.all_to_all(value, axes, 0, 0, tiled=True)]
    all_to_all x2 -> x5, starting transfers between devices: 15.7 us -> 29.6 us  [exchange(): return lax.all_to_all(value, axes, 0, 0, tiled=True)]
    unnamed x72 -> x102, local copies, waits for them, and re-layouts: 19.7 us -> 29.5 us
    ppermute x16 -> x19, starting transfers between devices: 21.8 us -> 30.7 us  [flip(): lax.ppermute(value, axes, [(index, index ^ bits) for index in range(count)])]
    ppermute x5 -> x6, starting transfers between devices: 17.1 us -> 12.1 us  [swap(): return lax.ppermute(value, CORE, [(0, 1), (1, 0)])]
  transfers between devices with their start and end apart: 26 -> 32, of which waited for: 17 -> 19; matrix products, arithmetic and copies ran while one was open for 1% -> 1% of each run, Pallas kernels for 5% -> 4%
where the time goes in v3:
time: 262 us; the launch traced here: 261 us
  waiting for transfers between devices  91.2 us (35%)
  starting transfers between devices  72.4 us (28%)
  Pallas kernels  33 us (13%)
  local copies, waits for them, and re-layouts  31.5 us (12%)
  blocking collectives  18 us (7%)
  between operations  14.5 us (6%)
    ppermute x19, waiting for transfers between devices, flip(): lax.ppermute(value, axes, [(index, index ^ bits) for index in range(count)])  74.8 us
    pallas_call x18, Pallas kernels, call(): pl.pallas_call(kernel, out_shape=[jax.ShapeDtypeStruct(shape, dtype) for...  33 us
    ppermute x19, starting transfers between devices, flip(): lax.ppermute(value, axes, [(index, index ^ bits) for index in range(count)])  30.7 us
    all_to_all x5, starting transfers between devices, exchange(): return lax.all_to_all(value, axes, 0, 0, tiled=True)  29.6 us
    unnamed x102, local copies, waits for them, and re-layouts  29.5 us
    all_to_all x1, blocking collectives, exchange(): return lax.all_to_all(value, axes, 0, 0, tiled=True)  18 us
    ppermute x6, starting transfers between devices, swap(): return lax.ppermute(value, CORE, [(0, 1), (1, 0)])  12.1 us
    all_to_all x5, waiting for transfers between devices, exchange(): return lax.all_to_all(value, axes, 0, 0, tiled=True)  9.34 us
  transfers between devices with their start and end apart: 32, of which 19 were waited for; matrix products, arithmetic and copies ran while one was open for 1% of the time, Pallas kernels for 4%

profile of v3, /device:TPU:1, one launch (start us, length us, event | category | flops | bytes accessed | tf_op | source)
XLA Modules:
  0.0 260.6 jit_solution(6620647294870316945)
XLA Ops:
  7.2 3.8 %shard_map.186 = (bf16[8,128,384]{2,1,0:T(8,128)(2,1)}, bf16[128,256]{1,0:T(8,128)(2,1)}, bf16[128,768]{1,0:T(8,128)(2,1)}) custom-call(bf16[2,128,768]{2,1,0:T(8,128)(2,1)} %tok_ref.5, f32[768]{0:T(1024)} %gain_ref.7, f32[768]{0:T(1024)} %shift_ref.2, bf16[768,2304]{1,0:T(8,128)(2,1)} %w_ref.3), custom_call_target="tpu_custom_call" | custom-call | flops 1000000000 | bytes 2000000 | tf_op jit(solution)/shard_map/pallas_call | solution.py:102
  11.0 18.0 %all_to_all.30.same_ref.kvs_ref = bf16[8,128,384]{2,1,0:T(8,128)(2,1)S(1)} all-to-all(bf16[8,128,384]{2,1,0:T(8,128)(2,1)} %get-tuple-element.48), channel_id=1, replica_groups=mesh['y'=4,'xl'=2,'c'=2,'zh'=2,'zl'=2,'xh'=2] {'y','xl'}, dimensions={0} | all-to-all | bytes 1572864 | tf_op jit(solution)/shard_map/all_to_all | solution.py:491
  30.9 1.9 collective-permute-done.other_ref.kvo_ref
  33.7 3.2 %shard_map.187 = bf16[8,128,256]{2,1,0:T(8,128)(2,1)} custom-call(s32[2,32]{1,0:T(2,128)S(1)} %copy-done.50, bf16[128,256]{1,0:T(8,128)(2,1)S(1)} %copy-done.25, bf16[8,128,384]{2,1,0:T(8,128)(2,1)S(1)} %all_to_all.30.same_ref.kvs_ref, bf16[8,128,384]{2,1,0:T(8,128)(2,1)S(1)} %collective-permute-done.other_ref.kvo_ref), custom_call_target="tpu_custom_call" | custom-call | flops 2000000000 | bytes 2000000 | tf_op jit(solution)/shard_map/pallas_call | solution.py:102
  36.9 6.5 %all-to-all-start.1 = ((bf16[8,128,256]{2,1,0:T(8,128)(2,1)}), bf16[8,128,256]{2,1,0:T(8,128)(2,1)S(1)}, u32[]{:S(2)}, u32[]{:S(2)}) async-start(bf16[8,128,256]{2,1,0:T(8,128)(2,1)} %shard_map.187), calls=%async_computation.1 | async-start | bytes 1048576 | tf_op jit(solution)/shard_map/all_to_all | solution.py:491
  44.8 9.3 %all-to-all-done.1.mixed_ref = bf16[8,128,256]{2,1,0:T(8,128)(2,1)S(1)} async-done(((bf16[8,128,256]{2,1,0:T(8,128)(2,1)}), bf16[8,128,256]{2,1,0:T(8,128)(2,1)S(1)}, u32[]{:S(2)}, u32[]{:S(2)}) %all-to-all-start.1) | async-done | bytes 524320 | tf_op jit(solution)/shard_map/all_to_all | solution.py:491
  55.3 2.4 shard_map.188
  62.9 3.6 %all-to-all-start.2 = ((bf16[8,64,768]{2,1,0:T(8,128)(2,1)}), bf16[8,64,768]{2,1,0:T(8,128)(2,1)S(1)}, u32[]{:S(2)}, u32[]{:S(2)}) async-start(bf16[8,64,768]{2,1,0:T(8,128)(2,1)} %copy-done.17), calls=%async_computation.2 | async-start | bytes 1572864 | tf_op jit(solution)/shard_map/all_to_all | solution.py:491
  67.8 18.5 %collective-permute-done.2.two_ref = bf16[4,48,768]{2,1,0:T(8,128)(2,1)S(1)} collective-permute-done((bf16[4,48,768]{2,1,0:T(8,128)(2,1)S(1)}, bf16[4,48,768]{2,1,0:T(8,128)(2,1)S(1)}, u32[]{:S(2)}, u32[]{:S(2)}) %collective-permute-start.2) | collective-permute-done | bytes 294944 | tf_op jit(solution)/shard_map/ppermute | solution.py:511
  92.0 7.4 %all-to-all-start.3 = ((bf16[32,32,256]{2,1,0:T(8,128)(2,1)}), bf16[32,32,256]{2,1,0:T(8,128)(2,1)S(1)}, u32[]{:S(2)}, u32[]{:S(2)}) async-start(bf16[32,32,256]{2,1,0:T(8,128)(2,1)} %get-tuple-element.61), calls=%async_computation.3 | async-start | bytes 1048576 | tf_op jit(solution)/shard_map/all_to_all | solution.py:491
  100.7 8.0 %collective-permute-done.6.two_ref = bf16[2,48,768]{2,1,0:T(8,128)(2,1)S(1)} collective-permute-done((bf16[2,48,768]{2,1,0:T(8,128)(2,1)}, bf16[2,48,768]{2,1,0:T(8,128)(2,1)S(1)}, u32[]{:S(2)}, u32[]{:S(2)}) %collective-permute-start.6) | collective-permute-done | bytes 147488 | tf_op jit(solution)/shard_map/ppermute | solution.py:511
  108.8 2.8 %collective-permute-start.7 = (bf16[1,48,768]{2,1,0:T(8,128)(2,1)S(1)}, bf16[1,48,768]{2,1,0:T(8,128)(2,1)S(1)}, u32[]{:S(2)}, u32[]{:S(2)}) collective-permute-start(bf16[1,48,768]{2,1,0:T(8,128)(2,1)S(1)} %get-tuple-element.65), channel_id=1, source_target_pairs={{0,64},{32,96},{64,0},{96,32},{1,65},{33,97},{65,1},{97,33},{2,66}... | collective-permute-start | bytes 221192 | tf_op jit(solution)/shard_map/ppermute | solution.py:511
  111.6 4.6 %collective-permute-start.5 = (bf16[32,768]{1,0:T(8,128)(2,1)S(1)}, bf16[32,768]{1,0:T(8,128)(2,1)S(1)}, u32[]{:S(2)}, u32[]{:S(2)}) collective-permute-start(bf16[32,768]{1,0:T(8,128)(2,1)S(1)} %get-tuple-element.62.refs_1_.low0_ref), channel_id=1, source_target_pairs={{0,3},{1,2},{2,1},{3,0},{4,7},{5,6},{6,5},{7,4},{8,11},{9,10},{10,... | collective-permute-start | bytes 147464 | tf_op jit(solution)/shard_map/ppermute | solution.py:511
  120.9 3.1 %collective-permute-start.8 = (bf16[8,128,256]{2,1,0:T(8,128)(2,1)S(1)}, bf16[8,128,256]{2,1,0:T(8,128)(2,1)S(1)}, u32[]{:S(2)}, u32[]{:S(2)}) collective-permute-start(bf16[8,128,256]{2,1,0:T(8,128)(2,1)S(1)} %shard_map.196.gs_ref), channel_id=1, source_target_pairs={{0,8},{8,0},{1,9},{9,1},{2,10},{10,2},{3,11},{11,3},{4,12},{12,4},... | collective-permute-start | bytes 1572872 | tf_op jit(solution)/shard_map/ppermute | solution.py:495
  137.1 3.9 %shard_map.197 = (bf16[128,640]{1,0:T(8,128)(2,1)S(1)}, bf16[16,48,384]{2,1,0:T(8,128)(2,1)S(1)}, bf16[16,48,384]{2,1,0:T(8,128)(2,1)S(1)}) custom-call(s32[2,32]{1,0:T(2,128)S(1)} %copy-done.50, bf16[8,128,384]{2,1,0:T(8,128)(2,1)S(1)} %copy-done.16, bf16[8,128,384]{2,1,0:T(8,128)(2,1)S(1)} %copy-done.42, bf16[8,2,128,256]{3,2,1,0:T(8,128)(2,1)S(1)} %bitcast.6, ...), custom_call_target="tpu_custom_call" | custom-call | flops 8000000000 | bytes 2000000 | tf_op jit(solution)/shard_map/pallas_call | solution.py:102
  144.8 4.4 %all-to-all-start.4 = ((bf16[16,48,384]{2,1,0:T(8,128)(2,1)}), bf16[16,48,384]{2,1,0:T(8,128)(2,1)}, u32[]{:S(2)}, u32[]{:S(2)}) async-start(bf16[16,48,384]{2,1,0:T(8,128)(2,1)} %copy-done.2), calls=%async_computation.4 | async-start | bytes 1179648 | tf_op jit(solution)/shard_map/all_to_all | solution.py:491
  155.5 3.3 %collective-permute-done.9.one_ref = bf16[32,768]{1,0:T(8,128)(2,1)S(1)} collective-permute-done((bf16[32,768]{1,0:T(8,128)(2,1)S(1)}, bf16[32,768]{1,0:T(8,128)(2,1)S(1)}, u32[]{:S(2)}, u32[]{:S(2)}) %collective-permute-start.9) | collective-permute-done | bytes 49184 | tf_op jit(solution)/shard_map/ppermute | solution.py:511
  158.8 3.8 %collective-permute-done.10.two_ref = bf16[32,768]{1,0:T(8,128)(2,1)S(1)} collective-permute-done((bf16[32,768]{1,0:T(8,128)(2,1)S(1)}, bf16[32,768]{1,0:T(8,128)(2,1)S(1)}, u32[]{:S(2)}, u32[]{:S(2)}) %collective-permute-start.10) | collective-permute-done | bytes 49184 | tf_op jit(solution)/shard_map/ppermute | solution.py:511
  163.0 4.9 %shard_map.203 = bf16[64,48,384]{2,1,0:T(8,128)(2,1)S(1)} custom-call(bf16[16,48,384]{2,1,0:T(8,128)(2,1)} %shard_map.202.in_ref), custom_call_target="tpu_custom_call" | custom-call | flops 100000000 | bytes 2000000 | tf_op jit(solution)/shard_map/pallas_call | solution.py:102
  169.3 7.7 %all-to-all-start.5 = ((bf16[64,48,384]{2,1,0:T(8,128)(2,1)}), bf16[64,48,384]{2,1,0:T(8,128)(2,1)S(1)}, u32[]{:S(2)}, u32[]{:S(2)}) async-start(bf16[64,48,384]{2,1,0:T(8,128)(2,1)} %copy-done.1), calls=%async_computation.5 | async-start | bytes 4718592 | tf_op jit(solution)/shard_map/all_to_all | solution.py:491
  177.8 4.7 %collective-permute-start.18 = (bf16[80,768]{1,0:T(8,128)(2,1)S(1)}, bf16[80,768]{1,0:T(8,128)(2,1)S(1)}, u32[]{:S(2)}, u32[]{:S(2)}) collective-permute-start(bf16[80,768]{1,0:T(8,128)(2,1)S(1)} %shard_map.199.refs_0_.refs_1_), channel_id=1, source_target_pairs={{0,7},{1,6},{2,5},{3,4},{4,3},{5,2},{6,1},{7,0},{8,15},{9,14},{10,... | collective-permute-start | bytes 368648 | tf_op jit(solution)/shard_map/ppermute | solution.py:511
  185.9 2.2 collective-permute-start.14
  188.2 23.3 %collective-permute-done.18.refs_7_ = bf16[80,768]{1,0:T(8,128)(2,1)S(1)} collective-permute-done((bf16[80,768]{1,0:T(8,128)(2,1)S(1)}, bf16[80,768]{1,0:T(8,128)(2,1)S(1)}, u32[]{:S(2)}, u32[]{:S(2)}) %collective-permute-start.18) | collective-permute-done | bytes 122912 | tf_op jit(solution)/shard_map/ppermute | solution.py:511
  211.5 4.4 %collective-permute-done.17.refs_6_ = bf16[80,768]{1,0:T(8,128)(2,1)S(1)} collective-permute-done((bf16[80,768]{1,0:T(8,128)(2,1)S(1)}, bf16[80,768]{1,0:T(8,128)(2,1)S(1)}, u32[]{:S(2)}, u32[]{:S(2)}) %collective-permute-start.17) | collective-permute-done | bytes 122912 | tf_op jit(solution)/shard_map/ppermute | solution.py:511
  216.0 3.3 %collective-permute-start.12 = (bf16[80,768]{1,0:T(8,128)(2,1)S(1)}, bf16[80,768]{1,0:T(8,128)(2,1)S(1)}, u32[]{:S(2)}, u32[]{:S(2)}) collective-permute-start(bf16[80,768]{1,0:T(8,128)(2,1)S(1)} %shard_map.199.refs_0_.refs_1_), channel_id=1, source_target_pairs={{0,1},{1,0},{2,3},{3,2},{4,5},{5,4},{6,7},{7,6},{8,9},{9,8},{10,11... | collective-permute-start | bytes 368648 | tf_op jit(solution)/shard_map/ppermute | solution.py:511
  219.3 3.2 %collective-permute-done.12.refs_1_ = bf16[80,768]{1,0:T(8,128)(2,1)S(1)} collective-permute-done((bf16[80,768]{1,0:T(8,128)(2,1)S(1)}, bf16[80,768]{1,0:T(8,128)(2,1)S(1)}, u32[]{:S(2)}, u32[]{:S(2)}) %collective-permute-start.12) | collective-permute-done | bytes 122912 | tf_op jit(solution)/shard_map/ppermute | solution.py:511
  225.9 2.2 collective-permute-start.21
  229.3 2.7 %collective-permute-done.22 = f32[8,768]{1,0:T(8,128)S(1)} collective-permute-done((f32[8,768]{1,0:T(8,128)S(1)}, f32[8,768]{1,0:T(8,128)S(1)}, u32[]{:S(2)}, u32[]{:S(2)}) %collective-permute-start.22) | collective-permute-done | bytes 24608 | tf_op jit(solution)/shard_map/ppermute | solution.py:511
  233.5 2.7 %collective-permute-done.23 = f32[8,768]{1,0:T(8,128)S(1)} collective-permute-done((f32[8,768]{1,0:T(8,128)S(1)}, f32[8,768]{1,0:T(8,128)S(1)}, u32[]{:S(2)}, u32[]{:S(2)}) %collective-permute-start.23) | collective-permute-done | bytes 24608 | tf_op jit(solution)/shard_map/ppermute | solution.py:511
  243.6 3.5 %collective-permute-start.24 = (bf16[8,8,48,384]{3,2,1,0:T(8,128)(2,1)S(1)}, bf16[8,8,48,384]{3,2,1,0:T(8,128)(2,1)S(1)}, u32[]{:S(2)}, u32[]{:S(2)}) collective-permute-start(bf16[8,8,48,384]{3,2,1,0:T(8,128)(2,1)S(1)} %shard_map.205.in_ref), channel_id=1, source_target_pairs={{0,8},{8,0},{1,9},{9,1},{2,10},{10,2},{3,11},{11,3},{4,12},{12,4},... | collective-permute-start | bytes 7077896 | tf_op jit(solution)/shard_map/ppermute | solution.py:495
  247.8 2.4 shard_map.206
  251.3 2.4 shard_map.207
  (165 shorter events, 67.8 us)
Async XLA Ops:
  29.0 3.8 %collective-permute-start = (bf16[8,128,384]{2,1,0:T(8,128)(2,1)S(1)}, bf16[8,128,384]{2,1,0:T(8,128)(2,1)S(1)}, u32[]{:S(2)}, u32[]{:S(2)}) collective-permute-start(bf16[8,128,384]{2,1,0:T(8,128)(2,1)S(1)} %all_to_all.30.same_ref.kvs_ref), channel_id=1, source_target_pairs={{0,8},{8,0},{1,9},{9,1},{2,10},{10,2},{3,11},{11,3},{4,12},{12,4},... | collective-permute-start | bytes 2359304 | tf_op jit(solution)/shard_map/ppermute | solution.py:495
  36.9 17.2 %all-to-all-start.1 = ((bf16[8,128,256]{2,1,0:T(8,128)(2,1)}), bf16[8,128,256]{2,1,0:T(8,128)(2,1)S(1)}, u32[]{:S(2)}, u32[]{:S(2)}) async-start(bf16[8,128,256]{2,1,0:T(8,128)(2,1)} %shard_map.187), calls=%async_computation.1 | async-start | bytes 1048576 | tf_op jit(solution)/shard_map/all_to_all | solution.py:491
  43.4 81.4 %all-gather.3.cloned.1.call-start = ((), (), s32[]{:S(2)}) async-start(), calls=%async_computation.6 | async-start | bytes 1114112 | tf_op jit(solution)/shard_map/all_gather | solution.py:540
  61.2 5.3 %collective-permute-start.1 = (bf16[8,48,768]{2,1,0:T(8,128)(2,1)}, bf16[8,48,768]{2,1,0:T(8,128)(2,1)}, u32[]{:S(2)}, u32[]{:S(2)}) collective-permute-start(bf16[8,48,768]{2,1,0:T(8,128)(2,1)} %get-tuple-element.56), channel_id=1, source_target_pairs={{0,8},{8,0},{1,9},{9,1},{2,10},{10,2},{3,11},{11,3},{4,12},{12,4},... | collective-permute-start | bytes 1769480 | tf_op jit(solution)/shard_map/ppermute | solution.py:495
  62.9 24.1 %all-to-all-start.2 = ((bf16[8,64,768]{2,1,0:T(8,128)(2,1)}), bf16[8,64,768]{2,1,0:T(8,128)(2,1)S(1)}, u32[]{:S(2)}, u32[]{:S(2)}) async-start(bf16[8,64,768]{2,1,0:T(8,128)(2,1)} %copy-done.17), calls=%async_computation.2 | async-start | bytes 1572864 | tf_op jit(solution)/shard_map/all_to_all | solution.py:491
  67.7 18.6 %collective-permute-start.2 = (bf16[4,48,768]{2,1,0:T(8,128)(2,1)S(1)}, bf16[4,48,768]{2,1,0:T(8,128)(2,1)S(1)}, u32[]{:S(2)}, u32[]{:S(2)}) collective-permute-start(bf16[4,48,768]{2,1,0:T(8,128)(2,1)S(1)} %get-tuple-element.58), channel_id=1, source_target_pairs={{0,16},{16,0},{1,17},{17,1},{2,18},{18,2},{3,19},{19,3},{4,20},{20... | collective-permute-start | bytes 884744 | tf_op jit(solution)/shard_map/ppermute | solution.py:511
  92.0 28.9 %all-to-all-start.3 = ((bf16[32,32,256]{2,1,0:T(8,128)(2,1)}), bf16[32,32,256]{2,1,0:T(8,128)(2,1)S(1)}, u32[]{:S(2)}, u32[]{:S(2)}) async-start(bf16[32,32,256]{2,1,0:T(8,128)(2,1)} %get-tuple-element.61), calls=%async_computation.3 | async-start | bytes 1048576 | tf_op jit(solution)/shard_map/all_to_all | solution.py:491
  99.4 9.3 %collective-permute-start.6 = (bf16[2,48,768]{2,1,0:T(8,128)(2,1)}, bf16[2,48,768]{2,1,0:T(8,128)(2,1)S(1)}, u32[]{:S(2)}, u32[]{:S(2)}) collective-permute-start(bf16[2,48,768]{2,1,0:T(8,128)(2,1)} %copy-done.48), channel_id=1, source_target_pairs={{0,32},{32,0},{64,96},{96,64},{1,33},{33,1},{65,97},{97,65},{2,34}... | collective-permute-start | bytes 442376 | tf_op jit(solution)/shard_map/ppermute | solution.py:511
  108.8 7.7 %collective-permute-start.7 = (bf16[1,48,768]{2,1,0:T(8,128)(2,1)S(1)}, bf16[1,48,768]{2,1,0:T(8,128)(2,1)S(1)}, u32[]{:S(2)}, u32[]{:S(2)}) collective-permute-start(bf16[1,48,768]{2,1,0:T(8,128)(2,1)S(1)} %get-tuple-element.65), channel_id=1, source_target_pairs={{0,64},{32,96},{64,0},{96,32},{1,65},{33,97},{65,1},{97,33},{2,66}... | collective-permute-start | bytes 221192 | tf_op jit(solution)/shard_map/ppermute | solution.py:511
  111.6 6.1 %collective-permute-start.5 = (bf16[32,768]{1,0:T(8,128)(2,1)S(1)}, bf16[32,768]{1,0:T(8,128)(2,1)S(1)}, u32[]{:S(2)}, u32[]{:S(2)}) collective-permute-start(bf16[32,768]{1,0:T(8,128)(2,1)S(1)} %get-tuple-element.62.refs_1_.low0_ref), channel_id=1, source_target_pairs={{0,3},{1,2},{2,1},{3,0},{4,7},{5,6},{6,5},{7,4},{8,11},{9,10},{10,... | collective-permute-start | bytes 147464 | tf_op jit(solution)/shard_map/ppermute | solution.py:511
  116.2 3.2 %collective-permute-start.4 = (bf16[32,768]{1,0:T(8,128)(2,1)S(1)}, bf16[32,768]{1,0:T(8,128)(2,1)S(1)}, u32[]{:S(2)}, u32[]{:S(2)}) collective-permute-start(bf16[32,768]{1,0:T(8,128)(2,1)S(1)} %get-tuple-element.62.refs_1_.low0_ref), channel_id=1, source_target_pairs={{0,2},{1,3},{2,0},{3,1},{4,6},{5,7},{6,4},{7,5},{8,10},{9,11},{10,... | collective-permute-start | bytes 147464 | tf_op jit(solution)/shard_map/ppermute | solution.py:511
  116.4 4.4 %collective-permute-start.3 = (bf16[32,768]{1,0:T(8,128)(2,1)S(1)}, bf16[32,768]{1,0:T(8,128)(2,1)S(1)}, u32[]{:S(2)}, u32[]{:S(2)}) collective-permute-start(bf16[32,768]{1,0:T(8,128)(2,1)S(1)} %get-tuple-element.62.refs_1_.low0_ref), channel_id=1, source_target_pairs={{0,1},{1,0},{2,3},{3,2},{4,5},{5,4},{6,7},{7,6},{8,9},{9,8},{10,11... | collective-permute-start | bytes 147464 | tf_op jit(solution)/shard_map/ppermute | solution.py:511
  120.9 4.7 %collective-permute-start.8 = (bf16[8,128,256]{2,1,0:T(8,128)(2,1)S(1)}, bf16[8,128,256]{2,1,0:T(8,128)(2,1)S(1)}, u32[]{:S(2)}, u32[]{:S(2)}) collective-permute-start(bf16[8,128,256]{2,1,0:T(8,128)(2,1)S(1)} %shard_map.196.gs_ref), channel_id=1, source_target_pairs={{0,8},{8,0},{1,9},{9,1},{2,10},{10,2},{3,11},{11,3},{4,12},{12,4},... | collective-permute-start | bytes 1572872 | tf_op jit(solution)/shard_map/ppermute | solution.py:495
  141.7 2.0 collective-permute-start.19
  144.8 18.2 %all-to-all-start.4 = ((bf16[16,48,384]{2,1,0:T(8,128)(2,1)}), bf16[16,48,384]{2,1,0:T(8,128)(2,1)}, u32[]{:S(2)}, u32[]{:S(2)}) async-start(bf16[16,48,384]{2,1,0:T(8,128)(2,1)} %copy-done.2), calls=%async_computation.4 | async-start | bytes 1179648 | tf_op jit(solution)/shard_map/all_to_all | solution.py:491
  151.3 7.5 %collective-permute-start.9 = (bf16[32,768]{1,0:T(8,128)(2,1)S(1)}, bf16[32,768]{1,0:T(8,128)(2,1)S(1)}, u32[]{:S(2)}, u32[]{:S(2)}) collective-permute-start(bf16[32,768]{1,0:T(8,128)(2,1)S(1)} %get-tuple-element.69), channel_id=1, source_target_pairs={{0,1},{1,0},{2,3},{3,2},{4,5},{5,4},{6,7},{7,6},{8,9},{9,8},{10,11... | collective-permute-start | bytes 147464 | tf_op jit(solution)/shard_map/ppermute | solution.py:511
  153.1 9.5 %collective-permute-start.10 = (bf16[32,768]{1,0:T(8,128)(2,1)S(1)}, bf16[32,768]{1,0:T(8,128)(2,1)S(1)}, u32[]{:S(2)}, u32[]{:S(2)}) collective-permute-start(bf16[32,768]{1,0:T(8,128)(2,1)S(1)} %get-tuple-element.70), channel_id=1, source_target_pairs={{0,2},{1,3},{2,0},{3,1},{4,6},{5,7},{6,4},{7,5},{8,10},{9,11},{10,... | collective-permute-start | bytes 147464 | tf_op jit(solution)/shard_map/ppermute | solution.py:511
  153.6 8.9 %collective-permute-start.11 = (bf16[32,768]{1,0:T(8,128)(2,1)S(1)}, bf16[32,768]{1,0:T(8,128)(2,1)S(1)}, u32[]{:S(2)}, u32[]{:S(2)}) collective-permute-start(bf16[32,768]{1,0:T(8,128)(2,1)S(1)} %get-tuple-element.71), channel_id=1, source_target_pairs={{0,3},{1,2},{2,1},{3,0},{4,7},{5,6},{6,5},{7,4},{8,11},{9,10},{10,... | collective-permute-start | bytes 147464 | tf_op jit(solution)/shard_map/ppermute | solution.py:511
  169.3 69.6 %all-to-all-start.5 = ((bf16[64,48,384]{2,1,0:T(8,128)(2,1)}), bf16[64,48,384]{2,1,0:T(8,128)(2,1)S(1)}, u32[]{:S(2)}, u32[]{:S(2)}) async-start(bf16[64,48,384]{2,1,0:T(8,128)(2,1)} %copy-done.1), calls=%async_computation.5 | async-start | bytes 4718592 | tf_op jit(solution)/shard_map/all_to_all | solution.py:491
  177.1 59.1 %all-gather.5.cloned.1.call-start = ((), (), s32[]{:S(2)}) async-start(), calls=%async_computation.7 | async-start | bytes 1253376 | tf_op jit(solution)/shard_map/all_gather | solution.py:582
  177.8 33.7 %collective-permute-start.18 = (bf16[80,768]{1,0:T(8,128)(2,1)S(1)}, bf16[80,768]{1,0:T(8,128)(2,1)S(1)}, u32[]{:S(2)}, u32[]{:S(2)}) collective-permute-start(bf16[80,768]{1,0:T(8,128)(2,1)S(1)} %shard_map.199.refs_0_.refs_1_), channel_id=1, source_target_pairs={{0,7},{1,6},{2,5},{3,4},{4,3},{5,2},{6,1},{7,0},{8,15},{9,14},{10,... | collective-permute-start | bytes 368648 | tf_op jit(solution)/shard_map/ppermute | solution.py:511
  182.5 33.4 %collective-permute-start.17 = (bf16[80,768]{1,0:T(8,128)(2,1)S(1)}, bf16[80,768]{1,0:T(8,128)(2,1)S(1)}, u32[]{:S(2)}, u32[]{:S(2)}) collective-permute-start(bf16[80,768]{1,0:T(8,128)(2,1)S(1)} %shard_map.199.refs_0_.refs_1_), channel_id=1, source_target_pairs={{0,6},{1,7},{2,4},{3,5},{4,2},{5,3},{6,0},{7,1},{8,14},{9,15},{10,... | collective-permute-start | bytes 368648 | tf_op jit(solution)/shard_map/ppermute | solution.py:511
  182.8 36.5 %collective-permute-start.16 = (bf16[80,768]{1,0:T(8,128)(2,1)S(1)}, bf16[80,768]{1,0:T(8,128)(2,1)S(1)}, u32[]{:S(2)}, u32[]{:S(2)}) collective-permute-start(bf16[80,768]{1,0:T(8,128)(2,1)S(1)} %shard_map.199.refs_0_.refs_1_), channel_id=1, source_target_pairs={{0,5},{1,4},{2,7},{3,6},{4,1},{5,0},{6,3},{7,2},{8,13},{9,12},{10,... | collective-permute-start | bytes 368648 | tf_op jit(solution)/shard_map/ppermute | solution.py:511
  184.3 35.0 %collective-permute-start.15 = (bf16[80,768]{1,0:T(8,128)(2,1)S(1)}, bf16[80,768]{1,0:T(8,128)(2,1)S(1)}, u32[]{:S(2)}, u32[]{:S(2)}) collective-permute-start(bf16[80,768]{1,0:T(8,128)(2,1)S(1)} %shard_map.199.refs_0_.refs_1_), channel_id=1, source_target_pairs={{0,4},{1,5},{2,6},{3,7},{4,0},{5,1},{6,2},{7,3},{8,12},{9,13},{10,... | collective-permute-start | bytes 368648 | tf_op jit(solution)/shard_map/ppermute | solution.py:511
  185.9 33.3 %collective-permute-start.14 = (bf16[80,768]{1,0:T(8,128)(2,1)S(1)}, bf16[80,768]{1,0:T(8,128)(2,1)S(1)}, u32[]{:S(2)}, u32[]{:S(2)}) collective-permute-start(bf16[80,768]{1,0:T(8,128)(2,1)S(1)} %shard_map.199.refs_0_.refs_1_), channel_id=1, source_target_pairs={{0,3},{1,2},{2,1},{3,0},{4,7},{5,6},{6,5},{7,4},{8,11},{9,10},{10,... | collective-permute-start | bytes 368648 | tf_op jit(solution)/shard_map/ppermute | solution.py:511
  211.5 7.8 %collective-permute-start.13 = (bf16[80,768]{1,0:T(8,128)(2,1)S(1)}, bf16[80,768]{1,0:T(8,128)(2,1)S(1)}, u32[]{:S(2)}, u32[]{:S(2)}) collective-permute-start(bf16[80,768]{1,0:T(8,128)(2,1)S(1)} %shard_map.199.refs_0_.refs_1_), channel_id=1, source_target_pairs={{0,2},{1,3},{2,0},{3,1},{4,6},{5,7},{6,4},{7,5},{8,10},{9,11},{10,... | collective-permute-start | bytes 368648 | tf_op jit(solution)/shard_map/ppermute | solution.py:511
  216.0 6.5 %collective-permute-start.12 = (bf16[80,768]{1,0:T(8,128)(2,1)S(1)}, bf16[80,768]{1,0:T(8,128)(2,1)S(1)}, u32[]{:S(2)}, u32[]{:S(2)}) collective-permute-start(bf16[80,768]{1,0:T(8,128)(2,1)S(1)} %shard_map.199.refs_0_.refs_1_), channel_id=1, source_target_pairs={{0,1},{1,0},{2,3},{3,2},{4,5},{5,4},{6,7},{7,6},{8,9},{9,8},{10,11... | collective-permute-start | bytes 368648 | tf_op jit(solution)/shard_map/ppermute | solution.py:511
  223.6 2.3 collective-permute-start.20
  225.9 3.4 %collective-permute-start.21 = (f32[8,768]{1,0:T(8,128)S(1)}, f32[8,768]{1,0:T(8,128)S(1)}, u32[]{:S(2)}, u32[]{:S(2)}) collective-permute-start(f32[8,768]{1,0:T(8,128)S(1)} %add.14), channel_id=1, source_target_pairs={{0,16},{16,0},{32,48},{48,32},{64,80},{80,64},{96,112},{112,96},{1... | collective-permute-start | bytes 73736 | tf_op jit(solution)/shard_map/ppermute | solution.py:511
  229.3 2.7 %collective-permute-start.22 = (f32[8,768]{1,0:T(8,128)S(1)}, f32[8,768]{1,0:T(8,128)S(1)}, u32[]{:S(2)}, u32[]{:S(2)}) collective-permute-start(f32[8,768]{1,0:T(8,128)S(1)} %add.15), channel_id=1, source_target_pairs={{0,32},{16,48},{32,0},{48,16},{64,96},{80,112},{96,64},{112,80},{1... | collective-permute-start | bytes 73736 | tf_op jit(solution)/shard_map/ppermute | solution.py:511
  232.0 4.2 %collective-permute-start.23 = (f32[8,768]{1,0:T(8,128)S(1)}, f32[8,768]{1,0:T(8,128)S(1)}, u32[]{:S(2)}, u32[]{:S(2)}) collective-permute-start(f32[8,768]{1,0:T(8,128)S(1)} %add.16), channel_id=1, source_target_pairs={{0,64},{16,80},{32,96},{48,112},{64,0},{80,16},{96,32},{112,48},{1... | collective-permute-start | bytes 73736 | tf_op jit(solution)/shard_map/ppermute | solution.py:511
  243.6 7.7 %collective-permute-start.24 = (bf16[8,8,48,384]{3,2,1,0:T(8,128)(2,1)S(1)}, bf16[8,8,48,384]{3,2,1,0:T(8,128)(2,1)S(1)}, u32[]{:S(2)}, u32[]{:S(2)}) collective-permute-start(bf16[8,8,48,384]{3,2,1,0:T(8,128)(2,1)S(1)} %shard_map.205.in_ref), channel_id=1, source_target_pairs={{0,8},{8,0},{1,9},{9,1},{2,10},{10,2},{3,11},{11,3},{4,12},{12,4},... | collective-permute-start | bytes 7077896 | tf_op jit(solution)/shard_map/ppermute | solution.py:495
  (51 other events, 340.6 us)
Sparse Core Ops, SparseCore 0:
  63.1 29.4 all-gather.2
  180.2 44.8 all-gather.4

commit v4 on v3

--- a/solution.py
+++ b/solution.py
@@ -97,18 +97,24 @@
     return out
 
 
+def pin(value):
+    return pltpu.with_memory_space_constraint(value, pltpu.HBM)
+
+
 def call(kernel, outs, ins, cost, scratch=(), vmem=16, aliases=None):
-    places = {"V": pltpu.VMEM, "H": pltpu.HBM, "S": pltpu.SMEM}
+    places = {"V": pltpu.VMEM, "H": pltpu.HBM, "S": pltpu.SMEM, "L": pltpu.VMEM}
     return pl.pallas_call(
         kernel,
-        out_shape=[jax.ShapeDtypeStruct(shape, dtype) for shape, dtype, _ in outs],
+        out_shape=[
+            (pltpu.HBM if place in "HL" else jax.ShapeDtypeStruct)(shape, dtype) for shape, dtype, place in outs
+        ],
         in_specs=[pl.BlockSpec(memory_space=places[place]) for _, place in ins],
         out_specs=[pl.BlockSpec(memory_space=places[place]) for _, _, place in outs],
         scratch_shapes=list(scratch),
         input_output_aliases=aliases or {},
         cost_estimate=pl.CostEstimate(flops=cost, bytes_accessed=2000000, transcendentals=0),
         compiler_params=pltpu.CompilerParams(vmem_limit_bytes=vmem * 2**20),
-    )(*[value for value, _ in ins])
+    )(*[pin(value) if place in "HL" else value for value, place in ins])
 
 
 DMA = pltpu.SemaphoreType.DMA
@@ -242,16 +248,26 @@
             ref[tile, :, 384:] = down_buf[tile * 48:(tile + 1) * 48, pl.ds(column, 384)].astype(BF)
 
 
-def halve_kernel(bit_of, one_ref, two_ref, keep_ref, send_ref):
-    bit = bit_of()
-    for ref, owner in ((keep_ref, bit), (send_ref, 1 - bit)):
-        for index in range(ref.shape[0]):
-            at = 2 * index + owner
-            ref[index] = (one_ref[at].astype(F32) + two_ref[at].astype(F32)).astype(BF)
+def split_kernel(one_ref, two_ref, *refs):
+    y = lax.axis_index("y")
+    for k, ref in enumerate(refs):
+        for xl in range(2):
+            at = (y ^ k) * 2 + xl
+            ref[xl] = (one_ref[at].astype(F32) + two_ref[at].astype(F32)).astype(BF)
+
+
+def halve_kernel(*refs):
+    parts, (keep_ref, send_ref) = refs[:4], refs[4:]
+    xl = lax.axis_index("xl")
+    for ref, at in ((keep_ref, xl), (send_ref, 1 - xl)):
+        total = parts[0][at].astype(F32)
+        for part in parts[1:]:
+            total = total + part[at].astype(F32)
+        ref[...] = total.astype(BF)
 
 
 def pair_kernel(one_ref, two_ref, out_ref):
-    out_ref[...] = (one_ref[0].astype(F32) + two_ref[0].astype(F32)).astype(BF)
+    out_ref[...] = (one_ref[...].astype(F32) + two_ref[...].astype(F32)).astype(BF)
 
 
 def middle_kernel(
@@ -389,21 +405,29 @@
     copy.wait()
 
 
-def sum_kernel(in_ref, out_ref, buf, sem):
+def sum_kernel(in_ref, vec_ref, out_ref, buf, sem):
     total = in_ref[0].astype(F32)
     for index in range(1, 16):
         total = total + in_ref[index].astype(F32)
-    buf[...] = total.astype(BF)
-    wait_all(send_copies(buf, out_ref, range(64), sem))
+    vectors = vec_ref[...][:4]
+    block = jnp.concatenate([total, vectors[:, :384], vectors[:, 384:]], axis=0).astype(BF)
+    for index in range(8):
+        buf[index] = block
+    wait_all(send_copies(buf, out_ref, range(8), sem))
 
 
 def spread_kernel(turn, in_ref, *refs):
-    qkv_ref, out_ref, qkv_buf, out_buf, sem, out_sem = refs[-6:]
+    qkv_buf, out_buf, sem, out_sem = refs[-4:]
+    qkv_ref, out_ref, *vec_refs = refs[3:-4] if turn else refs[:-4]
     owner = lax.axis_index(CORE)
     owner = 1 - owner if turn else owner
     copies = []
+    vectors = jnp.zeros((8, 384), F32)
     for tile in range(8):
-        block = [in_ref[tile, index].astype(F32) for index in range(8)]
+        whole = [in_ref[tile, index].astype(F32) for index in range(8)]
+        block = [value[:48] for value in whole]
+        for value in whole:
+            vectors = vectors + value[48:]
         for part, half, at in ((1, 0, 0), (2, 0, 192), (0, 4, 0)):
             qkv_buf[tile, :, part * D:(part + 1) * D] = jnp.concatenate(
                 [block[half + group][:, at:at + 192] for group in range(4)], axis=1
@@ -422,6 +446,12 @@
             )
             copy.start()
             copies.append(copy)
+    if turn:
+        vectors = vectors + refs[0][...]
+        for k, ref in enumerate(vec_refs):
+            ref[...] = jnp.concatenate([vectors[k:k + 1], vectors[4 + k:5 + k]], axis=1).reshape(D)
+    else:
+        vec_refs[0][...] = vectors
     wait_all(copies)
 
 
@@ -454,7 +484,8 @@
 
 
 def input_kernel(
-    own_ref, one_ref, two_ref, three_ref, tok_ref, gain_ref, grad_ref, result_ref, vec_ref, out_ref, x_buf, sem
+    own_ref, one_ref, two_ref, three_ref, tok_ref, gain_ref, grad_ref, result_ref, vec_ref, out_ref, sums_ref,
+    x_buf, sem,
 ):
     start = pl.multiple_of(group_index() * BLK, BLK)
     copy = pltpu.make_async_copy(tok_ref.at[lax.axis_index(MICRO), pl.ds(start, BLK)], x_buf, sem)
@@ -467,24 +498,20 @@
     grad = grad_ref[...] + norm_back(total, unit, inverse, gain_ref[...].reshape(1, D))
     gain1 = jnp.sum(total * unit, axis=0, keepdims=True)
     shift1 = jnp.sum(total, axis=0, keepdims=True)
-    vectors = jnp.concatenate([gain1, shift1, vec_ref[...][:2], jnp.zeros((12, D), F32)], axis=0)
+    sums_ref[...] = jnp.concatenate([gain1, shift1, vec_ref[...][:2], jnp.zeros((4, D), F32)], axis=0)
     out_ref[:BLK] = grad.astype(BF)
-    out_ref[BLK:2 * BLK] = result_ref[...]
-    out_ref[2 * BLK:] = vectors.astype(BF)
+    out_ref[BLK:] = result_ref[...]
 
 
 def unpack_kernel(*refs):
-    parts, (grad_ref, result_ref, vec_ref) = refs[:8], refs[8:]
+    parts, (grad_ref, result_ref) = refs[:8], refs[9:]
     micro = lax.axis_index(MICRO)
     group = group_index()
-    total = jnp.zeros((16, D), F32)
     for k, ref in enumerate(parts):
         rows = pl.ds(pl.multiple_of((group ^ (k % 4)) * BLK, BLK), BLK)
         where = micro ^ (k // 4)
         grad_ref[where, rows] = ref[:BLK].astype(F32)
-        result_ref[where, rows] = ref[BLK:2 * BLK]
-        total = total + ref[2 * BLK:].astype(F32)
-    vec_ref[...] = total[:8]
+        result_ref[where, rows] = ref[BLK:]
 
 
 def exchange(value, axes):
@@ -517,36 +544,34 @@
     w_out_pad = jnp.pad(w_out.reshape(4, 192, D), ((0, 0), (HD, 0), (0, 0)))
     kv_send, query, normed = call(
         project_kernel,
-        [((8, TOK, 384), BF, "H"), ((TOK, 256), BF, "V"), ((TOK, D), BF, "V")],
+        [((8, TOK, 384), BF, "H"), ((TOK, 256), BF, "L"), ((TOK, D), BF, "L")],
         [(tokens, "H"), (ln1_gain, "H"), (ln1_shift, "H"), (w_qkv, "H")],
         10**9,
         [
             pltpu.VMEM((TOK, D), BF), pltpu.VMEM((3, D, 384), BF), pltpu.VMEM((TOK, 384), BF),
             pltpu.VMEM((D,), F32), pltpu.VMEM((D,), F32), DMA, DMA((3,)), DMA((8,)), DMA, DMA,
         ],
-        vmem=56,
     )
     kv_same = exchange(kv_send, CHIP)
     kv_other = swap(kv_same)
     (mixed_send,) = call(
         attend_kernel,
         [((8, TOK, 256), BF, "H")],
-        [(scene_of_block, "S"), (query, "V"), (kv_same, "V"), (kv_other, "V")],
+        [(scene_of_block, "S"), (query, "L"), (kv_same, "V"), (kv_other, "V")],
         2 * 10**9,
         [pltpu.VMEM((TOK, 256), BF), DMA((8,))],
     )
     mixed = exchange(mixed_send, NARROW)
-    query, _ = lax.optimization_barrier((query, kv_same))
     queries = lax.all_gather(query, WIDE, axis=0, tiled=True).reshape(8, 2, TOK, 256)
     ff_send, middle, normed2, act, grad_pre = call(
         forward_kernel,
         [
-            ((8, 2 * BLK, D), BF, "H"), ((8, BLK, D), F32, "V"), ((2 * TOK, D), BF, "V"),
+            ((8, 2 * BLK, D), BF, "H"), ((8, BLK, D), F32, "L"), ((2 * TOK, D), BF, "V"),
             ((2 * TOK, FFL), BF, "V"), ((2 * TOK, FFL), BF, "V"),
         ],
         [
-            (mixed, "V"), (tokens, "V"), (out_grad, "V"), (w_out_pad, "V"), (ln2_gain, "V"), (ln2_shift, "V"),
-            (w_up, "V"), (w_down, "V"),
+            (mixed, "V"), (tokens, "L"), (out_grad, "L"), (w_out_pad, "L"), (ln2_gain, "L"), (ln2_shift, "L"),
+            (w_up, "L"), (w_down, "L"),
         ],
         4 * 10**9,
         [pltpu.VMEM((8, BLK, D), BF), pltpu.VMEM((8, BLK, D), BF), DMA((2,))],
@@ -555,55 +580,45 @@
     keep, send = call(
         ff_grads_kernel,
         [((8, 48, D), BF, "V")] * 2,
-        [(normed2, "V"), (act, "V"), (grad_pre, "V"), (out_grad, "V")],
+        [(normed2, "V"), (act, "V"), (grad_pre, "V"), (out_grad, "L")],
         2 * 10**9,
         [pltpu.VMEM((D, FFL), F32), pltpu.VMEM((FFL, D), F32)],
     )
-    pieces = [(keep, send)]
-    for count, bit_of, move in (
-        (4, lambda: lax.axis_index("xl"), swap),
-        (2, lambda: lax.axis_index("y") % 2, lambda value: flip(value, "xl", 2, 1)),
-        (1, lambda: lax.axis_index("y") // 2, lambda value: flip(value, "y", 4, 1)),
-    ):
-        keep, send = pieces[-1]
-        pieces.append(
-            call(
-                functools.partial(halve_kernel, bit_of),
-                [((count, 48, D), BF, "V")] * 2,
-                [(keep, "V"), (move(send), "V")],
-                10**8,
-            )
-        )
-    ff_sums = after(ff_sums, pieces[2][0])
-    keep, send = pieces[3]
+    pieces = call(
+        split_kernel, [((2, 48, D), BF, "L")] * 4, [(keep, "V"), (swap(send), "V")], 10**8
+    )
+    pieces = [pieces[0]] + [flip(pieces[k], "y", 4, k) for k in (1, 2, 3)]
+    keep, send = call(
+        halve_kernel, [((48, D), BF, "L")] * 2, [(pieces[0], "L")] + [(piece, "V") for piece in pieces[1:]], 10**8
+    )
+    ff_sums = after(ff_sums, pin(keep))
     (ff_part,) = call(
-        pair_kernel, [((48, D), BF, "V")], [(keep, "V"), (flip(send, "y", 4, 2), "V")], 10**7
+        pair_kernel, [((48, D), BF, "L")], [(keep, "L"), (flip(send, "xl", 2, 1), "V")], 10**7
     )
     ff_all = lax.all_gather(ff_part, WIDE, axis=0, tiled=True)
     grad_send, low, grad_mid, result_part, vec2 = call(
         middle_kernel,
         [
-            ((32, BLK, 256), BF, "H"), ((BLK, D), BF, "V"), ((BLK, D), F32, "V"), ((BLK, D), BF, "V"),
-            ((8, D), F32, "V"),
+            ((32, BLK, 256), BF, "H"), ((BLK, D), BF, "L"), ((BLK, D), F32, "L"), ((BLK, D), BF, "L"),
+            ((8, D), F32, "L"),
         ],
-        [(ff_sums, "V"), (middle, "V"), (out_grad, "V"), (mixed, "V"), (w_out_pad, "V"), (ln2_gain, "V")],
+        [(ff_sums, "V"), (middle, "L"), (out_grad, "L"), (mixed, "L"), (w_out_pad, "L"), (ln2_gain, "L")],
         10**9,
         [pltpu.VMEM((4, BLK, 256), BF), DMA((32,))],
     )
     grad_same = exchange(grad_send, (*CHIP, *GROUP)).reshape(8, TOK, 256)
-    lows = [low] + [flip(low, GROUP, 4, k) for k in (1, 2, 3)]
-    grad_same = after(grad_same, *lows, ff_part)
+    lows = [flip(low, GROUP, 4, k) for k in (1, 2, 3)]
+    grad_same = after(grad_same, *lows, pin(ff_part))
     grad_other = swap(grad_same)
     gqkv, keep, send = call(
         attend_back_kernel,
-        [((TOK, 640), BF, "V"), ((16, 48, 384), BF, "V"), ((16, 48, 384), BF, "V")],
+        [((TOK, 640), BF, "L"), ((16, 48, 384), BF, "V"), ((16, 48, 384), BF, "V")],
         [
-            (scene_of_block, "S"), (kv_same, "V"), (kv_other, "V"), (queries, "V"), (grad_same, "V"),
-            (grad_other, "V"), (normed, "V"), (mixed, "V"), *[(value, "V") for value in lows],
+            (scene_of_block, "S"), (kv_same, "L"), (kv_other, "L"), (queries, "L"), (grad_same, "V"),
+            (grad_other, "V"), (normed, "L"), (mixed, "L"), (low, "L"), *[(value, "V") for value in lows],
         ],
         8 * 10**9,
         [pltpu.VMEM((D, 640), F32)],
-        vmem=24,
     )
     (weight_send,) = call(
         add_kernel,
@@ -615,64 +630,59 @@
     weight_parts = exchange(weight_send, (*CHIP, MICRO))
     own, *sends = call(
         normed_grad_kernel,
-        [((BLK, D), F32, "V")] + [((BLK, D), BF, "V")] * 3,
-        [(gqkv, "V"), (w_qkv, "H")],
+        [((BLK, D), F32, "L")] + [((BLK, D), BF, "L")] * 3,
+        [(gqkv, "L"), (w_qkv, "H")],
         10**9,
         [pltpu.VMEM((3, D, 384), BF), pltpu.VMEM((TOK, D), F32), DMA((3,))],
     )
     parts = [flip(value, GROUP, 4, k + 1) for k, value in enumerate(sends)]
-    (packed,) = call(
+    packed, sums = call(
         input_kernel,
-        [((80, D), BF, "V")],
+        [((2 * BLK, D), BF, "L"), ((8, D), F32, "L")],
         [
-            (own, "V"), *[(value, "V") for value in parts], (tokens, "H"), (ln1_gain, "V"), (grad_mid, "V"),
-            (result_part, "V"), (vec2, "V"),
+            (own, "L"), *[(value, "V") for value in parts], (tokens, "H"), (ln1_gain, "L"), (grad_mid, "L"),
+            (result_part, "L"), (vec2, "L"),
         ],
         10**8,
         [pltpu.VMEM((BLK, D), BF), DMA],
     )
     everyone = [packed] + [flip(packed, NARROW, 8, k) for k in range(1, 8)]
-    input_grad, result, vectors = call(
+    input_grad, result = call(
         unpack_kernel,
-        [((2, TOK, D), F32, "V"), ((2, TOK, D), BF, "V"), ((8, D), F32, "V")],
-        [(value, "V") for value in everyone],
+        [((2, TOK, D), F32, "L"), ((2, TOK, D), BF, "L")],
+        [(packed, "L"), *[(value, "V") for value in everyone[1:]], (ff_all, "H")],
         10**8,
     )
-    weight_parts = after(weight_parts, packed)
     (weight_total,) = call(
         sum_kernel,
-        [((64, 48, 384), BF, "H")],
-        [(weight_parts, "V")],
+        [((8, 8, 56, 384), BF, "H")],
+        [(weight_parts, "V"), (sums, "L")],
         10**8,
-        [pltpu.VMEM((48, 384), BF), DMA((64,))],
-    )
-    weight_same = exchange(weight_total, (*CHIP, *NARROW)).reshape(8, 8, 48, 384)
-    vectors = vectors + swap(vectors)
-    for bits in (1, 2, 4):
-        vectors = vectors + flip(vectors, CHIP, 8, bits)
+        [pltpu.VMEM((8, 56, 384), BF), DMA((8,))],
+    )
+    weight_same = exchange(weight_total.reshape(64, 56, 384), (*CHIP, *NARROW)).reshape(8, 8, 56, 384)
     up_grad, down_grad = call(
-        spread_ff_kernel, [((D, FFL), F32, "V"), ((FFL, D), F32, "V")], [(ff_all, "V")], 10**7
-    )
-    weight_same = after(weight_same, vectors, input_grad, result, up_grad, down_grad)
+        spread_ff_kernel, [((D, FFL), F32, "L"), ((FFL, D), F32, "L")], [(ff_all, "L")], 10**7
+    )
+    weight_same = after(weight_same, *map(pin, (input_grad, result, up_grad, down_grad)))
     weight_other = swap(weight_same)
     scratch = [
         pltpu.VMEM((8, 48, 3 * D), F32), pltpu.VMEM((4, 2, 48, D), F32), DMA((8,)), DMA((4, 2)),
     ]
     grads = [((D, 3 * D), F32, "H"), ((D, D), F32, "H")]
     half = call(
-        functools.partial(spread_kernel, False), grads, [(weight_same, "V")], 10**8, scratch
-    )
-    qkv_grad, out_proj_grad = call(
+        functools.partial(spread_kernel, False), grads + [((8, 384), F32, "V")], [(weight_same, "V")], 10**8, scratch
+    )
+    qkv_grad, out_proj_grad, *vectors = call(
         functools.partial(spread_kernel, True),
-        grads,
-        [(weight_other, "V"), (half[0], "H"), (half[1], "H")],
+        grads + [((D,), F32, "L")] * 4,
+        [(weight_other, "V"), (half[2], "V"), (half[0], "H"), (half[1], "H")],
         10**8,
         scratch,
-        aliases={1: 0, 2: 1},
+        aliases={2: 0, 3: 1},
     )
     return (
-        result, input_grad, qkv_grad, out_proj_grad, vectors[0], vectors[1], vectors[2], vectors[3], up_grad,
-        down_grad,
+        result, input_grad, qkv_grad, out_proj_grad, *vectors, up_grad, down_grad
     )
 
 

time: 262 us -> 221 us (0.84)
  local copies, waits for them, and re-layouts: 31.5 us -> 1.28 us
  waiting for transfers between devices: 91.2 us -> 71.2 us
  Pallas kernels: 33 us -> 47.5 us
  starting transfers between devices: 72.4 us -> 67.4 us
    ppermute x19 -> x17, waiting for transfers between devices: 74.8 us -> 44.5 us  [flip(): lax.ppermute(value, axes, [(index, index ^ bits) for index in range(count)])]
    unnamed x102 -> x14, local copies, waits for them, and re-layouts: 29.5 us -> 0.03 us
    pallas_call x18 -> x17, Pallas kernels: 33 us -> 47.5 us  [call(): pl.pallas_call(kernel, out_shape=[(pltpu.HBM if place in 'HL' else jax.Sh...]
    all_gather x1, waiting for transfers between devices: 0.01 us -> 6.42 us  [shards(): ff_all = lax.all_gather(ff_part, WIDE, axis=0, tiled=True)]
    ppermute x6 -> x5, starting transfers between devices: 12.1 us -> 8.03 us  [swap(): return lax.ppermute(value, CORE, [(0, 1), (1, 0)])]
    ppermute x19 -> x17, starting transfers between devices: 30.7 us -> 27.3 us  [flip(): lax.ppermute(value, axes, [(index, index ^ bits) for index in range(count)])]
    ppermute x6 -> x5, waiting for transfers between devices: 6.25 us -> 7.48 us  [swap(): return lax.ppermute(value, CORE, [(0, 1), (1, 0)])]
  transfers between devices with their start and end apart: 32 -> 29, of which waited for: 19 -> 17; matrix products, arithmetic and copies ran while one was open for 1% -> 1% of each run, Pallas kernels for 4% -> 14%
where the time goes in v4:
time: 221 us; the launch traced here: 220 us
  waiting for transfers between devices  71.2 us (32%)
  starting transfers between devices  67.4 us (30%)
  Pallas kernels  47.5 us (21%)
  blocking collectives  18 us (8%)
  between operations  14.3 us (6%)
    pallas_call x17, Pallas kernels, call(): pl.pallas_call(kernel, out_shape=[(pltpu.HBM if place in 'HL' else jax.Sh...  47.5 us
    ppermute x17, waiting for transfers between devices, flip(): lax.ppermute(value, axes, [(index, index ^ bits) for index in range(count)])  44.5 us
    all_to_all x5, starting transfers between devices, exchange(): return lax.all_to_all(value, axes, 0, 0, tiled=True)  32 us
    ppermute x17, starting transfers between devices, flip(): lax.ppermute(value, axes, [(index, index ^ bits) for index in range(count)])  27.3 us
    all_to_all x1, blocking collectives, exchange(): return lax.all_to_all(value, axes, 0, 0, tiled=True)  18 us
    all_to_all x5, waiting for transfers between devices, exchange(): return lax.all_to_all(value, axes, 0, 0, tiled=True)  11.5 us
    ppermute x5, starting transfers between devices, swap(): return lax.ppermute(value, CORE, [(0, 1), (1, 0)])  8.03 us
    ppermute x5, waiting for transfers between devices, swap(): return lax.ppermute(value, CORE, [(0, 1), (1, 0)])  7.48 us
  transfers between devices with their start and end apart: 29, of which 17 were waited for; matrix products, arithmetic and copies ran while one was open for 1% of the time, Pallas kernels for 14%

profile of v4, /device:TPU:1, one launch (start us, length us, event | category | flops | bytes accessed | tf_op | source)
XLA Modules:
  0.0 219.8 jit_solution(17178978276133272194)
XLA Ops:
  7.2 3.8 %shard_map.186 = (bf16[8,128,384]{2,1,0:T(8,128)(2,1)}, bf16[128,256]{1,0:T(8,128)(2,1)}, bf16[128,768]{1,0:T(8,128)(2,1)}) custom-call(bf16[2,128,768]{2,1,0:T(8,128)(2,1)} %tok_ref.5, f32[768]{0:T(1024)} %gain_ref.7, f32[768]{0:T(1024)} %shift_ref.2, bf16[768,2304]{1,0:T(8,128)(2,1)} %w_ref.3), custom_call_target="tpu_custom_call" | custom-call | flops 1000000000 | bytes 2000000 | tf_op jit(solution)/shard_map/pallas_call | solution.py:106
  11.0 18.0 %all_to_all.30.same_ref.kvs_ref = bf16[8,128,384]{2,1,0:T(8,128)(2,1)S(1)} all-to-all(bf16[8,128,384]{2,1,0:T(8,128)(2,1)} %get-tuple-element.53), channel_id=1, replica_groups=mesh['y'=4,'xl'=2,'c'=2,'zh'=2,'zl'=2,'xh'=2] {'y','xl'}, dimensions={0} | all-to-all | bytes 1572864 | tf_op jit(solution)/shard_map/all_to_all | solution.py:518
  32.8 2.8 %shard_map.187 = bf16[8,128,256]{2,1,0:T(8,128)(2,1)} custom-call(s32[2,32]{1,0:T(2,128)S(1)} %copy-done.3, bf16[128,256]{1,0:T(8,128)(2,1)} %get-tuple-element.54.q_ref, bf16[8,128,384]{2,1,0:T(8,128)(2,1)S(1)} %all_to_all.30.same_ref.kvs_ref, bf16[8,128,384]{2,1,0:T(8,128)(2,1)S(1)} %collective-permute-done.other_ref.kvo_ref), custom_call_target="tpu_custom_call" | custom-call | flops 2000000000 | bytes 2000000 | tf_op jit(solution)/shard_map/pallas_call | solution.py:106
  35.6 8.2 %all-to-all-start.1 = ((bf16[8,128,256]{2,1,0:T(8,128)(2,1)}), bf16[8,128,256]{2,1,0:T(8,128)(2,1)S(1)}, u32[]{:S(2)}, u32[]{:S(2)}) async-start(bf16[8,128,256]{2,1,0:T(8,128)(2,1)} %shard_map.187), calls=%async_computation.1 | async-start | bytes 1048576 | tf_op jit(solution)/shard_map/all_to_all | solution.py:518
  45.8 8.8 %all-to-all-done.1.mixed_ref = bf16[8,128,256]{2,1,0:T(8,128)(2,1)S(1)} async-done(((bf16[8,128,256]{2,1,0:T(8,128)(2,1)}), bf16[8,128,256]{2,1,0:T(8,128)(2,1)S(1)}, u32[]{:S(2)}, u32[]{:S(2)}) %all-to-all-start.1) | async-done | bytes 524320 | tf_op jit(solution)/shard_map/all_to_all | solution.py:518
  54.5 5.8 %shard_map.188 = (bf16[8,64,768]{2,1,0:T(8,128)(2,1)}, f32[8,32,768]{2,1,0:T(8,128)}, bf16[256,768]{1,0:T(8,128)(2,1)S(1)}, bf16[256,384]{1,0:T(8,128)(2,1)S(1)}, bf16[256,384]{1,0:T(8,128)(2,1)S(1)}) custom-call(bf16[8,128,256]{2,1,0:T(8,128)(2,1)S(1)} %all-to-all-done.1.mixed_ref, bf16[2,128,768]{2,1,0:T(8,128)(2,1)} %tok_ref.5, ...), custom_call_target="tpu_custom_call" | custom-call | flops 4000000000 | bytes 2000000 | tf_op jit(solution)/shard_map/pallas_call | solution.py:106
  64.2 3.5 %all-to-all-start.2 = ((bf16[8,64,768]{2,1,0:T(8,128)(2,1)}), bf16[8,64,768]{2,1,0:T(8,128)(2,1)S(1)}, u32[]{:S(2)}, u32[]{:S(2)}) async-start(bf16[8,64,768]{2,1,0:T(8,128)(2,1)} %get-tuple-element.55), calls=%async_computation.2 | async-start | bytes 1572864 | tf_op jit(solution)/shard_map/all_to_all | solution.py:518
  69.5 3.0 %collective-permute-start.4 = (bf16[2,48,768]{2,1,0:T(8,128)(2,1)}, bf16[2,48,768]{2,1,0:T(8,128)(2,1)S(1)}, u32[]{:S(2)}, u32[]{:S(2)}) collective-permute-start(bf16[2,48,768]{2,1,0:T(8,128)(2,1)} %get-tuple-element.64), channel_id=1, source_target_pairs={{0,96},{32,64},{64,32},{96,0},{1,97},{33,65},{65,33},{97,1},{2,98}... | collective-permute-start | bytes 442376 | tf_op jit(solution)/shard_map/ppermute | solution.py:538
  72.5 2.6 %collective-permute-done.2.refs_1_ = bf16[2,48,768]{2,1,0:T(8,128)(2,1)S(1)} collective-permute-done((bf16[2,48,768]{2,1,0:T(8,128)(2,1)}, bf16[2,48,768]{2,1,0:T(8,128)(2,1)S(1)}, u32[]{:S(2)}, u32[]{:S(2)}) %collective-permute-start.2) | collective-permute-done | bytes 147488 | tf_op jit(solution)/shard_map/ppermute | solution.py:538
  75.1 3.2 %collective-permute-done.3.refs_2_ = bf16[2,48,768]{2,1,0:T(8,128)(2,1)S(1)} collective-permute-done((bf16[2,48,768]{2,1,0:T(8,128)(2,1)}, bf16[2,48,768]{2,1,0:T(8,128)(2,1)S(1)}, u32[]{:S(2)}, u32[]{:S(2)}) %collective-permute-start.3) | collective-permute-done | bytes 147488 | tf_op jit(solution)/shard_map/ppermute | solution.py:538
  81.2 2.7 %all-to-all-done.2.refs_0_ = bf16[8,64,768]{2,1,0:T(8,128)(2,1)S(1)} async-done(((bf16[8,64,768]{2,1,0:T(8,128)(2,1)}), bf16[8,64,768]{2,1,0:T(8,128)(2,1)S(1)}, u32[]{:S(2)}, u32[]{:S(2)}) %all-to-all-start.2) | async-done | bytes 786464 | tf_op jit(solution)/shard_map/all_to_all | solution.py:518
  83.9 4.5 %shard_map.193 = (bf16[32,32,256]{2,1,0:T(8,128)(2,1)}, bf16[32,768]{1,0:T(8,128)(2,1)}, f32[32,768]{1,0:T(8,128)}, bf16[32,768]{1,0:T(8,128)(2,1)}, f32[8,768]{1,0:T(8,128)}) custom-call(bf16[8,64,768]{2,1,0:T(8,128)(2,1)S(1)} %shard_map.192.sums_ref, f32[8,32,768]{2,1,0:T(8,128)} %get-tuple-element.66.middle_ref, bf16[2,128,768]{2,1,0:T(8,128)(2,1)} %og_ref.5, ...), custom_call_target="tpu_custom_call" | custom-call | flops 1000000000 | bytes 2000000 | tf_op jit(solution)/shard_map/pallas_call | solution.py:106
  88.4 4.8 %all-to-all-start.3 = ((bf16[32,32,256]{2,1,0:T(8,128)(2,1)}), bf16[32,32,256]{2,1,0:T(8,128)(2,1)S(1)}, u32[]{:S(2)}, u32[]{:S(2)}) async-start(bf16[32,32,256]{2,1,0:T(8,128)(2,1)} %get-tuple-element.67), calls=%async_computation.3 | async-start | bytes 1048576 | tf_op jit(solution)/shard_map/all_to_all | solution.py:518
  94.5 3.3 %collective-permute-start.7 = (bf16[32,768]{1,0:T(8,128)(2,1)}, bf16[32,768]{1,0:T(8,128)(2,1)S(1)}, u32[]{:S(2)}, u32[]{:S(2)}) collective-permute-start(bf16[32,768]{1,0:T(8,128)(2,1)} %get-tuple-element.68.low0_ref), channel_id=1, source_target_pairs={{0,3},{1,2},{2,1},{3,0},{4,7},{5,6},{6,5},{7,4},{8,11},{9,10},{10,... | collective-permute-start | bytes 147464 | tf_op jit(solution)/shard_map/ppermute | solution.py:538
  104.3 3.7 %collective-permute-start.9 = (bf16[8,128,256]{2,1,0:T(8,128)(2,1)S(1)}, bf16[8,128,256]{2,1,0:T(8,128)(2,1)S(1)}, u32[]{:S(2)}, u32[]{:S(2)}) collective-permute-start(bf16[8,128,256]{2,1,0:T(8,128)(2,1)S(1)} %shard_map.195.gs_ref), channel_id=1, source_target_pairs={{0,8},{8,0},{1,9},{9,1},{2,10},{10,2},{3,11},{11,3},{4,12},{12,4},... | collective-permute-start | bytes 1572872 | tf_op jit(solution)/shard_map/ppermute | solution.py:522
  109.6 4.7 %shard_map.196 = (bf16[128,640]{1,0:T(8,128)(2,1)}, bf16[16,48,384]{2,1,0:T(8,128)(2,1)S(1)}, bf16[16,48,384]{2,1,0:T(8,128)(2,1)S(1)}) custom-call(s32[2,32]{1,0:T(2,128)S(1)} %copy-done.3, bf16[8,128,384]{2,1,0:T(8,128)(2,1)} %copy-done.1, bf16[8,128,384]{2,1,0:T(8,128)(2,1)} %copy-done.2, bf16[8,2,128,256]{3,2,1,0:T(8,128)(2,1)} %bitcast.9, ...), custom_call_target="tpu_custom_call" | custom-call | flops 8000000000 | bytes 2000000 | tf_op jit(solution)/shard_map/pallas_call | solution.py:106
  117.3 6.8 %all-to-all-start.4 = ((bf16[16,48,384]{2,1,0:T(8,128)(2,1)}), bf16[16,48,384]{2,1,0:T(8,128)(2,1)S(1)}, u32[]{:S(2)}, u32[]{:S(2)}) async-start(bf16[16,48,384]{2,1,0:T(8,128)(2,1)} %shard_map.200), calls=%async_computation.4 | async-start | bytes 1179648 | tf_op jit(solution)/shard_map/all_to_all | solution.py:518
  124.1 3.6 %shard_map.197 = (f32[32,768]{1,0:T(8,128)}, bf16[32,768]{1,0:T(8,128)(2,1)}, bf16[32,768]{1,0:T(8,128)(2,1)}, bf16[32,768]{1,0:T(8,128)(2,1)}) custom-call(bf16[128,640]{1,0:T(8,128)(2,1)} %get-tuple-element.71.gqkv_ref, bf16[768,2304]{1,0:T(8,128)(2,1)} %w_ref.3), custom_call_target="tpu_custom_call" | custom-call | flops 1000000000 | bytes 2000000 | tf_op jit(solution)/shard_map/pallas_call | solution.py:106
  129.4 2.5 %collective-permute-start.12 = (bf16[32,768]{1,0:T(8,128)(2,1)}, bf16[32,768]{1,0:T(8,128)(2,1)S(1)}, u32[]{:S(2)}, u32[]{:S(2)}) collective-permute-start(bf16[32,768]{1,0:T(8,128)(2,1)} %get-tuple-element.75), channel_id=1, source_target_pairs={{0,3},{1,2},{2,1},{3,0},{4,7},{5,6},{6,5},{7,4},{8,11},{9,10},{10,... | collective-permute-start | bytes 147464 | tf_op jit(solution)/shard_map/ppermute | solution.py:538
  133.3 3.1 %collective-permute-done.11.two_ref = bf16[32,768]{1,0:T(8,128)(2,1)S(1)} collective-permute-done((bf16[32,768]{1,0:T(8,128)(2,1)}, bf16[32,768]{1,0:T(8,128)(2,1)S(1)}, u32[]{:S(2)}, u32[]{:S(2)}) %collective-permute-start.11) | collective-permute-done | bytes 49184 | tf_op jit(solution)/shard_map/ppermute | solution.py:538
  136.4 2.7 %shard_map.198 = (bf16[64,768]{1,0:T(8,128)(2,1)}, f32[8,768]{1,0:T(8,128)}) custom-call(f32[32,768]{1,0:T(8,128)} %get-tuple-element.72.own_ref, bf16[32,768]{1,0:T(8,128)(2,1)S(1)} %collective-permute-done.10.one_ref, bf16[32,768]{1,0:T(8,128)(2,1)S(1)} %collective-permute-done.11.two_ref, bf16[32,768]{1,0:T(8,128)(2,1)S(1)} %collective-permute-done.12.three_ref, ...), custom_call_target="tpu_custom_call" | custom-call | flops 100000000 | bytes 2000000 | tf_op jit(solution)/shard_map/pallas_call | solution.py:106
  139.1 2.4 %shard_map.201 = bf16[8,8,56,384]{3,2,1,0:T(8,128)(2,1)} custom-call(bf16[16,48,384]{2,1,0:T(8,128)(2,1)S(1)} %all-to-all-done.4.in_ref, f32[8,768]{1,0:T(8,128)} %get-tuple-element.84.vec_ref), custom_call_target="tpu_custom_call" | custom-call | flops 100000000 | bytes 2000000 | tf_op jit(solution)/shard_map/pallas_call | solution.py:106
  141.6 8.7 %all-to-all-start.5 = ((bf16[64,56,384]{2,1,0:T(8,128)(2,1)}), bf16[64,56,384]{2,1,0:T(8,128)(2,1)S(1)}, u32[]{:S(2)}, u32[]{:S(2)}) async-start(bf16[64,56,384]{2,1,0:T(8,128)(2,1)} %bitcast.7), calls=%async_computation.5 | async-start | bytes 5505024 | tf_op jit(solution)/shard_map/all_to_all | solution.py:518
  151.0 4.7 %collective-permute-start.19 = (bf16[64,768]{1,0:T(8,128)(2,1)S(1)}, bf16[64,768]{1,0:T(8,128)(2,1)S(1)}, u32[]{:S(2)}, u32[]{:S(2)}) collective-permute-start(bf16[64,768]{1,0:T(8,128)(2,1)S(1)} %copy-done.5), channel_id=1, source_target_pairs={{0,7},{1,6},{2,5},{3,4},{4,3},{5,2},{6,1},{7,0},{8,15},{9,14},{10,... | collective-permute-start | bytes 294920 | tf_op jit(solution)/shard_map/ppermute | solution.py:538
  161.4 25.8 %collective-permute-done.19.refs_7_ = bf16[64,768]{1,0:T(8,128)(2,1)S(1)} collective-permute-done((bf16[64,768]{1,0:T(8,128)(2,1)S(1)}, bf16[64,768]{1,0:T(8,128)(2,1)S(1)}, u32[]{:S(2)}, u32[]{:S(2)}) %collective-permute-start.19) | collective-permute-done | bytes 98336 | tf_op jit(solution)/shard_map/ppermute | solution.py:538
  187.2 3.0 %collective-permute-done.18.refs_6_ = bf16[64,768]{1,0:T(8,128)(2,1)S(1)} collective-permute-done((bf16[64,768]{1,0:T(8,128)(2,1)S(1)}, bf16[64,768]{1,0:T(8,128)(2,1)S(1)}, u32[]{:S(2)}, u32[]{:S(2)}) %collective-permute-start.18) | collective-permute-done | bytes 98336 | tf_op jit(solution)/shard_map/ppermute | solution.py:538
  190.2 3.4 %collective-permute-start.13 = (bf16[64,768]{1,0:T(8,128)(2,1)S(1)}, bf16[64,768]{1,0:T(8,128)(2,1)S(1)}, u32[]{:S(2)}, u32[]{:S(2)}) collective-permute-start(bf16[64,768]{1,0:T(8,128)(2,1)S(1)} %copy-done.5), channel_id=1, source_target_pairs={{0,1},{1,0},{2,3},{3,2},{4,5},{5,4},{6,7},{7,6},{8,9},{9,8},{10,11... | collective-permute-start | bytes 294920 | tf_op jit(solution)/shard_map/ppermute | solution.py:538
  193.6 6.4 %all-gather.5.cloned.1.call-done.refs_8_.in_ref = bf16[768,768]{1,0:T(8,128)(2,1)} async-done(((bf16[48,768]{1,0:T(8,128)(2,1)}), bf16[768,768]{1,0:T(8,128)(2,1)}) %all-gather.5.cloned.1.call-update) | async-done | bytes 1179664 | tf_op jit(solution)/shard_map/all_gather | solution.py:598
  200.0 2.7 %shard_map.202 = (f32[768,384]{1,0:T(8,128)}, f32[384,768]{1,0:T(8,128)}) custom-call(bf16[768,768]{1,0:T(8,128)(2,1)} %all-gather.5.cloned.1.call-done.refs_8_.in_ref), custom_call_target="tpu_custom_call" | custom-call | flops 10000000 | bytes 2000000 | tf_op jit(solution)/shard_map/pallas_call | solution.py:106
  205.1 2.4 %shard_map.204 = (f32[768,2304]{1,0:T(8,128)}, f32[768,768]{1,0:T(8,128)}, f32[8,384]{1,0:T(8,128)S(1)}) custom-call(bf16[8,8,56,384]{3,2,1,0:T(8,128)(2,1)S(1)} %shard_map.203.in_ref), custom_call_target="tpu_custom_call" | custom-call | flops 100000000 | bytes 2000000 | tf_op jit(solution)/shard_map/pallas_call | solution.py:106
  207.5 2.4 %collective-permute-done.21.in_ref = bf16[8,8,56,384]{3,2,1,0:T(8,128)(2,1)S(1)} collective-permute-done((bf16[8,8,56,384]{3,2,1,0:T(8,128)(2,1)S(1)}, bf16[8,8,56,384]{3,2,1,0:T(8,128)(2,1)S(1)}, u32[]{:S(2)}, u32[]{:S(2)}) %collective-permute-start.21) | collective-permute-done | bytes 2752544 | tf_op jit(solution)/shard_map/ppermute | solution.py:522
  209.9 3.0 %shard_map.205 = (f32[768,2304]{1,0:T(8,128)}, f32[768,768]{1,0:T(8,128)}, f32[768]{0:T(1024)}, f32[768]{0:T(1024)}, f32[768]{0:T(1024)}, /*index=5*/f32[768]{0:T(1024)}) custom-call(bf16[8,8,56,384]{3,2,1,0:T(8,128)(2,1)S(1)} %collective-permute-done.21.in_ref, ...), custom_call_target="tpu_custom_call", output_to_operand_aliasing={{0}: (2, {}), {1}: (3, {})} | custom-call | flops 100000000 | bytes 2000000 | tf_op jit(solution)/shard_map/pallas_call | solution.py:106
  (64 shorter events, 38.3 us)
Async XLA Ops:
  7.2 25.6 %copy-start.3 = (s32[2,32]{1,0:T(2,128)S(1)}, s32[2,32]{1,0:T(2,128)}, u32[]{:S(2)}) copy-start(s32[2,32]{1,0:T(2,128)} %scene_ref.3) | copy-start | bytes 772
  29.0 3.8 %collective-permute-start = (bf16[8,128,384]{2,1,0:T(8,128)(2,1)S(1)}, bf16[8,128,384]{2,1,0:T(8,128)(2,1)S(1)}, u32[]{:S(2)}, u32[]{:S(2)}) collective-permute-start(bf16[8,128,384]{2,1,0:T(8,128)(2,1)S(1)} %all_to_all.30.same_ref.kvs_ref), channel_id=1, source_target_pairs={{0,8},{8,0},{1,9},{9,1},{2,10},{10,2},{3,11},{11,3},{4,12},{12,4},... | collective-permute-start | bytes 2359304 | tf_op jit(solution)/shard_map/ppermute | solution.py:522
  32.8 11.7 %copy-start.4 = (bf16[768,768]{1,0:T(8,128)(2,1)S(1)}, bf16[768,768]{1,0:T(8,128)(2,1)}, u32[]{:S(2)}) copy-start(bf16[768,768]{1,0:T(8,128)(2,1)} %param.16) | copy-start | bytes 3538948
  35.6 19.0 %all-to-all-start.1 = ((bf16[8,128,256]{2,1,0:T(8,128)(2,1)}), bf16[8,128,256]{2,1,0:T(8,128)(2,1)S(1)}, u32[]{:S(2)}, u32[]{:S(2)}) async-start(bf16[8,128,256]{2,1,0:T(8,128)(2,1)} %shard_map.187), calls=%async_computation.1 | async-start | bytes 1048576 | tf_op jit(solution)/shard_map/all_to_all | solution.py:518
  43.8 64.3 %all-gather.3.cloned.1.call-start = ((), (), s32[]{:S(2)}) async-start(), calls=%async_computation.6 | async-start | bytes 1114112 | tf_op jit(solution)/shard_map/all_gather | solution.py:565
  62.4 5.3 %collective-permute-start.1 = (bf16[8,48,768]{2,1,0:T(8,128)(2,1)S(1)}, bf16[8,48,768]{2,1,0:T(8,128)(2,1)S(1)}, u32[]{:S(2)}, u32[]{:S(2)}) collective-permute-start(bf16[8,48,768]{2,1,0:T(8,128)(2,1)S(1)} %get-tuple-element.60), channel_id=1, source_target_pairs={{0,8},{8,0},{1,9},{9,1},{2,10},{10,2},{3,11},{11,3},{4,12},{12,4},... | collective-permute-start | bytes 1769480 | tf_op jit(solution)/shard_map/ppermute | solution.py:522
  64.2 19.7 %all-to-all-start.2 = ((bf16[8,64,768]{2,1,0:T(8,128)(2,1)}), bf16[8,64,768]{2,1,0:T(8,128)(2,1)S(1)}, u32[]{:S(2)}, u32[]{:S(2)}) async-start(bf16[8,64,768]{2,1,0:T(8,128)(2,1)} %get-tuple-element.55), calls=%async_computation.2 | async-start | bytes 1572864 | tf_op jit(solution)/shard_map/all_to_all | solution.py:518
  68.6 6.5 %collective-permute-start.2 = (bf16[2,48,768]{2,1,0:T(8,128)(2,1)}, bf16[2,48,768]{2,1,0:T(8,128)(2,1)S(1)}, u32[]{:S(2)}, u32[]{:S(2)}) collective-permute-start(bf16[2,48,768]{2,1,0:T(8,128)(2,1)} %get-tuple-element.62), channel_id=1, source_target_pairs={{0,32},{32,0},{64,96},{96,64},{1,33},{33,1},{65,97},{97,65},{2,34}... | collective-permute-start | bytes 442376 | tf_op jit(solution)/shard_map/ppermute | solution.py:538
  68.6 9.7 %collective-permute-start.3 = (bf16[2,48,768]{2,1,0:T(8,128)(2,1)}, bf16[2,48,768]{2,1,0:T(8,128)(2,1)S(1)}, u32[]{:S(2)}, u32[]{:S(2)}) collective-permute-start(bf16[2,48,768]{2,1,0:T(8,128)(2,1)} %get-tuple-element.63), channel_id=1, source_target_pairs={{0,64},{32,96},{64,0},{96,32},{1,65},{33,97},{65,1},{97,33},{2,66}... | collective-permute-start | bytes 442376 | tf_op jit(solution)/shard_map/ppermute | solution.py:538
  69.5 10.0 %collective-permute-start.4 = (bf16[2,48,768]{2,1,0:T(8,128)(2,1)}, bf16[2,48,768]{2,1,0:T(8,128)(2,1)S(1)}, u32[]{:S(2)}, u32[]{:S(2)}) collective-permute-start(bf16[2,48,768]{2,1,0:T(8,128)(2,1)} %get-tuple-element.64), channel_id=1, source_target_pairs={{0,96},{32,64},{64,32},{96,0},{1,97},{33,65},{65,33},{97,1},{2,98}... | collective-permute-start | bytes 442376 | tf_op jit(solution)/shard_map/ppermute | solution.py:538
  88.4 15.9 %all-to-all-start.3 = ((bf16[32,32,256]{2,1,0:T(8,128)(2,1)}), bf16[32,32,256]{2,1,0:T(8,128)(2,1)S(1)}, u32[]{:S(2)}, u32[]{:S(2)}) async-start(bf16[32,32,256]{2,1,0:T(8,128)(2,1)} %get-tuple-element.67), calls=%async_computation.3 | async-start | bytes 1048576 | tf_op jit(solution)/shard_map/all_to_all | solution.py:518
  93.2 7.5 %collective-permute-start.8 = (bf16[48,768]{1,0:T(8,128)(2,1)S(1)}, bf16[48,768]{1,0:T(8,128)(2,1)S(1)}, u32[]{:S(2)}, u32[]{:S(2)}) collective-permute-start(bf16[48,768]{1,0:T(8,128)(2,1)S(1)} %copy-done.6), channel_id=1, source_target_pairs={{0,16},{16,0},{1,17},{17,1},{2,18},{18,2},{3,19},{19,3},{4,20},{20... | collective-permute-start | bytes 221192 | tf_op jit(solution)/shard_map/ppermute | solution.py:538
  94.5 9.7 %collective-permute-start.7 = (bf16[32,768]{1,0:T(8,128)(2,1)}, bf16[32,768]{1,0:T(8,128)(2,1)S(1)}, u32[]{:S(2)}, u32[]{:S(2)}) collective-permute-start(bf16[32,768]{1,0:T(8,128)(2,1)} %get-tuple-element.68.low0_ref), channel_id=1, source_target_pairs={{0,3},{1,2},{2,1},{3,0},{4,7},{5,6},{6,5},{7,4},{8,11},{9,10},{10,... | collective-permute-start | bytes 147464 | tf_op jit(solution)/shard_map/ppermute | solution.py:538
  97.8 6.4 %collective-permute-start.6 = (bf16[32,768]{1,0:T(8,128)(2,1)}, bf16[32,768]{1,0:T(8,128)(2,1)S(1)}, u32[]{:S(2)}, u32[]{:S(2)}) collective-permute-start(bf16[32,768]{1,0:T(8,128)(2,1)} %get-tuple-element.68.low0_ref), channel_id=1, source_target_pairs={{0,2},{1,3},{2,0},{3,1},{4,6},{5,7},{6,4},{7,5},{8,10},{9,11},{10,... | collective-permute-start | bytes 147464 | tf_op jit(solution)/shard_map/ppermute | solution.py:538
  98.1 6.2 %collective-permute-start.5 = (bf16[32,768]{1,0:T(8,128)(2,1)}, bf16[32,768]{1,0:T(8,128)(2,1)S(1)}, u32[]{:S(2)}, u32[]{:S(2)}) collective-permute-start(bf16[32,768]{1,0:T(8,128)(2,1)} %get-tuple-element.68.low0_ref), channel_id=1, source_target_pairs={{0,1},{1,0},{2,3},{3,2},{4,5},{5,4},{6,7},{7,6},{8,9},{9,8},{10,11... | collective-permute-start | bytes 147464 | tf_op jit(solution)/shard_map/ppermute | solution.py:538
  104.3 5.3 %collective-permute-start.9 = (bf16[8,128,256]{2,1,0:T(8,128)(2,1)S(1)}, bf16[8,128,256]{2,1,0:T(8,128)(2,1)S(1)}, u32[]{:S(2)}, u32[]{:S(2)}) collective-permute-start(bf16[8,128,256]{2,1,0:T(8,128)(2,1)S(1)} %shard_map.195.gs_ref), channel_id=1, source_target_pairs={{0,8},{8,0},{1,9},{9,1},{2,10},{10,2},{3,11},{11,3},{4,12},{12,4},... | collective-permute-start | bytes 1572872 | tf_op jit(solution)/shard_map/ppermute | solution.py:522
  114.3 2.0 collective-permute-start.20
  117.3 21.8 %all-to-all-start.4 = ((bf16[16,48,384]{2,1,0:T(8,128)(2,1)}), bf16[16,48,384]{2,1,0:T(8,128)(2,1)S(1)}, u32[]{:S(2)}, u32[]{:S(2)}) async-start(bf16[16,48,384]{2,1,0:T(8,128)(2,1)} %shard_map.200), calls=%async_computation.4 | async-start | bytes 1179648 | tf_op jit(solution)/shard_map/all_to_all | solution.py:518
  127.7 5.6 %collective-permute-start.10 = (bf16[32,768]{1,0:T(8,128)(2,1)}, bf16[32,768]{1,0:T(8,128)(2,1)S(1)}, u32[]{:S(2)}, u32[]{:S(2)}) collective-permute-start(bf16[32,768]{1,0:T(8,128)(2,1)} %get-tuple-element.73), channel_id=1, source_target_pairs={{0,1},{1,0},{2,3},{3,2},{4,5},{5,4},{6,7},{7,6},{8,9},{9,8},{10,11... | collective-permute-start | bytes 147464 | tf_op jit(solution)/shard_map/ppermute | solution.py:538
  128.8 7.6 %collective-permute-start.11 = (bf16[32,768]{1,0:T(8,128)(2,1)}, bf16[32,768]{1,0:T(8,128)(2,1)S(1)}, u32[]{:S(2)}, u32[]{:S(2)}) collective-permute-start(bf16[32,768]{1,0:T(8,128)(2,1)} %get-tuple-element.74), channel_id=1, source_target_pairs={{0,2},{1,3},{2,0},{3,1},{4,6},{5,7},{6,4},{7,5},{8,10},{9,11},{10,... | collective-permute-start | bytes 147464 | tf_op jit(solution)/shard_map/ppermute | solution.py:538
  129.4 7.0 %collective-permute-start.12 = (bf16[32,768]{1,0:T(8,128)(2,1)}, bf16[32,768]{1,0:T(8,128)(2,1)S(1)}, u32[]{:S(2)}, u32[]{:S(2)}) collective-permute-start(bf16[32,768]{1,0:T(8,128)(2,1)} %get-tuple-element.75), channel_id=1, source_target_pairs={{0,3},{1,2},{2,1},{3,0},{4,7},{5,6},{6,5},{7,4},{8,11},{9,10},{10,... | collective-permute-start | bytes 147464 | tf_op jit(solution)/shard_map/ppermute | solution.py:538
  141.6 9.5 %copy-start.5 = (bf16[64,768]{1,0:T(8,128)(2,1)S(1)}, bf16[64,768]{1,0:T(8,128)(2,1)}, u32[]{:S(2)}) copy-start(bf16[64,768]{1,0:T(8,128)(2,1)} %get-tuple-element.79.refs_0_) | copy-start | bytes 294916
  141.6 63.2 %all-to-all-start.5 = ((bf16[64,56,384]{2,1,0:T(8,128)(2,1)}), bf16[64,56,384]{2,1,0:T(8,128)(2,1)S(1)}, u32[]{:S(2)}, u32[]{:S(2)}) async-start(bf16[64,56,384]{2,1,0:T(8,128)(2,1)} %bitcast.7), calls=%async_computation.5 | async-start | bytes 5505024 | tf_op jit(solution)/shard_map/all_to_all | solution.py:518
  150.3 49.8 %all-gather.5.cloned.1.call-start = ((), (), s32[]{:S(2)}) async-start(), calls=%async_computation.7 | async-start | bytes 1253376 | tf_op jit(solution)/shard_map/all_gather | solution.py:598
  151.0 36.2 %collective-permute-start.19 = (bf16[64,768]{1,0:T(8,128)(2,1)S(1)}, bf16[64,768]{1,0:T(8,128)(2,1)S(1)}, u32[]{:S(2)}, u32[]{:S(2)}) collective-permute-start(bf16[64,768]{1,0:T(8,128)(2,1)S(1)} %copy-done.5), channel_id=1, source_target_pairs={{0,7},{1,6},{2,5},{3,4},{4,3},{5,2},{6,1},{7,0},{8,15},{9,14},{10,... | collective-permute-start | bytes 294920 | tf_op jit(solution)/shard_map/ppermute | solution.py:538
  155.7 34.5 %collective-permute-start.18 = (bf16[64,768]{1,0:T(8,128)(2,1)S(1)}, bf16[64,768]{1,0:T(8,128)(2,1)S(1)}, u32[]{:S(2)}, u32[]{:S(2)}) collective-permute-start(bf16[64,768]{1,0:T(8,128)(2,1)S(1)} %copy-done.5), channel_id=1, source_target_pairs={{0,6},{1,7},{2,4},{3,5},{4,2},{5,3},{6,0},{7,1},{8,14},{9,15},{10,... | collective-permute-start | bytes 294920 | tf_op jit(solution)/shard_map/ppermute | solution.py:538
  156.0 46.8 %collective-permute-start.17 = (bf16[64,768]{1,0:T(8,128)(2,1)S(1)}, bf16[64,768]{1,0:T(8,128)(2,1)S(1)}, u32[]{:S(2)}, u32[]{:S(2)}) collective-permute-start(bf16[64,768]{1,0:T(8,128)(2,1)S(1)} %copy-done.5), channel_id=1, source_target_pairs={{0,5},{1,4},{2,7},{3,6},{4,1},{5,0},{6,3},{7,2},{8,13},{9,12},{10,... | collective-permute-start | bytes 294920 | tf_op jit(solution)/shard_map/ppermute | solution.py:538
  157.5 45.3 %collective-permute-start.16 = (bf16[64,768]{1,0:T(8,128)(2,1)S(1)}, bf16[64,768]{1,0:T(8,128)(2,1)S(1)}, u32[]{:S(2)}, u32[]{:S(2)}) collective-permute-start(bf16[64,768]{1,0:T(8,128)(2,1)S(1)} %copy-done.5), channel_id=1, source_target_pairs={{0,4},{1,5},{2,6},{3,7},{4,0},{5,1},{6,2},{7,3},{8,12},{9,13},{10,... | collective-permute-start | bytes 294920 | tf_op jit(solution)/shard_map/ppermute | solution.py:538
  159.2 43.6 %collective-permute-start.15 = (bf16[64,768]{1,0:T(8,128)(2,1)S(1)}, bf16[64,768]{1,0:T(8,128)(2,1)S(1)}, u32[]{:S(2)}, u32[]{:S(2)}) collective-permute-start(bf16[64,768]{1,0:T(8,128)(2,1)S(1)} %copy-done.5), channel_id=1, source_target_pairs={{0,3},{1,2},{2,1},{3,0},{4,7},{5,6},{6,5},{7,4},{8,11},{9,10},{10,... | collective-permute-start | bytes 294920 | tf_op jit(solution)/shard_map/ppermute | solution.py:538
  187.2 15.6 %collective-permute-start.14 = (bf16[64,768]{1,0:T(8,128)(2,1)S(1)}, bf16[64,768]{1,0:T(8,128)(2,1)S(1)}, u32[]{:S(2)}, u32[]{:S(2)}) collective-permute-start(bf16[64,768]{1,0:T(8,128)(2,1)S(1)} %copy-done.5), channel_id=1, source_target_pairs={{0,2},{1,3},{2,0},{3,1},{4,6},{5,7},{6,4},{7,5},{8,10},{9,11},{10,... | collective-permute-start | bytes 294920 | tf_op jit(solution)/shard_map/ppermute | solution.py:538
  190.2 12.6 %collective-permute-start.13 = (bf16[64,768]{1,0:T(8,128)(2,1)S(1)}, bf16[64,768]{1,0:T(8,128)(2,1)S(1)}, u32[]{:S(2)}, u32[]{:S(2)}) collective-permute-start(bf16[64,768]{1,0:T(8,128)(2,1)S(1)} %copy-done.5), channel_id=1, source_target_pairs={{0,1},{1,0},{2,3},{3,2},{4,5},{5,4},{6,7},{7,6},{8,9},{9,8},{10,11... | collective-permute-start | bytes 294920 | tf_op jit(solution)/shard_map/ppermute | solution.py:538
  204.8 5.1 %collective-permute-start.21 = (bf16[8,8,56,384]{3,2,1,0:T(8,128)(2,1)S(1)}, bf16[8,8,56,384]{3,2,1,0:T(8,128)(2,1)S(1)}, u32[]{:S(2)}, u32[]{:S(2)}) collective-permute-start(bf16[8,8,56,384]{3,2,1,0:T(8,128)(2,1)S(1)} %shard_map.203.in_ref), channel_id=1, source_target_pairs={{0,8},{8,0},{1,9},{9,1},{2,10},{10,2},{3,11},{11,3},{4,12},{12,4},... | collective-permute-start | bytes 8257544 | tf_op jit(solution)/shard_map/ppermute | solution.py:522
  (4 other events, 24.5 us)
Sparse Core Ops, SparseCore 0:
  46.3 33.3 all-gather.2
  152.8 47.1 all-gather.4

commit v5 on v4

--- a/solution.py
+++ b/solution.py
@@ -144,7 +144,7 @@
 
 
 def project_kernel(
-    tok_ref, gain_ref, shift_ref, w_ref, kv_ref, q_ref, normed_ref,
+    tok_ref, gain_ref, shift_ref, w_ref, kv_ref, normed_ref,
     x_buf, w_buf, kv_buf, gain_buf, shift_buf, x_sem, w_sem, kv_sem, gain_sem, shift_sem,
 ):
     copy_x = pltpu.make_async_copy(tok_ref.at[lax.axis_index(MICRO)], x_buf, x_sem)
@@ -164,22 +164,21 @@
         full = mm(normed, w_buf[slot])
         return jnp.where(odd, full[:, 192:], full[:, :192]).astype(BF)
 
-    kv_buf[...] = jnp.concatenate([part(0), part(1)], axis=1)
+    kv_buf[...] = jnp.concatenate([part(0), part(1), part(2), jnp.zeros((TOK, HD), BF)], axis=1)
     sends = send_copies(kv_buf, kv_ref, range(8), kv_sem)
     normed_ref[...] = normed
-    q_ref[...] = jnp.concatenate([part(2), jnp.zeros((TOK, HD), BF)], axis=1)
     wait_all(sends)
 
 
-def attend_kernel(scene_ref, q_ref, same_ref, other_ref, out_ref, buf, sem):
+def attend_kernel(scene_ref, same_ref, other_ref, out_ref, buf, sem):
     first, big = span(scene_ref)
 
     def run(count):
         rows = count * TOK
         keys = jnp.concatenate(
-            [ref[pl.ds(first, count)].reshape(rows, 384) for ref in (same_ref, other_ref)], axis=0
+            [ref[pl.ds(first, count), :, :384].reshape(rows, 384) for ref in (same_ref, other_ref)], axis=0
         )
-        query = q_ref[...]
+        query = same_ref[chip_index(), :, 384:]
         q0, q1 = halves(query[:, :128])
         blocks = [keys[:, :128], keys[:, 128:256], keys[:, 256:]]
         mixed = []
@@ -271,26 +270,33 @@
 
 
 def middle_kernel(
-    sums_ref, middle_ref, og_ref, mixed_ref, wo_ref, gain_ref,
-    out_ref, low_ref, grad_ref, result_ref, vec_ref, buf, sem,
+    sums_ref, middle_ref, og_ref, tok_ref, mixed_ref, wo_ref, gain_ref,
+    out_ref, low_ref, grad_ref, result_ref, vec_ref, x_ref, buf, middle_buf, og_buf, mixed_buf, x_sem, in_sem, sem,
 ):
     micro = lax.axis_index(MICRO)
     group = group_index()
-    start = pl.multiple_of(group * BLK, BLK)
+    block = pl.ds(pl.multiple_of(group * BLK, BLK), BLK)
+    loads = [
+        pltpu.make_async_copy(middle_ref.at[micro * 4 + group], middle_buf, in_sem.at[0]),
+        pltpu.make_async_copy(og_ref.at[micro, block], og_buf, in_sem.at[1]),
+        pltpu.make_async_copy(mixed_ref.at[pl.ds(micro * 4, 4), block], mixed_buf, in_sem.at[2]),
+        pltpu.make_async_copy(tok_ref.at[micro, block], x_ref, x_sem),
+    ]
+    for load in loads:
+        load.start()
     total = sums_ref[0].astype(F32)
     for index in range(1, 8):
         total = total + sums_ref[index].astype(F32)
     branch, grad = total[:BLK], total[BLK:]
-    middle = middle_ref[micro * 4 + group]
+    wait_all(loads)
+    middle = middle_buf[...]
     unit, inverse = normalized(middle)
-    grad_mid = og_ref[micro, pl.ds(start, BLK)].astype(F32) + norm_back(
-        grad, unit, inverse, gain_ref[...].reshape(1, D)
-    )
+    grad_mid = og_buf[...].astype(F32) + norm_back(grad, unit, inverse, gain_ref[...].reshape(1, D))
     low = grad_mid.astype(BF)
     lane = lax.broadcasted_iota(jnp.int32, (BLK, 256), 1)
     sends = []
     for head_group in range(4):
-        mixed = mixed_ref[micro * 4 + head_group, pl.ds(start, BLK)].astype(F32)
+        mixed = mixed_buf[head_group].astype(F32)
         back = mm_nt(low, wo_ref[head_group]).astype(BF).astype(F32)
         product = mixed * back
         columns = []
@@ -312,8 +318,9 @@
 
 
 def attend_back_kernel(
-    scene_ref, kvs_ref, kvo_ref, q_ref, gs_ref, go_ref, normed_ref, mixed_ref, low0_ref, low1_ref, low2_ref,
-    low3_ref, gqkv_ref, keep_ref, send_ref, grad_buf,
+    scene_ref, kvs_ref, kvo_ref, gs_ref, go_ref, normed_ref, mixed_ref, low0_ref, low1_ref, low2_ref, low3_ref, w_ref,
+    own_ref, one_ref, two_ref, three_ref, keep_ref, send_ref,
+    kv_buf, gqkv_buf, grad_buf, part_buf, mixed_buf, w_buf, kv_sem, mixed_sem, w_sem,
 ):
     first, big = span(scene_ref)
     chip = chip_index()
@@ -323,29 +330,30 @@
 
     def run(count):
         rows = count * TOK
+        loads = [
+            pltpu.make_async_copy(ref.at[pl.ds(first, count)], kv_buf.at[slot, pl.ds(0, count)], kv_sem.at[slot])
+            for slot, ref in enumerate((kvs_ref, kvo_ref))
+        ]
+        for load in loads:
+            load.start()
 
         def cut(value):
             return [value[:, at:at + 128] for at in range(0, value.shape[1], 128)]
 
-        def gathered(one, two, width):
-            return cut(jnp.concatenate(
-                [ref[pl.ds(first, count)].reshape(rows, width) for ref in (one, two)], axis=0
-            ))
-
-        kv = gathered(kvs_ref, kvo_ref, 384)
-        grad = gathered(gs_ref, go_ref, 256)
-        query = cut(jnp.concatenate(
-            [q_ref[pl.ds(first, count), which].reshape(rows, 256) for which in (core, 1 - core)], axis=0
+        grad = cut(jnp.concatenate(
+            [ref[pl.ds(first, count)].reshape(rows, 256) for ref in (gs_ref, go_ref)], axis=0
         ))
-        kv_own = cut(kvs_ref[chip])
-        q_own = cut(q_ref[chip, core])
         g_own = cut(gs_ref[chip])
-        q_heads = [*halves(q_own[0]), q_own[1]]
         g_heads = [halves(g_own[0])[1], *halves(g_own[1])]
-        k_heads = [*halves(kv_own[0]), halves(kv_own[1])[0]]
-        v_heads = [halves(kv_own[1])[1], *halves(kv_own[2])]
         own_stats = g_own[0].astype(F32)
         all_stats = grad[0].astype(F32).T
+        wait_all(loads)
+        every = cut(jnp.concatenate([kv_buf[slot, :count].reshape(rows, 640) for slot in range(2)], axis=0))
+        kv, query = every[:3], every[3:]
+        own = cut(kv_buf[0, chip - first])
+        q_heads = [*halves(own[3]), own[4]]
+        k_heads = [*halves(own[0]), halves(own[1])[0]]
+        v_heads = [halves(own[1])[1], *halves(own[2])]
 
         def column(at):
             return own_stats[:, at:at + 1] + own_stats[:, at + 1:at + 2] + own_stats[:, at + 2:at + 3]
@@ -364,12 +372,17 @@
             dv.append(mm(probs.astype(BF), grad[gb]))
             dk.append(mm((probs * gap).astype(BF), query[qb]) * scale)
         tail = dq[2]
-        gqkv_ref[...] = jnp.concatenate(
+        gqkv_buf[...] = jnp.concatenate(
             [join(dk[0], dk[1]), join(dk[2], dv[0]), join(dv[1], dv[2]), join(dq[0], dq[1]),
              join(tail, jnp.zeros_like(tail))],
             axis=1,
         ).astype(BF)
 
+    index = lax.axis_index(MICRO) * 4 + group
+    load_mixed = pltpu.make_async_copy(mixed_ref.at[index], mixed_buf, mixed_sem)
+    load_mixed.start()
+    loads = weight_copies(w_ref, w_buf, w_sem)
+
     @pl.when(big)
     def _():
         run(5)
@@ -378,11 +391,11 @@
     def _():
         run(1)
 
-    grad_buf[...] = mm_tn(normed_ref[...], gqkv_ref[...])
-    index = lax.axis_index(MICRO) * 4 + group
+    grad_buf[...] = mm_tn(normed_ref[...], gqkv_buf[...])
+    load_mixed.wait()
     low = jnp.concatenate([ref[...] for ref in (low0_ref, low1_ref, low2_ref, low3_ref)], axis=0)
     mixed = jnp.concatenate(
-        [mixed_ref[index, pl.ds(pl.multiple_of((group ^ k) * BLK, BLK), BLK)] for k in range(4)], axis=0
+        [mixed_buf[pl.ds(pl.multiple_of((group ^ k) * BLK, BLK), BLK)] for k in range(4)], axis=0
     )
     out = mm_tn(mixed, low)[HD:]
     for ref, owner in ((keep_ref, core), (send_ref, 1 - core)):
@@ -396,6 +409,21 @@
             ref[2 * tile + 1] = jnp.concatenate(
                 [rows[:, 384:576], jnp.where(owner == 1, pieces[1], pieces[0])], axis=1
             ).astype(BF)
+
+    odd = (group % 2) == 1
+    total = jnp.zeros((TOK, D), F32)
+    for slot in range(3):
+        loads[slot].wait()
+        part = gqkv_buf[:, slot * 192:(slot + 1) * 192]
+        zero = jnp.zeros_like(part)
+        wide = jnp.where(
+            odd, jnp.concatenate([zero, part], axis=1), jnp.concatenate([part, zero], axis=1)
+        )
+        total = total + mm_nt(wide, w_buf[slot])
+    part_buf[...] = total
+    own_ref[...] = part_buf[pl.ds(pl.multiple_of(group * BLK, BLK), BLK)]
+    for k, ref in ((1, one_ref), (2, two_ref), (3, three_ref)):
+        ref[...] = part_buf[pl.ds(pl.multiple_of((group ^ k) * BLK, BLK), BLK)].astype(BF)
 
 
 def add_kernel(one_ref, two_ref, out_ref, buf, sem):
@@ -455,46 +483,34 @@
     wait_all(copies)
 
 
-def spread_ff_kernel(in_ref, up_ref, down_ref):
-    up_ref[...] = in_ref[:, :384].astype(F32)
-    for tile in range(16):
-        half = (tile % 2) * 384
-        down_ref[(tile // 2) * 48:(tile // 2 + 1) * 48, half:half + 384] = in_ref[
-            tile * 48:(tile + 1) * 48, 384:
-        ].astype(F32)
-
-
-def normed_grad_kernel(gqkv_ref, w_ref, own_ref, one_ref, two_ref, three_ref, w_buf, buf, w_sem):
-    copies = weight_copies(w_ref, w_buf, w_sem)
-    group = group_index()
-    odd = (group % 2) == 1
-    total = jnp.zeros((TOK, D), F32)
-    for slot in range(3):
-        copies[slot].wait()
-        part = gqkv_ref[:, slot * 192:(slot + 1) * 192]
-        zero = jnp.zeros_like(part)
-        wide = jnp.where(
-            odd, jnp.concatenate([zero, part], axis=1), jnp.concatenate([part, zero], axis=1)
-        )
-        total = total + mm_nt(wide, w_buf[slot])
-    buf[...] = total
-    own_ref[...] = buf[pl.ds(pl.multiple_of(group * BLK, BLK), BLK)]
-    for k, ref in ((1, one_ref), (2, two_ref), (3, three_ref)):
-        ref[...] = buf[pl.ds(pl.multiple_of((group ^ k) * BLK, BLK), BLK)].astype(BF)
+def stack_kernel(*refs):
+    y = lax.axis_index("y")
+    for k, ref in enumerate(refs[:4]):
+        refs[4][y ^ k] = ref[...]
+
+
+def spread_ff_kernel(*refs):
+    up_ref, down_ref = refs[4:]
+    xl, core = lax.axis_index("xl"), lax.axis_index(CORE)
+    for index, ref in enumerate(refs[:4]):
+        chip_xl = xl ^ (index % 2)
+        owner = core ^ (index // 2)
+        for y in range(4):
+            chip = y * 2 + chip_xl
+            block = ref[y].astype(F32)
+            up_ref[pl.ds(pl.multiple_of((chip * 2 + owner) * 48, 16), 48)] = block[:, :384]
+            down_ref[
+                pl.ds(pl.multiple_of(chip * 48, 16), 48), pl.ds(pl.multiple_of(owner * 384, 128), 384)
+            ] = block[:, 384:]
 
 
 def input_kernel(
-    own_ref, one_ref, two_ref, three_ref, tok_ref, gain_ref, grad_ref, result_ref, vec_ref, out_ref, sums_ref,
-    x_buf, sem,
+    own_ref, one_ref, two_ref, three_ref, x_ref, gain_ref, grad_ref, result_ref, vec_ref, out_ref, sums_ref
 ):
-    start = pl.multiple_of(group_index() * BLK, BLK)
-    copy = pltpu.make_async_copy(tok_ref.at[lax.axis_index(MICRO), pl.ds(start, BLK)], x_buf, sem)
-    copy.start()
     total = own_ref[...]
     for ref in (one_ref, two_ref, three_ref):
         total = total + ref[...].astype(F32)
-    copy.wait()
-    unit, inverse = normalized(x_buf[...].astype(F32))
+    unit, inverse = normalized(x_ref[...].astype(F32))
     grad = grad_ref[...] + norm_back(total, unit, inverse, gain_ref[...].reshape(1, D))
     gain1 = jnp.sum(total * unit, axis=0, keepdims=True)
     shift1 = jnp.sum(total, axis=0, keepdims=True)
@@ -504,7 +520,7 @@
 
 
 def unpack_kernel(*refs):
-    parts, (grad_ref, result_ref) = refs[:8], refs[9:]
+    parts, (grad_ref, result_ref) = refs[:8], refs[8:]
     micro = lax.axis_index(MICRO)
     group = group_index()
     for k, ref in enumerate(parts):
@@ -542,13 +558,13 @@
     tokens, scene_of_block, ln1_gain, ln1_shift, w_qkv, w_out, ln2_gain, ln2_shift, w_up, w_down, out_grad
 ):
     w_out_pad = jnp.pad(w_out.reshape(4, 192, D), ((0, 0), (HD, 0), (0, 0)))
-    kv_send, query, normed = call(
+    kv_send, normed = call(
         project_kernel,
-        [((8, TOK, 384), BF, "H"), ((TOK, 256), BF, "L"), ((TOK, D), BF, "L")],
+        [((8, TOK, 640), BF, "H"), ((TOK, D), BF, "L")],
         [(tokens, "H"), (ln1_gain, "H"), (ln1_shift, "H"), (w_qkv, "H")],
         10**9,
         [
-            pltpu.VMEM((TOK, D), BF), pltpu.VMEM((3, D, 384), BF), pltpu.VMEM((TOK, 384), BF),
+            pltpu.VMEM((TOK, D), BF), pltpu.VMEM((3, D, 384), BF), pltpu.VMEM((TOK, 640), BF),
             pltpu.VMEM((D,), F32), pltpu.VMEM((D,), F32), DMA, DMA((3,)), DMA((8,)), DMA, DMA,
         ],
     )
@@ -557,12 +573,11 @@
     (mixed_send,) = call(
         attend_kernel,
         [((8, TOK, 256), BF, "H")],
-        [(scene_of_block, "S"), (query, "L"), (kv_same, "V"), (kv_other, "V")],
+        [(scene_of_block, "S"), (kv_same, "V"), (kv_other, "V")],
         2 * 10**9,
         [pltpu.VMEM((TOK, 256), BF), DMA((8,))],
     )
     mixed = exchange(mixed_send, NARROW)
-    queries = lax.all_gather(query, WIDE, axis=0, tiled=True).reshape(8, 2, TOK, 256)
     ff_send, middle, normed2, act, grad_pre = call(
         forward_kernel,
         [
@@ -570,8 +585,8 @@
             ((2 * TOK, FFL), BF, "V"), ((2 * TOK, FFL), BF, "V"),
         ],
         [
-            (mixed, "V"), (tokens, "L"), (out_grad, "L"), (w_out_pad, "L"), (ln2_gain, "L"), (ln2_shift, "L"),
-            (w_up, "L"), (w_down, "L"),
+            (mixed, "V"), (tokens, "V"), (out_grad, "V"), (w_out_pad, "V"), (ln2_gain, "L"), (ln2_shift, "L"),
+            (w_up, "V"), (w_down, "V"),
         ],
         4 * 10**9,
         [pltpu.VMEM((8, BLK, D), BF), pltpu.VMEM((8, BLK, D), BF), DMA((2,))],
@@ -589,36 +604,50 @@
     )
     pieces = [pieces[0]] + [flip(pieces[k], "y", 4, k) for k in (1, 2, 3)]
     keep, send = call(
-        halve_kernel, [((48, D), BF, "L")] * 2, [(pieces[0], "L")] + [(piece, "V") for piece in pieces[1:]], 10**8
+        halve_kernel,
+        [((48, D), BF, "L")] * 2,
+        [(pieces[0], "L")] + [(piece, "V") for piece in pieces[1:]],
+        10**8,
     )
     ff_sums = after(ff_sums, pin(keep))
+    grad_send, low, grad_mid, result_part, vec2, x_part = call(
+        middle_kernel,
+        [
+            ((32, BLK, 256), BF, "H"), ((BLK, D), BF, "L"), ((BLK, D), F32, "L"), ((BLK, D), BF, "L"),
+            ((8, D), F32, "L"), ((BLK, D), BF, "L"),
+        ],
+        [
+            (ff_sums, "V"), (middle, "H"), (out_grad, "H"), (tokens, "H"), (mixed, "H"), (w_out_pad, "V"),
+            (ln2_gain, "L"),
+        ],
+        10**9,
+        [
+            pltpu.VMEM((4, BLK, 256), BF), pltpu.VMEM((BLK, D), F32), pltpu.VMEM((BLK, D), BF),
+            pltpu.VMEM((4, BLK, 256), BF), DMA, DMA((3,)), DMA((32,)),
+        ],
+    )
     (ff_part,) = call(
         pair_kernel, [((48, D), BF, "L")], [(keep, "L"), (flip(send, "xl", 2, 1), "V")], 10**7
     )
-    ff_all = lax.all_gather(ff_part, WIDE, axis=0, tiled=True)
-    grad_send, low, grad_mid, result_part, vec2 = call(
-        middle_kernel,
-        [
-            ((32, BLK, 256), BF, "H"), ((BLK, D), BF, "L"), ((BLK, D), F32, "L"), ((BLK, D), BF, "L"),
-            ((8, D), F32, "L"),
-        ],
-        [(ff_sums, "V"), (middle, "L"), (out_grad, "L"), (mixed, "L"), (w_out_pad, "L"), (ln2_gain, "L")],
-        10**9,
-        [pltpu.VMEM((4, BLK, 256), BF), DMA((32,))],
-    )
+    ff_parts = [flip(ff_part, "y", 4, k) for k in (1, 2, 3)]
     grad_same = exchange(grad_send, (*CHIP, *GROUP)).reshape(8, TOK, 256)
     lows = [flip(low, GROUP, 4, k) for k in (1, 2, 3)]
-    grad_same = after(grad_same, *lows, pin(ff_part))
+    grad_same = after(grad_same, *lows, *ff_parts)
     grad_other = swap(grad_same)
-    gqkv, keep, send = call(
+    own, *sends, keep, send = call(
         attend_back_kernel,
-        [((TOK, 640), BF, "L"), ((16, 48, 384), BF, "V"), ((16, 48, 384), BF, "V")],
-        [
-            (scene_of_block, "S"), (kv_same, "L"), (kv_other, "L"), (queries, "L"), (grad_same, "V"),
-            (grad_other, "V"), (normed, "L"), (mixed, "L"), (low, "L"), *[(value, "V") for value in lows],
+        [((BLK, D), F32, "L")] + [((BLK, D), BF, "L")] * 3 + [((16, 48, 384), BF, "V")] * 2,
+        [
+            (scene_of_block, "S"), (kv_same, "H"), (kv_other, "H"), (grad_same, "V"), (grad_other, "V"),
+            (normed, "L"), (mixed, "H"), (low, "L"), *[(value, "V") for value in lows], (w_qkv, "H"),
         ],
         8 * 10**9,
-        [pltpu.VMEM((D, 640), F32)],
+        [
+            pltpu.VMEM((2, 5, TOK, 640), BF), pltpu.VMEM((TOK, 640), BF), pltpu.VMEM((D, 640), F32),
+            pltpu.VMEM((TOK, D), F32), pltpu.VMEM((TOK, 256), BF), pltpu.VMEM((3, D, 384), BF),
+            DMA((2,)), DMA, DMA((3,)),
+        ],
+        vmem=24,
     )
     (weight_send,) = call(
         add_kernel,
@@ -627,32 +656,25 @@
         10**8,
         [pltpu.VMEM((16, 48, 384), BF), DMA],
     )
+    parts = [flip(value, GROUP, 4, k + 1) for k, value in enumerate(sends)]
     weight_parts = exchange(weight_send, (*CHIP, MICRO))
-    own, *sends = call(
-        normed_grad_kernel,
-        [((BLK, D), F32, "L")] + [((BLK, D), BF, "L")] * 3,
-        [(gqkv, "L"), (w_qkv, "H")],
-        10**9,
-        [pltpu.VMEM((3, D, 384), BF), pltpu.VMEM((TOK, D), F32), DMA((3,))],
-    )
-    parts = [flip(value, GROUP, 4, k + 1) for k, value in enumerate(sends)]
+    (ff_near,) = call(
+        stack_kernel,
+        [((4, 48, D), BF, "L")],
+        [(ff_part, "L"), *[(value, "V") for value in ff_parts]],
+        10**7,
+    )
+    ff_far = flip(ff_near, "xl", 2, 1)
     packed, sums = call(
         input_kernel,
         [((2 * BLK, D), BF, "L"), ((8, D), F32, "L")],
         [
-            (own, "L"), *[(value, "V") for value in parts], (tokens, "H"), (ln1_gain, "L"), (grad_mid, "L"),
+            (own, "L"), *[(value, "V") for value in parts], (x_part, "L"), (ln1_gain, "L"), (grad_mid, "L"),
             (result_part, "L"), (vec2, "L"),
         ],
         10**8,
-        [pltpu.VMEM((BLK, D), BF), DMA],
-    )
-    everyone = [packed] + [flip(packed, NARROW, 8, k) for k in range(1, 8)]
-    input_grad, result = call(
-        unpack_kernel,
-        [((2, TOK, D), F32, "L"), ((2, TOK, D), BF, "L")],
-        [(packed, "L"), *[(value, "V") for value in everyone[1:]], (ff_all, "H")],
-        10**8,
-    )
+    )
+    weight_parts = after(weight_parts, ff_far, pin(sums))
     (weight_total,) = call(
         sum_kernel,
         [((8, 8, 56, 384), BF, "H")],
@@ -660,10 +682,20 @@
         10**8,
         [pltpu.VMEM((8, 56, 384), BF), DMA((8,))],
     )
+    everyone = [packed] + [flip(packed, NARROW, 8, k) for k in range(1, 8)]
+    input_grad, result = call(
+        unpack_kernel,
+        [((2, TOK, D), F32, "L"), ((2, TOK, D), BF, "L")],
+        [(packed, "L"), *[(value, "V") for value in everyone[1:]]],
+        10**8,
+    )
+    up_grad, down_grad = call(
+        spread_ff_kernel,
+        [((D, FFL), F32, "L"), ((FFL, D), F32, "L")],
+        [(ff_near, "L"), (ff_far, "V"), (swap(ff_near), "V"), (swap(ff_far), "V")],
+        10**7,
+    )
     weight_same = exchange(weight_total.reshape(64, 56, 384), (*CHIP, *NARROW)).reshape(8, 8, 56, 384)
-    up_grad, down_grad = call(
-        spread_ff_kernel, [((D, FFL), F32, "L"), ((FFL, D), F32, "L")], [(ff_all, "L")], 10**7
-    )
     weight_same = after(weight_same, *map(pin, (input_grad, result, up_grad, down_grad)))
     weight_other = swap(weight_same)
     scratch = [
@@ -671,7 +703,11 @@
     ]
     grads = [((D, 3 * D), F32, "H"), ((D, D), F32, "H")]
     half = call(
-        functools.partial(spread_kernel, False), grads + [((8, 384), F32, "V")], [(weight_same, "V")], 10**8, scratch
+        functools.partial(spread_kernel, False),
+        grads + [((8, 384), F32, "V")],
+        [(weight_same, "V")],
+        10**8,
+        scratch,
     )
     qkv_grad, out_proj_grad, *vectors = call(
         functools.partial(spread_kernel, True),

time: 221 us -> 229 us (1.036)
  between operations: 14.3 us -> 1.08 us
  starting transfers between devices: 67.4 us -> 78.6 us
  blocking collectives: 18 us -> 23.7 us
  local copies, waits for them, and re-layouts: 1.28 us -> 5.65 us
    ppermute x17 -> x21, waiting for transfers between devices: 44.5 us -> 53.1 us  [flip(): lax.ppermute(value, axes, [(index, index ^ bits) for index in range(count)])]
    ppermute x17 -> x21, starting transfers between devices: 27.3 us -> 33.9 us  [flip(): lax.ppermute(value, axes, [(index, index ^ bits) for index in range(count)])]
    all_gather x2 -> x0, waiting for transfers between devices: 6.42 us -> none  [the longest x1 6.42 us: shards(): ff_all = lax.all_gather(ff_part, WIDE, axis=0, tiled=True)]
    all_to_all x1, blocking collectives: 18 us -> 23.7 us  [exchange(): return lax.all_to_all(value, axes, 0, 0, tiled=True)]
    ppermute x5 -> x7, starting transfers between devices: 8.03 us -> 13.5 us  [swap(): return lax.ppermute(value, CORE, [(0, 1), (1, 0)])]
    unnamed x14 -> x28, local copies, waits for them, and re-layouts: 0.03 us -> 4.28 us
    ppermute x5 -> x7, waiting for transfers between devices: 7.48 us -> 8.11 us  [swap(): return lax.ppermute(value, CORE, [(0, 1), (1, 0)])]
  transfers between devices with their start and end apart: 29 -> 33, of which waited for: 17 -> 15; matrix products, arithmetic and copies ran while one was open for 1% -> 1% of each run, Pallas kernels for 14% -> 6%
where the time goes in v5:
time: 229 us; the launch traced here: 227 us
  starting transfers between devices  78.6 us (34%)
  waiting for transfers between devices  70.5 us (31%)
  Pallas kernels  47.8 us (21%)
  blocking collectives  23.7 us (10%)
  local copies, waits for them, and re-layouts  5.65 us (2%)
    ppermute x21, waiting for transfers between devices, flip(): lax.ppermute(value, axes, [(index, index ^ bits) for index in range(count)])  53.1 us
    pallas_call x17, Pallas kernels, call(): pl.pallas_call(kernel, out_shape=[(pltpu.HBM if place in 'HL' else jax.Sh...  47.8 us
    ppermute x21, starting transfers between devices, flip(): lax.ppermute(value, axes, [(index, index ^ bits) for index in range(count)])  33.9 us
    all_to_all x5, starting transfers between devices, exchange(): return lax.all_to_all(value, axes, 0, 0, tiled=True)  31.2 us
    all_to_all x1, blocking collectives, exchange(): return lax.all_to_all(value, axes, 0, 0, tiled=True)  23.7 us
    ppermute x7, starting transfers between devices, swap(): return lax.ppermute(value, CORE, [(0, 1), (1, 0)])  13.5 us
    all_to_all x5, waiting for transfers between devices, exchange(): return lax.all_to_all(value, axes, 0, 0, tiled=True)  9.38 us
    ppermute x7, waiting for transfers between devices, swap(): return lax.ppermute(value, CORE, [(0, 1), (1, 0)])  8.11 us
  transfers between devices with their start and end apart: 33, of which 15 were waited for; matrix products, arithmetic and copies ran while one was open for 1% of the time, Pallas kernels for 6%

profile of v5, /device:TPU:1, one launch (start us, length us, event | category | flops | bytes accessed | tf_op | source)
XLA Modules:
  0.0 227.4 jit_solution(6398041135541123413)
XLA Ops:
  0.7 4.3 %shard_map.186 = (bf16[8,128,640]{2,1,0:T(8,128)(2,1)}, bf16[128,768]{1,0:T(8,128)(2,1)}) custom-call(bf16[2,128,768]{2,1,0:T(8,128)(2,1)} %tok_ref.5, f32[768]{0:T(1024)} %gain_ref.7, f32[768]{0:T(1024)} %shift_ref.2, bf16[768,2304]{1,0:T(8,128)(2,1)} %w_ref.3), custom_call_target="tpu_custom_call" | custom-call | flops 1000000000 | bytes 2000000 | tf_op jit(solution)/shard_map/pallas_call | solution.py:106
  5.0 23.7 %all_to_all.30.same_ref.kvs_ref = bf16[8,128,640]{2,1,0:T(8,128)(2,1)S(1)} all-to-all(bf16[8,128,640]{2,1,0:T(8,128)(2,1)} %get-tuple-element.52), channel_id=1, replica_groups=mesh['y'=4,'xl'=2,'c'=2,'zh'=2,'zl'=2,'xh'=2] {'y','xl'}, dimensions={0} | all-to-all | bytes 2621440 | tf_op jit(solution)/shard_map/all_to_all | solution.py:534
  30.6 2.7 %collective-permute-done.other_ref.kvo_ref = bf16[8,128,640]{2,1,0:T(8,128)(2,1)S(1)} collective-permute-done((bf16[8,128,640]{2,1,0:T(8,128)(2,1)S(1)}, bf16[8,128,640]{2,1,0:T(8,128)(2,1)S(1)}, u32[]{:S(2)}, u32[]{:S(2)}) %collective-permute-start) | collective-permute-done | bytes 1310752 | tf_op jit(solution)/shard_map/ppermute | solution.py:538
  33.3 3.2 %shard_map.187 = bf16[8,128,256]{2,1,0:T(8,128)(2,1)} custom-call(s32[2,32]{1,0:T(2,128)S(1)} %copy-done.7, bf16[8,128,640]{2,1,0:T(8,128)(2,1)S(1)} %all_to_all.30.same_ref.kvs_ref, bf16[8,128,640]{2,1,0:T(8,128)(2,1)S(1)} %collective-permute-done.other_ref.kvo_ref), custom_call_target="tpu_custom_call" | custom-call | flops 2000000000 | bytes 2000000 | tf_op jit(solution)/shard_map/pallas_call | solution.py:106
  38.6 6.5 %all-to-all-start.1 = ((bf16[8,128,256]{2,1,0:T(8,128)(2,1)}), bf16[8,128,256]{2,1,0:T(8,128)(2,1)S(1)}, u32[]{:S(2)}, u32[]{:S(2)}) async-start(bf16[8,128,256]{2,1,0:T(8,128)(2,1)} %shard_map.187), calls=%async_computation.1 | async-start | bytes 1048576 | tf_op jit(solution)/shard_map/all_to_all | solution.py:534
  46.5 9.4 %all-to-all-done.1.mixed_ref = bf16[8,128,256]{2,1,0:T(8,128)(2,1)S(1)} async-done(((bf16[8,128,256]{2,1,0:T(8,128)(2,1)}), bf16[8,128,256]{2,1,0:T(8,128)(2,1)S(1)}, u32[]{:S(2)}, u32[]{:S(2)}) %all-to-all-start.1) | async-done | bytes 524320 | tf_op jit(solution)/shard_map/all_to_all | solution.py:534
  58.0 4.4 %shard_map.188 = (bf16[8,64,768]{2,1,0:T(8,128)(2,1)}, f32[8,32,768]{2,1,0:T(8,128)}, bf16[256,768]{1,0:T(8,128)(2,1)S(1)}, bf16[256,384]{1,0:T(8,128)(2,1)S(1)}, bf16[256,384]{1,0:T(8,128)(2,1)S(1)}) custom-call(bf16[8,128,256]{2,1,0:T(8,128)(2,1)S(1)} %all-to-all-done.1.mixed_ref, bf16[2,128,768]{2,1,0:T(8,128)(2,1)S(1)} %copy-done.1, ...), custom_call_target="tpu_custom_call" | custom-call | flops 4000000000 | bytes 2000000 | tf_op jit(solution)/shard_map/pallas_call | solution.py:106
  62.4 2.8 %shard_map.189 = (bf16[8,48,768]{2,1,0:T(8,128)(2,1)S(1)}, bf16[8,48,768]{2,1,0:T(8,128)(2,1)}) custom-call(bf16[256,768]{1,0:T(8,128)(2,1)S(1)} %get-tuple-element.54.normed_ref, bf16[256,384]{1,0:T(8,128)(2,1)S(1)} %get-tuple-element.55.act_ref, bf16[256,384]{1,0:T(8,128)(2,1)S(1)} %get-tuple-element.56.gpre_ref, bf16[2,128,768]{2,1,0:T(8,128)(2,1)} %og_ref.5), custom_call_target="tpu_custom_call" | custom-call | flops 2000000000 | bytes 2000000 | tf_op jit(solution)/shard_map/pallas_call | solution.py:106
  66.9 3.5 %all-to-all-start.2 = ((bf16[8,64,768]{2,1,0:T(8,128)(2,1)}), bf16[8,64,768]{2,1,0:T(8,128)(2,1)S(1)}, u32[]{:S(2)}, u32[]{:S(2)}) async-start(bf16[8,64,768]{2,1,0:T(8,128)(2,1)} %get-tuple-element.53), calls=%async_computation.2 | async-start | bytes 1572864 | tf_op jit(solution)/shard_map/all_to_all | solution.py:534
  77.1 4.3 %collective-permute-done.3.refs_2_ = bf16[2,48,768]{2,1,0:T(8,128)(2,1)S(1)} collective-permute-done((bf16[2,48,768]{2,1,0:T(8,128)(2,1)}, bf16[2,48,768]{2,1,0:T(8,128)(2,1)S(1)}, u32[]{:S(2)}, u32[]{:S(2)}) %collective-permute-start.3) | collective-permute-done | bytes 147488 | tf_op jit(solution)/shard_map/ppermute | solution.py:554
  81.4 2.4 %collective-permute-done.4.refs_3_ = bf16[2,48,768]{2,1,0:T(8,128)(2,1)S(1)} collective-permute-done((bf16[2,48,768]{2,1,0:T(8,128)(2,1)}, bf16[2,48,768]{2,1,0:T(8,128)(2,1)S(1)}, u32[]{:S(2)}, u32[]{:S(2)}) %collective-permute-start.4) | collective-permute-done | bytes 147488 | tf_op jit(solution)/shard_map/ppermute | solution.py:554
  85.4 4.2 %shard_map.193 = (bf16[32,32,256]{2,1,0:T(8,128)(2,1)}, bf16[32,768]{1,0:T(8,128)(2,1)}, f32[32,768]{1,0:T(8,128)}, bf16[32,768]{1,0:T(8,128)(2,1)}, f32[8,768]{1,0:T(8,128)}, /*index=5*/bf16[32,768]{1,0:T(8,128)(2,1)}) custom-call(bf16[8,64,768]{2,1,0:T(8,128)(2,1)S(1)} %shard_map.192.sums_ref, f32[8,32,768]{2,1,0:T(8,128)} %get-tuple-element.64.middle_ref, ...), custom_call_target="tpu_custom_call" | custom-call | flops 1000000000 | bytes 2000000 | tf_op jit(solution)/shard_map/pallas_call | solution.py:106
  89.7 6.2 %all-to-all-start.3 = ((bf16[32,32,256]{2,1,0:T(8,128)(2,1)}), bf16[32,32,256]{2,1,0:T(8,128)(2,1)S(1)}, u32[]{:S(2)}, u32[]{:S(2)}) async-start(bf16[32,32,256]{2,1,0:T(8,128)(2,1)} %get-tuple-element.65), calls=%async_computation.3 | async-start | bytes 1048576 | tf_op jit(solution)/shard_map/all_to_all | solution.py:534
  97.2 3.3 %collective-permute-start.7 = (bf16[32,768]{1,0:T(8,128)(2,1)}, bf16[32,768]{1,0:T(8,128)(2,1)S(1)}, u32[]{:S(2)}, u32[]{:S(2)}) collective-permute-start(bf16[32,768]{1,0:T(8,128)(2,1)} %get-tuple-element.66.low0_ref), channel_id=1, source_target_pairs={{0,3},{1,2},{2,1},{3,0},{4,7},{5,6},{6,5},{7,4},{8,11},{9,10},{10,... | collective-permute-start | bytes 147464 | tf_op jit(solution)/shard_map/ppermute | solution.py:554
  100.5 3.2 %collective-permute-done.8.two_ref = bf16[48,768]{1,0:T(8,128)(2,1)S(1)} collective-permute-done((bf16[48,768]{1,0:T(8,128)(2,1)S(1)}, bf16[48,768]{1,0:T(8,128)(2,1)S(1)}, u32[]{:S(2)}, u32[]{:S(2)}) %collective-permute-start.8) | collective-permute-done | bytes 73760 | tf_op jit(solution)/shard_map/ppermute | solution.py:554
  105.2 2.5 %collective-permute-start.11 = (bf16[48,768]{1,0:T(8,128)(2,1)}, bf16[48,768]{1,0:T(8,128)(2,1)S(1)}, u32[]{:S(2)}, u32[]{:S(2)}) collective-permute-start(bf16[48,768]{1,0:T(8,128)(2,1)} %shard_map.194.refs_0_), channel_id=1, source_target_pairs={{0,96},{32,64},{64,32},{96,0},{1,97},{33,65},{65,33},{97,1},{2,98}... | collective-permute-start | bytes 221192 | tf_op jit(solution)/shard_map/ppermute | solution.py:554
  109.7 2.4 %collective-permute-start.5 = (bf16[32,768]{1,0:T(8,128)(2,1)}, bf16[32,768]{1,0:T(8,128)(2,1)S(1)}, u32[]{:S(2)}, u32[]{:S(2)}) collective-permute-start(bf16[32,768]{1,0:T(8,128)(2,1)} %get-tuple-element.66.low0_ref), channel_id=1, source_target_pairs={{0,1},{1,0},{2,3},{3,2},{4,5},{5,4},{6,7},{7,6},{8,9},{9,8},{10,11... | collective-permute-start | bytes 147464 | tf_op jit(solution)/shard_map/ppermute | solution.py:554
  114.4 5.2 %collective-permute-start.12 = (bf16[8,128,256]{2,1,0:T(8,128)(2,1)S(1)}, bf16[8,128,256]{2,1,0:T(8,128)(2,1)S(1)}, u32[]{:S(2)}, u32[]{:S(2)}) collective-permute-start(bf16[8,128,256]{2,1,0:T(8,128)(2,1)S(1)} %shard_map.195.gs_ref), channel_id=1, source_target_pairs={{0,8},{8,0},{1,9},{9,1},{2,10},{10,2},{3,11},{11,3},{4,12},{12,4},... | collective-permute-start | bytes 1572872 | tf_op jit(solution)/shard_map/ppermute | solution.py:538
  121.1 7.9 %shard_map.196 = (f32[32,768]{1,0:T(8,128)}, bf16[32,768]{1,0:T(8,128)(2,1)}, bf16[32,768]{1,0:T(8,128)(2,1)}, bf16[32,768]{1,0:T(8,128)(2,1)}, bf16[16,48,384]{...) custom-call(s32[2,32]{1,0:T(2,128)S(1)} %copy-done.7, bf16[8,128,640]{2,1,0:T(8,128)(2,1)} %copy-done.2, ...), custom_call_target="tpu_custom_call" | custom-call | flops 8000000000 | bytes 2000000 | tf_op jit(solution)/shard_map/pallas_call | solution.py:106
  132.1 6.2 %all-to-all-start.4 = ((bf16[16,48,384]{2,1,0:T(8,128)(2,1)}), bf16[16,48,384]{2,1,0:T(8,128)(2,1)S(1)}, u32[]{:S(2)}, u32[]{:S(2)}) async-start(bf16[16,48,384]{2,1,0:T(8,128)(2,1)} %shard_map.199), calls=%async_computation.4 | async-start | bytes 1179648 | tf_op jit(solution)/shard_map/all_to_all | solution.py:534
  141.3 2.7 %collective-permute-start.13 = (bf16[32,768]{1,0:T(8,128)(2,1)S(1)}, bf16[32,768]{1,0:T(8,128)(2,1)S(1)}, u32[]{:S(2)}, u32[]{:S(2)}) collective-permute-start(bf16[32,768]{1,0:T(8,128)(2,1)S(1)} %copy-done.13), channel_id=1, source_target_pairs={{0,1},{1,0},{2,3},{3,2},{4,5},{5,4},{6,7},{7,6},{8,9},{9,8},{10,11... | collective-permute-start | bytes 147464 | tf_op jit(solution)/shard_map/ppermute | solution.py:554
  145.5 9.5 %collective-permute-done.13.one_ref = bf16[32,768]{1,0:T(8,128)(2,1)S(1)} collective-permute-done((bf16[32,768]{1,0:T(8,128)(2,1)S(1)}, bf16[32,768]{1,0:T(8,128)(2,1)S(1)}, u32[]{:S(2)}, u32[]{:S(2)}) %collective-permute-start.13) | collective-permute-done | bytes 49184 | tf_op jit(solution)/shard_map/ppermute | solution.py:554
  157.3 2.4 %shard_map.202 = bf16[8,8,56,384]{3,2,1,0:T(8,128)(2,1)} custom-call(bf16[16,48,384]{2,1,0:T(8,128)(2,1)S(1)} %shard_map.201.in_ref, f32[8,768]{1,0:T(8,128)} %get-tuple-element.82.refs_2_.vec_ref), custom_call_target="tpu_custom_call" | custom-call | flops 100000000 | bytes 2000000 | tf_op jit(solution)/shard_map/pallas_call | solution.py:106
  159.8 8.7 %all-to-all-start.5 = ((bf16[64,56,384]{2,1,0:T(8,128)(2,1)}), bf16[64,56,384]{2,1,0:T(8,128)(2,1)S(1)}, u32[]{:S(2)}, u32[]{:S(2)}) async-start(bf16[64,56,384]{2,1,0:T(8,128)(2,1)} %bitcast.6), calls=%async_computation.5 | async-start | bytes 5505024 | tf_op jit(solution)/shard_map/all_to_all | solution.py:534
  170.8 4.9 %collective-permute-start.22 = (bf16[64,768]{1,0:T(8,128)(2,1)S(1)}, bf16[64,768]{1,0:T(8,128)(2,1)S(1)}, u32[]{:S(2)}, u32[]{:S(2)}) collective-permute-start(bf16[64,768]{1,0:T(8,128)(2,1)S(1)} %copy-done.9), channel_id=1, source_target_pairs={{0,7},{1,6},{2,5},{3,4},{4,3},{5,2},{6,1},{7,0},{8,15},{9,14},{10,... | collective-permute-start | bytes 294920 | tf_op jit(solution)/shard_map/ppermute | solution.py:554
  178.8 2.6 %collective-permute-start.18 = (bf16[64,768]{1,0:T(8,128)(2,1)S(1)}, bf16[64,768]{1,0:T(8,128)(2,1)S(1)}, u32[]{:S(2)}, u32[]{:S(2)}) collective-permute-start(bf16[64,768]{1,0:T(8,128)(2,1)S(1)} %copy-done.9), channel_id=1, source_target_pairs={{0,3},{1,2},{2,1},{3,0},{4,7},{5,6},{6,5},{7,4},{8,11},{9,10},{10,... | collective-permute-start | bytes 294920 | tf_op jit(solution)/shard_map/ppermute | solution.py:554
  181.4 22.6 %collective-permute-done.22.refs_7_ = bf16[64,768]{1,0:T(8,128)(2,1)S(1)} collective-permute-done((bf16[64,768]{1,0:T(8,128)(2,1)S(1)}, bf16[64,768]{1,0:T(8,128)(2,1)S(1)}, u32[]{:S(2)}, u32[]{:S(2)}) %collective-permute-start.22) | collective-permute-done | bytes 98336 | tf_op jit(solution)/shard_map/ppermute | solution.py:554
  204.3 6.3 %collective-permute-done.21.refs_6_ = bf16[64,768]{1,0:T(8,128)(2,1)S(1)} collective-permute-done((bf16[64,768]{1,0:T(8,128)(2,1)S(1)}, bf16[64,768]{1,0:T(8,128)(2,1)S(1)}, u32[]{:S(2)}, u32[]{:S(2)}) %collective-permute-start.21) | collective-permute-done | bytes 98336 | tf_op jit(solution)/shard_map/ppermute | solution.py:554
  212.7 2.6 %shard_map.203 = (f32[768,384]{1,0:T(8,128)}, f32[384,768]{1,0:T(8,128)}) custom-call(bf16[4,48,768]{2,1,0:T(8,128)(2,1)} %shard_map.200.refs_0_, bf16[4,48,768]{2,1,0:T(8,128)(2,1)S(1)} %collective-permute-done.24.refs_1_, bf16[4,48,768]{2,1,0:T(8,128)(2,1)S(1)} %collective-permute-done.25.refs_2_, bf16[4,48,768]{2,1,0:T(8,128)(2,1)S(1)} %collective-permute-done.26.refs_3_), custom_call_target="tpu_custom_call" | custom-call | flops 10000000 | bytes 2000000 | tf_op jit(solution)/shard_map/pallas_call | solution.py:106
  219.5 2.4 %shard_map.205 = (f32[768,2304]{1,0:T(8,128)}, f32[768,768]{1,0:T(8,128)}, f32[8,384]{1,0:T(8,128)S(1)}) custom-call(bf16[8,8,56,384]{3,2,1,0:T(8,128)(2,1)S(1)} %shard_map.204.in_ref), custom_call_target="tpu_custom_call" | custom-call | flops 100000000 | bytes 2000000 | tf_op jit(solution)/shard_map/pallas_call | solution.py:106
  221.9 2.3 %collective-permute-done.27.in_ref = bf16[8,8,56,384]{3,2,1,0:T(8,128)(2,1)S(1)} collective-permute-done((bf16[8,8,56,384]{3,2,1,0:T(8,128)(2,1)S(1)}, bf16[8,8,56,384]{3,2,1,0:T(8,128)(2,1)S(1)}, u32[]{:S(2)}, u32[]{:S(2)}) %collective-permute-start.27) | collective-permute-done | bytes 2752544 | tf_op jit(solution)/shard_map/ppermute | solution.py:538
  224.2 3.0 %shard_map.206 = (f32[768,2304]{1,0:T(8,128)}, f32[768,768]{1,0:T(8,128)}, f32[768]{0:T(1024)}, f32[768]{0:T(1024)}, f32[768]{0:T(1024)}, /*index=5*/f32[768]{0:T(1024)}) custom-call(bf16[8,8,56,384]{3,2,1,0:T(8,128)(2,1)S(1)} %collective-permute-done.27.in_ref, ...), custom_call_target="tpu_custom_call", output_to_operand_aliasing={{0}: (2, {}), {1}: (3, {})} | custom-call | flops 100000000 | bytes 2000000 | tf_op jit(solution)/shard_map/pallas_call | solution.py:106
  (85 shorter events, 48.0 us)
Async XLA Ops:
  28.7 4.5 %collective-permute-start = (bf16[8,128,640]{2,1,0:T(8,128)(2,1)S(1)}, bf16[8,128,640]{2,1,0:T(8,128)(2,1)S(1)}, u32[]{:S(2)}, u32[]{:S(2)}) collective-permute-start(bf16[8,128,640]{2,1,0:T(8,128)(2,1)S(1)} %all_to_all.30.same_ref.kvs_ref), channel_id=1, source_target_pairs={{0,8},{8,0},{1,9},{9,1},{2,10},{10,2},{3,11},{11,3},{4,12},{12,4},... | collective-permute-start | bytes 3932168 | tf_op jit(solution)/shard_map/ppermute | solution.py:538
  38.6 17.3 %all-to-all-start.1 = ((bf16[8,128,256]{2,1,0:T(8,128)(2,1)}), bf16[8,128,256]{2,1,0:T(8,128)(2,1)S(1)}, u32[]{:S(2)}, u32[]{:S(2)}) async-start(bf16[8,128,256]{2,1,0:T(8,128)(2,1)} %shard_map.187), calls=%async_computation.1 | async-start | bytes 1048576 | tf_op jit(solution)/shard_map/all_to_all | solution.py:534
  65.2 5.3 %collective-permute-start.1 = (bf16[8,48,768]{2,1,0:T(8,128)(2,1)}, bf16[8,48,768]{2,1,0:T(8,128)(2,1)S(1)}, u32[]{:S(2)}, u32[]{:S(2)}) collective-permute-start(bf16[8,48,768]{2,1,0:T(8,128)(2,1)} %get-tuple-element.58), channel_id=1, source_target_pairs={{0,8},{8,0},{1,9},{9,1},{2,10},{10,2},{3,11},{11,3},{4,12},{12,4},... | collective-permute-start | bytes 1769480 | tf_op jit(solution)/shard_map/ppermute | solution.py:538
  66.9 18.5 %all-to-all-start.2 = ((bf16[8,64,768]{2,1,0:T(8,128)(2,1)}), bf16[8,64,768]{2,1,0:T(8,128)(2,1)S(1)}, u32[]{:S(2)}, u32[]{:S(2)}) async-start(bf16[8,64,768]{2,1,0:T(8,128)(2,1)} %get-tuple-element.53), calls=%async_computation.2 | async-start | bytes 1572864 | tf_op jit(solution)/shard_map/all_to_all | solution.py:534
  71.4 5.7 %collective-permute-start.2 = (bf16[2,48,768]{2,1,0:T(8,128)(2,1)}, bf16[2,48,768]{2,1,0:T(8,128)(2,1)S(1)}, u32[]{:S(2)}, u32[]{:S(2)}) collective-permute-start(bf16[2,48,768]{2,1,0:T(8,128)(2,1)} %get-tuple-element.60), channel_id=1, source_target_pairs={{0,32},{32,0},{64,96},{96,64},{1,33},{33,1},{65,97},{97,65},{2,34}... | collective-permute-start | bytes 442376 | tf_op jit(solution)/shard_map/ppermute | solution.py:554
  72.2 9.2 %collective-permute-start.3 = (bf16[2,48,768]{2,1,0:T(8,128)(2,1)}, bf16[2,48,768]{2,1,0:T(8,128)(2,1)S(1)}, u32[]{:S(2)}, u32[]{:S(2)}) collective-permute-start(bf16[2,48,768]{2,1,0:T(8,128)(2,1)} %get-tuple-element.61), channel_id=1, source_target_pairs={{0,64},{32,96},{64,0},{96,32},{1,65},{33,97},{65,1},{97,33},{2,66}... | collective-permute-start | bytes 442376 | tf_op jit(solution)/shard_map/ppermute | solution.py:554
  73.9 9.9 %collective-permute-start.4 = (bf16[2,48,768]{2,1,0:T(8,128)(2,1)}, bf16[2,48,768]{2,1,0:T(8,128)(2,1)S(1)}, u32[]{:S(2)}, u32[]{:S(2)}) collective-permute-start(bf16[2,48,768]{2,1,0:T(8,128)(2,1)} %get-tuple-element.62), channel_id=1, source_target_pairs={{0,96},{32,64},{64,32},{96,0},{1,97},{33,65},{65,33},{97,1},{2,98}... | collective-permute-start | bytes 442376 | tf_op jit(solution)/shard_map/ppermute | solution.py:554
  89.7 24.7 %all-to-all-start.3 = ((bf16[32,32,256]{2,1,0:T(8,128)(2,1)}), bf16[32,32,256]{2,1,0:T(8,128)(2,1)S(1)}, u32[]{:S(2)}, u32[]{:S(2)}) async-start(bf16[32,32,256]{2,1,0:T(8,128)(2,1)} %get-tuple-element.65), calls=%async_computation.3 | async-start | bytes 1048576 | tf_op jit(solution)/shard_map/all_to_all | solution.py:534
  95.9 7.8 %collective-permute-start.8 = (bf16[48,768]{1,0:T(8,128)(2,1)S(1)}, bf16[48,768]{1,0:T(8,128)(2,1)S(1)}, u32[]{:S(2)}, u32[]{:S(2)}) collective-permute-start(bf16[48,768]{1,0:T(8,128)(2,1)S(1)} %copy-done.10), channel_id=1, source_target_pairs={{0,16},{16,0},{1,17},{17,1},{2,18},{18,2},{3,19},{19,3},{4,20},{20... | collective-permute-start | bytes 221192 | tf_op jit(solution)/shard_map/ppermute | solution.py:554
  97.2 12.5 %collective-permute-start.7 = (bf16[32,768]{1,0:T(8,128)(2,1)}, bf16[32,768]{1,0:T(8,128)(2,1)S(1)}, u32[]{:S(2)}, u32[]{:S(2)}) collective-permute-start(bf16[32,768]{1,0:T(8,128)(2,1)} %get-tuple-element.66.low0_ref), channel_id=1, source_target_pairs={{0,3},{1,2},{2,1},{3,0},{4,7},{5,6},{6,5},{7,4},{8,11},{9,10},{10,... | collective-permute-start | bytes 147464 | tf_op jit(solution)/shard_map/ppermute | solution.py:554
  105.2 9.1 %collective-permute-start.11 = (bf16[48,768]{1,0:T(8,128)(2,1)}, bf16[48,768]{1,0:T(8,128)(2,1)S(1)}, u32[]{:S(2)}, u32[]{:S(2)}) collective-permute-start(bf16[48,768]{1,0:T(8,128)(2,1)} %shard_map.194.refs_0_), channel_id=1, source_target_pairs={{0,96},{32,64},{64,32},{96,0},{1,97},{33,65},{65,33},{97,1},{2,98}... | collective-permute-start | bytes 221192 | tf_op jit(solution)/shard_map/ppermute | solution.py:554
  107.7 6.6 %collective-permute-start.10 = (bf16[48,768]{1,0:T(8,128)(2,1)}, bf16[48,768]{1,0:T(8,128)(2,1)S(1)}, u32[]{:S(2)}, u32[]{:S(2)}) collective-permute-start(bf16[48,768]{1,0:T(8,128)(2,1)} %shard_map.194.refs_0_), channel_id=1, source_target_pairs={{0,64},{32,96},{64,0},{96,32},{1,65},{33,97},{65,1},{97,33},{2,66}... | collective-permute-start | bytes 221192 | tf_op jit(solution)/shard_map/ppermute | solution.py:554
  108.2 6.1 %collective-permute-start.9 = (bf16[48,768]{1,0:T(8,128)(2,1)}, bf16[48,768]{1,0:T(8,128)(2,1)S(1)}, u32[]{:S(2)}, u32[]{:S(2)}) collective-permute-start(bf16[48,768]{1,0:T(8,128)(2,1)} %shard_map.194.refs_0_), channel_id=1, source_target_pairs={{0,32},{32,0},{64,96},{96,64},{1,33},{33,1},{65,97},{97,65},{2,34}... | collective-permute-start | bytes 221192 | tf_op jit(solution)/shard_map/ppermute | solution.py:554
  108.5 3.6 %collective-permute-start.6 = (bf16[32,768]{1,0:T(8,128)(2,1)}, bf16[32,768]{1,0:T(8,128)(2,1)S(1)}, u32[]{:S(2)}, u32[]{:S(2)}) collective-permute-start(bf16[32,768]{1,0:T(8,128)(2,1)} %get-tuple-element.66.low0_ref), channel_id=1, source_target_pairs={{0,2},{1,3},{2,0},{3,1},{4,6},{5,7},{6,4},{7,5},{8,10},{9,11},{10,... | collective-permute-start | bytes 147464 | tf_op jit(solution)/shard_map/ppermute | solution.py:554
  109.7 4.7 %collective-permute-start.5 = (bf16[32,768]{1,0:T(8,128)(2,1)}, bf16[32,768]{1,0:T(8,128)(2,1)S(1)}, u32[]{:S(2)}, u32[]{:S(2)}) collective-permute-start(bf16[32,768]{1,0:T(8,128)(2,1)} %get-tuple-element.66.low0_ref), channel_id=1, source_target_pairs={{0,1},{1,0},{2,3},{3,2},{4,5},{5,4},{6,7},{7,6},{8,9},{9,8},{10,11... | collective-permute-start | bytes 147464 | tf_op jit(solution)/shard_map/ppermute | solution.py:554
  114.4 6.7 %collective-permute-start.12 = (bf16[8,128,256]{2,1,0:T(8,128)(2,1)S(1)}, bf16[8,128,256]{2,1,0:T(8,128)(2,1)S(1)}, u32[]{:S(2)}, u32[]{:S(2)}) collective-permute-start(bf16[8,128,256]{2,1,0:T(8,128)(2,1)S(1)} %shard_map.195.gs_ref), channel_id=1, source_target_pairs={{0,8},{8,0},{1,9},{9,1},{2,10},{10,2},{3,11},{11,3},{4,12},{12,4},... | collective-permute-start | bytes 1572872 | tf_op jit(solution)/shard_map/ppermute | solution.py:538
  132.1 25.2 %all-to-all-start.4 = ((bf16[16,48,384]{2,1,0:T(8,128)(2,1)}), bf16[16,48,384]{2,1,0:T(8,128)(2,1)S(1)}, u32[]{:S(2)}, u32[]{:S(2)}) async-start(bf16[16,48,384]{2,1,0:T(8,128)(2,1)} %shard_map.199), calls=%async_computation.4 | async-start | bytes 1179648 | tf_op jit(solution)/shard_map/all_to_all | solution.py:534
  140.0 17.3 %collective-permute-start.24 = (bf16[4,48,768]{2,1,0:T(8,128)(2,1)}, bf16[4,48,768]{2,1,0:T(8,128)(2,1)S(1)}, u32[]{:S(2)}, u32[]{:S(2)}) collective-permute-start(bf16[4,48,768]{2,1,0:T(8,128)(2,1)} %shard_map.200.refs_0_), channel_id=1, source_target_pairs={{0,16},{16,0},{1,17},{17,1},{2,18},{18,2},{3,19},{19,3},{4,20},{20... | collective-permute-start | bytes 884744 | tf_op jit(solution)/shard_map/ppermute | solution.py:554
  141.3 13.6 %collective-permute-start.13 = (bf16[32,768]{1,0:T(8,128)(2,1)S(1)}, bf16[32,768]{1,0:T(8,128)(2,1)S(1)}, u32[]{:S(2)}, u32[]{:S(2)}) collective-permute-start(bf16[32,768]{1,0:T(8,128)(2,1)S(1)} %copy-done.13), channel_id=1, source_target_pairs={{0,1},{1,0},{2,3},{3,2},{4,5},{5,4},{6,7},{7,6},{8,9},{9,8},{10,11... | collective-permute-start | bytes 147464 | tf_op jit(solution)/shard_map/ppermute | solution.py:554
  144.0 10.9 %collective-permute-start.14 = (bf16[32,768]{1,0:T(8,128)(2,1)S(1)}, bf16[32,768]{1,0:T(8,128)(2,1)S(1)}, u32[]{:S(2)}, u32[]{:S(2)}) collective-permute-start(bf16[32,768]{1,0:T(8,128)(2,1)S(1)} %copy-done.12), channel_id=1, source_target_pairs={{0,2},{1,3},{2,0},{3,1},{4,6},{5,7},{6,4},{7,5},{8,10},{9,11},{10,... | collective-permute-start | bytes 147464 | tf_op jit(solution)/shard_map/ppermute | solution.py:554
  144.0 11.4 %collective-permute-start.15 = (bf16[32,768]{1,0:T(8,128)(2,1)S(1)}, bf16[32,768]{1,0:T(8,128)(2,1)S(1)}, u32[]{:S(2)}, u32[]{:S(2)}) collective-permute-start(bf16[32,768]{1,0:T(8,128)(2,1)S(1)} %copy-done.11), channel_id=1, source_target_pairs={{0,3},{1,2},{2,1},{3,0},{4,7},{5,6},{6,5},{7,4},{8,11},{9,10},{10,... | collective-permute-start | bytes 147464 | tf_op jit(solution)/shard_map/ppermute | solution.py:554
  159.8 57.8 %all-to-all-start.5 = ((bf16[64,56,384]{2,1,0:T(8,128)(2,1)}), bf16[64,56,384]{2,1,0:T(8,128)(2,1)S(1)}, u32[]{:S(2)}, u32[]{:S(2)}) async-start(bf16[64,56,384]{2,1,0:T(8,128)(2,1)} %bitcast.6), calls=%async_computation.5 | async-start | bytes 5505024 | tf_op jit(solution)/shard_map/all_to_all | solution.py:534
  168.5 8.9 %collective-permute-start.25 = (bf16[4,48,768]{2,1,0:T(8,128)(2,1)S(1)}, bf16[4,48,768]{2,1,0:T(8,128)(2,1)S(1)}, u32[]{:S(2)}, u32[]{:S(2)}) collective-permute-start(bf16[4,48,768]{2,1,0:T(8,128)(2,1)S(1)} %copy-done.8), channel_id=1, source_target_pairs={{0,8},{8,0},{1,9},{9,1},{2,10},{10,2},{3,11},{11,3},{4,12},{12,4},... | collective-permute-start | bytes 884744 | tf_op jit(solution)/shard_map/ppermute | solution.py:538
  170.7 8.2 %collective-permute-start.26 = (bf16[4,48,768]{2,1,0:T(8,128)(2,1)S(1)}, bf16[4,48,768]{2,1,0:T(8,128)(2,1)S(1)}, u32[]{:S(2)}, u32[]{:S(2)}) collective-permute-start(bf16[4,48,768]{2,1,0:T(8,128)(2,1)S(1)} %collective-permute-done.24.refs_1_), channel_id=1, source_target_pairs={{0,8},{8,0},{1,9},{9,1},{2,10},{10,2},{3,11},{11,3},{4,12},{12,4},... | collective-permute-start | bytes 884744 | tf_op jit(solution)/shard_map/ppermute | solution.py:538
  170.8 33.2 %collective-permute-start.22 = (bf16[64,768]{1,0:T(8,128)(2,1)S(1)}, bf16[64,768]{1,0:T(8,128)(2,1)S(1)}, u32[]{:S(2)}, u32[]{:S(2)}) collective-permute-start(bf16[64,768]{1,0:T(8,128)(2,1)S(1)} %copy-done.9), channel_id=1, source_target_pairs={{0,7},{1,6},{2,5},{3,4},{4,3},{5,2},{6,1},{7,0},{8,15},{9,14},{10,... | collective-permute-start | bytes 294920 | tf_op jit(solution)/shard_map/ppermute | solution.py:554
  175.7 34.9 %collective-permute-start.21 = (bf16[64,768]{1,0:T(8,128)(2,1)S(1)}, bf16[64,768]{1,0:T(8,128)(2,1)S(1)}, u32[]{:S(2)}, u32[]{:S(2)}) collective-permute-start(bf16[64,768]{1,0:T(8,128)(2,1)S(1)} %copy-done.9), channel_id=1, source_target_pairs={{0,6},{1,7},{2,4},{3,5},{4,2},{5,3},{6,0},{7,1},{8,14},{9,15},{10,... | collective-permute-start | bytes 294920 | tf_op jit(solution)/shard_map/ppermute | solution.py:554
  175.9 39.3 %collective-permute-start.20 = (bf16[64,768]{1,0:T(8,128)(2,1)S(1)}, bf16[64,768]{1,0:T(8,128)(2,1)S(1)}, u32[]{:S(2)}, u32[]{:S(2)}) collective-permute-start(bf16[64,768]{1,0:T(8,128)(2,1)S(1)} %copy-done.9), channel_id=1, source_target_pairs={{0,5},{1,4},{2,7},{3,6},{4,1},{5,0},{6,3},{7,2},{8,13},{9,12},{10,... | collective-permute-start | bytes 294920 | tf_op jit(solution)/shard_map/ppermute | solution.py:554
  177.4 37.9 %collective-permute-start.19 = (bf16[64,768]{1,0:T(8,128)(2,1)S(1)}, bf16[64,768]{1,0:T(8,128)(2,1)S(1)}, u32[]{:S(2)}, u32[]{:S(2)}) collective-permute-start(bf16[64,768]{1,0:T(8,128)(2,1)S(1)} %copy-done.9), channel_id=1, source_target_pairs={{0,4},{1,5},{2,6},{3,7},{4,0},{5,1},{6,2},{7,3},{8,12},{9,13},{10,... | collective-permute-start | bytes 294920 | tf_op jit(solution)/shard_map/ppermute | solution.py:554
  178.8 36.5 %collective-permute-start.18 = (bf16[64,768]{1,0:T(8,128)(2,1)S(1)}, bf16[64,768]{1,0:T(8,128)(2,1)S(1)}, u32[]{:S(2)}, u32[]{:S(2)}) collective-permute-start(bf16[64,768]{1,0:T(8,128)(2,1)S(1)} %copy-done.9), channel_id=1, source_target_pairs={{0,3},{1,2},{2,1},{3,0},{4,7},{5,6},{6,5},{7,4},{8,11},{9,10},{10,... | collective-permute-start | bytes 294920 | tf_op jit(solution)/shard_map/ppermute | solution.py:554
  204.0 11.3 %collective-permute-start.17 = (bf16[64,768]{1,0:T(8,128)(2,1)S(1)}, bf16[64,768]{1,0:T(8,128)(2,1)S(1)}, u32[]{:S(2)}, u32[]{:S(2)}) collective-permute-start(bf16[64,768]{1,0:T(8,128)(2,1)S(1)} %copy-done.9), channel_id=1, source_target_pairs={{0,2},{1,3},{2,0},{3,1},{4,6},{5,7},{6,4},{7,5},{8,10},{9,11},{10,... | collective-permute-start | bytes 294920 | tf_op jit(solution)/shard_map/ppermute | solution.py:554
  210.6 5.0 %collective-permute-start.16 = (bf16[64,768]{1,0:T(8,128)(2,1)S(1)}, bf16[64,768]{1,0:T(8,128)(2,1)S(1)}, u32[]{:S(2)}, u32[]{:S(2)}) collective-permute-start(bf16[64,768]{1,0:T(8,128)(2,1)S(1)} %copy-done.9), channel_id=1, source_target_pairs={{0,1},{1,0},{2,3},{3,2},{4,5},{5,4},{6,7},{7,6},{8,9},{9,8},{10,11... | collective-permute-start | bytes 294920 | tf_op jit(solution)/shard_map/ppermute | solution.py:554
  217.5 6.7 %collective-permute-start.27 = (bf16[8,8,56,384]{3,2,1,0:T(8,128)(2,1)S(1)}, bf16[8,8,56,384]{3,2,1,0:T(8,128)(2,1)S(1)}, u32[]{:S(2)}, u32[]{:S(2)}) collective-permute-start(bf16[8,8,56,384]{3,2,1,0:T(8,128)(2,1)S(1)} %shard_map.204.in_ref), channel_id=1, source_target_pairs={{0,8},{8,0},{1,9},{9,1},{2,10},{10,2},{3,11},{11,3},{4,12},{12,4},... | collective-permute-start | bytes 8257544 | tf_op jit(solution)/shard_map/ppermute | solution.py:538
  (15 other events, 150.5 us)

commit v6 on v5

--- a/solution.py
+++ b/solution.py
@@ -112,7 +112,7 @@
         out_specs=[pl.BlockSpec(memory_space=places[place]) for _, _, place in outs],
         scratch_shapes=list(scratch),
         input_output_aliases=aliases or {},
-        cost_estimate=pl.CostEstimate(flops=cost, bytes_accessed=2000000, transcendentals=0),
+        cost_estimate=pl.CostEstimate(flops=1000, bytes_accessed=1000, transcendentals=0),
         compiler_params=pltpu.CompilerParams(vmem_limit_bytes=vmem * 2**20),
     )(*[pin(value) if place in "HL" else value for value, place in ins])
 
@@ -144,7 +144,7 @@
 
 
 def project_kernel(
-    tok_ref, gain_ref, shift_ref, w_ref, kv_ref, normed_ref,
+    tok_ref, gain_ref, shift_ref, w_ref, kv_ref, q_ref, normed_ref,
     x_buf, w_buf, kv_buf, gain_buf, shift_buf, x_sem, w_sem, kv_sem, gain_sem, shift_sem,
 ):
     copy_x = pltpu.make_async_copy(tok_ref.at[lax.axis_index(MICRO)], x_buf, x_sem)
@@ -164,21 +164,22 @@
         full = mm(normed, w_buf[slot])
         return jnp.where(odd, full[:, 192:], full[:, :192]).astype(BF)
 
-    kv_buf[...] = jnp.concatenate([part(0), part(1), part(2), jnp.zeros((TOK, HD), BF)], axis=1)
+    kv_buf[...] = jnp.concatenate([part(0), part(1)], axis=1)
     sends = send_copies(kv_buf, kv_ref, range(8), kv_sem)
     normed_ref[...] = normed
+    q_ref[...] = jnp.concatenate([part(2), jnp.zeros((TOK, HD), BF)], axis=1)
     wait_all(sends)
 
 
-def attend_kernel(scene_ref, same_ref, other_ref, out_ref, buf, sem):
+def attend_kernel(scene_ref, q_ref, same_ref, other_ref, out_ref, buf, sem):
     first, big = span(scene_ref)
 
     def run(count):
         rows = count * TOK
         keys = jnp.concatenate(
-            [ref[pl.ds(first, count), :, :384].reshape(rows, 384) for ref in (same_ref, other_ref)], axis=0
+            [ref[pl.ds(first, count)].reshape(rows, 384) for ref in (same_ref, other_ref)], axis=0
         )
-        query = same_ref[chip_index(), :, 384:]
+        query = q_ref[...]
         q0, q1 = halves(query[:, :128])
         blocks = [keys[:, :128], keys[:, 128:256], keys[:, 256:]]
         mixed = []
@@ -235,38 +236,16 @@
     second.wait()
 
 
-def ff_grads_kernel(normed_ref, act_ref, gpre_ref, og_ref, keep_ref, send_ref, up_buf, down_buf):
-    core = lax.axis_index(CORE)
-    up_buf[...] = mm_tn(normed_ref[...], gpre_ref[...])
-    down_buf[...] = mm_tn(act_ref[...], og_ref[...].reshape(2 * TOK, D))
-    for ref, owner in ((keep_ref, core), (send_ref, 1 - core)):
-        column = pl.multiple_of(owner * 384, 128)
-        for tile in range(8):
-            rows = pl.ds(pl.multiple_of((2 * tile + owner) * 48, 16), 48)
-            ref[tile, :, :384] = up_buf[rows].astype(BF)
-            ref[tile, :, 384:] = down_buf[tile * 48:(tile + 1) * 48, pl.ds(column, 384)].astype(BF)
-
-
-def split_kernel(one_ref, two_ref, *refs):
-    y = lax.axis_index("y")
-    for k, ref in enumerate(refs):
-        for xl in range(2):
-            at = (y ^ k) * 2 + xl
-            ref[xl] = (one_ref[at].astype(F32) + two_ref[at].astype(F32)).astype(BF)
-
-
-def halve_kernel(*refs):
-    parts, (keep_ref, send_ref) = refs[:4], refs[4:]
-    xl = lax.axis_index("xl")
-    for ref, at in ((keep_ref, xl), (send_ref, 1 - xl)):
-        total = parts[0][at].astype(F32)
-        for part in parts[1:]:
-            total = total + part[at].astype(F32)
-        ref[...] = total.astype(BF)
-
-
-def pair_kernel(one_ref, two_ref, out_ref):
-    out_ref[...] = (one_ref[...].astype(F32) + two_ref[...].astype(F32)).astype(BF)
+def ff_grads_kernel(normed_ref, act_ref, gpre_ref, og_ref, out_ref):
+    up = mm_tn(normed_ref[...], gpre_ref[...]).astype(BF)
+    grad_out = og_ref[...].reshape(2 * TOK, D)
+    down = mm_tn(act_ref[...], grad_out).astype(BF)
+    out_ref[:, :384] = up
+    for tile in range(16):
+        half = (tile % 2) * 384
+        out_ref[tile * 48:(tile + 1) * 48, 384:] = down[
+            (tile // 2) * 48:(tile // 2 + 1) * 48, half:half + 384
+        ]
 
 
 def middle_kernel(
@@ -318,9 +297,9 @@
 
 
 def attend_back_kernel(
-    scene_ref, kvs_ref, kvo_ref, gs_ref, go_ref, normed_ref, mixed_ref, low0_ref, low1_ref, low2_ref, low3_ref, w_ref,
+    scene_ref, kvs_ref, kvo_ref, q_ref, gs_ref, go_ref, normed_ref, mixed_ref, low0_ref, low1_ref, low2_ref, low3_ref, w_ref,
     own_ref, one_ref, two_ref, three_ref, keep_ref, send_ref,
-    kv_buf, gqkv_buf, grad_buf, part_buf, mixed_buf, w_buf, kv_sem, mixed_sem, w_sem,
+    kv_buf, q_buf, gqkv_buf, grad_buf, part_buf, mixed_buf, w_buf, kv_sem, q_sem, mixed_sem, w_sem,
 ):
     first, big = span(scene_ref)
     chip = chip_index()
@@ -333,6 +312,11 @@
         loads = [
             pltpu.make_async_copy(ref.at[pl.ds(first, count)], kv_buf.at[slot, pl.ds(0, count)], kv_sem.at[slot])
             for slot, ref in enumerate((kvs_ref, kvo_ref))
+        ] + [
+            pltpu.make_async_copy(
+                q_ref.at[pl.ds(first, count), which], q_buf.at[slot, pl.ds(0, count)], q_sem.at[slot]
+            )
+            for slot, which in enumerate((core, 1 - core))
         ]
         for load in loads:
             load.start()
@@ -348,9 +332,9 @@
         own_stats = g_own[0].astype(F32)
         all_stats = grad[0].astype(F32).T
         wait_all(loads)
-        every = cut(jnp.concatenate([kv_buf[slot, :count].reshape(rows, 640) for slot in range(2)], axis=0))
-        kv, query = every[:3], every[3:]
-        own = cut(kv_buf[0, chip - first])
+        kv = cut(jnp.concatenate([kv_buf[slot, :count].reshape(rows, 384) for slot in range(2)], axis=0))
+        query = cut(jnp.concatenate([q_buf[slot, :count].reshape(rows, 256) for slot in range(2)], axis=0))
+        own = cut(kv_buf[0, chip - first]) + cut(q_buf[0, chip - first])
         q_heads = [*halves(own[3]), own[4]]
         k_heads = [*halves(own[0]), halves(own[1])[0]]
         v_heads = [halves(own[1])[1], *halves(own[2])]
@@ -483,25 +467,13 @@
     wait_all(copies)
 
 
-def stack_kernel(*refs):
-    y = lax.axis_index("y")
-    for k, ref in enumerate(refs[:4]):
-        refs[4][y ^ k] = ref[...]
-
-
-def spread_ff_kernel(*refs):
-    up_ref, down_ref = refs[4:]
-    xl, core = lax.axis_index("xl"), lax.axis_index(CORE)
-    for index, ref in enumerate(refs[:4]):
-        chip_xl = xl ^ (index % 2)
-        owner = core ^ (index // 2)
-        for y in range(4):
-            chip = y * 2 + chip_xl
-            block = ref[y].astype(F32)
-            up_ref[pl.ds(pl.multiple_of((chip * 2 + owner) * 48, 16), 48)] = block[:, :384]
-            down_ref[
-                pl.ds(pl.multiple_of(chip * 48, 16), 48), pl.ds(pl.multiple_of(owner * 384, 128), 384)
-            ] = block[:, 384:]
+def spread_ff_kernel(in_ref, up_ref, down_ref):
+    up_ref[...] = in_ref[:, :384].astype(F32)
+    for tile in range(16):
+        half = (tile % 2) * 384
+        down_ref[(tile // 2) * 48:(tile // 2 + 1) * 48, half:half + 384] = in_ref[
+            tile * 48:(tile + 1) * 48, 384:
+        ].astype(F32)
 
 
 def input_kernel(
@@ -558,13 +530,13 @@
     tokens, scene_of_block, ln1_gain, ln1_shift, w_qkv, w_out, ln2_gain, ln2_shift, w_up, w_down, out_grad
 ):
     w_out_pad = jnp.pad(w_out.reshape(4, 192, D), ((0, 0), (HD, 0), (0, 0)))
-    kv_send, normed = call(
+    kv_send, query, normed = call(
         project_kernel,
-        [((8, TOK, 640), BF, "H"), ((TOK, D), BF, "L")],
+        [((8, TOK, 384), BF, "H"), ((TOK, 256), BF, "L"), ((TOK, D), BF, "L")],
         [(tokens, "H"), (ln1_gain, "H"), (ln1_shift, "H"), (w_qkv, "H")],
         10**9,
         [
-            pltpu.VMEM((TOK, D), BF), pltpu.VMEM((3, D, 384), BF), pltpu.VMEM((TOK, 640), BF),
+            pltpu.VMEM((TOK, D), BF), pltpu.VMEM((3, D, 384), BF), pltpu.VMEM((TOK, 384), BF),
             pltpu.VMEM((D,), F32), pltpu.VMEM((D,), F32), DMA, DMA((3,)), DMA((8,)), DMA, DMA,
         ],
     )
@@ -573,16 +545,17 @@
     (mixed_send,) = call(
         attend_kernel,
         [((8, TOK, 256), BF, "H")],
-        [(scene_of_block, "S"), (kv_same, "V"), (kv_other, "V")],
+        [(scene_of_block, "S"), (query, "L"), (kv_same, "V"), (kv_other, "V")],
         2 * 10**9,
         [pltpu.VMEM((TOK, 256), BF), DMA((8,))],
     )
     mixed = exchange(mixed_send, NARROW)
+    queries = lax.all_gather(after(pin(query), kv_same), WIDE, axis=0, tiled=True).reshape(8, 2, TOK, 256)
     ff_send, middle, normed2, act, grad_pre = call(
         forward_kernel,
         [
-            ((8, 2 * BLK, D), BF, "H"), ((8, BLK, D), F32, "L"), ((2 * TOK, D), BF, "V"),
-            ((2 * TOK, FFL), BF, "V"), ((2 * TOK, FFL), BF, "V"),
+            ((8, 2 * BLK, D), BF, "H"), ((8, BLK, D), F32, "L"), ((2 * TOK, D), BF, "L"),
+            ((2 * TOK, FFL), BF, "L"), ((2 * TOK, FFL), BF, "L"),
         ],
         [
             (mixed, "V"), (tokens, "V"), (out_grad, "V"), (w_out_pad, "V"), (ln2_gain, "L"), (ln2_shift, "L"),
@@ -592,24 +565,15 @@
         [pltpu.VMEM((8, BLK, D), BF), pltpu.VMEM((8, BLK, D), BF), DMA((2,))],
     )
     ff_sums = exchange(ff_send, NARROW)
-    keep, send = call(
+    (ff_grads,) = call(
         ff_grads_kernel,
-        [((8, 48, D), BF, "V")] * 2,
-        [(normed2, "V"), (act, "V"), (grad_pre, "V"), (out_grad, "L")],
+        [((D, D), BF, "L")],
+        [(normed2, "L"), (act, "L"), (grad_pre, "L"), (out_grad, "L")],
         2 * 10**9,
-        [pltpu.VMEM((D, FFL), F32), pltpu.VMEM((FFL, D), F32)],
-    )
-    pieces = call(
-        split_kernel, [((2, 48, D), BF, "L")] * 4, [(keep, "V"), (swap(send), "V")], 10**8
-    )
-    pieces = [pieces[0]] + [flip(pieces[k], "y", 4, k) for k in (1, 2, 3)]
-    keep, send = call(
-        halve_kernel,
-        [((48, D), BF, "L")] * 2,
-        [(pieces[0], "L")] + [(piece, "V") for piece in pieces[1:]],
-        10**8,
-    )
-    ff_sums = after(ff_sums, pin(keep))
+    )
+    ff_part = lax.psum_scatter(ff_grads, WIDE, scatter_dimension=0, tiled=True)
+    ff_all = lax.all_gather(ff_part, WIDE, axis=0, tiled=True)
+    ff_sums = after(ff_sums, pin(ff_grads))
     grad_send, low, grad_mid, result_part, vec2, x_part = call(
         middle_kernel,
         [
@@ -626,26 +590,24 @@
             pltpu.VMEM((4, BLK, 256), BF), DMA, DMA((3,)), DMA((32,)),
         ],
     )
-    (ff_part,) = call(
-        pair_kernel, [((48, D), BF, "L")], [(keep, "L"), (flip(send, "xl", 2, 1), "V")], 10**7
-    )
-    ff_parts = [flip(ff_part, "y", 4, k) for k in (1, 2, 3)]
     grad_same = exchange(grad_send, (*CHIP, *GROUP)).reshape(8, TOK, 256)
     lows = [flip(low, GROUP, 4, k) for k in (1, 2, 3)]
-    grad_same = after(grad_same, *lows, *ff_parts)
+    grad_same = after(grad_same, *lows)
     grad_other = swap(grad_same)
     own, *sends, keep, send = call(
         attend_back_kernel,
         [((BLK, D), F32, "L")] + [((BLK, D), BF, "L")] * 3 + [((16, 48, 384), BF, "V")] * 2,
         [
-            (scene_of_block, "S"), (kv_same, "H"), (kv_other, "H"), (grad_same, "V"), (grad_other, "V"),
-            (normed, "L"), (mixed, "H"), (low, "L"), *[(value, "V") for value in lows], (w_qkv, "H"),
+            (scene_of_block, "S"), (kv_same, "H"), (kv_other, "H"), (queries, "H"), (grad_same, "V"), (grad_other, "V"),
+            (normed, "L"), (mixed, "H"), (low, "L"), *[(value, "V") for value in lows],
+            (w_qkv, "H"),
         ],
         8 * 10**9,
         [
-            pltpu.VMEM((2, 5, TOK, 640), BF), pltpu.VMEM((TOK, 640), BF), pltpu.VMEM((D, 640), F32),
+            pltpu.VMEM((2, 5, TOK, 384), BF), pltpu.VMEM((2, 5, TOK, 256), BF), pltpu.VMEM((TOK, 640), BF),
+            pltpu.VMEM((D, 640), F32),
             pltpu.VMEM((TOK, D), F32), pltpu.VMEM((TOK, 256), BF), pltpu.VMEM((3, D, 384), BF),
-            DMA((2,)), DMA, DMA((3,)),
+            DMA((2,)), DMA((2,)), DMA, DMA((3,)),
         ],
         vmem=24,
     )
@@ -658,13 +620,6 @@
     )
     parts = [flip(value, GROUP, 4, k + 1) for k, value in enumerate(sends)]
     weight_parts = exchange(weight_send, (*CHIP, MICRO))
-    (ff_near,) = call(
-        stack_kernel,
-        [((4, 48, D), BF, "L")],
-        [(ff_part, "L"), *[(value, "V") for value in ff_parts]],
-        10**7,
-    )
-    ff_far = flip(ff_near, "xl", 2, 1)
     packed, sums = call(
         input_kernel,
         [((2 * BLK, D), BF, "L"), ((8, D), F32, "L")],
@@ -674,7 +629,7 @@
         ],
         10**8,
     )
-    weight_parts = after(weight_parts, ff_far, pin(sums))
+    weight_parts = after(weight_parts, pin(sums), pin(ff_part))
     (weight_total,) = call(
         sum_kernel,
         [((8, 8, 56, 384), BF, "H")],
@@ -690,10 +645,7 @@
         10**8,
     )
     up_grad, down_grad = call(
-        spread_ff_kernel,
-        [((D, FFL), F32, "L"), ((FFL, D), F32, "L")],
-        [(ff_near, "L"), (ff_far, "V"), (swap(ff_near), "V"), (swap(ff_far), "V")],
-        10**7,
+        spread_ff_kernel, [((D, FFL), F32, "L"), ((FFL, D), F32, "L")], [(ff_all, "L")], 10**7
     )
     weight_same = exchange(weight_total.reshape(64, 56, 384), (*CHIP, *NARROW)).reshape(8, 8, 56, 384)
     weight_same = after(weight_same, *map(pin, (input_grad, result, up_grad, down_grad)))

time: 229 us -> 218 us (0.952)
  starting transfers between devices: 78.6 us -> 63.2 us
  between operations: 1.08 us -> 14 us
  Pallas kernels: 47.8 us -> 40.1 us
  waiting for transfers between devices: 70.5 us -> 76.4 us
  blocking collectives: 23.7 us -> 18 us
    ppermute x21 -> x13, starting transfers between devices: 33.9 us -> 22.8 us  [flip(): lax.ppermute(value, axes, [(index, index ^ bits) for index in range(count)])]
    all_to_all x5, waiting for transfers between devices: 9.38 us -> 19.9 us  [exchange(): return lax.all_to_all(value, axes, 0, 0, tiled=True)]
    pallas_call x17 -> x13, Pallas kernels: 47.8 us -> 40.1 us  [call(): pl.pallas_call(kernel, out_shape=[(pltpu.HBM if place in 'HL' else jax.Sh...]
    ppermute x21 -> x13, waiting for transfers between devices: 53.1 us -> 47.2 us  [flip(): lax.ppermute(value, axes, [(index, index ^ bits) for index in range(count)])]
    all_to_all x1, blocking collectives: 23.7 us -> 18 us  [exchange(): return lax.all_to_all(value, axes, 0, 0, tiled=True)]
    ppermute x7 -> x4, starting transfers between devices: 13.5 us -> 10.1 us  [swap(): return lax.ppermute(value, CORE, [(0, 1), (1, 0)])]
    ppermute x7 -> x4, waiting for transfers between devices: 8.11 us -> 7.37 us  [swap(): return lax.ppermute(value, CORE, [(0, 1), (1, 0)])]
  transfers between devices with their start and end apart: 33 -> 25, of which waited for: 15 -> 15; matrix products, arithmetic and copies ran while one was open for 1% -> 1% of each run, Pallas kernels for 6% -> 13%
where the time goes in v6:
time: 218 us; the launch traced here: 217 us
  waiting for transfers between devices  76.4 us (35%)
  starting transfers between devices  63.2 us (29%)
  Pallas kernels  40.1 us (18%)
  blocking collectives  18 us (8%)
  between operations  14 us (6%)
  local copies, waits for them, and re-layouts  5.41 us (2%)
    ppermute x13, waiting for transfers between devices, flip(): lax.ppermute(value, axes, [(index, index ^ bits) for index in range(count)])  47.2 us
    pallas_call x13, Pallas kernels, call(): pl.pallas_call(kernel, out_shape=[(pltpu.HBM if place in 'HL' else jax.Sh...  40.1 us
    all_to_all x5, starting transfers between devices, exchange(): return lax.all_to_all(value, axes, 0, 0, tiled=True)  30.2 us
    ppermute x13, starting transfers between devices, flip(): lax.ppermute(value, axes, [(index, index ^ bits) for index in range(count)])  22.8 us
    all_to_all x5, waiting for transfers between devices, exchange(): return lax.all_to_all(value, axes, 0, 0, tiled=True)  19.9 us
    all_to_all x1, blocking collectives, exchange(): return lax.all_to_all(value, axes, 0, 0, tiled=True)  18 us
    ppermute x4, starting transfers between devices, swap(): return lax.ppermute(value, CORE, [(0, 1), (1, 0)])  10.1 us
    ppermute x4, waiting for transfers between devices, swap(): return lax.ppermute(value, CORE, [(0, 1), (1, 0)])  7.37 us
  transfers between devices with their start and end apart: 25, of which 15 were waited for; matrix products, arithmetic and copies ran while one was open for 1% of the time, Pallas kernels for 13%

profile of v6, /device:TPU:1, one launch (start us, length us, event | category | flops | bytes accessed | tf_op | source)
XLA Modules:
  0.0 217.0 jit_solution(4672629499340079870)
XLA Ops:
  7.2 3.8 %shard_map.186 = (bf16[8,128,384]{2,1,0:T(8,128)(2,1)}, bf16[128,256]{1,0:T(8,128)(2,1)}, bf16[128,768]{1,0:T(8,128)(2,1)}) custom-call(bf16[2,128,768]{2,1,0:T(8,128)(2,1)} %tok_ref.5, f32[768]{0:T(1024)} %gain_ref.7, f32[768]{0:T(1024)} %shift_ref.2, bf16[768,2304]{1,0:T(8,128)(2,1)} %w_ref.3), custom_call_target="tpu_custom_call" | custom-call | flops 1000 | bytes 1000 | tf_op jit(solution)/shard_map/pallas_call | solution.py:106
  11.0 18.0 %all_to_all.30.refs_1_.same_ref.kvs_ref = bf16[8,128,384]{2,1,0:T(8,128)(2,1)S(1)} all-to-all(bf16[8,128,384]{2,1,0:T(8,128)(2,1)} %get-tuple-element.45), channel_id=1, replica_groups=mesh['y'=4,'xl'=2,'c'=2,'zh'=2,'zl'=2,'xh'=2] {'y','xl'}, dimensions={0} | all-to-all | bytes 1572864 | tf_op jit(solution)/shard_map/all_to_all | solution.py:506
  29.0 1.9 collective-permute-start
  30.9 1.9 collective-permute-done.other_ref.kvo_ref
  32.8 2.6 %shard_map.188 = bf16[8,128,256]{2,1,0:T(8,128)(2,1)} custom-call(s32[2,32]{1,0:T(2,128)S(1)} %copy-done.7, bf16[128,256]{1,0:T(8,128)(2,1)} %get-tuple-element.46.refs_0_.q_ref, bf16[8,128,384]{2,1,0:T(8,128)(2,1)S(1)} %all_to_all.30.refs_1_.same_ref.kvs_ref, bf16[8,128,384]{2,1,0:T(8,128)(2,1)S(1)} %collective-permute-done.other_ref.kvo_ref), custom_call_target="tpu_custom_call" | custom-call | flops 1000 | bytes 1000 | tf_op jit(solution)/shard_map/pallas_call | solution.py:106
  37.0 7.3 %all-to-all-start.1 = ((bf16[8,128,256]{2,1,0:T(8,128)(2,1)}), bf16[8,128,256]{2,1,0:T(8,128)(2,1)S(1)}, u32[]{:S(2)}, u32[]{:S(2)}) async-start(bf16[8,128,256]{2,1,0:T(8,128)(2,1)} %shard_map.188), calls=%async_computation.1 | async-start | bytes 1048576 | tf_op jit(solution)/shard_map/all_to_all | solution.py:506
  45.7 9.8 %all-to-all-done.1.mixed_ref = bf16[8,128,256]{2,1,0:T(8,128)(2,1)S(1)} async-done(((bf16[8,128,256]{2,1,0:T(8,128)(2,1)}), bf16[8,128,256]{2,1,0:T(8,128)(2,1)S(1)}, u32[]{:S(2)}, u32[]{:S(2)}) %all-to-all-start.1) | async-done | bytes 524320 | tf_op jit(solution)/shard_map/all_to_all | solution.py:506
  58.6 4.7 %shard_map.189 = (bf16[8,64,768]{2,1,0:T(8,128)(2,1)}, f32[8,32,768]{2,1,0:T(8,128)}, bf16[256,768]{1,0:T(8,128)(2,1)}, bf16[256,384]{1,0:T(8,128)(2,1)}, bf16[256,384]{1,0:T(8,128)(2,1)}) custom-call(bf16[8,128,256]{2,1,0:T(8,128)(2,1)S(1)} %all-to-all-done.1.mixed_ref, bf16[2,128,768]{2,1,0:T(8,128)(2,1)S(1)} %copy-done.3, ...), custom_call_target="tpu_custom_call" | custom-call | flops 1000 | bytes 1000 | tf_op jit(solution)/shard_map/pallas_call | solution.py:106
  63.3 3.6 %all-to-all-start.2 = ((bf16[8,64,768]{2,1,0:T(8,128)(2,1)}), bf16[8,64,768]{2,1,0:T(8,128)(2,1)S(1)}, u32[]{:S(2)}, u32[]{:S(2)}) async-start(bf16[8,64,768]{2,1,0:T(8,128)(2,1)} %get-tuple-element.47), calls=%async_computation.2 | async-start | bytes 1572864 | tf_op jit(solution)/shard_map/all_to_all | solution.py:506
  66.9 2.9 %shard_map.190.refs_1_ = bf16[768,768]{1,0:T(8,128)(2,1)} custom-call(bf16[256,768]{1,0:T(8,128)(2,1)} %get-tuple-element.48.normed_ref, bf16[256,384]{1,0:T(8,128)(2,1)} %get-tuple-element.49.act_ref, bf16[256,384]{1,0:T(8,128)(2,1)} %get-tuple-element.50.gpre_ref, bf16[2,128,768]{2,1,0:T(8,128)(2,1)} %og_ref.5), custom_call_target="tpu_custom_call" | custom-call | flops 1000 | bytes 1000 | tf_op jit(solution)/shard_map/pallas_call | solution.py:106
  69.8 10.1 %all-to-all-done.2.refs_0_ = bf16[8,64,768]{2,1,0:T(8,128)(2,1)S(1)} async-done(((bf16[8,64,768]{2,1,0:T(8,128)(2,1)}), bf16[8,64,768]{2,1,0:T(8,128)(2,1)S(1)}, u32[]{:S(2)}, u32[]{:S(2)}) %all-to-all-start.2) | async-done | bytes 786464 | tf_op jit(solution)/shard_map/all_to_all | solution.py:506
  79.9 4.2 %shard_map.192 = (bf16[32,32,256]{2,1,0:T(8,128)(2,1)}, bf16[32,768]{1,0:T(8,128)(2,1)}, f32[32,768]{1,0:T(8,128)}, bf16[32,768]{1,0:T(8,128)(2,1)}, f32[8,768]{1,0:T(8,128)}, /*index=5*/bf16[32,768]{1,0:T(8,128)(2,1)}) custom-call(bf16[8,64,768]{2,1,0:T(8,128)(2,1)S(1)} %shard_map.191.sums_ref, f32[8,32,768]{2,1,0:T(8,128)} %get-tuple-element.51.middle_ref, ...), custom_call_target="tpu_custom_call" | custom-call | flops 1000 | bytes 1000 | tf_op jit(solution)/shard_map/pallas_call | solution.py:106
  84.1 3.9 %all-to-all-start.3 = ((bf16[32,32,256]{2,1,0:T(8,128)(2,1)}), bf16[32,32,256]{2,1,0:T(8,128)(2,1)S(1)}, u32[]{:S(2)}, u32[]{:S(2)}) async-start(bf16[32,32,256]{2,1,0:T(8,128)(2,1)} %get-tuple-element.52), calls=%async_computation.3 | async-start | bytes 1048576 | tf_op jit(solution)/shard_map/all_to_all | solution.py:506
  88.0 3.6 %collective-permute-start.3 = (bf16[32,768]{1,0:T(8,128)(2,1)}, bf16[32,768]{1,0:T(8,128)(2,1)S(1)}, u32[]{:S(2)}, u32[]{:S(2)}) collective-permute-start(bf16[32,768]{1,0:T(8,128)(2,1)} %get-tuple-element.53.low0_ref), channel_id=1, source_target_pairs={{0,3},{1,2},{2,1},{3,0},{4,7},{5,6},{6,5},{7,4},{8,11},{9,10},{10,... | collective-permute-start | bytes 147464 | tf_op jit(solution)/shard_map/ppermute | solution.py:526
  92.3 6.8 %collective-permute-done.3.refs_3_.low3_ref = bf16[32,768]{1,0:T(8,128)(2,1)S(1)} collective-permute-done((bf16[32,768]{1,0:T(8,128)(2,1)}, bf16[32,768]{1,0:T(8,128)(2,1)S(1)}, u32[]{:S(2)}, u32[]{:S(2)}) %collective-permute-start.3) | collective-permute-done | bytes 49184 | tf_op jit(solution)/shard_map/ppermute | solution.py:526
  99.3 5.2 %collective-permute-start.4 = (bf16[8,128,256]{2,1,0:T(8,128)(2,1)S(1)}, bf16[8,128,256]{2,1,0:T(8,128)(2,1)S(1)}, u32[]{:S(2)}, u32[]{:S(2)}) collective-permute-start(bf16[8,128,256]{2,1,0:T(8,128)(2,1)S(1)} %shard_map.193.gs_ref), channel_id=1, source_target_pairs={{0,8},{8,0},{1,9},{9,1},{2,10},{10,2},{3,11},{11,3},{4,12},{12,4},... | collective-permute-start | bytes 1572872 | tf_op jit(solution)/shard_map/ppermute | solution.py:510
  106.0 6.5 %shard_map.194 = (f32[32,768]{1,0:T(8,128)}, bf16[32,768]{1,0:T(8,128)(2,1)}, bf16[32,768]{1,0:T(8,128)(2,1)}, bf16[32,768]{1,0:T(8,128)(2,1)}, bf16[16,48,384]{...) custom-call(s32[2,32]{1,0:T(2,128)S(1)} %copy-done.7, bf16[8,128,384]{2,1,0:T(8,128)(2,1)} %copy-done, ...), custom_call_target="tpu_custom_call" | custom-call | flops 1000 | bytes 1000 | tf_op jit(solution)/shard_map/pallas_call | solution.py:106
  115.6 5.1 %all-to-all-start.4 = ((bf16[16,48,384]{2,1,0:T(8,128)(2,1)}), bf16[16,48,384]{2,1,0:T(8,128)(2,1)S(1)}, u32[]{:S(2)}, u32[]{:S(2)}) async-start(bf16[16,48,384]{2,1,0:T(8,128)(2,1)} %shard_map.197), calls=%async_computation.4 | async-start | bytes 1179648 | tf_op jit(solution)/shard_map/all_to_all | solution.py:506
  124.9 7.5 %collective-permute-done.5.one_ref = bf16[32,768]{1,0:T(8,128)(2,1)S(1)} collective-permute-done((bf16[32,768]{1,0:T(8,128)(2,1)S(1)}, bf16[32,768]{1,0:T(8,128)(2,1)S(1)}, u32[]{:S(2)}, u32[]{:S(2)}) %collective-permute-start.5) | collective-permute-done | bytes 49184 | tf_op jit(solution)/shard_map/ppermute | solution.py:526
  134.3 1.9 shard_map.195
  136.2 2.4 %shard_map.199 = bf16[8,8,56,384]{3,2,1,0:T(8,128)(2,1)} custom-call(bf16[16,48,384]{2,1,0:T(8,128)(2,1)S(1)} %shard_map.198.in_ref, f32[8,768]{1,0:T(8,128)} %get-tuple-element.68.refs_1_.vec_ref), custom_call_target="tpu_custom_call" | custom-call | flops 1000 | bytes 1000 | tf_op jit(solution)/shard_map/pallas_call | solution.py:106
  138.6 10.4 %all-to-all-start.5 = ((bf16[64,56,384]{2,1,0:T(8,128)(2,1)}), bf16[64,56,384]{2,1,0:T(8,128)(2,1)S(1)}, u32[]{:S(2)}, u32[]{:S(2)}) async-start(bf16[64,56,384]{2,1,0:T(8,128)(2,1)} %bitcast.7), calls=%async_computation.6 | async-start | bytes 5505024 | tf_op jit(solution)/shard_map/all_to_all | solution.py:506
  149.7 4.7 %collective-permute-start.14 = (bf16[64,768]{1,0:T(8,128)(2,1)S(1)}, bf16[64,768]{1,0:T(8,128)(2,1)S(1)}, u32[]{:S(2)}, u32[]{:S(2)}) collective-permute-start(bf16[64,768]{1,0:T(8,128)(2,1)S(1)} %copy-done.8), channel_id=1, source_target_pairs={{0,7},{1,6},{2,5},{3,4},{4,3},{5,2},{6,1},{7,0},{8,15},{9,14},{10,... | collective-permute-start | bytes 294920 | tf_op jit(solution)/shard_map/ppermute | solution.py:526
  157.9 2.2 %collective-permute-start.10 = (bf16[64,768]{1,0:T(8,128)(2,1)S(1)}, bf16[64,768]{1,0:T(8,128)(2,1)S(1)}, u32[]{:S(2)}, u32[]{:S(2)}) collective-permute-start(bf16[64,768]{1,0:T(8,128)(2,1)S(1)} %copy-done.8), channel_id=1, source_target_pairs={{0,3},{1,2},{2,1},{3,0},{4,7},{5,6},{6,5},{7,4},{8,11},{9,10},{10,... | collective-permute-start | bytes 294920 | tf_op jit(solution)/shard_map/ppermute | solution.py:526
  160.1 27.1 %collective-permute-done.14.refs_7_ = bf16[64,768]{1,0:T(8,128)(2,1)S(1)} collective-permute-done((bf16[64,768]{1,0:T(8,128)(2,1)S(1)}, bf16[64,768]{1,0:T(8,128)(2,1)S(1)}, u32[]{:S(2)}, u32[]{:S(2)}) %collective-permute-start.14) | collective-permute-done | bytes 98336 | tf_op jit(solution)/shard_map/ppermute | solution.py:526
  188.7 4.0 %collective-permute-start.8 = (bf16[64,768]{1,0:T(8,128)(2,1)S(1)}, bf16[64,768]{1,0:T(8,128)(2,1)S(1)}, u32[]{:S(2)}, u32[]{:S(2)}) collective-permute-start(bf16[64,768]{1,0:T(8,128)(2,1)S(1)} %copy-done.8), channel_id=1, source_target_pairs={{0,1},{1,0},{2,3},{3,2},{4,5},{5,4},{6,7},{7,6},{8,9},{9,8},{10,11... | collective-permute-start | bytes 294920 | tf_op jit(solution)/shard_map/ppermute | solution.py:526
  195.0 2.0 shard_map.196
  197.4 2.7 %shard_map.200 = (f32[768,384]{1,0:T(8,128)}, f32[384,768]{1,0:T(8,128)}) custom-call(bf16[768,768]{1,0:T(8,128)(2,1)} %all-gather.5.cloned.1.call-done.in_ref), custom_call_target="tpu_custom_call" | custom-call | flops 1000 | bytes 1000 | tf_op jit(solution)/shard_map/pallas_call | solution.py:106
  200.1 2.6 %collective-permute-start.16 = (bf16[8,8,56,384]{3,2,1,0:T(8,128)(2,1)S(1)}, bf16[8,8,56,384]{3,2,1,0:T(8,128)(2,1)S(1)}, u32[]{:S(2)}, u32[]{:S(2)}) collective-permute-start(bf16[8,8,56,384]{3,2,1,0:T(8,128)(2,1)S(1)} %shard_map.201.in_ref), channel_id=1, source_target_pairs={{0,8},{8,0},{1,9},{9,1},{2,10},{10,2},{3,11},{11,3},{4,12},{12,4},... | collective-permute-start | bytes 8257544 | tf_op jit(solution)/shard_map/ppermute | solution.py:510
  202.7 2.4 %shard_map.202 = (f32[768,2304]{1,0:T(8,128)}, f32[768,768]{1,0:T(8,128)}, f32[8,384]{1,0:T(8,128)S(1)}) custom-call(bf16[8,8,56,384]{3,2,1,0:T(8,128)(2,1)S(1)} %shard_map.201.in_ref), custom_call_target="tpu_custom_call" | custom-call | flops 1000 | bytes 1000 | tf_op jit(solution)/shard_map/pallas_call | solution.py:106
  205.2 2.3 %collective-permute-done.16.in_ref = bf16[8,8,56,384]{3,2,1,0:T(8,128)(2,1)S(1)} collective-permute-done((bf16[8,8,56,384]{3,2,1,0:T(8,128)(2,1)S(1)}, bf16[8,8,56,384]{3,2,1,0:T(8,128)(2,1)S(1)}, u32[]{:S(2)}, u32[]{:S(2)}) %collective-permute-start.16) | collective-permute-done | bytes 2752544 | tf_op jit(solution)/shard_map/ppermute | solution.py:510
  207.5 3.0 %shard_map.203 = (f32[768,2304]{1,0:T(8,128)}, f32[768,768]{1,0:T(8,128)}, f32[768]{0:T(1024)}, f32[768]{0:T(1024)}, f32[768]{0:T(1024)}, /*index=5*/f32[768]{0:T(1024)}) custom-call(bf16[8,8,56,384]{3,2,1,0:T(8,128)(2,1)S(1)} %collective-permute-done.16.in_ref, ...), custom_call_target="tpu_custom_call", output_to_operand_aliasing={{0}: (2, {}), {1}: (3, {})} | custom-call | flops 1000 | bytes 1000 | tf_op jit(solution)/shard_map/pallas_call | solution.py:106
  (65 shorter events, 26.1 us)
Async XLA Ops:
  7.2 25.6 %copy-start.7 = (s32[2,32]{1,0:T(2,128)S(1)}, s32[2,32]{1,0:T(2,128)}, u32[]{:S(2)}) copy-start(s32[2,32]{1,0:T(2,128)} %scene_ref.3) | copy-start | bytes 772
  29.0 16.7 %copy-start = (bf16[8,128,384]{2,1,0:T(8,128)(2,1)}, bf16[8,128,384]{2,1,0:T(8,128)(2,1)S(1)}, u32[]{:S(2)}) copy-start(bf16[8,128,384]{2,1,0:T(8,128)(2,1)S(1)} %all_to_all.30.refs_1_.same_ref.kvs_ref) | copy-start | bytes 2359300
  29.0 3.8 %collective-permute-start = (bf16[8,128,384]{2,1,0:T(8,128)(2,1)S(1)}, bf16[8,128,384]{2,1,0:T(8,128)(2,1)S(1)}, u32[]{:S(2)}, u32[]{:S(2)}) collective-permute-start(bf16[8,128,384]{2,1,0:T(8,128)(2,1)S(1)} %all_to_all.30.refs_1_.same_ref.kvs_ref), channel_id=1, source_target_pairs={{0,8},{8,0},{1,9},{9,1},{2,10},{10,2},{3,11},{11,3},{4,12},{12,4},... | collective-permute-start | bytes 2359304 | tf_op jit(solution)/shard_map/ppermute | solution.py:510
  36.3 19.2 %copy-start.2 = (bf16[2,128,768]{2,1,0:T(8,128)(2,1)S(1)}, bf16[2,128,768]{2,1,0:T(8,128)(2,1)}, u32[]{:S(2)}) copy-start(bf16[2,128,768]{2,1,0:T(8,128)(2,1)} %og_ref.5) | copy-start | bytes 1179652
  36.3 68.2 %all-gather.3.cloned.1.call-start = ((), (), s32[]{:S(2)}) async-start(), calls=%async_computation.7 | async-start | bytes 1114112 | tf_op jit(solution)/shard_map/all_gather | solution.py:553
  37.0 18.5 %all-to-all-start.1 = ((bf16[8,128,256]{2,1,0:T(8,128)(2,1)}), bf16[8,128,256]{2,1,0:T(8,128)(2,1)S(1)}, u32[]{:S(2)}, u32[]{:S(2)}) async-start(bf16[8,128,256]{2,1,0:T(8,128)(2,1)} %shard_map.188), calls=%async_computation.1 | async-start | bytes 1048576 | tf_op jit(solution)/shard_map/all_to_all | solution.py:506
  63.3 16.6 %all-to-all-start.2 = ((bf16[8,64,768]{2,1,0:T(8,128)(2,1)}), bf16[8,64,768]{2,1,0:T(8,128)(2,1)S(1)}, u32[]{:S(2)}, u32[]{:S(2)}) async-start(bf16[8,64,768]{2,1,0:T(8,128)(2,1)} %get-tuple-element.47), calls=%async_computation.2 | async-start | bytes 1572864 | tf_op jit(solution)/shard_map/all_to_all | solution.py:506
  66.9 69.3 %reduce-scatter.2.cloned.1.call-start = ((), (), s32[]{:S(2)}) async-start(), calls=%async_computation.8 | async-start | bytes 1253376 | tf_op jit(solution)/shard_map/reduce_scatter | solution.py:574
  84.1 15.2 %all-to-all-start.3 = ((bf16[32,32,256]{2,1,0:T(8,128)(2,1)}), bf16[32,32,256]{2,1,0:T(8,128)(2,1)S(1)}, u32[]{:S(2)}, u32[]{:S(2)}) async-start(bf16[32,32,256]{2,1,0:T(8,128)(2,1)} %get-tuple-element.52), calls=%async_computation.3 | async-start | bytes 1048576 | tf_op jit(solution)/shard_map/all_to_all | solution.py:506
  88.0 11.0 %collective-permute-start.3 = (bf16[32,768]{1,0:T(8,128)(2,1)}, bf16[32,768]{1,0:T(8,128)(2,1)S(1)}, u32[]{:S(2)}, u32[]{:S(2)}) collective-permute-start(bf16[32,768]{1,0:T(8,128)(2,1)} %get-tuple-element.53.low0_ref), channel_id=1, source_target_pairs={{0,3},{1,2},{2,1},{3,0},{4,7},{5,6},{6,5},{7,4},{8,11},{9,10},{10,... | collective-permute-start | bytes 147464 | tf_op jit(solution)/shard_map/ppermute | solution.py:526
  91.6 7.4 %collective-permute-start.2 = (bf16[32,768]{1,0:T(8,128)(2,1)}, bf16[32,768]{1,0:T(8,128)(2,1)S(1)}, u32[]{:S(2)}, u32[]{:S(2)}) collective-permute-start(bf16[32,768]{1,0:T(8,128)(2,1)} %get-tuple-element.53.low0_ref), channel_id=1, source_target_pairs={{0,2},{1,3},{2,0},{3,1},{4,6},{5,7},{6,4},{7,5},{8,10},{9,11},{10,... | collective-permute-start | bytes 147464 | tf_op jit(solution)/shard_map/ppermute | solution.py:526
  91.9 7.4 %collective-permute-start.1 = (bf16[32,768]{1,0:T(8,128)(2,1)}, bf16[32,768]{1,0:T(8,128)(2,1)S(1)}, u32[]{:S(2)}, u32[]{:S(2)}) collective-permute-start(bf16[32,768]{1,0:T(8,128)(2,1)} %get-tuple-element.53.low0_ref), channel_id=1, source_target_pairs={{0,1},{1,0},{2,3},{3,2},{4,5},{5,4},{6,7},{7,6},{8,9},{9,8},{10,11... | collective-permute-start | bytes 147464 | tf_op jit(solution)/shard_map/ppermute | solution.py:526
  99.3 6.7 %collective-permute-start.4 = (bf16[8,128,256]{2,1,0:T(8,128)(2,1)S(1)}, bf16[8,128,256]{2,1,0:T(8,128)(2,1)S(1)}, u32[]{:S(2)}, u32[]{:S(2)}) collective-permute-start(bf16[8,128,256]{2,1,0:T(8,128)(2,1)S(1)} %shard_map.193.gs_ref), channel_id=1, source_target_pairs={{0,8},{8,0},{1,9},{9,1},{2,10},{10,2},{3,11},{11,3},{4,12},{12,4},... | collective-permute-start | bytes 1572872 | tf_op jit(solution)/shard_map/ppermute | solution.py:510
  112.5 8.2 %copy-start.11 = (bf16[32,768]{1,0:T(8,128)(2,1)S(1)}, bf16[32,768]{1,0:T(8,128)(2,1)}, u32[]{:S(2)}) copy-start(bf16[32,768]{1,0:T(8,128)(2,1)} %get-tuple-element.56) | copy-start | bytes 147460
  112.6 9.8 %copy-start.10 = (bf16[32,768]{1,0:T(8,128)(2,1)S(1)}, bf16[32,768]{1,0:T(8,128)(2,1)}, u32[]{:S(2)}) copy-start(bf16[32,768]{1,0:T(8,128)(2,1)} %get-tuple-element.57) | copy-start | bytes 147460
  112.6 10.6 %copy-start.9 = (bf16[32,768]{1,0:T(8,128)(2,1)S(1)}, bf16[32,768]{1,0:T(8,128)(2,1)}, u32[]{:S(2)}) copy-start(bf16[32,768]{1,0:T(8,128)(2,1)} %get-tuple-element.58) | copy-start | bytes 147460
  112.6 2.1 collective-permute-start.15
  115.6 20.5 %all-to-all-start.4 = ((bf16[16,48,384]{2,1,0:T(8,128)(2,1)}), bf16[16,48,384]{2,1,0:T(8,128)(2,1)S(1)}, u32[]{:S(2)}, u32[]{:S(2)}) async-start(bf16[16,48,384]{2,1,0:T(8,128)(2,1)} %shard_map.197), calls=%async_computation.4 | async-start | bytes 1179648 | tf_op jit(solution)/shard_map/all_to_all | solution.py:506
  120.7 11.8 %collective-permute-start.5 = (bf16[32,768]{1,0:T(8,128)(2,1)S(1)}, bf16[32,768]{1,0:T(8,128)(2,1)S(1)}, u32[]{:S(2)}, u32[]{:S(2)}) collective-permute-start(bf16[32,768]{1,0:T(8,128)(2,1)S(1)} %copy-done.11), channel_id=1, source_target_pairs={{0,1},{1,0},{2,3},{3,2},{4,5},{5,4},{6,7},{7,6},{8,9},{9,8},{10,11... | collective-permute-start | bytes 147464 | tf_op jit(solution)/shard_map/ppermute | solution.py:526
  122.3 10.1 %collective-permute-start.6 = (bf16[32,768]{1,0:T(8,128)(2,1)S(1)}, bf16[32,768]{1,0:T(8,128)(2,1)S(1)}, u32[]{:S(2)}, u32[]{:S(2)}) collective-permute-start(bf16[32,768]{1,0:T(8,128)(2,1)S(1)} %copy-done.10), channel_id=1, source_target_pairs={{0,2},{1,3},{2,0},{3,1},{4,6},{5,7},{6,4},{7,5},{8,10},{9,11},{10,... | collective-permute-start | bytes 147464 | tf_op jit(solution)/shard_map/ppermute | solution.py:526
  123.1 11.1 %collective-permute-start.7 = (bf16[32,768]{1,0:T(8,128)(2,1)S(1)}, bf16[32,768]{1,0:T(8,128)(2,1)S(1)}, u32[]{:S(2)}, u32[]{:S(2)}) collective-permute-start(bf16[32,768]{1,0:T(8,128)(2,1)S(1)} %copy-done.9), channel_id=1, source_target_pairs={{0,3},{1,2},{2,1},{3,0},{4,7},{5,6},{6,5},{7,4},{8,11},{9,10},{10,... | collective-permute-start | bytes 147464 | tf_op jit(solution)/shard_map/ppermute | solution.py:526
  138.6 11.1 %copy-start.8 = (bf16[64,768]{1,0:T(8,128)(2,1)S(1)}, bf16[64,768]{1,0:T(8,128)(2,1)}, u32[]{:S(2)}) copy-start(bf16[64,768]{1,0:T(8,128)(2,1)} %get-tuple-element.63.refs_0_) | copy-start | bytes 294916
  138.6 61.5 %all-to-all-start.5 = ((bf16[64,56,384]{2,1,0:T(8,128)(2,1)}), bf16[64,56,384]{2,1,0:T(8,128)(2,1)S(1)}, u32[]{:S(2)}, u32[]{:S(2)}) async-start(bf16[64,56,384]{2,1,0:T(8,128)(2,1)} %bitcast.7), calls=%async_computation.6 | async-start | bytes 5505024 | tf_op jit(solution)/shard_map/all_to_all | solution.py:506
  149.0 48.4 %all-gather.5.cloned.1.call-start = ((), (), s32[]{:S(2)}) async-start(), calls=%async_computation.9 | async-start | bytes 1253376 | tf_op jit(solution)/shard_map/all_gather | solution.py:575
  149.7 37.4 %collective-permute-start.14 = (bf16[64,768]{1,0:T(8,128)(2,1)S(1)}, bf16[64,768]{1,0:T(8,128)(2,1)S(1)}, u32[]{:S(2)}, u32[]{:S(2)}) collective-permute-start(bf16[64,768]{1,0:T(8,128)(2,1)S(1)} %copy-done.8), channel_id=1, source_target_pairs={{0,7},{1,6},{2,5},{3,4},{4,3},{5,2},{6,1},{7,0},{8,15},{9,14},{10,... | collective-permute-start | bytes 294920 | tf_op jit(solution)/shard_map/ppermute | solution.py:526
  154.5 34.2 %collective-permute-start.13 = (bf16[64,768]{1,0:T(8,128)(2,1)S(1)}, bf16[64,768]{1,0:T(8,128)(2,1)S(1)}, u32[]{:S(2)}, u32[]{:S(2)}) collective-permute-start(bf16[64,768]{1,0:T(8,128)(2,1)S(1)} %copy-done.8), channel_id=1, source_target_pairs={{0,6},{1,7},{2,4},{3,5},{4,2},{5,3},{6,0},{7,1},{8,14},{9,15},{10,... | collective-permute-start | bytes 294920 | tf_op jit(solution)/shard_map/ppermute | solution.py:526
  154.7 37.9 %collective-permute-start.12 = (bf16[64,768]{1,0:T(8,128)(2,1)S(1)}, bf16[64,768]{1,0:T(8,128)(2,1)S(1)}, u32[]{:S(2)}, u32[]{:S(2)}) collective-permute-start(bf16[64,768]{1,0:T(8,128)(2,1)S(1)} %copy-done.8), channel_id=1, source_target_pairs={{0,5},{1,4},{2,7},{3,6},{4,1},{5,0},{6,3},{7,2},{8,13},{9,12},{10,... | collective-permute-start | bytes 294920 | tf_op jit(solution)/shard_map/ppermute | solution.py:526
  156.2 36.5 %collective-permute-start.11 = (bf16[64,768]{1,0:T(8,128)(2,1)S(1)}, bf16[64,768]{1,0:T(8,128)(2,1)S(1)}, u32[]{:S(2)}, u32[]{:S(2)}) collective-permute-start(bf16[64,768]{1,0:T(8,128)(2,1)S(1)} %copy-done.8), channel_id=1, source_target_pairs={{0,4},{1,5},{2,6},{3,7},{4,0},{5,1},{6,2},{7,3},{8,12},{9,13},{10,... | collective-permute-start | bytes 294920 | tf_op jit(solution)/shard_map/ppermute | solution.py:526
  157.9 34.8 %collective-permute-start.10 = (bf16[64,768]{1,0:T(8,128)(2,1)S(1)}, bf16[64,768]{1,0:T(8,128)(2,1)S(1)}, u32[]{:S(2)}, u32[]{:S(2)}) collective-permute-start(bf16[64,768]{1,0:T(8,128)(2,1)S(1)} %copy-done.8), channel_id=1, source_target_pairs={{0,3},{1,2},{2,1},{3,0},{4,7},{5,6},{6,5},{7,4},{8,11},{9,10},{10,... | collective-permute-start | bytes 294920 | tf_op jit(solution)/shard_map/ppermute | solution.py:526
  187.2 6.3 %collective-permute-start.9 = (bf16[64,768]{1,0:T(8,128)(2,1)S(1)}, bf16[64,768]{1,0:T(8,128)(2,1)S(1)}, u32[]{:S(2)}, u32[]{:S(2)}) collective-permute-start(bf16[64,768]{1,0:T(8,128)(2,1)S(1)} %copy-done.8), channel_id=1, source_target_pairs={{0,2},{1,3},{2,0},{3,1},{4,6},{5,7},{6,4},{7,5},{8,10},{9,11},{10,... | collective-permute-start | bytes 294920 | tf_op jit(solution)/shard_map/ppermute | solution.py:526
  188.7 6.3 %collective-permute-start.8 = (bf16[64,768]{1,0:T(8,128)(2,1)S(1)}, bf16[64,768]{1,0:T(8,128)(2,1)S(1)}, u32[]{:S(2)}, u32[]{:S(2)}) collective-permute-start(bf16[64,768]{1,0:T(8,128)(2,1)S(1)} %copy-done.8), channel_id=1, source_target_pairs={{0,1},{1,0},{2,3},{3,2},{4,5},{5,4},{6,7},{7,6},{8,9},{9,8},{10,11... | collective-permute-start | bytes 294920 | tf_op jit(solution)/shard_map/ppermute | solution.py:526
  200.1 7.3 %collective-permute-start.16 = (bf16[8,8,56,384]{3,2,1,0:T(8,128)(2,1)S(1)}, bf16[8,8,56,384]{3,2,1,0:T(8,128)(2,1)S(1)}, u32[]{:S(2)}, u32[]{:S(2)}) collective-permute-start(bf16[8,8,56,384]{3,2,1,0:T(8,128)(2,1)S(1)} %shard_map.201.in_ref), channel_id=1, source_target_pairs={{0,8},{8,0},{1,9},{9,1},{2,10},{10,2},{3,11},{11,3},{4,12},{12,4},... | collective-permute-start | bytes 8257544 | tf_op jit(solution)/shard_map/ppermute | solution.py:510
  (5 other events, 8.7 us)
Sparse Core Ops, SparseCore 0:
  38.8 33.9 all-gather.2
  75.8 59.4 reduce-scatter.1
  151.5 45.8 all-gather.4

commit v7 on v5

--- a/solution.py
+++ b/solution.py
@@ -112,7 +112,7 @@
         out_specs=[pl.BlockSpec(memory_space=places[place]) for _, _, place in outs],
         scratch_shapes=list(scratch),
         input_output_aliases=aliases or {},
-        cost_estimate=pl.CostEstimate(flops=cost, bytes_accessed=2000000, transcendentals=0),
+        cost_estimate=pl.CostEstimate(flops=1000, bytes_accessed=1000, transcendentals=0),
         compiler_params=pltpu.CompilerParams(vmem_limit_bytes=vmem * 2**20),
     )(*[pin(value) if place in "HL" else value for value, place in ins])
 
@@ -207,28 +207,42 @@
 
 def forward_kernel(
     mixed_ref, tok_ref, og_ref, wo_ref, gain_ref, shift_ref, up_ref, down_ref,
-    out_ref, middle_ref, normed_ref, act_ref, gpre_ref, grad_buf, branch_buf, sem,
+    out_ref, middle_ref, normed_ref, act_ref, gpre_ref,
+    tok_buf, og_buf, up_buf, down_buf, grad_buf, branch_buf, in_sem, sem,
 ):
-    total = tok_ref[...].reshape(2 * TOK, D).astype(F32)
+    loads = [
+        pltpu.make_async_copy(ref, buf, in_sem.at[index])
+        for index, (ref, buf) in enumerate(
+            ((tok_ref, tok_buf), (up_ref, up_buf), (og_ref, og_buf), (down_ref, down_buf))
+        )
+    ]
+    for load in loads:
+        load.start()
+    total = jnp.zeros((2 * TOK, D), F32)
     for group in range(4):
         rows = jnp.concatenate([mixed_ref[group], mixed_ref[4 + group]], axis=0)
         total = total + mm(rows, wo_ref[group])
+    loads[0].wait()
+    total = total + tok_buf[...].reshape(2 * TOK, D).astype(F32)
     middle_ref[...] = total.reshape(8, BLK, D)
     unit, _ = normalized(total)
     normed = (unit * gain_ref[...].reshape(1, D) + shift_ref[...].reshape(1, D)).astype(BF)
     normed_ref[...] = normed
-    pre = mm(normed, up_ref[...])
+    loads[1].wait()
+    pre = mm(normed, up_buf[...])
     cdf = 0.5 * (1.0 + lax.erf(pre * (0.5**0.5)))
     slope = cdf + pre * jnp.exp(-0.5 * pre * pre) * 0.3989422804014327
-    grad_out = og_ref[...].reshape(2 * TOK, D)
-    gpre = (mm_nt(grad_out, down_ref[...]) * slope).astype(BF)
+    loads[2].wait()
+    loads[3].wait()
+    grad_out = og_buf[...].reshape(2 * TOK, D)
+    gpre = (mm_nt(grad_out, down_buf[...]) * slope).astype(BF)
     gpre_ref[...] = gpre
-    grad_buf[...] = mm_nt(gpre, up_ref[...]).astype(BF).reshape(8, BLK, D)
+    grad_buf[...] = mm_nt(gpre, up_buf[...]).astype(BF).reshape(8, BLK, D)
     first = pltpu.make_async_copy(grad_buf, out_ref.at[:, pl.ds(BLK, BLK)], sem.at[0])
     first.start()
     act = (pre * cdf).astype(BF)
     act_ref[...] = act
-    branch_buf[...] = mm(act, down_ref[...]).astype(BF).reshape(8, BLK, D)
+    branch_buf[...] = mm(act, down_buf[...]).astype(BF).reshape(8, BLK, D)
     second = pltpu.make_async_copy(branch_buf, out_ref.at[:, pl.ds(0, BLK)], sem.at[1])
     second.start()
     first.wait()
@@ -266,7 +280,9 @@
 
 
 def pair_kernel(one_ref, two_ref, out_ref):
-    out_ref[...] = (one_ref[...].astype(F32) + two_ref[...].astype(F32)).astype(BF)
+    total = (one_ref[...].astype(F32) + two_ref[...].astype(F32)).astype(BF)
+    out_ref[0] = total[:, :384]
+    out_ref[1] = total[:, 384:]
 
 
 def middle_kernel(
@@ -294,7 +310,6 @@
     grad_mid = og_buf[...].astype(F32) + norm_back(grad, unit, inverse, gain_ref[...].reshape(1, D))
     low = grad_mid.astype(BF)
     lane = lax.broadcasted_iota(jnp.int32, (BLK, 256), 1)
-    sends = []
     for head_group in range(4):
         mixed = mixed_buf[head_group].astype(F32)
         back = mm_nt(low, wo_ref[head_group]).astype(BF).astype(F32)
@@ -305,9 +320,7 @@
             columns += three(jnp.sum(jnp.where(inside, product, 0.0), axis=-1, keepdims=True))
         stats = put_columns(256, BLK, 9, columns)
         buf[head_group] = jnp.where(lane < 9, mixed, jnp.where(lane < HD, stats, back)).astype(BF)
-        sends += send_copies(
-            buf.at[head_group], out_ref, [chip * 4 + head_group for chip in range(8)], sem
-        )
+    sends = send_copies(buf, out_ref, range(8), sem)
     low_ref[...] = low
     grad_ref[...] = grad_mid
     result_ref[...] = (middle + branch).astype(BF)
@@ -318,9 +331,8 @@
 
 
 def attend_back_kernel(
-    scene_ref, kvs_ref, kvo_ref, gs_ref, go_ref, normed_ref, mixed_ref, low0_ref, low1_ref, low2_ref, low3_ref, w_ref,
-    own_ref, one_ref, two_ref, three_ref, keep_ref, send_ref,
-    kv_buf, gqkv_buf, grad_buf, part_buf, mixed_buf, w_buf, kv_sem, mixed_sem, w_sem,
+    scene_ref, kvs_ref, kvo_ref, gs_ref, go_ref, normed_ref, mixed_ref, low0_ref, low1_ref, low2_ref, low3_ref,
+    gqkv_ref, keep_ref, send_ref, kv_buf, grad_buf, mixed_buf, kv_sem, mixed_sem,
 ):
     first, big = span(scene_ref)
     chip = chip_index()
@@ -372,7 +384,7 @@
             dv.append(mm(probs.astype(BF), grad[gb]))
             dk.append(mm((probs * gap).astype(BF), query[qb]) * scale)
         tail = dq[2]
-        gqkv_buf[...] = jnp.concatenate(
+        gqkv_ref[...] = jnp.concatenate(
             [join(dk[0], dk[1]), join(dk[2], dv[0]), join(dv[1], dv[2]), join(dq[0], dq[1]),
              join(tail, jnp.zeros_like(tail))],
             axis=1,
@@ -381,7 +393,6 @@
     index = lax.axis_index(MICRO) * 4 + group
     load_mixed = pltpu.make_async_copy(mixed_ref.at[index], mixed_buf, mixed_sem)
     load_mixed.start()
-    loads = weight_copies(w_ref, w_buf, w_sem)
 
     @pl.when(big)
     def _():
@@ -391,7 +402,7 @@
     def _():
         run(1)
 
-    grad_buf[...] = mm_tn(normed_ref[...], gqkv_buf[...])
+    grad_buf[...] = mm_tn(normed_ref[...], gqkv_ref[...])
     load_mixed.wait()
     low = jnp.concatenate([ref[...] for ref in (low0_ref, low1_ref, low2_ref, low3_ref)], axis=0)
     mixed = jnp.concatenate(
@@ -410,33 +421,62 @@
                 [rows[:, 384:576], jnp.where(owner == 1, pieces[1], pieces[0])], axis=1
             ).astype(BF)
 
+def normed_grad_kernel(
+    gqkv_ref, tok_ref, w_ref, vec_ref, own_ref, one_ref, two_ref, three_ref, sums_ref,
+    x_buf, part_buf, w_buf, x_sem, w_sem,
+):
+    load = pltpu.make_async_copy(tok_ref.at[lax.axis_index(MICRO)], x_buf, x_sem)
+    load.start()
+    loads = weight_copies(w_ref, w_buf, w_sem)
+    group = group_index()
     odd = (group % 2) == 1
+    load.wait()
+    unit, _ = normalized(x_buf[...].astype(F32))
     total = jnp.zeros((TOK, D), F32)
     for slot in range(3):
-        loads[slot].wait()
-        part = gqkv_buf[:, slot * 192:(slot + 1) * 192]
+        part = gqkv_ref[:, slot * 192:(slot + 1) * 192]
         zero = jnp.zeros_like(part)
         wide = jnp.where(
             odd, jnp.concatenate([zero, part], axis=1), jnp.concatenate([part, zero], axis=1)
         )
+        loads[slot].wait()
         total = total + mm_nt(wide, w_buf[slot])
     part_buf[...] = total
     own_ref[...] = part_buf[pl.ds(pl.multiple_of(group * BLK, BLK), BLK)]
     for k, ref in ((1, one_ref), (2, two_ref), (3, three_ref)):
         ref[...] = part_buf[pl.ds(pl.multiple_of((group ^ k) * BLK, BLK), BLK)].astype(BF)
-
-
-def add_kernel(one_ref, two_ref, out_ref, buf, sem):
+    gain1 = jnp.sum(total * unit, axis=0, keepdims=True)
+    shift1 = jnp.sum(total, axis=0, keepdims=True)
+    sums_ref[...] = jnp.concatenate([gain1, shift1, vec_ref[...][:2], jnp.zeros((4, D), F32)], axis=0)
+
+
+def add_kernel(one_ref, two_ref, ff_ref, out_ref, buf, sem, ff_sem):
+    micro = lax.axis_index(MICRO)
+    copies = []
+    for chip in range(8):
+        for half in range(2):
+            copy = pltpu.make_async_copy(
+                ff_ref.at[half], out_ref.at[2 * chip + micro, pl.ds(48 * (1 + half), 48)], ff_sem.at[chip, half]
+            )
+            copy.start()
+            copies.append(copy)
     buf[...] = (one_ref[...].astype(F32) + two_ref[...].astype(F32)).astype(BF)
-    copy = pltpu.make_async_copy(buf, out_ref, sem)
+    copy = pltpu.make_async_copy(buf, out_ref.at[:, pl.ds(0, 48)], sem)
     copy.start()
-    copy.wait()
+    copies.append(copy)
+    wait_all(copies)
+
+
+def pick_kernel(in_ref, out_ref):
+    micro = lax.axis_index(MICRO)
+    for chip in range(8):
+        out_ref[chip] = in_ref[2 * chip + micro, 48:]
 
 
 def sum_kernel(in_ref, vec_ref, out_ref, buf, sem):
-    total = in_ref[0].astype(F32)
+    total = in_ref[0, :48].astype(F32)
     for index in range(1, 16):
-        total = total + in_ref[index].astype(F32)
+        total = total + in_ref[index, :48].astype(F32)
     vectors = vec_ref[...][:4]
     block = jnp.concatenate([total, vectors[:, :384], vectors[:, 384:]], axis=0).astype(BF)
     for index in range(8):
@@ -483,38 +523,24 @@
     wait_all(copies)
 
 
-def stack_kernel(*refs):
-    y = lax.axis_index("y")
-    for k, ref in enumerate(refs[:4]):
-        refs[4][y ^ k] = ref[...]
-
-
-def spread_ff_kernel(*refs):
-    up_ref, down_ref = refs[4:]
-    xl, core = lax.axis_index("xl"), lax.axis_index(CORE)
-    for index, ref in enumerate(refs[:4]):
-        chip_xl = xl ^ (index % 2)
-        owner = core ^ (index // 2)
-        for y in range(4):
-            chip = y * 2 + chip_xl
-            block = ref[y].astype(F32)
-            up_ref[pl.ds(pl.multiple_of((chip * 2 + owner) * 48, 16), 48)] = block[:, :384]
-            down_ref[
-                pl.ds(pl.multiple_of(chip * 48, 16), 48), pl.ds(pl.multiple_of(owner * 384, 128), 384)
-            ] = block[:, 384:]
+def spread_ff_kernel(same_ref, other_ref, up_ref, down_ref):
+    core = lax.axis_index(CORE)
+    for ref, owner in ((same_ref, core), (other_ref, 1 - core)):
+        for chip in range(8):
+            up_ref[pl.ds(pl.multiple_of((chip * 2 + owner) * 48, 16), 48)] = ref[chip, :48].astype(F32)
+            down_ref[chip * 48:(chip + 1) * 48, pl.ds(pl.multiple_of(owner * 384, 128), 384)] = ref[
+                chip, 48:
+            ].astype(F32)
 
 
 def input_kernel(
-    own_ref, one_ref, two_ref, three_ref, x_ref, gain_ref, grad_ref, result_ref, vec_ref, out_ref, sums_ref
+    own_ref, one_ref, two_ref, three_ref, x_ref, gain_ref, grad_ref, result_ref, out_ref
 ):
     total = own_ref[...]
     for ref in (one_ref, two_ref, three_ref):
         total = total + ref[...].astype(F32)
     unit, inverse = normalized(x_ref[...].astype(F32))
     grad = grad_ref[...] + norm_back(total, unit, inverse, gain_ref[...].reshape(1, D))
-    gain1 = jnp.sum(total * unit, axis=0, keepdims=True)
-    shift1 = jnp.sum(total, axis=0, keepdims=True)
-    sums_ref[...] = jnp.concatenate([gain1, shift1, vec_ref[...][:2], jnp.zeros((4, D), F32)], axis=0)
     out_ref[:BLK] = grad.astype(BF)
     out_ref[BLK:] = result_ref[...]
 
@@ -585,11 +611,14 @@
             ((2 * TOK, FFL), BF, "V"), ((2 * TOK, FFL), BF, "V"),
         ],
         [
-            (mixed, "V"), (tokens, "V"), (out_grad, "V"), (w_out_pad, "V"), (ln2_gain, "L"), (ln2_shift, "L"),
-            (w_up, "V"), (w_down, "V"),
+            (mixed, "V"), (tokens, "H"), (out_grad, "H"), (w_out_pad, "V"), (ln2_gain, "L"), (ln2_shift, "L"),
+            (w_up, "H"), (w_down, "H"),
         ],
         4 * 10**9,
-        [pltpu.VMEM((8, BLK, D), BF), pltpu.VMEM((8, BLK, D), BF), DMA((2,))],
+        [
+            pltpu.VMEM((2, TOK, D), BF), pltpu.VMEM((2, TOK, D), BF), pltpu.VMEM((D, FFL), BF),
+            pltpu.VMEM((FFL, D), BF), pltpu.VMEM((8, BLK, D), BF), pltpu.VMEM((8, BLK, D), BF), DMA((4,)), DMA((2,)),
+        ],
     )
     ff_sums = exchange(ff_send, NARROW)
     keep, send = call(
@@ -613,7 +642,7 @@
     grad_send, low, grad_mid, result_part, vec2, x_part = call(
         middle_kernel,
         [
-            ((32, BLK, 256), BF, "H"), ((BLK, D), BF, "L"), ((BLK, D), F32, "L"), ((BLK, D), BF, "L"),
+            ((8, 4, BLK, 256), BF, "H"), ((BLK, D), BF, "L"), ((BLK, D), F32, "L"), ((BLK, D), BF, "L"),
             ((8, D), F32, "L"), ((BLK, D), BF, "L"),
         ],
         [
@@ -623,58 +652,46 @@
         10**9,
         [
             pltpu.VMEM((4, BLK, 256), BF), pltpu.VMEM((BLK, D), F32), pltpu.VMEM((BLK, D), BF),
-            pltpu.VMEM((4, BLK, 256), BF), DMA, DMA((3,)), DMA((32,)),
+            pltpu.VMEM((4, BLK, 256), BF), DMA, DMA((3,)), DMA((8,)),
         ],
     )
     (ff_part,) = call(
-        pair_kernel, [((48, D), BF, "L")], [(keep, "L"), (flip(send, "xl", 2, 1), "V")], 10**7
-    )
-    ff_parts = [flip(ff_part, "y", 4, k) for k in (1, 2, 3)]
-    grad_same = exchange(grad_send, (*CHIP, *GROUP)).reshape(8, TOK, 256)
+        pair_kernel, [((2, 48, 384), BF, "L")], [(keep, "L"), (flip(send, "xl", 2, 1), "V")], 10**7
+    )
+    grad_same = exchange(grad_send.reshape(32, BLK, 256), (*CHIP, *GROUP)).reshape(8, TOK, 256)
     lows = [flip(low, GROUP, 4, k) for k in (1, 2, 3)]
-    grad_same = after(grad_same, *lows, *ff_parts)
+    grad_same = after(grad_same, *lows, pin(ff_part))
     grad_other = swap(grad_same)
-    own, *sends, keep, send = call(
+    gqkv, keep, send = call(
         attend_back_kernel,
-        [((BLK, D), F32, "L")] + [((BLK, D), BF, "L")] * 3 + [((16, 48, 384), BF, "V")] * 2,
+        [((TOK, 640), BF, "L")] + [((16, 48, 384), BF, "V")] * 2,
         [
             (scene_of_block, "S"), (kv_same, "H"), (kv_other, "H"), (grad_same, "V"), (grad_other, "V"),
-            (normed, "L"), (mixed, "H"), (low, "L"), *[(value, "V") for value in lows], (w_qkv, "H"),
+            (normed, "L"), (mixed, "H"), (low, "L"), *[(value, "V") for value in lows],
         ],
         8 * 10**9,
         [
-            pltpu.VMEM((2, 5, TOK, 640), BF), pltpu.VMEM((TOK, 640), BF), pltpu.VMEM((D, 640), F32),
-            pltpu.VMEM((TOK, D), F32), pltpu.VMEM((TOK, 256), BF), pltpu.VMEM((3, D, 384), BF),
-            DMA((2,)), DMA, DMA((3,)),
+            pltpu.VMEM((2, 5, TOK, 640), BF), pltpu.VMEM((D, 640), F32), pltpu.VMEM((TOK, 256), BF), DMA((2,)), DMA,
         ],
         vmem=24,
     )
     (weight_send,) = call(
         add_kernel,
-        [((16, 48, 384), BF, "H")],
-        [(keep, "V"), (swap(send), "V")],
+        [((16, 144, 384), BF, "H")],
+        [(keep, "V"), (swap(send), "V"), (ff_part, "L")],
         10**8,
-        [pltpu.VMEM((16, 48, 384), BF), DMA],
+        [pltpu.VMEM((16, 48, 384), BF), DMA, DMA((8, 2))],
+    )
+    weight_parts = exchange(weight_send, (*CHIP, MICRO))
+    own, *sends, sums = call(
+        normed_grad_kernel,
+        [((BLK, D), F32, "L")] + [((BLK, D), BF, "L")] * 3 + [((8, D), F32, "L")],
+        [(gqkv, "L"), (tokens, "H"), (w_qkv, "H"), (vec2, "L")],
+        10**9,
+        [pltpu.VMEM((TOK, D), BF), pltpu.VMEM((TOK, D), F32), pltpu.VMEM((3, D, 384), BF), DMA, DMA((3,))],
     )
     parts = [flip(value, GROUP, 4, k + 1) for k, value in enumerate(sends)]
-    weight_parts = exchange(weight_send, (*CHIP, MICRO))
-    (ff_near,) = call(
-        stack_kernel,
-        [((4, 48, D), BF, "L")],
-        [(ff_part, "L"), *[(value, "V") for value in ff_parts]],
-        10**7,
-    )
-    ff_far = flip(ff_near, "xl", 2, 1)
-    packed, sums = call(
-        input_kernel,
-        [((2 * BLK, D), BF, "L"), ((8, D), F32, "L")],
-        [
-            (own, "L"), *[(value, "V") for value in parts], (x_part, "L"), (ln1_gain, "L"), (grad_mid, "L"),
-            (result_part, "L"), (vec2, "L"),
-        ],
-        10**8,
-    )
-    weight_parts = after(weight_parts, ff_far, pin(sums))
+    weight_parts = after(weight_parts, pin(sums), *parts)
     (weight_total,) = call(
         sum_kernel,
         [((8, 8, 56, 384), BF, "H")],
@@ -682,17 +699,27 @@
         10**8,
         [pltpu.VMEM((8, 56, 384), BF), DMA((8,))],
     )
-    everyone = [packed] + [flip(packed, NARROW, 8, k) for k in range(1, 8)]
+    (packed,) = call(
+        input_kernel,
+        [((2 * BLK, D), BF, "L")],
+        [
+            (own, "L"), *[(value, "V") for value in parts], (x_part, "L"), (ln1_gain, "L"), (grad_mid, "L"),
+            (result_part, "L"),
+        ],
+        10**8,
+    )
+    others = {k: flip(packed, NARROW, 8, k) for k in (7, 5, 6, 3, 1, 4, 2)}
     input_grad, result = call(
         unpack_kernel,
         [((2, TOK, D), F32, "L"), ((2, TOK, D), BF, "L")],
-        [(packed, "L"), *[(value, "V") for value in everyone[1:]]],
+        [(packed, "L"), *[(others[k], "V") for k in range(1, 8)]],
         10**8,
     )
+    (ff_same,) = call(pick_kernel, [((8, 96, 384), BF, "V")], [(weight_parts, "V")], 10**7)
     up_grad, down_grad = call(
         spread_ff_kernel,
         [((D, FFL), F32, "L"), ((FFL, D), F32, "L")],
-        [(ff_near, "L"), (ff_far, "V"), (swap(ff_near), "V"), (swap(ff_far), "V")],
+        [(ff_same, "V"), (swap(ff_same), "V")],
         10**7,
     )
     weight_same = exchange(weight_total.reshape(64, 56, 384), (*CHIP, *NARROW)).reshape(8, 8, 56, 384)

time: 229 us -> 227 us (level)
  waiting for transfers between devices: 70.5 us -> 85.2 us
  starting transfers between devices: 78.6 us -> 64.8 us
  local copies, waits for them, and re-layouts: 5.65 us -> 1.18 us
    ppermute x21 -> x17, waiting for transfers between devices: 53.1 us -> 66.1 us  [flip(): lax.ppermute(value, axes, [(index, index ^ bits) for index in range(count)])]
    ppermute x21 -> x17, starting transfers between devices: 33.9 us -> 23.6 us  [flip(): lax.ppermute(value, axes, [(index, index ^ bits) for index in range(count)])]
    all_to_all x5, waiting for transfers between devices: 9.38 us -> 12.6 us  [exchange(): return lax.all_to_all(value, axes, 0, 0, tiled=True)]
    unnamed x28 -> x12, local copies, waits for them, and re-layouts: 4.28 us -> 1.07 us
    ppermute x7 -> x6, starting transfers between devices: 13.5 us -> 10.3 us  [swap(): return lax.ppermute(value, CORE, [(0, 1), (1, 0)])]
    ppermute x7 -> x6, waiting for transfers between devices: 8.11 us -> 6.52 us  [swap(): return lax.ppermute(value, CORE, [(0, 1), (1, 0)])]
    pallas_call x17 -> x18, Pallas kernels: 47.8 us -> 49.3 us  [call(): pl.pallas_call(kernel, out_shape=[(pltpu.HBM if place in 'HL' else jax.Sh...]
  transfers between devices with their start and end apart: 33 -> 28, of which waited for: 15 -> 18; matrix products, arithmetic and copies ran while one was open for 1% -> 0% of each run, Pallas kernels for 6% -> 8%
where the time goes in v7:
time: 227 us; the launch traced here: 225 us
  waiting for transfers between devices  85.2 us (38%)
  starting transfers between devices  64.8 us (29%)
  Pallas kernels  49.3 us (22%)
  blocking collectives  23.7 us (10%)
    ppermute x17, waiting for transfers between devices, flip(): lax.ppermute(value, axes, [(index, index ^ bits) for index in range(count)])  66.1 us
    pallas_call x18, Pallas kernels, call(): pl.pallas_call(kernel, out_shape=[(pltpu.HBM if place in 'HL' else jax.Sh...  49.3 us
    all_to_all x5, starting transfers between devices, exchange(): return lax.all_to_all(value, axes, 0, 0, tiled=True)  30.9 us
    all_to_all x1, blocking collectives, exchange(): return lax.all_to_all(value, axes, 0, 0, tiled=True)  23.7 us
    ppermute x17, starting transfers between devices, flip(): lax.ppermute(value, axes, [(index, index ^ bits) for index in range(count)])  23.6 us
    all_to_all x5, waiting for transfers between devices, exchange(): return lax.all_to_all(value, axes, 0, 0, tiled=True)  12.6 us
    ppermute x6, starting transfers between devices, swap(): return lax.ppermute(value, CORE, [(0, 1), (1, 0)])  10.3 us
    ppermute x6, waiting for transfers between devices, swap(): return lax.ppermute(value, CORE, [(0, 1), (1, 0)])  6.52 us
  transfers between devices with their start and end apart: 28, of which 18 were waited for; matrix products, arithmetic and copies ran while one was open for 0% of the time, Pallas kernels for 8%

profile of v7, /device:TPU:1, one launch (start us, length us, event | category | flops | bytes accessed | tf_op | source)
XLA Modules:
  0.0 225.2 jit_solution(2792976990145580882)
XLA Ops:
  0.6 4.3 %shard_map.186 = (bf16[8,128,640]{2,1,0:T(8,128)(2,1)}, bf16[128,768]{1,0:T(8,128)(2,1)}) custom-call(bf16[2,128,768]{2,1,0:T(8,128)(2,1)} %tok_ref.7, f32[768]{0:T(1024)} %gain_ref.7, f32[768]{0:T(1024)} %shift_ref.2, bf16[768,2304]{1,0:T(8,128)(2,1)} %w_ref.3), custom_call_target="tpu_custom_call" | custom-call | flops 1000 | bytes 1000 | tf_op jit(solution)/shard_map/pallas_call | solution.py:106
  5.0 23.7 %all_to_all.30.same_ref.kvs_ref = bf16[8,128,640]{2,1,0:T(8,128)(2,1)S(1)} all-to-all(bf16[8,128,640]{2,1,0:T(8,128)(2,1)} %get-tuple-element.52), channel_id=1, replica_groups=mesh['y'=4,'xl'=2,'c'=2,'zh'=2,'zl'=2,'xh'=2] {'y','xl'}, dimensions={0} | all-to-all | bytes 2621440 | tf_op jit(solution)/shard_map/all_to_all | solution.py:560
  30.6 2.7 %collective-permute-done.other_ref.kvo_ref = bf16[8,128,640]{2,1,0:T(8,128)(2,1)S(1)} collective-permute-done((bf16[8,128,640]{2,1,0:T(8,128)(2,1)S(1)}, bf16[8,128,640]{2,1,0:T(8,128)(2,1)S(1)}, u32[]{:S(2)}, u32[]{:S(2)}) %collective-permute-start) | collective-permute-done | bytes 1310752 | tf_op jit(solution)/shard_map/ppermute | solution.py:564
  33.3 2.3 %shard_map.187 = bf16[8,128,256]{2,1,0:T(8,128)(2,1)} custom-call(s32[2,32]{1,0:T(2,128)S(1)} %copy-done.3, bf16[8,128,640]{2,1,0:T(8,128)(2,1)S(1)} %all_to_all.30.same_ref.kvs_ref, bf16[8,128,640]{2,1,0:T(8,128)(2,1)S(1)} %collective-permute-done.other_ref.kvo_ref), custom_call_target="tpu_custom_call" | custom-call | flops 1000 | bytes 1000 | tf_op jit(solution)/shard_map/pallas_call | solution.py:106
  36.6 7.3 %all-to-all-start.1 = ((bf16[8,128,256]{2,1,0:T(8,128)(2,1)}), bf16[8,128,256]{2,1,0:T(8,128)(2,1)S(1)}, u32[]{:S(2)}, u32[]{:S(2)}) async-start(bf16[8,128,256]{2,1,0:T(8,128)(2,1)} %shard_map.187), calls=%async_computation.1 | async-start | bytes 1048576 | tf_op jit(solution)/shard_map/all_to_all | solution.py:560
  44.0 10.6 %all-to-all-done.1.mixed_ref = bf16[8,128,256]{2,1,0:T(8,128)(2,1)S(1)} async-done(((bf16[8,128,256]{2,1,0:T(8,128)(2,1)}), bf16[8,128,256]{2,1,0:T(8,128)(2,1)S(1)}, u32[]{:S(2)}, u32[]{:S(2)}) %all-to-all-start.1) | async-done | bytes 524320 | tf_op jit(solution)/shard_map/all_to_all | solution.py:560
  54.7 5.6 %shard_map.188 = (bf16[8,64,768]{2,1,0:T(8,128)(2,1)}, f32[8,32,768]{2,1,0:T(8,128)}, bf16[256,768]{1,0:T(8,128)(2,1)S(1)}, bf16[256,384]{1,0:T(8,128)(2,1)S(1)}, bf16[256,384]{1,0:T(8,128)(2,1)S(1)}) custom-call(bf16[8,128,256]{2,1,0:T(8,128)(2,1)S(1)} %all-to-all-done.1.mixed_ref, bf16[2,128,768]{2,1,0:T(8,128)(2,1)} %tok_ref.7, ...), custom_call_target="tpu_custom_call" | custom-call | flops 1000 | bytes 1000 | tf_op jit(solution)/shard_map/pallas_call | solution.py:106
  60.3 2.8 %shard_map.189 = (bf16[8,48,768]{2,1,0:T(8,128)(2,1)S(1)}, bf16[8,48,768]{2,1,0:T(8,128)(2,1)}) custom-call(bf16[256,768]{1,0:T(8,128)(2,1)S(1)} %get-tuple-element.54.normed_ref, bf16[256,384]{1,0:T(8,128)(2,1)S(1)} %get-tuple-element.55.act_ref, bf16[256,384]{1,0:T(8,128)(2,1)S(1)} %get-tuple-element.56.gpre_ref, bf16[2,128,768]{2,1,0:T(8,128)(2,1)} %og_ref.5), custom_call_target="tpu_custom_call" | custom-call | flops 1000 | bytes 1000 | tf_op jit(solution)/shard_map/pallas_call | solution.py:106
  64.8 3.5 %all-to-all-start.2 = ((bf16[8,64,768]{2,1,0:T(8,128)(2,1)}), bf16[8,64,768]{2,1,0:T(8,128)(2,1)S(1)}, u32[]{:S(2)}, u32[]{:S(2)}) async-start(bf16[8,64,768]{2,1,0:T(8,128)(2,1)} %get-tuple-element.53), calls=%async_computation.2 | async-start | bytes 1572864 | tf_op jit(solution)/shard_map/all_to_all | solution.py:560
  69.2 2.6 %collective-permute-start.3 = (bf16[2,48,768]{2,1,0:T(8,128)(2,1)}, bf16[2,48,768]{2,1,0:T(8,128)(2,1)S(1)}, u32[]{:S(2)}, u32[]{:S(2)}) collective-permute-start(bf16[2,48,768]{2,1,0:T(8,128)(2,1)} %get-tuple-element.61), channel_id=1, source_target_pairs={{0,64},{32,96},{64,0},{96,32},{1,65},{33,97},{65,1},{97,33},{2,66}... | collective-permute-start | bytes 442376 | tf_op jit(solution)/shard_map/ppermute | solution.py:580
  74.9 4.3 %collective-permute-done.3.refs_2_ = bf16[2,48,768]{2,1,0:T(8,128)(2,1)S(1)} collective-permute-done((bf16[2,48,768]{2,1,0:T(8,128)(2,1)}, bf16[2,48,768]{2,1,0:T(8,128)(2,1)S(1)}, u32[]{:S(2)}, u32[]{:S(2)}) %collective-permute-start.3) | collective-permute-done | bytes 147488 | tf_op jit(solution)/shard_map/ppermute | solution.py:580
  79.2 2.4 %collective-permute-done.4.refs_3_ = bf16[2,48,768]{2,1,0:T(8,128)(2,1)S(1)} collective-permute-done((bf16[2,48,768]{2,1,0:T(8,128)(2,1)}, bf16[2,48,768]{2,1,0:T(8,128)(2,1)S(1)}, u32[]{:S(2)}, u32[]{:S(2)}) %collective-permute-start.4) | collective-permute-done | bytes 147488 | tf_op jit(solution)/shard_map/ppermute | solution.py:580
  83.3 4.1 %shard_map.193 = (bf16[8,4,32,256]{3,2,1,0:T(8,128)(2,1)}, bf16[32,768]{1,0:T(8,128)(2,1)}, f32[32,768]{1,0:T(8,128)}, bf16[32,768]{1,0:T(8,128)(2,1)}, f32[8,768]{1,0:T(8,128)}, /*index=5*/bf16[32,768]{1,0:T(8,128)(2,1)}) custom-call(bf16[8,64,768]{2,1,0:T(8,128)(2,1)S(1)} %shard_map.192.sums_ref, f32[8,32,768]{2,1,0:T(8,128)} %get-tuple-element.64.middle_ref, ...), custom_call_target="tpu_custom_call" | custom-call | flops 1000 | bytes 1000 | tf_op jit(solution)/shard_map/pallas_call | solution.py:106
  87.4 6.2 %all-to-all-start.3 = ((bf16[32,32,256]{2,1,0:T(8,128)(2,1)}), bf16[32,32,256]{2,1,0:T(8,128)(2,1)S(1)}, u32[]{:S(2)}, u32[]{:S(2)}) async-start(bf16[32,32,256]{2,1,0:T(8,128)(2,1)} %bitcast.8), calls=%async_computation.3 | async-start | bytes 1048576 | tf_op jit(solution)/shard_map/all_to_all | solution.py:560
  95.0 3.3 %collective-permute-start.7 = (bf16[32,768]{1,0:T(8,128)(2,1)}, bf16[32,768]{1,0:T(8,128)(2,1)S(1)}, u32[]{:S(2)}, u32[]{:S(2)}) collective-permute-start(bf16[32,768]{1,0:T(8,128)(2,1)} %get-tuple-element.66.low0_ref), channel_id=1, source_target_pairs={{0,3},{1,2},{2,1},{3,0},{4,7},{5,6},{6,5},{7,4},{8,11},{9,10},{10,... | collective-permute-start | bytes 147464 | tf_op jit(solution)/shard_map/ppermute | solution.py:580
  99.1 2.4 %collective-permute-done.8.two_ref = bf16[48,768]{1,0:T(8,128)(2,1)S(1)} collective-permute-done((bf16[48,768]{1,0:T(8,128)(2,1)S(1)}, bf16[48,768]{1,0:T(8,128)(2,1)S(1)}, u32[]{:S(2)}, u32[]{:S(2)}) %collective-permute-start.8) | collective-permute-done | bytes 73760 | tf_op jit(solution)/shard_map/ppermute | solution.py:580
  105.1 3.2 %collective-permute-start.9 = (bf16[8,128,256]{2,1,0:T(8,128)(2,1)S(1)}, bf16[8,128,256]{2,1,0:T(8,128)(2,1)S(1)}, u32[]{:S(2)}, u32[]{:S(2)}) collective-permute-start(bf16[8,128,256]{2,1,0:T(8,128)(2,1)S(1)} %shard_map.195.gs_ref), channel_id=1, source_target_pairs={{0,8},{8,0},{1,9},{9,1},{2,10},{10,2},{3,11},{11,3},{4,12},{12,4},... | collective-permute-start | bytes 1572872 | tf_op jit(solution)/shard_map/ppermute | solution.py:564
  109.8 4.8 %shard_map.196 = (bf16[128,640]{1,0:T(8,128)(2,1)}, bf16[16,48,384]{2,1,0:T(8,128)(2,1)S(1)}, bf16[16,48,384]{2,1,0:T(8,128)(2,1)S(1)}) custom-call(s32[2,32]{1,0:T(2,128)S(1)} %copy-done.3, bf16[8,128,640]{2,1,0:T(8,128)(2,1)} %copy-done, bf16[8,128,640]{2,1,0:T(8,128)(2,1)} %copy-done.2, bf16[8,128,256]{2,1,0:T(8,128)(2,1)S(1)} %shard_map.195.gs_ref, ...), custom_call_target="tpu_custom_call" | custom-call | flops 1000 | bytes 1000 | tf_op jit(solution)/shard_map/pallas_call | solution.py:106
  116.7 2.1 shard_map.200
  118.8 7.3 %all-to-all-start.4 = ((bf16[16,144,384]{2,1,0:T(8,128)(2,1)}), bf16[16,144,384]{2,1,0:T(8,128)(2,1)S(1)}, u32[]{:S(2)}, u32[]{:S(2)}) async-start(bf16[16,144,384]{2,1,0:T(8,128)(2,1)} %shard_map.200), calls=%async_computation.4 | async-start | bytes 3538944 | tf_op jit(solution)/shard_map/all_to_all | solution.py:560
  126.1 4.1 %shard_map.197 = (f32[32,768]{1,0:T(8,128)}, bf16[32,768]{1,0:T(8,128)(2,1)}, bf16[32,768]{1,0:T(8,128)(2,1)}, bf16[32,768]{1,0:T(8,128)(2,1)}, f32[8,768]{1,0:T(8,128)}) custom-call(bf16[128,640]{1,0:T(8,128)(2,1)} %get-tuple-element.69.gqkv_ref, bf16[2,128,768]{2,1,0:T(8,128)(2,1)} %tok_ref.7, bf16[768,2304]{1,0:T(8,128)(2,1)} %w_ref.3, ...), custom_call_target="tpu_custom_call" | custom-call | flops 1000 | bytes 1000 | tf_op jit(solution)/shard_map/pallas_call | solution.py:106
  132.1 2.3 %collective-permute-start.12 = (bf16[32,768]{1,0:T(8,128)(2,1)}, bf16[32,768]{1,0:T(8,128)(2,1)S(1)}, u32[]{:S(2)}, u32[]{:S(2)}) collective-permute-start(bf16[32,768]{1,0:T(8,128)(2,1)} %get-tuple-element.74), channel_id=1, source_target_pairs={{0,3},{1,2},{2,1},{3,0},{4,7},{5,6},{6,5},{7,4},{8,11},{9,10},{10,... | collective-permute-start | bytes 147464 | tf_op jit(solution)/shard_map/ppermute | solution.py:580
  134.4 16.9 %collective-permute-done.10.one_ref.refs_2_ = bf16[32,768]{1,0:T(8,128)(2,1)S(1)} collective-permute-done((bf16[32,768]{1,0:T(8,128)(2,1)}, bf16[32,768]{1,0:T(8,128)(2,1)S(1)}, u32[]{:S(2)}, u32[]{:S(2)}) %collective-permute-start.10) | collective-permute-done | bytes 49184 | tf_op jit(solution)/shard_map/ppermute | solution.py:580
  151.3 2.0 collective-permute-done.12.three_ref.refs_4_
  155.3 2.4 %shard_map.202 = bf16[8,8,56,384]{3,2,1,0:T(8,128)(2,1)} custom-call(bf16[16,144,384]{2,1,0:T(8,128)(2,1)S(1)} %shard_map.201.in_ref, f32[8,768]{1,0:T(8,128)} %get-tuple-element.82.refs_1_.vec_ref), custom_call_target="tpu_custom_call" | custom-call | flops 1000 | bytes 1000 | tf_op jit(solution)/shard_map/pallas_call | solution.py:106
  157.7 6.6 %all-to-all-start.5 = ((bf16[64,56,384]{2,1,0:T(8,128)(2,1)}), bf16[64,56,384]{2,1,0:T(8,128)(2,1)}, u32[]{:S(2)}, u32[]{:S(2)}) async-start(bf16[64,56,384]{2,1,0:T(8,128)(2,1)} %bitcast.6), calls=%async_computation.5 | async-start | bytes 5505024 | tf_op jit(solution)/shard_map/all_to_all | solution.py:560
  168.0 4.8 %collective-permute-start.19 = (bf16[64,768]{1,0:T(8,128)(2,1)}, bf16[64,768]{1,0:T(8,128)(2,1)S(1)}, u32[]{:S(2)}, u32[]{:S(2)}) collective-permute-start(bf16[64,768]{1,0:T(8,128)(2,1)} %shard_map.198.refs_0_), channel_id=1, source_target_pairs={{0,7},{1,6},{2,5},{3,4},{4,3},{5,2},{6,1},{7,0},{8,15},{9,14},{10,... | collective-permute-start | bytes 294920 | tf_op jit(solution)/shard_map/ppermute | solution.py:580
  176.1 23.8 %collective-permute-done.19.refs_7_ = bf16[64,768]{1,0:T(8,128)(2,1)S(1)} collective-permute-done((bf16[64,768]{1,0:T(8,128)(2,1)}, bf16[64,768]{1,0:T(8,128)(2,1)S(1)}, u32[]{:S(2)}, u32[]{:S(2)}) %collective-permute-start.19) | collective-permute-done | bytes 98336 | tf_op jit(solution)/shard_map/ppermute | solution.py:580
  199.9 6.7 %collective-permute-done.18.refs_6_ = bf16[64,768]{1,0:T(8,128)(2,1)S(1)} collective-permute-done((bf16[64,768]{1,0:T(8,128)(2,1)}, bf16[64,768]{1,0:T(8,128)(2,1)S(1)}, u32[]{:S(2)}, u32[]{:S(2)}) %collective-permute-start.18) | collective-permute-done | bytes 98336 | tf_op jit(solution)/shard_map/ppermute | solution.py:580
  208.5 3.3 %collective-permute-done.14.refs_2_ = bf16[64,768]{1,0:T(8,128)(2,1)S(1)} collective-permute-done((bf16[64,768]{1,0:T(8,128)(2,1)}, bf16[64,768]{1,0:T(8,128)(2,1)S(1)}, u32[]{:S(2)}, u32[]{:S(2)}) %collective-permute-start.14) | collective-permute-done | bytes 98336 | tf_op jit(solution)/shard_map/ppermute | solution.py:580
  217.1 4.2 %shard_map.206 = (f32[768,2304]{1,0:T(8,128)}, f32[768,768]{1,0:T(8,128)}, f32[8,384]{1,0:T(8,128)S(1)}) custom-call(bf16[8,8,56,384]{3,2,1,0:T(8,128)(2,1)} %shard_map.205.in_ref), custom_call_target="tpu_custom_call" | custom-call | flops 1000 | bytes 1000 | tf_op jit(solution)/shard_map/pallas_call | solution.py:106
  222.0 3.0 %shard_map.207 = (f32[768,2304]{1,0:T(8,128)}, f32[768,768]{1,0:T(8,128)}, f32[768]{0:T(1024)}, f32[768]{0:T(1024)}, f32[768]{0:T(1024)}, /*index=5*/f32[768]{0:T(1024)}) custom-call(bf16[8,8,56,384]{3,2,1,0:T(8,128)(2,1)S(1)} %collective-permute-done.22.in_ref, ...), custom_call_target="tpu_custom_call", output_to_operand_aliasing={{0}: (2, {}), {1}: (3, {})} | custom-call | flops 1000 | bytes 1000 | tf_op jit(solution)/shard_map/pallas_call | solution.py:106
  (60 shorter events, 38.6 us)
Async XLA Ops:
  5.0 28.3 %copy-start.3 = (s32[2,32]{1,0:T(2,128)S(1)}, s32[2,32]{1,0:T(2,128)}, u32[]{:S(2)}) copy-start(s32[2,32]{1,0:T(2,128)} %scene_ref.3) | copy-start | bytes 772
  28.7 7.9 %copy-start = (bf16[8,128,640]{2,1,0:T(8,128)(2,1)}, bf16[8,128,640]{2,1,0:T(8,128)(2,1)S(1)}, u32[]{:S(2)}) copy-start(bf16[8,128,640]{2,1,0:T(8,128)(2,1)S(1)} %all_to_all.30.same_ref.kvs_ref) | copy-start | bytes 3932164
  28.7 15.2 %copy-start.4 = (bf16[768,768]{1,0:T(8,128)(2,1)S(1)}, bf16[768,768]{1,0:T(8,128)(2,1)}, u32[]{:S(2)}) copy-start(bf16[768,768]{1,0:T(8,128)(2,1)} %param.16) | copy-start | bytes 3538948
  28.7 4.5 %collective-permute-start = (bf16[8,128,640]{2,1,0:T(8,128)(2,1)S(1)}, bf16[8,128,640]{2,1,0:T(8,128)(2,1)S(1)}, u32[]{:S(2)}, u32[]{:S(2)}) collective-permute-start(bf16[8,128,640]{2,1,0:T(8,128)(2,1)S(1)} %all_to_all.30.same_ref.kvs_ref), channel_id=1, source_target_pairs={{0,8},{8,0},{1,9},{9,1},{2,10},{10,2},{3,11},{11,3},{4,12},{12,4},... | collective-permute-start | bytes 3932168 | tf_op jit(solution)/shard_map/ppermute | solution.py:564
  36.6 18.0 %all-to-all-start.1 = ((bf16[8,128,256]{2,1,0:T(8,128)(2,1)}), bf16[8,128,256]{2,1,0:T(8,128)(2,1)S(1)}, u32[]{:S(2)}, u32[]{:S(2)}) async-start(bf16[8,128,256]{2,1,0:T(8,128)(2,1)} %shard_map.187), calls=%async_computation.1 | async-start | bytes 1048576 | tf_op jit(solution)/shard_map/all_to_all | solution.py:560
  63.1 5.3 %collective-permute-start.1 = (bf16[8,48,768]{2,1,0:T(8,128)(2,1)}, bf16[8,48,768]{2,1,0:T(8,128)(2,1)S(1)}, u32[]{:S(2)}, u32[]{:S(2)}) collective-permute-start(bf16[8,48,768]{2,1,0:T(8,128)(2,1)} %get-tuple-element.58), channel_id=1, source_target_pairs={{0,8},{8,0},{1,9},{9,1},{2,10},{10,2},{3,11},{11,3},{4,12},{12,4},... | collective-permute-start | bytes 1769480 | tf_op jit(solution)/shard_map/ppermute | solution.py:564
  64.8 18.5 %all-to-all-start.2 = ((bf16[8,64,768]{2,1,0:T(8,128)(2,1)}), bf16[8,64,768]{2,1,0:T(8,128)(2,1)S(1)}, u32[]{:S(2)}, u32[]{:S(2)}) async-start(bf16[8,64,768]{2,1,0:T(8,128)(2,1)} %get-tuple-element.53), calls=%async_computation.2 | async-start | bytes 1572864 | tf_op jit(solution)/shard_map/all_to_all | solution.py:560
  69.2 5.7 %collective-permute-start.2 = (bf16[2,48,768]{2,1,0:T(8,128)(2,1)}, bf16[2,48,768]{2,1,0:T(8,128)(2,1)S(1)}, u32[]{:S(2)}, u32[]{:S(2)}) collective-permute-start(bf16[2,48,768]{2,1,0:T(8,128)(2,1)} %get-tuple-element.60), channel_id=1, source_target_pairs={{0,32},{32,0},{64,96},{96,64},{1,33},{33,1},{65,97},{97,65},{2,34}... | collective-permute-start | bytes 442376 | tf_op jit(solution)/shard_map/ppermute | solution.py:580
  69.2 10.0 %collective-permute-start.3 = (bf16[2,48,768]{2,1,0:T(8,128)(2,1)}, bf16[2,48,768]{2,1,0:T(8,128)(2,1)S(1)}, u32[]{:S(2)}, u32[]{:S(2)}) collective-permute-start(bf16[2,48,768]{2,1,0:T(8,128)(2,1)} %get-tuple-element.61), channel_id=1, source_target_pairs={{0,64},{32,96},{64,0},{96,32},{1,65},{33,97},{65,1},{97,33},{2,66}... | collective-permute-start | bytes 442376 | tf_op jit(solution)/shard_map/ppermute | solution.py:580
  71.8 9.9 %collective-permute-start.4 = (bf16[2,48,768]{2,1,0:T(8,128)(2,1)}, bf16[2,48,768]{2,1,0:T(8,128)(2,1)S(1)}, u32[]{:S(2)}, u32[]{:S(2)}) collective-permute-start(bf16[2,48,768]{2,1,0:T(8,128)(2,1)} %get-tuple-element.62), channel_id=1, source_target_pairs={{0,96},{32,64},{64,32},{96,0},{1,97},{33,65},{65,33},{97,1},{2,98}... | collective-permute-start | bytes 442376 | tf_op jit(solution)/shard_map/ppermute | solution.py:580
  83.3 10.3 %copy-start.5 = (bf16[48,768]{1,0:T(8,128)(2,1)S(1)}, bf16[48,768]{1,0:T(8,128)(2,1)}, u32[]{:S(2)}) copy-start(bf16[48,768]{1,0:T(8,128)(2,1)} %get-tuple-element.67) | copy-start | bytes 221188
  87.4 17.7 %all-to-all-start.3 = ((bf16[32,32,256]{2,1,0:T(8,128)(2,1)}), bf16[32,32,256]{2,1,0:T(8,128)(2,1)S(1)}, u32[]{:S(2)}, u32[]{:S(2)}) async-start(bf16[32,32,256]{2,1,0:T(8,128)(2,1)} %bitcast.8), calls=%async_computation.3 | async-start | bytes 1048576 | tf_op jit(solution)/shard_map/all_to_all | solution.py:560
  93.6 7.8 %collective-permute-start.8 = (bf16[48,768]{1,0:T(8,128)(2,1)S(1)}, bf16[48,768]{1,0:T(8,128)(2,1)S(1)}, u32[]{:S(2)}, u32[]{:S(2)}) collective-permute-start(bf16[48,768]{1,0:T(8,128)(2,1)S(1)} %copy-done.5), channel_id=1, source_target_pairs={{0,16},{16,0},{1,17},{17,1},{2,18},{18,2},{3,19},{19,3},{4,20},{20... | collective-permute-start | bytes 221192 | tf_op jit(solution)/shard_map/ppermute | solution.py:580
  95.0 10.0 %collective-permute-start.7 = (bf16[32,768]{1,0:T(8,128)(2,1)}, bf16[32,768]{1,0:T(8,128)(2,1)S(1)}, u32[]{:S(2)}, u32[]{:S(2)}) collective-permute-start(bf16[32,768]{1,0:T(8,128)(2,1)} %get-tuple-element.66.low0_ref), channel_id=1, source_target_pairs={{0,3},{1,2},{2,1},{3,0},{4,7},{5,6},{6,5},{7,4},{8,11},{9,10},{10,... | collective-permute-start | bytes 147464 | tf_op jit(solution)/shard_map/ppermute | solution.py:580
  98.2 6.7 %collective-permute-start.6 = (bf16[32,768]{1,0:T(8,128)(2,1)}, bf16[32,768]{1,0:T(8,128)(2,1)S(1)}, u32[]{:S(2)}, u32[]{:S(2)}) collective-permute-start(bf16[32,768]{1,0:T(8,128)(2,1)} %get-tuple-element.66.low0_ref), channel_id=1, source_target_pairs={{0,2},{1,3},{2,0},{3,1},{4,6},{5,7},{6,4},{7,5},{8,10},{9,11},{10,... | collective-permute-start | bytes 147464 | tf_op jit(solution)/shard_map/ppermute | solution.py:580
  98.5 6.5 %collective-permute-start.5 = (bf16[32,768]{1,0:T(8,128)(2,1)}, bf16[32,768]{1,0:T(8,128)(2,1)S(1)}, u32[]{:S(2)}, u32[]{:S(2)}) collective-permute-start(bf16[32,768]{1,0:T(8,128)(2,1)} %get-tuple-element.66.low0_ref), channel_id=1, source_target_pairs={{0,1},{1,0},{2,3},{3,2},{4,5},{5,4},{6,7},{7,6},{8,9},{9,8},{10,11... | collective-permute-start | bytes 147464 | tf_op jit(solution)/shard_map/ppermute | solution.py:580
  105.1 4.7 %collective-permute-start.9 = (bf16[8,128,256]{2,1,0:T(8,128)(2,1)S(1)}, bf16[8,128,256]{2,1,0:T(8,128)(2,1)S(1)}, u32[]{:S(2)}, u32[]{:S(2)}) collective-permute-start(bf16[8,128,256]{2,1,0:T(8,128)(2,1)S(1)} %shard_map.195.gs_ref), channel_id=1, source_target_pairs={{0,8},{8,0},{1,9},{9,1},{2,10},{10,2},{3,11},{11,3},{4,12},{12,4},... | collective-permute-start | bytes 1572872 | tf_op jit(solution)/shard_map/ppermute | solution.py:564
  114.6 2.1 collective-permute-start.20
  118.8 36.5 %all-to-all-start.4 = ((bf16[16,144,384]{2,1,0:T(8,128)(2,1)}), bf16[16,144,384]{2,1,0:T(8,128)(2,1)S(1)}, u32[]{:S(2)}, u32[]{:S(2)}) async-start(bf16[16,144,384]{2,1,0:T(8,128)(2,1)} %shard_map.200), calls=%async_computation.4 | async-start | bytes 3538944 | tf_op jit(solution)/shard_map/all_to_all | solution.py:560
  130.2 21.1 %collective-permute-start.10 = (bf16[32,768]{1,0:T(8,128)(2,1)}, bf16[32,768]{1,0:T(8,128)(2,1)S(1)}, u32[]{:S(2)}, u32[]{:S(2)}) collective-permute-start(bf16[32,768]{1,0:T(8,128)(2,1)} %get-tuple-element.72), channel_id=1, source_target_pairs={{0,1},{1,0},{2,3},{3,2},{4,5},{5,4},{6,7},{7,6},{8,9},{9,8},{10,11... | collective-permute-start | bytes 147464 | tf_op jit(solution)/shard_map/ppermute | solution.py:580
  132.0 19.2 %collective-permute-start.11 = (bf16[32,768]{1,0:T(8,128)(2,1)}, bf16[32,768]{1,0:T(8,128)(2,1)S(1)}, u32[]{:S(2)}, u32[]{:S(2)}) collective-permute-start(bf16[32,768]{1,0:T(8,128)(2,1)} %get-tuple-element.73), channel_id=1, source_target_pairs={{0,2},{1,3},{2,0},{3,1},{4,6},{5,7},{6,4},{7,5},{8,10},{9,11},{10,... | collective-permute-start | bytes 147464 | tf_op jit(solution)/shard_map/ppermute | solution.py:580
  132.1 21.1 %collective-permute-start.12 = (bf16[32,768]{1,0:T(8,128)(2,1)}, bf16[32,768]{1,0:T(8,128)(2,1)S(1)}, u32[]{:S(2)}, u32[]{:S(2)}) collective-permute-start(bf16[32,768]{1,0:T(8,128)(2,1)} %get-tuple-element.74), channel_id=1, source_target_pairs={{0,3},{1,2},{2,1},{3,0},{4,7},{5,6},{6,5},{7,4},{8,11},{9,10},{10,... | collective-permute-start | bytes 147464 | tf_op jit(solution)/shard_map/ppermute | solution.py:580
  157.7 58.1 %all-to-all-start.5 = ((bf16[64,56,384]{2,1,0:T(8,128)(2,1)}), bf16[64,56,384]{2,1,0:T(8,128)(2,1)}, u32[]{:S(2)}, u32[]{:S(2)}) async-start(bf16[64,56,384]{2,1,0:T(8,128)(2,1)} %bitcast.6), calls=%async_computation.5 | async-start | bytes 5505024 | tf_op jit(solution)/shard_map/all_to_all | solution.py:560
  164.3 49.9 %collective-permute-start.21 = (bf16[8,96,384]{2,1,0:T(8,128)(2,1)S(1)}, bf16[8,96,384]{2,1,0:T(8,128)(2,1)S(1)}, u32[]{:S(2)}, u32[]{:S(2)}) collective-permute-start(bf16[8,96,384]{2,1,0:T(8,128)(2,1)S(1)} %shard_map.203.same_ref), channel_id=1, source_target_pairs={{0,8},{8,0},{1,9},{9,1},{2,10},{10,2},{3,11},{11,3},{4,12},{12,4},... | collective-permute-start | bytes 1769480 | tf_op jit(solution)/shard_map/ppermute | solution.py:564
  168.0 31.8 %collective-permute-start.19 = (bf16[64,768]{1,0:T(8,128)(2,1)}, bf16[64,768]{1,0:T(8,128)(2,1)S(1)}, u32[]{:S(2)}, u32[]{:S(2)}) collective-permute-start(bf16[64,768]{1,0:T(8,128)(2,1)} %shard_map.198.refs_0_), channel_id=1, source_target_pairs={{0,7},{1,6},{2,5},{3,4},{4,3},{5,2},{6,1},{7,0},{8,15},{9,14},{10,... | collective-permute-start | bytes 294920 | tf_op jit(solution)/shard_map/ppermute | solution.py:580
  172.9 33.7 %collective-permute-start.18 = (bf16[64,768]{1,0:T(8,128)(2,1)}, bf16[64,768]{1,0:T(8,128)(2,1)S(1)}, u32[]{:S(2)}, u32[]{:S(2)}) collective-permute-start(bf16[64,768]{1,0:T(8,128)(2,1)} %shard_map.198.refs_0_), channel_id=1, source_target_pairs={{0,6},{1,7},{2,4},{3,5},{4,2},{5,3},{6,0},{7,1},{8,14},{9,15},{10,... | collective-permute-start | bytes 294920 | tf_op jit(solution)/shard_map/ppermute | solution.py:580
  173.2 33.4 %collective-permute-start.17 = (bf16[64,768]{1,0:T(8,128)(2,1)}, bf16[64,768]{1,0:T(8,128)(2,1)S(1)}, u32[]{:S(2)}, u32[]{:S(2)}) collective-permute-start(bf16[64,768]{1,0:T(8,128)(2,1)} %shard_map.198.refs_0_), channel_id=1, source_target_pairs={{0,5},{1,4},{2,7},{3,6},{4,1},{5,0},{6,3},{7,2},{8,13},{9,12},{10,... | collective-permute-start | bytes 294920 | tf_op jit(solution)/shard_map/ppermute | solution.py:580
  174.6 33.9 %collective-permute-start.16 = (bf16[64,768]{1,0:T(8,128)(2,1)}, bf16[64,768]{1,0:T(8,128)(2,1)S(1)}, u32[]{:S(2)}, u32[]{:S(2)}) collective-permute-start(bf16[64,768]{1,0:T(8,128)(2,1)} %shard_map.198.refs_0_), channel_id=1, source_target_pairs={{0,4},{1,5},{2,6},{3,7},{4,0},{5,1},{6,2},{7,3},{8,12},{9,13},{10,... | collective-permute-start | bytes 294920 | tf_op jit(solution)/shard_map/ppermute | solution.py:580
  199.8 8.7 %collective-permute-start.15 = (bf16[64,768]{1,0:T(8,128)(2,1)}, bf16[64,768]{1,0:T(8,128)(2,1)S(1)}, u32[]{:S(2)}, u32[]{:S(2)}) collective-permute-start(bf16[64,768]{1,0:T(8,128)(2,1)} %shard_map.198.refs_0_), channel_id=1, source_target_pairs={{0,3},{1,2},{2,1},{3,0},{4,7},{5,6},{6,5},{7,4},{8,11},{9,10},{10,... | collective-permute-start | bytes 294920 | tf_op jit(solution)/shard_map/ppermute | solution.py:580
  206.6 5.3 %collective-permute-start.14 = (bf16[64,768]{1,0:T(8,128)(2,1)}, bf16[64,768]{1,0:T(8,128)(2,1)S(1)}, u32[]{:S(2)}, u32[]{:S(2)}) collective-permute-start(bf16[64,768]{1,0:T(8,128)(2,1)} %shard_map.198.refs_0_), channel_id=1, source_target_pairs={{0,2},{1,3},{2,0},{3,1},{4,6},{5,7},{6,4},{7,5},{8,10},{9,11},{10,... | collective-permute-start | bytes 294920 | tf_op jit(solution)/shard_map/ppermute | solution.py:580
  206.6 5.6 %collective-permute-start.13 = (bf16[64,768]{1,0:T(8,128)(2,1)}, bf16[64,768]{1,0:T(8,128)(2,1)S(1)}, u32[]{:S(2)}, u32[]{:S(2)}) collective-permute-start(bf16[64,768]{1,0:T(8,128)(2,1)} %shard_map.198.refs_0_), channel_id=1, source_target_pairs={{0,1},{1,0},{2,3},{3,2},{4,5},{5,4},{6,7},{7,6},{8,9},{9,8},{10,11... | collective-permute-start | bytes 294920 | tf_op jit(solution)/shard_map/ppermute | solution.py:580
  215.8 6.2 %collective-permute-start.22 = (bf16[8,8,56,384]{3,2,1,0:T(8,128)(2,1)}, bf16[8,8,56,384]{3,2,1,0:T(8,128)(2,1)S(1)}, u32[]{:S(2)}, u32[]{:S(2)}) collective-permute-start(bf16[8,8,56,384]{3,2,1,0:T(8,128)(2,1)} %shard_map.205.in_ref), channel_id=1, source_target_pairs={{0,8},{8,0},{1,9},{9,1},{2,10},{10,2},{3,11},{11,3},{4,12},{12,4},... | collective-permute-start | bytes 8257544 | tf_op jit(solution)/shard_map/ppermute | solution.py:564
  (2 other events, 6.7 us)

commit v8 on v7

--- a/solution.py
+++ b/solution.py
@@ -144,7 +144,7 @@
 
 
 def project_kernel(
-    tok_ref, gain_ref, shift_ref, w_ref, kv_ref, normed_ref,
+    tok_ref, gain_ref, shift_ref, w_ref, kv_ref, q_ref, normed_ref,
     x_buf, w_buf, kv_buf, gain_buf, shift_buf, x_sem, w_sem, kv_sem, gain_sem, shift_sem,
 ):
     copy_x = pltpu.make_async_copy(tok_ref.at[lax.axis_index(MICRO)], x_buf, x_sem)
@@ -164,21 +164,22 @@
         full = mm(normed, w_buf[slot])
         return jnp.where(odd, full[:, 192:], full[:, :192]).astype(BF)
 
-    kv_buf[...] = jnp.concatenate([part(0), part(1), part(2), jnp.zeros((TOK, HD), BF)], axis=1)
+    kv_buf[...] = jnp.concatenate([part(0), part(1)], axis=1)
     sends = send_copies(kv_buf, kv_ref, range(8), kv_sem)
     normed_ref[...] = normed
+    q_ref[...] = jnp.concatenate([part(2), jnp.zeros((TOK, HD), BF)], axis=1)
     wait_all(sends)
 
 
-def attend_kernel(scene_ref, same_ref, other_ref, out_ref, buf, sem):
+def attend_kernel(scene_ref, q_ref, same_ref, other_ref, out_ref, buf, sem):
     first, big = span(scene_ref)
 
     def run(count):
         rows = count * TOK
         keys = jnp.concatenate(
-            [ref[pl.ds(first, count), :, :384].reshape(rows, 384) for ref in (same_ref, other_ref)], axis=0
+            [ref[pl.ds(first, count)].reshape(rows, 384) for ref in (same_ref, other_ref)], axis=0
         )
-        query = same_ref[chip_index(), :, 384:]
+        query = q_ref[...]
         q0, q1 = halves(query[:, :128])
         blocks = [keys[:, :128], keys[:, 128:256], keys[:, 256:]]
         mixed = []
@@ -280,9 +281,7 @@
 
 
 def pair_kernel(one_ref, two_ref, out_ref):
-    total = (one_ref[...].astype(F32) + two_ref[...].astype(F32)).astype(BF)
-    out_ref[0] = total[:, :384]
-    out_ref[1] = total[:, 384:]
+    out_ref[...] = (one_ref[...].astype(F32) + two_ref[...].astype(F32)).astype(BF)
 
 
 def middle_kernel(
@@ -331,8 +330,8 @@
 
 
 def attend_back_kernel(
-    scene_ref, kvs_ref, kvo_ref, gs_ref, go_ref, normed_ref, mixed_ref, low0_ref, low1_ref, low2_ref, low3_ref,
-    gqkv_ref, keep_ref, send_ref, kv_buf, grad_buf, mixed_buf, kv_sem, mixed_sem,
+    scene_ref, kvs_ref, kvo_ref, q_ref, gs_ref, go_ref, normed_ref, mixed_ref, low0_ref, low1_ref, low2_ref, low3_ref,
+    gqkv_ref, keep_ref, send_ref, kv_buf, q_buf, grad_buf, mixed_buf, kv_sem, q_sem, mixed_sem,
 ):
     first, big = span(scene_ref)
     chip = chip_index()
@@ -345,6 +344,11 @@
         loads = [
             pltpu.make_async_copy(ref.at[pl.ds(first, count)], kv_buf.at[slot, pl.ds(0, count)], kv_sem.at[slot])
             for slot, ref in enumerate((kvs_ref, kvo_ref))
+        ] + [
+            pltpu.make_async_copy(
+                q_ref.at[pl.ds(first, count), which], q_buf.at[slot, pl.ds(0, count)], q_sem.at[slot]
+            )
+            for slot, which in enumerate((core, 1 - core))
         ]
         for load in loads:
             load.start()
@@ -360,9 +364,9 @@
         own_stats = g_own[0].astype(F32)
         all_stats = grad[0].astype(F32).T
         wait_all(loads)
-        every = cut(jnp.concatenate([kv_buf[slot, :count].reshape(rows, 640) for slot in range(2)], axis=0))
-        kv, query = every[:3], every[3:]
-        own = cut(kv_buf[0, chip - first])
+        kv = cut(jnp.concatenate([kv_buf[slot, :count].reshape(rows, 384) for slot in range(2)], axis=0))
+        query = cut(jnp.concatenate([q_buf[slot, :count].reshape(rows, 256) for slot in range(2)], axis=0))
+        own = cut(kv_buf[0, chip - first]) + cut(q_buf[0, chip - first])
         q_heads = [*halves(own[3]), own[4]]
         k_heads = [*halves(own[0]), halves(own[1])[0]]
         v_heads = [halves(own[1])[1], *halves(own[2])]
@@ -450,33 +454,17 @@
     sums_ref[...] = jnp.concatenate([gain1, shift1, vec_ref[...][:2], jnp.zeros((4, D), F32)], axis=0)
 
 
-def add_kernel(one_ref, two_ref, ff_ref, out_ref, buf, sem, ff_sem):
-    micro = lax.axis_index(MICRO)
-    copies = []
-    for chip in range(8):
-        for half in range(2):
-            copy = pltpu.make_async_copy(
-                ff_ref.at[half], out_ref.at[2 * chip + micro, pl.ds(48 * (1 + half), 48)], ff_sem.at[chip, half]
-            )
-            copy.start()
-            copies.append(copy)
+def add_kernel(one_ref, two_ref, out_ref, buf, sem):
     buf[...] = (one_ref[...].astype(F32) + two_ref[...].astype(F32)).astype(BF)
-    copy = pltpu.make_async_copy(buf, out_ref.at[:, pl.ds(0, 48)], sem)
+    copy = pltpu.make_async_copy(buf, out_ref, sem)
     copy.start()
-    copies.append(copy)
-    wait_all(copies)
-
-
-def pick_kernel(in_ref, out_ref):
-    micro = lax.axis_index(MICRO)
-    for chip in range(8):
-        out_ref[chip] = in_ref[2 * chip + micro, 48:]
+    copy.wait()
 
 
 def sum_kernel(in_ref, vec_ref, out_ref, buf, sem):
-    total = in_ref[0, :48].astype(F32)
+    total = in_ref[0].astype(F32)
     for index in range(1, 16):
-        total = total + in_ref[index, :48].astype(F32)
+        total = total + in_ref[index].astype(F32)
     vectors = vec_ref[...][:4]
     block = jnp.concatenate([total, vectors[:, :384], vectors[:, 384:]], axis=0).astype(BF)
     for index in range(8):
@@ -523,37 +511,33 @@
     wait_all(copies)
 
 
-def spread_ff_kernel(same_ref, other_ref, up_ref, down_ref):
-    core = lax.axis_index(CORE)
-    for ref, owner in ((same_ref, core), (other_ref, 1 - core)):
-        for chip in range(8):
-            up_ref[pl.ds(pl.multiple_of((chip * 2 + owner) * 48, 16), 48)] = ref[chip, :48].astype(F32)
-            down_ref[chip * 48:(chip + 1) * 48, pl.ds(pl.multiple_of(owner * 384, 128), 384)] = ref[
-                chip, 48:
-            ].astype(F32)
+def spread_ff_kernel(in_ref, up_ref, down_ref):
+    up_ref[...] = in_ref[:, :384].astype(F32)
+    for tile in range(16):
+        half = (tile % 2) * 384
+        down_ref[(tile // 2) * 48:(tile // 2 + 1) * 48, half:half + 384] = in_ref[
+            tile * 48:(tile + 1) * 48, 384:
+        ].astype(F32)
 
 
 def input_kernel(
-    own_ref, one_ref, two_ref, three_ref, x_ref, gain_ref, grad_ref, result_ref, out_ref
+    own_ref, one_ref, two_ref, three_ref, x_ref, gain_ref, grad_ref, result_ref, out_ref, buf, sem
 ):
     total = own_ref[...]
     for ref in (one_ref, two_ref, three_ref):
         total = total + ref[...].astype(F32)
     unit, inverse = normalized(x_ref[...].astype(F32))
     grad = grad_ref[...] + norm_back(total, unit, inverse, gain_ref[...].reshape(1, D))
-    out_ref[:BLK] = grad.astype(BF)
-    out_ref[BLK:] = result_ref[...]
-
-
-def unpack_kernel(*refs):
-    parts, (grad_ref, result_ref) = refs[:8], refs[8:]
-    micro = lax.axis_index(MICRO)
-    group = group_index()
-    for k, ref in enumerate(parts):
-        rows = pl.ds(pl.multiple_of((group ^ (k % 4)) * BLK, BLK), BLK)
-        where = micro ^ (k // 4)
-        grad_ref[where, rows] = ref[:BLK].astype(F32)
-        result_ref[where, rows] = ref[BLK:]
+    buf[:BLK] = grad.astype(BF)
+    buf[BLK:] = result_ref[...]
+    wait_all(send_copies(buf, out_ref, range(8), sem))
+
+
+def unpack_kernel(in_ref, unused_ref, grad_ref, result_ref):
+    for index in range(8):
+        rows = slice(index % 4 * BLK, (index % 4 + 1) * BLK)
+        grad_ref[index // 4, rows] = in_ref[index, :BLK].astype(F32)
+        result_ref[index // 4, rows] = in_ref[index, BLK:]
 
 
 def exchange(value, axes):
@@ -584,13 +568,13 @@
     tokens, scene_of_block, ln1_gain, ln1_shift, w_qkv, w_out, ln2_gain, ln2_shift, w_up, w_down, out_grad
 ):
     w_out_pad = jnp.pad(w_out.reshape(4, 192, D), ((0, 0), (HD, 0), (0, 0)))
-    kv_send, normed = call(
+    kv_send, query, normed = call(
         project_kernel,
-        [((8, TOK, 640), BF, "H"), ((TOK, D), BF, "L")],
+        [((8, TOK, 384), BF, "H"), ((TOK, 256), BF, "L"), ((TOK, D), BF, "L")],
         [(tokens, "H"), (ln1_gain, "H"), (ln1_shift, "H"), (w_qkv, "H")],
         10**9,
         [
-            pltpu.VMEM((TOK, D), BF), pltpu.VMEM((3, D, 384), BF), pltpu.VMEM((TOK, 640), BF),
+            pltpu.VMEM((TOK, D), BF), pltpu.VMEM((3, D, 384), BF), pltpu.VMEM((TOK, 384), BF),
             pltpu.VMEM((D,), F32), pltpu.VMEM((D,), F32), DMA, DMA((3,)), DMA((8,)), DMA, DMA,
         ],
     )
@@ -599,11 +583,12 @@
     (mixed_send,) = call(
         attend_kernel,
         [((8, TOK, 256), BF, "H")],
-        [(scene_of_block, "S"), (kv_same, "V"), (kv_other, "V")],
+        [(scene_of_block, "S"), (query, "L"), (kv_same, "V"), (kv_other, "V")],
         2 * 10**9,
         [pltpu.VMEM((TOK, 256), BF), DMA((8,))],
     )
     mixed = exchange(mixed_send, NARROW)
+    queries = lax.all_gather(after(pin(query), kv_same), WIDE, axis=0, tiled=True).reshape(8, 2, TOK, 256)
     ff_send, middle, normed2, act, grad_pre = call(
         forward_kernel,
         [
@@ -656,8 +641,9 @@
         ],
     )
     (ff_part,) = call(
-        pair_kernel, [((2, 48, 384), BF, "L")], [(keep, "L"), (flip(send, "xl", 2, 1), "V")], 10**7
-    )
+        pair_kernel, [((48, D), BF, "L")], [(keep, "L"), (flip(send, "xl", 2, 1), "V")], 10**7
+    )
+    ff_all = lax.all_gather(ff_part, WIDE, axis=0, tiled=True)
     grad_same = exchange(grad_send.reshape(32, BLK, 256), (*CHIP, *GROUP)).reshape(8, TOK, 256)
     lows = [flip(low, GROUP, 4, k) for k in (1, 2, 3)]
     grad_same = after(grad_same, *lows, pin(ff_part))
@@ -666,21 +652,22 @@
         attend_back_kernel,
         [((TOK, 640), BF, "L")] + [((16, 48, 384), BF, "V")] * 2,
         [
-            (scene_of_block, "S"), (kv_same, "H"), (kv_other, "H"), (grad_same, "V"), (grad_other, "V"),
+            (scene_of_block, "S"), (kv_same, "H"), (kv_other, "H"), (queries, "H"), (grad_same, "V"), (grad_other, "V"),
             (normed, "L"), (mixed, "H"), (low, "L"), *[(value, "V") for value in lows],
         ],
         8 * 10**9,
         [
-            pltpu.VMEM((2, 5, TOK, 640), BF), pltpu.VMEM((D, 640), F32), pltpu.VMEM((TOK, 256), BF), DMA((2,)), DMA,
+            pltpu.VMEM((2, 5, TOK, 384), BF), pltpu.VMEM((2, 5, TOK, 256), BF), pltpu.VMEM((D, 640), F32),
+            pltpu.VMEM((TOK, 256), BF), DMA((2,)), DMA((2,)), DMA,
         ],
         vmem=24,
     )
     (weight_send,) = call(
         add_kernel,
-        [((16, 144, 384), BF, "H")],
-        [(keep, "V"), (swap(send), "V"), (ff_part, "L")],
+        [((16, 48, 384), BF, "H")],
+        [(keep, "V"), (swap(send), "V")],
         10**8,
-        [pltpu.VMEM((16, 48, 384), BF), DMA, DMA((8, 2))],
+        [pltpu.VMEM((16, 48, 384), BF), DMA],
     )
     weight_parts = exchange(weight_send, (*CHIP, MICRO))
     own, *sends, sums = call(
@@ -691,7 +678,7 @@
         [pltpu.VMEM((TOK, D), BF), pltpu.VMEM((TOK, D), F32), pltpu.VMEM((3, D, 384), BF), DMA, DMA((3,))],
     )
     parts = [flip(value, GROUP, 4, k + 1) for k, value in enumerate(sends)]
-    weight_parts = after(weight_parts, pin(sums), *parts)
+    weight_parts = after(weight_parts, pin(sums))
     (weight_total,) = call(
         sum_kernel,
         [((8, 8, 56, 384), BF, "H")],
@@ -701,29 +688,20 @@
     )
     (packed,) = call(
         input_kernel,
-        [((2 * BLK, D), BF, "L")],
+        [((8, 2 * BLK, D), BF, "H")],
         [
             (own, "L"), *[(value, "V") for value in parts], (x_part, "L"), (ln1_gain, "L"), (grad_mid, "L"),
             (result_part, "L"),
         ],
         10**8,
-    )
-    others = {k: flip(packed, NARROW, 8, k) for k in (7, 5, 6, 3, 1, 4, 2)}
-    input_grad, result = call(
-        unpack_kernel,
-        [((2, TOK, D), F32, "L"), ((2, TOK, D), BF, "L")],
-        [(packed, "L"), *[(others[k], "V") for k in range(1, 8)]],
-        10**8,
-    )
-    (ff_same,) = call(pick_kernel, [((8, 96, 384), BF, "V")], [(weight_parts, "V")], 10**7)
+        [pltpu.VMEM((2 * BLK, D), BF), DMA((8,))],
+    )
     up_grad, down_grad = call(
-        spread_ff_kernel,
-        [((D, FFL), F32, "L"), ((FFL, D), F32, "L")],
-        [(ff_same, "V"), (swap(ff_same), "V")],
-        10**7,
+        spread_ff_kernel, [((D, FFL), F32, "L"), ((FFL, D), F32, "L")], [(ff_all, "L")], 10**7
     )
     weight_same = exchange(weight_total.reshape(64, 56, 384), (*CHIP, *NARROW)).reshape(8, 8, 56, 384)
-    weight_same = after(weight_same, *map(pin, (input_grad, result, up_grad, down_grad)))
+    weight_same = after(weight_same, pin(packed), pin(up_grad), pin(down_grad))
+    everyone = exchange(after(pin(packed), weight_same), NARROW)
     weight_other = swap(weight_same)
     scratch = [
         pltpu.VMEM((8, 48, 3 * D), F32), pltpu.VMEM((4, 2, 48, D), F32), DMA((8,)), DMA((4, 2)),
@@ -744,6 +722,9 @@
         scratch,
         aliases={2: 0, 3: 1},
     )
+    input_grad, result = call(
+        unpack_kernel, [((2, TOK, D), F32, "L"), ((2, TOK, D), BF, "L")], [(everyone, "V"), (vectors[0], "H")], 10**8
+    )
     return (
         result, input_grad, qkv_grad, out_proj_grad, *vectors, up_grad, down_grad
     )

time: 227 us -> 227 us (level)
  between operations: 1 us -> 14.3 us
  starting transfers between devices: 64.8 us -> 58.9 us
  blocking collectives: 23.7 us -> 18 us
  waiting for transfers between devices: 85.2 us -> 82.9 us
    ppermute x17 -> x10, waiting for transfers between devices: 66.1 us -> 41.9 us  [flip(): lax.ppermute(value, axes, [(index, index ^ bits) for index in range(count)])]
    all_gather x0 -> x2, waiting for transfers between devices: none -> 11.2 us  [the longest x1 11.2 us: shards(): ff_all = lax.all_gather(ff_part, WIDE, axis=0, tiled=True)]
    all_to_all x5 -> x6, waiting for transfers between devices: 12.6 us -> 23.2 us  [exchange(): return lax.all_to_all(value, axes, 0, 0, tiled=True)]
    ppermute x17 -> x10, starting transfers between devices: 23.6 us -> 13.6 us  [flip(): lax.ppermute(value, axes, [(index, index ^ bits) for index in range(count)])]
    all_to_all x5 -> x6, starting transfers between devices: 30.9 us -> 37.5 us  [exchange(): return lax.all_to_all(value, axes, 0, 0, tiled=True)]
    all_to_all x1, blocking collectives: 23.7 us -> 18 us  [exchange(): return lax.all_to_all(value, axes, 0, 0, tiled=True)]
    ppermute x6 -> x5, starting transfers between devices: 10.3 us -> 7.79 us  [swap(): return lax.ppermute(value, CORE, [(0, 1), (1, 0)])]
    ppermute x6 -> x5, waiting for transfers between devices: 6.52 us -> 5.09 us  [swap(): return lax.ppermute(value, CORE, [(0, 1), (1, 0)])]
  transfers between devices with their start and end apart: 28 -> 23, of which waited for: 18 -> 16; matrix products, arithmetic and copies ran while one was open for 0% -> 1% of each run, Pallas kernels for 8% -> 15%
where the time goes in v8:
time: 227 us; the launch traced here: 226 us
  waiting for transfers between devices  82.9 us (37%)
  starting transfers between devices  58.9 us (26%)
  Pallas kernels  49.5 us (22%)
  blocking collectives  18 us (8%)
  between operations  14.3 us (6%)
  local copies, waits for them, and re-layouts  2.28 us (1%)
    pallas_call x17, Pallas kernels, call(): pl.pallas_call(kernel, out_shape=[(pltpu.HBM if place in 'HL' else jax.Sh...  49.5 us
    ppermute x10, waiting for transfers between devices, flip(): lax.ppermute(value, axes, [(index, index ^ bits) for index in range(count)])  41.9 us
    all_to_all x6, starting transfers between devices, exchange(): return lax.all_to_all(value, axes, 0, 0, tiled=True)  37.5 us
    all_to_all x6, waiting for transfers between devices, exchange(): return lax.all_to_all(value, axes, 0, 0, tiled=True)  23.2 us
    all_to_all x1, blocking collectives, exchange(): return lax.all_to_all(value, axes, 0, 0, tiled=True)  18 us
    ppermute x10, starting transfers between devices, flip(): lax.ppermute(value, axes, [(index, index ^ bits) for index in range(count)])  13.6 us
    all_gather x1, waiting for transfers between devices, shards(): ff_all = lax.all_gather(ff_part, WIDE, axis=0, tiled=True)  11.2 us
    ppermute x5, starting transfers between devices, swap(): return lax.ppermute(value, CORE, [(0, 1), (1, 0)])  7.79 us
  transfers between devices with their start and end apart: 23, of which 16 were waited for; matrix products, arithmetic and copies ran while one was open for 1% of the time, Pallas kernels for 15%

profile of v8, /device:TPU:1, one launch (start us, length us, event | category | flops | bytes accessed | tf_op | source)
XLA Modules:
  0.0 225.9 jit_solution(11074370597866464857)
XLA Ops:
  7.2 3.8 %shard_map.186 = (bf16[8,128,384]{2,1,0:T(8,128)(2,1)}, bf16[128,256]{1,0:T(8,128)(2,1)}, bf16[128,768]{1,0:T(8,128)(2,1)}) custom-call(bf16[2,128,768]{2,1,0:T(8,128)(2,1)} %tok_ref.7, f32[768]{0:T(1024)} %gain_ref.7, f32[768]{0:T(1024)} %shift_ref.2, bf16[768,2304]{1,0:T(8,128)(2,1)} %w_ref.3), custom_call_target="tpu_custom_call" | custom-call | flops 1000 | bytes 1000 | tf_op jit(solution)/shard_map/pallas_call | solution.py:106
  11.0 18.0 %all_to_all.35.refs_1_.same_ref.kvs_ref = bf16[8,128,384]{2,1,0:T(8,128)(2,1)S(1)} all-to-all(bf16[8,128,384]{2,1,0:T(8,128)(2,1)} %get-tuple-element.53), channel_id=1, replica_groups=mesh['y'=4,'xl'=2,'c'=2,'zh'=2,'zl'=2,'xh'=2] {'y','xl'}, dimensions={0} | all-to-all | bytes 1572864 | tf_op jit(solution)/shard_map/all_to_all | solution.py:544
  32.8 2.6 %shard_map.188 = bf16[8,128,256]{2,1,0:T(8,128)(2,1)} custom-call(s32[2,32]{1,0:T(2,128)S(1)} %copy-done.3, bf16[128,256]{1,0:T(8,128)(2,1)} %get-tuple-element.54.refs_0_.q_ref, bf16[8,128,384]{2,1,0:T(8,128)(2,1)S(1)} %all_to_all.35.refs_1_.same_ref.kvs_ref, bf16[8,128,384]{2,1,0:T(8,128)(2,1)S(1)} %collective-permute-done.other_ref.kvo_ref), custom_call_target="tpu_custom_call" | custom-call | flops 1000 | bytes 1000 | tf_op jit(solution)/shard_map/pallas_call | solution.py:106
  36.3 7.2 %all-to-all-start.1 = ((bf16[8,128,256]{2,1,0:T(8,128)(2,1)}), bf16[8,128,256]{2,1,0:T(8,128)(2,1)S(1)}, u32[]{:S(2)}, u32[]{:S(2)}) async-start(bf16[8,128,256]{2,1,0:T(8,128)(2,1)} %shard_map.188), calls=%async_computation.1 | async-start | bytes 1048576 | tf_op jit(solution)/shard_map/all_to_all | solution.py:544
  45.6 8.6 %all-to-all-done.1.mixed_ref = bf16[8,128,256]{2,1,0:T(8,128)(2,1)S(1)} async-done(((bf16[8,128,256]{2,1,0:T(8,128)(2,1)}), bf16[8,128,256]{2,1,0:T(8,128)(2,1)S(1)}, u32[]{:S(2)}, u32[]{:S(2)}) %all-to-all-start.1) | async-done | bytes 524320 | tf_op jit(solution)/shard_map/all_to_all | solution.py:544
  54.2 5.6 %shard_map.189 = (bf16[8,64,768]{2,1,0:T(8,128)(2,1)}, f32[8,32,768]{2,1,0:T(8,128)}, bf16[256,768]{1,0:T(8,128)(2,1)S(1)}, bf16[256,384]{1,0:T(8,128)(2,1)S(1)}, bf16[256,384]{1,0:T(8,128)(2,1)S(1)}) custom-call(bf16[8,128,256]{2,1,0:T(8,128)(2,1)S(1)} %all-to-all-done.1.mixed_ref, bf16[2,128,768]{2,1,0:T(8,128)(2,1)} %tok_ref.7, ...), custom_call_target="tpu_custom_call" | custom-call | flops 1000 | bytes 1000 | tf_op jit(solution)/shard_map/pallas_call | solution.py:106
  59.8 2.8 %shard_map.190 = (bf16[8,48,768]{2,1,0:T(8,128)(2,1)S(1)}, bf16[8,48,768]{2,1,0:T(8,128)(2,1)}) custom-call(bf16[256,768]{1,0:T(8,128)(2,1)S(1)} %get-tuple-element.56.normed_ref, bf16[256,384]{1,0:T(8,128)(2,1)S(1)} %get-tuple-element.57.act_ref, bf16[256,384]{1,0:T(8,128)(2,1)S(1)} %get-tuple-element.58.gpre_ref, bf16[2,128,768]{2,1,0:T(8,128)(2,1)} %og_ref.5), custom_call_target="tpu_custom_call" | custom-call | flops 1000 | bytes 1000 | tf_op jit(solution)/shard_map/pallas_call | solution.py:106
  64.4 3.6 %all-to-all-start.2 = ((bf16[8,64,768]{2,1,0:T(8,128)(2,1)}), bf16[8,64,768]{2,1,0:T(8,128)(2,1)S(1)}, u32[]{:S(2)}, u32[]{:S(2)}) async-start(bf16[8,64,768]{2,1,0:T(8,128)(2,1)} %get-tuple-element.55), calls=%async_computation.2 | async-start | bytes 1572864 | tf_op jit(solution)/shard_map/all_to_all | solution.py:544
  71.6 2.1 collective-permute-start.4
  73.7 2.4 %collective-permute-done.2.refs_1_ = bf16[2,48,768]{2,1,0:T(8,128)(2,1)S(1)} collective-permute-done((bf16[2,48,768]{2,1,0:T(8,128)(2,1)}, bf16[2,48,768]{2,1,0:T(8,128)(2,1)S(1)}, u32[]{:S(2)}, u32[]{:S(2)}) %collective-permute-start.2) | collective-permute-done | bytes 147488 | tf_op jit(solution)/shard_map/ppermute | solution.py:564
  76.1 4.0 %collective-permute-done.3.refs_2_ = bf16[2,48,768]{2,1,0:T(8,128)(2,1)S(1)} collective-permute-done((bf16[2,48,768]{2,1,0:T(8,128)(2,1)}, bf16[2,48,768]{2,1,0:T(8,128)(2,1)S(1)}, u32[]{:S(2)}, u32[]{:S(2)}) %collective-permute-start.3) | collective-permute-done | bytes 147488 | tf_op jit(solution)/shard_map/ppermute | solution.py:564
  84.0 4.1 %shard_map.194 = (bf16[8,4,32,256]{3,2,1,0:T(8,128)(2,1)}, bf16[32,768]{1,0:T(8,128)(2,1)}, f32[32,768]{1,0:T(8,128)}, bf16[32,768]{1,0:T(8,128)(2,1)}, f32[8,768]{1,0:T(8,128)}, /*index=5*/bf16[32,768]{1,0:T(8,128)(2,1)}) custom-call(bf16[8,64,768]{2,1,0:T(8,128)(2,1)S(1)} %shard_map.193.sums_ref, f32[8,32,768]{2,1,0:T(8,128)} %get-tuple-element.66.middle_ref, ...), custom_call_target="tpu_custom_call" | custom-call | flops 1000 | bytes 1000 | tf_op jit(solution)/shard_map/pallas_call | solution.py:106
  88.2 6.2 %all-to-all-start.3 = ((bf16[32,32,256]{2,1,0:T(8,128)(2,1)}), bf16[32,32,256]{2,1,0:T(8,128)(2,1)S(1)}, u32[]{:S(2)}, u32[]{:S(2)}) async-start(bf16[32,32,256]{2,1,0:T(8,128)(2,1)} %bitcast.11), calls=%async_computation.3 | async-start | bytes 1048576 | tf_op jit(solution)/shard_map/all_to_all | solution.py:544
  95.7 3.3 %collective-permute-start.7 = (bf16[32,768]{1,0:T(8,128)(2,1)}, bf16[32,768]{1,0:T(8,128)(2,1)S(1)}, u32[]{:S(2)}, u32[]{:S(2)}) collective-permute-start(bf16[32,768]{1,0:T(8,128)(2,1)} %get-tuple-element.68.low0_ref), channel_id=1, source_target_pairs={{0,3},{1,2},{2,1},{3,0},{4,7},{5,6},{6,5},{7,4},{8,11},{9,10},{10,... | collective-permute-start | bytes 147464 | tf_op jit(solution)/shard_map/ppermute | solution.py:564
  99.9 2.2 collective-permute-done.8.two_ref
  105.7 3.5 %collective-permute-start.9 = (bf16[8,128,256]{2,1,0:T(8,128)(2,1)S(1)}, bf16[8,128,256]{2,1,0:T(8,128)(2,1)S(1)}, u32[]{:S(2)}, u32[]{:S(2)}) collective-permute-start(bf16[8,128,256]{2,1,0:T(8,128)(2,1)S(1)} %shard_map.196.gs_ref), channel_id=1, source_target_pairs={{0,8},{8,0},{1,9},{9,1},{2,10},{10,2},{3,11},{11,3},{4,12},{12,4},... | collective-permute-start | bytes 1572872 | tf_op jit(solution)/shard_map/ppermute | solution.py:548
  110.7 4.8 %shard_map.197 = (bf16[128,640]{1,0:T(8,128)(2,1)}, bf16[16,48,384]{2,1,0:T(8,128)(2,1)S(1)}, bf16[16,48,384]{2,1,0:T(8,128)(2,1)S(1)}) custom-call(s32[2,32]{1,0:T(2,128)S(1)} %copy-done.3, bf16[8,128,384]{2,1,0:T(8,128)(2,1)} %copy-done, bf16[8,128,384]{2,1,0:T(8,128)(2,1)} %copy-done.2, bf16[8,2,128,256]{3,2,1,0:T(8,128)(2,1)} %bitcast.10, ...), custom_call_target="tpu_custom_call" | custom-call | flops 1000 | bytes 1000 | tf_op jit(solution)/shard_map/pallas_call | solution.py:106
  118.6 7.2 %all-to-all-start.4 = ((bf16[16,48,384]{2,1,0:T(8,128)(2,1)}), bf16[16,48,384]{2,1,0:T(8,128)(2,1)S(1)}, u32[]{:S(2)}, u32[]{:S(2)}) async-start(bf16[16,48,384]{2,1,0:T(8,128)(2,1)} %shard_map.200), calls=%async_computation.4 | async-start | bytes 1179648 | tf_op jit(solution)/shard_map/all_to_all | solution.py:544
  125.8 4.1 %shard_map.198 = (f32[32,768]{1,0:T(8,128)}, bf16[32,768]{1,0:T(8,128)(2,1)}, bf16[32,768]{1,0:T(8,128)(2,1)}, bf16[32,768]{1,0:T(8,128)(2,1)}, f32[8,768]{1,0:T(8,128)}) custom-call(bf16[128,640]{1,0:T(8,128)(2,1)} %get-tuple-element.71.gqkv_ref, bf16[2,128,768]{2,1,0:T(8,128)(2,1)} %tok_ref.7, bf16[768,2304]{1,0:T(8,128)(2,1)} %w_ref.3, ...), custom_call_target="tpu_custom_call" | custom-call | flops 1000 | bytes 1000 | tf_op jit(solution)/shard_map/pallas_call | solution.py:106
  129.8 6.6 %all-to-all-done.4.refs_0_ = bf16[16,48,384]{2,1,0:T(8,128)(2,1)S(1)} async-done(((bf16[16,48,384]{2,1,0:T(8,128)(2,1)}), bf16[16,48,384]{2,1,0:T(8,128)(2,1)S(1)}, u32[]{:S(2)}, u32[]{:S(2)}) %all-to-all-start.4) | async-done | bytes 589856 | tf_op jit(solution)/shard_map/all_to_all | solution.py:544
  136.5 2.4 %shard_map.202 = bf16[8,8,56,384]{3,2,1,0:T(8,128)(2,1)} custom-call(bf16[16,48,384]{2,1,0:T(8,128)(2,1)S(1)} %shard_map.201.in_ref, f32[8,768]{1,0:T(8,128)} %get-tuple-element.82.refs_1_.vec_ref), custom_call_target="tpu_custom_call" | custom-call | flops 1000 | bytes 1000 | tf_op jit(solution)/shard_map/pallas_call | solution.py:106
  138.9 6.8 %all-to-all-start.5 = ((bf16[64,56,384]{2,1,0:T(8,128)(2,1)}), bf16[64,56,384]{2,1,0:T(8,128)(2,1)S(1)}, u32[]{:S(2)}, u32[]{:S(2)}) async-start(bf16[64,56,384]{2,1,0:T(8,128)(2,1)} %bitcast.8), calls=%async_computation.5 | async-start | bytes 5505024 | tf_op jit(solution)/shard_map/all_to_all | solution.py:544
  146.5 2.6 %collective-permute-start.10 = (bf16[32,768]{1,0:T(8,128)(2,1)S(1)}, bf16[32,768]{1,0:T(8,128)(2,1)S(1)}, u32[]{:S(2)}, u32[]{:S(2)}) collective-permute-start(bf16[32,768]{1,0:T(8,128)(2,1)S(1)} %copy-done.7), channel_id=1, source_target_pairs={{0,1},{1,0},{2,3},{3,2},{4,5},{5,4},{6,7},{7,6},{8,9},{9,8},{10,11... | collective-permute-start | bytes 147464 | tf_op jit(solution)/shard_map/ppermute | solution.py:564
  150.8 28.1 %collective-permute-done.10.one_ref = bf16[32,768]{1,0:T(8,128)(2,1)S(1)} collective-permute-done((bf16[32,768]{1,0:T(8,128)(2,1)S(1)}, bf16[32,768]{1,0:T(8,128)(2,1)S(1)}, u32[]{:S(2)}, u32[]{:S(2)}) %collective-permute-start.10) | collective-permute-done | bytes 49184 | tf_op jit(solution)/shard_map/ppermute | solution.py:564
  178.8 2.2 collective-permute-done.12.three_ref
  181.0 2.2 shard_map.199.refs_1_.refs_0_
  183.2 11.2 %all-gather.5.cloned.1.call-done.in_ref = bf16[768,768]{1,0:T(8,128)(2,1)} async-done(((bf16[48,768]{1,0:T(8,128)(2,1)}), bf16[768,768]{1,0:T(8,128)(2,1)}) %all-gather.5.cloned.1.call-update) | async-done | bytes 1179664 | tf_op jit(solution)/shard_map/all_gather | solution.py:646
  194.5 2.7 %shard_map.203 = (f32[768,384]{1,0:T(8,128)}, f32[384,768]{1,0:T(8,128)}) custom-call(bf16[768,768]{1,0:T(8,128)(2,1)} %all-gather.5.cloned.1.call-done.in_ref), custom_call_target="tpu_custom_call" | custom-call | flops 1000 | bytes 1000 | tf_op jit(solution)/shard_map/pallas_call | solution.py:106
  197.5 6.5 %all-to-all-start.6 = ((bf16[8,64,768]{2,1,0:T(8,128)(2,1)}), bf16[8,64,768]{2,1,0:T(8,128)(2,1)S(1)}, u32[]{:S(2)}, u32[]{:S(2)}) async-start(bf16[8,64,768]{2,1,0:T(8,128)(2,1)} %shard_map.205), calls=%async_computation.6 | async-start | bytes 1572864 | tf_op jit(solution)/shard_map/all_to_all | solution.py:544
  204.0 2.4 %shard_map.206 = (f32[768,2304]{1,0:T(8,128)}, f32[768,768]{1,0:T(8,128)}, f32[8,384]{1,0:T(8,128)S(1)}) custom-call(bf16[8,8,56,384]{3,2,1,0:T(8,128)(2,1)S(1)} %shard_map.204.refs_1_.in_ref), custom_call_target="tpu_custom_call" | custom-call | flops 1000 | bytes 1000 | tf_op jit(solution)/shard_map/pallas_call | solution.py:106
  206.4 4.8 %shard_map.207 = (f32[768,2304]{1,0:T(8,128)}, f32[768,768]{1,0:T(8,128)}, f32[768]{0:T(1024)}, f32[768]{0:T(1024)}, f32[768]{0:T(1024)}, /*index=5*/f32[768]{0:T(1024)}) custom-call(bf16[8,8,56,384]{3,2,1,0:T(8,128)(2,1)} %collective-permute-done.14.in_ref, f32[8,384]{1,0:T(8,128)S(1)} %get-tuple-element.85.refs_0_, ...), custom_call_target="tpu_custom_call", output_to_operand_aliasing={{0}: (2, {}), {1}: (3, {})} | custom-call | flops 1000 | bytes 1000 | tf_op jit(solution)/shard_map/pallas_call | solution.py:106
  211.3 6.7 %all-to-all-done.6.in_ref = bf16[8,64,768]{2,1,0:T(8,128)(2,1)S(1)} async-done(((bf16[8,64,768]{2,1,0:T(8,128)(2,1)}), bf16[8,64,768]{2,1,0:T(8,128)(2,1)S(1)}, u32[]{:S(2)}, u32[]{:S(2)}) %all-to-all-start.6) | async-done | bytes 786464 | tf_op jit(solution)/shard_map/all_to_all | solution.py:544
  (57 shorter events, 30.1 us)
Async XLA Ops:
  7.2 25.6 %copy-start.3 = (s32[2,32]{1,0:T(2,128)S(1)}, s32[2,32]{1,0:T(2,128)}, u32[]{:S(2)}) copy-start(s32[2,32]{1,0:T(2,128)} %scene_ref.3) | copy-start | bytes 772
  29.0 16.6 %copy-start = (bf16[8,128,384]{2,1,0:T(8,128)(2,1)}, bf16[8,128,384]{2,1,0:T(8,128)(2,1)S(1)}, u32[]{:S(2)}) copy-start(bf16[8,128,384]{2,1,0:T(8,128)(2,1)S(1)} %all_to_all.35.refs_1_.same_ref.kvs_ref) | copy-start | bytes 2359300
  29.0 3.8 %collective-permute-start = (bf16[8,128,384]{2,1,0:T(8,128)(2,1)S(1)}, bf16[8,128,384]{2,1,0:T(8,128)(2,1)S(1)}, u32[]{:S(2)}, u32[]{:S(2)}) collective-permute-start(bf16[8,128,384]{2,1,0:T(8,128)(2,1)S(1)} %all_to_all.35.refs_1_.same_ref.kvs_ref), channel_id=1, source_target_pairs={{0,8},{8,0},{1,9},{9,1},{2,10},{10,2},{3,11},{11,3},{4,12},{12,4},... | collective-permute-start | bytes 2359304 | tf_op jit(solution)/shard_map/ppermute | solution.py:548
  35.4 0.9 copy-start.2
  36.3 18.0 %all-to-all-start.1 = ((bf16[8,128,256]{2,1,0:T(8,128)(2,1)}), bf16[8,128,256]{2,1,0:T(8,128)(2,1)S(1)}, u32[]{:S(2)}, u32[]{:S(2)}) async-start(bf16[8,128,256]{2,1,0:T(8,128)(2,1)} %shard_map.188), calls=%async_computation.1 | async-start | bytes 1048576 | tf_op jit(solution)/shard_map/all_to_all | solution.py:544
  43.5 65.7 %all-gather.3.cloned.1.call-start = ((), (), s32[]{:S(2)}) async-start(), calls=%async_computation.7 | async-start | bytes 1114112 | tf_op jit(solution)/shard_map/all_gather | solution.py:591
  54.2 10.1 %copy-start.1 = (bf16[8,128,256]{2,1,0:T(8,128)(2,1)}, bf16[8,128,256]{2,1,0:T(8,128)(2,1)S(1)}, u32[]{:S(2)}) copy-start(bf16[8,128,256]{2,1,0:T(8,128)(2,1)S(1)} %all-to-all-done.1.mixed_ref) | copy-start | bytes 1572868
  62.6 5.3 %collective-permute-start.1 = (bf16[8,48,768]{2,1,0:T(8,128)(2,1)}, bf16[8,48,768]{2,1,0:T(8,128)(2,1)}, u32[]{:S(2)}, u32[]{:S(2)}) collective-permute-start(bf16[8,48,768]{2,1,0:T(8,128)(2,1)} %get-tuple-element.60), channel_id=1, source_target_pairs={{0,8},{8,0},{1,9},{9,1},{2,10},{10,2},{3,11},{11,3},{4,12},{12,4},... | collective-permute-start | bytes 1769480 | tf_op jit(solution)/shard_map/ppermute | solution.py:548
  64.4 19.7 %all-to-all-start.2 = ((bf16[8,64,768]{2,1,0:T(8,128)(2,1)}), bf16[8,64,768]{2,1,0:T(8,128)(2,1)S(1)}, u32[]{:S(2)}, u32[]{:S(2)}) async-start(bf16[8,64,768]{2,1,0:T(8,128)(2,1)} %get-tuple-element.55), calls=%async_computation.2 | async-start | bytes 1572864 | tf_op jit(solution)/shard_map/all_to_all | solution.py:544
  69.8 6.3 %collective-permute-start.2 = (bf16[2,48,768]{2,1,0:T(8,128)(2,1)}, bf16[2,48,768]{2,1,0:T(8,128)(2,1)S(1)}, u32[]{:S(2)}, u32[]{:S(2)}) collective-permute-start(bf16[2,48,768]{2,1,0:T(8,128)(2,1)} %get-tuple-element.62), channel_id=1, source_target_pairs={{0,32},{32,0},{64,96},{96,64},{1,33},{33,1},{65,97},{97,65},{2,34}... | collective-permute-start | bytes 442376 | tf_op jit(solution)/shard_map/ppermute | solution.py:564
  70.6 9.5 %collective-permute-start.3 = (bf16[2,48,768]{2,1,0:T(8,128)(2,1)}, bf16[2,48,768]{2,1,0:T(8,128)(2,1)S(1)}, u32[]{:S(2)}, u32[]{:S(2)}) collective-permute-start(bf16[2,48,768]{2,1,0:T(8,128)(2,1)} %get-tuple-element.63), channel_id=1, source_target_pairs={{0,64},{32,96},{64,0},{96,32},{1,65},{33,97},{65,1},{97,33},{2,66}... | collective-permute-start | bytes 442376 | tf_op jit(solution)/shard_map/ppermute | solution.py:564
  71.6 9.5 %collective-permute-start.4 = (bf16[2,48,768]{2,1,0:T(8,128)(2,1)}, bf16[2,48,768]{2,1,0:T(8,128)(2,1)S(1)}, u32[]{:S(2)}, u32[]{:S(2)}) collective-permute-start(bf16[2,48,768]{2,1,0:T(8,128)(2,1)} %get-tuple-element.64), channel_id=1, source_target_pairs={{0,96},{32,64},{64,32},{96,0},{1,97},{33,65},{65,33},{97,1},{2,98}... | collective-permute-start | bytes 442376 | tf_op jit(solution)/shard_map/ppermute | solution.py:564
  84.0 10.4 %copy-start.4 = (bf16[48,768]{1,0:T(8,128)(2,1)S(1)}, bf16[48,768]{1,0:T(8,128)(2,1)}, u32[]{:S(2)}) copy-start(bf16[48,768]{1,0:T(8,128)(2,1)} %get-tuple-element.69) | copy-start | bytes 221188
  88.2 17.5 %all-to-all-start.3 = ((bf16[32,32,256]{2,1,0:T(8,128)(2,1)}), bf16[32,32,256]{2,1,0:T(8,128)(2,1)S(1)}, u32[]{:S(2)}, u32[]{:S(2)}) async-start(bf16[32,32,256]{2,1,0:T(8,128)(2,1)} %bitcast.11), calls=%async_computation.3 | async-start | bytes 1048576 | tf_op jit(solution)/shard_map/all_to_all | solution.py:544
  94.4 7.7 %collective-permute-start.8 = (bf16[48,768]{1,0:T(8,128)(2,1)S(1)}, bf16[48,768]{1,0:T(8,128)(2,1)S(1)}, u32[]{:S(2)}, u32[]{:S(2)}) collective-permute-start(bf16[48,768]{1,0:T(8,128)(2,1)S(1)} %copy-done.4), channel_id=1, source_target_pairs={{0,16},{16,0},{1,17},{17,1},{2,18},{18,2},{3,19},{19,3},{4,20},{20... | collective-permute-start | bytes 221192 | tf_op jit(solution)/shard_map/ppermute | solution.py:564
  95.7 9.8 %collective-permute-start.7 = (bf16[32,768]{1,0:T(8,128)(2,1)}, bf16[32,768]{1,0:T(8,128)(2,1)S(1)}, u32[]{:S(2)}, u32[]{:S(2)}) collective-permute-start(bf16[32,768]{1,0:T(8,128)(2,1)} %get-tuple-element.68.low0_ref), channel_id=1, source_target_pairs={{0,3},{1,2},{2,1},{3,0},{4,7},{5,6},{6,5},{7,4},{8,11},{9,10},{10,... | collective-permute-start | bytes 147464 | tf_op jit(solution)/shard_map/ppermute | solution.py:564
  99.0 6.5 %collective-permute-start.6 = (bf16[32,768]{1,0:T(8,128)(2,1)}, bf16[32,768]{1,0:T(8,128)(2,1)S(1)}, u32[]{:S(2)}, u32[]{:S(2)}) collective-permute-start(bf16[32,768]{1,0:T(8,128)(2,1)} %get-tuple-element.68.low0_ref), channel_id=1, source_target_pairs={{0,2},{1,3},{2,0},{3,1},{4,6},{5,7},{6,4},{7,5},{8,10},{9,11},{10,... | collective-permute-start | bytes 147464 | tf_op jit(solution)/shard_map/ppermute | solution.py:564
  99.3 6.4 %collective-permute-start.5 = (bf16[32,768]{1,0:T(8,128)(2,1)}, bf16[32,768]{1,0:T(8,128)(2,1)S(1)}, u32[]{:S(2)}, u32[]{:S(2)}) collective-permute-start(bf16[32,768]{1,0:T(8,128)(2,1)} %get-tuple-element.68.low0_ref), channel_id=1, source_target_pairs={{0,1},{1,0},{2,3},{3,2},{4,5},{5,4},{6,7},{7,6},{8,9},{9,8},{10,11... | collective-permute-start | bytes 147464 | tf_op jit(solution)/shard_map/ppermute | solution.py:564
  105.7 5.0 %collective-permute-start.9 = (bf16[8,128,256]{2,1,0:T(8,128)(2,1)S(1)}, bf16[8,128,256]{2,1,0:T(8,128)(2,1)S(1)}, u32[]{:S(2)}, u32[]{:S(2)}) collective-permute-start(bf16[8,128,256]{2,1,0:T(8,128)(2,1)S(1)} %shard_map.196.gs_ref), channel_id=1, source_target_pairs={{0,8},{8,0},{1,9},{9,1},{2,10},{10,2},{3,11},{11,3},{4,12},{12,4},... | collective-permute-start | bytes 1572872 | tf_op jit(solution)/shard_map/ppermute | solution.py:548
  115.5 2.1 collective-permute-start.13
  118.6 17.9 %all-to-all-start.4 = ((bf16[16,48,384]{2,1,0:T(8,128)(2,1)}), bf16[16,48,384]{2,1,0:T(8,128)(2,1)S(1)}, u32[]{:S(2)}, u32[]{:S(2)}) async-start(bf16[16,48,384]{2,1,0:T(8,128)(2,1)} %shard_map.200), calls=%async_computation.4 | async-start | bytes 1179648 | tf_op jit(solution)/shard_map/all_to_all | solution.py:544
  138.9 7.6 %copy-start.7 = (bf16[32,768]{1,0:T(8,128)(2,1)S(1)}, bf16[32,768]{1,0:T(8,128)(2,1)}, u32[]{:S(2)}) copy-start(bf16[32,768]{1,0:T(8,128)(2,1)} %get-tuple-element.74) | copy-start | bytes 147460
  138.9 10.2 %copy-start.6 = (bf16[32,768]{1,0:T(8,128)(2,1)S(1)}, bf16[32,768]{1,0:T(8,128)(2,1)}, u32[]{:S(2)}) copy-start(bf16[32,768]{1,0:T(8,128)(2,1)} %get-tuple-element.75) | copy-start | bytes 147460
  138.9 11.4 %copy-start.5 = (bf16[32,768]{1,0:T(8,128)(2,1)S(1)}, bf16[32,768]{1,0:T(8,128)(2,1)}, u32[]{:S(2)}) copy-start(bf16[32,768]{1,0:T(8,128)(2,1)} %get-tuple-element.76) | copy-start | bytes 147460
  138.9 58.3 %all-to-all-start.5 = ((bf16[64,56,384]{2,1,0:T(8,128)(2,1)}), bf16[64,56,384]{2,1,0:T(8,128)(2,1)S(1)}, u32[]{:S(2)}, u32[]{:S(2)}) async-start(bf16[64,56,384]{2,1,0:T(8,128)(2,1)} %bitcast.8), calls=%async_computation.5 | async-start | bytes 5505024 | tf_op jit(solution)/shard_map/all_to_all | solution.py:544
  145.8 48.7 %all-gather.5.cloned.1.call-start = ((), (), s32[]{:S(2)}) async-start(), calls=%async_computation.8 | async-start | bytes 1253376 | tf_op jit(solution)/shard_map/all_gather | solution.py:646
  146.5 32.3 %collective-permute-start.10 = (bf16[32,768]{1,0:T(8,128)(2,1)S(1)}, bf16[32,768]{1,0:T(8,128)(2,1)S(1)}, u32[]{:S(2)}, u32[]{:S(2)}) collective-permute-start(bf16[32,768]{1,0:T(8,128)(2,1)S(1)} %copy-done.7), channel_id=1, source_target_pairs={{0,1},{1,0},{2,3},{3,2},{4,5},{5,4},{6,7},{7,6},{8,9},{9,8},{10,11... | collective-permute-start | bytes 147464 | tf_op jit(solution)/shard_map/ppermute | solution.py:564
  149.1 29.7 %collective-permute-start.11 = (bf16[32,768]{1,0:T(8,128)(2,1)S(1)}, bf16[32,768]{1,0:T(8,128)(2,1)S(1)}, u32[]{:S(2)}, u32[]{:S(2)}) collective-permute-start(bf16[32,768]{1,0:T(8,128)(2,1)S(1)} %copy-done.6), channel_id=1, source_target_pairs={{0,2},{1,3},{2,0},{3,1},{4,6},{5,7},{6,4},{7,5},{8,10},{9,11},{10,... | collective-permute-start | bytes 147464 | tf_op jit(solution)/shard_map/ppermute | solution.py:564
  150.3 30.7 %collective-permute-start.12 = (bf16[32,768]{1,0:T(8,128)(2,1)S(1)}, bf16[32,768]{1,0:T(8,128)(2,1)S(1)}, u32[]{:S(2)}, u32[]{:S(2)}) collective-permute-start(bf16[32,768]{1,0:T(8,128)(2,1)S(1)} %copy-done.5), channel_id=1, source_target_pairs={{0,3},{1,2},{2,1},{3,0},{4,7},{5,6},{6,5},{7,4},{8,11},{9,10},{10,... | collective-permute-start | bytes 147464 | tf_op jit(solution)/shard_map/ppermute | solution.py:564
  197.2 9.2 %collective-permute-start.14 = (bf16[8,8,56,384]{3,2,1,0:T(8,128)(2,1)S(1)}, bf16[8,8,56,384]{3,2,1,0:T(8,128)(2,1)}, u32[]{:S(2)}, u32[]{:S(2)}) collective-permute-start(bf16[8,8,56,384]{3,2,1,0:T(8,128)(2,1)S(1)} %shard_map.204.refs_1_.in_ref), channel_id=1, source_target_pairs={{0,8},{8,0},{1,9},{9,1},{2,10},{10,2},{3,11},{11,3},{4,12},{12,4},... | collective-permute-start | bytes 8257544 | tf_op jit(solution)/shard_map/ppermute | solution.py:548
  197.5 20.5 %all-to-all-start.6 = ((bf16[8,64,768]{2,1,0:T(8,128)(2,1)}), bf16[8,64,768]{2,1,0:T(8,128)(2,1)S(1)}, u32[]{:S(2)}, u32[]{:S(2)}) async-start(bf16[8,64,768]{2,1,0:T(8,128)(2,1)} %shard_map.205), calls=%async_computation.6 | async-start | bytes 1572864 | tf_op jit(solution)/shard_map/all_to_all | solution.py:544
Sparse Core Ops, SparseCore 0:
  46.0 34.1 all-gather.2
  148.9 45.5 all-gather.4

commit v9 on v8

--- a/solution.py
+++ b/solution.py
@@ -132,10 +132,10 @@
         copy.wait()
 
 
-def weight_copies(w_ref, w_buf, w_sem):
+def weight_copies(w_ref, w_buf, w_sem, parts=(1, 2, 0)):
     group = group_index()
     copies = []
-    for slot, part in enumerate((1, 2, 0)):
+    for slot, part in enumerate(parts):
         column = pl.multiple_of(part * D + (group // 2) * 384, 128)
         copy = pltpu.make_async_copy(w_ref.at[:, pl.ds(column, 384)], w_buf.at[slot], w_sem.at[slot])
         copy.start()
@@ -143,8 +143,13 @@
     return copies
 
 
+def own_heads(full):
+    odd = (group_index() % 2) == 1
+    return jnp.where(odd, full[:, 192:], full[:, :192]).astype(BF)
+
+
 def project_kernel(
-    tok_ref, gain_ref, shift_ref, w_ref, kv_ref, q_ref, normed_ref,
+    tok_ref, gain_ref, shift_ref, w_ref, kv_ref, normed_ref,
     x_buf, w_buf, kv_buf, gain_buf, shift_buf, x_sem, w_sem, kv_sem, gain_sem, shift_sem,
 ):
     copy_x = pltpu.make_async_copy(tok_ref.at[lax.axis_index(MICRO)], x_buf, x_sem)
@@ -153,22 +158,23 @@
     copy_gain.start()
     copy_shift = pltpu.make_async_copy(shift_ref, shift_buf, shift_sem)
     copy_shift.start()
-    copies = weight_copies(w_ref, w_buf, w_sem)
+    copies = weight_copies(w_ref, w_buf, w_sem, (1, 2))
     wait_all([copy_x, copy_gain, copy_shift])
     unit, _ = normalized(x_buf[...].astype(F32))
     normed = (unit * gain_buf[...].reshape(1, D) + shift_buf[...].reshape(1, D)).astype(BF)
-    odd = (group_index() % 2) == 1
-
-    def part(slot):
+    normed_ref[...] = normed
+    parts = []
+    for slot in range(2):
         copies[slot].wait()
-        full = mm(normed, w_buf[slot])
-        return jnp.where(odd, full[:, 192:], full[:, :192]).astype(BF)
-
-    kv_buf[...] = jnp.concatenate([part(0), part(1)], axis=1)
-    sends = send_copies(kv_buf, kv_ref, range(8), kv_sem)
-    normed_ref[...] = normed
-    q_ref[...] = jnp.concatenate([part(2), jnp.zeros((TOK, HD), BF)], axis=1)
-    wait_all(sends)
+        parts.append(own_heads(mm(normed, w_buf[slot])))
+    kv_buf[...] = jnp.concatenate(parts, axis=1)
+    wait_all(send_copies(kv_buf, kv_ref, range(8), kv_sem))
+
+
+def query_kernel(normed_ref, w_ref, q_ref, w_buf, w_sem):
+    weight_copies(w_ref, w_buf, w_sem, (0,))[0].wait()
+    part = own_heads(mm(normed_ref[...], w_buf[0]))
+    q_ref[...] = jnp.concatenate([part, jnp.zeros((TOK, HD), BF)], axis=1)
 
 
 def attend_kernel(scene_ref, q_ref, same_ref, other_ref, out_ref, buf, sem):
@@ -209,7 +215,7 @@
 def forward_kernel(
     mixed_ref, tok_ref, og_ref, wo_ref, gain_ref, shift_ref, up_ref, down_ref,
     out_ref, middle_ref, normed_ref, act_ref, gpre_ref,
-    tok_buf, og_buf, up_buf, down_buf, grad_buf, branch_buf, in_sem, sem,
+    tok_buf, og_buf, up_buf, down_buf, grad_buf, branch_buf, middle_buf, in_sem, sem,
 ):
     loads = [
         pltpu.make_async_copy(ref, buf, in_sem.at[index])
@@ -225,7 +231,8 @@
         total = total + mm(rows, wo_ref[group])
     loads[0].wait()
     total = total + tok_buf[...].reshape(2 * TOK, D).astype(F32)
-    middle_ref[...] = total.reshape(8, BLK, D)
+    middle_buf[...] = total.reshape(8, BLK, D)
+    middle_ref[...] = middle_buf[lax.axis_index(MICRO) * 4 + group_index()]
     unit, _ = normalized(total)
     normed = (unit * gain_ref[...].reshape(1, D) + shift_ref[...].reshape(1, D)).astype(BF)
     normed_ref[...] = normed
@@ -292,7 +299,7 @@
     group = group_index()
     block = pl.ds(pl.multiple_of(group * BLK, BLK), BLK)
     loads = [
-        pltpu.make_async_copy(middle_ref.at[micro * 4 + group], middle_buf, in_sem.at[0]),
+        pltpu.make_async_copy(middle_ref, middle_buf, in_sem.at[0]),
         pltpu.make_async_copy(og_ref.at[micro, block], og_buf, in_sem.at[1]),
         pltpu.make_async_copy(mixed_ref.at[pl.ds(micro * 4, 4), block], mixed_buf, in_sem.at[2]),
         pltpu.make_async_copy(tok_ref.at[micro, block], x_ref, x_sem),
@@ -568,17 +575,25 @@
     tokens, scene_of_block, ln1_gain, ln1_shift, w_qkv, w_out, ln2_gain, ln2_shift, w_up, w_down, out_grad
 ):
     w_out_pad = jnp.pad(w_out.reshape(4, 192, D), ((0, 0), (HD, 0), (0, 0)))
-    kv_send, query, normed = call(
+    kv_send, normed = call(
         project_kernel,
-        [((8, TOK, 384), BF, "H"), ((TOK, 256), BF, "L"), ((TOK, D), BF, "L")],
+        [((8, TOK, 384), BF, "H"), ((TOK, D), BF, "L")],
         [(tokens, "H"), (ln1_gain, "H"), (ln1_shift, "H"), (w_qkv, "H")],
         10**9,
         [
-            pltpu.VMEM((TOK, D), BF), pltpu.VMEM((3, D, 384), BF), pltpu.VMEM((TOK, 384), BF),
-            pltpu.VMEM((D,), F32), pltpu.VMEM((D,), F32), DMA, DMA((3,)), DMA((8,)), DMA, DMA,
-        ],
+            pltpu.VMEM((TOK, D), BF), pltpu.VMEM((2, D, 384), BF), pltpu.VMEM((TOK, 384), BF),
+            pltpu.VMEM((D,), F32), pltpu.VMEM((D,), F32), DMA, DMA((2,)), DMA((8,)), DMA, DMA,
+        ],
+    )
+    (query,) = call(
+        query_kernel,
+        [((TOK, 256), BF, "L")],
+        [(normed, "L"), (w_qkv, "H")],
+        10**8,
+        [pltpu.VMEM((1, D, 384), BF), DMA((1,))],
     )
     kv_same = exchange(kv_send, CHIP)
+    kv_same = after(kv_same, pin(query))
     kv_other = swap(kv_same)
     (mixed_send,) = call(
         attend_kernel,
@@ -592,7 +607,7 @@
     ff_send, middle, normed2, act, grad_pre = call(
         forward_kernel,
         [
-            ((8, 2 * BLK, D), BF, "H"), ((8, BLK, D), F32, "L"), ((2 * TOK, D), BF, "V"),
+            ((8, 2 * BLK, D), BF, "H"), ((BLK, D), F32, "L"), ((2 * TOK, D), BF, "V"),
             ((2 * TOK, FFL), BF, "V"), ((2 * TOK, FFL), BF, "V"),
         ],
         [
@@ -602,7 +617,8 @@
         4 * 10**9,
         [
             pltpu.VMEM((2, TOK, D), BF), pltpu.VMEM((2, TOK, D), BF), pltpu.VMEM((D, FFL), BF),
-            pltpu.VMEM((FFL, D), BF), pltpu.VMEM((8, BLK, D), BF), pltpu.VMEM((8, BLK, D), BF), DMA((4,)), DMA((2,)),
+            pltpu.VMEM((FFL, D), BF), pltpu.VMEM((8, BLK, D), BF), pltpu.VMEM((8, BLK, D), BF),
+            pltpu.VMEM((8, BLK, D), F32), DMA((4,)), DMA((2,)),
         ],
     )
     ff_sums = exchange(ff_send, NARROW)
@@ -640,6 +656,7 @@
             pltpu.VMEM((4, BLK, 256), BF), DMA, DMA((3,)), DMA((8,)),
         ],
     )
+    send = after(pin(send), pin(low))
     (ff_part,) = call(
         pair_kernel, [((48, D), BF, "L")], [(keep, "L"), (flip(send, "xl", 2, 1), "V")], 10**7
     )
@@ -678,7 +695,7 @@
         [pltpu.VMEM((TOK, D), BF), pltpu.VMEM((TOK, D), F32), pltpu.VMEM((3, D, 384), BF), DMA, DMA((3,))],
     )
     parts = [flip(value, GROUP, 4, k + 1) for k, value in enumerate(sends)]
-    weight_parts = after(weight_parts, pin(sums))
+    weight_parts = after(weight_parts, pin(sums), *parts, pin(ff_all))
     (weight_total,) = call(
         sum_kernel,
         [((8, 8, 56, 384), BF, "H")],

time: 227 us -> 220 us (0.969)
  blocking collectives: 18 us -> 0 us
  starting transfers between devices: 58.9 us -> 68.9 us
  Pallas kernels: 49.5 us -> 52.3 us
    all_to_all x6 -> x7, waiting for transfers between devices: 23.2 us -> 53.4 us  [exchange(): return lax.all_to_all(value, axes, 0, 0, tiled=True)]
    ppermute x10, waiting for transfers between devices: 41.9 us -> 21.7 us  [flip(): lax.ppermute(value, axes, [(index, index ^ bits) for index in range(count)])]
    all_to_all x1 -> x0, blocking collectives: 18 us -> none  [exchange(): return lax.all_to_all(value, axes, 0, 0, tiled=True)]
    all_gather x1, waiting for transfers between devices: 11.2 us -> 0.01 us  [shards(): ff_all = lax.all_gather(ff_part, WIDE, axis=0, tiled=True)]
    all_to_all x6 -> x7, starting transfers between devices: 37.5 us -> 42.9 us  [exchange(): return lax.all_to_all(value, axes, 0, 0, tiled=True)]
    ppermute x5, starting transfers between devices: 7.79 us -> 13.2 us  [swap(): return lax.ppermute(value, CORE, [(0, 1), (1, 0)])]
    pallas_call x17 -> x18, Pallas kernels: 49.5 us -> 52.3 us  [call(): pl.pallas_call(kernel, out_shape=[(pltpu.HBM if place in 'HL' else jax.Sh...]
  transfers between devices with their start and end apart: 23 -> 24, of which waited for: 16 -> 15; matrix products, arithmetic and copies ran while one was open for 1% -> 1% of each run, Pallas kernels for 15% -> 19%
where the time goes in v9:
time: 220 us; the launch traced here: 219 us
  waiting for transfers between devices  80.9 us (37%)
  starting transfers between devices  68.9 us (31%)
  Pallas kernels  52.3 us (24%)
  between operations  14.3 us (6%)
  local copies, waits for them, and re-layouts  2.26 us (1%)
    all_to_all x7, waiting for transfers between devices, exchange(): return lax.all_to_all(value, axes, 0, 0, tiled=True)  53.4 us
    pallas_call x18, Pallas kernels, call(): pl.pallas_call(kernel, out_shape=[(pltpu.HBM if place in 'HL' else jax.Sh...  52.3 us
    all_to_all x7, starting transfers between devices, exchange(): return lax.all_to_all(value, axes, 0, 0, tiled=True)  42.9 us
    ppermute x10, waiting for transfers between devices, flip(): lax.ppermute(value, axes, [(index, index ^ bits) for index in range(count)])  21.7 us
    ppermute x5, starting transfers between devices, swap(): return lax.ppermute(value, CORE, [(0, 1), (1, 0)])  13.2 us
    ppermute x10, starting transfers between devices, flip(): lax.ppermute(value, axes, [(index, index ^ bits) for index in range(count)])  12.7 us
    ppermute x5, waiting for transfers between devices, swap(): return lax.ppermute(value, CORE, [(0, 1), (1, 0)])  5.09 us
  transfers between devices with their start and end apart: 24, of which 15 were waited for; matrix products, arithmetic and copies ran while one was open for 1% of the time, Pallas kernels for 19%

profile of v9, /device:TPU:1, one launch (start us, length us, event | category | flops | bytes accessed | tf_op | source)
XLA Modules:
  0.0 218.6 jit_solution(14589207717706968535)
XLA Ops:
  7.2 3.7 %shard_map.186 = (bf16[8,128,384]{2,1,0:T(8,128)(2,1)}, bf16[128,768]{1,0:T(8,128)(2,1)}) custom-call(bf16[2,128,768]{2,1,0:T(8,128)(2,1)} %tok_ref.7, f32[768]{0:T(1024)} %gain_ref.7, f32[768]{0:T(1024)} %shift_ref.2, bf16[768,2304]{1,0:T(8,128)(2,1)} %w_ref.5), custom_call_target="tpu_custom_call" | custom-call | flops 1000 | bytes 1000 | tf_op jit(solution)/shard_map/pallas_call | solution.py:106
  10.9 6.0 %all-to-all-start = ((bf16[8,128,384]{2,1,0:T(8,128)(2,1)}), bf16[8,128,384]{2,1,0:T(8,128)(2,1)S(1)}, u32[]{:S(2)}, u32[]{:S(2)}) async-start(bf16[8,128,384]{2,1,0:T(8,128)(2,1)} %get-tuple-element.52), calls=%async_computation | async-start | bytes 1572864 | tf_op jit(solution)/shard_map/all_to_all | solution.py:551
  16.8 3.0 %shard_map.187.refs_1_.refs_0_.q_ref = bf16[128,256]{1,0:T(8,128)(2,1)} custom-call(bf16[128,768]{1,0:T(8,128)(2,1)} %get-tuple-element.53.normed_ref, bf16[768,2304]{1,0:T(8,128)(2,1)} %w_ref.5), custom_call_target="tpu_custom_call" | custom-call | flops 1000 | bytes 1000 | tf_op jit(solution)/shard_map/pallas_call | solution.py:106
  19.9 8.6 %all-to-all-done.refs_0_ = bf16[8,128,384]{2,1,0:T(8,128)(2,1)S(1)} async-done(((bf16[8,128,384]{2,1,0:T(8,128)(2,1)}), bf16[8,128,384]{2,1,0:T(8,128)(2,1)S(1)}, u32[]{:S(2)}, u32[]{:S(2)}) %all-to-all-start) | async-done | bytes 786464 | tf_op jit(solution)/shard_map/all_to_all | solution.py:551
  32.6 2.6 %shard_map.190 = bf16[8,128,256]{2,1,0:T(8,128)(2,1)} custom-call(s32[2,32]{1,0:T(2,128)S(1)} %copy-done.3, bf16[128,256]{1,0:T(8,128)(2,1)} %shard_map.187.refs_1_.refs_0_.q_ref, bf16[8,128,384]{2,1,0:T(8,128)(2,1)S(1)} %shard_map.188.refs_1_.same_ref.kvs_ref, bf16[8,128,384]{2,1,0:T(8,128)(2,1)S(1)} %collective-permute-done.other_ref.kvo_ref), custom_call_target="tpu_custom_call" | custom-call | flops 1000 | bytes 1000 | tf_op jit(solution)/shard_map/pallas_call | solution.py:106
  36.8 7.2 %all-to-all-start.1 = ((bf16[8,128,256]{2,1,0:T(8,128)(2,1)}), bf16[8,128,256]{2,1,0:T(8,128)(2,1)S(1)}, u32[]{:S(2)}, u32[]{:S(2)}) async-start(bf16[8,128,256]{2,1,0:T(8,128)(2,1)} %shard_map.190), calls=%async_computation.1 | async-start | bytes 1048576 | tf_op jit(solution)/shard_map/all_to_all | solution.py:551
  45.4 10.0 %all-to-all-done.1.mixed_ref = bf16[8,128,256]{2,1,0:T(8,128)(2,1)S(1)} async-done(((bf16[8,128,256]{2,1,0:T(8,128)(2,1)}), bf16[8,128,256]{2,1,0:T(8,128)(2,1)S(1)}, u32[]{:S(2)}, u32[]{:S(2)}) %all-to-all-start.1) | async-done | bytes 524320 | tf_op jit(solution)/shard_map/all_to_all | solution.py:551
  55.5 5.5 %shard_map.191 = (bf16[8,64,768]{2,1,0:T(8,128)(2,1)}, f32[32,768]{1,0:T(8,128)}, bf16[256,768]{1,0:T(8,128)(2,1)S(1)}, bf16[256,384]{1,0:T(8,128)(2,1)S(1)}, bf16[256,384]{1,0:T(8,128)(2,1)S(1)}) custom-call(bf16[8,128,256]{2,1,0:T(8,128)(2,1)S(1)} %all-to-all-done.1.mixed_ref, bf16[2,128,768]{2,1,0:T(8,128)(2,1)} %tok_ref.7, bf16[2,128,768]{2,1,0:T(8,128)(2,1)} %og_ref.5, ...), custom_call_target="tpu_custom_call" | custom-call | flops 1000 | bytes 1000 | tf_op jit(solution)/shard_map/pallas_call | solution.py:106
  60.9 2.8 %shard_map.192 = (bf16[8,48,768]{2,1,0:T(8,128)(2,1)S(1)}, bf16[8,48,768]{2,1,0:T(8,128)(2,1)}) custom-call(bf16[256,768]{1,0:T(8,128)(2,1)S(1)} %get-tuple-element.55.normed_ref, bf16[256,384]{1,0:T(8,128)(2,1)S(1)} %get-tuple-element.56.act_ref, bf16[256,384]{1,0:T(8,128)(2,1)S(1)} %get-tuple-element.57.gpre_ref, bf16[2,128,768]{2,1,0:T(8,128)(2,1)} %og_ref.5), custom_call_target="tpu_custom_call" | custom-call | flops 1000 | bytes 1000 | tf_op jit(solution)/shard_map/pallas_call | solution.py:106
  65.5 3.5 %all-to-all-start.2 = ((bf16[8,64,768]{2,1,0:T(8,128)(2,1)}), bf16[8,64,768]{2,1,0:T(8,128)(2,1)S(1)}, u32[]{:S(2)}, u32[]{:S(2)}) async-start(bf16[8,64,768]{2,1,0:T(8,128)(2,1)} %get-tuple-element.54), calls=%async_computation.2 | async-start | bytes 1572864 | tf_op jit(solution)/shard_map/all_to_all | solution.py:551
  71.0 2.6 %collective-permute-start.3 = (bf16[2,48,768]{2,1,0:T(8,128)(2,1)}, bf16[2,48,768]{2,1,0:T(8,128)(2,1)S(1)}, u32[]{:S(2)}, u32[]{:S(2)}) collective-permute-start(bf16[2,48,768]{2,1,0:T(8,128)(2,1)} %get-tuple-element.62), channel_id=1, source_target_pairs={{0,64},{32,96},{64,0},{96,32},{1,65},{33,97},{65,1},{97,33},{2,66}... | collective-permute-start | bytes 442376 | tf_op jit(solution)/shard_map/ppermute | solution.py:571
  76.7 4.3 %collective-permute-done.3.refs_2_ = bf16[2,48,768]{2,1,0:T(8,128)(2,1)S(1)} collective-permute-done((bf16[2,48,768]{2,1,0:T(8,128)(2,1)}, bf16[2,48,768]{2,1,0:T(8,128)(2,1)S(1)}, u32[]{:S(2)}, u32[]{:S(2)}) %collective-permute-start.3) | collective-permute-done | bytes 147488 | tf_op jit(solution)/shard_map/ppermute | solution.py:571
  81.1 2.4 %collective-permute-done.4.refs_3_ = bf16[2,48,768]{2,1,0:T(8,128)(2,1)S(1)} collective-permute-done((bf16[2,48,768]{2,1,0:T(8,128)(2,1)}, bf16[2,48,768]{2,1,0:T(8,128)(2,1)S(1)}, u32[]{:S(2)}, u32[]{:S(2)}) %collective-permute-start.4) | collective-permute-done | bytes 147488 | tf_op jit(solution)/shard_map/ppermute | solution.py:571
  85.2 4.1 %shard_map.196 = (bf16[8,4,32,256]{3,2,1,0:T(8,128)(2,1)}, bf16[32,768]{1,0:T(8,128)(2,1)}, f32[32,768]{1,0:T(8,128)}, bf16[32,768]{1,0:T(8,128)(2,1)}, f32[8,768]{1,0:T(8,128)}, /*index=5*/bf16[32,768]{1,0:T(8,128)(2,1)}) custom-call(bf16[8,64,768]{2,1,0:T(8,128)(2,1)S(1)} %shard_map.195.sums_ref, f32[32,768]{1,0:T(8,128)} %get-tuple-element.65.middle_ref, ...), custom_call_target="tpu_custom_call" | custom-call | flops 1000 | bytes 1000 | tf_op jit(solution)/shard_map/pallas_call | solution.py:106
  89.6 3.1 %collective-permute-done.8.two_ref = bf16[48,768]{1,0:T(8,128)(2,1)S(1)} collective-permute-done((bf16[48,768]{1,0:T(8,128)(2,1)}, bf16[48,768]{1,0:T(8,128)(2,1)S(1)}, u32[]{:S(2)}, u32[]{:S(2)}) %collective-permute-start.8) | collective-permute-done | bytes 73760 | tf_op jit(solution)/shard_map/ppermute | solution.py:571
  94.3 6.1 %all-to-all-start.3 = ((bf16[32,32,256]{2,1,0:T(8,128)(2,1)}), bf16[32,32,256]{2,1,0:T(8,128)(2,1)S(1)}, u32[]{:S(2)}, u32[]{:S(2)}) async-start(bf16[32,32,256]{2,1,0:T(8,128)(2,1)} %bitcast.11), calls=%async_computation.3 | async-start | bytes 1048576 | tf_op jit(solution)/shard_map/all_to_all | solution.py:551
  100.4 3.7 %collective-permute-start.7 = (bf16[32,768]{1,0:T(8,128)(2,1)}, bf16[32,768]{1,0:T(8,128)(2,1)S(1)}, u32[]{:S(2)}, u32[]{:S(2)}) collective-permute-start(bf16[32,768]{1,0:T(8,128)(2,1)} %get-tuple-element.67.refs_1_.low0_ref), channel_id=1, source_target_pairs={{0,3},{1,2},{2,1},{3,0},{4,7},{5,6},{6,5},{7,4},{8,11},{9,10},{10,... | collective-permute-start | bytes 147464 | tf_op jit(solution)/shard_map/ppermute | solution.py:571
  104.6 4.7 %collective-permute-done.7.refs_3_.low3_ref = bf16[32,768]{1,0:T(8,128)(2,1)S(1)} collective-permute-done((bf16[32,768]{1,0:T(8,128)(2,1)}, bf16[32,768]{1,0:T(8,128)(2,1)S(1)}, u32[]{:S(2)}, u32[]{:S(2)}) %collective-permute-start.7) | collective-permute-done | bytes 49184 | tf_op jit(solution)/shard_map/ppermute | solution.py:571
  110.4 4.3 %collective-permute-start.9 = (bf16[8,128,256]{2,1,0:T(8,128)(2,1)S(1)}, bf16[8,128,256]{2,1,0:T(8,128)(2,1)S(1)}, u32[]{:S(2)}, u32[]{:S(2)}) collective-permute-start(bf16[8,128,256]{2,1,0:T(8,128)(2,1)S(1)} %shard_map.199.gs_ref), channel_id=1, source_target_pairs={{0,8},{8,0},{1,9},{9,1},{2,10},{10,2},{3,11},{11,3},{4,12},{12,4},... | collective-permute-start | bytes 1572872 | tf_op jit(solution)/shard_map/ppermute | solution.py:555
  116.2 4.8 %shard_map.200 = (bf16[128,640]{1,0:T(8,128)(2,1)}, bf16[16,48,384]{2,1,0:T(8,128)(2,1)S(1)}, bf16[16,48,384]{2,1,0:T(8,128)(2,1)S(1)}) custom-call(s32[2,32]{1,0:T(2,128)S(1)} %copy-done.3, bf16[8,128,384]{2,1,0:T(8,128)(2,1)} %copy-done, bf16[8,128,384]{2,1,0:T(8,128)(2,1)} %copy-done.2, bf16[8,2,128,256]{3,2,1,0:T(8,128)(2,1)} %bitcast.10, ...), custom_call_target="tpu_custom_call" | custom-call | flops 1000 | bytes 1000 | tf_op jit(solution)/shard_map/pallas_call | solution.py:106
  124.1 7.3 %all-to-all-start.4 = ((bf16[16,48,384]{2,1,0:T(8,128)(2,1)}), bf16[16,48,384]{2,1,0:T(8,128)(2,1)S(1)}, u32[]{:S(2)}, u32[]{:S(2)}) async-start(bf16[16,48,384]{2,1,0:T(8,128)(2,1)} %shard_map.203), calls=%async_computation.4 | async-start | bytes 1179648 | tf_op jit(solution)/shard_map/all_to_all | solution.py:551
  131.4 4.1 %shard_map.201 = (f32[32,768]{1,0:T(8,128)}, bf16[32,768]{1,0:T(8,128)(2,1)}, bf16[32,768]{1,0:T(8,128)(2,1)}, bf16[32,768]{1,0:T(8,128)(2,1)}, f32[8,768]{1,0:T(8,128)}) custom-call(bf16[128,640]{1,0:T(8,128)(2,1)} %get-tuple-element.69.gqkv_ref, bf16[2,128,768]{2,1,0:T(8,128)(2,1)} %tok_ref.7, bf16[768,2304]{1,0:T(8,128)(2,1)} %w_ref.5, ...), custom_call_target="tpu_custom_call" | custom-call | flops 1000 | bytes 1000 | tf_op jit(solution)/shard_map/pallas_call | solution.py:106
  141.4 2.6 %collective-permute-done.11.two_ref.refs_3_ = bf16[32,768]{1,0:T(8,128)(2,1)S(1)} collective-permute-done((bf16[32,768]{1,0:T(8,128)(2,1)}, bf16[32,768]{1,0:T(8,128)(2,1)S(1)}, u32[]{:S(2)}, u32[]{:S(2)}) %collective-permute-start.11) | collective-permute-done | bytes 49184 | tf_op jit(solution)/shard_map/ppermute | solution.py:571
  144.0 2.4 %shard_map.205 = bf16[8,8,56,384]{3,2,1,0:T(8,128)(2,1)} custom-call(bf16[16,48,384]{2,1,0:T(8,128)(2,1)S(1)} %shard_map.204.in_ref, f32[8,768]{1,0:T(8,128)} %get-tuple-element.80.refs_1_.vec_ref), custom_call_target="tpu_custom_call" | custom-call | flops 1000 | bytes 1000 | tf_op jit(solution)/shard_map/pallas_call | solution.py:106
  146.4 9.0 %all-to-all-start.5 = ((bf16[64,56,384]{2,1,0:T(8,128)(2,1)}), bf16[64,56,384]{2,1,0:T(8,128)(2,1)S(1)}, u32[]{:S(2)}, u32[]{:S(2)}) async-start(bf16[64,56,384]{2,1,0:T(8,128)(2,1)} %bitcast.8), calls=%async_computation.5 | async-start | bytes 5505024 | tf_op jit(solution)/shard_map/all_to_all | solution.py:551
  157.6 2.8 %shard_map.206 = (f32[768,384]{1,0:T(8,128)}, f32[384,768]{1,0:T(8,128)}) custom-call(bf16[768,768]{1,0:T(8,128)(2,1)} %all-gather.5.cloned.1.call-done.refs_5_.in_ref), custom_call_target="tpu_custom_call" | custom-call | flops 1000 | bytes 1000 | tf_op jit(solution)/shard_map/pallas_call | solution.py:106
  160.3 27.8 %all-to-all-done.5 = bf16[64,56,384]{2,1,0:T(8,128)(2,1)S(1)} async-done(((bf16[64,56,384]{2,1,0:T(8,128)(2,1)}), bf16[64,56,384]{2,1,0:T(8,128)(2,1)S(1)}, u32[]{:S(2)}, u32[]{:S(2)}) %all-to-all-start.5) | async-done | bytes 2752544 | tf_op jit(solution)/shard_map/all_to_all | solution.py:551
  188.1 4.5 %collective-permute-start.14 = (bf16[8,8,56,384]{3,2,1,0:T(8,128)(2,1)S(1)}, bf16[8,8,56,384]{3,2,1,0:T(8,128)(2,1)}, u32[]{:S(2)}, u32[]{:S(2)}) collective-permute-start(bf16[8,8,56,384]{3,2,1,0:T(8,128)(2,1)S(1)} %shard_map.207.refs_1_.in_ref), channel_id=1, source_target_pairs={{0,8},{8,0},{1,9},{9,1},{2,10},{10,2},{3,11},{11,3},{4,12},{12,4},... | collective-permute-start | bytes 8257544 | tf_op jit(solution)/shard_map/ppermute | solution.py:555
  192.7 3.8 %all-to-all-start.6 = ((bf16[8,64,768]{2,1,0:T(8,128)(2,1)}), bf16[8,64,768]{2,1,0:T(8,128)(2,1)S(1)}, u32[]{:S(2)}, u32[]{:S(2)}) async-start(bf16[8,64,768]{2,1,0:T(8,128)(2,1)} %shard_map.208), calls=%async_computation.6 | async-start | bytes 1572864 | tf_op jit(solution)/shard_map/all_to_all | solution.py:551
  196.5 2.4 %shard_map.209 = (f32[768,2304]{1,0:T(8,128)}, f32[768,768]{1,0:T(8,128)}, f32[8,384]{1,0:T(8,128)S(1)}) custom-call(bf16[8,8,56,384]{3,2,1,0:T(8,128)(2,1)S(1)} %shard_map.207.refs_1_.in_ref), custom_call_target="tpu_custom_call" | custom-call | flops 1000 | bytes 1000 | tf_op jit(solution)/shard_map/pallas_call | solution.py:106
  198.9 4.8 %shard_map.210 = (f32[768,2304]{1,0:T(8,128)}, f32[768,768]{1,0:T(8,128)}, f32[768]{0:T(1024)}, f32[768]{0:T(1024)}, f32[768]{0:T(1024)}, /*index=5*/f32[768]{0:T(1024)}) custom-call(bf16[8,8,56,384]{3,2,1,0:T(8,128)(2,1)} %collective-permute-done.14.in_ref, f32[8,384]{1,0:T(8,128)S(1)} %get-tuple-element.83.refs_0_, ...), custom_call_target="tpu_custom_call", output_to_operand_aliasing={{0}: (2, {}), {1}: (3, {})} | custom-call | flops 1000 | bytes 1000 | tf_op jit(solution)/shard_map/pallas_call | solution.py:106
  203.8 6.9 %all-to-all-done.6.in_ref = bf16[8,64,768]{2,1,0:T(8,128)(2,1)S(1)} async-done(((bf16[8,64,768]{2,1,0:T(8,128)(2,1)}), bf16[8,64,768]{2,1,0:T(8,128)(2,1)S(1)}, u32[]{:S(2)}, u32[]{:S(2)}) %all-to-all-start.6) | async-done | bytes 786464 | tf_op jit(solution)/shard_map/all_to_all | solution.py:551
  (53 shorter events, 32.7 us)
Async XLA Ops:
  10.9 17.6 %all-to-all-start = ((bf16[8,128,384]{2,1,0:T(8,128)(2,1)}), bf16[8,128,384]{2,1,0:T(8,128)(2,1)S(1)}, u32[]{:S(2)}, u32[]{:S(2)}) async-start(bf16[8,128,384]{2,1,0:T(8,128)(2,1)} %get-tuple-element.52), calls=%async_computation | async-start | bytes 1572864 | tf_op jit(solution)/shard_map/all_to_all | solution.py:551
  16.8 15.8 %copy-start.3 = (s32[2,32]{1,0:T(2,128)S(1)}, s32[2,32]{1,0:T(2,128)}, u32[]{:S(2)}) copy-start(s32[2,32]{1,0:T(2,128)} %scene_ref.3) | copy-start | bytes 772
  28.5 16.9 %copy-start = (bf16[8,128,384]{2,1,0:T(8,128)(2,1)}, bf16[8,128,384]{2,1,0:T(8,128)(2,1)S(1)}, u32[]{:S(2)}) copy-start(bf16[8,128,384]{2,1,0:T(8,128)(2,1)S(1)} %shard_map.188.refs_1_.same_ref.kvs_ref) | copy-start | bytes 2359300
  28.5 4.1 %collective-permute-start = (bf16[8,128,384]{2,1,0:T(8,128)(2,1)S(1)}, bf16[8,128,384]{2,1,0:T(8,128)(2,1)S(1)}, u32[]{:S(2)}, u32[]{:S(2)}) collective-permute-start(bf16[8,128,384]{2,1,0:T(8,128)(2,1)S(1)} %shard_map.188.refs_1_.same_ref.kvs_ref), channel_id=1, source_target_pairs={{0,8},{8,0},{1,9},{9,1},{2,10},{10,2},{3,11},{11,3},{4,12},{12,4},... | collective-permute-start | bytes 2359304 | tf_op jit(solution)/shard_map/ppermute | solution.py:555
  35.2 0.9 copy-start.2
  36.1 78.6 %all-gather.3.cloned.1.call-start = ((), (), s32[]{:S(2)}) async-start(), calls=%async_computation.7 | async-start | bytes 1114112 | tf_op jit(solution)/shard_map/all_gather | solution.py:606
  36.8 18.6 %all-to-all-start.1 = ((bf16[8,128,256]{2,1,0:T(8,128)(2,1)}), bf16[8,128,256]{2,1,0:T(8,128)(2,1)S(1)}, u32[]{:S(2)}, u32[]{:S(2)}) async-start(bf16[8,128,256]{2,1,0:T(8,128)(2,1)} %shard_map.190), calls=%async_computation.1 | async-start | bytes 1048576 | tf_op jit(solution)/shard_map/all_to_all | solution.py:551
  55.4 10.1 %copy-start.1 = (bf16[8,128,256]{2,1,0:T(8,128)(2,1)}, bf16[8,128,256]{2,1,0:T(8,128)(2,1)S(1)}, u32[]{:S(2)}) copy-start(bf16[8,128,256]{2,1,0:T(8,128)(2,1)S(1)} %all-to-all-done.1.mixed_ref) | copy-start | bytes 1572868
  63.7 5.4 %collective-permute-start.1 = (bf16[8,48,768]{2,1,0:T(8,128)(2,1)}, bf16[8,48,768]{2,1,0:T(8,128)(2,1)}, u32[]{:S(2)}, u32[]{:S(2)}) collective-permute-start(bf16[8,48,768]{2,1,0:T(8,128)(2,1)} %get-tuple-element.59), channel_id=1, source_target_pairs={{0,8},{8,0},{1,9},{9,1},{2,10},{10,2},{3,11},{11,3},{4,12},{12,4},... | collective-permute-start | bytes 1769480 | tf_op jit(solution)/shard_map/ppermute | solution.py:555
  65.5 19.6 %all-to-all-start.2 = ((bf16[8,64,768]{2,1,0:T(8,128)(2,1)}), bf16[8,64,768]{2,1,0:T(8,128)(2,1)S(1)}, u32[]{:S(2)}, u32[]{:S(2)}) async-start(bf16[8,64,768]{2,1,0:T(8,128)(2,1)} %get-tuple-element.54), calls=%async_computation.2 | async-start | bytes 1572864 | tf_op jit(solution)/shard_map/all_to_all | solution.py:551
  69.1 74.9 %all-gather.5.cloned.1.call-start = ((), (), s32[]{:S(2)}) async-start(), calls=%async_computation.8 | async-start | bytes 1253376 | tf_op jit(solution)/shard_map/all_gather | solution.py:663
  71.0 5.7 %collective-permute-start.2 = (bf16[2,48,768]{2,1,0:T(8,128)(2,1)}, bf16[2,48,768]{2,1,0:T(8,128)(2,1)S(1)}, u32[]{:S(2)}, u32[]{:S(2)}) collective-permute-start(bf16[2,48,768]{2,1,0:T(8,128)(2,1)} %get-tuple-element.61), channel_id=1, source_target_pairs={{0,32},{32,0},{64,96},{96,64},{1,33},{33,1},{65,97},{97,65},{2,34}... | collective-permute-start | bytes 442376 | tf_op jit(solution)/shard_map/ppermute | solution.py:571
  71.0 10.0 %collective-permute-start.3 = (bf16[2,48,768]{2,1,0:T(8,128)(2,1)}, bf16[2,48,768]{2,1,0:T(8,128)(2,1)S(1)}, u32[]{:S(2)}, u32[]{:S(2)}) collective-permute-start(bf16[2,48,768]{2,1,0:T(8,128)(2,1)} %get-tuple-element.62), channel_id=1, source_target_pairs={{0,64},{32,96},{64,0},{96,32},{1,65},{33,97},{65,1},{97,33},{2,66}... | collective-permute-start | bytes 442376 | tf_op jit(solution)/shard_map/ppermute | solution.py:571
  73.7 9.9 %collective-permute-start.4 = (bf16[2,48,768]{2,1,0:T(8,128)(2,1)}, bf16[2,48,768]{2,1,0:T(8,128)(2,1)S(1)}, u32[]{:S(2)}, u32[]{:S(2)}) collective-permute-start(bf16[2,48,768]{2,1,0:T(8,128)(2,1)} %get-tuple-element.63), channel_id=1, source_target_pairs={{0,96},{32,64},{64,32},{96,0},{1,97},{33,65},{65,33},{97,1},{2,98}... | collective-permute-start | bytes 442376 | tf_op jit(solution)/shard_map/ppermute | solution.py:571
  89.2 3.5 %collective-permute-start.8 = (bf16[48,768]{1,0:T(8,128)(2,1)}, bf16[48,768]{1,0:T(8,128)(2,1)S(1)}, u32[]{:S(2)}, u32[]{:S(2)}) collective-permute-start(bf16[48,768]{1,0:T(8,128)(2,1)} %shard_map.197), channel_id=1, source_target_pairs={{0,16},{16,0},{1,17},{17,1},{2,18},{18,2},{3,19},{19,3},{4,20},{20... | collective-permute-start | bytes 221192 | tf_op jit(solution)/shard_map/ppermute | solution.py:571
  94.3 16.1 %all-to-all-start.3 = ((bf16[32,32,256]{2,1,0:T(8,128)(2,1)}), bf16[32,32,256]{2,1,0:T(8,128)(2,1)S(1)}, u32[]{:S(2)}, u32[]{:S(2)}) async-start(bf16[32,32,256]{2,1,0:T(8,128)(2,1)} %bitcast.11), calls=%async_computation.3 | async-start | bytes 1048576 | tf_op jit(solution)/shard_map/all_to_all | solution.py:551
  100.4 8.9 %collective-permute-start.7 = (bf16[32,768]{1,0:T(8,128)(2,1)}, bf16[32,768]{1,0:T(8,128)(2,1)S(1)}, u32[]{:S(2)}, u32[]{:S(2)}) collective-permute-start(bf16[32,768]{1,0:T(8,128)(2,1)} %get-tuple-element.67.refs_1_.low0_ref), channel_id=1, source_target_pairs={{0,3},{1,2},{2,1},{3,0},{4,7},{5,6},{6,5},{7,4},{8,11},{9,10},{10,... | collective-permute-start | bytes 147464 | tf_op jit(solution)/shard_map/ppermute | solution.py:571
  104.1 6.3 %collective-permute-start.6 = (bf16[32,768]{1,0:T(8,128)(2,1)}, bf16[32,768]{1,0:T(8,128)(2,1)S(1)}, u32[]{:S(2)}, u32[]{:S(2)}) collective-permute-start(bf16[32,768]{1,0:T(8,128)(2,1)} %get-tuple-element.67.refs_1_.low0_ref), channel_id=1, source_target_pairs={{0,2},{1,3},{2,0},{3,1},{4,6},{5,7},{6,4},{7,5},{8,10},{9,11},{10,... | collective-permute-start | bytes 147464 | tf_op jit(solution)/shard_map/ppermute | solution.py:571
  104.4 6.0 %collective-permute-start.5 = (bf16[32,768]{1,0:T(8,128)(2,1)}, bf16[32,768]{1,0:T(8,128)(2,1)S(1)}, u32[]{:S(2)}, u32[]{:S(2)}) collective-permute-start(bf16[32,768]{1,0:T(8,128)(2,1)} %get-tuple-element.67.refs_1_.low0_ref), channel_id=1, source_target_pairs={{0,1},{1,0},{2,3},{3,2},{4,5},{5,4},{6,7},{7,6},{8,9},{9,8},{10,11... | collective-permute-start | bytes 147464 | tf_op jit(solution)/shard_map/ppermute | solution.py:571
  110.4 5.8 %collective-permute-start.9 = (bf16[8,128,256]{2,1,0:T(8,128)(2,1)S(1)}, bf16[8,128,256]{2,1,0:T(8,128)(2,1)S(1)}, u32[]{:S(2)}, u32[]{:S(2)}) collective-permute-start(bf16[8,128,256]{2,1,0:T(8,128)(2,1)S(1)} %shard_map.199.gs_ref), channel_id=1, source_target_pairs={{0,8},{8,0},{1,9},{9,1},{2,10},{10,2},{3,11},{11,3},{4,12},{12,4},... | collective-permute-start | bytes 1572872 | tf_op jit(solution)/shard_map/ppermute | solution.py:555
  121.0 2.1 collective-permute-start.13
  124.1 19.8 %all-to-all-start.4 = ((bf16[16,48,384]{2,1,0:T(8,128)(2,1)}), bf16[16,48,384]{2,1,0:T(8,128)(2,1)S(1)}, u32[]{:S(2)}, u32[]{:S(2)}) async-start(bf16[16,48,384]{2,1,0:T(8,128)(2,1)} %shard_map.203), calls=%async_computation.4 | async-start | bytes 1179648 | tf_op jit(solution)/shard_map/all_to_all | solution.py:551
  135.5 5.8 %collective-permute-start.10 = (bf16[32,768]{1,0:T(8,128)(2,1)}, bf16[32,768]{1,0:T(8,128)(2,1)S(1)}, u32[]{:S(2)}, u32[]{:S(2)}) collective-permute-start(bf16[32,768]{1,0:T(8,128)(2,1)} %get-tuple-element.72), channel_id=1, source_target_pairs={{0,1},{1,0},{2,3},{3,2},{4,5},{5,4},{6,7},{7,6},{8,9},{9,8},{10,11... | collective-permute-start | bytes 147464 | tf_op jit(solution)/shard_map/ppermute | solution.py:571
  137.6 6.3 %collective-permute-start.11 = (bf16[32,768]{1,0:T(8,128)(2,1)}, bf16[32,768]{1,0:T(8,128)(2,1)S(1)}, u32[]{:S(2)}, u32[]{:S(2)}) collective-permute-start(bf16[32,768]{1,0:T(8,128)(2,1)} %get-tuple-element.73), channel_id=1, source_target_pairs={{0,2},{1,3},{2,0},{3,1},{4,6},{5,7},{6,4},{7,5},{8,10},{9,11},{10,... | collective-permute-start | bytes 147464 | tf_op jit(solution)/shard_map/ppermute | solution.py:571
  137.7 6.2 %collective-permute-start.12 = (bf16[32,768]{1,0:T(8,128)(2,1)}, bf16[32,768]{1,0:T(8,128)(2,1)S(1)}, u32[]{:S(2)}, u32[]{:S(2)}) collective-permute-start(bf16[32,768]{1,0:T(8,128)(2,1)} %get-tuple-element.74), channel_id=1, source_target_pairs={{0,3},{1,2},{2,1},{3,0},{4,7},{5,6},{6,5},{7,4},{8,11},{9,10},{10,... | collective-permute-start | bytes 147464 | tf_op jit(solution)/shard_map/ppermute | solution.py:571
  146.4 41.7 %all-to-all-start.5 = ((bf16[64,56,384]{2,1,0:T(8,128)(2,1)}), bf16[64,56,384]{2,1,0:T(8,128)(2,1)S(1)}, u32[]{:S(2)}, u32[]{:S(2)}) async-start(bf16[64,56,384]{2,1,0:T(8,128)(2,1)} %bitcast.8), calls=%async_computation.5 | async-start | bytes 5505024 | tf_op jit(solution)/shard_map/all_to_all | solution.py:551
  188.1 10.8 %collective-permute-start.14 = (bf16[8,8,56,384]{3,2,1,0:T(8,128)(2,1)S(1)}, bf16[8,8,56,384]{3,2,1,0:T(8,128)(2,1)}, u32[]{:S(2)}, u32[]{:S(2)}) collective-permute-start(bf16[8,8,56,384]{3,2,1,0:T(8,128)(2,1)S(1)} %shard_map.207.refs_1_.in_ref), channel_id=1, source_target_pairs={{0,8},{8,0},{1,9},{9,1},{2,10},{10,2},{3,11},{11,3},{4,12},{12,4},... | collective-permute-start | bytes 8257544 | tf_op jit(solution)/shard_map/ppermute | solution.py:555
  192.7 18.1 %all-to-all-start.6 = ((bf16[8,64,768]{2,1,0:T(8,128)(2,1)}), bf16[8,64,768]{2,1,0:T(8,128)(2,1)S(1)}, u32[]{:S(2)}, u32[]{:S(2)}) async-start(bf16[8,64,768]{2,1,0:T(8,128)(2,1)} %shard_map.208), calls=%async_computation.6 | async-start | bytes 1572864 | tf_op jit(solution)/shard_map/all_to_all | solution.py:551
Sparse Core Ops, SparseCore 0:
  38.6 33.1 all-gather.2
  94.4 35.2 all-gather.4

commit v10 on v9

--- a/solution.py
+++ b/solution.py
@@ -112,7 +112,7 @@
         out_specs=[pl.BlockSpec(memory_space=places[place]) for _, _, place in outs],
         scratch_shapes=list(scratch),
         input_output_aliases=aliases or {},
-        cost_estimate=pl.CostEstimate(flops=1000, bytes_accessed=1000, transcendentals=0),
+        cost_estimate=pl.CostEstimate(flops=cost, bytes_accessed=1000, transcendentals=0),
         compiler_params=pltpu.CompilerParams(vmem_limit_bytes=vmem * 2**20),
     )(*[pin(value) if place in "HL" else value for value, place in ins])
 
@@ -177,7 +177,9 @@
     q_ref[...] = jnp.concatenate([part, jnp.zeros((TOK, HD), BF)], axis=1)
 
 
-def attend_kernel(scene_ref, q_ref, same_ref, other_ref, out_ref, buf, sem):
+def attend_kernel(scene_ref, q_ref, same_ref, other_ref, out_ref, buf, q_buf, sem, q_sem):
+    load = pltpu.make_async_copy(q_ref, q_buf, q_sem)
+    load.start()
     first, big = span(scene_ref)
 
     def run(count):
@@ -185,7 +187,8 @@
         keys = jnp.concatenate(
             [ref[pl.ds(first, count)].reshape(rows, 384) for ref in (same_ref, other_ref)], axis=0
         )
-        query = q_ref[...]
+        load.wait()
+        query = q_buf[...]
         q0, q1 = halves(query[:, :128])
         blocks = [keys[:, :128], keys[:, 128:256], keys[:, 256:]]
         mixed = []
@@ -215,12 +218,15 @@
 def forward_kernel(
     mixed_ref, tok_ref, og_ref, wo_ref, gain_ref, shift_ref, up_ref, down_ref,
     out_ref, middle_ref, normed_ref, act_ref, gpre_ref,
-    tok_buf, og_buf, up_buf, down_buf, grad_buf, branch_buf, middle_buf, in_sem, sem,
+    tok_buf, og_buf, up_buf, down_buf, gain_buf, shift_buf, grad_buf, branch_buf, middle_buf, in_sem, sem,
 ):
     loads = [
         pltpu.make_async_copy(ref, buf, in_sem.at[index])
         for index, (ref, buf) in enumerate(
-            ((tok_ref, tok_buf), (up_ref, up_buf), (og_ref, og_buf), (down_ref, down_buf))
+            (
+                (tok_ref, tok_buf), (up_ref, up_buf), (og_ref, og_buf), (down_ref, down_buf), (gain_ref, gain_buf),
+                (shift_ref, shift_buf),
+            )
         )
     ]
     for load in loads:
@@ -232,9 +238,13 @@
     loads[0].wait()
     total = total + tok_buf[...].reshape(2 * TOK, D).astype(F32)
     middle_buf[...] = total.reshape(8, BLK, D)
-    middle_ref[...] = middle_buf[lax.axis_index(MICRO) * 4 + group_index()]
+    third = pltpu.make_async_copy(
+        middle_buf.at[lax.axis_index(MICRO) * 4 + group_index()], middle_ref, sem.at[2]
+    )
+    third.start()
     unit, _ = normalized(total)
-    normed = (unit * gain_ref[...].reshape(1, D) + shift_ref[...].reshape(1, D)).astype(BF)
+    wait_all(loads[4:])
+    normed = (unit * gain_buf[...].reshape(1, D) + shift_buf[...].reshape(1, D)).astype(BF)
     normed_ref[...] = normed
     loads[1].wait()
     pre = mm(normed, up_buf[...])
@@ -253,8 +263,7 @@
     branch_buf[...] = mm(act, down_buf[...]).astype(BF).reshape(8, BLK, D)
     second = pltpu.make_async_copy(branch_buf, out_ref.at[:, pl.ds(0, BLK)], sem.at[1])
     second.start()
-    first.wait()
-    second.wait()
+    wait_all([first, second, third])
 
 
 def ff_grads_kernel(normed_ref, act_ref, gpre_ref, og_ref, keep_ref, send_ref, up_buf, down_buf):
@@ -292,8 +301,9 @@
 
 
 def middle_kernel(
-    sums_ref, middle_ref, og_ref, tok_ref, mixed_ref, wo_ref, gain_ref,
-    out_ref, low_ref, grad_ref, result_ref, vec_ref, x_ref, buf, middle_buf, og_buf, mixed_buf, x_sem, in_sem, sem,
+    sums_ref, middle_ref, og_ref, mixed_ref, wo_ref, gain_ref,
+    out_ref, low_ref, grad_ref, result_ref, vec_ref,
+    buf, middle_buf, og_buf, mixed_buf, gain_buf, low_buf, grad_buf, result_buf, vec_buf, in_sem, sem, rest_sem,
 ):
     micro = lax.axis_index(MICRO)
     group = group_index()
@@ -302,7 +312,7 @@
         pltpu.make_async_copy(middle_ref, middle_buf, in_sem.at[0]),
         pltpu.make_async_copy(og_ref.at[micro, block], og_buf, in_sem.at[1]),
         pltpu.make_async_copy(mixed_ref.at[pl.ds(micro * 4, 4), block], mixed_buf, in_sem.at[2]),
-        pltpu.make_async_copy(tok_ref.at[micro, block], x_ref, x_sem),
+        pltpu.make_async_copy(gain_ref, gain_buf, in_sem.at[3]),
     ]
     for load in loads:
         load.start()
@@ -313,8 +323,22 @@
     wait_all(loads)
     middle = middle_buf[...]
     unit, inverse = normalized(middle)
-    grad_mid = og_buf[...].astype(F32) + norm_back(grad, unit, inverse, gain_ref[...].reshape(1, D))
+    grad_mid = og_buf[...].astype(F32) + norm_back(grad, unit, inverse, gain_buf[...].reshape(1, D))
     low = grad_mid.astype(BF)
+    low_buf[...] = low
+    grad_buf[...] = grad_mid
+    result_buf[...] = (middle + branch).astype(BF)
+    gain_grad = jnp.sum(grad * unit, axis=0, keepdims=True)
+    shift_grad = jnp.sum(grad, axis=0, keepdims=True)
+    vec_buf[...] = jnp.concatenate([gain_grad, shift_grad, jnp.zeros((6, D), F32)], axis=0)
+    stores = [
+        pltpu.make_async_copy(source, target, rest_sem.at[index])
+        for index, (source, target) in enumerate(
+            ((low_buf, low_ref), (grad_buf, grad_ref), (result_buf, result_ref), (vec_buf, vec_ref))
+        )
+    ]
+    for store in stores:
+        store.start()
     lane = lax.broadcasted_iota(jnp.int32, (BLK, 256), 1)
     for head_group in range(4):
         mixed = mixed_buf[head_group].astype(F32)
@@ -327,23 +351,26 @@
         stats = put_columns(256, BLK, 9, columns)
         buf[head_group] = jnp.where(lane < 9, mixed, jnp.where(lane < HD, stats, back)).astype(BF)
     sends = send_copies(buf, out_ref, range(8), sem)
-    low_ref[...] = low
-    grad_ref[...] = grad_mid
-    result_ref[...] = (middle + branch).astype(BF)
-    gain_grad = jnp.sum(grad * unit, axis=0, keepdims=True)
-    shift_grad = jnp.sum(grad, axis=0, keepdims=True)
-    vec_ref[...] = jnp.concatenate([gain_grad, shift_grad, jnp.zeros((6, D), F32)], axis=0)
+    wait_all(stores)
     wait_all(sends)
 
 
 def attend_back_kernel(
-    scene_ref, kvs_ref, kvo_ref, q_ref, gs_ref, go_ref, normed_ref, mixed_ref, low0_ref, low1_ref, low2_ref, low3_ref,
-    gqkv_ref, keep_ref, send_ref, kv_buf, q_buf, grad_buf, mixed_buf, kv_sem, q_sem, mixed_sem,
+    scene_ref, kvs_ref, kvo_ref, q_ref, gs_ref, go_ref, normed_ref, mixed_ref, low_ref, low1_ref, low2_ref, low3_ref,
+    gqkv_ref, keep_ref, send_ref,
+    kv_buf, q_buf, gqkv_buf, grad_buf, mixed_buf, normed_buf, low_buf, kv_sem, q_sem, in_sem, out_sem,
 ):
     first, big = span(scene_ref)
     chip = chip_index()
     core = lax.axis_index(CORE)
     group = group_index()
+    index = lax.axis_index(MICRO) * 4 + group
+    first_loads = [
+        pltpu.make_async_copy(source, target, in_sem.at[slot])
+        for slot, (source, target) in enumerate(
+            ((normed_ref, normed_buf), (mixed_ref.at[index], mixed_buf), (low_ref, low_buf))
+        )
+    ]
     scale = HD**-0.5
 
     def run(count):
@@ -357,7 +384,7 @@
             )
             for slot, which in enumerate((core, 1 - core))
         ]
-        for load in loads:
+        for load in loads + first_loads:
             load.start()
 
         def cut(value):
@@ -395,15 +422,12 @@
             dv.append(mm(probs.astype(BF), grad[gb]))
             dk.append(mm((probs * gap).astype(BF), query[qb]) * scale)
         tail = dq[2]
-        gqkv_ref[...] = jnp.concatenate(
+        gqkv_buf[...] = jnp.concatenate(
             [join(dk[0], dk[1]), join(dk[2], dv[0]), join(dv[1], dv[2]), join(dq[0], dq[1]),
              join(tail, jnp.zeros_like(tail))],
             axis=1,
         ).astype(BF)
 
-    index = lax.axis_index(MICRO) * 4 + group
-    load_mixed = pltpu.make_async_copy(mixed_ref.at[index], mixed_buf, mixed_sem)
-    load_mixed.start()
 
     @pl.when(big)
     def _():
@@ -413,9 +437,12 @@
     def _():
         run(1)
 
-    grad_buf[...] = mm_tn(normed_ref[...], gqkv_ref[...])
-    load_mixed.wait()
-    low = jnp.concatenate([ref[...] for ref in (low0_ref, low1_ref, low2_ref, low3_ref)], axis=0)
+    store = pltpu.make_async_copy(gqkv_buf, gqkv_ref, out_sem)
+    store.start()
+    wait_all(first_loads)
+
+    grad_buf[...] = mm_tn(normed_buf[...], gqkv_buf[...])
+    low = jnp.concatenate([ref[...] for ref in (low_buf, low1_ref, low2_ref, low3_ref)], axis=0)
     mixed = jnp.concatenate(
         [mixed_buf[pl.ds(pl.multiple_of((group ^ k) * BLK, BLK), BLK)] for k in range(4)], axis=0
     )
@@ -431,6 +458,8 @@
             ref[2 * tile + 1] = jnp.concatenate(
                 [rows[:, 384:576], jnp.where(owner == 1, pieces[1], pieces[0])], axis=1
             ).astype(BF)
+    store.wait()
+
 
 def normed_grad_kernel(
     gqkv_ref, tok_ref, w_ref, vec_ref, own_ref, one_ref, two_ref, three_ref, sums_ref,
@@ -468,11 +497,14 @@
     copy.wait()
 
 
-def sum_kernel(in_ref, vec_ref, out_ref, buf, sem):
+def sum_kernel(in_ref, vec_ref, out_ref, buf, vec_buf, sem, vec_sem):
+    load = pltpu.make_async_copy(vec_ref, vec_buf, vec_sem)
+    load.start()
     total = in_ref[0].astype(F32)
     for index in range(1, 16):
         total = total + in_ref[index].astype(F32)
-    vectors = vec_ref[...][:4]
+    load.wait()
+    vectors = vec_buf[...][:4]
     block = jnp.concatenate([total, vectors[:, :384], vectors[:, 384:]], axis=0).astype(BF)
     for index in range(8):
         buf[index] = block
@@ -528,12 +560,16 @@
 
 
 def input_kernel(
-    own_ref, one_ref, two_ref, three_ref, x_ref, gain_ref, grad_ref, result_ref, out_ref, buf, sem
+    own_ref, one_ref, two_ref, three_ref, tok_ref, gain_ref, grad_ref, result_ref, out_ref, buf, x_buf, sem, x_sem
 ):
+    start = pl.multiple_of(group_index() * BLK, BLK)
+    load = pltpu.make_async_copy(tok_ref.at[lax.axis_index(MICRO), pl.ds(start, BLK)], x_buf, x_sem)
+    load.start()
+    load.wait()
     total = own_ref[...]
     for ref in (one_ref, two_ref, three_ref):
         total = total + ref[...].astype(F32)
-    unit, inverse = normalized(x_ref[...].astype(F32))
+    unit, inverse = normalized(x_buf[...].astype(F32))
     grad = grad_ref[...] + norm_back(total, unit, inverse, gain_ref[...].reshape(1, D))
     buf[:BLK] = grad.astype(BF)
     buf[BLK:] = result_ref[...]
@@ -579,7 +615,7 @@
         project_kernel,
         [((8, TOK, 384), BF, "H"), ((TOK, D), BF, "L")],
         [(tokens, "H"), (ln1_gain, "H"), (ln1_shift, "H"), (w_qkv, "H")],
-        10**9,
+        1000,
         [
             pltpu.VMEM((TOK, D), BF), pltpu.VMEM((2, D, 384), BF), pltpu.VMEM((TOK, 384), BF),
             pltpu.VMEM((D,), F32), pltpu.VMEM((D,), F32), DMA, DMA((2,)), DMA((8,)), DMA, DMA,
@@ -589,7 +625,7 @@
         query_kernel,
         [((TOK, 256), BF, "L")],
         [(normed, "L"), (w_qkv, "H")],
-        10**8,
+        1000,
         [pltpu.VMEM((1, D, 384), BF), DMA((1,))],
     )
     kv_same = exchange(kv_send, CHIP)
@@ -598,27 +634,27 @@
     (mixed_send,) = call(
         attend_kernel,
         [((8, TOK, 256), BF, "H")],
-        [(scene_of_block, "S"), (query, "L"), (kv_same, "V"), (kv_other, "V")],
-        2 * 10**9,
-        [pltpu.VMEM((TOK, 256), BF), DMA((8,))],
+        [(scene_of_block, "S"), (query, "H"), (kv_same, "V"), (kv_other, "V")],
+        1000,
+        [pltpu.VMEM((TOK, 256), BF), pltpu.VMEM((TOK, 256), BF), DMA((8,)), DMA],
     )
     mixed = exchange(mixed_send, NARROW)
     queries = lax.all_gather(after(pin(query), kv_same), WIDE, axis=0, tiled=True).reshape(8, 2, TOK, 256)
     ff_send, middle, normed2, act, grad_pre = call(
         forward_kernel,
         [
-            ((8, 2 * BLK, D), BF, "H"), ((BLK, D), F32, "L"), ((2 * TOK, D), BF, "V"),
+            ((8, 2 * BLK, D), BF, "H"), ((BLK, D), F32, "H"), ((2 * TOK, D), BF, "V"),
             ((2 * TOK, FFL), BF, "V"), ((2 * TOK, FFL), BF, "V"),
         ],
         [
-            (mixed, "V"), (tokens, "H"), (out_grad, "H"), (w_out_pad, "V"), (ln2_gain, "L"), (ln2_shift, "L"),
+            (mixed, "V"), (tokens, "H"), (out_grad, "H"), (w_out_pad, "V"), (ln2_gain, "H"), (ln2_shift, "H"),
             (w_up, "H"), (w_down, "H"),
         ],
-        4 * 10**9,
+        1000,
         [
             pltpu.VMEM((2, TOK, D), BF), pltpu.VMEM((2, TOK, D), BF), pltpu.VMEM((D, FFL), BF),
-            pltpu.VMEM((FFL, D), BF), pltpu.VMEM((8, BLK, D), BF), pltpu.VMEM((8, BLK, D), BF),
-            pltpu.VMEM((8, BLK, D), F32), DMA((4,)), DMA((2,)),
+            pltpu.VMEM((FFL, D), BF), pltpu.VMEM((D,), F32), pltpu.VMEM((D,), F32), pltpu.VMEM((8, BLK, D), BF),
+            pltpu.VMEM((8, BLK, D), BF), pltpu.VMEM((8, BLK, D), F32), DMA((6,)), DMA((3,)),
         ],
     )
     ff_sums = exchange(ff_send, NARROW)
@@ -626,39 +662,39 @@
         ff_grads_kernel,
         [((8, 48, D), BF, "V")] * 2,
         [(normed2, "V"), (act, "V"), (grad_pre, "V"), (out_grad, "L")],
-        2 * 10**9,
+        1000,
         [pltpu.VMEM((D, FFL), F32), pltpu.VMEM((FFL, D), F32)],
     )
     pieces = call(
-        split_kernel, [((2, 48, D), BF, "L")] * 4, [(keep, "V"), (swap(send), "V")], 10**8
+        split_kernel, [((2, 48, D), BF, "L")] * 4, [(keep, "V"), (swap(send), "V")], 1000
     )
     pieces = [pieces[0]] + [flip(pieces[k], "y", 4, k) for k in (1, 2, 3)]
     keep, send = call(
         halve_kernel,
         [((48, D), BF, "L")] * 2,
         [(pieces[0], "L")] + [(piece, "V") for piece in pieces[1:]],
-        10**8,
+        1000,
     )
     ff_sums = after(ff_sums, pin(keep))
-    grad_send, low, grad_mid, result_part, vec2, x_part = call(
+    grad_send, low, grad_mid, result_part, vec2 = call(
         middle_kernel,
         [
-            ((8, 4, BLK, 256), BF, "H"), ((BLK, D), BF, "L"), ((BLK, D), F32, "L"), ((BLK, D), BF, "L"),
-            ((8, D), F32, "L"), ((BLK, D), BF, "L"),
-        ],
-        [
-            (ff_sums, "V"), (middle, "H"), (out_grad, "H"), (tokens, "H"), (mixed, "H"), (w_out_pad, "V"),
-            (ln2_gain, "L"),
-        ],
-        10**9,
+            ((8, 4, BLK, 256), BF, "H"), ((BLK, D), BF, "H"), ((BLK, D), F32, "H"), ((BLK, D), BF, "H"),
+            ((8, D), F32, "H"),
+        ],
+        [
+            (ff_sums, "V"), (middle, "H"), (out_grad, "H"), (mixed, "H"), (w_out_pad, "V"), (ln2_gain, "H"),
+        ],
+        1000,
         [
             pltpu.VMEM((4, BLK, 256), BF), pltpu.VMEM((BLK, D), F32), pltpu.VMEM((BLK, D), BF),
-            pltpu.VMEM((4, BLK, 256), BF), DMA, DMA((3,)), DMA((8,)),
+            pltpu.VMEM((4, BLK, 256), BF), pltpu.VMEM((D,), F32), pltpu.VMEM((BLK, D), BF), pltpu.VMEM((BLK, D), F32),
+            pltpu.VMEM((BLK, D), BF), pltpu.VMEM((8, D), F32), DMA((4,)), DMA((8,)), DMA((4,)),
         ],
     )
     send = after(pin(send), pin(low))
     (ff_part,) = call(
-        pair_kernel, [((48, D), BF, "L")], [(keep, "L"), (flip(send, "xl", 2, 1), "V")], 10**7
+        pair_kernel, [((48, D), BF, "L")], [(keep, "L"), (flip(send, "xl", 2, 1), "V")], 1000
     )
     ff_all = lax.all_gather(ff_part, WIDE, axis=0, tiled=True)
     grad_same = exchange(grad_send.reshape(32, BLK, 256), (*CHIP, *GROUP)).reshape(8, TOK, 256)
@@ -667,15 +703,16 @@
     grad_other = swap(grad_same)
     gqkv, keep, send = call(
         attend_back_kernel,
-        [((TOK, 640), BF, "L")] + [((16, 48, 384), BF, "V")] * 2,
+        [((TOK, 640), BF, "H")] + [((16, 48, 384), BF, "V")] * 2,
         [
             (scene_of_block, "S"), (kv_same, "H"), (kv_other, "H"), (queries, "H"), (grad_same, "V"), (grad_other, "V"),
-            (normed, "L"), (mixed, "H"), (low, "L"), *[(value, "V") for value in lows],
-        ],
-        8 * 10**9,
-        [
-            pltpu.VMEM((2, 5, TOK, 384), BF), pltpu.VMEM((2, 5, TOK, 256), BF), pltpu.VMEM((D, 640), F32),
-            pltpu.VMEM((TOK, 256), BF), DMA((2,)), DMA((2,)), DMA,
+            (normed, "H"), (mixed, "H"), (low, "H"), *[(value, "V") for value in lows],
+        ],
+        10**9,
+        [
+            pltpu.VMEM((2, 5, TOK, 384), BF), pltpu.VMEM((2, 5, TOK, 256), BF), pltpu.VMEM((TOK, 640), BF),
+            pltpu.VMEM((D, 640), F32), pltpu.VMEM((TOK, 256), BF), pltpu.VMEM((TOK, D), BF), pltpu.VMEM((BLK, D), BF),
+            DMA((2,)), DMA((2,)), DMA((3,)), DMA,
         ],
         vmem=24,
     )
@@ -683,7 +720,7 @@
         add_kernel,
         [((16, 48, 384), BF, "H")],
         [(keep, "V"), (swap(send), "V")],
-        10**8,
+        1000,
         [pltpu.VMEM((16, 48, 384), BF), DMA],
     )
     weight_parts = exchange(weight_send, (*CHIP, MICRO))
@@ -691,7 +728,7 @@
         normed_grad_kernel,
         [((BLK, D), F32, "L")] + [((BLK, D), BF, "L")] * 3 + [((8, D), F32, "L")],
         [(gqkv, "L"), (tokens, "H"), (w_qkv, "H"), (vec2, "L")],
-        10**9,
+        1000,
         [pltpu.VMEM((TOK, D), BF), pltpu.VMEM((TOK, D), F32), pltpu.VMEM((3, D, 384), BF), DMA, DMA((3,))],
     )
     parts = [flip(value, GROUP, 4, k + 1) for k, value in enumerate(sends)]
@@ -699,22 +736,22 @@
     (weight_total,) = call(
         sum_kernel,
         [((8, 8, 56, 384), BF, "H")],
-        [(weight_parts, "V"), (sums, "L")],
-        10**8,
-        [pltpu.VMEM((8, 56, 384), BF), DMA((8,))],
+        [(weight_parts, "V"), (sums, "H")],
+        1000,
+        [pltpu.VMEM((8, 56, 384), BF), pltpu.VMEM((8, D), F32), DMA((8,)), DMA],
     )
     (packed,) = call(
         input_kernel,
         [((8, 2 * BLK, D), BF, "H")],
         [
-            (own, "L"), *[(value, "V") for value in parts], (x_part, "L"), (ln1_gain, "L"), (grad_mid, "L"),
+            (own, "L"), *[(value, "V") for value in parts], (tokens, "H"), (ln1_gain, "L"), (grad_mid, "L"),
             (result_part, "L"),
         ],
-        10**8,
-        [pltpu.VMEM((2 * BLK, D), BF), DMA((8,))],
+        1000,
+        [pltpu.VMEM((2 * BLK, D), BF), pltpu.VMEM((BLK, D), BF), DMA((8,)), DMA],
     )
     up_grad, down_grad = call(
-        spread_ff_kernel, [((D, FFL), F32, "L"), ((FFL, D), F32, "L")], [(ff_all, "L")], 10**7
+        spread_ff_kernel, [((D, FFL), F32, "L"), ((FFL, D), F32, "L")], [(ff_all, "L")], 1000
     )
     weight_same = exchange(weight_total.reshape(64, 56, 384), (*CHIP, *NARROW)).reshape(8, 8, 56, 384)
     weight_same = after(weight_same, pin(packed), pin(up_grad), pin(down_grad))
@@ -728,19 +765,19 @@
         functools.partial(spread_kernel, False),
         grads + [((8, 384), F32, "V")],
         [(weight_same, "V")],
-        10**8,
+        1000,
         scratch,
     )
     qkv_grad, out_proj_grad, *vectors = call(
         functools.partial(spread_kernel, True),
         grads + [((D,), F32, "L")] * 4,
         [(weight_other, "V"), (half[2], "V"), (half[0], "H"), (half[1], "H")],
-        10**8,
+        1000,
         scratch,
         aliases={2: 0, 3: 1},
     )
     input_grad, result = call(
-        unpack_kernel, [((2, TOK, D), F32, "L"), ((2, TOK, D), BF, "L")], [(everyone, "V"), (vectors[0], "H")], 10**8
+        unpack_kernel, [((2, TOK, D), F32, "L"), ((2, TOK, D), BF, "L")], [(everyone, "V"), (vectors[0], "H")], 1000
     )
     return (
         result, input_grad, qkv_grad, out_proj_grad, *vectors, up_grad, down_grad

time: 220 us -> 214 us (0.973)
  waiting for transfers between devices: 80.9 us -> 77.4 us
    ppermute x5, starting transfers between devices: 13.2 us -> 10.1 us  [swap(): return lax.ppermute(value, CORE, [(0, 1), (1, 0)])]
    ppermute x10, waiting for transfers between devices: 21.7 us -> 18.9 us  [flip(): lax.ppermute(value, axes, [(index, index ^ bits) for index in range(count)])]
    pallas_call x18, Pallas kernels: 52.3 us -> 50.1 us  [call(): pl.pallas_call(kernel, out_shape=[(pltpu.HBM if place in 'HL' else jax.Sh...]
  transfers between devices with their start and end apart: 24 -> 24, of which waited for: 15 -> 14; matrix products, arithmetic and copies ran while one was open for 1% -> 1% of each run, Pallas kernels for 19% -> 19%
where the time goes in v10:
time: 214 us; the launch traced here: 213 us
  waiting for transfers between devices  77.4 us (36%)
  starting transfers between devices  68.6 us (32%)
  Pallas kernels  50.1 us (23%)
  between operations  14.3 us (7%)
  local copies, waits for them, and re-layouts  2.26 us (1%)
    all_to_all x7, waiting for transfers between devices, exchange(): return lax.all_to_all(value, axes, 0, 0, tiled=True)  52.6 us
    pallas_call x18, Pallas kernels, call(): pl.pallas_call(kernel, out_shape=[(pltpu.HBM if place in 'HL' else jax.Sh...  50.1 us
    all_to_all x7, starting transfers between devices, exchange(): return lax.all_to_all(value, axes, 0, 0, tiled=True)  45 us
    ppermute x10, waiting for transfers between devices, flip(): lax.ppermute(value, axes, [(index, index ^ bits) for index in range(count)])  18.9 us
    ppermute x10, starting transfers between devices, flip(): lax.ppermute(value, axes, [(index, index ^ bits) for index in range(count)])  13.5 us
    ppermute x5, starting transfers between devices, swap(): return lax.ppermute(value, CORE, [(0, 1), (1, 0)])  10.1 us
    ppermute x5, waiting for transfers between devices, swap(): return lax.ppermute(value, CORE, [(0, 1), (1, 0)])  5.11 us
  transfers between devices with their start and end apart: 24, of which 14 were waited for; matrix products, arithmetic and copies ran while one was open for 1% of the time, Pallas kernels for 19%

profile of v10, /device:TPU:1, one launch (start us, length us, event | category | flops | bytes accessed | tf_op | source)
XLA Modules:
  0.0 212.6 jit_solution(14443146687148075199)
XLA Ops:
  7.2 3.7 %shard_map.186 = (bf16[8,128,384]{2,1,0:T(8,128)(2,1)}, bf16[128,768]{1,0:T(8,128)(2,1)}) custom-call(bf16[2,128,768]{2,1,0:T(8,128)(2,1)} %tok_ref.7, f32[768]{0:T(1024)} %gain_ref.7, f32[768]{0:T(1024)} %shift_ref.2, bf16[768,2304]{1,0:T(8,128)(2,1)} %w_ref.5), custom_call_target="tpu_custom_call" | custom-call | flops 1000 | bytes 1000 | tf_op jit(solution)/shard_map/pallas_call | solution.py:106
  10.9 6.0 %all-to-all-start = ((bf16[8,128,384]{2,1,0:T(8,128)(2,1)}), bf16[8,128,384]{2,1,0:T(8,128)(2,1)S(1)}, u32[]{:S(2)}, u32[]{:S(2)}) async-start(bf16[8,128,384]{2,1,0:T(8,128)(2,1)} %get-tuple-element.51), calls=%async_computation | async-start | bytes 1572864 | tf_op jit(solution)/shard_map/all_to_all | solution.py:587
  16.9 3.0 %shard_map.187.refs_1_.refs_0_.q_ref = bf16[128,256]{1,0:T(8,128)(2,1)} custom-call(bf16[128,768]{1,0:T(8,128)(2,1)} %get-tuple-element.52.normed_ref, bf16[768,2304]{1,0:T(8,128)(2,1)} %w_ref.5), custom_call_target="tpu_custom_call" | custom-call | flops 1000 | bytes 1000 | tf_op jit(solution)/shard_map/pallas_call | solution.py:106
  19.9 8.6 %all-to-all-done.refs_0_ = bf16[8,128,384]{2,1,0:T(8,128)(2,1)S(1)} async-done(((bf16[8,128,384]{2,1,0:T(8,128)(2,1)}), bf16[8,128,384]{2,1,0:T(8,128)(2,1)S(1)}, u32[]{:S(2)}, u32[]{:S(2)}) %all-to-all-start) | async-done | bytes 786464 | tf_op jit(solution)/shard_map/all_to_all | solution.py:587
  32.6 3.1 %shard_map.190 = bf16[8,128,256]{2,1,0:T(8,128)(2,1)} custom-call(s32[2,32]{1,0:T(2,128)S(1)} %copy-done.3, bf16[128,256]{1,0:T(8,128)(2,1)} %shard_map.187.refs_1_.refs_0_.q_ref, bf16[8,128,384]{2,1,0:T(8,128)(2,1)S(1)} %shard_map.188.refs_1_.same_ref.kvs_ref, bf16[8,128,384]{2,1,0:T(8,128)(2,1)S(1)} %collective-permute-done.other_ref.kvo_ref), custom_call_target="tpu_custom_call" | custom-call | flops 1000 | bytes 1000 | tf_op jit(solution)/shard_map/pallas_call | solution.py:106
  37.3 7.2 %all-to-all-start.1 = ((bf16[8,128,256]{2,1,0:T(8,128)(2,1)}), bf16[8,128,256]{2,1,0:T(8,128)(2,1)S(1)}, u32[]{:S(2)}, u32[]{:S(2)}) async-start(bf16[8,128,256]{2,1,0:T(8,128)(2,1)} %shard_map.190), calls=%async_computation.1 | async-start | bytes 1048576 | tf_op jit(solution)/shard_map/all_to_all | solution.py:587
  45.9 10.0 %all-to-all-done.1.mixed_ref = bf16[8,128,256]{2,1,0:T(8,128)(2,1)S(1)} async-done(((bf16[8,128,256]{2,1,0:T(8,128)(2,1)}), bf16[8,128,256]{2,1,0:T(8,128)(2,1)S(1)}, u32[]{:S(2)}, u32[]{:S(2)}) %all-to-all-start.1) | async-done | bytes 524320 | tf_op jit(solution)/shard_map/all_to_all | solution.py:587
  56.0 4.1 %shard_map.191 = (bf16[8,64,768]{2,1,0:T(8,128)(2,1)}, f32[32,768]{1,0:T(8,128)}, bf16[256,768]{1,0:T(8,128)(2,1)S(1)}, bf16[256,384]{1,0:T(8,128)(2,1)S(1)}, bf16[256,384]{1,0:T(8,128)(2,1)S(1)}) custom-call(bf16[8,128,256]{2,1,0:T(8,128)(2,1)S(1)} %all-to-all-done.1.mixed_ref, bf16[2,128,768]{2,1,0:T(8,128)(2,1)} %tok_ref.7, bf16[2,128,768]{2,1,0:T(8,128)(2,1)} %og_ref.5, ...), custom_call_target="tpu_custom_call" | custom-call | flops 1000 | bytes 1000 | tf_op jit(solution)/shard_map/pallas_call | solution.py:106
  60.1 2.8 %shard_map.192 = (bf16[8,48,768]{2,1,0:T(8,128)(2,1)S(1)}, bf16[8,48,768]{2,1,0:T(8,128)(2,1)}) custom-call(bf16[256,768]{1,0:T(8,128)(2,1)S(1)} %get-tuple-element.54.normed_ref, bf16[256,384]{1,0:T(8,128)(2,1)S(1)} %get-tuple-element.55.act_ref, bf16[256,384]{1,0:T(8,128)(2,1)S(1)} %get-tuple-element.56.gpre_ref, bf16[2,128,768]{2,1,0:T(8,128)(2,1)} %og_ref.5), custom_call_target="tpu_custom_call" | custom-call | flops 1000 | bytes 1000 | tf_op jit(solution)/shard_map/pallas_call | solution.py:106
  64.6 3.5 %all-to-all-start.2 = ((bf16[8,64,768]{2,1,0:T(8,128)(2,1)}), bf16[8,64,768]{2,1,0:T(8,128)(2,1)S(1)}, u32[]{:S(2)}, u32[]{:S(2)}) async-start(bf16[8,64,768]{2,1,0:T(8,128)(2,1)} %get-tuple-element.53), calls=%async_computation.2 | async-start | bytes 1572864 | tf_op jit(solution)/shard_map/all_to_all | solution.py:587
  71.2 2.8 %collective-permute-start.4 = (bf16[2,48,768]{2,1,0:T(8,128)(2,1)}, bf16[2,48,768]{2,1,0:T(8,128)(2,1)S(1)}, u32[]{:S(2)}, u32[]{:S(2)}) collective-permute-start(bf16[2,48,768]{2,1,0:T(8,128)(2,1)} %get-tuple-element.62), channel_id=1, source_target_pairs={{0,96},{32,64},{64,32},{96,0},{1,97},{33,65},{65,33},{97,1},{2,98}... | collective-permute-start | bytes 442376 | tf_op jit(solution)/shard_map/ppermute | solution.py:607
  75.8 2.9 %collective-permute-done.3.refs_2_ = bf16[2,48,768]{2,1,0:T(8,128)(2,1)S(1)} collective-permute-done((bf16[2,48,768]{2,1,0:T(8,128)(2,1)}, bf16[2,48,768]{2,1,0:T(8,128)(2,1)S(1)}, u32[]{:S(2)}, u32[]{:S(2)}) %collective-permute-start.3) | collective-permute-done | bytes 147488 | tf_op jit(solution)/shard_map/ppermute | solution.py:607
  78.6 2.6 %collective-permute-done.4.refs_3_ = bf16[2,48,768]{2,1,0:T(8,128)(2,1)S(1)} collective-permute-done((bf16[2,48,768]{2,1,0:T(8,128)(2,1)}, bf16[2,48,768]{2,1,0:T(8,128)(2,1)S(1)}, u32[]{:S(2)}, u32[]{:S(2)}) %collective-permute-start.4) | collective-permute-done | bytes 147488 | tf_op jit(solution)/shard_map/ppermute | solution.py:607
  82.8 2.7 %shard_map.196 = (bf16[8,4,32,256]{3,2,1,0:T(8,128)(2,1)}, bf16[32,768]{1,0:T(8,128)(2,1)}, f32[32,768]{1,0:T(8,128)}, bf16[32,768]{1,0:T(8,128)(2,1)}, f32[8,768]{1,0:T(8,128)}) custom-call(bf16[8,64,768]{2,1,0:T(8,128)(2,1)S(1)} %shard_map.195.sums_ref, f32[32,768]{1,0:T(8,128)} %get-tuple-element.64.middle_ref, bf16[2,128,768]{2,1,0:T(8,128)(2,1)} %og_ref.5, ...), custom_call_target="tpu_custom_call" | custom-call | flops 1000 | bytes 1000 | tf_op jit(solution)/shard_map/pallas_call | solution.py:106
  86.7 8.1 %all-to-all-start.3 = ((bf16[32,32,256]{2,1,0:T(8,128)(2,1)}), bf16[32,32,256]{2,1,0:T(8,128)(2,1)S(1)}, u32[]{:S(2)}, u32[]{:S(2)}) async-start(bf16[32,32,256]{2,1,0:T(8,128)(2,1)} %bitcast.11), calls=%async_computation.3 | async-start | bytes 1048576 | tf_op jit(solution)/shard_map/all_to_all | solution.py:587
  96.4 3.7 %collective-permute-start.7 = (bf16[32,768]{1,0:T(8,128)(2,1)}, bf16[32,768]{1,0:T(8,128)(2,1)S(1)}, u32[]{:S(2)}, u32[]{:S(2)}) collective-permute-start(bf16[32,768]{1,0:T(8,128)(2,1)} %get-tuple-element.66.refs_1_.low_ref), channel_id=1, source_target_pairs={{0,3},{1,2},{2,1},{3,0},{4,7},{5,6},{6,5},{7,4},{8,11},{9,10},{10,... | collective-permute-start | bytes 147464 | tf_op jit(solution)/shard_map/ppermute | solution.py:607
  100.7 3.4 %collective-permute-done.7.refs_3_.low3_ref = bf16[32,768]{1,0:T(8,128)(2,1)S(1)} collective-permute-done((bf16[32,768]{1,0:T(8,128)(2,1)}, bf16[32,768]{1,0:T(8,128)(2,1)S(1)}, u32[]{:S(2)}, u32[]{:S(2)}) %collective-permute-start.7) | collective-permute-done | bytes 49184 | tf_op jit(solution)/shard_map/ppermute | solution.py:607
  104.1 3.4 %collective-permute-done.6.refs_2_.low2_ref = bf16[32,768]{1,0:T(8,128)(2,1)S(1)} collective-permute-done((bf16[32,768]{1,0:T(8,128)(2,1)}, bf16[32,768]{1,0:T(8,128)(2,1)S(1)}, u32[]{:S(2)}, u32[]{:S(2)}) %collective-permute-start.6) | collective-permute-done | bytes 49184 | tf_op jit(solution)/shard_map/ppermute | solution.py:607
  110.3 4.1 %shard_map.200 = (bf16[128,640]{1,0:T(8,128)(2,1)}, bf16[16,48,384]{2,1,0:T(8,128)(2,1)S(1)}, bf16[16,48,384]{2,1,0:T(8,128)(2,1)S(1)}) custom-call(s32[2,32]{1,0:T(2,128)S(1)} %copy-done.3, bf16[8,128,384]{2,1,0:T(8,128)(2,1)} %copy-done, bf16[8,128,384]{2,1,0:T(8,128)(2,1)} %copy-done.2, bf16[8,2,128,256]{3,2,1,0:T(8,128)(2,1)} %bitcast.10, ...), custom_call_target="tpu_custom_call" | custom-call | flops 1000000000 | bytes 1000 | tf_op jit(solution)/shard_map/pallas_call | solution.py:106
  117.4 7.7 %all-to-all-start.4 = ((bf16[16,48,384]{2,1,0:T(8,128)(2,1)}), bf16[16,48,384]{2,1,0:T(8,128)(2,1)S(1)}, u32[]{:S(2)}, u32[]{:S(2)}) async-start(bf16[16,48,384]{2,1,0:T(8,128)(2,1)} %shard_map.203), calls=%async_computation.4 | async-start | bytes 1179648 | tf_op jit(solution)/shard_map/all_to_all | solution.py:587
  125.2 4.1 %shard_map.201 = (f32[32,768]{1,0:T(8,128)}, bf16[32,768]{1,0:T(8,128)(2,1)}, bf16[32,768]{1,0:T(8,128)(2,1)}, bf16[32,768]{1,0:T(8,128)(2,1)}, f32[8,768]{1,0:T(8,128)}) custom-call(bf16[128,640]{1,0:T(8,128)(2,1)} %get-tuple-element.68.gqkv_ref, bf16[2,128,768]{2,1,0:T(8,128)(2,1)} %tok_ref.7, bf16[768,2304]{1,0:T(8,128)(2,1)} %w_ref.5, ...), custom_call_target="tpu_custom_call" | custom-call | flops 1000 | bytes 1000 | tf_op jit(solution)/shard_map/pallas_call | solution.py:106
  133.5 2.4 %collective-permute-done.10.one_ref.refs_2_ = bf16[32,768]{1,0:T(8,128)(2,1)S(1)} collective-permute-done((bf16[32,768]{1,0:T(8,128)(2,1)}, bf16[32,768]{1,0:T(8,128)(2,1)S(1)}, u32[]{:S(2)}, u32[]{:S(2)}) %collective-permute-start.10) | collective-permute-done | bytes 49184 | tf_op jit(solution)/shard_map/ppermute | solution.py:607
  138.3 2.4 %shard_map.205 = bf16[8,8,56,384]{3,2,1,0:T(8,128)(2,1)} custom-call(bf16[16,48,384]{2,1,0:T(8,128)(2,1)S(1)} %shard_map.204.in_ref, f32[8,768]{1,0:T(8,128)} %get-tuple-element.78.refs_1_.vec_ref), custom_call_target="tpu_custom_call" | custom-call | flops 1000 | bytes 1000 | tf_op jit(solution)/shard_map/pallas_call | solution.py:106
  140.7 8.7 %all-to-all-start.5 = ((bf16[64,56,384]{2,1,0:T(8,128)(2,1)}), bf16[64,56,384]{2,1,0:T(8,128)(2,1)S(1)}, u32[]{:S(2)}, u32[]{:S(2)}) async-start(bf16[64,56,384]{2,1,0:T(8,128)(2,1)} %bitcast.8), calls=%async_computation.5 | async-start | bytes 5505024 | tf_op jit(solution)/shard_map/all_to_all | solution.py:587
  149.4 3.0 %shard_map.202.refs_1_.refs_0_ = bf16[8,64,768]{2,1,0:T(8,128)(2,1)} custom-call(f32[32,768]{1,0:T(8,128)} %get-tuple-element.70.own_ref, bf16[32,768]{1,0:T(8,128)(2,1)S(1)} %collective-permute-done.10.one_ref.refs_2_, bf16[32,768]{1,0:T(8,128)(2,1)S(1)} %collective-permute-done.11.two_ref.refs_3_, ...), custom_call_target="tpu_custom_call" | custom-call | flops 1000 | bytes 1000 | tf_op jit(solution)/shard_map/pallas_call | solution.py:106
  152.3 2.8 %shard_map.206 = (f32[768,384]{1,0:T(8,128)}, f32[384,768]{1,0:T(8,128)}) custom-call(bf16[768,768]{1,0:T(8,128)(2,1)} %all-gather.5.cloned.1.call-done.refs_5_.in_ref), custom_call_target="tpu_custom_call" | custom-call | flops 1000 | bytes 1000 | tf_op jit(solution)/shard_map/pallas_call | solution.py:106
  155.1 27.0 %all-to-all-done.5 = bf16[64,56,384]{2,1,0:T(8,128)(2,1)S(1)} async-done(((bf16[64,56,384]{2,1,0:T(8,128)(2,1)}), bf16[64,56,384]{2,1,0:T(8,128)(2,1)S(1)}, u32[]{:S(2)}, u32[]{:S(2)}) %all-to-all-start.5) | async-done | bytes 2752544 | tf_op jit(solution)/shard_map/all_to_all | solution.py:587
  182.1 4.5 %collective-permute-start.14 = (bf16[8,8,56,384]{3,2,1,0:T(8,128)(2,1)S(1)}, bf16[8,8,56,384]{3,2,1,0:T(8,128)(2,1)}, u32[]{:S(2)}, u32[]{:S(2)}) collective-permute-start(bf16[8,8,56,384]{3,2,1,0:T(8,128)(2,1)S(1)} %shard_map.207.refs_1_.in_ref), channel_id=1, source_target_pairs={{0,8},{8,0},{1,9},{9,1},{2,10},{10,2},{3,11},{11,3},{4,12},{12,4},... | collective-permute-start | bytes 8257544 | tf_op jit(solution)/shard_map/ppermute | solution.py:591
  186.6 3.8 %all-to-all-start.6 = ((bf16[8,64,768]{2,1,0:T(8,128)(2,1)}), bf16[8,64,768]{2,1,0:T(8,128)(2,1)S(1)}, u32[]{:S(2)}, u32[]{:S(2)}) async-start(bf16[8,64,768]{2,1,0:T(8,128)(2,1)} %shard_map.208), calls=%async_computation.6 | async-start | bytes 1572864 | tf_op jit(solution)/shard_map/all_to_all | solution.py:587
  190.4 2.4 %shard_map.209 = (f32[768,2304]{1,0:T(8,128)}, f32[768,768]{1,0:T(8,128)}, f32[8,384]{1,0:T(8,128)S(1)}) custom-call(bf16[8,8,56,384]{3,2,1,0:T(8,128)(2,1)S(1)} %shard_map.207.refs_1_.in_ref), custom_call_target="tpu_custom_call" | custom-call | flops 1000 | bytes 1000 | tf_op jit(solution)/shard_map/pallas_call | solution.py:106
  192.9 4.8 %shard_map.210 = (f32[768,2304]{1,0:T(8,128)}, f32[768,768]{1,0:T(8,128)}, f32[768]{0:T(1024)}, f32[768]{0:T(1024)}, f32[768]{0:T(1024)}, /*index=5*/f32[768]{0:T(1024)}) custom-call(bf16[8,8,56,384]{3,2,1,0:T(8,128)(2,1)} %collective-permute-done.14.in_ref, f32[8,384]{1,0:T(8,128)S(1)} %get-tuple-element.81.refs_0_, ...), custom_call_target="tpu_custom_call", output_to_operand_aliasing={{0}: (2, {}), {1}: (3, {})} | custom-call | flops 1000 | bytes 1000 | tf_op jit(solution)/shard_map/pallas_call | solution.py:106
  197.7 6.9 %all-to-all-done.6.in_ref = bf16[8,64,768]{2,1,0:T(8,128)(2,1)S(1)} async-done(((bf16[8,64,768]{2,1,0:T(8,128)(2,1)}), bf16[8,64,768]{2,1,0:T(8,128)(2,1)S(1)}, u32[]{:S(2)}, u32[]{:S(2)}) %all-to-all-start.6) | async-done | bytes 786464 | tf_op jit(solution)/shard_map/all_to_all | solution.py:587
  (53 shorter events, 32.0 us)
Async XLA Ops:
  10.9 17.6 %all-to-all-start = ((bf16[8,128,384]{2,1,0:T(8,128)(2,1)}), bf16[8,128,384]{2,1,0:T(8,128)(2,1)S(1)}, u32[]{:S(2)}, u32[]{:S(2)}) async-start(bf16[8,128,384]{2,1,0:T(8,128)(2,1)} %get-tuple-element.51), calls=%async_computation | async-start | bytes 1572864 | tf_op jit(solution)/shard_map/all_to_all | solution.py:587
  16.8 15.8 %copy-start.3 = (s32[2,32]{1,0:T(2,128)S(1)}, s32[2,32]{1,0:T(2,128)}, u32[]{:S(2)}) copy-start(s32[2,32]{1,0:T(2,128)} %scene_ref.3) | copy-start | bytes 772
  28.5 17.4 %copy-start = (bf16[8,128,384]{2,1,0:T(8,128)(2,1)}, bf16[8,128,384]{2,1,0:T(8,128)(2,1)S(1)}, u32[]{:S(2)}) copy-start(bf16[8,128,384]{2,1,0:T(8,128)(2,1)S(1)} %shard_map.188.refs_1_.same_ref.kvs_ref) | copy-start | bytes 2359300
  28.5 4.1 %collective-permute-start = (bf16[8,128,384]{2,1,0:T(8,128)(2,1)S(1)}, bf16[8,128,384]{2,1,0:T(8,128)(2,1)S(1)}, u32[]{:S(2)}, u32[]{:S(2)}) collective-permute-start(bf16[8,128,384]{2,1,0:T(8,128)(2,1)S(1)} %shard_map.188.refs_1_.same_ref.kvs_ref), channel_id=1, source_target_pairs={{0,8},{8,0},{1,9},{9,1},{2,10},{10,2},{3,11},{11,3},{4,12},{12,4},... | collective-permute-start | bytes 2359304 | tf_op jit(solution)/shard_map/ppermute | solution.py:591
  35.7 0.9 copy-start.2
  36.6 72.2 %all-gather.3.cloned.1.call-start = ((), (), s32[]{:S(2)}) async-start(), calls=%async_computation.7 | async-start | bytes 1114112 | tf_op jit(solution)/shard_map/all_gather | solution.py:642
  37.3 18.6 %all-to-all-start.1 = ((bf16[8,128,256]{2,1,0:T(8,128)(2,1)}), bf16[8,128,256]{2,1,0:T(8,128)(2,1)S(1)}, u32[]{:S(2)}, u32[]{:S(2)}) async-start(bf16[8,128,256]{2,1,0:T(8,128)(2,1)} %shard_map.190), calls=%async_computation.1 | async-start | bytes 1048576 | tf_op jit(solution)/shard_map/all_to_all | solution.py:587
  56.0 8.7 %copy-start.1 = (bf16[8,128,256]{2,1,0:T(8,128)(2,1)}, bf16[8,128,256]{2,1,0:T(8,128)(2,1)S(1)}, u32[]{:S(2)}) copy-start(bf16[8,128,256]{2,1,0:T(8,128)(2,1)S(1)} %all-to-all-done.1.mixed_ref) | copy-start | bytes 1572868
  62.9 5.3 %collective-permute-start.1 = (bf16[8,48,768]{2,1,0:T(8,128)(2,1)}, bf16[8,48,768]{2,1,0:T(8,128)(2,1)}, u32[]{:S(2)}, u32[]{:S(2)}) collective-permute-start(bf16[8,48,768]{2,1,0:T(8,128)(2,1)} %get-tuple-element.58), channel_id=1, source_target_pairs={{0,8},{8,0},{1,9},{9,1},{2,10},{10,2},{3,11},{11,3},{4,12},{12,4},... | collective-permute-start | bytes 1769480 | tf_op jit(solution)/shard_map/ppermute | solution.py:591
  64.6 18.2 %all-to-all-start.2 = ((bf16[8,64,768]{2,1,0:T(8,128)(2,1)}), bf16[8,64,768]{2,1,0:T(8,128)(2,1)S(1)}, u32[]{:S(2)}, u32[]{:S(2)}) async-start(bf16[8,64,768]{2,1,0:T(8,128)(2,1)} %get-tuple-element.53), calls=%async_computation.2 | async-start | bytes 1572864 | tf_op jit(solution)/shard_map/all_to_all | solution.py:587
  70.1 5.7 %collective-permute-start.2 = (bf16[2,48,768]{2,1,0:T(8,128)(2,1)}, bf16[2,48,768]{2,1,0:T(8,128)(2,1)S(1)}, u32[]{:S(2)}, u32[]{:S(2)}) collective-permute-start(bf16[2,48,768]{2,1,0:T(8,128)(2,1)} %get-tuple-element.60), channel_id=1, source_target_pairs={{0,32},{32,0},{64,96},{96,64},{1,33},{33,1},{65,97},{97,65},{2,34}... | collective-permute-start | bytes 442376 | tf_op jit(solution)/shard_map/ppermute | solution.py:607
  70.1 8.5 %collective-permute-start.3 = (bf16[2,48,768]{2,1,0:T(8,128)(2,1)}, bf16[2,48,768]{2,1,0:T(8,128)(2,1)S(1)}, u32[]{:S(2)}, u32[]{:S(2)}) collective-permute-start(bf16[2,48,768]{2,1,0:T(8,128)(2,1)} %get-tuple-element.61), channel_id=1, source_target_pairs={{0,64},{32,96},{64,0},{96,32},{1,65},{33,97},{65,1},{97,33},{2,66}... | collective-permute-start | bytes 442376 | tf_op jit(solution)/shard_map/ppermute | solution.py:607
  71.2 10.0 %collective-permute-start.4 = (bf16[2,48,768]{2,1,0:T(8,128)(2,1)}, bf16[2,48,768]{2,1,0:T(8,128)(2,1)S(1)}, u32[]{:S(2)}, u32[]{:S(2)}) collective-permute-start(bf16[2,48,768]{2,1,0:T(8,128)(2,1)} %get-tuple-element.62), channel_id=1, source_target_pairs={{0,96},{32,64},{64,32},{96,0},{1,97},{33,65},{65,33},{97,1},{2,98}... | collective-permute-start | bytes 442376 | tf_op jit(solution)/shard_map/ppermute | solution.py:607
  85.6 9.3 %collective-permute-start.8 = (bf16[48,768]{1,0:T(8,128)(2,1)}, bf16[48,768]{1,0:T(8,128)(2,1)S(1)}, u32[]{:S(2)}, u32[]{:S(2)}) collective-permute-start(bf16[48,768]{1,0:T(8,128)(2,1)} %shard_map.197), channel_id=1, source_target_pairs={{0,16},{16,0},{1,17},{17,1},{2,18},{18,2},{3,19},{19,3},{4,20},{20... | collective-permute-start | bytes 221192 | tf_op jit(solution)/shard_map/ppermute | solution.py:607
  86.7 20.8 %all-to-all-start.3 = ((bf16[32,32,256]{2,1,0:T(8,128)(2,1)}), bf16[32,32,256]{2,1,0:T(8,128)(2,1)S(1)}, u32[]{:S(2)}, u32[]{:S(2)}) async-start(bf16[32,32,256]{2,1,0:T(8,128)(2,1)} %bitcast.11), calls=%async_computation.3 | async-start | bytes 1048576 | tf_op jit(solution)/shard_map/all_to_all | solution.py:587
  94.8 43.4 %all-gather.5.cloned.1.call-start = ((), (), s32[]{:S(2)}) async-start(), calls=%async_computation.8 | async-start | bytes 1253376 | tf_op jit(solution)/shard_map/all_gather | solution.py:699
  96.4 7.6 %collective-permute-start.7 = (bf16[32,768]{1,0:T(8,128)(2,1)}, bf16[32,768]{1,0:T(8,128)(2,1)S(1)}, u32[]{:S(2)}, u32[]{:S(2)}) collective-permute-start(bf16[32,768]{1,0:T(8,128)(2,1)} %get-tuple-element.66.refs_1_.low_ref), channel_id=1, source_target_pairs={{0,3},{1,2},{2,1},{3,0},{4,7},{5,6},{6,5},{7,4},{8,11},{9,10},{10,... | collective-permute-start | bytes 147464 | tf_op jit(solution)/shard_map/ppermute | solution.py:607
  100.1 7.4 %collective-permute-start.6 = (bf16[32,768]{1,0:T(8,128)(2,1)}, bf16[32,768]{1,0:T(8,128)(2,1)S(1)}, u32[]{:S(2)}, u32[]{:S(2)}) collective-permute-start(bf16[32,768]{1,0:T(8,128)(2,1)} %get-tuple-element.66.refs_1_.low_ref), channel_id=1, source_target_pairs={{0,2},{1,3},{2,0},{3,1},{4,6},{5,7},{6,4},{7,5},{8,10},{9,11},{10,... | collective-permute-start | bytes 147464 | tf_op jit(solution)/shard_map/ppermute | solution.py:607
  100.4 7.1 %collective-permute-start.5 = (bf16[32,768]{1,0:T(8,128)(2,1)}, bf16[32,768]{1,0:T(8,128)(2,1)S(1)}, u32[]{:S(2)}, u32[]{:S(2)}) collective-permute-start(bf16[32,768]{1,0:T(8,128)(2,1)} %get-tuple-element.66.refs_1_.low_ref), channel_id=1, source_target_pairs={{0,1},{1,0},{2,3},{3,2},{4,5},{5,4},{6,7},{7,6},{8,9},{9,8},{10,11... | collective-permute-start | bytes 147464 | tf_op jit(solution)/shard_map/ppermute | solution.py:607
  107.5 2.8 %collective-permute-start.9 = (bf16[8,128,256]{2,1,0:T(8,128)(2,1)S(1)}, bf16[8,128,256]{2,1,0:T(8,128)(2,1)S(1)}, u32[]{:S(2)}, u32[]{:S(2)}) collective-permute-start(bf16[8,128,256]{2,1,0:T(8,128)(2,1)S(1)} %shard_map.199.gs_ref), channel_id=1, source_target_pairs={{0,8},{8,0},{1,9},{9,1},{2,10},{10,2},{3,11},{11,3},{4,12},{12,4},... | collective-permute-start | bytes 1572872 | tf_op jit(solution)/shard_map/ppermute | solution.py:591
  114.4 2.1 collective-permute-start.13
  117.4 20.8 %all-to-all-start.4 = ((bf16[16,48,384]{2,1,0:T(8,128)(2,1)}), bf16[16,48,384]{2,1,0:T(8,128)(2,1)S(1)}, u32[]{:S(2)}, u32[]{:S(2)}) async-start(bf16[16,48,384]{2,1,0:T(8,128)(2,1)} %shard_map.203), calls=%async_computation.4 | async-start | bytes 1179648 | tf_op jit(solution)/shard_map/all_to_all | solution.py:587
  129.3 6.7 %collective-permute-start.10 = (bf16[32,768]{1,0:T(8,128)(2,1)}, bf16[32,768]{1,0:T(8,128)(2,1)S(1)}, u32[]{:S(2)}, u32[]{:S(2)}) collective-permute-start(bf16[32,768]{1,0:T(8,128)(2,1)} %get-tuple-element.71), channel_id=1, source_target_pairs={{0,1},{1,0},{2,3},{3,2},{4,5},{5,4},{6,7},{7,6},{8,9},{9,8},{10,11... | collective-permute-start | bytes 147464 | tf_op jit(solution)/shard_map/ppermute | solution.py:607
  131.1 7.2 %collective-permute-start.11 = (bf16[32,768]{1,0:T(8,128)(2,1)}, bf16[32,768]{1,0:T(8,128)(2,1)S(1)}, u32[]{:S(2)}, u32[]{:S(2)}) collective-permute-start(bf16[32,768]{1,0:T(8,128)(2,1)} %get-tuple-element.72), channel_id=1, source_target_pairs={{0,2},{1,3},{2,0},{3,1},{4,6},{5,7},{6,4},{7,5},{8,10},{9,11},{10,... | collective-permute-start | bytes 147464 | tf_op jit(solution)/shard_map/ppermute | solution.py:607
  131.7 6.5 %collective-permute-start.12 = (bf16[32,768]{1,0:T(8,128)(2,1)}, bf16[32,768]{1,0:T(8,128)(2,1)S(1)}, u32[]{:S(2)}, u32[]{:S(2)}) collective-permute-start(bf16[32,768]{1,0:T(8,128)(2,1)} %get-tuple-element.73), channel_id=1, source_target_pairs={{0,3},{1,2},{2,1},{3,0},{4,7},{5,6},{6,5},{7,4},{8,11},{9,10},{10,... | collective-permute-start | bytes 147464 | tf_op jit(solution)/shard_map/ppermute | solution.py:607
  140.7 41.5 %all-to-all-start.5 = ((bf16[64,56,384]{2,1,0:T(8,128)(2,1)}), bf16[64,56,384]{2,1,0:T(8,128)(2,1)S(1)}, u32[]{:S(2)}, u32[]{:S(2)}) async-start(bf16[64,56,384]{2,1,0:T(8,128)(2,1)} %bitcast.8), calls=%async_computation.5 | async-start | bytes 5505024 | tf_op jit(solution)/shard_map/all_to_all | solution.py:587
  182.1 10.8 %collective-permute-start.14 = (bf16[8,8,56,384]{3,2,1,0:T(8,128)(2,1)S(1)}, bf16[8,8,56,384]{3,2,1,0:T(8,128)(2,1)}, u32[]{:S(2)}, u32[]{:S(2)}) collective-permute-start(bf16[8,8,56,384]{3,2,1,0:T(8,128)(2,1)S(1)} %shard_map.207.refs_1_.in_ref), channel_id=1, source_target_pairs={{0,8},{8,0},{1,9},{9,1},{2,10},{10,2},{3,11},{11,3},{4,12},{12,4},... | collective-permute-start | bytes 8257544 | tf_op jit(solution)/shard_map/ppermute | solution.py:591
  186.6 18.0 %all-to-all-start.6 = ((bf16[8,64,768]{2,1,0:T(8,128)(2,1)}), bf16[8,64,768]{2,1,0:T(8,128)(2,1)S(1)}, u32[]{:S(2)}, u32[]{:S(2)}) async-start(bf16[8,64,768]{2,1,0:T(8,128)(2,1)} %shard_map.208), calls=%async_computation.6 | async-start | bytes 1572864 | tf_op jit(solution)/shard_map/all_to_all | solution.py:587
Sparse Core Ops, SparseCore 0:
  39.1 33.2 all-gather.2
  97.4 36.9 all-gather.4

commit v11 on v10

--- a/solution.py
+++ b/solution.py
@@ -132,13 +132,14 @@
         copy.wait()
 
 
-def weight_copies(w_ref, w_buf, w_sem, parts=(1, 2, 0)):
+def weight_copies(w_ref, w_buf, w_sem, parts=(1, 2, 0), start=True):
     group = group_index()
     copies = []
     for slot, part in enumerate(parts):
         column = pl.multiple_of(part * D + (group // 2) * 384, 128)
         copy = pltpu.make_async_copy(w_ref.at[:, pl.ds(column, 384)], w_buf.at[slot], w_sem.at[slot])
-        copy.start()
+        if start:
+            copy.start()
         copies.append(copy)
     return copies
 
@@ -357,8 +358,8 @@
 
 def attend_back_kernel(
     scene_ref, kvs_ref, kvo_ref, q_ref, gs_ref, go_ref, normed_ref, mixed_ref, low_ref, low1_ref, low2_ref, low3_ref,
-    gqkv_ref, keep_ref, send_ref,
-    kv_buf, q_buf, gqkv_buf, grad_buf, mixed_buf, normed_buf, low_buf, kv_sem, q_sem, in_sem, out_sem,
+    w_ref, gqkv_ref, w_out_ref, keep_ref, send_ref,
+    kv_buf, q_buf, grad_buf, mixed_buf, normed_buf, low_buf, kv_sem, q_sem, in_sem, w_sem,
 ):
     first, big = span(scene_ref)
     chip = chip_index()
@@ -386,6 +387,7 @@
         ]
         for load in loads + first_loads:
             load.start()
+        weight_copies(w_ref, w_out_ref, w_sem)
 
         def cut(value):
             return [value[:, at:at + 128] for at in range(0, value.shape[1], 128)]
@@ -422,7 +424,7 @@
             dv.append(mm(probs.astype(BF), grad[gb]))
             dk.append(mm((probs * gap).astype(BF), query[qb]) * scale)
         tail = dq[2]
-        gqkv_buf[...] = jnp.concatenate(
+        gqkv_ref[...] = jnp.concatenate(
             [join(dk[0], dk[1]), join(dk[2], dv[0]), join(dv[1], dv[2]), join(dq[0], dq[1]),
              join(tail, jnp.zeros_like(tail))],
             axis=1,
@@ -437,11 +439,9 @@
     def _():
         run(1)
 
-    store = pltpu.make_async_copy(gqkv_buf, gqkv_ref, out_sem)
-    store.start()
     wait_all(first_loads)
 
-    grad_buf[...] = mm_tn(normed_buf[...], gqkv_buf[...])
+    grad_buf[...] = mm_tn(normed_buf[...], gqkv_ref[...])
     low = jnp.concatenate([ref[...] for ref in (low_buf, low1_ref, low2_ref, low3_ref)], axis=0)
     mixed = jnp.concatenate(
         [mixed_buf[pl.ds(pl.multiple_of((group ^ k) * BLK, BLK), BLK)] for k in range(4)], axis=0
@@ -458,20 +458,21 @@
             ref[2 * tile + 1] = jnp.concatenate(
                 [rows[:, 384:576], jnp.where(owner == 1, pieces[1], pieces[0])], axis=1
             ).astype(BF)
-    store.wait()
+    wait_all(weight_copies(w_ref, w_out_ref, w_sem, start=False))
 
 
 def normed_grad_kernel(
-    gqkv_ref, tok_ref, w_ref, vec_ref, own_ref, one_ref, two_ref, three_ref, sums_ref,
-    x_buf, part_buf, w_buf, x_sem, w_sem,
+    gqkv_ref, w_ref, tok_ref, vec_ref, own_ref, one_ref, two_ref, three_ref, sums_ref,
+    x_buf, vec_buf, part_buf, low_buf, sums_buf, in_sem, out_sem,
 ):
-    load = pltpu.make_async_copy(tok_ref.at[lax.axis_index(MICRO)], x_buf, x_sem)
-    load.start()
-    loads = weight_copies(w_ref, w_buf, w_sem)
+    loads = [
+        pltpu.make_async_copy(tok_ref.at[lax.axis_index(MICRO)], x_buf, in_sem.at[0]),
+        pltpu.make_async_copy(vec_ref, vec_buf, in_sem.at[1]),
+    ]
+    for load in loads:
+        load.start()
     group = group_index()
     odd = (group % 2) == 1
-    load.wait()
-    unit, _ = normalized(x_buf[...].astype(F32))
     total = jnp.zeros((TOK, D), F32)
     for slot in range(3):
         part = gqkv_ref[:, slot * 192:(slot + 1) * 192]
@@ -479,18 +480,25 @@
         wide = jnp.where(
             odd, jnp.concatenate([zero, part], axis=1), jnp.concatenate([part, zero], axis=1)
         )
-        loads[slot].wait()
-        total = total + mm_nt(wide, w_buf[slot])
+        total = total + mm_nt(wide, w_ref[slot])
     part_buf[...] = total
-    own_ref[...] = part_buf[pl.ds(pl.multiple_of(group * BLK, BLK), BLK)]
-    for k, ref in ((1, one_ref), (2, two_ref), (3, three_ref)):
-        ref[...] = part_buf[pl.ds(pl.multiple_of((group ^ k) * BLK, BLK), BLK)].astype(BF)
+    low_buf[...] = total.astype(BF)
+    stores = []
+    for k, ref in enumerate((own_ref, one_ref, two_ref, three_ref)):
+        rows = pl.ds(pl.multiple_of((group ^ k) * BLK, BLK), BLK)
+        stores.append(pltpu.make_async_copy((low_buf if k else part_buf).at[rows], ref, out_sem.at[k]))
+        stores[-1].start()
+    wait_all(loads)
+    unit, _ = normalized(x_buf[...].astype(F32))
     gain1 = jnp.sum(total * unit, axis=0, keepdims=True)
     shift1 = jnp.sum(total, axis=0, keepdims=True)
-    sums_ref[...] = jnp.concatenate([gain1, shift1, vec_ref[...][:2], jnp.zeros((4, D), F32)], axis=0)
-
-
-def add_kernel(one_ref, two_ref, out_ref, buf, sem):
+    sums_buf[...] = jnp.concatenate([gain1, shift1, vec_buf[...][:2], jnp.zeros((4, D), F32)], axis=0)
+    stores.append(pltpu.make_async_copy(sums_buf, sums_ref, out_sem.at[4]))
+    stores[-1].start()
+    wait_all(stores)
+
+
+def add_kernel(one_ref, two_ref, unused_ref, out_ref, buf, sem):
     buf[...] = (one_ref[...].astype(F32) + two_ref[...].astype(F32)).astype(BF)
     copy = pltpu.make_async_copy(buf, out_ref, sem)
     copy.start()
@@ -560,7 +568,7 @@
 
 
 def input_kernel(
-    own_ref, one_ref, two_ref, three_ref, tok_ref, gain_ref, grad_ref, result_ref, out_ref, buf, x_buf, sem, x_sem
+    own_ref, one_ref, two_ref, three_ref, tok_ref, gain_ref, grad_ref, result_ref, unused_ref, out_ref, buf, x_buf, sem, x_sem
 ):
     start = pl.multiple_of(group_index() * BLK, BLK)
     load = pltpu.make_async_copy(tok_ref.at[lax.axis_index(MICRO), pl.ds(start, BLK)], x_buf, x_sem)
@@ -669,13 +677,12 @@
         split_kernel, [((2, 48, D), BF, "L")] * 4, [(keep, "V"), (swap(send), "V")], 1000
     )
     pieces = [pieces[0]] + [flip(pieces[k], "y", 4, k) for k in (1, 2, 3)]
-    keep, send = call(
+    ff_keep, ff_send = call(
         halve_kernel,
         [((48, D), BF, "L")] * 2,
         [(pieces[0], "L")] + [(piece, "V") for piece in pieces[1:]],
         1000,
     )
-    ff_sums = after(ff_sums, pin(keep))
     grad_send, low, grad_mid, result_part, vec2 = call(
         middle_kernel,
         [
@@ -692,52 +699,54 @@
             pltpu.VMEM((BLK, D), BF), pltpu.VMEM((8, D), F32), DMA((4,)), DMA((8,)), DMA((4,)),
         ],
     )
-    send = after(pin(send), pin(low))
-    (ff_part,) = call(
-        pair_kernel, [((48, D), BF, "L")], [(keep, "L"), (flip(send, "xl", 2, 1), "V")], 1000
-    )
-    ff_all = lax.all_gather(ff_part, WIDE, axis=0, tiled=True)
+    grad_send = after(pin(grad_send), *pieces[1:])
     grad_same = exchange(grad_send.reshape(32, BLK, 256), (*CHIP, *GROUP)).reshape(8, TOK, 256)
     lows = [flip(low, GROUP, 4, k) for k in (1, 2, 3)]
-    grad_same = after(grad_same, *lows, pin(ff_part))
+    grad_same = after(grad_same, *lows, pin(ff_send))
     grad_other = swap(grad_same)
-    gqkv, keep, send = call(
+    far = flip(ff_send, "xl", 2, 1)
+    gqkv, w_own, keep, send = call(
         attend_back_kernel,
-        [((TOK, 640), BF, "H")] + [((16, 48, 384), BF, "V")] * 2,
+        [((TOK, 640), BF, "V"), ((3, D, 384), BF, "V")] + [((16, 48, 384), BF, "V")] * 2,
         [
             (scene_of_block, "S"), (kv_same, "H"), (kv_other, "H"), (queries, "H"), (grad_same, "V"), (grad_other, "V"),
-            (normed, "H"), (mixed, "H"), (low, "H"), *[(value, "V") for value in lows],
+            (normed, "H"), (mixed, "H"), (low, "H"), *[(value, "V") for value in lows], (w_qkv, "H"),
         ],
         10**9,
         [
-            pltpu.VMEM((2, 5, TOK, 384), BF), pltpu.VMEM((2, 5, TOK, 256), BF), pltpu.VMEM((TOK, 640), BF),
-            pltpu.VMEM((D, 640), F32), pltpu.VMEM((TOK, 256), BF), pltpu.VMEM((TOK, D), BF), pltpu.VMEM((BLK, D), BF),
-            DMA((2,)), DMA((2,)), DMA((3,)), DMA,
+            pltpu.VMEM((2, 5, TOK, 384), BF), pltpu.VMEM((2, 5, TOK, 256), BF), pltpu.VMEM((D, 640), F32),
+            pltpu.VMEM((TOK, 256), BF), pltpu.VMEM((TOK, D), BF), pltpu.VMEM((BLK, D), BF),
+            DMA((2,)), DMA((2,)), DMA((3,)), DMA((3,)),
         ],
         vmem=24,
+    )
+    own, *sends, sums = call(
+        normed_grad_kernel,
+        [((BLK, D), F32, "H")] + [((BLK, D), BF, "H")] * 3 + [((8, D), F32, "H")],
+        [(gqkv, "V"), (w_own, "V"), (tokens, "H"), (vec2, "H")],
+        1000,
+        [
+            pltpu.VMEM((TOK, D), BF), pltpu.VMEM((8, D), F32), pltpu.VMEM((TOK, D), F32), pltpu.VMEM((TOK, D), BF),
+            pltpu.VMEM((8, D), F32), DMA((2,)), DMA((5,)),
+        ],
     )
     (weight_send,) = call(
         add_kernel,
         [((16, 48, 384), BF, "H")],
-        [(keep, "V"), (swap(send), "V")],
+        [(keep, "V"), (swap(send), "V"), (own, "H")],
         1000,
         [pltpu.VMEM((16, 48, 384), BF), DMA],
     )
+    (ff_part,) = call(pair_kernel, [((48, D), BF, "L")], [(ff_keep, "L"), (far, "V")], 1000)
+    ff_all = lax.all_gather(ff_part, WIDE, axis=0, tiled=True)
     weight_parts = exchange(weight_send, (*CHIP, MICRO))
-    own, *sends, sums = call(
-        normed_grad_kernel,
-        [((BLK, D), F32, "L")] + [((BLK, D), BF, "L")] * 3 + [((8, D), F32, "L")],
-        [(gqkv, "L"), (tokens, "H"), (w_qkv, "H"), (vec2, "L")],
-        1000,
-        [pltpu.VMEM((TOK, D), BF), pltpu.VMEM((TOK, D), F32), pltpu.VMEM((3, D, 384), BF), DMA, DMA((3,))],
-    )
     parts = [flip(value, GROUP, 4, k + 1) for k, value in enumerate(sends)]
-    weight_parts = after(weight_parts, pin(sums), *parts, pin(ff_all))
+    weight_parts = after(weight_parts, pin(sums), *parts)
     (weight_total,) = call(
         sum_kernel,
         [((8, 8, 56, 384), BF, "H")],
         [(weight_parts, "V"), (sums, "H")],
-        1000,
+        4 * 10**10,
         [pltpu.VMEM((8, 56, 384), BF), pltpu.VMEM((8, D), F32), DMA((8,)), DMA],
     )
     (packed,) = call(
@@ -745,13 +754,13 @@
         [((8, 2 * BLK, D), BF, "H")],
         [
             (own, "L"), *[(value, "V") for value in parts], (tokens, "H"), (ln1_gain, "L"), (grad_mid, "L"),
-            (result_part, "L"),
+            (result_part, "L"), (weight_total, "H"),
         ],
         1000,
         [pltpu.VMEM((2 * BLK, D), BF), pltpu.VMEM((BLK, D), BF), DMA((8,)), DMA],
     )
     up_grad, down_grad = call(
-        spread_ff_kernel, [((D, FFL), F32, "L"), ((FFL, D), F32, "L")], [(ff_all, "L")], 1000
+        spread_ff_kernel, [((D, FFL), F32, "L"), ((FFL, D), F32, "L")], [(ff_all, "L")], 5 * 10**10
     )
     weight_same = exchange(weight_total.reshape(64, 56, 384), (*CHIP, *NARROW)).reshape(8, 8, 56, 384)
     weight_same = after(weight_same, pin(packed), pin(up_grad), pin(down_grad))

time: 214 us -> 218 us (1.019)
  waiting for transfers between devices: 77.4 us -> 88.3 us
  starting transfers between devices: 68.6 us -> 63.3 us
    all_gather x1, waiting for transfers between devices: 0.01 us -> 39.3 us  [shards(): ff_all = lax.all_gather(ff_part, WIDE, axis=0, tiled=True)]
    all_to_all x7, waiting for transfers between devices: 52.6 us -> 34.8 us  [exchange(): return lax.all_to_all(value, axes, 0, 0, tiled=True)]
    ppermute x10, waiting for transfers between devices: 18.9 us -> 10 us  [flip(): lax.ppermute(value, axes, [(index, index ^ bits) for index in range(count)])]
    all_to_all x7, starting transfers between devices: 45 us -> 42.1 us  [exchange(): return lax.all_to_all(value, axes, 0, 0, tiled=True)]
    ppermute x5, starting transfers between devices: 10.1 us -> 7.49 us  [swap(): return lax.ppermute(value, CORE, [(0, 1), (1, 0)])]
  transfers between devices with their start and end apart: 24 -> 24, of which waited for: 14 -> 13; matrix products, arithmetic and copies ran while one was open for 1% -> 1% of each run, Pallas kernels for 19% -> 16%
where the time goes in v11:
time: 218 us; the launch traced here: 217 us
  waiting for transfers between devices  88.3 us (41%)
  starting transfers between devices  63.3 us (29%)
  Pallas kernels  48.7 us (22%)
  between operations  14.3 us (7%)
  local copies, waits for them, and re-layouts  2.29 us (1%)
    pallas_call x18, Pallas kernels, call(): pl.pallas_call(kernel, out_shape=[(pltpu.HBM if place in 'HL' else jax.Sh...  48.7 us
    all_to_all x7, starting transfers between devices, exchange(): return lax.all_to_all(value, axes, 0, 0, tiled=True)  42.1 us
    all_gather x1, waiting for transfers between devices, shards(): ff_all = lax.all_gather(ff_part, WIDE, axis=0, tiled=True)  39.3 us
    all_to_all x7, waiting for transfers between devices, exchange(): return lax.all_to_all(value, axes, 0, 0, tiled=True)  34.8 us
    ppermute x10, starting transfers between devices, flip(): lax.ppermute(value, axes, [(index, index ^ bits) for index in range(count)])  13.7 us
    ppermute x10, waiting for transfers between devices, flip(): lax.ppermute(value, axes, [(index, index ^ bits) for index in range(count)])  10 us
    ppermute x5, starting transfers between devices, swap(): return lax.ppermute(value, CORE, [(0, 1), (1, 0)])  7.49 us
  transfers between devices with their start and end apart: 24, of which 13 were waited for; matrix products, arithmetic and copies ran while one was open for 1% of the time, Pallas kernels for 16%

profile of v11, /device:TPU:1, one launch (start us, length us, event | category | flops | bytes accessed | tf_op | source)
XLA Modules:
  0.0 217.0 jit_solution(9079828202128335754)
XLA Ops:
  7.2 3.7 %shard_map.186 = (bf16[8,128,384]{2,1,0:T(8,128)(2,1)}, bf16[128,768]{1,0:T(8,128)(2,1)}) custom-call(bf16[2,128,768]{2,1,0:T(8,128)(2,1)} %tok_ref.7, f32[768]{0:T(1024)} %gain_ref.7, f32[768]{0:T(1024)} %shift_ref.2, bf16[768,2304]{1,0:T(8,128)(2,1)} %w_ref.5), custom_call_target="tpu_custom_call" | custom-call | flops 1000 | bytes 1000 | tf_op jit(solution)/shard_map/pallas_call | solution.py:106
  10.9 6.0 %all-to-all-start = ((bf16[8,128,384]{2,1,0:T(8,128)(2,1)}), bf16[8,128,384]{2,1,0:T(8,128)(2,1)S(1)}, u32[]{:S(2)}, u32[]{:S(2)}) async-start(bf16[8,128,384]{2,1,0:T(8,128)(2,1)} %get-tuple-element.52), calls=%async_computation | async-start | bytes 1572864 | tf_op jit(solution)/shard_map/all_to_all | solution.py:595
  16.9 3.0 %shard_map.187.refs_1_.refs_0_.q_ref = bf16[128,256]{1,0:T(8,128)(2,1)} custom-call(bf16[128,768]{1,0:T(8,128)(2,1)} %get-tuple-element.53.normed_ref, bf16[768,2304]{1,0:T(8,128)(2,1)} %w_ref.5), custom_call_target="tpu_custom_call" | custom-call | flops 1000 | bytes 1000 | tf_op jit(solution)/shard_map/pallas_call | solution.py:106
  19.9 8.6 %all-to-all-done.refs_0_ = bf16[8,128,384]{2,1,0:T(8,128)(2,1)S(1)} async-done(((bf16[8,128,384]{2,1,0:T(8,128)(2,1)}), bf16[8,128,384]{2,1,0:T(8,128)(2,1)S(1)}, u32[]{:S(2)}, u32[]{:S(2)}) %all-to-all-start) | async-done | bytes 786464 | tf_op jit(solution)/shard_map/all_to_all | solution.py:595
  28.5 2.2 collective-permute-start
  32.6 3.1 %shard_map.190 = bf16[8,128,256]{2,1,0:T(8,128)(2,1)} custom-call(s32[2,32]{1,0:T(2,128)S(1)} %copy-done.3, bf16[128,256]{1,0:T(8,128)(2,1)} %shard_map.187.refs_1_.refs_0_.q_ref, bf16[8,128,384]{2,1,0:T(8,128)(2,1)S(1)} %shard_map.188.refs_1_.same_ref.kvs_ref, bf16[8,128,384]{2,1,0:T(8,128)(2,1)S(1)} %collective-permute-done.other_ref.kvo_ref), custom_call_target="tpu_custom_call" | custom-call | flops 1000 | bytes 1000 | tf_op jit(solution)/shard_map/pallas_call | solution.py:106
  36.6 7.2 %all-to-all-start.1 = ((bf16[8,128,256]{2,1,0:T(8,128)(2,1)}), bf16[8,128,256]{2,1,0:T(8,128)(2,1)S(1)}, u32[]{:S(2)}, u32[]{:S(2)}) async-start(bf16[8,128,256]{2,1,0:T(8,128)(2,1)} %shard_map.190), calls=%async_computation.1 | async-start | bytes 1048576 | tf_op jit(solution)/shard_map/all_to_all | solution.py:595
  45.9 8.6 %all-to-all-done.1.mixed_ref = bf16[8,128,256]{2,1,0:T(8,128)(2,1)S(1)} async-done(((bf16[8,128,256]{2,1,0:T(8,128)(2,1)}), bf16[8,128,256]{2,1,0:T(8,128)(2,1)S(1)}, u32[]{:S(2)}, u32[]{:S(2)}) %all-to-all-start.1) | async-done | bytes 524320 | tf_op jit(solution)/shard_map/all_to_all | solution.py:595
  54.5 4.1 %shard_map.191 = (bf16[8,64,768]{2,1,0:T(8,128)(2,1)}, f32[32,768]{1,0:T(8,128)}, bf16[256,768]{1,0:T(8,128)(2,1)S(1)}, bf16[256,384]{1,0:T(8,128)(2,1)S(1)}, bf16[256,384]{1,0:T(8,128)(2,1)S(1)}) custom-call(bf16[8,128,256]{2,1,0:T(8,128)(2,1)S(1)} %all-to-all-done.1.mixed_ref, bf16[2,128,768]{2,1,0:T(8,128)(2,1)} %tok_ref.7, bf16[2,128,768]{2,1,0:T(8,128)(2,1)} %og_ref.5, ...), custom_call_target="tpu_custom_call" | custom-call | flops 1000 | bytes 1000 | tf_op jit(solution)/shard_map/pallas_call | solution.py:106
  58.7 2.8 %shard_map.193 = (bf16[8,48,768]{2,1,0:T(8,128)(2,1)S(1)}, bf16[8,48,768]{2,1,0:T(8,128)(2,1)}) custom-call(bf16[256,768]{1,0:T(8,128)(2,1)S(1)} %get-tuple-element.57.normed_ref, bf16[256,384]{1,0:T(8,128)(2,1)S(1)} %get-tuple-element.58.act_ref, bf16[256,384]{1,0:T(8,128)(2,1)S(1)} %get-tuple-element.59.gpre_ref, bf16[2,128,768]{2,1,0:T(8,128)(2,1)} %og_ref.5), custom_call_target="tpu_custom_call" | custom-call | flops 1000 | bytes 1000 | tf_op jit(solution)/shard_map/pallas_call | solution.py:106
  63.2 3.5 %all-to-all-start.2 = ((bf16[8,64,768]{2,1,0:T(8,128)(2,1)}), bf16[8,64,768]{2,1,0:T(8,128)(2,1)S(1)}, u32[]{:S(2)}, u32[]{:S(2)}) async-start(bf16[8,64,768]{2,1,0:T(8,128)(2,1)} %get-tuple-element.54), calls=%async_computation.2 | async-start | bytes 1572864 | tf_op jit(solution)/shard_map/all_to_all | solution.py:595
  69.2 2.1 collective-permute-start.3
  72.5 10.5 %all-to-all-done.2.sums_ref = bf16[8,64,768]{2,1,0:T(8,128)(2,1)S(1)} async-done(((bf16[8,64,768]{2,1,0:T(8,128)(2,1)}), bf16[8,64,768]{2,1,0:T(8,128)(2,1)S(1)}, u32[]{:S(2)}, u32[]{:S(2)}) %all-to-all-start.2) | async-done | bytes 786464 | tf_op jit(solution)/shard_map/all_to_all | solution.py:595
  83.0 2.7 %shard_map.192 = (bf16[8,4,32,256]{3,2,1,0:T(8,128)(2,1)}, bf16[32,768]{1,0:T(8,128)(2,1)}, f32[32,768]{1,0:T(8,128)}, bf16[32,768]{1,0:T(8,128)(2,1)}, f32[8,768]{1,0:T(8,128)}) custom-call(bf16[8,64,768]{2,1,0:T(8,128)(2,1)S(1)} %all-to-all-done.2.sums_ref, f32[32,768]{1,0:T(8,128)} %get-tuple-element.55.middle_ref, bf16[2,128,768]{2,1,0:T(8,128)(2,1)} %og_ref.5, ...), custom_call_target="tpu_custom_call" | custom-call | flops 1000 | bytes 1000 | tf_op jit(solution)/shard_map/pallas_call | solution.py:106
  85.8 3.9 %all-to-all-start.3 = ((bf16[32,32,256]{2,1,0:T(8,128)(2,1)}), bf16[32,32,256]{2,1,0:T(8,128)(2,1)S(1)}, u32[]{:S(2)}, u32[]{:S(2)}) async-start(bf16[32,32,256]{2,1,0:T(8,128)(2,1)} %bitcast.9), calls=%async_computation.3 | async-start | bytes 1048576 | tf_op jit(solution)/shard_map/all_to_all | solution.py:595
  89.7 3.6 %collective-permute-start.7 = (bf16[32,768]{1,0:T(8,128)(2,1)S(1)}, bf16[32,768]{1,0:T(8,128)(2,1)S(1)}, u32[]{:S(2)}, u32[]{:S(2)}) collective-permute-start(bf16[32,768]{1,0:T(8,128)(2,1)S(1)} %copy-done.5), channel_id=1, source_target_pairs={{0,3},{1,2},{2,1},{3,0},{4,7},{5,6},{6,5},{7,4},{8,11},{9,10},{10,... | collective-permute-start | bytes 147464 | tf_op jit(solution)/shard_map/ppermute | solution.py:615
  95.5 4.8 %collective-permute-done.7.refs_3_.low3_ref = bf16[32,768]{1,0:T(8,128)(2,1)S(1)} collective-permute-done((bf16[32,768]{1,0:T(8,128)(2,1)S(1)}, bf16[32,768]{1,0:T(8,128)(2,1)S(1)}, u32[]{:S(2)}, u32[]{:S(2)}) %collective-permute-start.7) | collective-permute-done | bytes 49184 | tf_op jit(solution)/shard_map/ppermute | solution.py:615
  100.7 2.9 %collective-permute-start.8 = (bf16[8,128,256]{2,1,0:T(8,128)(2,1)S(1)}, bf16[8,128,256]{2,1,0:T(8,128)(2,1)S(1)}, u32[]{:S(2)}, u32[]{:S(2)}) collective-permute-start(bf16[8,128,256]{2,1,0:T(8,128)(2,1)S(1)} %shard_map.197.gs_ref), channel_id=1, source_target_pairs={{0,8},{8,0},{1,9},{9,1},{2,10},{10,2},{3,11},{11,3},{4,12},{12,4},... | collective-permute-start | bytes 1572872 | tf_op jit(solution)/shard_map/ppermute | solution.py:599
  105.2 4.4 %shard_map.198 = (bf16[128,640]{1,0:T(8,128)(2,1)S(1)}, bf16[3,768,384]{2,1,0:T(8,128)(2,1)S(1)}, bf16[16,48,384]{2,1,0:T(8,128)(2,1)S(1)}, bf16[16,48,384]{2,1,0:T(8,128)(2,1)S(1)}) custom-call(s32[2,32]{1,0:T(2,128)S(1)} %copy-done.3, bf16[8,128,384]{2,1,0:T(8,128)(2,1)} %copy-done, bf16[8,128,384]{2,1,0:T(8,128)(2,1)} %copy-done.2, ...), custom_call_target="tpu_custom_call" | custom-call | flops 1000000000 | bytes 1000 | tf_op jit(solution)/shard_map/pallas_call | solution.py:106
  110.0 2.3 %shard_map.199 = (f32[32,768]{1,0:T(8,128)}, bf16[32,768]{1,0:T(8,128)(2,1)}, bf16[32,768]{1,0:T(8,128)(2,1)}, bf16[32,768]{1,0:T(8,128)(2,1)}, f32[8,768]{1,0:T(8,128)}) custom-call(bf16[128,640]{1,0:T(8,128)(2,1)S(1)} %get-tuple-element.68.gqkv_ref, bf16[3,768,384]{2,1,0:T(8,128)(2,1)S(1)} %get-tuple-element.69.w_ref, bf16[2,128,768]{2,1,0:T(8,128)(2,1)} %tok_ref.7, ...), custom_call_target="tpu_custom_call" | custom-call | flops 1000 | bytes 1000 | tf_op jit(solution)/shard_map/pallas_call | solution.py:106
  113.4 4.8 %all-to-all-start.4 = ((bf16[16,48,384]{2,1,0:T(8,128)(2,1)}), bf16[16,48,384]{2,1,0:T(8,128)(2,1)S(1)}, u32[]{:S(2)}, u32[]{:S(2)}) async-start(bf16[16,48,384]{2,1,0:T(8,128)(2,1)} %shard_map.200), calls=%async_computation.4 | async-start | bytes 1179648 | tf_op jit(solution)/shard_map/all_to_all | solution.py:595
  121.7 2.2 %collective-permute-start.11 = (bf16[32,768]{1,0:T(8,128)(2,1)S(1)}, bf16[32,768]{1,0:T(8,128)(2,1)S(1)}, u32[]{:S(2)}, u32[]{:S(2)}) collective-permute-start(bf16[32,768]{1,0:T(8,128)(2,1)S(1)} %copy-done.6), channel_id=1, source_target_pairs={{0,3},{1,2},{2,1},{3,0},{4,7},{5,6},{6,5},{7,4},{8,11},{9,10},{10,... | collective-permute-start | bytes 147464 | tf_op jit(solution)/shard_map/ppermute | solution.py:615
  123.9 4.2 %collective-permute-done.13.two_ref = bf16[48,768]{1,0:T(8,128)(2,1)S(1)} collective-permute-done((bf16[48,768]{1,0:T(8,128)(2,1)S(1)}, bf16[48,768]{1,0:T(8,128)(2,1)S(1)}, u32[]{:S(2)}, u32[]{:S(2)}) %collective-permute-start.13) | collective-permute-done | bytes 73760 | tf_op jit(solution)/shard_map/ppermute | solution.py:615
  130.7 2.4 %shard_map.202.unused_ref = bf16[8,8,56,384]{3,2,1,0:T(8,128)(2,1)} custom-call(bf16[16,48,384]{2,1,0:T(8,128)(2,1)S(1)} %shard_map.201.in_ref, f32[8,768]{1,0:T(8,128)} %get-tuple-element.79.refs_1_.vec_ref), custom_call_target="tpu_custom_call" | custom-call | flops 40000000000 | bytes 1000 | tf_op jit(solution)/shard_map/pallas_call | solution.py:106
  133.1 9.2 %all-to-all-start.5 = ((bf16[64,56,384]{2,1,0:T(8,128)(2,1)}), bf16[64,56,384]{2,1,0:T(8,128)(2,1)S(1)}, u32[]{:S(2)}, u32[]{:S(2)}) async-start(bf16[64,56,384]{2,1,0:T(8,128)(2,1)} %bitcast.8), calls=%async_computation.5 | async-start | bytes 5505024 | tf_op jit(solution)/shard_map/all_to_all | solution.py:595
  142.3 3.0 %shard_map.203.refs_1_.refs_0_ = bf16[8,64,768]{2,1,0:T(8,128)(2,1)} custom-call(f32[32,768]{1,0:T(8,128)} %get-tuple-element.71.unused_ref.own_ref, bf16[32,768]{1,0:T(8,128)(2,1)S(1)} %collective-permute-done.9.refs_2_.one_ref, bf16[32,768]{1,0:T(8,128)(2,1)S(1)} %collective-permute-done.10.refs_3_.two_ref, ...), custom_call_target="tpu_custom_call" | custom-call | flops 1000 | bytes 1000 | tf_op jit(solution)/shard_map/pallas_call | solution.py:106
  145.3 39.3 %all-gather.5.cloned.1.call-done.in_ref = bf16[768,768]{1,0:T(8,128)(2,1)} async-done(((bf16[48,768]{1,0:T(8,128)(2,1)}), bf16[768,768]{1,0:T(8,128)(2,1)}) %all-gather.5.cloned.1.call-update) | async-done | bytes 1179664 | tf_op jit(solution)/shard_map/all_gather | solution.py:741
  184.6 2.7 %shard_map.205 = (f32[768,384]{1,0:T(8,128)}, f32[384,768]{1,0:T(8,128)}) custom-call(bf16[768,768]{1,0:T(8,128)(2,1)} %all-gather.5.cloned.1.call-done.in_ref), custom_call_target="tpu_custom_call" | custom-call | flops 49999998976 | bytes 1000 | tf_op jit(solution)/shard_map/pallas_call | solution.py:106
  187.6 7.5 %all-to-all-start.6 = ((bf16[8,64,768]{2,1,0:T(8,128)(2,1)}), bf16[8,64,768]{2,1,0:T(8,128)(2,1)S(1)}, u32[]{:S(2)}, u32[]{:S(2)}) async-start(bf16[8,64,768]{2,1,0:T(8,128)(2,1)} %shard_map.207), calls=%async_computation.6 | async-start | bytes 1572864 | tf_op jit(solution)/shard_map/all_to_all | solution.py:595
  195.1 2.4 %shard_map.208 = (f32[768,2304]{1,0:T(8,128)}, f32[768,768]{1,0:T(8,128)}, f32[8,384]{1,0:T(8,128)S(1)}) custom-call(bf16[8,8,56,384]{3,2,1,0:T(8,128)(2,1)S(1)} %shard_map.206.refs_1_.in_ref), custom_call_target="tpu_custom_call" | custom-call | flops 1000 | bytes 1000 | tf_op jit(solution)/shard_map/pallas_call | solution.py:106
  197.5 4.8 %shard_map.209 = (f32[768,2304]{1,0:T(8,128)}, f32[768,768]{1,0:T(8,128)}, f32[768]{0:T(1024)}, f32[768]{0:T(1024)}, f32[768]{0:T(1024)}, /*index=5*/f32[768]{0:T(1024)}) custom-call(bf16[8,8,56,384]{3,2,1,0:T(8,128)(2,1)} %collective-permute-done.14.in_ref, f32[8,384]{1,0:T(8,128)S(1)} %get-tuple-element.83.refs_0_, ...), custom_call_target="tpu_custom_call", output_to_operand_aliasing={{0}: (2, {}), {1}: (3, {})} | custom-call | flops 1000 | bytes 1000 | tf_op jit(solution)/shard_map/pallas_call | solution.py:106
  202.4 6.7 %all-to-all-done.6.in_ref = bf16[8,64,768]{2,1,0:T(8,128)(2,1)S(1)} async-done(((bf16[8,64,768]{2,1,0:T(8,128)(2,1)}), bf16[8,64,768]{2,1,0:T(8,128)(2,1)S(1)}, u32[]{:S(2)}, u32[]{:S(2)}) %all-to-all-start.6) | async-done | bytes 786464 | tf_op jit(solution)/shard_map/all_to_all | solution.py:595
  (62 shorter events, 23.2 us)
Async XLA Ops:
  10.9 17.6 %all-to-all-start = ((bf16[8,128,384]{2,1,0:T(8,128)(2,1)}), bf16[8,128,384]{2,1,0:T(8,128)(2,1)S(1)}, u32[]{:S(2)}, u32[]{:S(2)}) async-start(bf16[8,128,384]{2,1,0:T(8,128)(2,1)} %get-tuple-element.52), calls=%async_computation | async-start | bytes 1572864 | tf_op jit(solution)/shard_map/all_to_all | solution.py:595
  16.8 15.8 %copy-start.3 = (s32[2,32]{1,0:T(2,128)S(1)}, s32[2,32]{1,0:T(2,128)}, u32[]{:S(2)}) copy-start(s32[2,32]{1,0:T(2,128)} %scene_ref.3) | copy-start | bytes 772
  28.5 17.4 %copy-start = (bf16[8,128,384]{2,1,0:T(8,128)(2,1)}, bf16[8,128,384]{2,1,0:T(8,128)(2,1)S(1)}, u32[]{:S(2)}) copy-start(bf16[8,128,384]{2,1,0:T(8,128)(2,1)S(1)} %shard_map.188.refs_1_.same_ref.kvs_ref) | copy-start | bytes 2359300
  28.5 4.1 %collective-permute-start = (bf16[8,128,384]{2,1,0:T(8,128)(2,1)S(1)}, bf16[8,128,384]{2,1,0:T(8,128)(2,1)S(1)}, u32[]{:S(2)}, u32[]{:S(2)}) collective-permute-start(bf16[8,128,384]{2,1,0:T(8,128)(2,1)S(1)} %shard_map.188.refs_1_.same_ref.kvs_ref), channel_id=1, source_target_pairs={{0,8},{8,0},{1,9},{9,1},{2,10},{10,2},{3,11},{11,3},{4,12},{12,4},... | collective-permute-start | bytes 2359304 | tf_op jit(solution)/shard_map/ppermute | solution.py:599
  36.6 18.0 %all-to-all-start.1 = ((bf16[8,128,256]{2,1,0:T(8,128)(2,1)}), bf16[8,128,256]{2,1,0:T(8,128)(2,1)S(1)}, u32[]{:S(2)}, u32[]{:S(2)}) async-start(bf16[8,128,256]{2,1,0:T(8,128)(2,1)} %shard_map.190), calls=%async_computation.1 | async-start | bytes 1048576 | tf_op jit(solution)/shard_map/all_to_all | solution.py:595
  43.8 59.9 %all-gather.3.cloned.1.call-start = ((), (), s32[]{:S(2)}) async-start(), calls=%async_computation.7 | async-start | bytes 1114112 | tf_op jit(solution)/shard_map/all_gather | solution.py:650
  54.5 6.9 %copy-start.1 = (bf16[8,128,256]{2,1,0:T(8,128)(2,1)}, bf16[8,128,256]{2,1,0:T(8,128)(2,1)S(1)}, u32[]{:S(2)}) copy-start(bf16[8,128,256]{2,1,0:T(8,128)(2,1)S(1)} %all-to-all-done.1.mixed_ref) | copy-start | bytes 1572868
  61.5 5.2 %collective-permute-start.1 = (bf16[8,48,768]{2,1,0:T(8,128)(2,1)}, bf16[8,48,768]{2,1,0:T(8,128)(2,1)}, u32[]{:S(2)}, u32[]{:S(2)}) collective-permute-start(bf16[8,48,768]{2,1,0:T(8,128)(2,1)} %get-tuple-element.61), channel_id=1, source_target_pairs={{0,8},{8,0},{1,9},{9,1},{2,10},{10,2},{3,11},{11,3},{4,12},{12,4},... | collective-permute-start | bytes 1769480 | tf_op jit(solution)/shard_map/ppermute | solution.py:599
  63.2 19.8 %all-to-all-start.2 = ((bf16[8,64,768]{2,1,0:T(8,128)(2,1)}), bf16[8,64,768]{2,1,0:T(8,128)(2,1)S(1)}, u32[]{:S(2)}, u32[]{:S(2)}) async-start(bf16[8,64,768]{2,1,0:T(8,128)(2,1)} %get-tuple-element.54), calls=%async_computation.2 | async-start | bytes 1572864 | tf_op jit(solution)/shard_map/all_to_all | solution.py:595
  68.6 17.1 %collective-permute-start.2 = (bf16[2,48,768]{2,1,0:T(8,128)(2,1)}, bf16[2,48,768]{2,1,0:T(8,128)(2,1)S(1)}, u32[]{:S(2)}, u32[]{:S(2)}) collective-permute-start(bf16[2,48,768]{2,1,0:T(8,128)(2,1)} %get-tuple-element.62), channel_id=1, source_target_pairs={{0,32},{32,0},{64,96},{96,64},{1,33},{33,1},{65,97},{97,65},{2,34}... | collective-permute-start | bytes 442376 | tf_op jit(solution)/shard_map/ppermute | solution.py:615
  69.2 16.5 %collective-permute-start.3 = (bf16[2,48,768]{2,1,0:T(8,128)(2,1)}, bf16[2,48,768]{2,1,0:T(8,128)(2,1)S(1)}, u32[]{:S(2)}, u32[]{:S(2)}) collective-permute-start(bf16[2,48,768]{2,1,0:T(8,128)(2,1)} %get-tuple-element.63), channel_id=1, source_target_pairs={{0,64},{32,96},{64,0},{96,32},{1,65},{33,97},{65,1},{97,33},{2,66}... | collective-permute-start | bytes 442376 | tf_op jit(solution)/shard_map/ppermute | solution.py:615
  71.3 14.4 %collective-permute-start.4 = (bf16[2,48,768]{2,1,0:T(8,128)(2,1)}, bf16[2,48,768]{2,1,0:T(8,128)(2,1)S(1)}, u32[]{:S(2)}, u32[]{:S(2)}) collective-permute-start(bf16[2,48,768]{2,1,0:T(8,128)(2,1)} %get-tuple-element.64), channel_id=1, source_target_pairs={{0,96},{32,64},{64,32},{96,0},{1,97},{33,65},{65,33},{97,1},{2,98}... | collective-permute-start | bytes 442376 | tf_op jit(solution)/shard_map/ppermute | solution.py:615
  85.7 4.0 %copy-start.5 = (bf16[32,768]{1,0:T(8,128)(2,1)S(1)}, bf16[32,768]{1,0:T(8,128)(2,1)}, u32[]{:S(2)}) copy-start(bf16[32,768]{1,0:T(8,128)(2,1)} %get-tuple-element.65.low_ref) | copy-start | bytes 147460
  85.8 14.9 %all-to-all-start.3 = ((bf16[32,32,256]{2,1,0:T(8,128)(2,1)}), bf16[32,32,256]{2,1,0:T(8,128)(2,1)S(1)}, u32[]{:S(2)}, u32[]{:S(2)}) async-start(bf16[32,32,256]{2,1,0:T(8,128)(2,1)} %bitcast.9), calls=%async_computation.3 | async-start | bytes 1048576 | tf_op jit(solution)/shard_map/all_to_all | solution.py:595
  89.7 10.6 %collective-permute-start.7 = (bf16[32,768]{1,0:T(8,128)(2,1)S(1)}, bf16[32,768]{1,0:T(8,128)(2,1)S(1)}, u32[]{:S(2)}, u32[]{:S(2)}) collective-permute-start(bf16[32,768]{1,0:T(8,128)(2,1)S(1)} %copy-done.5), channel_id=1, source_target_pairs={{0,3},{1,2},{2,1},{3,0},{4,7},{5,6},{6,5},{7,4},{8,11},{9,10},{10,... | collective-permute-start | bytes 147464 | tf_op jit(solution)/shard_map/ppermute | solution.py:615
  93.3 7.0 %collective-permute-start.6 = (bf16[32,768]{1,0:T(8,128)(2,1)S(1)}, bf16[32,768]{1,0:T(8,128)(2,1)S(1)}, u32[]{:S(2)}, u32[]{:S(2)}) collective-permute-start(bf16[32,768]{1,0:T(8,128)(2,1)S(1)} %copy-done.5), channel_id=1, source_target_pairs={{0,2},{1,3},{2,0},{3,1},{4,6},{5,7},{6,4},{7,5},{8,10},{9,11},{10,... | collective-permute-start | bytes 147464 | tf_op jit(solution)/shard_map/ppermute | solution.py:615
  93.6 6.7 %collective-permute-start.5 = (bf16[32,768]{1,0:T(8,128)(2,1)S(1)}, bf16[32,768]{1,0:T(8,128)(2,1)S(1)}, u32[]{:S(2)}, u32[]{:S(2)}) collective-permute-start(bf16[32,768]{1,0:T(8,128)(2,1)S(1)} %copy-done.5), channel_id=1, source_target_pairs={{0,1},{1,0},{2,3},{3,2},{4,5},{5,4},{6,7},{7,6},{8,9},{9,8},{10,11... | collective-permute-start | bytes 147464 | tf_op jit(solution)/shard_map/ppermute | solution.py:615
  100.7 4.5 %collective-permute-start.8 = (bf16[8,128,256]{2,1,0:T(8,128)(2,1)S(1)}, bf16[8,128,256]{2,1,0:T(8,128)(2,1)S(1)}, u32[]{:S(2)}, u32[]{:S(2)}) collective-permute-start(bf16[8,128,256]{2,1,0:T(8,128)(2,1)S(1)} %shard_map.197.gs_ref), channel_id=1, source_target_pairs={{0,8},{8,0},{1,9},{9,1},{2,10},{10,2},{3,11},{11,3},{4,12},{12,4},... | collective-permute-start | bytes 1572872 | tf_op jit(solution)/shard_map/ppermute | solution.py:599
  109.6 2.8 %collective-permute-start.12 = (bf16[16,48,384]{2,1,0:T(8,128)(2,1)S(1)}, bf16[16,48,384]{2,1,0:T(8,128)(2,1)S(1)}, u32[]{:S(2)}, u32[]{:S(2)}) collective-permute-start(bf16[16,48,384]{2,1,0:T(8,128)(2,1)S(1)} %get-tuple-element.78), channel_id=1, source_target_pairs={{0,8},{8,0},{1,9},{9,1},{2,10},{10,2},{3,11},{11,3},{4,12},{12,4},... | collective-permute-start | bytes 1769480 | tf_op jit(solution)/shard_map/ppermute | solution.py:599
  110.0 8.3 %copy-start.4 = (bf16[48,768]{1,0:T(8,128)(2,1)S(1)}, bf16[48,768]{1,0:T(8,128)(2,1)}, u32[]{:S(2)}) copy-start(bf16[48,768]{1,0:T(8,128)(2,1)} %get-tuple-element.67.refs_4_) | copy-start | bytes 221188
  112.4 7.4 %copy-start.8 = (bf16[32,768]{1,0:T(8,128)(2,1)S(1)}, bf16[32,768]{1,0:T(8,128)(2,1)}, u32[]{:S(2)}) copy-start(bf16[32,768]{1,0:T(8,128)(2,1)} %get-tuple-element.72) | copy-start | bytes 147460
  112.4 9.3 %copy-start.7 = (bf16[32,768]{1,0:T(8,128)(2,1)S(1)}, bf16[32,768]{1,0:T(8,128)(2,1)}, u32[]{:S(2)}) copy-start(bf16[32,768]{1,0:T(8,128)(2,1)} %get-tuple-element.73) | copy-start | bytes 147460
  112.4 9.3 %copy-start.6 = (bf16[32,768]{1,0:T(8,128)(2,1)S(1)}, bf16[32,768]{1,0:T(8,128)(2,1)}, u32[]{:S(2)}) copy-start(bf16[32,768]{1,0:T(8,128)(2,1)} %get-tuple-element.74) | copy-start | bytes 147460
  113.4 17.3 %all-to-all-start.4 = ((bf16[16,48,384]{2,1,0:T(8,128)(2,1)}), bf16[16,48,384]{2,1,0:T(8,128)(2,1)S(1)}, u32[]{:S(2)}, u32[]{:S(2)}) async-start(bf16[16,48,384]{2,1,0:T(8,128)(2,1)} %shard_map.200), calls=%async_computation.4 | async-start | bytes 1179648 | tf_op jit(solution)/shard_map/all_to_all | solution.py:595
  118.3 66.3 %all-gather.5.cloned.1.call-start = ((), (), s32[]{:S(2)}) async-start(), calls=%async_computation.8 | async-start | bytes 1253376 | tf_op jit(solution)/shard_map/all_gather | solution.py:741
  118.3 9.8 %collective-permute-start.13 = (bf16[48,768]{1,0:T(8,128)(2,1)S(1)}, bf16[48,768]{1,0:T(8,128)(2,1)S(1)}, u32[]{:S(2)}, u32[]{:S(2)}) collective-permute-start(bf16[48,768]{1,0:T(8,128)(2,1)S(1)} %copy-done.4), channel_id=1, source_target_pairs={{0,16},{16,0},{1,17},{17,1},{2,18},{18,2},{3,19},{19,3},{4,20},{20... | collective-permute-start | bytes 221192 | tf_op jit(solution)/shard_map/ppermute | solution.py:615
  119.8 10.1 %collective-permute-start.9 = (bf16[32,768]{1,0:T(8,128)(2,1)S(1)}, bf16[32,768]{1,0:T(8,128)(2,1)S(1)}, u32[]{:S(2)}, u32[]{:S(2)}) collective-permute-start(bf16[32,768]{1,0:T(8,128)(2,1)S(1)} %copy-done.8), channel_id=1, source_target_pairs={{0,1},{1,0},{2,3},{3,2},{4,5},{5,4},{6,7},{7,6},{8,9},{9,8},{10,11... | collective-permute-start | bytes 147464 | tf_op jit(solution)/shard_map/ppermute | solution.py:615
  121.7 9.0 %collective-permute-start.10 = (bf16[32,768]{1,0:T(8,128)(2,1)S(1)}, bf16[32,768]{1,0:T(8,128)(2,1)S(1)}, u32[]{:S(2)}, u32[]{:S(2)}) collective-permute-start(bf16[32,768]{1,0:T(8,128)(2,1)S(1)} %copy-done.7), channel_id=1, source_target_pairs={{0,2},{1,3},{2,0},{3,1},{4,6},{5,7},{6,4},{7,5},{8,10},{9,11},{10,... | collective-permute-start | bytes 147464 | tf_op jit(solution)/shard_map/ppermute | solution.py:615
  121.7 9.0 %collective-permute-start.11 = (bf16[32,768]{1,0:T(8,128)(2,1)S(1)}, bf16[32,768]{1,0:T(8,128)(2,1)S(1)}, u32[]{:S(2)}, u32[]{:S(2)}) collective-permute-start(bf16[32,768]{1,0:T(8,128)(2,1)S(1)} %copy-done.6), channel_id=1, source_target_pairs={{0,3},{1,2},{2,1},{3,0},{4,7},{5,6},{6,5},{7,4},{8,11},{9,10},{10,... | collective-permute-start | bytes 147464 | tf_op jit(solution)/shard_map/ppermute | solution.py:615
  133.1 54.2 %all-to-all-start.5 = ((bf16[64,56,384]{2,1,0:T(8,128)(2,1)}), bf16[64,56,384]{2,1,0:T(8,128)(2,1)S(1)}, u32[]{:S(2)}, u32[]{:S(2)}) async-start(bf16[64,56,384]{2,1,0:T(8,128)(2,1)} %bitcast.8), calls=%async_computation.5 | async-start | bytes 5505024 | tf_op jit(solution)/shard_map/all_to_all | solution.py:595
  187.3 10.2 %collective-permute-start.14 = (bf16[8,8,56,384]{3,2,1,0:T(8,128)(2,1)S(1)}, bf16[8,8,56,384]{3,2,1,0:T(8,128)(2,1)}, u32[]{:S(2)}, u32[]{:S(2)}) collective-permute-start(bf16[8,8,56,384]{3,2,1,0:T(8,128)(2,1)S(1)} %shard_map.206.refs_1_.in_ref), channel_id=1, source_target_pairs={{0,8},{8,0},{1,9},{9,1},{2,10},{10,2},{3,11},{11,3},{4,12},{12,4},... | collective-permute-start | bytes 8257544 | tf_op jit(solution)/shard_map/ppermute | solution.py:599
  187.6 21.4 %all-to-all-start.6 = ((bf16[8,64,768]{2,1,0:T(8,128)(2,1)}), bf16[8,64,768]{2,1,0:T(8,128)(2,1)S(1)}, u32[]{:S(2)}, u32[]{:S(2)}) async-start(bf16[8,64,768]{2,1,0:T(8,128)(2,1)} %shard_map.207), calls=%async_computation.6 | async-start | bytes 1572864 | tf_op jit(solution)/shard_map/all_to_all | solution.py:595
  (1 other events, 0.9 us)
Sparse Core Ops, SparseCore 0:
  46.3 34.0 all-gather.2
  129.8 54.7 all-gather.4

commit v12 on v11

--- a/solution.py
+++ b/solution.py
@@ -683,6 +683,7 @@
         [(pieces[0], "L")] + [(piece, "V") for piece in pieces[1:]],
         1000,
     )
+    ff_sums = after(ff_sums, pin(ff_keep))
     grad_send, low, grad_mid, result_part, vec2 = call(
         middle_kernel,
         [
@@ -699,12 +700,13 @@
             pltpu.VMEM((BLK, D), BF), pltpu.VMEM((8, D), F32), DMA((4,)), DMA((8,)), DMA((4,)),
         ],
     )
-    grad_send = after(pin(grad_send), *pieces[1:])
+    far = flip(after(pin(ff_send), pin(low)), "xl", 2, 1)
+    (ff_part,) = call(pair_kernel, [((48, D), BF, "L")], [(ff_keep, "L"), (far, "V")], 1000)
+    ff_all = lax.all_gather(ff_part, WIDE, axis=0, tiled=True)
     grad_same = exchange(grad_send.reshape(32, BLK, 256), (*CHIP, *GROUP)).reshape(8, TOK, 256)
     lows = [flip(low, GROUP, 4, k) for k in (1, 2, 3)]
-    grad_same = after(grad_same, *lows, pin(ff_send))
+    grad_same = after(grad_same, *lows, pin(ff_part))
     grad_other = swap(grad_same)
-    far = flip(ff_send, "xl", 2, 1)
     gqkv, w_own, keep, send = call(
         attend_back_kernel,
         [((TOK, 640), BF, "V"), ((3, D, 384), BF, "V")] + [((16, 48, 384), BF, "V")] * 2,
@@ -737,16 +739,14 @@
         1000,
         [pltpu.VMEM((16, 48, 384), BF), DMA],
     )
-    (ff_part,) = call(pair_kernel, [((48, D), BF, "L")], [(ff_keep, "L"), (far, "V")], 1000)
-    ff_all = lax.all_gather(ff_part, WIDE, axis=0, tiled=True)
     weight_parts = exchange(weight_send, (*CHIP, MICRO))
     parts = [flip(value, GROUP, 4, k + 1) for k, value in enumerate(sends)]
-    weight_parts = after(weight_parts, pin(sums), *parts)
+    weight_parts = after(weight_parts, pin(sums), *parts, pin(ff_all))
     (weight_total,) = call(
         sum_kernel,
         [((8, 8, 56, 384), BF, "H")],
         [(weight_parts, "V"), (sums, "H")],
-        4 * 10**10,
+        1000,
         [pltpu.VMEM((8, 56, 384), BF), pltpu.VMEM((8, D), F32), DMA((8,)), DMA],
     )
     (packed,) = call(
@@ -760,7 +760,7 @@
         [pltpu.VMEM((2 * BLK, D), BF), pltpu.VMEM((BLK, D), BF), DMA((8,)), DMA],
     )
     up_grad, down_grad = call(
-        spread_ff_kernel, [((D, FFL), F32, "L"), ((FFL, D), F32, "L")], [(ff_all, "L")], 5 * 10**10
+        spread_ff_kernel, [((D, FFL), F32, "L"), ((FFL, D), F32, "L")], [(ff_all, "L")], 1000
     )
     weight_same = exchange(weight_total.reshape(64, 56, 384), (*CHIP, *NARROW)).reshape(8, 8, 56, 384)
     weight_same = after(weight_same, pin(packed), pin(up_grad), pin(down_grad))

time: 218 us -> 213 us (0.977)
  waiting for transfers between devices: 88.3 us -> 79.8 us
  Pallas kernels: 48.7 us -> 51.1 us
    all_gather x1, waiting for transfers between devices: 39.3 us -> 0.01 us  [shards(): ff_all = lax.all_gather(ff_part, WIDE, axis=0, tiled=True)]
    all_to_all x7, waiting for transfers between devices: 34.8 us -> 53.9 us  [exchange(): return lax.all_to_all(value, axes, 0, 0, tiled=True)]
    ppermute x10, waiting for transfers between devices: 10 us -> 21.7 us  [flip(): lax.ppermute(value, axes, [(index, index ^ bits) for index in range(count)])]
    pallas_call x18, Pallas kernels: 48.7 us -> 51.1 us  [call(): pl.pallas_call(kernel, out_shape=[(pltpu.HBM if place in 'HL' else jax.Sh...]
  transfers between devices with their start and end apart: 24 -> 24, of which waited for: 13 -> 14; matrix products, arithmetic and copies ran while one was open for 1% -> 1% of each run, Pallas kernels for 16% -> 19%
where the time goes in v12:
time: 213 us
  waiting for transfers between devices  79.8 us (37%)
  starting transfers between devices  65.1 us (31%)
  Pallas kernels  51.1 us (24%)
  between operations  14.3 us (7%)
  local copies, waits for them, and re-layouts  2.28 us (1%)
    all_to_all x7, waiting for transfers between devices, exchange(): return lax.all_to_all(value, axes, 0, 0, tiled=True)  53.9 us
    pallas_call x18, Pallas kernels, call(): pl.pallas_call(kernel, out_shape=[(pltpu.HBM if place in 'HL' else jax.Sh...  51.1 us
    all_to_all x7, starting transfers between devices, exchange(): return lax.all_to_all(value, axes, 0, 0, tiled=True)  43.2 us
    ppermute x10, waiting for transfers between devices, flip(): lax.ppermute(value, axes, [(index, index ^ bits) for index in range(count)])  21.7 us
    ppermute x10, starting transfers between devices, flip(): lax.ppermute(value, axes, [(index, index ^ bits) for index in range(count)])  12.4 us
    ppermute x5, starting transfers between devices, swap(): return lax.ppermute(value, CORE, [(0, 1), (1, 0)])  9.53 us
  transfers between devices with their start and end apart: 24, of which 14 were waited for; matrix products, arithmetic and copies ran while one was open for 1% of the time, Pallas kernels for 19%

profile of v12, /device:TPU:1, one launch (start us, length us, event | category | flops | bytes accessed | tf_op | source)
XLA Modules:
  0.0 212.6 jit_solution(15640433433867736431)
XLA Ops:
  7.2 3.7 %shard_map.186 = (bf16[8,128,384]{2,1,0:T(8,128)(2,1)}, bf16[128,768]{1,0:T(8,128)(2,1)}) custom-call(bf16[2,128,768]{2,1,0:T(8,128)(2,1)} %tok_ref.7, f32[768]{0:T(1024)} %gain_ref.7, f32[768]{0:T(1024)} %shift_ref.2, bf16[768,2304]{1,0:T(8,128)(2,1)} %w_ref.5), custom_call_target="tpu_custom_call" | custom-call | flops 1000 | bytes 1000 | tf_op jit(solution)/shard_map/pallas_call | solution.py:106
  10.9 6.0 %all-to-all-start = ((bf16[8,128,384]{2,1,0:T(8,128)(2,1)}), bf16[8,128,384]{2,1,0:T(8,128)(2,1)S(1)}, u32[]{:S(2)}, u32[]{:S(2)}) async-start(bf16[8,128,384]{2,1,0:T(8,128)(2,1)} %get-tuple-element.52), calls=%async_computation | async-start | bytes 1572864 | tf_op jit(solution)/shard_map/all_to_all | solution.py:595
  16.9 3.0 %shard_map.187.refs_1_.refs_0_.q_ref = bf16[128,256]{1,0:T(8,128)(2,1)} custom-call(bf16[128,768]{1,0:T(8,128)(2,1)} %get-tuple-element.53.normed_ref, bf16[768,2304]{1,0:T(8,128)(2,1)} %w_ref.5), custom_call_target="tpu_custom_call" | custom-call | flops 1000 | bytes 1000 | tf_op jit(solution)/shard_map/pallas_call | solution.py:106
  19.9 8.6 %all-to-all-done.refs_0_ = bf16[8,128,384]{2,1,0:T(8,128)(2,1)S(1)} async-done(((bf16[8,128,384]{2,1,0:T(8,128)(2,1)}), bf16[8,128,384]{2,1,0:T(8,128)(2,1)S(1)}, u32[]{:S(2)}, u32[]{:S(2)}) %all-to-all-start) | async-done | bytes 786464 | tf_op jit(solution)/shard_map/all_to_all | solution.py:595
  32.6 4.0 %shard_map.190 = bf16[8,128,256]{2,1,0:T(8,128)(2,1)} custom-call(s32[2,32]{1,0:T(2,128)S(1)} %copy-done.3, bf16[128,256]{1,0:T(8,128)(2,1)} %shard_map.187.refs_1_.refs_0_.q_ref, bf16[8,128,384]{2,1,0:T(8,128)(2,1)S(1)} %shard_map.188.refs_1_.same_ref.kvs_ref, bf16[8,128,384]{2,1,0:T(8,128)(2,1)S(1)} %collective-permute-done.other_ref.kvo_ref), custom_call_target="tpu_custom_call" | custom-call | flops 1000 | bytes 1000 | tf_op jit(solution)/shard_map/pallas_call | solution.py:106
  38.2 7.2 %all-to-all-start.1 = ((bf16[8,128,256]{2,1,0:T(8,128)(2,1)}), bf16[8,128,256]{2,1,0:T(8,128)(2,1)S(1)}, u32[]{:S(2)}, u32[]{:S(2)}) async-start(bf16[8,128,256]{2,1,0:T(8,128)(2,1)} %shard_map.190), calls=%async_computation.1 | async-start | bytes 1048576 | tf_op jit(solution)/shard_map/all_to_all | solution.py:595
  46.8 10.1 %all-to-all-done.1.mixed_ref = bf16[8,128,256]{2,1,0:T(8,128)(2,1)S(1)} async-done(((bf16[8,128,256]{2,1,0:T(8,128)(2,1)}), bf16[8,128,256]{2,1,0:T(8,128)(2,1)S(1)}, u32[]{:S(2)}, u32[]{:S(2)}) %all-to-all-start.1) | async-done | bytes 524320 | tf_op jit(solution)/shard_map/all_to_all | solution.py:595
  56.9 4.1 %shard_map.191 = (bf16[8,64,768]{2,1,0:T(8,128)(2,1)}, f32[32,768]{1,0:T(8,128)}, bf16[256,768]{1,0:T(8,128)(2,1)S(1)}, bf16[256,384]{1,0:T(8,128)(2,1)S(1)}, bf16[256,384]{1,0:T(8,128)(2,1)S(1)}) custom-call(bf16[8,128,256]{2,1,0:T(8,128)(2,1)S(1)} %all-to-all-done.1.mixed_ref, bf16[2,128,768]{2,1,0:T(8,128)(2,1)} %tok_ref.7, bf16[2,128,768]{2,1,0:T(8,128)(2,1)} %og_ref.5, ...), custom_call_target="tpu_custom_call" | custom-call | flops 1000 | bytes 1000 | tf_op jit(solution)/shard_map/pallas_call | solution.py:106
  61.0 2.8 %shard_map.192 = (bf16[8,48,768]{2,1,0:T(8,128)(2,1)S(1)}, bf16[8,48,768]{2,1,0:T(8,128)(2,1)}) custom-call(bf16[256,768]{1,0:T(8,128)(2,1)S(1)} %get-tuple-element.55.normed_ref, bf16[256,384]{1,0:T(8,128)(2,1)S(1)} %get-tuple-element.56.act_ref, bf16[256,384]{1,0:T(8,128)(2,1)S(1)} %get-tuple-element.57.gpre_ref, bf16[2,128,768]{2,1,0:T(8,128)(2,1)} %og_ref.5), custom_call_target="tpu_custom_call" | custom-call | flops 1000 | bytes 1000 | tf_op jit(solution)/shard_map/pallas_call | solution.py:106
  65.9 3.5 %all-to-all-start.2 = ((bf16[8,64,768]{2,1,0:T(8,128)(2,1)}), bf16[8,64,768]{2,1,0:T(8,128)(2,1)S(1)}, u32[]{:S(2)}, u32[]{:S(2)}) async-start(bf16[8,64,768]{2,1,0:T(8,128)(2,1)} %get-tuple-element.54), calls=%async_computation.2 | async-start | bytes 1572864 | tf_op jit(solution)/shard_map/all_to_all | solution.py:595
  71.4 3.9 %collective-permute-start.4 = (bf16[2,48,768]{2,1,0:T(8,128)(2,1)}, bf16[2,48,768]{2,1,0:T(8,128)(2,1)S(1)}, u32[]{:S(2)}, u32[]{:S(2)}) collective-permute-start(bf16[2,48,768]{2,1,0:T(8,128)(2,1)} %get-tuple-element.63), channel_id=1, source_target_pairs={{0,96},{32,64},{64,32},{96,0},{1,97},{33,65},{65,33},{97,1},{2,98}... | collective-permute-start | bytes 442376 | tf_op jit(solution)/shard_map/ppermute | solution.py:615
  78.6 3.4 %collective-permute-done.4.refs_3_ = bf16[2,48,768]{2,1,0:T(8,128)(2,1)S(1)} collective-permute-done((bf16[2,48,768]{2,1,0:T(8,128)(2,1)}, bf16[2,48,768]{2,1,0:T(8,128)(2,1)S(1)}, u32[]{:S(2)}, u32[]{:S(2)}) %collective-permute-start.4) | collective-permute-done | bytes 147488 | tf_op jit(solution)/shard_map/ppermute | solution.py:615
  84.0 2.7 %shard_map.196 = (bf16[8,4,32,256]{3,2,1,0:T(8,128)(2,1)}, bf16[32,768]{1,0:T(8,128)(2,1)}, f32[32,768]{1,0:T(8,128)}, bf16[32,768]{1,0:T(8,128)(2,1)}, f32[8,768]{1,0:T(8,128)}) custom-call(bf16[8,64,768]{2,1,0:T(8,128)(2,1)S(1)} %shard_map.195.sums_ref, f32[32,768]{1,0:T(8,128)} %get-tuple-element.65.middle_ref, bf16[2,128,768]{2,1,0:T(8,128)(2,1)} %og_ref.5, ...), custom_call_target="tpu_custom_call" | custom-call | flops 1000 | bytes 1000 | tf_op jit(solution)/shard_map/pallas_call | solution.py:106
  86.8 8.0 %all-to-all-start.3 = ((bf16[32,32,256]{2,1,0:T(8,128)(2,1)}), bf16[32,32,256]{2,1,0:T(8,128)(2,1)S(1)}, u32[]{:S(2)}, u32[]{:S(2)}) async-start(bf16[32,32,256]{2,1,0:T(8,128)(2,1)} %bitcast.11), calls=%async_computation.3 | async-start | bytes 1048576 | tf_op jit(solution)/shard_map/all_to_all | solution.py:595
  96.5 3.7 %collective-permute-start.7 = (bf16[32,768]{1,0:T(8,128)(2,1)}, bf16[32,768]{1,0:T(8,128)(2,1)S(1)}, u32[]{:S(2)}, u32[]{:S(2)}) collective-permute-start(bf16[32,768]{1,0:T(8,128)(2,1)} %get-tuple-element.67.refs_1_.low_ref), channel_id=1, source_target_pairs={{0,3},{1,2},{2,1},{3,0},{4,7},{5,6},{6,5},{7,4},{8,11},{9,10},{10,... | collective-permute-start | bytes 147464 | tf_op jit(solution)/shard_map/ppermute | solution.py:615
  100.7 3.4 %collective-permute-done.7.refs_3_.low3_ref = bf16[32,768]{1,0:T(8,128)(2,1)S(1)} collective-permute-done((bf16[32,768]{1,0:T(8,128)(2,1)}, bf16[32,768]{1,0:T(8,128)(2,1)S(1)}, u32[]{:S(2)}, u32[]{:S(2)}) %collective-permute-start.7) | collective-permute-done | bytes 49184 | tf_op jit(solution)/shard_map/ppermute | solution.py:615
  104.1 3.4 %collective-permute-done.6.refs_2_.low2_ref = bf16[32,768]{1,0:T(8,128)(2,1)S(1)} collective-permute-done((bf16[32,768]{1,0:T(8,128)(2,1)}, bf16[32,768]{1,0:T(8,128)(2,1)S(1)}, u32[]{:S(2)}, u32[]{:S(2)}) %collective-permute-start.6) | collective-permute-done | bytes 49184 | tf_op jit(solution)/shard_map/ppermute | solution.py:615
  110.3 5.9 %shard_map.200 = (bf16[128,640]{1,0:T(8,128)(2,1)S(1)}, bf16[3,768,384]{2,1,0:T(8,128)(2,1)S(1)}, bf16[16,48,384]{2,1,0:T(8,128)(2,1)S(1)}, bf16[16,48,384]{2,1,0:T(8,128)(2,1)S(1)}) custom-call(s32[2,32]{1,0:T(2,128)S(1)} %copy-done.3, bf16[8,128,384]{2,1,0:T(8,128)(2,1)} %copy-done, bf16[8,128,384]{2,1,0:T(8,128)(2,1)} %copy-done.2, ...), custom_call_target="tpu_custom_call" | custom-call | flops 1000000000 | bytes 1000 | tf_op jit(solution)/shard_map/pallas_call | solution.py:106
  120.1 6.2 %all-to-all-start.4 = ((bf16[16,48,384]{2,1,0:T(8,128)(2,1)}), bf16[16,48,384]{2,1,0:T(8,128)(2,1)S(1)}, u32[]{:S(2)}, u32[]{:S(2)}) async-start(bf16[16,48,384]{2,1,0:T(8,128)(2,1)} %shard_map.202), calls=%async_computation.4 | async-start | bytes 1179648 | tf_op jit(solution)/shard_map/all_to_all | solution.py:595
  127.3 3.3 %collective-permute-start.12 = (bf16[32,768]{1,0:T(8,128)(2,1)S(1)}, bf16[32,768]{1,0:T(8,128)(2,1)S(1)}, u32[]{:S(2)}, u32[]{:S(2)}) collective-permute-start(bf16[32,768]{1,0:T(8,128)(2,1)S(1)} %copy-done.4), channel_id=1, source_target_pairs={{0,3},{1,2},{2,1},{3,0},{4,7},{5,6},{6,5},{7,4},{8,11},{9,10},{10,... | collective-permute-start | bytes 147464 | tf_op jit(solution)/shard_map/ppermute | solution.py:615
  130.5 5.2 %collective-permute-done.10.refs_2_.one_ref = bf16[32,768]{1,0:T(8,128)(2,1)S(1)} collective-permute-done((bf16[32,768]{1,0:T(8,128)(2,1)S(1)}, bf16[32,768]{1,0:T(8,128)(2,1)S(1)}, u32[]{:S(2)}, u32[]{:S(2)}) %collective-permute-start.10) | collective-permute-done | bytes 49184 | tf_op jit(solution)/shard_map/ppermute | solution.py:615
  135.8 2.8 %collective-permute-done.12.refs_4_.three_ref = bf16[32,768]{1,0:T(8,128)(2,1)S(1)} collective-permute-done((bf16[32,768]{1,0:T(8,128)(2,1)S(1)}, bf16[32,768]{1,0:T(8,128)(2,1)S(1)}, u32[]{:S(2)}, u32[]{:S(2)}) %collective-permute-start.12) | collective-permute-done | bytes 49184 | tf_op jit(solution)/shard_map/ppermute | solution.py:615
  138.6 2.4 %shard_map.204.unused_ref = bf16[8,8,56,384]{3,2,1,0:T(8,128)(2,1)} custom-call(bf16[16,48,384]{2,1,0:T(8,128)(2,1)S(1)} %shard_map.203.in_ref, f32[8,768]{1,0:T(8,128)} %get-tuple-element.80.refs_1_.vec_ref), custom_call_target="tpu_custom_call" | custom-call | flops 1000 | bytes 1000 | tf_op jit(solution)/shard_map/pallas_call | solution.py:106
  141.0 8.5 %all-to-all-start.5 = ((bf16[64,56,384]{2,1,0:T(8,128)(2,1)}), bf16[64,56,384]{2,1,0:T(8,128)(2,1)S(1)}, u32[]{:S(2)}, u32[]{:S(2)}) async-start(bf16[64,56,384]{2,1,0:T(8,128)(2,1)} %bitcast.8), calls=%async_computation.5 | async-start | bytes 5505024 | tf_op jit(solution)/shard_map/all_to_all | solution.py:595
  149.5 2.8 %shard_map.206 = (f32[768,384]{1,0:T(8,128)}, f32[384,768]{1,0:T(8,128)}) custom-call(bf16[768,768]{1,0:T(8,128)(2,1)} %all-gather.5.cloned.1.call-done.refs_5_.in_ref), custom_call_target="tpu_custom_call" | custom-call | flops 1000 | bytes 1000 | tf_op jit(solution)/shard_map/pallas_call | solution.py:106
  152.2 3.0 %shard_map.205.refs_1_.refs_0_ = bf16[8,64,768]{2,1,0:T(8,128)(2,1)} custom-call(f32[32,768]{1,0:T(8,128)} %get-tuple-element.72.unused_ref.own_ref, bf16[32,768]{1,0:T(8,128)(2,1)S(1)} %collective-permute-done.10.refs_2_.one_ref, bf16[32,768]{1,0:T(8,128)(2,1)S(1)} %collective-permute-done.11.refs_3_.two_ref, ...), custom_call_target="tpu_custom_call" | custom-call | flops 1000 | bytes 1000 | tf_op jit(solution)/shard_map/pallas_call | solution.py:106
  155.2 28.0 %all-to-all-done.5 = bf16[64,56,384]{2,1,0:T(8,128)(2,1)S(1)} async-done(((bf16[64,56,384]{2,1,0:T(8,128)(2,1)}), bf16[64,56,384]{2,1,0:T(8,128)(2,1)S(1)}, u32[]{:S(2)}, u32[]{:S(2)}) %all-to-all-start.5) | async-done | bytes 2752544 | tf_op jit(solution)/shard_map/all_to_all | solution.py:595
  183.2 3.5 %collective-permute-start.14 = (bf16[8,8,56,384]{3,2,1,0:T(8,128)(2,1)S(1)}, bf16[8,8,56,384]{3,2,1,0:T(8,128)(2,1)}, u32[]{:S(2)}, u32[]{:S(2)}) collective-permute-start(bf16[8,8,56,384]{3,2,1,0:T(8,128)(2,1)S(1)} %shard_map.207.refs_1_.in_ref), channel_id=1, source_target_pairs={{0,8},{8,0},{1,9},{9,1},{2,10},{10,2},{3,11},{11,3},{4,12},{12,4},... | collective-permute-start | bytes 8257544 | tf_op jit(solution)/shard_map/ppermute | solution.py:599
  186.8 3.7 %all-to-all-start.6 = ((bf16[8,64,768]{2,1,0:T(8,128)(2,1)}), bf16[8,64,768]{2,1,0:T(8,128)(2,1)S(1)}, u32[]{:S(2)}, u32[]{:S(2)}) async-start(bf16[8,64,768]{2,1,0:T(8,128)(2,1)} %shard_map.208), calls=%async_computation.6 | async-start | bytes 1572864 | tf_op jit(solution)/shard_map/all_to_all | solution.py:595
  190.5 2.4 %shard_map.209 = (f32[768,2304]{1,0:T(8,128)}, f32[768,768]{1,0:T(8,128)}, f32[8,384]{1,0:T(8,128)S(1)}) custom-call(bf16[8,8,56,384]{3,2,1,0:T(8,128)(2,1)S(1)} %shard_map.207.refs_1_.in_ref), custom_call_target="tpu_custom_call" | custom-call | flops 1000 | bytes 1000 | tf_op jit(solution)/shard_map/pallas_call | solution.py:106
  192.9 4.8 %shard_map.210 = (f32[768,2304]{1,0:T(8,128)}, f32[768,768]{1,0:T(8,128)}, f32[768]{0:T(1024)}, f32[768]{0:T(1024)}, f32[768]{0:T(1024)}, /*index=5*/f32[768]{0:T(1024)}) custom-call(bf16[8,8,56,384]{3,2,1,0:T(8,128)(2,1)} %collective-permute-done.14.in_ref, f32[8,384]{1,0:T(8,128)S(1)} %get-tuple-element.83.refs_0_, ...), custom_call_target="tpu_custom_call", output_to_operand_aliasing={{0}: (2, {}), {1}: (3, {})} | custom-call | flops 1000 | bytes 1000 | tf_op jit(solution)/shard_map/pallas_call | solution.py:106
  197.8 6.9 %all-to-all-done.6.in_ref = bf16[8,64,768]{2,1,0:T(8,128)(2,1)S(1)} async-done(((bf16[8,64,768]{2,1,0:T(8,128)(2,1)}), bf16[8,64,768]{2,1,0:T(8,128)(2,1)S(1)}, u32[]{:S(2)}, u32[]{:S(2)}) %all-to-all-start.6) | async-done | bytes 786464 | tf_op jit(solution)/shard_map/all_to_all | solution.py:595
  (59 shorter events, 27.2 us)
Async XLA Ops:
  10.9 17.6 %all-to-all-start = ((bf16[8,128,384]{2,1,0:T(8,128)(2,1)}), bf16[8,128,384]{2,1,0:T(8,128)(2,1)S(1)}, u32[]{:S(2)}, u32[]{:S(2)}) async-start(bf16[8,128,384]{2,1,0:T(8,128)(2,1)} %get-tuple-element.52), calls=%async_computation | async-start | bytes 1572864 | tf_op jit(solution)/shard_map/all_to_all | solution.py:595
  16.8 15.8 %copy-start.3 = (s32[2,32]{1,0:T(2,128)S(1)}, s32[2,32]{1,0:T(2,128)}, u32[]{:S(2)}) copy-start(s32[2,32]{1,0:T(2,128)} %scene_ref.3) | copy-start | bytes 772
  28.5 18.3 %copy-start = (bf16[8,128,384]{2,1,0:T(8,128)(2,1)}, bf16[8,128,384]{2,1,0:T(8,128)(2,1)S(1)}, u32[]{:S(2)}) copy-start(bf16[8,128,384]{2,1,0:T(8,128)(2,1)S(1)} %shard_map.188.refs_1_.same_ref.kvs_ref) | copy-start | bytes 2359300
  28.5 4.1 %collective-permute-start = (bf16[8,128,384]{2,1,0:T(8,128)(2,1)S(1)}, bf16[8,128,384]{2,1,0:T(8,128)(2,1)S(1)}, u32[]{:S(2)}, u32[]{:S(2)}) collective-permute-start(bf16[8,128,384]{2,1,0:T(8,128)(2,1)S(1)} %shard_map.188.refs_1_.same_ref.kvs_ref), channel_id=1, source_target_pairs={{0,8},{8,0},{1,9},{9,1},{2,10},{10,2},{3,11},{11,3},{4,12},{12,4},... | collective-permute-start | bytes 2359304 | tf_op jit(solution)/shard_map/ppermute | solution.py:599
  36.6 0.9 copy-start.2
  37.5 71.3 %all-gather.3.cloned.1.call-start = ((), (), s32[]{:S(2)}) async-start(), calls=%async_computation.7 | async-start | bytes 1114112 | tf_op jit(solution)/shard_map/all_gather | solution.py:650
  38.2 18.7 %all-to-all-start.1 = ((bf16[8,128,256]{2,1,0:T(8,128)(2,1)}), bf16[8,128,256]{2,1,0:T(8,128)(2,1)S(1)}, u32[]{:S(2)}, u32[]{:S(2)}) async-start(bf16[8,128,256]{2,1,0:T(8,128)(2,1)} %shard_map.190), calls=%async_computation.1 | async-start | bytes 1048576 | tf_op jit(solution)/shard_map/all_to_all | solution.py:595
  56.9 6.9 %copy-start.1 = (bf16[8,128,256]{2,1,0:T(8,128)(2,1)}, bf16[8,128,256]{2,1,0:T(8,128)(2,1)S(1)}, u32[]{:S(2)}) copy-start(bf16[8,128,256]{2,1,0:T(8,128)(2,1)S(1)} %all-to-all-done.1.mixed_ref) | copy-start | bytes 1572868
  63.8 5.7 %collective-permute-start.1 = (bf16[8,48,768]{2,1,0:T(8,128)(2,1)}, bf16[8,48,768]{2,1,0:T(8,128)(2,1)}, u32[]{:S(2)}, u32[]{:S(2)}) collective-permute-start(bf16[8,48,768]{2,1,0:T(8,128)(2,1)} %get-tuple-element.59), channel_id=1, source_target_pairs={{0,8},{8,0},{1,9},{9,1},{2,10},{10,2},{3,11},{11,3},{4,12},{12,4},... | collective-permute-start | bytes 1769480 | tf_op jit(solution)/shard_map/ppermute | solution.py:599
  65.9 18.1 %all-to-all-start.2 = ((bf16[8,64,768]{2,1,0:T(8,128)(2,1)}), bf16[8,64,768]{2,1,0:T(8,128)(2,1)S(1)}, u32[]{:S(2)}, u32[]{:S(2)}) async-start(bf16[8,64,768]{2,1,0:T(8,128)(2,1)} %get-tuple-element.54), calls=%async_computation.2 | async-start | bytes 1572864 | tf_op jit(solution)/shard_map/all_to_all | solution.py:595
  71.4 5.7 %collective-permute-start.2 = (bf16[2,48,768]{2,1,0:T(8,128)(2,1)}, bf16[2,48,768]{2,1,0:T(8,128)(2,1)S(1)}, u32[]{:S(2)}, u32[]{:S(2)}) collective-permute-start(bf16[2,48,768]{2,1,0:T(8,128)(2,1)} %get-tuple-element.61), channel_id=1, source_target_pairs={{0,32},{32,0},{64,96},{96,64},{1,33},{33,1},{65,97},{97,65},{2,34}... | collective-permute-start | bytes 442376 | tf_op jit(solution)/shard_map/ppermute | solution.py:615
  71.4 7.2 %collective-permute-start.3 = (bf16[2,48,768]{2,1,0:T(8,128)(2,1)}, bf16[2,48,768]{2,1,0:T(8,128)(2,1)S(1)}, u32[]{:S(2)}, u32[]{:S(2)}) collective-permute-start(bf16[2,48,768]{2,1,0:T(8,128)(2,1)} %get-tuple-element.62), channel_id=1, source_target_pairs={{0,64},{32,96},{64,0},{96,32},{1,65},{33,97},{65,1},{97,33},{2,66}... | collective-permute-start | bytes 442376 | tf_op jit(solution)/shard_map/ppermute | solution.py:615
  71.4 10.7 %collective-permute-start.4 = (bf16[2,48,768]{2,1,0:T(8,128)(2,1)}, bf16[2,48,768]{2,1,0:T(8,128)(2,1)S(1)}, u32[]{:S(2)}, u32[]{:S(2)}) collective-permute-start(bf16[2,48,768]{2,1,0:T(8,128)(2,1)} %get-tuple-element.63), channel_id=1, source_target_pairs={{0,96},{32,64},{64,32},{96,0},{1,97},{33,65},{65,33},{97,1},{2,98}... | collective-permute-start | bytes 442376 | tf_op jit(solution)/shard_map/ppermute | solution.py:615
  86.7 8.2 %collective-permute-start.8 = (bf16[48,768]{1,0:T(8,128)(2,1)}, bf16[48,768]{1,0:T(8,128)(2,1)S(1)}, u32[]{:S(2)}, u32[]{:S(2)}) collective-permute-start(bf16[48,768]{1,0:T(8,128)(2,1)} %shard_map.197), channel_id=1, source_target_pairs={{0,16},{16,0},{1,17},{17,1},{2,18},{18,2},{3,19},{19,3},{4,20},{20... | collective-permute-start | bytes 221192 | tf_op jit(solution)/shard_map/ppermute | solution.py:615
  86.8 20.8 %all-to-all-start.3 = ((bf16[32,32,256]{2,1,0:T(8,128)(2,1)}), bf16[32,32,256]{2,1,0:T(8,128)(2,1)S(1)}, u32[]{:S(2)}, u32[]{:S(2)}) async-start(bf16[32,32,256]{2,1,0:T(8,128)(2,1)} %bitcast.11), calls=%async_computation.3 | async-start | bytes 1048576 | tf_op jit(solution)/shard_map/all_to_all | solution.py:595
  94.8 43.8 %all-gather.5.cloned.1.call-start = ((), (), s32[]{:S(2)}) async-start(), calls=%async_computation.8 | async-start | bytes 1253376 | tf_op jit(solution)/shard_map/all_gather | solution.py:705
  96.5 7.6 %collective-permute-start.7 = (bf16[32,768]{1,0:T(8,128)(2,1)}, bf16[32,768]{1,0:T(8,128)(2,1)S(1)}, u32[]{:S(2)}, u32[]{:S(2)}) collective-permute-start(bf16[32,768]{1,0:T(8,128)(2,1)} %get-tuple-element.67.refs_1_.low_ref), channel_id=1, source_target_pairs={{0,3},{1,2},{2,1},{3,0},{4,7},{5,6},{6,5},{7,4},{8,11},{9,10},{10,... | collective-permute-start | bytes 147464 | tf_op jit(solution)/shard_map/ppermute | solution.py:615
  100.2 7.4 %collective-permute-start.6 = (bf16[32,768]{1,0:T(8,128)(2,1)}, bf16[32,768]{1,0:T(8,128)(2,1)S(1)}, u32[]{:S(2)}, u32[]{:S(2)}) collective-permute-start(bf16[32,768]{1,0:T(8,128)(2,1)} %get-tuple-element.67.refs_1_.low_ref), channel_id=1, source_target_pairs={{0,2},{1,3},{2,0},{3,1},{4,6},{5,7},{6,4},{7,5},{8,10},{9,11},{10,... | collective-permute-start | bytes 147464 | tf_op jit(solution)/shard_map/ppermute | solution.py:615
  100.5 7.1 %collective-permute-start.5 = (bf16[32,768]{1,0:T(8,128)(2,1)}, bf16[32,768]{1,0:T(8,128)(2,1)S(1)}, u32[]{:S(2)}, u32[]{:S(2)}) collective-permute-start(bf16[32,768]{1,0:T(8,128)(2,1)} %get-tuple-element.67.refs_1_.low_ref), channel_id=1, source_target_pairs={{0,1},{1,0},{2,3},{3,2},{4,5},{5,4},{6,7},{7,6},{8,9},{9,8},{10,11... | collective-permute-start | bytes 147464 | tf_op jit(solution)/shard_map/ppermute | solution.py:615
  107.6 2.8 %collective-permute-start.9 = (bf16[8,128,256]{2,1,0:T(8,128)(2,1)S(1)}, bf16[8,128,256]{2,1,0:T(8,128)(2,1)S(1)}, u32[]{:S(2)}, u32[]{:S(2)}) collective-permute-start(bf16[8,128,256]{2,1,0:T(8,128)(2,1)S(1)} %shard_map.199.gs_ref), channel_id=1, source_target_pairs={{0,8},{8,0},{1,9},{9,1},{2,10},{10,2},{3,11},{11,3},{4,12},{12,4},... | collective-permute-start | bytes 1572872 | tf_op jit(solution)/shard_map/ppermute | solution.py:599
  116.3 2.8 %collective-permute-start.13 = (bf16[16,48,384]{2,1,0:T(8,128)(2,1)S(1)}, bf16[16,48,384]{2,1,0:T(8,128)(2,1)S(1)}, u32[]{:S(2)}, u32[]{:S(2)}) collective-permute-start(bf16[16,48,384]{2,1,0:T(8,128)(2,1)S(1)} %get-tuple-element.79), channel_id=1, source_target_pairs={{0,8},{8,0},{1,9},{9,1},{2,10},{10,2},{3,11},{11,3},{4,12},{12,4},... | collective-permute-start | bytes 1769480 | tf_op jit(solution)/shard_map/ppermute | solution.py:599
  119.1 7.2 %copy-start.6 = (bf16[32,768]{1,0:T(8,128)(2,1)S(1)}, bf16[32,768]{1,0:T(8,128)(2,1)}, u32[]{:S(2)}) copy-start(bf16[32,768]{1,0:T(8,128)(2,1)} %get-tuple-element.73) | copy-start | bytes 147460
  119.1 7.6 %copy-start.5 = (bf16[32,768]{1,0:T(8,128)(2,1)S(1)}, bf16[32,768]{1,0:T(8,128)(2,1)}, u32[]{:S(2)}) copy-start(bf16[32,768]{1,0:T(8,128)(2,1)} %get-tuple-element.74) | copy-start | bytes 147460
  119.1 8.2 %copy-start.4 = (bf16[32,768]{1,0:T(8,128)(2,1)S(1)}, bf16[32,768]{1,0:T(8,128)(2,1)}, u32[]{:S(2)}) copy-start(bf16[32,768]{1,0:T(8,128)(2,1)} %get-tuple-element.75) | copy-start | bytes 147460
  120.1 18.5 %all-to-all-start.4 = ((bf16[16,48,384]{2,1,0:T(8,128)(2,1)}), bf16[16,48,384]{2,1,0:T(8,128)(2,1)S(1)}, u32[]{:S(2)}, u32[]{:S(2)}) async-start(bf16[16,48,384]{2,1,0:T(8,128)(2,1)} %shard_map.202), calls=%async_computation.4 | async-start | bytes 1179648 | tf_op jit(solution)/shard_map/all_to_all | solution.py:595
  126.3 9.5 %collective-permute-start.10 = (bf16[32,768]{1,0:T(8,128)(2,1)S(1)}, bf16[32,768]{1,0:T(8,128)(2,1)S(1)}, u32[]{:S(2)}, u32[]{:S(2)}) collective-permute-start(bf16[32,768]{1,0:T(8,128)(2,1)S(1)} %copy-done.6), channel_id=1, source_target_pairs={{0,1},{1,0},{2,3},{3,2},{4,5},{5,4},{6,7},{7,6},{8,9},{9,8},{10,11... | collective-permute-start | bytes 147464 | tf_op jit(solution)/shard_map/ppermute | solution.py:615
  126.7 9.1 %collective-permute-start.11 = (bf16[32,768]{1,0:T(8,128)(2,1)S(1)}, bf16[32,768]{1,0:T(8,128)(2,1)S(1)}, u32[]{:S(2)}, u32[]{:S(2)}) collective-permute-start(bf16[32,768]{1,0:T(8,128)(2,1)S(1)} %copy-done.5), channel_id=1, source_target_pairs={{0,2},{1,3},{2,0},{3,1},{4,6},{5,7},{6,4},{7,5},{8,10},{9,11},{10,... | collective-permute-start | bytes 147464 | tf_op jit(solution)/shard_map/ppermute | solution.py:615
  127.3 11.3 %collective-permute-start.12 = (bf16[32,768]{1,0:T(8,128)(2,1)S(1)}, bf16[32,768]{1,0:T(8,128)(2,1)S(1)}, u32[]{:S(2)}, u32[]{:S(2)}) collective-permute-start(bf16[32,768]{1,0:T(8,128)(2,1)S(1)} %copy-done.4), channel_id=1, source_target_pairs={{0,3},{1,2},{2,1},{3,0},{4,7},{5,6},{6,5},{7,4},{8,11},{9,10},{10,... | collective-permute-start | bytes 147464 | tf_op jit(solution)/shard_map/ppermute | solution.py:615
  141.0 42.2 %all-to-all-start.5 = ((bf16[64,56,384]{2,1,0:T(8,128)(2,1)}), bf16[64,56,384]{2,1,0:T(8,128)(2,1)S(1)}, u32[]{:S(2)}, u32[]{:S(2)}) async-start(bf16[64,56,384]{2,1,0:T(8,128)(2,1)} %bitcast.8), calls=%async_computation.5 | async-start | bytes 5505024 | tf_op jit(solution)/shard_map/all_to_all | solution.py:595
  183.2 9.7 %collective-permute-start.14 = (bf16[8,8,56,384]{3,2,1,0:T(8,128)(2,1)S(1)}, bf16[8,8,56,384]{3,2,1,0:T(8,128)(2,1)}, u32[]{:S(2)}, u32[]{:S(2)}) collective-permute-start(bf16[8,8,56,384]{3,2,1,0:T(8,128)(2,1)S(1)} %shard_map.207.refs_1_.in_ref), channel_id=1, source_target_pairs={{0,8},{8,0},{1,9},{9,1},{2,10},{10,2},{3,11},{11,3},{4,12},{12,4},... | collective-permute-start | bytes 8257544 | tf_op jit(solution)/shard_map/ppermute | solution.py:599
  186.8 18.0 %all-to-all-start.6 = ((bf16[8,64,768]{2,1,0:T(8,128)(2,1)}), bf16[8,64,768]{2,1,0:T(8,128)(2,1)S(1)}, u32[]{:S(2)}, u32[]{:S(2)}) async-start(bf16[8,64,768]{2,1,0:T(8,128)(2,1)} %shard_map.208), calls=%async_computation.6 | async-start | bytes 1572864 | tf_op jit(solution)/shard_map/all_to_all | solution.py:595
Sparse Core Ops, SparseCore 0:
  40.0 32.3 all-gather.2
  97.4 37.1 all-gather.4

commit v13 on v12

--- a/solution.py
+++ b/solution.py
@@ -176,6 +176,21 @@
     weight_copies(w_ref, w_buf, w_sem, (0,))[0].wait()
     part = own_heads(mm(normed_ref[...], w_buf[0]))
     q_ref[...] = jnp.concatenate([part, jnp.zeros((TOK, HD), BF)], axis=1)
+
+
+def block_query_kernel(normed_ref, w_ref, out_ref, x_buf, w_buf, x_sem, w_sem):
+    block = pl.ds(pl.multiple_of(group_index() * BLK, BLK), BLK)
+    loads = [
+        pltpu.make_async_copy(normed_ref.at[block], x_buf, x_sem),
+        pltpu.make_async_copy(w_ref.at[:, pl.ds(0, D)], w_buf, w_sem),
+    ]
+    for load in loads:
+        load.start()
+    wait_all(loads)
+    query = mm(x_buf[...], w_buf[...]).astype(BF)
+    zero = jnp.zeros((BLK, HD), BF)
+    for group in range(4):
+        out_ref[group] = jnp.concatenate([query[:, group * 192:(group + 1) * 192], zero], axis=1)
 
 
 def attend_kernel(scene_ref, q_ref, same_ref, other_ref, out_ref, buf, q_buf, sem, q_sem):
@@ -302,9 +317,9 @@
 
 
 def middle_kernel(
-    sums_ref, middle_ref, og_ref, mixed_ref, wo_ref, gain_ref,
+    sums_ref, middle_ref, og_ref, mixed_ref, wo_ref, gain_ref, query_ref,
     out_ref, low_ref, grad_ref, result_ref, vec_ref,
-    buf, middle_buf, og_buf, mixed_buf, gain_buf, low_buf, grad_buf, result_buf, vec_buf, in_sem, sem, rest_sem,
+    buf, middle_buf, og_buf, mixed_buf, gain_buf, query_buf, low_buf, grad_buf, result_buf, vec_buf, in_sem, sem, rest_sem,
 ):
     micro = lax.axis_index(MICRO)
     group = group_index()
@@ -314,6 +329,7 @@
         pltpu.make_async_copy(og_ref.at[micro, block], og_buf, in_sem.at[1]),
         pltpu.make_async_copy(mixed_ref.at[pl.ds(micro * 4, 4), block], mixed_buf, in_sem.at[2]),
         pltpu.make_async_copy(gain_ref, gain_buf, in_sem.at[3]),
+        pltpu.make_async_copy(query_ref, query_buf, in_sem.at[4]),
     ]
     for load in loads:
         load.start()
@@ -350,16 +366,17 @@
             inside = (lane >= (head + 1) * HD) & (lane < (head + 2) * HD)
             columns += three(jnp.sum(jnp.where(inside, product, 0.0), axis=-1, keepdims=True))
         stats = put_columns(256, BLK, 9, columns)
-        buf[head_group] = jnp.where(lane < 9, mixed, jnp.where(lane < HD, stats, back)).astype(BF)
+        buf[head_group, :, :256] = jnp.where(lane < 9, mixed, jnp.where(lane < HD, stats, back)).astype(BF)
+        buf[head_group, :, 256:] = query_buf[head_group]
     sends = send_copies(buf, out_ref, range(8), sem)
     wait_all(stores)
     wait_all(sends)
 
 
 def attend_back_kernel(
-    scene_ref, kvs_ref, kvo_ref, q_ref, gs_ref, go_ref, normed_ref, mixed_ref, low_ref, low1_ref, low2_ref, low3_ref,
+    scene_ref, kvs_ref, kvo_ref, gs_ref, go_ref, normed_ref, mixed_ref, low_ref, low1_ref, low2_ref, low3_ref,
     w_ref, gqkv_ref, w_out_ref, keep_ref, send_ref,
-    kv_buf, q_buf, grad_buf, mixed_buf, normed_buf, low_buf, kv_sem, q_sem, in_sem, w_sem,
+    kv_buf, grad_buf, mixed_buf, normed_buf, low_buf, kv_sem, in_sem, w_sem,
 ):
     first, big = span(scene_ref)
     chip = chip_index()
@@ -379,11 +396,6 @@
         loads = [
             pltpu.make_async_copy(ref.at[pl.ds(first, count)], kv_buf.at[slot, pl.ds(0, count)], kv_sem.at[slot])
             for slot, ref in enumerate((kvs_ref, kvo_ref))
-        ] + [
-            pltpu.make_async_copy(
-                q_ref.at[pl.ds(first, count), which], q_buf.at[slot, pl.ds(0, count)], q_sem.at[slot]
-            )
-            for slot, which in enumerate((core, 1 - core))
         ]
         for load in loads + first_loads:
             load.start()
@@ -392,17 +404,17 @@
         def cut(value):
             return [value[:, at:at + 128] for at in range(0, value.shape[1], 128)]
 
-        grad = cut(jnp.concatenate(
-            [ref[pl.ds(first, count)].reshape(rows, 256) for ref in (gs_ref, go_ref)], axis=0
+        every = cut(jnp.concatenate(
+            [ref[pl.ds(first, count)].reshape(rows, 512) for ref in (gs_ref, go_ref)], axis=0
         ))
+        grad, query = every[:2], every[2:]
         g_own = cut(gs_ref[chip])
         g_heads = [halves(g_own[0])[1], *halves(g_own[1])]
         own_stats = g_own[0].astype(F32)
         all_stats = grad[0].astype(F32).T
         wait_all(loads)
         kv = cut(jnp.concatenate([kv_buf[slot, :count].reshape(rows, 384) for slot in range(2)], axis=0))
-        query = cut(jnp.concatenate([q_buf[slot, :count].reshape(rows, 256) for slot in range(2)], axis=0))
-        own = cut(kv_buf[0, chip - first]) + cut(q_buf[0, chip - first])
+        own = cut(kv_buf[0, chip - first]) + g_own[2:]
         q_heads = [*halves(own[3]), own[4]]
         k_heads = [*halves(own[0]), halves(own[1])[0]]
         v_heads = [halves(own[1])[1], *halves(own[2])]
@@ -558,13 +570,25 @@
     wait_all(copies)
 
 
-def spread_ff_kernel(in_ref, up_ref, down_ref):
-    up_ref[...] = in_ref[:, :384].astype(F32)
-    for tile in range(16):
-        half = (tile % 2) * 384
-        down_ref[(tile // 2) * 48:(tile // 2 + 1) * 48, half:half + 384] = in_ref[
-            tile * 48:(tile + 1) * 48, 384:
-        ].astype(F32)
+def stack_kernel(*refs):
+    y = lax.axis_index("y")
+    for k, ref in enumerate(refs[:4]):
+        refs[4][y ^ k] = ref[...]
+
+
+def spread_ff_kernel(*refs):
+    up_ref, down_ref = refs[4:]
+    xl, core = lax.axis_index("xl"), lax.axis_index(CORE)
+    for index, ref in enumerate(refs[:4]):
+        chip_xl = xl ^ (index % 2)
+        owner = core ^ (index // 2)
+        for y in range(4):
+            chip = y * 2 + chip_xl
+            block = ref[y].astype(F32)
+            up_ref[pl.ds(pl.multiple_of((chip * 2 + owner) * 48, 16), 48)] = block[:, :384]
+            down_ref[
+                pl.ds(pl.multiple_of(chip * 48, 16), 48), pl.ds(pl.multiple_of(owner * 384, 128), 384)
+            ] = block[:, 384:]
 
 
 def input_kernel(
@@ -584,7 +608,7 @@
     wait_all(send_copies(buf, out_ref, range(8), sem))
 
 
-def unpack_kernel(in_ref, unused_ref, grad_ref, result_ref):
+def unpack_kernel(in_ref, unused_ref, other_ref, grad_ref, result_ref):
     for index in range(8):
         rows = slice(index % 4 * BLK, (index % 4 + 1) * BLK)
         grad_ref[index // 4, rows] = in_ref[index, :BLK].astype(F32)
@@ -647,7 +671,13 @@
         [pltpu.VMEM((TOK, 256), BF), pltpu.VMEM((TOK, 256), BF), DMA((8,)), DMA],
     )
     mixed = exchange(mixed_send, NARROW)
-    queries = lax.all_gather(after(pin(query), kv_same), WIDE, axis=0, tiled=True).reshape(8, 2, TOK, 256)
+    (block_query,) = call(
+        block_query_kernel,
+        [((4, BLK, 256), BF, "L")],
+        [(normed, "H"), (w_qkv, "H")],
+        1000,
+        [pltpu.VMEM((BLK, D), BF), pltpu.VMEM((D, D), BF), DMA, DMA],
+    )
     ff_send, middle, normed2, act, grad_pre = call(
         forward_kernel,
         [
@@ -687,23 +717,24 @@
     grad_send, low, grad_mid, result_part, vec2 = call(
         middle_kernel,
         [
-            ((8, 4, BLK, 256), BF, "H"), ((BLK, D), BF, "H"), ((BLK, D), F32, "H"), ((BLK, D), BF, "H"),
+            ((8, 4, BLK, 512), BF, "H"), ((BLK, D), BF, "H"), ((BLK, D), F32, "H"), ((BLK, D), BF, "H"),
             ((8, D), F32, "H"),
         ],
         [
             (ff_sums, "V"), (middle, "H"), (out_grad, "H"), (mixed, "H"), (w_out_pad, "V"), (ln2_gain, "H"),
-        ],
-        1000,
-        [
-            pltpu.VMEM((4, BLK, 256), BF), pltpu.VMEM((BLK, D), F32), pltpu.VMEM((BLK, D), BF),
-            pltpu.VMEM((4, BLK, 256), BF), pltpu.VMEM((D,), F32), pltpu.VMEM((BLK, D), BF), pltpu.VMEM((BLK, D), F32),
-            pltpu.VMEM((BLK, D), BF), pltpu.VMEM((8, D), F32), DMA((4,)), DMA((8,)), DMA((4,)),
+            (block_query, "H"),
+        ],
+        1000,
+        [
+            pltpu.VMEM((4, BLK, 512), BF), pltpu.VMEM((BLK, D), F32), pltpu.VMEM((BLK, D), BF),
+            pltpu.VMEM((4, BLK, 256), BF), pltpu.VMEM((D,), F32), pltpu.VMEM((4, BLK, 256), BF), pltpu.VMEM((BLK, D), BF), pltpu.VMEM((BLK, D), F32),
+            pltpu.VMEM((BLK, D), BF), pltpu.VMEM((8, D), F32), DMA((5,)), DMA((8,)), DMA((4,)),
         ],
     )
     far = flip(after(pin(ff_send), pin(low)), "xl", 2, 1)
     (ff_part,) = call(pair_kernel, [((48, D), BF, "L")], [(ff_keep, "L"), (far, "V")], 1000)
-    ff_all = lax.all_gather(ff_part, WIDE, axis=0, tiled=True)
-    grad_same = exchange(grad_send.reshape(32, BLK, 256), (*CHIP, *GROUP)).reshape(8, TOK, 256)
+    ff_parts = [flip(ff_part, "y", 4, k) for k in (1, 2, 3)]
+    grad_same = exchange(grad_send.reshape(32, BLK, 512), (*CHIP, *GROUP)).reshape(8, TOK, 512)
     lows = [flip(low, GROUP, 4, k) for k in (1, 2, 3)]
     grad_same = after(grad_same, *lows, pin(ff_part))
     grad_other = swap(grad_same)
@@ -711,14 +742,14 @@
         attend_back_kernel,
         [((TOK, 640), BF, "V"), ((3, D, 384), BF, "V")] + [((16, 48, 384), BF, "V")] * 2,
         [
-            (scene_of_block, "S"), (kv_same, "H"), (kv_other, "H"), (queries, "H"), (grad_same, "V"), (grad_other, "V"),
+            (scene_of_block, "S"), (kv_same, "H"), (kv_other, "H"), (grad_same, "V"), (grad_other, "V"),
             (normed, "H"), (mixed, "H"), (low, "H"), *[(value, "V") for value in lows], (w_qkv, "H"),
         ],
         10**9,
         [
-            pltpu.VMEM((2, 5, TOK, 384), BF), pltpu.VMEM((2, 5, TOK, 256), BF), pltpu.VMEM((D, 640), F32),
+            pltpu.VMEM((2, 5, TOK, 384), BF), pltpu.VMEM((D, 640), F32),
             pltpu.VMEM((TOK, 256), BF), pltpu.VMEM((TOK, D), BF), pltpu.VMEM((BLK, D), BF),
-            DMA((2,)), DMA((2,)), DMA((3,)), DMA((3,)),
+            DMA((2,)), DMA((3,)), DMA((3,)),
         ],
         vmem=24,
     )
@@ -741,7 +772,7 @@
     )
     weight_parts = exchange(weight_send, (*CHIP, MICRO))
     parts = [flip(value, GROUP, 4, k + 1) for k, value in enumerate(sends)]
-    weight_parts = after(weight_parts, pin(sums), *parts, pin(ff_all))
+    weight_parts = after(weight_parts, pin(sums), *parts, *ff_parts)
     (weight_total,) = call(
         sum_kernel,
         [((8, 8, 56, 384), BF, "H")],
@@ -759,13 +790,23 @@
         1000,
         [pltpu.VMEM((2 * BLK, D), BF), pltpu.VMEM((BLK, D), BF), DMA((8,)), DMA],
     )
-    up_grad, down_grad = call(
-        spread_ff_kernel, [((D, FFL), F32, "L"), ((FFL, D), F32, "L")], [(ff_all, "L")], 1000
-    )
+    (ff_near,) = call(
+        stack_kernel,
+        [((4, 48, D), BF, "L")],
+        [(ff_part, "L"), *[(value, "V") for value in ff_parts]],
+        1000,
+    )
+    ff_far = flip(ff_near, "xl", 2, 1)
     weight_same = exchange(weight_total.reshape(64, 56, 384), (*CHIP, *NARROW)).reshape(8, 8, 56, 384)
-    weight_same = after(weight_same, pin(packed), pin(up_grad), pin(down_grad))
+    weight_same = after(weight_same, pin(packed), ff_far)
     everyone = exchange(after(pin(packed), weight_same), NARROW)
     weight_other = swap(weight_same)
+    up_grad, down_grad = call(
+        spread_ff_kernel,
+        [((D, FFL), F32, "L"), ((FFL, D), F32, "L")],
+        [(ff_near, "L"), (ff_far, "V"), (swap(ff_near), "V"), (swap(ff_far), "V")],
+        1000,
+    )
     scratch = [
         pltpu.VMEM((8, 48, 3 * D), F32), pltpu.VMEM((4, 2, 48, D), F32), DMA((8,)), DMA((4, 2)),
     ]
@@ -786,7 +827,7 @@
         aliases={2: 0, 3: 1},
     )
     input_grad, result = call(
-        unpack_kernel, [((2, TOK, D), F32, "L"), ((2, TOK, D), BF, "L")], [(everyone, "V"), (vectors[0], "H")], 1000
+        unpack_kernel, [((2, TOK, D), F32, "L"), ((2, TOK, D), BF, "L")], [(everyone, "V"), (vectors[0], "H"), (up_grad, "H")], 1000
     )
     return (
         result, input_grad, qkv_grad, out_proj_grad, *vectors, up_grad, down_grad

time: 213 us -> 212 us (level)
  between operations: 14.3 us -> 0.92 us
  starting transfers between devices: 65.1 us -> 74.3 us
    all_to_all x7, waiting for transfers between devices: 53.9 us -> 19.2 us  [exchange(): return lax.all_to_all(value, axes, 0, 0, tiled=True)]
    ppermute x10 -> x14, waiting for transfers between devices: 21.7 us -> 54.1 us  [flip(): lax.ppermute(value, axes, [(index, index ^ bits) for index in range(count)])]
    ppermute x10 -> x14, starting transfers between devices: 12.4 us -> 16.4 us  [flip(): lax.ppermute(value, axes, [(index, index ^ bits) for index in range(count)])]
    all_to_all x7, starting transfers between devices: 43.2 us -> 47.1 us  [exchange(): return lax.all_to_all(value, axes, 0, 0, tiled=True)]
    ppermute x5 -> x7, waiting for transfers between devices: 3.45 us -> 5.91 us  [swap(): return lax.ppermute(value, CORE, [(0, 1), (1, 0)])]
    pallas_call x18 -> x20, Pallas kernels: 51.1 us -> 52.6 us  [call(): pl.pallas_call(kernel, out_shape=[(pltpu.HBM if place in 'HL' else jax.Sh...]
    ppermute x5 -> x7, starting transfers between devices: 9.53 us -> 10.9 us  [swap(): return lax.ppermute(value, CORE, [(0, 1), (1, 0)])]
  transfers between devices with their start and end apart: 24 -> 28, of which waited for: 14 -> 16; matrix products, arithmetic and copies ran while one was open for 1% -> 1% of each run, Pallas kernels for 19% -> 13%
where the time goes in v13:
time: 212 us; the launch traced here: 211 us
  waiting for transfers between devices  79.2 us (37%)
  starting transfers between devices  74.3 us (35%)
  Pallas kernels  52.6 us (25%)
  local copies, waits for them, and re-layouts  3.95 us (2%)
    ppermute x14, waiting for transfers between devices, flip(): lax.ppermute(value, axes, [(index, index ^ bits) for index in range(count)])  54.1 us
    pallas_call x20, Pallas kernels, call(): pl.pallas_call(kernel, out_shape=[(pltpu.HBM if place in 'HL' else jax.Sh...  52.6 us
    all_to_all x7, starting transfers between devices, exchange(): return lax.all_to_all(value, axes, 0, 0, tiled=True)  47.1 us
    all_to_all x7, waiting for transfers between devices, exchange(): return lax.all_to_all(value, axes, 0, 0, tiled=True)  19.2 us
    ppermute x14, starting transfers between devices, flip(): lax.ppermute(value, axes, [(index, index ^ bits) for index in range(count)])  16.4 us
    ppermute x7, starting transfers between devices, swap(): return lax.ppermute(value, CORE, [(0, 1), (1, 0)])  10.9 us
    ppermute x7, waiting for transfers between devices, swap(): return lax.ppermute(value, CORE, [(0, 1), (1, 0)])  5.91 us
  transfers between devices with their start and end apart: 28, of which 16 were waited for; matrix products, arithmetic and copies ran while one was open for 1% of the time, Pallas kernels for 13%

profile of v13, /device:TPU:1, one launch (start us, length us, event | category | flops | bytes accessed | tf_op | source)
XLA Modules:
  0.0 211.0 jit_solution(5737036196672413604)
XLA Ops:
  0.6 3.7 %shard_map.186 = (bf16[8,128,384]{2,1,0:T(8,128)(2,1)}, bf16[128,768]{1,0:T(8,128)(2,1)}) custom-call(bf16[2,128,768]{2,1,0:T(8,128)(2,1)} %tok_ref.7, f32[768]{0:T(1024)} %gain_ref.7, f32[768]{0:T(1024)} %shift_ref.2, bf16[768,2304]{1,0:T(8,128)(2,1)} %w_ref.7), custom_call_target="tpu_custom_call" | custom-call | flops 1000 | bytes 1000 | tf_op jit(solution)/shard_map/pallas_call | solution.py:106
  4.3 6.0 %all-to-all-start = ((bf16[8,128,384]{2,1,0:T(8,128)(2,1)}), bf16[8,128,384]{2,1,0:T(8,128)(2,1)S(1)}, u32[]{:S(2)}, u32[]{:S(2)}) async-start(bf16[8,128,384]{2,1,0:T(8,128)(2,1)} %get-tuple-element.52), calls=%async_computation | async-start | bytes 1572864 | tf_op jit(solution)/shard_map/all_to_all | solution.py:619
  10.3 3.0 %shard_map.187.refs_1_.q_ref = bf16[128,256]{1,0:T(8,128)(2,1)} custom-call(bf16[128,768]{1,0:T(8,128)(2,1)} %get-tuple-element.53.normed_ref, bf16[768,2304]{1,0:T(8,128)(2,1)} %w_ref.7), custom_call_target="tpu_custom_call" | custom-call | flops 1000 | bytes 1000 | tf_op jit(solution)/shard_map/pallas_call | solution.py:106
  13.4 8.6 %all-to-all-done.refs_0_ = bf16[8,128,384]{2,1,0:T(8,128)(2,1)S(1)} async-done(((bf16[8,128,384]{2,1,0:T(8,128)(2,1)}), bf16[8,128,384]{2,1,0:T(8,128)(2,1)S(1)}, u32[]{:S(2)}, u32[]{:S(2)}) %all-to-all-start) | async-done | bytes 786464 | tf_op jit(solution)/shard_map/all_to_all | solution.py:619
  26.1 3.1 %shard_map.189 = bf16[8,128,256]{2,1,0:T(8,128)(2,1)} custom-call(s32[2,32]{1,0:T(2,128)S(1)} %copy-done.5, bf16[128,256]{1,0:T(8,128)(2,1)} %shard_map.187.refs_1_.q_ref, bf16[8,128,384]{2,1,0:T(8,128)(2,1)S(1)} %shard_map.188.same_ref.kvs_ref, bf16[8,128,384]{2,1,0:T(8,128)(2,1)S(1)} %collective-permute-done.other_ref.kvo_ref), custom_call_target="tpu_custom_call" | custom-call | flops 1000 | bytes 1000 | tf_op jit(solution)/shard_map/pallas_call | solution.py:106
  30.1 8.1 %all-to-all-start.1 = ((bf16[8,128,256]{2,1,0:T(8,128)(2,1)}), bf16[8,128,256]{2,1,0:T(8,128)(2,1)S(1)}, u32[]{:S(2)}, u32[]{:S(2)}) async-start(bf16[8,128,256]{2,1,0:T(8,128)(2,1)} %shard_map.189), calls=%async_computation.1 | async-start | bytes 1048576 | tf_op jit(solution)/shard_map/all_to_all | solution.py:619
  39.5 9.4 %all-to-all-done.1.mixed_ref = bf16[8,128,256]{2,1,0:T(8,128)(2,1)S(1)} async-done(((bf16[8,128,256]{2,1,0:T(8,128)(2,1)}), bf16[8,128,256]{2,1,0:T(8,128)(2,1)S(1)}, u32[]{:S(2)}, u32[]{:S(2)}) %all-to-all-start.1) | async-done | bytes 524320 | tf_op jit(solution)/shard_map/all_to_all | solution.py:619
  48.9 4.1 %shard_map.190 = (bf16[8,64,768]{2,1,0:T(8,128)(2,1)}, f32[32,768]{1,0:T(8,128)}, bf16[256,768]{1,0:T(8,128)(2,1)S(1)}, bf16[256,384]{1,0:T(8,128)(2,1)S(1)}, bf16[256,384]{1,0:T(8,128)(2,1)S(1)}) custom-call(bf16[8,128,256]{2,1,0:T(8,128)(2,1)S(1)} %all-to-all-done.1.mixed_ref, bf16[2,128,768]{2,1,0:T(8,128)(2,1)} %tok_ref.7, bf16[2,128,768]{2,1,0:T(8,128)(2,1)} %og_ref.5, ...), custom_call_target="tpu_custom_call" | custom-call | flops 1000 | bytes 1000 | tf_op jit(solution)/shard_map/pallas_call | solution.py:106
  53.1 2.8 %shard_map.191 = (bf16[8,48,768]{2,1,0:T(8,128)(2,1)S(1)}, bf16[8,48,768]{2,1,0:T(8,128)(2,1)}) custom-call(bf16[256,768]{1,0:T(8,128)(2,1)S(1)} %get-tuple-element.55.normed_ref, bf16[256,384]{1,0:T(8,128)(2,1)S(1)} %get-tuple-element.56.act_ref, bf16[256,384]{1,0:T(8,128)(2,1)S(1)} %get-tuple-element.57.gpre_ref, bf16[2,128,768]{2,1,0:T(8,128)(2,1)} %og_ref.5), custom_call_target="tpu_custom_call" | custom-call | flops 1000 | bytes 1000 | tf_op jit(solution)/shard_map/pallas_call | solution.py:106
  57.6 3.5 %all-to-all-start.2 = ((bf16[8,64,768]{2,1,0:T(8,128)(2,1)}), bf16[8,64,768]{2,1,0:T(8,128)(2,1)S(1)}, u32[]{:S(2)}, u32[]{:S(2)}) async-start(bf16[8,64,768]{2,1,0:T(8,128)(2,1)} %get-tuple-element.54), calls=%async_computation.2 | async-start | bytes 1572864 | tf_op jit(solution)/shard_map/all_to_all | solution.py:619
  63.9 3.0 %collective-permute-start.4 = (bf16[2,48,768]{2,1,0:T(8,128)(2,1)}, bf16[2,48,768]{2,1,0:T(8,128)(2,1)S(1)}, u32[]{:S(2)}, u32[]{:S(2)}) collective-permute-start(bf16[2,48,768]{2,1,0:T(8,128)(2,1)} %get-tuple-element.63), channel_id=1, source_target_pairs={{0,96},{32,64},{64,32},{96,0},{1,97},{33,65},{65,33},{97,1},{2,98}... | collective-permute-start | bytes 442376 | tf_op jit(solution)/shard_map/ppermute | solution.py:639
  66.9 2.3 %shard_map.195.query_ref = bf16[4,32,256]{2,1,0:T(8,128)(2,1)} custom-call(bf16[128,768]{1,0:T(8,128)(2,1)} %get-tuple-element.53.normed_ref, bf16[768,2304]{1,0:T(8,128)(2,1)} %w_ref.7), custom_call_target="tpu_custom_call" | custom-call | flops 1000 | bytes 1000 | tf_op jit(solution)/shard_map/pallas_call | solution.py:106
  71.4 2.9 %collective-permute-done.4.refs_3_ = bf16[2,48,768]{2,1,0:T(8,128)(2,1)S(1)} collective-permute-done((bf16[2,48,768]{2,1,0:T(8,128)(2,1)}, bf16[2,48,768]{2,1,0:T(8,128)(2,1)S(1)}, u32[]{:S(2)}, u32[]{:S(2)}) %collective-permute-start.4) | collective-permute-done | bytes 147488 | tf_op jit(solution)/shard_map/ppermute | solution.py:639
  75.8 3.0 %shard_map.196 = (bf16[8,4,32,512]{3,2,1,0:T(8,128)(2,1)}, bf16[32,768]{1,0:T(8,128)(2,1)}, f32[32,768]{1,0:T(8,128)}, bf16[32,768]{1,0:T(8,128)(2,1)}, f32[8,768]{1,0:T(8,128)}) custom-call(bf16[8,64,768]{2,1,0:T(8,128)(2,1)S(1)} %shard_map.194.sums_ref, f32[32,768]{1,0:T(8,128)} %get-tuple-element.65.middle_ref, bf16[2,128,768]{2,1,0:T(8,128)(2,1)} %og_ref.5, ...), custom_call_target="tpu_custom_call" | custom-call | flops 1000 | bytes 1000 | tf_op jit(solution)/shard_map/pallas_call | solution.py:106
  78.8 7.4 %all-to-all-start.3 = ((bf16[32,32,512]{2,1,0:T(8,128)(2,1)}), bf16[32,32,512]{2,1,0:T(8,128)(2,1)S(1)}, u32[]{:S(2)}, u32[]{:S(2)}) async-start(bf16[32,32,512]{2,1,0:T(8,128)(2,1)} %bitcast.9), calls=%async_computation.3 | async-start | bytes 2097152 | tf_op jit(solution)/shard_map/all_to_all | solution.py:619
  87.6 2.4 %collective-permute-start.5 = (bf16[32,768]{1,0:T(8,128)(2,1)}, bf16[32,768]{1,0:T(8,128)(2,1)S(1)}, u32[]{:S(2)}, u32[]{:S(2)}) collective-permute-start(bf16[32,768]{1,0:T(8,128)(2,1)} %get-tuple-element.67.refs_1_.low_ref), channel_id=1, source_target_pairs={{0,1},{1,0},{2,3},{3,2},{4,5},{5,4},{6,7},{7,6},{8,9},{9,8},{10,11... | collective-permute-start | bytes 147464 | tf_op jit(solution)/shard_map/ppermute | solution.py:639
  91.7 8.0 %collective-permute-done.8.two_ref = bf16[48,768]{1,0:T(8,128)(2,1)S(1)} collective-permute-done((bf16[48,768]{1,0:T(8,128)(2,1)}, bf16[48,768]{1,0:T(8,128)(2,1)S(1)}, u32[]{:S(2)}, u32[]{:S(2)}) %collective-permute-start.8) | collective-permute-done | bytes 73760 | tf_op jit(solution)/shard_map/ppermute | solution.py:639
  104.2 2.3 %collective-permute-start.9 = (bf16[8,128,512]{2,1,0:T(8,128)(2,1)S(1)}, bf16[8,128,512]{2,1,0:T(8,128)(2,1)S(1)}, u32[]{:S(2)}, u32[]{:S(2)}) collective-permute-start(bf16[8,128,512]{2,1,0:T(8,128)(2,1)S(1)} %shard_map.199.gs_ref), channel_id=1, source_target_pairs={{0,8},{8,0},{1,9},{9,1},{2,10},{10,2},{3,11},{11,3},{4,12},{12,4},... | collective-permute-start | bytes 3145736 | tf_op jit(solution)/shard_map/ppermute | solution.py:623
  108.8 4.3 %shard_map.200 = (bf16[128,640]{1,0:T(8,128)(2,1)S(1)}, bf16[3,768,384]{2,1,0:T(8,128)(2,1)S(1)}, bf16[16,48,384]{2,1,0:T(8,128)(2,1)S(1)}, bf16[16,48,384]{2,1,0:T(8,128)(2,1)S(1)}) custom-call(s32[2,32]{1,0:T(2,128)S(1)} %copy-done.5, bf16[8,128,384]{2,1,0:T(8,128)(2,1)} %copy-done, bf16[8,128,384]{2,1,0:T(8,128)(2,1)} %copy-done.2, ...), custom_call_target="tpu_custom_call" | custom-call | flops 1000000000 | bytes 1000 | tf_op jit(solution)/shard_map/pallas_call | solution.py:106
  113.7 2.3 %shard_map.201 = (f32[32,768]{1,0:T(8,128)}, bf16[32,768]{1,0:T(8,128)(2,1)}, bf16[32,768]{1,0:T(8,128)(2,1)}, bf16[32,768]{1,0:T(8,128)(2,1)}, f32[8,768]{1,0:T(8,128)}) custom-call(bf16[128,640]{1,0:T(8,128)(2,1)S(1)} %get-tuple-element.69.gqkv_ref, bf16[3,768,384]{2,1,0:T(8,128)(2,1)S(1)} %get-tuple-element.70.w_ref, bf16[2,128,768]{2,1,0:T(8,128)(2,1)} %tok_ref.7, ...), custom_call_target="tpu_custom_call" | custom-call | flops 1000 | bytes 1000 | tf_op jit(solution)/shard_map/pallas_call | solution.py:106
  117.0 7.5 %all-to-all-start.4 = ((bf16[16,48,384]{2,1,0:T(8,128)(2,1)}), bf16[16,48,384]{2,1,0:T(8,128)(2,1)S(1)}, u32[]{:S(2)}, u32[]{:S(2)}) async-start(bf16[16,48,384]{2,1,0:T(8,128)(2,1)} %shard_map.202), calls=%async_computation.4 | async-start | bytes 1179648 | tf_op jit(solution)/shard_map/all_to_all | solution.py:619
  126.0 2.4 %collective-permute-start.15 = (bf16[48,768]{1,0:T(8,128)(2,1)S(1)}, bf16[48,768]{1,0:T(8,128)(2,1)S(1)}, u32[]{:S(2)}, u32[]{:S(2)}) collective-permute-start(bf16[48,768]{1,0:T(8,128)(2,1)S(1)} %copy-done.6), channel_id=1, source_target_pairs={{0,64},{32,96},{64,0},{96,32},{1,65},{33,97},{65,1},{97,33},{2,66}... | collective-permute-start | bytes 221192 | tf_op jit(solution)/shard_map/ppermute | solution.py:639
  129.7 4.7 %collective-permute-done.14.refs_5_.refs_1_ = bf16[48,768]{1,0:T(8,128)(2,1)S(1)} collective-permute-done((bf16[48,768]{1,0:T(8,128)(2,1)S(1)}, bf16[48,768]{1,0:T(8,128)(2,1)S(1)}, u32[]{:S(2)}, u32[]{:S(2)}) %collective-permute-start.14) | collective-permute-done | bytes 73760 | tf_op jit(solution)/shard_map/ppermute | solution.py:639
  139.8 2.4 %shard_map.204.unused_ref = bf16[8,8,56,384]{3,2,1,0:T(8,128)(2,1)} custom-call(bf16[16,48,384]{2,1,0:T(8,128)(2,1)S(1)} %shard_map.203.in_ref, f32[8,768]{1,0:T(8,128)} %get-tuple-element.80.refs_1_.vec_ref), custom_call_target="tpu_custom_call" | custom-call | flops 1000 | bytes 1000 | tf_op jit(solution)/shard_map/pallas_call | solution.py:106
  142.1 8.4 %all-to-all-start.5 = ((bf16[64,56,384]{2,1,0:T(8,128)(2,1)}), bf16[64,56,384]{2,1,0:T(8,128)(2,1)S(1)}, u32[]{:S(2)}, u32[]{:S(2)}) async-start(bf16[64,56,384]{2,1,0:T(8,128)(2,1)} %bitcast.7), calls=%async_computation.5 | async-start | bytes 5505024 | tf_op jit(solution)/shard_map/all_to_all | solution.py:619
  153.2 3.0 %shard_map.205.refs_1_.refs_0_ = bf16[8,64,768]{2,1,0:T(8,128)(2,1)} custom-call(f32[32,768]{1,0:T(8,128)} %get-tuple-element.72.unused_ref.own_ref, bf16[32,768]{1,0:T(8,128)(2,1)S(1)} %collective-permute-done.10.refs_2_.one_ref, bf16[32,768]{1,0:T(8,128)(2,1)S(1)} %collective-permute-done.11.refs_3_.two_ref, ...), custom_call_target="tpu_custom_call" | custom-call | flops 1000 | bytes 1000 | tf_op jit(solution)/shard_map/pallas_call | solution.py:106
  156.2 29.0 %collective-permute-done.17.refs_2_.refs_1_ = bf16[4,48,768]{2,1,0:T(8,128)(2,1)S(1)} collective-permute-done((bf16[4,48,768]{2,1,0:T(8,128)(2,1)}, bf16[4,48,768]{2,1,0:T(8,128)(2,1)S(1)}, u32[]{:S(2)}, u32[]{:S(2)}) %collective-permute-start.17) | collective-permute-done | bytes 294944 | tf_op jit(solution)/shard_map/ppermute | solution.py:639
  185.9 3.7 %collective-permute-start.18 = (bf16[8,8,56,384]{3,2,1,0:T(8,128)(2,1)S(1)}, bf16[8,8,56,384]{3,2,1,0:T(8,128)(2,1)}, u32[]{:S(2)}, u32[]{:S(2)}) collective-permute-start(bf16[8,8,56,384]{3,2,1,0:T(8,128)(2,1)S(1)} %shard_map.207.refs_1_.in_ref), channel_id=1, source_target_pairs={{0,8},{8,0},{1,9},{9,1},{2,10},{10,2},{3,11},{11,3},{4,12},{12,4},... | collective-permute-start | bytes 8257544 | tf_op jit(solution)/shard_map/ppermute | solution.py:623
  189.6 6.1 %all-to-all-start.6 = ((bf16[8,64,768]{2,1,0:T(8,128)(2,1)}), bf16[8,64,768]{2,1,0:T(8,128)(2,1)S(1)}, u32[]{:S(2)}, u32[]{:S(2)}) async-start(bf16[8,64,768]{2,1,0:T(8,128)(2,1)} %shard_map.208), calls=%async_computation.6 | async-start | bytes 1572864 | tf_op jit(solution)/shard_map/all_to_all | solution.py:619
  198.8 2.5 %shard_map.211 = (f32[768,384]{1,0:T(8,128)}, f32[384,768]{1,0:T(8,128)}) custom-call(bf16[4,48,768]{2,1,0:T(8,128)(2,1)} %shard_map.206.refs_0_, bf16[4,48,768]{2,1,0:T(8,128)(2,1)S(1)} %copy-done.4, bf16[4,48,768]{2,1,0:T(8,128)(2,1)S(1)} %collective-permute-done.19.refs_2_, bf16[4,48,768]{2,1,0:T(8,128)(2,1)S(1)} %collective-permute-done.20.refs_3_), custom_call_target="tpu_custom_call" | custom-call | flops 1000 | bytes 1000 | tf_op jit(solution)/shard_map/pallas_call | solution.py:106
  201.4 2.4 %shard_map.209 = (f32[768,2304]{1,0:T(8,128)}, f32[768,768]{1,0:T(8,128)}, f32[8,384]{1,0:T(8,128)S(1)}) custom-call(bf16[8,8,56,384]{3,2,1,0:T(8,128)(2,1)S(1)} %shard_map.207.refs_1_.in_ref), custom_call_target="tpu_custom_call" | custom-call | flops 1000 | bytes 1000 | tf_op jit(solution)/shard_map/pallas_call | solution.py:106
  203.8 4.8 %shard_map.210 = (f32[768,2304]{1,0:T(8,128)}, f32[768,768]{1,0:T(8,128)}, f32[768]{0:T(1024)}, f32[768]{0:T(1024)}, f32[768]{0:T(1024)}, /*index=5*/f32[768]{0:T(1024)}) custom-call(bf16[8,8,56,384]{3,2,1,0:T(8,128)(2,1)} %collective-permute-done.18.in_ref, f32[8,384]{1,0:T(8,128)S(1)} %get-tuple-element.81.refs_0_, ...), custom_call_target="tpu_custom_call", output_to_operand_aliasing={{0}: (2, {}), {1}: (3, {})} | custom-call | flops 1000 | bytes 1000 | tf_op jit(solution)/shard_map/pallas_call | solution.py:106
  (72 shorter events, 42.8 us)
Async XLA Ops:
  4.3 17.6 %all-to-all-start = ((bf16[8,128,384]{2,1,0:T(8,128)(2,1)}), bf16[8,128,384]{2,1,0:T(8,128)(2,1)S(1)}, u32[]{:S(2)}, u32[]{:S(2)}) async-start(bf16[8,128,384]{2,1,0:T(8,128)(2,1)} %get-tuple-element.52), calls=%async_computation | async-start | bytes 1572864 | tf_op jit(solution)/shard_map/all_to_all | solution.py:619
  10.3 15.8 %copy-start.5 = (s32[2,32]{1,0:T(2,128)S(1)}, s32[2,32]{1,0:T(2,128)}, u32[]{:S(2)}) copy-start(s32[2,32]{1,0:T(2,128)} %scene_ref.3) | copy-start | bytes 772
  22.0 17.5 %copy-start = (bf16[8,128,384]{2,1,0:T(8,128)(2,1)}, bf16[8,128,384]{2,1,0:T(8,128)(2,1)S(1)}, u32[]{:S(2)}) copy-start(bf16[8,128,384]{2,1,0:T(8,128)(2,1)S(1)} %shard_map.188.same_ref.kvs_ref) | copy-start | bytes 2359300
  22.0 4.1 %collective-permute-start = (bf16[8,128,384]{2,1,0:T(8,128)(2,1)S(1)}, bf16[8,128,384]{2,1,0:T(8,128)(2,1)S(1)}, u32[]{:S(2)}, u32[]{:S(2)}) collective-permute-start(bf16[8,128,384]{2,1,0:T(8,128)(2,1)S(1)} %shard_map.188.same_ref.kvs_ref), channel_id=1, source_target_pairs={{0,8},{8,0},{1,9},{9,1},{2,10},{10,2},{3,11},{11,3},{4,12},{12,4},... | collective-permute-start | bytes 2359304 | tf_op jit(solution)/shard_map/ppermute | solution.py:623
  30.1 18.8 %all-to-all-start.1 = ((bf16[8,128,256]{2,1,0:T(8,128)(2,1)}), bf16[8,128,256]{2,1,0:T(8,128)(2,1)S(1)}, u32[]{:S(2)}, u32[]{:S(2)}) async-start(bf16[8,128,256]{2,1,0:T(8,128)(2,1)} %shard_map.189), calls=%async_computation.1 | async-start | bytes 1048576 | tf_op jit(solution)/shard_map/all_to_all | solution.py:619
  55.8 5.3 %collective-permute-start.1 = (bf16[8,48,768]{2,1,0:T(8,128)(2,1)}, bf16[8,48,768]{2,1,0:T(8,128)(2,1)}, u32[]{:S(2)}, u32[]{:S(2)}) collective-permute-start(bf16[8,48,768]{2,1,0:T(8,128)(2,1)} %get-tuple-element.59), channel_id=1, source_target_pairs={{0,8},{8,0},{1,9},{9,1},{2,10},{10,2},{3,11},{11,3},{4,12},{12,4},... | collective-permute-start | bytes 1769480 | tf_op jit(solution)/shard_map/ppermute | solution.py:623
  57.6 18.3 %all-to-all-start.2 = ((bf16[8,64,768]{2,1,0:T(8,128)(2,1)}), bf16[8,64,768]{2,1,0:T(8,128)(2,1)S(1)}, u32[]{:S(2)}, u32[]{:S(2)}) async-start(bf16[8,64,768]{2,1,0:T(8,128)(2,1)} %get-tuple-element.54), calls=%async_computation.2 | async-start | bytes 1572864 | tf_op jit(solution)/shard_map/all_to_all | solution.py:619
  63.0 6.2 %collective-permute-start.2 = (bf16[2,48,768]{2,1,0:T(8,128)(2,1)}, bf16[2,48,768]{2,1,0:T(8,128)(2,1)S(1)}, u32[]{:S(2)}, u32[]{:S(2)}) collective-permute-start(bf16[2,48,768]{2,1,0:T(8,128)(2,1)} %get-tuple-element.61), channel_id=1, source_target_pairs={{0,32},{32,0},{64,96},{96,64},{1,33},{33,1},{65,97},{97,65},{2,34}... | collective-permute-start | bytes 442376 | tf_op jit(solution)/shard_map/ppermute | solution.py:639
  63.0 8.3 %collective-permute-start.3 = (bf16[2,48,768]{2,1,0:T(8,128)(2,1)}, bf16[2,48,768]{2,1,0:T(8,128)(2,1)S(1)}, u32[]{:S(2)}, u32[]{:S(2)}) collective-permute-start(bf16[2,48,768]{2,1,0:T(8,128)(2,1)} %get-tuple-element.62), channel_id=1, source_target_pairs={{0,64},{32,96},{64,0},{96,32},{1,65},{33,97},{65,1},{97,33},{2,66}... | collective-permute-start | bytes 442376 | tf_op jit(solution)/shard_map/ppermute | solution.py:639
  63.9 10.3 %collective-permute-start.4 = (bf16[2,48,768]{2,1,0:T(8,128)(2,1)}, bf16[2,48,768]{2,1,0:T(8,128)(2,1)S(1)}, u32[]{:S(2)}, u32[]{:S(2)}) collective-permute-start(bf16[2,48,768]{2,1,0:T(8,128)(2,1)} %get-tuple-element.63), channel_id=1, source_target_pairs={{0,96},{32,64},{64,32},{96,0},{1,97},{33,65},{65,33},{97,1},{2,98}... | collective-permute-start | bytes 442376 | tf_op jit(solution)/shard_map/ppermute | solution.py:639
  78.8 25.4 %all-to-all-start.3 = ((bf16[32,32,512]{2,1,0:T(8,128)(2,1)}), bf16[32,32,512]{2,1,0:T(8,128)(2,1)S(1)}, u32[]{:S(2)}, u32[]{:S(2)}) async-start(bf16[32,32,512]{2,1,0:T(8,128)(2,1)} %bitcast.9), calls=%async_computation.3 | async-start | bytes 2097152 | tf_op jit(solution)/shard_map/all_to_all | solution.py:619
  86.3 13.4 %collective-permute-start.8 = (bf16[48,768]{1,0:T(8,128)(2,1)}, bf16[48,768]{1,0:T(8,128)(2,1)S(1)}, u32[]{:S(2)}, u32[]{:S(2)}) collective-permute-start(bf16[48,768]{1,0:T(8,128)(2,1)} %shard_map.197), channel_id=1, source_target_pairs={{0,16},{16,0},{1,17},{17,1},{2,18},{18,2},{3,19},{19,3},{4,20},{20... | collective-permute-start | bytes 221192 | tf_op jit(solution)/shard_map/ppermute | solution.py:639
  87.6 14.7 %collective-permute-start.5 = (bf16[32,768]{1,0:T(8,128)(2,1)}, bf16[32,768]{1,0:T(8,128)(2,1)S(1)}, u32[]{:S(2)}, u32[]{:S(2)}) collective-permute-start(bf16[32,768]{1,0:T(8,128)(2,1)} %get-tuple-element.67.refs_1_.low_ref), channel_id=1, source_target_pairs={{0,1},{1,0},{2,3},{3,2},{4,5},{5,4},{6,7},{7,6},{8,9},{9,8},{10,11... | collective-permute-start | bytes 147464 | tf_op jit(solution)/shard_map/ppermute | solution.py:639
  90.0 12.3 %collective-permute-start.6 = (bf16[32,768]{1,0:T(8,128)(2,1)}, bf16[32,768]{1,0:T(8,128)(2,1)S(1)}, u32[]{:S(2)}, u32[]{:S(2)}) collective-permute-start(bf16[32,768]{1,0:T(8,128)(2,1)} %get-tuple-element.67.refs_1_.low_ref), channel_id=1, source_target_pairs={{0,2},{1,3},{2,0},{3,1},{4,6},{5,7},{6,4},{7,5},{8,10},{9,11},{10,... | collective-permute-start | bytes 147464 | tf_op jit(solution)/shard_map/ppermute | solution.py:639
  91.2 13.1 %collective-permute-start.7 = (bf16[32,768]{1,0:T(8,128)(2,1)}, bf16[32,768]{1,0:T(8,128)(2,1)S(1)}, u32[]{:S(2)}, u32[]{:S(2)}) collective-permute-start(bf16[32,768]{1,0:T(8,128)(2,1)} %get-tuple-element.67.refs_1_.low_ref), channel_id=1, source_target_pairs={{0,3},{1,2},{2,1},{3,0},{4,7},{5,6},{6,5},{7,4},{8,11},{9,10},{10,... | collective-permute-start | bytes 147464 | tf_op jit(solution)/shard_map/ppermute | solution.py:639
  104.2 4.6 %collective-permute-start.9 = (bf16[8,128,512]{2,1,0:T(8,128)(2,1)S(1)}, bf16[8,128,512]{2,1,0:T(8,128)(2,1)S(1)}, u32[]{:S(2)}, u32[]{:S(2)}) collective-permute-start(bf16[8,128,512]{2,1,0:T(8,128)(2,1)S(1)} %shard_map.199.gs_ref), channel_id=1, source_target_pairs={{0,8},{8,0},{1,9},{9,1},{2,10},{10,2},{3,11},{11,3},{4,12},{12,4},... | collective-permute-start | bytes 3145736 | tf_op jit(solution)/shard_map/ppermute | solution.py:623
  113.2 2.8 %collective-permute-start.13 = (bf16[16,48,384]{2,1,0:T(8,128)(2,1)S(1)}, bf16[16,48,384]{2,1,0:T(8,128)(2,1)S(1)}, u32[]{:S(2)}, u32[]{:S(2)}) collective-permute-start(bf16[16,48,384]{2,1,0:T(8,128)(2,1)S(1)} %get-tuple-element.79), channel_id=1, source_target_pairs={{0,8},{8,0},{1,9},{9,1},{2,10},{10,2},{3,11},{11,3},{4,12},{12,4},... | collective-permute-start | bytes 1769480 | tf_op jit(solution)/shard_map/ppermute | solution.py:623
  116.0 13.1 %copy-start.8 = (bf16[32,768]{1,0:T(8,128)(2,1)S(1)}, bf16[32,768]{1,0:T(8,128)(2,1)}, u32[]{:S(2)}) copy-start(bf16[32,768]{1,0:T(8,128)(2,1)} %get-tuple-element.74) | copy-start | bytes 147460
  116.0 18.4 %copy-start.7 = (bf16[32,768]{1,0:T(8,128)(2,1)S(1)}, bf16[32,768]{1,0:T(8,128)(2,1)}, u32[]{:S(2)}) copy-start(bf16[32,768]{1,0:T(8,128)(2,1)} %get-tuple-element.75) | copy-start | bytes 147460
  117.0 22.7 %all-to-all-start.4 = ((bf16[16,48,384]{2,1,0:T(8,128)(2,1)}), bf16[16,48,384]{2,1,0:T(8,128)(2,1)S(1)}, u32[]{:S(2)}, u32[]{:S(2)}) async-start(bf16[16,48,384]{2,1,0:T(8,128)(2,1)} %shard_map.202), calls=%async_computation.4 | async-start | bytes 1179648 | tf_op jit(solution)/shard_map/all_to_all | solution.py:619
  124.6 9.8 %collective-permute-start.14 = (bf16[48,768]{1,0:T(8,128)(2,1)S(1)}, bf16[48,768]{1,0:T(8,128)(2,1)S(1)}, u32[]{:S(2)}, u32[]{:S(2)}) collective-permute-start(bf16[48,768]{1,0:T(8,128)(2,1)S(1)} %copy-done.6), channel_id=1, source_target_pairs={{0,32},{32,0},{64,96},{96,64},{1,33},{33,1},{65,97},{97,65},{2,34}... | collective-permute-start | bytes 221192 | tf_op jit(solution)/shard_map/ppermute | solution.py:639
  126.0 11.5 %collective-permute-start.15 = (bf16[48,768]{1,0:T(8,128)(2,1)S(1)}, bf16[48,768]{1,0:T(8,128)(2,1)S(1)}, u32[]{:S(2)}, u32[]{:S(2)}) collective-permute-start(bf16[48,768]{1,0:T(8,128)(2,1)S(1)} %copy-done.6), channel_id=1, source_target_pairs={{0,64},{32,96},{64,0},{96,32},{1,65},{33,97},{65,1},{97,33},{2,66}... | collective-permute-start | bytes 221192 | tf_op jit(solution)/shard_map/ppermute | solution.py:639
  128.4 9.1 %collective-permute-start.16 = (bf16[48,768]{1,0:T(8,128)(2,1)S(1)}, bf16[48,768]{1,0:T(8,128)(2,1)S(1)}, u32[]{:S(2)}, u32[]{:S(2)}) collective-permute-start(bf16[48,768]{1,0:T(8,128)(2,1)S(1)} %copy-done.6), channel_id=1, source_target_pairs={{0,96},{32,64},{64,32},{96,0},{1,97},{33,65},{65,33},{97,1},{2,98}... | collective-permute-start | bytes 221192 | tf_op jit(solution)/shard_map/ppermute | solution.py:639
  128.5 9.0 %collective-permute-start.10 = (bf16[32,768]{1,0:T(8,128)(2,1)S(1)}, bf16[32,768]{1,0:T(8,128)(2,1)S(1)}, u32[]{:S(2)}, u32[]{:S(2)}) collective-permute-start(bf16[32,768]{1,0:T(8,128)(2,1)S(1)} %copy-done.9), channel_id=1, source_target_pairs={{0,1},{1,0},{2,3},{3,2},{4,5},{5,4},{6,7},{7,6},{8,9},{9,8},{10,11... | collective-permute-start | bytes 147464 | tf_op jit(solution)/shard_map/ppermute | solution.py:639
  129.1 8.4 %collective-permute-start.11 = (bf16[32,768]{1,0:T(8,128)(2,1)S(1)}, bf16[32,768]{1,0:T(8,128)(2,1)S(1)}, u32[]{:S(2)}, u32[]{:S(2)}) collective-permute-start(bf16[32,768]{1,0:T(8,128)(2,1)S(1)} %copy-done.8), channel_id=1, source_target_pairs={{0,2},{1,3},{2,0},{3,1},{4,6},{5,7},{6,4},{7,5},{8,10},{9,11},{10,... | collective-permute-start | bytes 147464 | tf_op jit(solution)/shard_map/ppermute | solution.py:639
  134.4 5.3 %collective-permute-start.12 = (bf16[32,768]{1,0:T(8,128)(2,1)S(1)}, bf16[32,768]{1,0:T(8,128)(2,1)S(1)}, u32[]{:S(2)}, u32[]{:S(2)}) collective-permute-start(bf16[32,768]{1,0:T(8,128)(2,1)S(1)} %copy-done.7), channel_id=1, source_target_pairs={{0,3},{1,2},{2,1},{3,0},{4,7},{5,6},{6,5},{7,4},{8,11},{9,10},{10,... | collective-permute-start | bytes 147464 | tf_op jit(solution)/shard_map/ppermute | solution.py:639
  142.1 43.0 %all-to-all-start.5 = ((bf16[64,56,384]{2,1,0:T(8,128)(2,1)}), bf16[64,56,384]{2,1,0:T(8,128)(2,1)S(1)}, u32[]{:S(2)}, u32[]{:S(2)}) async-start(bf16[64,56,384]{2,1,0:T(8,128)(2,1)} %bitcast.7), calls=%async_computation.5 | async-start | bytes 5505024 | tf_op jit(solution)/shard_map/all_to_all | solution.py:619
  152.2 33.0 %collective-permute-start.17 = (bf16[4,48,768]{2,1,0:T(8,128)(2,1)}, bf16[4,48,768]{2,1,0:T(8,128)(2,1)S(1)}, u32[]{:S(2)}, u32[]{:S(2)}) collective-permute-start(bf16[4,48,768]{2,1,0:T(8,128)(2,1)} %shard_map.206.refs_0_), channel_id=1, source_target_pairs={{0,16},{16,0},{1,17},{17,1},{2,18},{18,2},{3,19},{19,3},{4,20},{20... | collective-permute-start | bytes 884744 | tf_op jit(solution)/shard_map/ppermute | solution.py:639
  185.9 18.0 %collective-permute-start.18 = (bf16[8,8,56,384]{3,2,1,0:T(8,128)(2,1)S(1)}, bf16[8,8,56,384]{3,2,1,0:T(8,128)(2,1)}, u32[]{:S(2)}, u32[]{:S(2)}) collective-permute-start(bf16[8,8,56,384]{3,2,1,0:T(8,128)(2,1)S(1)} %shard_map.207.refs_1_.in_ref), channel_id=1, source_target_pairs={{0,8},{8,0},{1,9},{9,1},{2,10},{10,2},{3,11},{11,3},{4,12},{12,4},... | collective-permute-start | bytes 8257544 | tf_op jit(solution)/shard_map/ppermute | solution.py:623
  189.6 20.3 %all-to-all-start.6 = ((bf16[8,64,768]{2,1,0:T(8,128)(2,1)}), bf16[8,64,768]{2,1,0:T(8,128)(2,1)S(1)}, u32[]{:S(2)}, u32[]{:S(2)}) async-start(bf16[8,64,768]{2,1,0:T(8,128)(2,1)} %shard_map.208), calls=%async_computation.6 | async-start | bytes 1572864 | tf_op jit(solution)/shard_map/all_to_all | solution.py:619
  195.6 1.8 collective-permute-start.19
  195.9 1.9 collective-permute-start.20
  (6 other events, 35.1 us)

commit v14 on v13

--- a/solution.py
+++ b/solution.py
@@ -302,18 +302,11 @@
             ref[xl] = (one_ref[at].astype(F32) + two_ref[at].astype(F32)).astype(BF)
 
 
-def halve_kernel(*refs):
-    parts, (keep_ref, send_ref) = refs[:4], refs[4:]
-    xl = lax.axis_index("xl")
-    for ref, at in ((keep_ref, xl), (send_ref, 1 - xl)):
-        total = parts[0][at].astype(F32)
-        for part in parts[1:]:
-            total = total + part[at].astype(F32)
-        ref[...] = total.astype(BF)
-
-
-def pair_kernel(one_ref, two_ref, out_ref):
-    out_ref[...] = (one_ref[...].astype(F32) + two_ref[...].astype(F32)).astype(BF)
+def total_kernel(*refs):
+    total = refs[0][...].astype(F32)
+    for ref in refs[1:4]:
+        total = total + ref[...].astype(F32)
+    refs[4][...] = total.astype(BF)
 
 
 def middle_kernel(
@@ -474,12 +467,13 @@
 
 
 def normed_grad_kernel(
-    gqkv_ref, w_ref, tok_ref, vec_ref, own_ref, one_ref, two_ref, three_ref, sums_ref,
-    x_buf, vec_buf, part_buf, low_buf, sums_buf, in_sem, out_sem,
+    gqkv_ref, w_ref, tok_ref, vec_ref, near_ref, far_ref, own_ref, one_ref, two_ref, three_ref, sums_ref, ff_ref,
+    x_buf, vec_buf, near_buf, part_buf, low_buf, sums_buf, ff_buf, in_sem, out_sem,
 ):
     loads = [
         pltpu.make_async_copy(tok_ref.at[lax.axis_index(MICRO)], x_buf, in_sem.at[0]),
         pltpu.make_async_copy(vec_ref, vec_buf, in_sem.at[1]),
+        pltpu.make_async_copy(near_ref, near_buf, in_sem.at[2]),
     ]
     for load in loads:
         load.start()
@@ -501,6 +495,9 @@
         stores.append(pltpu.make_async_copy((low_buf if k else part_buf).at[rows], ref, out_sem.at[k]))
         stores[-1].start()
     wait_all(loads)
+    ff_buf[...] = (near_buf[...].astype(F32) + far_ref[...].astype(F32)).astype(BF)
+    stores.append(pltpu.make_async_copy(ff_buf, ff_ref, out_sem.at[5]))
+    stores[-1].start()
     unit, _ = normalized(x_buf[...].astype(F32))
     gain1 = jnp.sum(total * unit, axis=0, keepdims=True)
     shift1 = jnp.sum(total, axis=0, keepdims=True)
@@ -573,22 +570,16 @@
 def stack_kernel(*refs):
     y = lax.axis_index("y")
     for k, ref in enumerate(refs[:4]):
-        refs[4][y ^ k] = ref[...]
-
-
-def spread_ff_kernel(*refs):
-    up_ref, down_ref = refs[4:]
-    xl, core = lax.axis_index("xl"), lax.axis_index(CORE)
-    for index, ref in enumerate(refs[:4]):
-        chip_xl = xl ^ (index % 2)
-        owner = core ^ (index // 2)
-        for y in range(4):
-            chip = y * 2 + chip_xl
-            block = ref[y].astype(F32)
+        refs[5][pl.ds((y ^ k) * 2, 2)] = ref[...]
+
+
+def spread_ff_kernel(same_ref, other_ref, up_ref, down_ref):
+    core = lax.axis_index(CORE)
+    for ref, owner in ((same_ref, core), (other_ref, 1 - core)):
+        for chip in range(8):
+            block = ref[chip].astype(F32)
             up_ref[pl.ds(pl.multiple_of((chip * 2 + owner) * 48, 16), 48)] = block[:, :384]
-            down_ref[
-                pl.ds(pl.multiple_of(chip * 48, 16), 48), pl.ds(pl.multiple_of(owner * 384, 128), 384)
-            ] = block[:, 384:]
+            down_ref[chip * 48:(chip + 1) * 48, pl.ds(pl.multiple_of(owner * 384, 128), 384)] = block[:, 384:]
 
 
 def input_kernel(
@@ -707,13 +698,13 @@
         split_kernel, [((2, 48, D), BF, "L")] * 4, [(keep, "V"), (swap(send), "V")], 1000
     )
     pieces = [pieces[0]] + [flip(pieces[k], "y", 4, k) for k in (1, 2, 3)]
-    ff_keep, ff_send = call(
-        halve_kernel,
-        [((48, D), BF, "L")] * 2,
+    (ff_near,) = call(
+        total_kernel,
+        [((2, 48, D), BF, "L")],
         [(pieces[0], "L")] + [(piece, "V") for piece in pieces[1:]],
         1000,
     )
-    ff_sums = after(ff_sums, pin(ff_keep))
+    ff_sums = after(ff_sums, pin(ff_near))
     grad_send, low, grad_mid, result_part, vec2 = call(
         middle_kernel,
         [
@@ -731,13 +722,12 @@
             pltpu.VMEM((BLK, D), BF), pltpu.VMEM((8, D), F32), DMA((5,)), DMA((8,)), DMA((4,)),
         ],
     )
-    far = flip(after(pin(ff_send), pin(low)), "xl", 2, 1)
-    (ff_part,) = call(pair_kernel, [((48, D), BF, "L")], [(ff_keep, "L"), (far, "V")], 1000)
-    ff_parts = [flip(ff_part, "y", 4, k) for k in (1, 2, 3)]
     grad_same = exchange(grad_send.reshape(32, BLK, 512), (*CHIP, *GROUP)).reshape(8, TOK, 512)
     lows = [flip(low, GROUP, 4, k) for k in (1, 2, 3)]
-    grad_same = after(grad_same, *lows, pin(ff_part))
+    grad_same = after(grad_same, *lows)
     grad_other = swap(grad_same)
+    ff_near = after(pin(ff_near), grad_other)
+    ff_far = flip(ff_near, "xl", 2, 1)
     gqkv, w_own, keep, send = call(
         attend_back_kernel,
         [((TOK, 640), BF, "V"), ((3, D, 384), BF, "V")] + [((16, 48, 384), BF, "V")] * 2,
@@ -745,7 +735,7 @@
             (scene_of_block, "S"), (kv_same, "H"), (kv_other, "H"), (grad_same, "V"), (grad_other, "V"),
             (normed, "H"), (mixed, "H"), (low, "H"), *[(value, "V") for value in lows], (w_qkv, "H"),
         ],
-        10**9,
+        1000,
         [
             pltpu.VMEM((2, 5, TOK, 384), BF), pltpu.VMEM((D, 640), F32),
             pltpu.VMEM((TOK, 256), BF), pltpu.VMEM((TOK, D), BF), pltpu.VMEM((BLK, D), BF),
@@ -753,26 +743,27 @@
         ],
         vmem=24,
     )
-    own, *sends, sums = call(
+    own, *sends, sums, ff_part = call(
         normed_grad_kernel,
-        [((BLK, D), F32, "H")] + [((BLK, D), BF, "H")] * 3 + [((8, D), F32, "H")],
-        [(gqkv, "V"), (w_own, "V"), (tokens, "H"), (vec2, "H")],
-        1000,
-        [
-            pltpu.VMEM((TOK, D), BF), pltpu.VMEM((8, D), F32), pltpu.VMEM((TOK, D), F32), pltpu.VMEM((TOK, D), BF),
-            pltpu.VMEM((8, D), F32), DMA((2,)), DMA((5,)),
+        [((BLK, D), F32, "H")] + [((BLK, D), BF, "H")] * 3 + [((8, D), F32, "H"), ((2, 48, D), BF, "H")],
+        [(gqkv, "V"), (w_own, "V"), (tokens, "H"), (vec2, "H"), (ff_near, "H"), (ff_far, "V")],
+        1000,
+        [
+            pltpu.VMEM((TOK, D), BF), pltpu.VMEM((8, D), F32), pltpu.VMEM((2, 48, D), BF), pltpu.VMEM((TOK, D), F32),
+            pltpu.VMEM((TOK, D), BF), pltpu.VMEM((8, D), F32), pltpu.VMEM((2, 48, D), BF), DMA((3,)), DMA((6,)),
         ],
     )
     (weight_send,) = call(
         add_kernel,
         [((16, 48, 384), BF, "H")],
-        [(keep, "V"), (swap(send), "V"), (own, "H")],
+        [(keep, "V"), (swap(after(send, ff_far)), "V"), (own, "H")],
         1000,
         [pltpu.VMEM((16, 48, 384), BF), DMA],
     )
     weight_parts = exchange(weight_send, (*CHIP, MICRO))
     parts = [flip(value, GROUP, 4, k + 1) for k, value in enumerate(sends)]
-    weight_parts = after(weight_parts, pin(sums), *parts, *ff_parts)
+    weight_parts = after(weight_parts, pin(sums), *parts)
+    ff_parts = [flip(ff_part, "y", 4, k) for k in (1, 2, 3)]
     (weight_total,) = call(
         sum_kernel,
         [((8, 8, 56, 384), BF, "H")],
@@ -790,21 +781,20 @@
         1000,
         [pltpu.VMEM((2 * BLK, D), BF), pltpu.VMEM((BLK, D), BF), DMA((8,)), DMA],
     )
-    (ff_near,) = call(
+    weight_same = exchange(weight_total.reshape(64, 56, 384), (*CHIP, *NARROW)).reshape(8, 8, 56, 384)
+    (ff_same,) = call(
         stack_kernel,
-        [((4, 48, D), BF, "L")],
-        [(ff_part, "L"), *[(value, "V") for value in ff_parts]],
-        1000,
-    )
-    ff_far = flip(ff_near, "xl", 2, 1)
-    weight_same = exchange(weight_total.reshape(64, 56, 384), (*CHIP, *NARROW)).reshape(8, 8, 56, 384)
-    weight_same = after(weight_same, pin(packed), ff_far)
+        [((8, 48, D), BF, "L")],
+        [(ff_part, "L"), *[(value, "V") for value in ff_parts], (packed, "H")],
+        1000,
+    )
+    weight_same = after(weight_same, pin(packed), pin(ff_same))
     everyone = exchange(after(pin(packed), weight_same), NARROW)
     weight_other = swap(weight_same)
     up_grad, down_grad = call(
         spread_ff_kernel,
         [((D, FFL), F32, "L"), ((FFL, D), F32, "L")],
-        [(ff_near, "L"), (ff_far, "V"), (swap(ff_near), "V"), (swap(ff_far), "V")],
+        [(ff_same, "L"), (swap(ff_same), "V")],
         1000,
     )
     scratch = [

time: 212 us -> 211 us (level)
  starting transfers between devices: 74.3 us -> 71.2 us
  waiting for transfers between devices: 79.2 us -> 81.7 us
    all_to_all x7, starting transfers between devices: 47.1 us -> 44.5 us  [exchange(): return lax.all_to_all(value, axes, 0, 0, tiled=True)]
    pallas_call x20 -> x19, Pallas kernels: 52.6 us -> 53.7 us  [call(): pl.pallas_call(kernel, out_shape=[(pltpu.HBM if place in 'HL' else jax.Sh...]
    ppermute x14 -> x13, waiting for transfers between devices: 54.1 us -> 55 us  [flip(): lax.ppermute(value, axes, [(index, index ^ bits) for index in range(count)])]
    ppermute x7 -> x6, starting transfers between devices: 10.9 us -> 10.1 us  [swap(): return lax.ppermute(value, CORE, [(0, 1), (1, 0)])]
    ppermute x7 -> x6, waiting for transfers between devices: 5.91 us -> 6.12 us  [swap(): return lax.ppermute(value, CORE, [(0, 1), (1, 0)])]
    ppermute x14 -> x13, starting transfers between devices: 16.4 us -> 16.5 us  [flip(): lax.ppermute(value, axes, [(index, index ^ bits) for index in range(count)])]
  transfers between devices with their start and end apart: 28 -> 26, of which waited for: 16 -> 16; matrix products, arithmetic and copies ran while one was open for 1% -> 1% of each run, Pallas kernels for 13% -> 15%
where the time goes in v14:
time: 211 us; the launch traced here: 210 us
  waiting for transfers between devices  81.7 us (39%)
  starting transfers between devices  71.2 us (34%)
  Pallas kernels  53.8 us (25%)
  local copies, waits for them, and re-layouts  2.28 us (1%)
    ppermute x13, waiting for transfers between devices, flip(): lax.ppermute(value, axes, [(index, index ^ bits) for index in range(count)])  55 us
    pallas_call x19, Pallas kernels, call(): pl.pallas_call(kernel, out_shape=[(pltpu.HBM if place in 'HL' else jax.Sh...  53.7 us
    all_to_all x7, starting transfers between devices, exchange(): return lax.all_to_all(value, axes, 0, 0, tiled=True)  44.5 us
    all_to_all x7, waiting for transfers between devices, exchange(): return lax.all_to_all(value, axes, 0, 0, tiled=True)  20.6 us
    ppermute x13, starting transfers between devices, flip(): lax.ppermute(value, axes, [(index, index ^ bits) for index in range(count)])  16.5 us
    ppermute x6, starting transfers between devices, swap(): return lax.ppermute(value, CORE, [(0, 1), (1, 0)])  10.1 us
    ppermute x6, waiting for transfers between devices, swap(): return lax.ppermute(value, CORE, [(0, 1), (1, 0)])  6.12 us
  transfers between devices with their start and end apart: 26, of which 16 were waited for; matrix products, arithmetic and copies ran while one was open for 1% of the time, Pallas kernels for 15%

profile of v14, /device:TPU:1, one launch (start us, length us, event | category | flops | bytes accessed | tf_op | source)
XLA Modules:
  0.0 209.8 jit_solution(540332682296995322)
XLA Ops:
  0.6 3.7 %shard_map.186 = (bf16[8,128,384]{2,1,0:T(8,128)(2,1)}, bf16[128,768]{1,0:T(8,128)(2,1)}) custom-call(bf16[2,128,768]{2,1,0:T(8,128)(2,1)} %tok_ref.7, f32[768]{0:T(1024)} %gain_ref.7, f32[768]{0:T(1024)} %shift_ref.2, bf16[768,2304]{1,0:T(8,128)(2,1)} %w_ref.7), custom_call_target="tpu_custom_call" | custom-call | flops 1000 | bytes 1000 | tf_op jit(solution)/shard_map/pallas_call | solution.py:106
  4.3 6.0 %all-to-all-start = ((bf16[8,128,384]{2,1,0:T(8,128)(2,1)}), bf16[8,128,384]{2,1,0:T(8,128)(2,1)S(1)}, u32[]{:S(2)}, u32[]{:S(2)}) async-start(bf16[8,128,384]{2,1,0:T(8,128)(2,1)} %get-tuple-element.51), calls=%async_computation | async-start | bytes 1572864 | tf_op jit(solution)/shard_map/all_to_all | solution.py:610
  10.3 3.0 %shard_map.187.refs_1_.q_ref = bf16[128,256]{1,0:T(8,128)(2,1)} custom-call(bf16[128,768]{1,0:T(8,128)(2,1)} %get-tuple-element.52.normed_ref, bf16[768,2304]{1,0:T(8,128)(2,1)} %w_ref.7), custom_call_target="tpu_custom_call" | custom-call | flops 1000 | bytes 1000 | tf_op jit(solution)/shard_map/pallas_call | solution.py:106
  13.4 8.6 %all-to-all-done.refs_0_ = bf16[8,128,384]{2,1,0:T(8,128)(2,1)S(1)} async-done(((bf16[8,128,384]{2,1,0:T(8,128)(2,1)}), bf16[8,128,384]{2,1,0:T(8,128)(2,1)S(1)}, u32[]{:S(2)}, u32[]{:S(2)}) %all-to-all-start) | async-done | bytes 786464 | tf_op jit(solution)/shard_map/all_to_all | solution.py:610
  26.1 4.0 %shard_map.189 = bf16[8,128,256]{2,1,0:T(8,128)(2,1)} custom-call(s32[2,32]{1,0:T(2,128)S(1)} %copy-done.3, bf16[128,256]{1,0:T(8,128)(2,1)} %shard_map.187.refs_1_.q_ref, bf16[8,128,384]{2,1,0:T(8,128)(2,1)S(1)} %shard_map.188.same_ref.kvs_ref, bf16[8,128,384]{2,1,0:T(8,128)(2,1)S(1)} %collective-permute-done.other_ref.kvo_ref), custom_call_target="tpu_custom_call" | custom-call | flops 1000 | bytes 1000 | tf_op jit(solution)/shard_map/pallas_call | solution.py:106
  30.9 7.2 %all-to-all-start.1 = ((bf16[8,128,256]{2,1,0:T(8,128)(2,1)}), bf16[8,128,256]{2,1,0:T(8,128)(2,1)S(1)}, u32[]{:S(2)}, u32[]{:S(2)}) async-start(bf16[8,128,256]{2,1,0:T(8,128)(2,1)} %shard_map.189), calls=%async_computation.1 | async-start | bytes 1048576 | tf_op jit(solution)/shard_map/all_to_all | solution.py:610
  39.5 9.4 %all-to-all-done.1.mixed_ref = bf16[8,128,256]{2,1,0:T(8,128)(2,1)S(1)} async-done(((bf16[8,128,256]{2,1,0:T(8,128)(2,1)}), bf16[8,128,256]{2,1,0:T(8,128)(2,1)S(1)}, u32[]{:S(2)}, u32[]{:S(2)}) %all-to-all-start.1) | async-done | bytes 524320 | tf_op jit(solution)/shard_map/all_to_all | solution.py:610
  48.9 4.1 %shard_map.190 = (bf16[8,64,768]{2,1,0:T(8,128)(2,1)}, f32[32,768]{1,0:T(8,128)}, bf16[256,768]{1,0:T(8,128)(2,1)S(1)}, bf16[256,384]{1,0:T(8,128)(2,1)S(1)}, bf16[256,384]{1,0:T(8,128)(2,1)S(1)}) custom-call(bf16[8,128,256]{2,1,0:T(8,128)(2,1)S(1)} %all-to-all-done.1.mixed_ref, bf16[2,128,768]{2,1,0:T(8,128)(2,1)} %tok_ref.7, bf16[2,128,768]{2,1,0:T(8,128)(2,1)} %og_ref.5, ...), custom_call_target="tpu_custom_call" | custom-call | flops 1000 | bytes 1000 | tf_op jit(solution)/shard_map/pallas_call | solution.py:106
  53.1 2.8 %shard_map.191 = (bf16[8,48,768]{2,1,0:T(8,128)(2,1)S(1)}, bf16[8,48,768]{2,1,0:T(8,128)(2,1)}) custom-call(bf16[256,768]{1,0:T(8,128)(2,1)S(1)} %get-tuple-element.54.normed_ref, bf16[256,384]{1,0:T(8,128)(2,1)S(1)} %get-tuple-element.55.act_ref, bf16[256,384]{1,0:T(8,128)(2,1)S(1)} %get-tuple-element.56.gpre_ref, bf16[2,128,768]{2,1,0:T(8,128)(2,1)} %og_ref.5), custom_call_target="tpu_custom_call" | custom-call | flops 1000 | bytes 1000 | tf_op jit(solution)/shard_map/pallas_call | solution.py:106
  57.6 3.5 %all-to-all-start.2 = ((bf16[8,64,768]{2,1,0:T(8,128)(2,1)}), bf16[8,64,768]{2,1,0:T(8,128)(2,1)S(1)}, u32[]{:S(2)}, u32[]{:S(2)}) async-start(bf16[8,64,768]{2,1,0:T(8,128)(2,1)} %get-tuple-element.53), calls=%async_computation.2 | async-start | bytes 1572864 | tf_op jit(solution)/shard_map/all_to_all | solution.py:610
  63.9 3.0 %collective-permute-start.4 = (bf16[2,48,768]{2,1,0:T(8,128)(2,1)}, bf16[2,48,768]{2,1,0:T(8,128)(2,1)S(1)}, u32[]{:S(2)}, u32[]{:S(2)}) collective-permute-start(bf16[2,48,768]{2,1,0:T(8,128)(2,1)} %get-tuple-element.62), channel_id=1, source_target_pairs={{0,96},{32,64},{64,32},{96,0},{1,97},{33,65},{65,33},{97,1},{2,98}... | collective-permute-start | bytes 442376 | tf_op jit(solution)/shard_map/ppermute | solution.py:630
  71.4 2.9 %collective-permute-done.4.refs_3_ = bf16[2,48,768]{2,1,0:T(8,128)(2,1)S(1)} collective-permute-done((bf16[2,48,768]{2,1,0:T(8,128)(2,1)}, bf16[2,48,768]{2,1,0:T(8,128)(2,1)S(1)}, u32[]{:S(2)}, u32[]{:S(2)}) %collective-permute-start.4) | collective-permute-done | bytes 147488 | tf_op jit(solution)/shard_map/ppermute | solution.py:630
  75.9 3.0 %shard_map.196 = (bf16[8,4,32,512]{3,2,1,0:T(8,128)(2,1)}, bf16[32,768]{1,0:T(8,128)(2,1)}, f32[32,768]{1,0:T(8,128)}, bf16[32,768]{1,0:T(8,128)(2,1)}, f32[8,768]{1,0:T(8,128)}) custom-call(bf16[8,64,768]{2,1,0:T(8,128)(2,1)S(1)} %shard_map.194.sums_ref, f32[32,768]{1,0:T(8,128)} %get-tuple-element.63.middle_ref, bf16[2,128,768]{2,1,0:T(8,128)(2,1)} %og_ref.5, ...), custom_call_target="tpu_custom_call" | custom-call | flops 1000 | bytes 1000 | tf_op jit(solution)/shard_map/pallas_call | solution.py:106
  78.8 7.4 %all-to-all-start.3 = ((bf16[32,32,512]{2,1,0:T(8,128)(2,1)}), bf16[32,32,512]{2,1,0:T(8,128)(2,1)S(1)}, u32[]{:S(2)}, u32[]{:S(2)}) async-start(bf16[32,32,512]{2,1,0:T(8,128)(2,1)} %bitcast.9), calls=%async_computation.3 | async-start | bytes 2097152 | tf_op jit(solution)/shard_map/all_to_all | solution.py:610
  86.3 2.8 %collective-permute-start.5 = (bf16[32,768]{1,0:T(8,128)(2,1)}, bf16[32,768]{1,0:T(8,128)(2,1)S(1)}, u32[]{:S(2)}, u32[]{:S(2)}) collective-permute-start(bf16[32,768]{1,0:T(8,128)(2,1)} %get-tuple-element.65.low_ref), channel_id=1, source_target_pairs={{0,1},{1,0},{2,3},{3,2},{4,5},{5,4},{6,7},{7,6},{8,9},{9,8},{10,11... | collective-permute-start | bytes 147464 | tf_op jit(solution)/shard_map/ppermute | solution.py:630
  90.5 10.2 %collective-permute-done.5.refs_1_.low1_ref = bf16[32,768]{1,0:T(8,128)(2,1)S(1)} collective-permute-done((bf16[32,768]{1,0:T(8,128)(2,1)}, bf16[32,768]{1,0:T(8,128)(2,1)S(1)}, u32[]{:S(2)}, u32[]{:S(2)}) %collective-permute-start.5) | collective-permute-done | bytes 49184 | tf_op jit(solution)/shard_map/ppermute | solution.py:630
  103.3 2.5 %collective-permute-start.8 = (bf16[8,128,512]{2,1,0:T(8,128)(2,1)S(1)}, bf16[8,128,512]{2,1,0:T(8,128)(2,1)S(1)}, u32[]{:S(2)}, u32[]{:S(2)}) collective-permute-start(bf16[8,128,512]{2,1,0:T(8,128)(2,1)S(1)} %shard_map.197.gs_ref), channel_id=1, source_target_pairs={{0,8},{8,0},{1,9},{9,1},{2,10},{10,2},{3,11},{11,3},{4,12},{12,4},... | collective-permute-start | bytes 3145736 | tf_op jit(solution)/shard_map/ppermute | solution.py:614
  108.3 5.7 %shard_map.198 = (bf16[128,640]{1,0:T(8,128)(2,1)S(1)}, bf16[3,768,384]{2,1,0:T(8,128)(2,1)S(1)}, bf16[16,48,384]{2,1,0:T(8,128)(2,1)S(1)}, bf16[16,48,384]{2,1,0:T(8,128)(2,1)S(1)}) custom-call(s32[2,32]{1,0:T(2,128)S(1)} %copy-done.3, bf16[8,128,384]{2,1,0:T(8,128)(2,1)} %copy-done, bf16[8,128,384]{2,1,0:T(8,128)(2,1)} %copy-done.2, ...), custom_call_target="tpu_custom_call" | custom-call | flops 1000 | bytes 1000 | tf_op jit(solution)/shard_map/pallas_call | solution.py:106
  114.7 2.5 %shard_map.200 = (f32[32,768]{1,0:T(8,128)}, bf16[32,768]{1,0:T(8,128)(2,1)}, bf16[32,768]{1,0:T(8,128)(2,1)}, bf16[32,768]{1,0:T(8,128)(2,1)}, f32[8,768]{1,0:T(8,128)}, /*index=5*/bf16[2,48,768]{2,1,0:T(8,128)(2,1)}) custom-call(bf16[128,640]{1,0:T(8,128)(2,1)S(1)} %get-tuple-element.66.gqkv_ref, bf16[3,768,384]{2,1,0:T(8,128)(2,1)S(1)} %get-tuple-element.67.w_ref, ...), custom_call_target="tpu_custom_call" | custom-call | flops 1000 | bytes 1000 | tf_op jit(solution)/shard_map/pallas_call | solution.py:106
  118.3 5.7 %all-to-all-start.4 = ((bf16[16,48,384]{2,1,0:T(8,128)(2,1)}), bf16[16,48,384]{2,1,0:T(8,128)(2,1)S(1)}, u32[]{:S(2)}, u32[]{:S(2)}) async-start(bf16[16,48,384]{2,1,0:T(8,128)(2,1)} %shard_map.202), calls=%async_computation.4 | async-start | bytes 1179648 | tf_op jit(solution)/shard_map/all_to_all | solution.py:610
  125.7 2.5 %collective-permute-start.12 = (bf16[32,768]{1,0:T(8,128)(2,1)S(1)}, bf16[32,768]{1,0:T(8,128)(2,1)S(1)}, u32[]{:S(2)}, u32[]{:S(2)}) collective-permute-start(bf16[32,768]{1,0:T(8,128)(2,1)S(1)} %copy-done.5), channel_id=1, source_target_pairs={{0,3},{1,2},{2,1},{3,0},{4,7},{5,6},{6,5},{7,4},{8,11},{9,10},{10,... | collective-permute-start | bytes 147464 | tf_op jit(solution)/shard_map/ppermute | solution.py:630
  128.2 5.7 %collective-permute-done.10.refs_2_.one_ref = bf16[32,768]{1,0:T(8,128)(2,1)S(1)} collective-permute-done((bf16[32,768]{1,0:T(8,128)(2,1)S(1)}, bf16[32,768]{1,0:T(8,128)(2,1)S(1)}, u32[]{:S(2)}, u32[]{:S(2)}) %collective-permute-start.10) | collective-permute-done | bytes 49184 | tf_op jit(solution)/shard_map/ppermute | solution.py:630
  137.9 8.5 %all-to-all-start.5 = ((bf16[64,56,384]{2,1,0:T(8,128)(2,1)}), bf16[64,56,384]{2,1,0:T(8,128)(2,1)S(1)}, u32[]{:S(2)}, u32[]{:S(2)}) async-start(bf16[64,56,384]{2,1,0:T(8,128)(2,1)} %bitcast.7), calls=%async_computation.5 | async-start | bytes 5505024 | tf_op jit(solution)/shard_map/all_to_all | solution.py:610
  147.5 2.6 %collective-permute-start.15 = (bf16[2,48,768]{2,1,0:T(8,128)(2,1)S(1)}, bf16[2,48,768]{2,1,0:T(8,128)(2,1)S(1)}, u32[]{:S(2)}, u32[]{:S(2)}) collective-permute-start(bf16[2,48,768]{2,1,0:T(8,128)(2,1)S(1)} %copy-done.4), channel_id=1, source_target_pairs={{0,64},{32,96},{64,0},{96,32},{1,65},{33,97},{65,1},{97,33},{2,66}... | collective-permute-start | bytes 442376 | tf_op jit(solution)/shard_map/ppermute | solution.py:630
  150.4 3.0 %shard_map.205.refs_4_.refs_1_.refs_0_ = bf16[8,64,768]{2,1,0:T(8,128)(2,1)} custom-call(f32[32,768]{1,0:T(8,128)} %get-tuple-element.69.unused_ref.own_ref, bf16[32,768]{1,0:T(8,128)(2,1)S(1)} %collective-permute-done.10.refs_2_.one_ref, bf16[32,768]{1,0:T(8,128)(2,1)S(1)} %collective-permute-done.11.refs_3_.two_ref, ...), custom_call_target="tpu_custom_call" | custom-call | flops 1000 | bytes 1000 | tf_op jit(solution)/shard_map/pallas_call | solution.py:106
  153.3 24.7 %collective-permute-done.14.refs_1_ = bf16[2,48,768]{2,1,0:T(8,128)(2,1)S(1)} collective-permute-done((bf16[2,48,768]{2,1,0:T(8,128)(2,1)S(1)}, bf16[2,48,768]{2,1,0:T(8,128)(2,1)S(1)}, u32[]{:S(2)}, u32[]{:S(2)}) %collective-permute-start.14) | collective-permute-done | bytes 147488 | tf_op jit(solution)/shard_map/ppermute | solution.py:630
  178.0 5.8 %collective-permute-done.15.refs_2_ = bf16[2,48,768]{2,1,0:T(8,128)(2,1)S(1)} collective-permute-done((bf16[2,48,768]{2,1,0:T(8,128)(2,1)S(1)}, bf16[2,48,768]{2,1,0:T(8,128)(2,1)S(1)}, u32[]{:S(2)}, u32[]{:S(2)}) %collective-permute-start.15) | collective-permute-done | bytes 147488 | tf_op jit(solution)/shard_map/ppermute | solution.py:630
  185.6 2.7 %collective-permute-start.17 = (bf16[8,8,56,384]{3,2,1,0:T(8,128)(2,1)S(1)}, bf16[8,8,56,384]{3,2,1,0:T(8,128)(2,1)}, u32[]{:S(2)}, u32[]{:S(2)}) collective-permute-start(bf16[8,8,56,384]{3,2,1,0:T(8,128)(2,1)S(1)} %shard_map.207.refs_1_.in_ref), channel_id=1, source_target_pairs={{0,8},{8,0},{1,9},{9,1},{2,10},{10,2},{3,11},{11,3},{4,12},{12,4},... | collective-permute-start | bytes 8257544 | tf_op jit(solution)/shard_map/ppermute | solution.py:614
  188.3 6.2 %all-to-all-start.6 = ((bf16[8,64,768]{2,1,0:T(8,128)(2,1)}), bf16[8,64,768]{2,1,0:T(8,128)(2,1)S(1)}, u32[]{:S(2)}, u32[]{:S(2)}) async-start(bf16[8,64,768]{2,1,0:T(8,128)(2,1)} %shard_map.208), calls=%async_computation.6 | async-start | bytes 1572864 | tf_op jit(solution)/shard_map/all_to_all | solution.py:610
  196.7 2.6 %shard_map.211 = (f32[768,384]{1,0:T(8,128)}, f32[384,768]{1,0:T(8,128)}) custom-call(bf16[8,48,768]{2,1,0:T(8,128)(2,1)} %shard_map.206.refs_2_.same_ref, bf16[8,48,768]{2,1,0:T(8,128)(2,1)S(1)} %collective-permute-done.18.other_ref), custom_call_target="tpu_custom_call" | custom-call | flops 1000 | bytes 1000 | tf_op jit(solution)/shard_map/pallas_call | solution.py:106
  199.4 2.4 %shard_map.209 = (f32[768,2304]{1,0:T(8,128)}, f32[768,768]{1,0:T(8,128)}, f32[8,384]{1,0:T(8,128)S(1)}) custom-call(bf16[8,8,56,384]{3,2,1,0:T(8,128)(2,1)S(1)} %shard_map.207.refs_1_.in_ref), custom_call_target="tpu_custom_call" | custom-call | flops 1000 | bytes 1000 | tf_op jit(solution)/shard_map/pallas_call | solution.py:106
  201.8 4.8 %shard_map.210 = (f32[768,2304]{1,0:T(8,128)}, f32[768,768]{1,0:T(8,128)}, f32[768]{0:T(1024)}, f32[768]{0:T(1024)}, f32[768]{0:T(1024)}, /*index=5*/f32[768]{0:T(1024)}) custom-call(bf16[8,8,56,384]{3,2,1,0:T(8,128)(2,1)} %collective-permute-done.17.in_ref, f32[8,384]{1,0:T(8,128)S(1)} %get-tuple-element.79.refs_0_, ...), custom_call_target="tpu_custom_call", output_to_operand_aliasing={{0}: (2, {}), {1}: (3, {})} | custom-call | flops 1000 | bytes 1000 | tf_op jit(solution)/shard_map/pallas_call | solution.py:106
  (64 shorter events, 39.3 us)
Async XLA Ops:
  4.3 17.6 %all-to-all-start = ((bf16[8,128,384]{2,1,0:T(8,128)(2,1)}), bf16[8,128,384]{2,1,0:T(8,128)(2,1)S(1)}, u32[]{:S(2)}, u32[]{:S(2)}) async-start(bf16[8,128,384]{2,1,0:T(8,128)(2,1)} %get-tuple-element.51), calls=%async_computation | async-start | bytes 1572864 | tf_op jit(solution)/shard_map/all_to_all | solution.py:610
  10.3 15.8 %copy-start.3 = (s32[2,32]{1,0:T(2,128)S(1)}, s32[2,32]{1,0:T(2,128)}, u32[]{:S(2)}) copy-start(s32[2,32]{1,0:T(2,128)} %scene_ref.3) | copy-start | bytes 772
  22.0 17.5 %copy-start = (bf16[8,128,384]{2,1,0:T(8,128)(2,1)}, bf16[8,128,384]{2,1,0:T(8,128)(2,1)S(1)}, u32[]{:S(2)}) copy-start(bf16[8,128,384]{2,1,0:T(8,128)(2,1)S(1)} %shard_map.188.same_ref.kvs_ref) | copy-start | bytes 2359300
  22.0 4.1 %collective-permute-start = (bf16[8,128,384]{2,1,0:T(8,128)(2,1)S(1)}, bf16[8,128,384]{2,1,0:T(8,128)(2,1)S(1)}, u32[]{:S(2)}, u32[]{:S(2)}) collective-permute-start(bf16[8,128,384]{2,1,0:T(8,128)(2,1)S(1)} %shard_map.188.same_ref.kvs_ref), channel_id=1, source_target_pairs={{0,8},{8,0},{1,9},{9,1},{2,10},{10,2},{3,11},{11,3},{4,12},{12,4},... | collective-permute-start | bytes 2359304 | tf_op jit(solution)/shard_map/ppermute | solution.py:614
  30.9 18.0 %all-to-all-start.1 = ((bf16[8,128,256]{2,1,0:T(8,128)(2,1)}), bf16[8,128,256]{2,1,0:T(8,128)(2,1)S(1)}, u32[]{:S(2)}, u32[]{:S(2)}) async-start(bf16[8,128,256]{2,1,0:T(8,128)(2,1)} %shard_map.189), calls=%async_computation.1 | async-start | bytes 1048576 | tf_op jit(solution)/shard_map/all_to_all | solution.py:610
  48.9 8.7 %copy-start.1 = (bf16[8,128,256]{2,1,0:T(8,128)(2,1)}, bf16[8,128,256]{2,1,0:T(8,128)(2,1)S(1)}, u32[]{:S(2)}) copy-start(bf16[8,128,256]{2,1,0:T(8,128)(2,1)S(1)} %all-to-all-done.1.mixed_ref) | copy-start | bytes 1572868
  55.8 5.3 %collective-permute-start.1 = (bf16[8,48,768]{2,1,0:T(8,128)(2,1)}, bf16[8,48,768]{2,1,0:T(8,128)(2,1)}, u32[]{:S(2)}, u32[]{:S(2)}) collective-permute-start(bf16[8,48,768]{2,1,0:T(8,128)(2,1)} %get-tuple-element.58), channel_id=1, source_target_pairs={{0,8},{8,0},{1,9},{9,1},{2,10},{10,2},{3,11},{11,3},{4,12},{12,4},... | collective-permute-start | bytes 1769480 | tf_op jit(solution)/shard_map/ppermute | solution.py:614
  57.6 18.3 %all-to-all-start.2 = ((bf16[8,64,768]{2,1,0:T(8,128)(2,1)}), bf16[8,64,768]{2,1,0:T(8,128)(2,1)S(1)}, u32[]{:S(2)}, u32[]{:S(2)}) async-start(bf16[8,64,768]{2,1,0:T(8,128)(2,1)} %get-tuple-element.53), calls=%async_computation.2 | async-start | bytes 1572864 | tf_op jit(solution)/shard_map/all_to_all | solution.py:610
  63.1 6.2 %collective-permute-start.2 = (bf16[2,48,768]{2,1,0:T(8,128)(2,1)}, bf16[2,48,768]{2,1,0:T(8,128)(2,1)S(1)}, u32[]{:S(2)}, u32[]{:S(2)}) collective-permute-start(bf16[2,48,768]{2,1,0:T(8,128)(2,1)} %get-tuple-element.60), channel_id=1, source_target_pairs={{0,32},{32,0},{64,96},{96,64},{1,33},{33,1},{65,97},{97,65},{2,34}... | collective-permute-start | bytes 442376 | tf_op jit(solution)/shard_map/ppermute | solution.py:630
  63.1 8.3 %collective-permute-start.3 = (bf16[2,48,768]{2,1,0:T(8,128)(2,1)}, bf16[2,48,768]{2,1,0:T(8,128)(2,1)S(1)}, u32[]{:S(2)}, u32[]{:S(2)}) collective-permute-start(bf16[2,48,768]{2,1,0:T(8,128)(2,1)} %get-tuple-element.61), channel_id=1, source_target_pairs={{0,64},{32,96},{64,0},{96,32},{1,65},{33,97},{65,1},{97,33},{2,66}... | collective-permute-start | bytes 442376 | tf_op jit(solution)/shard_map/ppermute | solution.py:630
  63.9 10.3 %collective-permute-start.4 = (bf16[2,48,768]{2,1,0:T(8,128)(2,1)}, bf16[2,48,768]{2,1,0:T(8,128)(2,1)S(1)}, u32[]{:S(2)}, u32[]{:S(2)}) collective-permute-start(bf16[2,48,768]{2,1,0:T(8,128)(2,1)} %get-tuple-element.62), channel_id=1, source_target_pairs={{0,96},{32,64},{64,32},{96,0},{1,97},{33,65},{65,33},{97,1},{2,98}... | collective-permute-start | bytes 442376 | tf_op jit(solution)/shard_map/ppermute | solution.py:630
  78.8 24.4 %all-to-all-start.3 = ((bf16[32,32,512]{2,1,0:T(8,128)(2,1)}), bf16[32,32,512]{2,1,0:T(8,128)(2,1)S(1)}, u32[]{:S(2)}, u32[]{:S(2)}) async-start(bf16[32,32,512]{2,1,0:T(8,128)(2,1)} %bitcast.9), calls=%async_computation.3 | async-start | bytes 2097152 | tf_op jit(solution)/shard_map/all_to_all | solution.py:610
  86.3 14.4 %collective-permute-start.5 = (bf16[32,768]{1,0:T(8,128)(2,1)}, bf16[32,768]{1,0:T(8,128)(2,1)S(1)}, u32[]{:S(2)}, u32[]{:S(2)}) collective-permute-start(bf16[32,768]{1,0:T(8,128)(2,1)} %get-tuple-element.65.low_ref), channel_id=1, source_target_pairs={{0,1},{1,0},{2,3},{3,2},{4,5},{5,4},{6,7},{7,6},{8,9},{9,8},{10,11... | collective-permute-start | bytes 147464 | tf_op jit(solution)/shard_map/ppermute | solution.py:630
  89.1 11.7 %collective-permute-start.6 = (bf16[32,768]{1,0:T(8,128)(2,1)}, bf16[32,768]{1,0:T(8,128)(2,1)S(1)}, u32[]{:S(2)}, u32[]{:S(2)}) collective-permute-start(bf16[32,768]{1,0:T(8,128)(2,1)} %get-tuple-element.65.low_ref), channel_id=1, source_target_pairs={{0,2},{1,3},{2,0},{3,1},{4,6},{5,7},{6,4},{7,5},{8,10},{9,11},{10,... | collective-permute-start | bytes 147464 | tf_op jit(solution)/shard_map/ppermute | solution.py:630
  90.3 13.0 %collective-permute-start.7 = (bf16[32,768]{1,0:T(8,128)(2,1)}, bf16[32,768]{1,0:T(8,128)(2,1)S(1)}, u32[]{:S(2)}, u32[]{:S(2)}) collective-permute-start(bf16[32,768]{1,0:T(8,128)(2,1)} %get-tuple-element.65.low_ref), channel_id=1, source_target_pairs={{0,3},{1,2},{2,1},{3,0},{4,7},{5,6},{6,5},{7,4},{8,11},{9,10},{10,... | collective-permute-start | bytes 147464 | tf_op jit(solution)/shard_map/ppermute | solution.py:630
  103.3 4.7 %collective-permute-start.8 = (bf16[8,128,512]{2,1,0:T(8,128)(2,1)S(1)}, bf16[8,128,512]{2,1,0:T(8,128)(2,1)S(1)}, u32[]{:S(2)}, u32[]{:S(2)}) collective-permute-start(bf16[8,128,512]{2,1,0:T(8,128)(2,1)S(1)} %shard_map.197.gs_ref), channel_id=1, source_target_pairs={{0,8},{8,0},{1,9},{9,1},{2,10},{10,2},{3,11},{11,3},{4,12},{12,4},... | collective-permute-start | bytes 3145736 | tf_op jit(solution)/shard_map/ppermute | solution.py:614
  108.0 5.9 %collective-permute-start.9 = (bf16[2,48,768]{2,1,0:T(8,128)(2,1)}, bf16[2,48,768]{2,1,0:T(8,128)(2,1)S(1)}, u32[]{:S(2)}, u32[]{:S(2)}) collective-permute-start(bf16[2,48,768]{2,1,0:T(8,128)(2,1)} %shard_map.199.near_ref), channel_id=1, source_target_pairs={{0,16},{16,0},{1,17},{17,1},{2,18},{18,2},{3,19},{19,3},{4,20},{20... | collective-permute-start | bytes 442376 | tf_op jit(solution)/shard_map/ppermute | solution.py:630
  114.0 3.3 %collective-permute-start.13 = (bf16[16,48,384]{2,1,0:T(8,128)(2,1)S(1)}, bf16[16,48,384]{2,1,0:T(8,128)(2,1)S(1)}, u32[]{:S(2)}, u32[]{:S(2)}) collective-permute-start(bf16[16,48,384]{2,1,0:T(8,128)(2,1)S(1)} %shard_map.201), channel_id=1, source_target_pairs={{0,8},{8,0},{1,9},{9,1},{2,10},{10,2},{3,11},{11,3},{4,12},{12,4},... | collective-permute-start | bytes 1769480 | tf_op jit(solution)/shard_map/ppermute | solution.py:614
  117.2 8.4 %copy-start.6 = (bf16[32,768]{1,0:T(8,128)(2,1)S(1)}, bf16[32,768]{1,0:T(8,128)(2,1)}, u32[]{:S(2)}) copy-start(bf16[32,768]{1,0:T(8,128)(2,1)} %get-tuple-element.71) | copy-start | bytes 147460
  117.3 8.4 %copy-start.5 = (bf16[32,768]{1,0:T(8,128)(2,1)S(1)}, bf16[32,768]{1,0:T(8,128)(2,1)}, u32[]{:S(2)}) copy-start(bf16[32,768]{1,0:T(8,128)(2,1)} %get-tuple-element.72) | copy-start | bytes 147460
  118.3 17.2 %all-to-all-start.4 = ((bf16[16,48,384]{2,1,0:T(8,128)(2,1)}), bf16[16,48,384]{2,1,0:T(8,128)(2,1)S(1)}, u32[]{:S(2)}, u32[]{:S(2)}) async-start(bf16[16,48,384]{2,1,0:T(8,128)(2,1)} %shard_map.202), calls=%async_computation.4 | async-start | bytes 1179648 | tf_op jit(solution)/shard_map/all_to_all | solution.py:610
  124.0 10.0 %collective-permute-start.10 = (bf16[32,768]{1,0:T(8,128)(2,1)S(1)}, bf16[32,768]{1,0:T(8,128)(2,1)S(1)}, u32[]{:S(2)}, u32[]{:S(2)}) collective-permute-start(bf16[32,768]{1,0:T(8,128)(2,1)S(1)} %copy-done.7), channel_id=1, source_target_pairs={{0,1},{1,0},{2,3},{3,2},{4,5},{5,4},{6,7},{7,6},{8,9},{9,8},{10,11... | collective-permute-start | bytes 147464 | tf_op jit(solution)/shard_map/ppermute | solution.py:630
  125.7 8.2 %collective-permute-start.11 = (bf16[32,768]{1,0:T(8,128)(2,1)S(1)}, bf16[32,768]{1,0:T(8,128)(2,1)S(1)}, u32[]{:S(2)}, u32[]{:S(2)}) collective-permute-start(bf16[32,768]{1,0:T(8,128)(2,1)S(1)} %copy-done.6), channel_id=1, source_target_pairs={{0,2},{1,3},{2,0},{3,1},{4,6},{5,7},{6,4},{7,5},{8,10},{9,11},{10,... | collective-permute-start | bytes 147464 | tf_op jit(solution)/shard_map/ppermute | solution.py:630
  125.7 9.3 %collective-permute-start.12 = (bf16[32,768]{1,0:T(8,128)(2,1)S(1)}, bf16[32,768]{1,0:T(8,128)(2,1)S(1)}, u32[]{:S(2)}, u32[]{:S(2)}) collective-permute-start(bf16[32,768]{1,0:T(8,128)(2,1)S(1)} %copy-done.5), channel_id=1, source_target_pairs={{0,3},{1,2},{2,1},{3,0},{4,7},{5,6},{6,5},{7,4},{8,11},{9,10},{10,... | collective-permute-start | bytes 147464 | tf_op jit(solution)/shard_map/ppermute | solution.py:630
  137.8 8.6 %copy-start.4 = (bf16[2,48,768]{2,1,0:T(8,128)(2,1)S(1)}, bf16[2,48,768]{2,1,0:T(8,128)(2,1)}, u32[]{:S(2)}) copy-start(bf16[2,48,768]{2,1,0:T(8,128)(2,1)} %get-tuple-element.78.refs_0_) | copy-start | bytes 442372
  137.9 47.8 %all-to-all-start.5 = ((bf16[64,56,384]{2,1,0:T(8,128)(2,1)}), bf16[64,56,384]{2,1,0:T(8,128)(2,1)S(1)}, u32[]{:S(2)}, u32[]{:S(2)}) async-start(bf16[64,56,384]{2,1,0:T(8,128)(2,1)} %bitcast.7), calls=%async_computation.5 | async-start | bytes 5505024 | tf_op jit(solution)/shard_map/all_to_all | solution.py:610
  146.4 31.6 %collective-permute-start.14 = (bf16[2,48,768]{2,1,0:T(8,128)(2,1)S(1)}, bf16[2,48,768]{2,1,0:T(8,128)(2,1)S(1)}, u32[]{:S(2)}, u32[]{:S(2)}) collective-permute-start(bf16[2,48,768]{2,1,0:T(8,128)(2,1)S(1)} %copy-done.4), channel_id=1, source_target_pairs={{0,32},{32,0},{64,96},{96,64},{1,33},{33,1},{65,97},{97,65},{2,34}... | collective-permute-start | bytes 442376 | tf_op jit(solution)/shard_map/ppermute | solution.py:630
  147.5 36.3 %collective-permute-start.15 = (bf16[2,48,768]{2,1,0:T(8,128)(2,1)S(1)}, bf16[2,48,768]{2,1,0:T(8,128)(2,1)S(1)}, u32[]{:S(2)}, u32[]{:S(2)}) collective-permute-start(bf16[2,48,768]{2,1,0:T(8,128)(2,1)S(1)} %copy-done.4), channel_id=1, source_target_pairs={{0,64},{32,96},{64,0},{96,32},{1,65},{33,97},{65,1},{97,33},{2,66}... | collective-permute-start | bytes 442376 | tf_op jit(solution)/shard_map/ppermute | solution.py:630
  150.1 33.7 %collective-permute-start.16 = (bf16[2,48,768]{2,1,0:T(8,128)(2,1)S(1)}, bf16[2,48,768]{2,1,0:T(8,128)(2,1)S(1)}, u32[]{:S(2)}, u32[]{:S(2)}) collective-permute-start(bf16[2,48,768]{2,1,0:T(8,128)(2,1)S(1)} %copy-done.4), channel_id=1, source_target_pairs={{0,96},{32,64},{64,32},{96,0},{1,97},{33,65},{65,33},{97,1},{2,98}... | collective-permute-start | bytes 442376 | tf_op jit(solution)/shard_map/ppermute | solution.py:630
  185.6 16.2 %collective-permute-start.17 = (bf16[8,8,56,384]{3,2,1,0:T(8,128)(2,1)S(1)}, bf16[8,8,56,384]{3,2,1,0:T(8,128)(2,1)}, u32[]{:S(2)}, u32[]{:S(2)}) collective-permute-start(bf16[8,8,56,384]{3,2,1,0:T(8,128)(2,1)S(1)} %shard_map.207.refs_1_.in_ref), channel_id=1, source_target_pairs={{0,8},{8,0},{1,9},{9,1},{2,10},{10,2},{3,11},{11,3},{4,12},{12,4},... | collective-permute-start | bytes 8257544 | tf_op jit(solution)/shard_map/ppermute | solution.py:614
  188.3 20.4 %all-to-all-start.6 = ((bf16[8,64,768]{2,1,0:T(8,128)(2,1)}), bf16[8,64,768]{2,1,0:T(8,128)(2,1)S(1)}, u32[]{:S(2)}, u32[]{:S(2)}) async-start(bf16[8,64,768]{2,1,0:T(8,128)(2,1)} %shard_map.208), calls=%async_computation.6 | async-start | bytes 1572864 | tf_op jit(solution)/shard_map/all_to_all | solution.py:610
  194.5 2.2 %collective-permute-start.18 = (bf16[8,48,768]{2,1,0:T(8,128)(2,1)}, bf16[8,48,768]{2,1,0:T(8,128)(2,1)S(1)}, u32[]{:S(2)}, u32[]{:S(2)}) collective-permute-start(bf16[8,48,768]{2,1,0:T(8,128)(2,1)} %shard_map.206.refs_2_.same_ref), channel_id=1, source_target_pairs={{0,8},{8,0},{1,9},{9,1},{2,10},{10,2},{3,11},{11,3},{4,12},{12,4},... | collective-permute-start | bytes 1769480 | tf_op jit(solution)/shard_map/ppermute | solution.py:614
  (2 other events, 7.6 us)

commit v15 on v14

--- a/solution.py
+++ b/solution.py
@@ -386,10 +386,7 @@
 
     def run(count):
         rows = count * TOK
-        loads = [
-            pltpu.make_async_copy(ref.at[pl.ds(first, count)], kv_buf.at[slot, pl.ds(0, count)], kv_sem.at[slot])
-            for slot, ref in enumerate((kvs_ref, kvo_ref))
-        ]
+        loads = [pltpu.make_async_copy(kvs_ref.at[pl.ds(first, count)], kv_buf.at[pl.ds(0, count)], kv_sem)]
         for load in loads + first_loads:
             load.start()
         weight_copies(w_ref, w_out_ref, w_sem)
@@ -406,8 +403,10 @@
         own_stats = g_own[0].astype(F32)
         all_stats = grad[0].astype(F32).T
         wait_all(loads)
-        kv = cut(jnp.concatenate([kv_buf[slot, :count].reshape(rows, 384) for slot in range(2)], axis=0))
-        own = cut(kv_buf[0, chip - first]) + g_own[2:]
+        kv = cut(jnp.concatenate(
+            [kv_buf[:count].reshape(rows, 384), kvo_ref[pl.ds(first, count)].reshape(rows, 384)], axis=0
+        ))
+        own = cut(kv_buf[chip - first]) + g_own[2:]
         q_heads = [*halves(own[3]), own[4]]
         k_heads = [*halves(own[0]), halves(own[1])[0]]
         v_heads = [halves(own[1])[1], *halves(own[2])]
@@ -704,7 +703,6 @@
         [(pieces[0], "L")] + [(piece, "V") for piece in pieces[1:]],
         1000,
     )
-    ff_sums = after(ff_sums, pin(ff_near))
     grad_send, low, grad_mid, result_part, vec2 = call(
         middle_kernel,
         [
@@ -722,9 +720,12 @@
             pltpu.VMEM((BLK, D), BF), pltpu.VMEM((8, D), F32), DMA((5,)), DMA((8,)), DMA((4,)),
         ],
     )
+    grad_send = after(pin(grad_send), *pieces[1:])
     grad_same = exchange(grad_send.reshape(32, BLK, 512), (*CHIP, *GROUP)).reshape(8, TOK, 512)
     lows = [flip(low, GROUP, 4, k) for k in (1, 2, 3)]
-    grad_same = after(grad_same, *lows)
+    kv_same = after(pin(kv_same), low)
+    kv_other = swap(kv_same)
+    grad_same = after(grad_same, *lows, kv_other, pin(ff_near))
     grad_other = swap(grad_same)
     ff_near = after(pin(ff_near), grad_other)
     ff_far = flip(ff_near, "xl", 2, 1)
@@ -732,14 +733,14 @@
         attend_back_kernel,
         [((TOK, 640), BF, "V"), ((3, D, 384), BF, "V")] + [((16, 48, 384), BF, "V")] * 2,
         [
-            (scene_of_block, "S"), (kv_same, "H"), (kv_other, "H"), (grad_same, "V"), (grad_other, "V"),
+            (scene_of_block, "S"), (kv_same, "H"), (kv_other, "V"), (grad_same, "V"), (grad_other, "V"),
             (normed, "H"), (mixed, "H"), (low, "H"), *[(value, "V") for value in lows], (w_qkv, "H"),
         ],
         1000,
         [
-            pltpu.VMEM((2, 5, TOK, 384), BF), pltpu.VMEM((D, 640), F32),
+            pltpu.VMEM((5, TOK, 384), BF), pltpu.VMEM((D, 640), F32),
             pltpu.VMEM((TOK, 256), BF), pltpu.VMEM((TOK, D), BF), pltpu.VMEM((BLK, D), BF),
-            DMA((2,)), DMA((3,)), DMA((3,)),
+            DMA, DMA((3,)), DMA((3,)),
         ],
         vmem=24,
     )

time: 211 us -> 206 us (0.976)
  starting transfers between devices: 71.2 us -> 68.9 us
  Pallas kernels: 53.8 us -> 51.6 us
    ppermute x13, waiting for transfers between devices: 55 us -> 48.2 us  [flip(): lax.ppermute(value, axes, [(index, index ^ bits) for index in range(count)])]
    all_to_all x7, waiting for transfers between devices: 20.6 us -> 27 us  [exchange(): return lax.all_to_all(value, axes, 0, 0, tiled=True)]
    all_to_all x7, starting transfers between devices: 44.5 us -> 41.4 us  [exchange(): return lax.all_to_all(value, axes, 0, 0, tiled=True)]
    pallas_call x19, Pallas kernels: 53.7 us -> 51.6 us  [call(): pl.pallas_call(kernel, out_shape=[(pltpu.HBM if place in 'HL' else jax.Sh...]
    ppermute x6 -> x7, starting transfers between devices: 10.1 us -> 11.1 us  [swap(): return lax.ppermute(value, CORE, [(0, 1), (1, 0)])]
    ppermute x6 -> x7, waiting for transfers between devices: 6.12 us -> 6.12 us  [swap(): return lax.ppermute(value, CORE, [(0, 1), (1, 0)])]
  transfers between devices with their start and end apart: 26 -> 27, of which waited for: 16 -> 15; matrix products, arithmetic and copies ran while one was open for 1% -> 1% of each run, Pallas kernels for 15% -> 16%
where the time goes in v15:
time: 206 us; the launch traced here: 204 us
  waiting for transfers between devices  81.3 us (39%)
  starting transfers between devices  68.9 us (33%)
  Pallas kernels  51.6 us (25%)
    pallas_call x19, Pallas kernels, call(): pl.pallas_call(kernel, out_shape=[(pltpu.HBM if place in 'HL' else jax.Sh...  51.6 us
    ppermute x13, waiting for transfers between devices, flip(): lax.ppermute(value, axes, [(index, index ^ bits) for index in range(count)])  48.2 us
    all_to_all x7, starting transfers between devices, exchange(): return lax.all_to_all(value, axes, 0, 0, tiled=True)  41.4 us
    all_to_all x7, waiting for transfers between devices, exchange(): return lax.all_to_all(value, axes, 0, 0, tiled=True)  27 us
    ppermute x13, starting transfers between devices, flip(): lax.ppermute(value, axes, [(index, index ^ bits) for index in range(count)])  16.5 us
    ppermute x7, starting transfers between devices, swap(): return lax.ppermute(value, CORE, [(0, 1), (1, 0)])  11.1 us
    ppermute x7, waiting for transfers between devices, swap(): return lax.ppermute(value, CORE, [(0, 1), (1, 0)])  6.12 us
  transfers between devices with their start and end apart: 27, of which 15 were waited for; matrix products, arithmetic and copies ran while one was open for 1% of the time, Pallas kernels for 16%

profile of v15, /device:TPU:1, one launch (start us, length us, event | category | flops | bytes accessed | tf_op | source)
XLA Modules:
  0.0 204.2 jit_solution(6871591952621977666)
XLA Ops:
  0.6 3.7 %shard_map.186 = (bf16[8,128,384]{2,1,0:T(8,128)(2,1)}, bf16[128,768]{1,0:T(8,128)(2,1)}) custom-call(bf16[2,128,768]{2,1,0:T(8,128)(2,1)} %tok_ref.7, f32[768]{0:T(1024)} %gain_ref.7, f32[768]{0:T(1024)} %shift_ref.2, bf16[768,2304]{1,0:T(8,128)(2,1)} %w_ref.7), custom_call_target="tpu_custom_call" | custom-call | flops 1000 | bytes 1000 | tf_op jit(solution)/shard_map/pallas_call | solution.py:106
  4.3 6.0 %all-to-all-start = ((bf16[8,128,384]{2,1,0:T(8,128)(2,1)}), bf16[8,128,384]{2,1,0:T(8,128)(2,1)S(1)}, u32[]{:S(2)}, u32[]{:S(2)}) async-start(bf16[8,128,384]{2,1,0:T(8,128)(2,1)} %get-tuple-element.51), calls=%async_computation | async-start | bytes 1572864 | tf_op jit(solution)/shard_map/all_to_all | solution.py:609
  10.3 3.0 %shard_map.187.refs_1_.q_ref = bf16[128,256]{1,0:T(8,128)(2,1)} custom-call(bf16[128,768]{1,0:T(8,128)(2,1)} %get-tuple-element.52.normed_ref, bf16[768,2304]{1,0:T(8,128)(2,1)} %w_ref.7), custom_call_target="tpu_custom_call" | custom-call | flops 1000 | bytes 1000 | tf_op jit(solution)/shard_map/pallas_call | solution.py:106
  13.4 8.6 %all-to-all-done.refs_0_ = bf16[8,128,384]{2,1,0:T(8,128)(2,1)S(1)} async-done(((bf16[8,128,384]{2,1,0:T(8,128)(2,1)}), bf16[8,128,384]{2,1,0:T(8,128)(2,1)S(1)}, u32[]{:S(2)}, u32[]{:S(2)}) %all-to-all-start) | async-done | bytes 786464 | tf_op jit(solution)/shard_map/all_to_all | solution.py:609
  26.1 3.1 %shard_map.189 = bf16[8,128,256]{2,1,0:T(8,128)(2,1)} custom-call(s32[2,32]{1,0:T(2,128)S(1)} %copy-done.3, bf16[128,256]{1,0:T(8,128)(2,1)} %shard_map.187.refs_1_.q_ref, bf16[8,128,384]{2,1,0:T(8,128)(2,1)S(1)} %shard_map.188.same_ref.refs_0_, bf16[8,128,384]{2,1,0:T(8,128)(2,1)S(1)} %collective-permute-done.other_ref), custom_call_target="tpu_custom_call" | custom-call | flops 1000 | bytes 1000 | tf_op jit(solution)/shard_map/pallas_call | solution.py:106
  29.2 7.2 %all-to-all-start.1 = ((bf16[8,128,256]{2,1,0:T(8,128)(2,1)}), bf16[8,128,256]{2,1,0:T(8,128)(2,1)S(1)}, u32[]{:S(2)}, u32[]{:S(2)}) async-start(bf16[8,128,256]{2,1,0:T(8,128)(2,1)} %shard_map.189), calls=%async_computation.1 | async-start | bytes 1048576 | tf_op jit(solution)/shard_map/all_to_all | solution.py:609
  37.8 9.4 %all-to-all-done.1.mixed_ref = bf16[8,128,256]{2,1,0:T(8,128)(2,1)S(1)} async-done(((bf16[8,128,256]{2,1,0:T(8,128)(2,1)}), bf16[8,128,256]{2,1,0:T(8,128)(2,1)S(1)}, u32[]{:S(2)}, u32[]{:S(2)}) %all-to-all-start.1) | async-done | bytes 524320 | tf_op jit(solution)/shard_map/all_to_all | solution.py:609
  47.1 4.2 %shard_map.190 = (bf16[8,64,768]{2,1,0:T(8,128)(2,1)}, f32[32,768]{1,0:T(8,128)}, bf16[256,768]{1,0:T(8,128)(2,1)S(1)}, bf16[256,384]{1,0:T(8,128)(2,1)S(1)}, bf16[256,384]{1,0:T(8,128)(2,1)S(1)}) custom-call(bf16[8,128,256]{2,1,0:T(8,128)(2,1)S(1)} %all-to-all-done.1.mixed_ref, bf16[2,128,768]{2,1,0:T(8,128)(2,1)} %tok_ref.7, bf16[2,128,768]{2,1,0:T(8,128)(2,1)} %og_ref.5, ...), custom_call_target="tpu_custom_call" | custom-call | flops 1000 | bytes 1000 | tf_op jit(solution)/shard_map/pallas_call | solution.py:106
  51.3 2.8 %shard_map.194 = (bf16[8,48,768]{2,1,0:T(8,128)(2,1)S(1)}, bf16[8,48,768]{2,1,0:T(8,128)(2,1)}) custom-call(bf16[256,768]{1,0:T(8,128)(2,1)S(1)} %get-tuple-element.57.normed_ref, bf16[256,384]{1,0:T(8,128)(2,1)S(1)} %get-tuple-element.58.act_ref, bf16[256,384]{1,0:T(8,128)(2,1)S(1)} %get-tuple-element.59.gpre_ref, bf16[2,128,768]{2,1,0:T(8,128)(2,1)} %og_ref.5), custom_call_target="tpu_custom_call" | custom-call | flops 1000 | bytes 1000 | tf_op jit(solution)/shard_map/pallas_call | solution.py:106
  55.8 3.5 %all-to-all-start.2 = ((bf16[8,64,768]{2,1,0:T(8,128)(2,1)}), bf16[8,64,768]{2,1,0:T(8,128)(2,1)S(1)}, u32[]{:S(2)}, u32[]{:S(2)}) async-start(bf16[8,64,768]{2,1,0:T(8,128)(2,1)} %get-tuple-element.53), calls=%async_computation.2 | async-start | bytes 1572864 | tf_op jit(solution)/shard_map/all_to_all | solution.py:609
  67.5 6.4 %all-to-all-done.2.sums_ref = bf16[8,64,768]{2,1,0:T(8,128)(2,1)S(1)} async-done(((bf16[8,64,768]{2,1,0:T(8,128)(2,1)}), bf16[8,64,768]{2,1,0:T(8,128)(2,1)S(1)}, u32[]{:S(2)}, u32[]{:S(2)}) %all-to-all-start.2) | async-done | bytes 786464 | tf_op jit(solution)/shard_map/all_to_all | solution.py:609
  73.9 3.0 %shard_map.192 = (bf16[8,4,32,512]{3,2,1,0:T(8,128)(2,1)}, bf16[32,768]{1,0:T(8,128)(2,1)}, f32[32,768]{1,0:T(8,128)}, bf16[32,768]{1,0:T(8,128)(2,1)}, f32[8,768]{1,0:T(8,128)}) custom-call(bf16[8,64,768]{2,1,0:T(8,128)(2,1)S(1)} %all-to-all-done.2.sums_ref, f32[32,768]{1,0:T(8,128)} %get-tuple-element.54.middle_ref, bf16[2,128,768]{2,1,0:T(8,128)(2,1)} %og_ref.5, ...), custom_call_target="tpu_custom_call" | custom-call | flops 1000 | bytes 1000 | tf_op jit(solution)/shard_map/pallas_call | solution.py:106
  76.9 3.9 %all-to-all-start.3 = ((bf16[32,32,512]{2,1,0:T(8,128)(2,1)}), bf16[32,32,512]{2,1,0:T(8,128)(2,1)S(1)}, u32[]{:S(2)}, u32[]{:S(2)}) async-start(bf16[32,32,512]{2,1,0:T(8,128)(2,1)} %bitcast.8), calls=%async_computation.3 | async-start | bytes 2097152 | tf_op jit(solution)/shard_map/all_to_all | solution.py:609
  81.7 2.9 %collective-permute-start.6 = (bf16[32,768]{1,0:T(8,128)(2,1)S(1)}, bf16[32,768]{1,0:T(8,128)(2,1)S(1)}, u32[]{:S(2)}, u32[]{:S(2)}) collective-permute-start(bf16[32,768]{1,0:T(8,128)(2,1)S(1)} %copy-done.2), channel_id=1, source_target_pairs={{0,1},{1,0},{2,3},{3,2},{4,5},{5,4},{6,7},{7,6},{8,9},{9,8},{10,11... | collective-permute-start | bytes 147464 | tf_op jit(solution)/shard_map/ppermute | solution.py:629
  87.6 8.3 %collective-permute-done.6.refs_1_.low1_ref = bf16[32,768]{1,0:T(8,128)(2,1)S(1)} collective-permute-done((bf16[32,768]{1,0:T(8,128)(2,1)S(1)}, bf16[32,768]{1,0:T(8,128)(2,1)S(1)}, u32[]{:S(2)}, u32[]{:S(2)}) %collective-permute-start.6) | collective-permute-done | bytes 49184 | tf_op jit(solution)/shard_map/ppermute | solution.py:629
  95.8 2.4 %collective-permute-done.8.refs_3_.low3_ref = bf16[32,768]{1,0:T(8,128)(2,1)S(1)} collective-permute-done((bf16[32,768]{1,0:T(8,128)(2,1)S(1)}, bf16[32,768]{1,0:T(8,128)(2,1)S(1)}, u32[]{:S(2)}, u32[]{:S(2)}) %collective-permute-start.8) | collective-permute-done | bytes 49184 | tf_op jit(solution)/shard_map/ppermute | solution.py:629
  102.8 4.3 %shard_map.199 = (bf16[128,640]{1,0:T(8,128)(2,1)S(1)}, bf16[3,768,384]{2,1,0:T(8,128)(2,1)S(1)}, bf16[16,48,384]{2,1,0:T(8,128)(2,1)S(1)}, bf16[16,48,384]{2,1,0:T(8,128)(2,1)S(1)}) custom-call(s32[2,32]{1,0:T(2,128)S(1)} %copy-done.3, bf16[8,128,384]{2,1,0:T(8,128)(2,1)} %shard_map.193.kvs_ref, ...), custom_call_target="tpu_custom_call" | custom-call | flops 1000 | bytes 1000 | tf_op jit(solution)/shard_map/pallas_call | solution.py:106
  109.0 2.5 %shard_map.201 = (f32[32,768]{1,0:T(8,128)}, bf16[32,768]{1,0:T(8,128)(2,1)}, bf16[32,768]{1,0:T(8,128)(2,1)}, bf16[32,768]{1,0:T(8,128)(2,1)}, f32[8,768]{1,0:T(8,128)}, /*index=5*/bf16[2,48,768]{2,1,0:T(8,128)(2,1)}) custom-call(bf16[128,640]{1,0:T(8,128)(2,1)S(1)} %get-tuple-element.66.gqkv_ref, bf16[3,768,384]{2,1,0:T(8,128)(2,1)S(1)} %get-tuple-element.67.w_ref, ...), custom_call_target="tpu_custom_call" | custom-call | flops 1000 | bytes 1000 | tf_op jit(solution)/shard_map/pallas_call | solution.py:106
  112.5 6.0 %all-to-all-start.4 = ((bf16[16,48,384]{2,1,0:T(8,128)(2,1)}), bf16[16,48,384]{2,1,0:T(8,128)(2,1)S(1)}, u32[]{:S(2)}, u32[]{:S(2)}) async-start(bf16[16,48,384]{2,1,0:T(8,128)(2,1)} %shard_map.203), calls=%async_computation.4 | async-start | bytes 1179648 | tf_op jit(solution)/shard_map/all_to_all | solution.py:609
  119.4 3.4 %collective-permute-start.13 = (bf16[32,768]{1,0:T(8,128)(2,1)S(1)}, bf16[32,768]{1,0:T(8,128)(2,1)S(1)}, u32[]{:S(2)}, u32[]{:S(2)}) collective-permute-start(bf16[32,768]{1,0:T(8,128)(2,1)S(1)} %copy-done.5), channel_id=1, source_target_pairs={{0,3},{1,2},{2,1},{3,0},{4,7},{5,6},{6,5},{7,4},{8,11},{9,10},{10,... | collective-permute-start | bytes 147464 | tf_op jit(solution)/shard_map/ppermute | solution.py:629
  122.7 4.9 %collective-permute-done.11.refs_2_.one_ref = bf16[32,768]{1,0:T(8,128)(2,1)S(1)} collective-permute-done((bf16[32,768]{1,0:T(8,128)(2,1)S(1)}, bf16[32,768]{1,0:T(8,128)(2,1)S(1)}, u32[]{:S(2)}, u32[]{:S(2)}) %collective-permute-start.11) | collective-permute-done | bytes 49184 | tf_op jit(solution)/shard_map/ppermute | solution.py:629
  130.0 2.4 %shard_map.205.unused_ref = bf16[8,8,56,384]{3,2,1,0:T(8,128)(2,1)} custom-call(bf16[16,48,384]{2,1,0:T(8,128)(2,1)S(1)} %shard_map.204.in_ref, f32[8,768]{1,0:T(8,128)} %get-tuple-element.77.refs_1_.vec_ref), custom_call_target="tpu_custom_call" | custom-call | flops 1000 | bytes 1000 | tf_op jit(solution)/shard_map/pallas_call | solution.py:106
  132.4 8.3 %all-to-all-start.5 = ((bf16[64,56,384]{2,1,0:T(8,128)(2,1)}), bf16[64,56,384]{2,1,0:T(8,128)(2,1)S(1)}, u32[]{:S(2)}, u32[]{:S(2)}) async-start(bf16[64,56,384]{2,1,0:T(8,128)(2,1)} %bitcast.7), calls=%async_computation.5 | async-start | bytes 5505024 | tf_op jit(solution)/shard_map/all_to_all | solution.py:609
  141.9 2.6 %collective-permute-start.16 = (bf16[2,48,768]{2,1,0:T(8,128)(2,1)S(1)}, bf16[2,48,768]{2,1,0:T(8,128)(2,1)S(1)}, u32[]{:S(2)}, u32[]{:S(2)}) collective-permute-start(bf16[2,48,768]{2,1,0:T(8,128)(2,1)S(1)} %copy-done.4), channel_id=1, source_target_pairs={{0,64},{32,96},{64,0},{96,32},{1,65},{33,97},{65,1},{97,33},{2,66}... | collective-permute-start | bytes 442376 | tf_op jit(solution)/shard_map/ppermute | solution.py:629
  144.7 3.0 %shard_map.206.refs_4_.refs_1_.refs_0_ = bf16[8,64,768]{2,1,0:T(8,128)(2,1)} custom-call(f32[32,768]{1,0:T(8,128)} %get-tuple-element.69.unused_ref.own_ref, bf16[32,768]{1,0:T(8,128)(2,1)S(1)} %collective-permute-done.11.refs_2_.one_ref, bf16[32,768]{1,0:T(8,128)(2,1)S(1)} %collective-permute-done.12.refs_3_.two_ref, ...), custom_call_target="tpu_custom_call" | custom-call | flops 1000 | bytes 1000 | tf_op jit(solution)/shard_map/pallas_call | solution.py:106
  147.7 26.3 %collective-permute-done.15.refs_1_ = bf16[2,48,768]{2,1,0:T(8,128)(2,1)S(1)} collective-permute-done((bf16[2,48,768]{2,1,0:T(8,128)(2,1)S(1)}, bf16[2,48,768]{2,1,0:T(8,128)(2,1)S(1)}, u32[]{:S(2)}, u32[]{:S(2)}) %collective-permute-start.15) | collective-permute-done | bytes 147488 | tf_op jit(solution)/shard_map/ppermute | solution.py:629
  174.0 3.8 %collective-permute-done.16.refs_2_ = bf16[2,48,768]{2,1,0:T(8,128)(2,1)S(1)} collective-permute-done((bf16[2,48,768]{2,1,0:T(8,128)(2,1)S(1)}, bf16[2,48,768]{2,1,0:T(8,128)(2,1)S(1)}, u32[]{:S(2)}, u32[]{:S(2)}) %collective-permute-start.16) | collective-permute-done | bytes 147488 | tf_op jit(solution)/shard_map/ppermute | solution.py:629
  179.5 2.9 %collective-permute-start.18 = (bf16[8,8,56,384]{3,2,1,0:T(8,128)(2,1)S(1)}, bf16[8,8,56,384]{3,2,1,0:T(8,128)(2,1)}, u32[]{:S(2)}, u32[]{:S(2)}) collective-permute-start(bf16[8,8,56,384]{3,2,1,0:T(8,128)(2,1)S(1)} %shard_map.208.refs_1_.in_ref), channel_id=1, source_target_pairs={{0,8},{8,0},{1,9},{9,1},{2,10},{10,2},{3,11},{11,3},{4,12},{12,4},... | collective-permute-start | bytes 8257544 | tf_op jit(solution)/shard_map/ppermute | solution.py:613
  182.4 6.4 %all-to-all-start.6 = ((bf16[8,64,768]{2,1,0:T(8,128)(2,1)}), bf16[8,64,768]{2,1,0:T(8,128)(2,1)S(1)}, u32[]{:S(2)}, u32[]{:S(2)}) async-start(bf16[8,64,768]{2,1,0:T(8,128)(2,1)} %shard_map.209), calls=%async_computation.6 | async-start | bytes 1572864 | tf_op jit(solution)/shard_map/all_to_all | solution.py:609
  191.1 2.6 %shard_map.212 = (f32[768,384]{1,0:T(8,128)}, f32[384,768]{1,0:T(8,128)}) custom-call(bf16[8,48,768]{2,1,0:T(8,128)(2,1)} %shard_map.207.refs_2_.same_ref, bf16[8,48,768]{2,1,0:T(8,128)(2,1)S(1)} %collective-permute-done.19.other_ref), custom_call_target="tpu_custom_call" | custom-call | flops 1000 | bytes 1000 | tf_op jit(solution)/shard_map/pallas_call | solution.py:106
  193.7 2.4 %shard_map.210 = (f32[768,2304]{1,0:T(8,128)}, f32[768,768]{1,0:T(8,128)}, f32[8,384]{1,0:T(8,128)S(1)}) custom-call(bf16[8,8,56,384]{3,2,1,0:T(8,128)(2,1)S(1)} %shard_map.208.refs_1_.in_ref), custom_call_target="tpu_custom_call" | custom-call | flops 1000 | bytes 1000 | tf_op jit(solution)/shard_map/pallas_call | solution.py:106
  196.2 4.8 %shard_map.211 = (f32[768,2304]{1,0:T(8,128)}, f32[768,768]{1,0:T(8,128)}, f32[768]{0:T(1024)}, f32[768]{0:T(1024)}, f32[768]{0:T(1024)}, /*index=5*/f32[768]{0:T(1024)}) custom-call(bf16[8,8,56,384]{3,2,1,0:T(8,128)(2,1)} %collective-permute-done.18.in_ref, f32[8,384]{1,0:T(8,128)S(1)} %get-tuple-element.79.refs_0_, ...), custom_call_target="tpu_custom_call", output_to_operand_aliasing={{0}: (2, {}), {1}: (3, {})} | custom-call | flops 1000 | bytes 1000 | tf_op jit(solution)/shard_map/pallas_call | solution.py:106
  (67 shorter events, 38.2 us)
Async XLA Ops:
  4.3 17.6 %all-to-all-start = ((bf16[8,128,384]{2,1,0:T(8,128)(2,1)}), bf16[8,128,384]{2,1,0:T(8,128)(2,1)S(1)}, u32[]{:S(2)}, u32[]{:S(2)}) async-start(bf16[8,128,384]{2,1,0:T(8,128)(2,1)} %get-tuple-element.51), calls=%async_computation | async-start | bytes 1572864 | tf_op jit(solution)/shard_map/all_to_all | solution.py:609
  10.3 15.8 %copy-start.3 = (s32[2,32]{1,0:T(2,128)S(1)}, s32[2,32]{1,0:T(2,128)}, u32[]{:S(2)}) copy-start(s32[2,32]{1,0:T(2,128)} %scene_ref.3) | copy-start | bytes 772
  22.0 15.8 %copy-start = (bf16[8,128,384]{2,1,0:T(8,128)(2,1)}, bf16[8,128,384]{2,1,0:T(8,128)(2,1)S(1)}, u32[]{:S(2)}) copy-start(bf16[8,128,384]{2,1,0:T(8,128)(2,1)S(1)} %shard_map.188.same_ref.refs_0_) | copy-start | bytes 2359300
  22.0 4.1 %collective-permute-start = (bf16[8,128,384]{2,1,0:T(8,128)(2,1)S(1)}, bf16[8,128,384]{2,1,0:T(8,128)(2,1)S(1)}, u32[]{:S(2)}, u32[]{:S(2)}) collective-permute-start(bf16[8,128,384]{2,1,0:T(8,128)(2,1)S(1)} %shard_map.188.same_ref.refs_0_), channel_id=1, source_target_pairs={{0,8},{8,0},{1,9},{9,1},{2,10},{10,2},{3,11},{11,3},{4,12},{12,4},... | collective-permute-start | bytes 2359304 | tf_op jit(solution)/shard_map/ppermute | solution.py:613
  29.2 18.0 %all-to-all-start.1 = ((bf16[8,128,256]{2,1,0:T(8,128)(2,1)}), bf16[8,128,256]{2,1,0:T(8,128)(2,1)S(1)}, u32[]{:S(2)}, u32[]{:S(2)}) async-start(bf16[8,128,256]{2,1,0:T(8,128)(2,1)} %shard_map.189), calls=%async_computation.1 | async-start | bytes 1048576 | tf_op jit(solution)/shard_map/all_to_all | solution.py:609
  47.1 8.7 %copy-start.1 = (bf16[8,128,256]{2,1,0:T(8,128)(2,1)}, bf16[8,128,256]{2,1,0:T(8,128)(2,1)S(1)}, u32[]{:S(2)}) copy-start(bf16[8,128,256]{2,1,0:T(8,128)(2,1)S(1)} %all-to-all-done.1.mixed_ref) | copy-start | bytes 1572868
  54.1 5.3 %collective-permute-start.2 = (bf16[8,48,768]{2,1,0:T(8,128)(2,1)}, bf16[8,48,768]{2,1,0:T(8,128)(2,1)}, u32[]{:S(2)}, u32[]{:S(2)}) collective-permute-start(bf16[8,48,768]{2,1,0:T(8,128)(2,1)} %get-tuple-element.61), channel_id=1, source_target_pairs={{0,8},{8,0},{1,9},{9,1},{2,10},{10,2},{3,11},{11,3},{4,12},{12,4},... | collective-permute-start | bytes 1769480 | tf_op jit(solution)/shard_map/ppermute | solution.py:613
  55.8 18.1 %all-to-all-start.2 = ((bf16[8,64,768]{2,1,0:T(8,128)(2,1)}), bf16[8,64,768]{2,1,0:T(8,128)(2,1)S(1)}, u32[]{:S(2)}, u32[]{:S(2)}) async-start(bf16[8,64,768]{2,1,0:T(8,128)(2,1)} %get-tuple-element.53), calls=%async_computation.2 | async-start | bytes 1572864 | tf_op jit(solution)/shard_map/all_to_all | solution.py:609
  61.3 15.6 %collective-permute-start.3 = (bf16[2,48,768]{2,1,0:T(8,128)(2,1)}, bf16[2,48,768]{2,1,0:T(8,128)(2,1)S(1)}, u32[]{:S(2)}, u32[]{:S(2)}) collective-permute-start(bf16[2,48,768]{2,1,0:T(8,128)(2,1)} %get-tuple-element.62), channel_id=1, source_target_pairs={{0,32},{32,0},{64,96},{96,64},{1,33},{33,1},{65,97},{97,65},{2,34}... | collective-permute-start | bytes 442376 | tf_op jit(solution)/shard_map/ppermute | solution.py:629
  61.9 15.0 %collective-permute-start.4 = (bf16[2,48,768]{2,1,0:T(8,128)(2,1)}, bf16[2,48,768]{2,1,0:T(8,128)(2,1)S(1)}, u32[]{:S(2)}, u32[]{:S(2)}) collective-permute-start(bf16[2,48,768]{2,1,0:T(8,128)(2,1)} %get-tuple-element.63), channel_id=1, source_target_pairs={{0,64},{32,96},{64,0},{96,32},{1,65},{33,97},{65,1},{97,33},{2,66}... | collective-permute-start | bytes 442376 | tf_op jit(solution)/shard_map/ppermute | solution.py:629
  63.9 12.9 %collective-permute-start.5 = (bf16[2,48,768]{2,1,0:T(8,128)(2,1)}, bf16[2,48,768]{2,1,0:T(8,128)(2,1)S(1)}, u32[]{:S(2)}, u32[]{:S(2)}) collective-permute-start(bf16[2,48,768]{2,1,0:T(8,128)(2,1)} %get-tuple-element.64), channel_id=1, source_target_pairs={{0,96},{32,64},{64,32},{96,0},{1,97},{33,65},{65,33},{97,1},{2,98}... | collective-permute-start | bytes 442376 | tf_op jit(solution)/shard_map/ppermute | solution.py:629
  76.9 21.4 %all-to-all-start.3 = ((bf16[32,32,512]{2,1,0:T(8,128)(2,1)}), bf16[32,32,512]{2,1,0:T(8,128)(2,1)S(1)}, u32[]{:S(2)}, u32[]{:S(2)}) async-start(bf16[32,32,512]{2,1,0:T(8,128)(2,1)} %bitcast.8), calls=%async_computation.3 | async-start | bytes 2097152 | tf_op jit(solution)/shard_map/all_to_all | solution.py:609
  80.9 17.4 %collective-permute-start.1 = (bf16[8,128,384]{2,1,0:T(8,128)(2,1)}, bf16[8,128,384]{2,1,0:T(8,128)(2,1)S(1)}, u32[]{:S(2)}, u32[]{:S(2)}) collective-permute-start(bf16[8,128,384]{2,1,0:T(8,128)(2,1)} %shard_map.193.kvs_ref), channel_id=1, source_target_pairs={{0,8},{8,0},{1,9},{9,1},{2,10},{10,2},{3,11},{11,3},{4,12},{12,4},... | collective-permute-start | bytes 2359304 | tf_op jit(solution)/shard_map/ppermute | solution.py:613
  81.7 14.1 %collective-permute-start.6 = (bf16[32,768]{1,0:T(8,128)(2,1)S(1)}, bf16[32,768]{1,0:T(8,128)(2,1)S(1)}, u32[]{:S(2)}, u32[]{:S(2)}) collective-permute-start(bf16[32,768]{1,0:T(8,128)(2,1)S(1)} %copy-done.2), channel_id=1, source_target_pairs={{0,1},{1,0},{2,3},{3,2},{4,5},{5,4},{6,7},{7,6},{8,9},{9,8},{10,11... | collective-permute-start | bytes 147464 | tf_op jit(solution)/shard_map/ppermute | solution.py:629
  84.7 11.2 %collective-permute-start.7 = (bf16[32,768]{1,0:T(8,128)(2,1)S(1)}, bf16[32,768]{1,0:T(8,128)(2,1)S(1)}, u32[]{:S(2)}, u32[]{:S(2)}) collective-permute-start(bf16[32,768]{1,0:T(8,128)(2,1)S(1)} %copy-done.2), channel_id=1, source_target_pairs={{0,2},{1,3},{2,0},{3,1},{4,6},{5,7},{6,4},{7,5},{8,10},{9,11},{10,... | collective-permute-start | bytes 147464 | tf_op jit(solution)/shard_map/ppermute | solution.py:629
  85.9 12.4 %collective-permute-start.8 = (bf16[32,768]{1,0:T(8,128)(2,1)S(1)}, bf16[32,768]{1,0:T(8,128)(2,1)S(1)}, u32[]{:S(2)}, u32[]{:S(2)}) collective-permute-start(bf16[32,768]{1,0:T(8,128)(2,1)S(1)} %copy-done.2), channel_id=1, source_target_pairs={{0,3},{1,2},{2,1},{3,0},{4,7},{5,6},{6,5},{7,4},{8,11},{9,10},{10,... | collective-permute-start | bytes 147464 | tf_op jit(solution)/shard_map/ppermute | solution.py:629
  98.3 4.2 %collective-permute-start.9 = (bf16[8,128,512]{2,1,0:T(8,128)(2,1)S(1)}, bf16[8,128,512]{2,1,0:T(8,128)(2,1)S(1)}, u32[]{:S(2)}, u32[]{:S(2)}) collective-permute-start(bf16[8,128,512]{2,1,0:T(8,128)(2,1)S(1)} %shard_map.198.gs_ref), channel_id=1, source_target_pairs={{0,8},{8,0},{1,9},{9,1},{2,10},{10,2},{3,11},{11,3},{4,12},{12,4},... | collective-permute-start | bytes 3145736 | tf_op jit(solution)/shard_map/ppermute | solution.py:613
  102.5 5.3 %collective-permute-start.10 = (bf16[2,48,768]{2,1,0:T(8,128)(2,1)}, bf16[2,48,768]{2,1,0:T(8,128)(2,1)S(1)}, u32[]{:S(2)}, u32[]{:S(2)}) collective-permute-start(bf16[2,48,768]{2,1,0:T(8,128)(2,1)} %shard_map.200.near_ref), channel_id=1, source_target_pairs={{0,16},{16,0},{1,17},{17,1},{2,18},{18,2},{3,19},{19,3},{4,20},{20... | collective-permute-start | bytes 442376 | tf_op jit(solution)/shard_map/ppermute | solution.py:629
  107.8 3.8 %collective-permute-start.14 = (bf16[16,48,384]{2,1,0:T(8,128)(2,1)S(1)}, bf16[16,48,384]{2,1,0:T(8,128)(2,1)S(1)}, u32[]{:S(2)}, u32[]{:S(2)}) collective-permute-start(bf16[16,48,384]{2,1,0:T(8,128)(2,1)S(1)} %shard_map.202), channel_id=1, source_target_pairs={{0,8},{8,0},{1,9},{9,1},{2,10},{10,2},{3,11},{11,3},{4,12},{12,4},... | collective-permute-start | bytes 1769480 | tf_op jit(solution)/shard_map/ppermute | solution.py:613
  111.5 7.8 %copy-start.6 = (bf16[32,768]{1,0:T(8,128)(2,1)S(1)}, bf16[32,768]{1,0:T(8,128)(2,1)}, u32[]{:S(2)}) copy-start(bf16[32,768]{1,0:T(8,128)(2,1)} %get-tuple-element.71) | copy-start | bytes 147460
  112.5 17.5 %all-to-all-start.4 = ((bf16[16,48,384]{2,1,0:T(8,128)(2,1)}), bf16[16,48,384]{2,1,0:T(8,128)(2,1)S(1)}, u32[]{:S(2)}, u32[]{:S(2)}) async-start(bf16[16,48,384]{2,1,0:T(8,128)(2,1)} %shard_map.203), calls=%async_computation.4 | async-start | bytes 1179648 | tf_op jit(solution)/shard_map/all_to_all | solution.py:609
  118.5 9.1 %collective-permute-start.11 = (bf16[32,768]{1,0:T(8,128)(2,1)S(1)}, bf16[32,768]{1,0:T(8,128)(2,1)S(1)}, u32[]{:S(2)}, u32[]{:S(2)}) collective-permute-start(bf16[32,768]{1,0:T(8,128)(2,1)S(1)} %copy-done.7), channel_id=1, source_target_pairs={{0,1},{1,0},{2,3},{3,2},{4,5},{5,4},{6,7},{7,6},{8,9},{9,8},{10,11... | collective-permute-start | bytes 147464 | tf_op jit(solution)/shard_map/ppermute | solution.py:629
  119.4 8.2 %collective-permute-start.12 = (bf16[32,768]{1,0:T(8,128)(2,1)S(1)}, bf16[32,768]{1,0:T(8,128)(2,1)S(1)}, u32[]{:S(2)}, u32[]{:S(2)}) collective-permute-start(bf16[32,768]{1,0:T(8,128)(2,1)S(1)} %copy-done.6), channel_id=1, source_target_pairs={{0,2},{1,3},{2,0},{3,1},{4,6},{5,7},{6,4},{7,5},{8,10},{9,11},{10,... | collective-permute-start | bytes 147464 | tf_op jit(solution)/shard_map/ppermute | solution.py:629
  119.4 10.1 %collective-permute-start.13 = (bf16[32,768]{1,0:T(8,128)(2,1)S(1)}, bf16[32,768]{1,0:T(8,128)(2,1)S(1)}, u32[]{:S(2)}, u32[]{:S(2)}) collective-permute-start(bf16[32,768]{1,0:T(8,128)(2,1)S(1)} %copy-done.5), channel_id=1, source_target_pairs={{0,3},{1,2},{2,1},{3,0},{4,7},{5,6},{6,5},{7,4},{8,11},{9,10},{10,... | collective-permute-start | bytes 147464 | tf_op jit(solution)/shard_map/ppermute | solution.py:629
  132.4 8.4 %copy-start.4 = (bf16[2,48,768]{2,1,0:T(8,128)(2,1)S(1)}, bf16[2,48,768]{2,1,0:T(8,128)(2,1)}, u32[]{:S(2)}) copy-start(bf16[2,48,768]{2,1,0:T(8,128)(2,1)} %get-tuple-element.78.refs_0_) | copy-start | bytes 442372
  132.4 47.1 %all-to-all-start.5 = ((bf16[64,56,384]{2,1,0:T(8,128)(2,1)}), bf16[64,56,384]{2,1,0:T(8,128)(2,1)S(1)}, u32[]{:S(2)}, u32[]{:S(2)}) async-start(bf16[64,56,384]{2,1,0:T(8,128)(2,1)} %bitcast.7), calls=%async_computation.5 | async-start | bytes 5505024 | tf_op jit(solution)/shard_map/all_to_all | solution.py:609
  140.8 33.2 %collective-permute-start.15 = (bf16[2,48,768]{2,1,0:T(8,128)(2,1)S(1)}, bf16[2,48,768]{2,1,0:T(8,128)(2,1)S(1)}, u32[]{:S(2)}, u32[]{:S(2)}) collective-permute-start(bf16[2,48,768]{2,1,0:T(8,128)(2,1)S(1)} %copy-done.4), channel_id=1, source_target_pairs={{0,32},{32,0},{64,96},{96,64},{1,33},{33,1},{65,97},{97,65},{2,34}... | collective-permute-start | bytes 442376 | tf_op jit(solution)/shard_map/ppermute | solution.py:629
  141.9 35.9 %collective-permute-start.16 = (bf16[2,48,768]{2,1,0:T(8,128)(2,1)S(1)}, bf16[2,48,768]{2,1,0:T(8,128)(2,1)S(1)}, u32[]{:S(2)}, u32[]{:S(2)}) collective-permute-start(bf16[2,48,768]{2,1,0:T(8,128)(2,1)S(1)} %copy-done.4), channel_id=1, source_target_pairs={{0,64},{32,96},{64,0},{96,32},{1,65},{33,97},{65,1},{97,33},{2,66}... | collective-permute-start | bytes 442376 | tf_op jit(solution)/shard_map/ppermute | solution.py:629
  144.5 33.3 %collective-permute-start.17 = (bf16[2,48,768]{2,1,0:T(8,128)(2,1)S(1)}, bf16[2,48,768]{2,1,0:T(8,128)(2,1)S(1)}, u32[]{:S(2)}, u32[]{:S(2)}) collective-permute-start(bf16[2,48,768]{2,1,0:T(8,128)(2,1)S(1)} %copy-done.4), channel_id=1, source_target_pairs={{0,96},{32,64},{64,32},{96,0},{1,97},{33,65},{65,33},{97,1},{2,98}... | collective-permute-start | bytes 442376 | tf_op jit(solution)/shard_map/ppermute | solution.py:629
  179.5 16.6 %collective-permute-start.18 = (bf16[8,8,56,384]{3,2,1,0:T(8,128)(2,1)S(1)}, bf16[8,8,56,384]{3,2,1,0:T(8,128)(2,1)}, u32[]{:S(2)}, u32[]{:S(2)}) collective-permute-start(bf16[8,8,56,384]{3,2,1,0:T(8,128)(2,1)S(1)} %shard_map.208.refs_1_.in_ref), channel_id=1, source_target_pairs={{0,8},{8,0},{1,9},{9,1},{2,10},{10,2},{3,11},{11,3},{4,12},{12,4},... | collective-permute-start | bytes 8257544 | tf_op jit(solution)/shard_map/ppermute | solution.py:613
  182.4 20.6 %all-to-all-start.6 = ((bf16[8,64,768]{2,1,0:T(8,128)(2,1)}), bf16[8,64,768]{2,1,0:T(8,128)(2,1)S(1)}, u32[]{:S(2)}, u32[]{:S(2)}) async-start(bf16[8,64,768]{2,1,0:T(8,128)(2,1)} %shard_map.209), calls=%async_computation.6 | async-start | bytes 1572864 | tf_op jit(solution)/shard_map/all_to_all | solution.py:609
  188.8 2.2 %collective-permute-start.19 = (bf16[8,48,768]{2,1,0:T(8,128)(2,1)}, bf16[8,48,768]{2,1,0:T(8,128)(2,1)S(1)}, u32[]{:S(2)}, u32[]{:S(2)}) collective-permute-start(bf16[8,48,768]{2,1,0:T(8,128)(2,1)} %shard_map.207.refs_2_.same_ref), channel_id=1, source_target_pairs={{0,8},{8,0},{1,9},{9,1},{2,10},{10,2},{3,11},{11,3},{4,12},{12,4},... | collective-permute-start | bytes 1769480 | tf_op jit(solution)/shard_map/ppermute | solution.py:613
  (3 other events, 18.8 us)

commit v16 on v15

--- a/solution.py
+++ b/solution.py
@@ -566,19 +566,18 @@
     wait_all(copies)
 
 
-def stack_kernel(*refs):
-    y = lax.axis_index("y")
-    for k, ref in enumerate(refs[:4]):
-        refs[5][pl.ds((y ^ k) * 2, 2)] = ref[...]
-
-
-def spread_ff_kernel(same_ref, other_ref, up_ref, down_ref):
-    core = lax.axis_index(CORE)
-    for ref, owner in ((same_ref, core), (other_ref, 1 - core)):
-        for chip in range(8):
-            block = ref[chip].astype(F32)
+def spread_ff_kernel(*refs):
+    up_ref, down_ref = refs[8:]
+    y, core = lax.axis_index("y"), lax.axis_index(CORE)
+    for index, ref in enumerate(refs[:8]):
+        owner = core ^ (index // 4)
+        for xl in range(2):
+            chip = (y ^ (index % 4)) * 2 + xl
+            block = ref[xl].astype(F32)
             up_ref[pl.ds(pl.multiple_of((chip * 2 + owner) * 48, 16), 48)] = block[:, :384]
-            down_ref[chip * 48:(chip + 1) * 48, pl.ds(pl.multiple_of(owner * 384, 128), 384)] = block[:, 384:]
+            down_ref[
+                pl.ds(pl.multiple_of(chip * 48, 16), 48), pl.ds(pl.multiple_of(owner * 384, 128), 384)
+            ] = block[:, 384:]
 
 
 def input_kernel(
@@ -783,21 +782,9 @@
         [pltpu.VMEM((2 * BLK, D), BF), pltpu.VMEM((BLK, D), BF), DMA((8,)), DMA],
     )
     weight_same = exchange(weight_total.reshape(64, 56, 384), (*CHIP, *NARROW)).reshape(8, 8, 56, 384)
-    (ff_same,) = call(
-        stack_kernel,
-        [((8, 48, D), BF, "L")],
-        [(ff_part, "L"), *[(value, "V") for value in ff_parts], (packed, "H")],
-        1000,
-    )
-    weight_same = after(weight_same, pin(packed), pin(ff_same))
+    weight_same = after(weight_same, pin(packed))
     everyone = exchange(after(pin(packed), weight_same), NARROW)
     weight_other = swap(weight_same)
-    up_grad, down_grad = call(
-        spread_ff_kernel,
-        [((D, FFL), F32, "L"), ((FFL, D), F32, "L")],
-        [(ff_same, "L"), (swap(ff_same), "V")],
-        1000,
-    )
     scratch = [
         pltpu.VMEM((8, 48, 3 * D), F32), pltpu.VMEM((4, 2, 48, D), F32), DMA((8,)), DMA((4, 2)),
     ]
@@ -817,6 +804,14 @@
         scratch,
         aliases={2: 0, 3: 1},
     )
+    ff_parts = [after(value, pin(vectors[0])) for value in ff_parts]
+    ff_swapped = [swap(value) for value in (ff_part, *ff_parts)]
+    up_grad, down_grad = call(
+        spread_ff_kernel,
+        [((D, FFL), F32, "L"), ((FFL, D), F32, "L")],
+        [(ff_part, "L"), *[(value, "V") for value in ff_parts], *[(value, "V") for value in ff_swapped]],
+        1000,
+    )
     input_grad, result = call(
         unpack_kernel, [((2, TOK, D), F32, "L"), ((2, TOK, D), BF, "L")], [(everyone, "V"), (vectors[0], "H"), (up_grad, "H")], 1000
     )

time: 206 us -> 201 us (0.976)
  waiting for transfers between devices: 81.3 us -> 79.1 us
    ppermute x13, waiting for transfers between devices: 48.2 us -> 18.4 us  [flip(): lax.ppermute(value, axes, [(index, index ^ bits) for index in range(count)])]
    all_to_all x7, waiting for transfers between devices: 27 us -> 55.4 us  [exchange(): return lax.all_to_all(value, axes, 0, 0, tiled=True)]
    all_to_all x7, starting transfers between devices: 41.4 us -> 38.6 us  [exchange(): return lax.all_to_all(value, axes, 0, 0, tiled=True)]
    ppermute x7 -> x10, starting transfers between devices: 11.1 us -> 13.4 us  [swap(): return lax.ppermute(value, CORE, [(0, 1), (1, 0)])]
    pallas_call x19 -> x18, Pallas kernels: 51.6 us -> 49.6 us  [call(): pl.pallas_call(kernel, out_shape=[(pltpu.HBM if place in 'HL' else jax.Sh...]
    ppermute x7 -> x10, waiting for transfers between devices: 6.12 us -> 5.33 us  [swap(): return lax.ppermute(value, CORE, [(0, 1), (1, 0)])]
  transfers between devices with their start and end apart: 27 -> 30, of which waited for: 15 -> 15; matrix products, arithmetic and copies ran while one was open for 1% -> 1% of each run, Pallas kernels for 16% -> 16%
where the time goes in v16:
time: 201 us; the launch traced here: 199 us
  waiting for transfers between devices  79.1 us (39%)
  starting transfers between devices  68.3 us (34%)
  Pallas kernels  49.7 us (25%)
    all_to_all x7, waiting for transfers between devices, exchange(): return lax.all_to_all(value, axes, 0, 0, tiled=True)  55.4 us
    pallas_call x18, Pallas kernels, call(): pl.pallas_call(kernel, out_shape=[(pltpu.HBM if place in 'HL' else jax.Sh...  49.6 us
    all_to_all x7, starting transfers between devices, exchange(): return lax.all_to_all(value, axes, 0, 0, tiled=True)  38.6 us
    ppermute x13, waiting for transfers between devices, flip(): lax.ppermute(value, axes, [(index, index ^ bits) for index in range(count)])  18.4 us
    ppermute x13, starting transfers between devices, flip(): lax.ppermute(value, axes, [(index, index ^ bits) for index in range(count)])  16.4 us
    ppermute x10, starting transfers between devices, swap(): return lax.ppermute(value, CORE, [(0, 1), (1, 0)])  13.4 us
    ppermute x10, waiting for transfers between devices, swap(): return lax.ppermute(value, CORE, [(0, 1), (1, 0)])  5.33 us
  transfers between devices with their start and end apart: 30, of which 15 were waited for; matrix products, arithmetic and copies ran while one was open for 1% of the time, Pallas kernels for 16%

profile of v16, /device:TPU:1, one launch (start us, length us, event | category | flops | bytes accessed | tf_op | source)
XLA Modules:
  0.0 199.5 jit_solution(2957787447834552222)
XLA Ops:
  0.6 3.7 %shard_map.186 = (bf16[8,128,384]{2,1,0:T(8,128)(2,1)}, bf16[128,768]{1,0:T(8,128)(2,1)}) custom-call(bf16[2,128,768]{2,1,0:T(8,128)(2,1)} %tok_ref.7, f32[768]{0:T(1024)} %gain_ref.7, f32[768]{0:T(1024)} %shift_ref.2, bf16[768,2304]{1,0:T(8,128)(2,1)} %w_ref.7), custom_call_target="tpu_custom_call" | custom-call | flops 1000 | bytes 1000 | tf_op jit(solution)/shard_map/pallas_call | solution.py:106
  4.3 6.0 %all-to-all-start = ((bf16[8,128,384]{2,1,0:T(8,128)(2,1)}), bf16[8,128,384]{2,1,0:T(8,128)(2,1)S(1)}, u32[]{:S(2)}, u32[]{:S(2)}) async-start(bf16[8,128,384]{2,1,0:T(8,128)(2,1)} %get-tuple-element.51), calls=%async_computation | async-start | bytes 1572864 | tf_op jit(solution)/shard_map/all_to_all | solution.py:608
  10.3 3.0 %shard_map.187.refs_1_.q_ref = bf16[128,256]{1,0:T(8,128)(2,1)} custom-call(bf16[128,768]{1,0:T(8,128)(2,1)} %get-tuple-element.52.normed_ref, bf16[768,2304]{1,0:T(8,128)(2,1)} %w_ref.7), custom_call_target="tpu_custom_call" | custom-call | flops 1000 | bytes 1000 | tf_op jit(solution)/shard_map/pallas_call | solution.py:106
  13.4 8.6 %all-to-all-done.refs_0_ = bf16[8,128,384]{2,1,0:T(8,128)(2,1)S(1)} async-done(((bf16[8,128,384]{2,1,0:T(8,128)(2,1)}), bf16[8,128,384]{2,1,0:T(8,128)(2,1)S(1)}, u32[]{:S(2)}, u32[]{:S(2)}) %all-to-all-start) | async-done | bytes 786464 | tf_op jit(solution)/shard_map/all_to_all | solution.py:608
  26.1 3.1 %shard_map.189 = bf16[8,128,256]{2,1,0:T(8,128)(2,1)} custom-call(s32[2,32]{1,0:T(2,128)S(1)} %copy-done.3, bf16[128,256]{1,0:T(8,128)(2,1)} %shard_map.187.refs_1_.q_ref, bf16[8,128,384]{2,1,0:T(8,128)(2,1)S(1)} %shard_map.188.same_ref.refs_0_, bf16[8,128,384]{2,1,0:T(8,128)(2,1)S(1)} %collective-permute-done.other_ref), custom_call_target="tpu_custom_call" | custom-call | flops 1000 | bytes 1000 | tf_op jit(solution)/shard_map/pallas_call | solution.py:106
  29.2 8.1 %all-to-all-start.1 = ((bf16[8,128,256]{2,1,0:T(8,128)(2,1)}), bf16[8,128,256]{2,1,0:T(8,128)(2,1)S(1)}, u32[]{:S(2)}, u32[]{:S(2)}) async-start(bf16[8,128,256]{2,1,0:T(8,128)(2,1)} %shard_map.189), calls=%async_computation.1 | async-start | bytes 1048576 | tf_op jit(solution)/shard_map/all_to_all | solution.py:608
  38.7 9.4 %all-to-all-done.1.mixed_ref = bf16[8,128,256]{2,1,0:T(8,128)(2,1)S(1)} async-done(((bf16[8,128,256]{2,1,0:T(8,128)(2,1)}), bf16[8,128,256]{2,1,0:T(8,128)(2,1)S(1)}, u32[]{:S(2)}, u32[]{:S(2)}) %all-to-all-start.1) | async-done | bytes 524320 | tf_op jit(solution)/shard_map/all_to_all | solution.py:608
  48.0 4.2 %shard_map.190 = (bf16[8,64,768]{2,1,0:T(8,128)(2,1)}, f32[32,768]{1,0:T(8,128)}, bf16[256,768]{1,0:T(8,128)(2,1)S(1)}, bf16[256,384]{1,0:T(8,128)(2,1)S(1)}, bf16[256,384]{1,0:T(8,128)(2,1)S(1)}) custom-call(bf16[8,128,256]{2,1,0:T(8,128)(2,1)S(1)} %all-to-all-done.1.mixed_ref, bf16[2,128,768]{2,1,0:T(8,128)(2,1)} %tok_ref.7, bf16[2,128,768]{2,1,0:T(8,128)(2,1)} %og_ref.5, ...), custom_call_target="tpu_custom_call" | custom-call | flops 1000 | bytes 1000 | tf_op jit(solution)/shard_map/pallas_call | solution.py:106
  52.2 2.8 %shard_map.194 = (bf16[8,48,768]{2,1,0:T(8,128)(2,1)S(1)}, bf16[8,48,768]{2,1,0:T(8,128)(2,1)}) custom-call(bf16[256,768]{1,0:T(8,128)(2,1)S(1)} %get-tuple-element.57.normed_ref, bf16[256,384]{1,0:T(8,128)(2,1)S(1)} %get-tuple-element.58.act_ref, bf16[256,384]{1,0:T(8,128)(2,1)S(1)} %get-tuple-element.59.gpre_ref, bf16[2,128,768]{2,1,0:T(8,128)(2,1)} %og_ref.5), custom_call_target="tpu_custom_call" | custom-call | flops 1000 | bytes 1000 | tf_op jit(solution)/shard_map/pallas_call | solution.py:106
  56.7 3.5 %all-to-all-start.2 = ((bf16[8,64,768]{2,1,0:T(8,128)(2,1)}), bf16[8,64,768]{2,1,0:T(8,128)(2,1)S(1)}, u32[]{:S(2)}, u32[]{:S(2)}) async-start(bf16[8,64,768]{2,1,0:T(8,128)(2,1)} %get-tuple-element.53), calls=%async_computation.2 | async-start | bytes 1572864 | tf_op jit(solution)/shard_map/all_to_all | solution.py:608
  63.1 3.0 %collective-permute-start.5 = (bf16[2,48,768]{2,1,0:T(8,128)(2,1)}, bf16[2,48,768]{2,1,0:T(8,128)(2,1)S(1)}, u32[]{:S(2)}, u32[]{:S(2)}) collective-permute-start(bf16[2,48,768]{2,1,0:T(8,128)(2,1)} %get-tuple-element.64), channel_id=1, source_target_pairs={{0,96},{32,64},{64,32},{96,0},{1,97},{33,65},{65,33},{97,1},{2,98}... | collective-permute-start | bytes 442376 | tf_op jit(solution)/shard_map/ppermute | solution.py:628
  66.0 2.3 %shard_map.191.query_ref = bf16[4,32,256]{2,1,0:T(8,128)(2,1)} custom-call(bf16[128,768]{1,0:T(8,128)(2,1)} %get-tuple-element.52.normed_ref, bf16[768,2304]{1,0:T(8,128)(2,1)} %w_ref.7), custom_call_target="tpu_custom_call" | custom-call | flops 1000 | bytes 1000 | tf_op jit(solution)/shard_map/pallas_call | solution.py:106
  68.4 6.4 %all-to-all-done.2.sums_ref = bf16[8,64,768]{2,1,0:T(8,128)(2,1)S(1)} async-done(((bf16[8,64,768]{2,1,0:T(8,128)(2,1)}), bf16[8,64,768]{2,1,0:T(8,128)(2,1)S(1)}, u32[]{:S(2)}, u32[]{:S(2)}) %all-to-all-start.2) | async-done | bytes 786464 | tf_op jit(solution)/shard_map/all_to_all | solution.py:608
  74.8 3.0 %shard_map.192 = (bf16[8,4,32,512]{3,2,1,0:T(8,128)(2,1)}, bf16[32,768]{1,0:T(8,128)(2,1)}, f32[32,768]{1,0:T(8,128)}, bf16[32,768]{1,0:T(8,128)(2,1)}, f32[8,768]{1,0:T(8,128)}) custom-call(bf16[8,64,768]{2,1,0:T(8,128)(2,1)S(1)} %all-to-all-done.2.sums_ref, f32[32,768]{1,0:T(8,128)} %get-tuple-element.54.middle_ref, bf16[2,128,768]{2,1,0:T(8,128)(2,1)} %og_ref.5, ...), custom_call_target="tpu_custom_call" | custom-call | flops 1000 | bytes 1000 | tf_op jit(solution)/shard_map/pallas_call | solution.py:106
  77.8 3.9 %all-to-all-start.3 = ((bf16[32,32,512]{2,1,0:T(8,128)(2,1)}), bf16[32,32,512]{2,1,0:T(8,128)(2,1)S(1)}, u32[]{:S(2)}, u32[]{:S(2)}) async-start(bf16[32,32,512]{2,1,0:T(8,128)(2,1)} %bitcast.8), calls=%async_computation.3 | async-start | bytes 2097152 | tf_op jit(solution)/shard_map/all_to_all | solution.py:608
  82.6 2.9 %collective-permute-start.6 = (bf16[32,768]{1,0:T(8,128)(2,1)S(1)}, bf16[32,768]{1,0:T(8,128)(2,1)S(1)}, u32[]{:S(2)}, u32[]{:S(2)}) collective-permute-start(bf16[32,768]{1,0:T(8,128)(2,1)S(1)} %copy-done.2), channel_id=1, source_target_pairs={{0,1},{1,0},{2,3},{3,2},{4,5},{5,4},{6,7},{7,6},{8,9},{9,8},{10,11... | collective-permute-start | bytes 147464 | tf_op jit(solution)/shard_map/ppermute | solution.py:628
  88.4 8.3 %collective-permute-done.6.refs_1_.low1_ref = bf16[32,768]{1,0:T(8,128)(2,1)S(1)} collective-permute-done((bf16[32,768]{1,0:T(8,128)(2,1)S(1)}, bf16[32,768]{1,0:T(8,128)(2,1)S(1)}, u32[]{:S(2)}, u32[]{:S(2)}) %collective-permute-start.6) | collective-permute-done | bytes 49184 | tf_op jit(solution)/shard_map/ppermute | solution.py:628
  96.7 2.4 %collective-permute-done.8.refs_3_.low3_ref = bf16[32,768]{1,0:T(8,128)(2,1)S(1)} collective-permute-done((bf16[32,768]{1,0:T(8,128)(2,1)S(1)}, bf16[32,768]{1,0:T(8,128)(2,1)S(1)}, u32[]{:S(2)}, u32[]{:S(2)}) %collective-permute-start.8) | collective-permute-done | bytes 49184 | tf_op jit(solution)/shard_map/ppermute | solution.py:628
  103.7 4.3 %shard_map.199 = (bf16[128,640]{1,0:T(8,128)(2,1)S(1)}, bf16[3,768,384]{2,1,0:T(8,128)(2,1)S(1)}, bf16[16,48,384]{2,1,0:T(8,128)(2,1)S(1)}, bf16[16,48,384]{2,1,0:T(8,128)(2,1)S(1)}) custom-call(s32[2,32]{1,0:T(2,128)S(1)} %copy-done.3, bf16[8,128,384]{2,1,0:T(8,128)(2,1)} %shard_map.193.kvs_ref, ...), custom_call_target="tpu_custom_call" | custom-call | flops 1000 | bytes 1000 | tf_op jit(solution)/shard_map/pallas_call | solution.py:106
  109.8 2.5 %shard_map.201 = (f32[32,768]{1,0:T(8,128)}, bf16[32,768]{1,0:T(8,128)(2,1)}, bf16[32,768]{1,0:T(8,128)(2,1)}, bf16[32,768]{1,0:T(8,128)(2,1)}, f32[8,768]{1,0:T(8,128)}, /*index=5*/bf16[2,48,768]{2,1,0:T(8,128)(2,1)}) custom-call(bf16[128,640]{1,0:T(8,128)(2,1)S(1)} %get-tuple-element.66.gqkv_ref, bf16[3,768,384]{2,1,0:T(8,128)(2,1)S(1)} %get-tuple-element.67.w_ref, ...), custom_call_target="tpu_custom_call" | custom-call | flops 1000 | bytes 1000 | tf_op jit(solution)/shard_map/pallas_call | solution.py:106
  113.4 5.0 %all-to-all-start.4 = ((bf16[16,48,384]{2,1,0:T(8,128)(2,1)}), bf16[16,48,384]{2,1,0:T(8,128)(2,1)S(1)}, u32[]{:S(2)}, u32[]{:S(2)}) async-start(bf16[16,48,384]{2,1,0:T(8,128)(2,1)} %shard_map.203), calls=%async_computation.4 | async-start | bytes 1179648 | tf_op jit(solution)/shard_map/all_to_all | solution.py:608
  120.2 2.5 %collective-permute-start.13 = (bf16[32,768]{1,0:T(8,128)(2,1)S(1)}, bf16[32,768]{1,0:T(8,128)(2,1)S(1)}, u32[]{:S(2)}, u32[]{:S(2)}) collective-permute-start(bf16[32,768]{1,0:T(8,128)(2,1)S(1)} %copy-done.4), channel_id=1, source_target_pairs={{0,3},{1,2},{2,1},{3,0},{4,7},{5,6},{6,5},{7,4},{8,11},{9,10},{10,... | collective-permute-start | bytes 147464 | tf_op jit(solution)/shard_map/ppermute | solution.py:628
  122.7 5.7 %collective-permute-done.11.refs_2_.one_ref = bf16[32,768]{1,0:T(8,128)(2,1)S(1)} collective-permute-done((bf16[32,768]{1,0:T(8,128)(2,1)S(1)}, bf16[32,768]{1,0:T(8,128)(2,1)S(1)}, u32[]{:S(2)}, u32[]{:S(2)}) %collective-permute-start.11) | collective-permute-done | bytes 49184 | tf_op jit(solution)/shard_map/ppermute | solution.py:628
  129.9 2.4 %shard_map.205.unused_ref = bf16[8,8,56,384]{3,2,1,0:T(8,128)(2,1)} custom-call(bf16[16,48,384]{2,1,0:T(8,128)(2,1)S(1)} %shard_map.204.in_ref, f32[8,768]{1,0:T(8,128)} %get-tuple-element.77.refs_1_.vec_ref), custom_call_target="tpu_custom_call" | custom-call | flops 1000 | bytes 1000 | tf_op jit(solution)/shard_map/pallas_call | solution.py:106
  132.3 8.3 %all-to-all-start.5 = ((bf16[64,56,384]{2,1,0:T(8,128)(2,1)}), bf16[64,56,384]{2,1,0:T(8,128)(2,1)S(1)}, u32[]{:S(2)}, u32[]{:S(2)}) async-start(bf16[64,56,384]{2,1,0:T(8,128)(2,1)} %bitcast.7), calls=%async_computation.5 | async-start | bytes 5505024 | tf_op jit(solution)/shard_map/all_to_all | solution.py:608
  140.6 3.0 %shard_map.206.refs_1_.refs_0_ = bf16[8,64,768]{2,1,0:T(8,128)(2,1)} custom-call(f32[32,768]{1,0:T(8,128)} %get-tuple-element.69.unused_ref.own_ref, bf16[32,768]{1,0:T(8,128)(2,1)S(1)} %collective-permute-done.11.refs_2_.one_ref, bf16[32,768]{1,0:T(8,128)(2,1)S(1)} %collective-permute-done.12.refs_3_.two_ref, ...), custom_call_target="tpu_custom_call" | custom-call | flops 1000 | bytes 1000 | tf_op jit(solution)/shard_map/pallas_call | solution.py:106
  143.6 30.7 %all-to-all-done.5 = bf16[64,56,384]{2,1,0:T(8,128)(2,1)S(1)} async-done(((bf16[64,56,384]{2,1,0:T(8,128)(2,1)}), bf16[64,56,384]{2,1,0:T(8,128)(2,1)S(1)}, u32[]{:S(2)}, u32[]{:S(2)}) %all-to-all-start.5) | async-done | bytes 2752544 | tf_op jit(solution)/shard_map/all_to_all | solution.py:608
  174.3 3.6 %collective-permute-start.15 = (bf16[8,8,56,384]{3,2,1,0:T(8,128)(2,1)S(1)}, bf16[8,8,56,384]{3,2,1,0:T(8,128)(2,1)}, u32[]{:S(2)}, u32[]{:S(2)}) collective-permute-start(bf16[8,8,56,384]{3,2,1,0:T(8,128)(2,1)S(1)} %shard_map.207.refs_1_.in_ref), channel_id=1, source_target_pairs={{0,8},{8,0},{1,9},{9,1},{2,10},{10,2},{3,11},{11,3},{4,12},{12,4},... | collective-permute-start | bytes 8257544 | tf_op jit(solution)/shard_map/ppermute | solution.py:612
  177.9 3.7 %all-to-all-start.6 = ((bf16[8,64,768]{2,1,0:T(8,128)(2,1)}), bf16[8,64,768]{2,1,0:T(8,128)(2,1)S(1)}, u32[]{:S(2)}, u32[]{:S(2)}) async-start(bf16[8,64,768]{2,1,0:T(8,128)(2,1)} %shard_map.208), calls=%async_computation.6 | async-start | bytes 1572864 | tf_op jit(solution)/shard_map/all_to_all | solution.py:608
  186.6 2.4 %shard_map.209 = (f32[768,2304]{1,0:T(8,128)}, f32[768,768]{1,0:T(8,128)}, f32[8,384]{1,0:T(8,128)S(1)}) custom-call(bf16[8,8,56,384]{3,2,1,0:T(8,128)(2,1)S(1)} %shard_map.207.refs_1_.in_ref), custom_call_target="tpu_custom_call" | custom-call | flops 1000 | bytes 1000 | tf_op jit(solution)/shard_map/pallas_call | solution.py:106
  189.1 4.8 %shard_map.210 = (f32[768,2304]{1,0:T(8,128)}, f32[768,768]{1,0:T(8,128)}, f32[768]{0:T(1024)}, f32[768]{0:T(1024)}, f32[768]{0:T(1024)}, /*index=5*/f32[768]{0:T(1024)}) custom-call(bf16[8,8,56,384]{3,2,1,0:T(8,128)(2,1)} %collective-permute-done.15.in_ref, f32[8,384]{1,0:T(8,128)S(1)} %get-tuple-element.78.refs_0_, ...), custom_call_target="tpu_custom_call", output_to_operand_aliasing={{0}: (2, {}), {1}: (3, {})} | custom-call | flops 1000 | bytes 1000 | tf_op jit(solution)/shard_map/pallas_call | solution.py:106
  195.9 2.5 %shard_map.214 = (f32[768,384]{1,0:T(8,128)}, f32[384,768]{1,0:T(8,128)}) custom-call(bf16[2,48,768]{2,1,0:T(8,128)(2,1)} %get-tuple-element.82.refs_0_, bf16[2,48,768]{2,1,0:T(8,128)(2,1)S(1)} %shard_map.211.refs_1_, bf16[2,48,768]{2,1,0:T(8,128)(2,1)S(1)} %shard_map.212.refs_2_, bf16[2,48,768]{2,1,0:T(8,128)(2,1)S(1)} %shard_map.213.refs_3_, ...), custom_call_target="tpu_custom_call" | custom-call | flops 1000 | bytes 1000 | tf_op jit(solution)/shard_map/pallas_call | solution.py:106
  (73 shorter events, 32.4 us)
Async XLA Ops:
  4.3 17.6 %all-to-all-start = ((bf16[8,128,384]{2,1,0:T(8,128)(2,1)}), bf16[8,128,384]{2,1,0:T(8,128)(2,1)S(1)}, u32[]{:S(2)}, u32[]{:S(2)}) async-start(bf16[8,128,384]{2,1,0:T(8,128)(2,1)} %get-tuple-element.51), calls=%async_computation | async-start | bytes 1572864 | tf_op jit(solution)/shard_map/all_to_all | solution.py:608
  10.3 15.8 %copy-start.3 = (s32[2,32]{1,0:T(2,128)S(1)}, s32[2,32]{1,0:T(2,128)}, u32[]{:S(2)}) copy-start(s32[2,32]{1,0:T(2,128)} %scene_ref.3) | copy-start | bytes 772
  22.0 16.7 %copy-start = (bf16[8,128,384]{2,1,0:T(8,128)(2,1)}, bf16[8,128,384]{2,1,0:T(8,128)(2,1)S(1)}, u32[]{:S(2)}) copy-start(bf16[8,128,384]{2,1,0:T(8,128)(2,1)S(1)} %shard_map.188.same_ref.refs_0_) | copy-start | bytes 2359300
  22.0 4.1 %collective-permute-start = (bf16[8,128,384]{2,1,0:T(8,128)(2,1)S(1)}, bf16[8,128,384]{2,1,0:T(8,128)(2,1)S(1)}, u32[]{:S(2)}, u32[]{:S(2)}) collective-permute-start(bf16[8,128,384]{2,1,0:T(8,128)(2,1)S(1)} %shard_map.188.same_ref.refs_0_), channel_id=1, source_target_pairs={{0,8},{8,0},{1,9},{9,1},{2,10},{10,2},{3,11},{11,3},{4,12},{12,4},... | collective-permute-start | bytes 2359304 | tf_op jit(solution)/shard_map/ppermute | solution.py:612
  29.2 18.9 %all-to-all-start.1 = ((bf16[8,128,256]{2,1,0:T(8,128)(2,1)}), bf16[8,128,256]{2,1,0:T(8,128)(2,1)S(1)}, u32[]{:S(2)}, u32[]{:S(2)}) async-start(bf16[8,128,256]{2,1,0:T(8,128)(2,1)} %shard_map.189), calls=%async_computation.1 | async-start | bytes 1048576 | tf_op jit(solution)/shard_map/all_to_all | solution.py:608
  55.0 5.3 %collective-permute-start.2 = (bf16[8,48,768]{2,1,0:T(8,128)(2,1)}, bf16[8,48,768]{2,1,0:T(8,128)(2,1)}, u32[]{:S(2)}, u32[]{:S(2)}) collective-permute-start(bf16[8,48,768]{2,1,0:T(8,128)(2,1)} %get-tuple-element.61), channel_id=1, source_target_pairs={{0,8},{8,0},{1,9},{9,1},{2,10},{10,2},{3,11},{11,3},{4,12},{12,4},... | collective-permute-start | bytes 1769480 | tf_op jit(solution)/shard_map/ppermute | solution.py:612
  56.7 18.1 %all-to-all-start.2 = ((bf16[8,64,768]{2,1,0:T(8,128)(2,1)}), bf16[8,64,768]{2,1,0:T(8,128)(2,1)S(1)}, u32[]{:S(2)}, u32[]{:S(2)}) async-start(bf16[8,64,768]{2,1,0:T(8,128)(2,1)} %get-tuple-element.53), calls=%async_computation.2 | async-start | bytes 1572864 | tf_op jit(solution)/shard_map/all_to_all | solution.py:608
  62.2 15.5 %collective-permute-start.3 = (bf16[2,48,768]{2,1,0:T(8,128)(2,1)}, bf16[2,48,768]{2,1,0:T(8,128)(2,1)S(1)}, u32[]{:S(2)}, u32[]{:S(2)}) collective-permute-start(bf16[2,48,768]{2,1,0:T(8,128)(2,1)} %get-tuple-element.62), channel_id=1, source_target_pairs={{0,32},{32,0},{64,96},{96,64},{1,33},{33,1},{65,97},{97,65},{2,34}... | collective-permute-start | bytes 442376 | tf_op jit(solution)/shard_map/ppermute | solution.py:628
  62.2 15.6 %collective-permute-start.4 = (bf16[2,48,768]{2,1,0:T(8,128)(2,1)}, bf16[2,48,768]{2,1,0:T(8,128)(2,1)S(1)}, u32[]{:S(2)}, u32[]{:S(2)}) collective-permute-start(bf16[2,48,768]{2,1,0:T(8,128)(2,1)} %get-tuple-element.63), channel_id=1, source_target_pairs={{0,64},{32,96},{64,0},{96,32},{1,65},{33,97},{65,1},{97,33},{2,66}... | collective-permute-start | bytes 442376 | tf_op jit(solution)/shard_map/ppermute | solution.py:628
  63.1 14.7 %collective-permute-start.5 = (bf16[2,48,768]{2,1,0:T(8,128)(2,1)}, bf16[2,48,768]{2,1,0:T(8,128)(2,1)S(1)}, u32[]{:S(2)}, u32[]{:S(2)}) collective-permute-start(bf16[2,48,768]{2,1,0:T(8,128)(2,1)} %get-tuple-element.64), channel_id=1, source_target_pairs={{0,96},{32,64},{64,32},{96,0},{1,97},{33,65},{65,33},{97,1},{2,98}... | collective-permute-start | bytes 442376 | tf_op jit(solution)/shard_map/ppermute | solution.py:628
  77.8 21.4 %all-to-all-start.3 = ((bf16[32,32,512]{2,1,0:T(8,128)(2,1)}), bf16[32,32,512]{2,1,0:T(8,128)(2,1)S(1)}, u32[]{:S(2)}, u32[]{:S(2)}) async-start(bf16[32,32,512]{2,1,0:T(8,128)(2,1)} %bitcast.8), calls=%async_computation.3 | async-start | bytes 2097152 | tf_op jit(solution)/shard_map/all_to_all | solution.py:608
  81.8 17.4 %collective-permute-start.1 = (bf16[8,128,384]{2,1,0:T(8,128)(2,1)}, bf16[8,128,384]{2,1,0:T(8,128)(2,1)S(1)}, u32[]{:S(2)}, u32[]{:S(2)}) collective-permute-start(bf16[8,128,384]{2,1,0:T(8,128)(2,1)} %shard_map.193.kvs_ref), channel_id=1, source_target_pairs={{0,8},{8,0},{1,9},{9,1},{2,10},{10,2},{3,11},{11,3},{4,12},{12,4},... | collective-permute-start | bytes 2359304 | tf_op jit(solution)/shard_map/ppermute | solution.py:612
  82.6 14.1 %collective-permute-start.6 = (bf16[32,768]{1,0:T(8,128)(2,1)S(1)}, bf16[32,768]{1,0:T(8,128)(2,1)S(1)}, u32[]{:S(2)}, u32[]{:S(2)}) collective-permute-start(bf16[32,768]{1,0:T(8,128)(2,1)S(1)} %copy-done.2), channel_id=1, source_target_pairs={{0,1},{1,0},{2,3},{3,2},{4,5},{5,4},{6,7},{7,6},{8,9},{9,8},{10,11... | collective-permute-start | bytes 147464 | tf_op jit(solution)/shard_map/ppermute | solution.py:628
  85.5 11.2 %collective-permute-start.7 = (bf16[32,768]{1,0:T(8,128)(2,1)S(1)}, bf16[32,768]{1,0:T(8,128)(2,1)S(1)}, u32[]{:S(2)}, u32[]{:S(2)}) collective-permute-start(bf16[32,768]{1,0:T(8,128)(2,1)S(1)} %copy-done.2), channel_id=1, source_target_pairs={{0,2},{1,3},{2,0},{3,1},{4,6},{5,7},{6,4},{7,5},{8,10},{9,11},{10,... | collective-permute-start | bytes 147464 | tf_op jit(solution)/shard_map/ppermute | solution.py:628
  86.7 12.4 %collective-permute-start.8 = (bf16[32,768]{1,0:T(8,128)(2,1)S(1)}, bf16[32,768]{1,0:T(8,128)(2,1)S(1)}, u32[]{:S(2)}, u32[]{:S(2)}) collective-permute-start(bf16[32,768]{1,0:T(8,128)(2,1)S(1)} %copy-done.2), channel_id=1, source_target_pairs={{0,3},{1,2},{2,1},{3,0},{4,7},{5,6},{6,5},{7,4},{8,11},{9,10},{10,... | collective-permute-start | bytes 147464 | tf_op jit(solution)/shard_map/ppermute | solution.py:628
  99.2 4.2 %collective-permute-start.9 = (bf16[8,128,512]{2,1,0:T(8,128)(2,1)S(1)}, bf16[8,128,512]{2,1,0:T(8,128)(2,1)S(1)}, u32[]{:S(2)}, u32[]{:S(2)}) collective-permute-start(bf16[8,128,512]{2,1,0:T(8,128)(2,1)S(1)} %shard_map.198.gs_ref), channel_id=1, source_target_pairs={{0,8},{8,0},{1,9},{9,1},{2,10},{10,2},{3,11},{11,3},{4,12},{12,4},... | collective-permute-start | bytes 3145736 | tf_op jit(solution)/shard_map/ppermute | solution.py:612
  103.4 5.3 %collective-permute-start.10 = (bf16[2,48,768]{2,1,0:T(8,128)(2,1)}, bf16[2,48,768]{2,1,0:T(8,128)(2,1)S(1)}, u32[]{:S(2)}, u32[]{:S(2)}) collective-permute-start(bf16[2,48,768]{2,1,0:T(8,128)(2,1)} %shard_map.200.near_ref), channel_id=1, source_target_pairs={{0,16},{16,0},{1,17},{17,1},{2,18},{18,2},{3,19},{19,3},{4,20},{20... | collective-permute-start | bytes 442376 | tf_op jit(solution)/shard_map/ppermute | solution.py:628
  108.6 3.8 %collective-permute-start.14 = (bf16[16,48,384]{2,1,0:T(8,128)(2,1)S(1)}, bf16[16,48,384]{2,1,0:T(8,128)(2,1)S(1)}, u32[]{:S(2)}, u32[]{:S(2)}) collective-permute-start(bf16[16,48,384]{2,1,0:T(8,128)(2,1)S(1)} %shard_map.202), channel_id=1, source_target_pairs={{0,8},{8,0},{1,9},{9,1},{2,10},{10,2},{3,11},{11,3},{4,12},{12,4},... | collective-permute-start | bytes 1769480 | tf_op jit(solution)/shard_map/ppermute | solution.py:612
  113.4 16.5 %all-to-all-start.4 = ((bf16[16,48,384]{2,1,0:T(8,128)(2,1)}), bf16[16,48,384]{2,1,0:T(8,128)(2,1)S(1)}, u32[]{:S(2)}, u32[]{:S(2)}) async-start(bf16[16,48,384]{2,1,0:T(8,128)(2,1)} %shard_map.203), calls=%async_computation.4 | async-start | bytes 1179648 | tf_op jit(solution)/shard_map/all_to_all | solution.py:608
  118.4 10.0 %collective-permute-start.11 = (bf16[32,768]{1,0:T(8,128)(2,1)S(1)}, bf16[32,768]{1,0:T(8,128)(2,1)S(1)}, u32[]{:S(2)}, u32[]{:S(2)}) collective-permute-start(bf16[32,768]{1,0:T(8,128)(2,1)S(1)} %copy-done.6), channel_id=1, source_target_pairs={{0,1},{1,0},{2,3},{3,2},{4,5},{5,4},{6,7},{7,6},{8,9},{9,8},{10,11... | collective-permute-start | bytes 147464 | tf_op jit(solution)/shard_map/ppermute | solution.py:628
  120.2 8.2 %collective-permute-start.12 = (bf16[32,768]{1,0:T(8,128)(2,1)S(1)}, bf16[32,768]{1,0:T(8,128)(2,1)S(1)}, u32[]{:S(2)}, u32[]{:S(2)}) collective-permute-start(bf16[32,768]{1,0:T(8,128)(2,1)S(1)} %copy-done.5), channel_id=1, source_target_pairs={{0,2},{1,3},{2,0},{3,1},{4,6},{5,7},{6,4},{7,5},{8,10},{9,11},{10,... | collective-permute-start | bytes 147464 | tf_op jit(solution)/shard_map/ppermute | solution.py:628
  120.2 9.5 %collective-permute-start.13 = (bf16[32,768]{1,0:T(8,128)(2,1)S(1)}, bf16[32,768]{1,0:T(8,128)(2,1)S(1)}, u32[]{:S(2)}, u32[]{:S(2)}) collective-permute-start(bf16[32,768]{1,0:T(8,128)(2,1)S(1)} %copy-done.4), channel_id=1, source_target_pairs={{0,3},{1,2},{2,1},{3,0},{4,7},{5,6},{6,5},{7,4},{8,11},{9,10},{10,... | collective-permute-start | bytes 147464 | tf_op jit(solution)/shard_map/ppermute | solution.py:628
  132.3 42.0 %all-to-all-start.5 = ((bf16[64,56,384]{2,1,0:T(8,128)(2,1)}), bf16[64,56,384]{2,1,0:T(8,128)(2,1)S(1)}, u32[]{:S(2)}, u32[]{:S(2)}) async-start(bf16[64,56,384]{2,1,0:T(8,128)(2,1)} %bitcast.7), calls=%async_computation.5 | async-start | bytes 5505024 | tf_op jit(solution)/shard_map/all_to_all | solution.py:608
  174.3 14.7 %collective-permute-start.15 = (bf16[8,8,56,384]{3,2,1,0:T(8,128)(2,1)S(1)}, bf16[8,8,56,384]{3,2,1,0:T(8,128)(2,1)}, u32[]{:S(2)}, u32[]{:S(2)}) collective-permute-start(bf16[8,8,56,384]{3,2,1,0:T(8,128)(2,1)S(1)} %shard_map.207.refs_1_.in_ref), channel_id=1, source_target_pairs={{0,8},{8,0},{1,9},{9,1},{2,10},{10,2},{3,11},{11,3},{4,12},{12,4},... | collective-permute-start | bytes 8257544 | tf_op jit(solution)/shard_map/ppermute | solution.py:612
  177.9 20.5 %all-to-all-start.6 = ((bf16[8,64,768]{2,1,0:T(8,128)(2,1)}), bf16[8,64,768]{2,1,0:T(8,128)(2,1)S(1)}, u32[]{:S(2)}, u32[]{:S(2)}) async-start(bf16[8,64,768]{2,1,0:T(8,128)(2,1)} %shard_map.208), calls=%async_computation.6 | async-start | bytes 1572864 | tf_op jit(solution)/shard_map/all_to_all | solution.py:608
  181.6 12.3 %collective-permute-start.16 = (bf16[2,48,768]{2,1,0:T(8,128)(2,1)}, bf16[2,48,768]{2,1,0:T(8,128)(2,1)S(1)}, u32[]{:S(2)}, u32[]{:S(2)}) collective-permute-start(bf16[2,48,768]{2,1,0:T(8,128)(2,1)} %get-tuple-element.82.refs_0_), channel_id=1, source_target_pairs={{0,32},{32,0},{64,96},{96,64},{1,33},{33,1},{65,97},{97,65},{2,34}... | collective-permute-start | bytes 442376 | tf_op jit(solution)/shard_map/ppermute | solution.py:628
  181.9 12.1 %collective-permute-start.17 = (bf16[2,48,768]{2,1,0:T(8,128)(2,1)}, bf16[2,48,768]{2,1,0:T(8,128)(2,1)S(1)}, u32[]{:S(2)}, u32[]{:S(2)}) collective-permute-start(bf16[2,48,768]{2,1,0:T(8,128)(2,1)} %get-tuple-element.82.refs_0_), channel_id=1, source_target_pairs={{0,64},{32,96},{64,0},{96,32},{1,65},{33,97},{65,1},{97,33},{2,66}... | collective-permute-start | bytes 442376 | tf_op jit(solution)/shard_map/ppermute | solution.py:628
  183.9 10.6 %collective-permute-start.18 = (bf16[2,48,768]{2,1,0:T(8,128)(2,1)}, bf16[2,48,768]{2,1,0:T(8,128)(2,1)S(1)}, u32[]{:S(2)}, u32[]{:S(2)}) collective-permute-start(bf16[2,48,768]{2,1,0:T(8,128)(2,1)} %get-tuple-element.82.refs_0_), channel_id=1, source_target_pairs={{0,96},{32,64},{64,32},{96,0},{1,97},{33,65},{65,33},{97,1},{2,98}... | collective-permute-start | bytes 442376 | tf_op jit(solution)/shard_map/ppermute | solution.py:628
  185.5 9.3 %collective-permute-start.19 = (bf16[2,48,768]{2,1,0:T(8,128)(2,1)}, bf16[2,48,768]{2,1,0:T(8,128)(2,1)S(1)}, u32[]{:S(2)}, u32[]{:S(2)}) collective-permute-start(bf16[2,48,768]{2,1,0:T(8,128)(2,1)} %get-tuple-element.82.refs_0_), channel_id=1, source_target_pairs={{0,8},{8,0},{1,9},{9,1},{2,10},{10,2},{3,11},{11,3},{4,12},{12,4},... | collective-permute-start | bytes 442376 | tf_op jit(solution)/shard_map/ppermute | solution.py:612
  193.9 1.5 collective-permute-start.20
  194.1 1.5 collective-permute-start.21
  194.5 1.4 collective-permute-start.22
  (5 other events, 34.3 us)

commit v17 on v16

--- a/solution.py
+++ b/solution.py
@@ -529,13 +529,23 @@
 
 def spread_kernel(turn, in_ref, *refs):
     qkv_buf, out_buf, sem, out_sem = refs[-4:]
-    qkv_ref, out_ref, *vec_refs = refs[3:-4] if turn else refs[:-4]
+    if turn:
+        in_buf, in_sem = refs[-6:-4]
+        qkv_ref, out_ref, *vec_refs = refs[3:-6]
+        loads = [pltpu.make_async_copy(in_ref.at[tile], in_buf.at[tile], in_sem.at[tile]) for tile in range(8)]
+        for load in loads:
+            load.start()
+    else:
+        qkv_ref, out_ref, *vec_refs = refs[:-4]
+        in_buf = in_ref
     owner = lax.axis_index(CORE)
     owner = 1 - owner if turn else owner
     copies = []
     vectors = jnp.zeros((8, 384), F32)
     for tile in range(8):
-        whole = [in_ref[tile, index].astype(F32) for index in range(8)]
+        if turn:
+            loads[tile].wait()
+        whole = [in_buf[tile, index].astype(F32) for index in range(8)]
         block = [value[:48] for value in whole]
         for value in whole:
             vectors = vectors + value[48:]
@@ -567,17 +577,26 @@
 
 
 def spread_ff_kernel(*refs):
-    up_ref, down_ref = refs[8:]
+    up_ref, down_ref, up_buf, down_buf, up_sem, down_sem = refs[8:]
     y, core = lax.axis_index("y"), lax.axis_index(CORE)
-    for index, ref in enumerate(refs[:8]):
-        owner = core ^ (index // 4)
+    copies = []
+    for near in range(4):
         for xl in range(2):
-            chip = (y ^ (index % 4)) * 2 + xl
-            block = ref[xl].astype(F32)
-            up_ref[pl.ds(pl.multiple_of((chip * 2 + owner) * 48, 16), 48)] = block[:, :384]
-            down_ref[
-                pl.ds(pl.multiple_of(chip * 48, 16), 48), pl.ds(pl.multiple_of(owner * 384, 128), 384)
-            ] = block[:, 384:]
+            chip = (y ^ near) * 2 + xl
+            for index in (near, near + 4):
+                owner = core ^ (index // 4)
+                block = refs[index][xl].astype(F32)
+                up_buf[near, xl, pl.ds(pl.multiple_of(owner * 48, 16), 48)] = block[:, :384]
+                down_buf[near, xl, :, pl.ds(pl.multiple_of(owner * 384, 128), 384)] = block[:, 384:]
+            for source, target, rows, sem in ((up_buf, up_ref, 96, up_sem), (down_buf, down_ref, 48, down_sem)):
+                copy = pltpu.make_async_copy(
+                    source.at[near, xl],
+                    target.at[pl.ds(pl.multiple_of(chip * rows, 16), rows)],
+                    sem.at[near, xl],
+                )
+                copy.start()
+                copies.append(copy)
+    wait_all(copies)
 
 
 def input_kernel(
@@ -799,18 +818,19 @@
     qkv_grad, out_proj_grad, *vectors = call(
         functools.partial(spread_kernel, True),
         grads + [((D,), F32, "L")] * 4,
-        [(weight_other, "V"), (half[2], "V"), (half[0], "H"), (half[1], "H")],
-        1000,
-        scratch,
+        [(weight_other, "H"), (half[2], "V"), (half[0], "H"), (half[1], "H")],
+        1000,
+        [pltpu.VMEM((8, 8, 56, 384), BF), DMA((8,))] + scratch,
         aliases={2: 0, 3: 1},
     )
     ff_parts = [after(value, pin(vectors[0])) for value in ff_parts]
     ff_swapped = [swap(value) for value in (ff_part, *ff_parts)]
     up_grad, down_grad = call(
         spread_ff_kernel,
-        [((D, FFL), F32, "L"), ((FFL, D), F32, "L")],
+        [((D, FFL), F32, "H"), ((FFL, D), F32, "H")],
         [(ff_part, "L"), *[(value, "V") for value in ff_parts], *[(value, "V") for value in ff_swapped]],
         1000,
+        [pltpu.VMEM((4, 2, 96, FFL), F32), pltpu.VMEM((4, 2, 48, D), F32), DMA((4, 2)), DMA((4, 2))],
     )
     input_grad, result = call(
         unpack_kernel, [((2, TOK, D), F32, "L"), ((2, TOK, D), BF, "L")], [(everyone, "V"), (vectors[0], "H"), (up_grad, "H")], 1000

time: 201 us -> 201 us (level)
  transfers between devices with their start and end apart: 30 -> 30, of which waited for: 15 -> 13; matrix products, arithmetic and copies ran while one was open for 1% -> 1% of each run, Pallas kernels for 16% -> 15%
where the time goes in v17:
time: 201 us; the launch traced here: 199 us
  waiting for transfers between devices  79 us (39%)
  starting transfers between devices  69 us (34%)
  Pallas kernels  48.9 us (24%)
    all_to_all x7, waiting for transfers between devices, exchange(): return lax.all_to_all(value, axes, 0, 0, tiled=True)  55.6 us
    pallas_call x18, Pallas kernels, call(): pl.pallas_call(kernel, out_shape=[(pltpu.HBM if place in 'HL' else jax.Sh...  48.8 us
    all_to_all x7, starting transfers between devices, exchange(): return lax.all_to_all(value, axes, 0, 0, tiled=True)  38.5 us
    ppermute x13, waiting for transfers between devices, flip(): lax.ppermute(value, axes, [(index, index ^ bits) for index in range(count)])  18.2 us
    ppermute x13, starting transfers between devices, flip(): lax.ppermute(value, axes, [(index, index ^ bits) for index in range(count)])  16.4 us
    ppermute x10, starting transfers between devices, swap(): return lax.ppermute(value, CORE, [(0, 1), (1, 0)])  14.1 us
    ppermute x10, waiting for transfers between devices, swap(): return lax.ppermute(value, CORE, [(0, 1), (1, 0)])  5.22 us
  transfers between devices with their start and end apart: 30, of which 13 were waited for; matrix products, arithmetic and copies ran while one was open for 1% of the time, Pallas kernels for 15%

profile of v17, /device:TPU:1, one launch (start us, length us, event | category | flops | bytes accessed | tf_op | source)
XLA Modules:
  0.0 199.3 jit_solution(11420416811726292357)
XLA Ops:
  0.6 3.7 %shard_map.186 = (bf16[8,128,384]{2,1,0:T(8,128)(2,1)}, bf16[128,768]{1,0:T(8,128)(2,1)}) custom-call(bf16[2,128,768]{2,1,0:T(8,128)(2,1)} %tok_ref.7, f32[768]{0:T(1024)} %gain_ref.7, f32[768]{0:T(1024)} %shift_ref.2, bf16[768,2304]{1,0:T(8,128)(2,1)} %w_ref.7), custom_call_target="tpu_custom_call" | custom-call | flops 1000 | bytes 1000 | tf_op jit(solution)/shard_map/pallas_call | solution.py:106
  4.3 6.0 %all-to-all-start = ((bf16[8,128,384]{2,1,0:T(8,128)(2,1)}), bf16[8,128,384]{2,1,0:T(8,128)(2,1)S(1)}, u32[]{:S(2)}, u32[]{:S(2)}) async-start(bf16[8,128,384]{2,1,0:T(8,128)(2,1)} %get-tuple-element.51), calls=%async_computation | async-start | bytes 1572864 | tf_op jit(solution)/shard_map/all_to_all | solution.py:627
  10.3 3.0 %shard_map.187.refs_1_.q_ref = bf16[128,256]{1,0:T(8,128)(2,1)} custom-call(bf16[128,768]{1,0:T(8,128)(2,1)} %get-tuple-element.52.normed_ref, bf16[768,2304]{1,0:T(8,128)(2,1)} %w_ref.7), custom_call_target="tpu_custom_call" | custom-call | flops 1000 | bytes 1000 | tf_op jit(solution)/shard_map/pallas_call | solution.py:106
  13.4 8.6 %all-to-all-done.refs_0_ = bf16[8,128,384]{2,1,0:T(8,128)(2,1)S(1)} async-done(((bf16[8,128,384]{2,1,0:T(8,128)(2,1)}), bf16[8,128,384]{2,1,0:T(8,128)(2,1)S(1)}, u32[]{:S(2)}, u32[]{:S(2)}) %all-to-all-start) | async-done | bytes 786464 | tf_op jit(solution)/shard_map/all_to_all | solution.py:627
  26.1 3.1 %shard_map.189 = bf16[8,128,256]{2,1,0:T(8,128)(2,1)} custom-call(s32[2,32]{1,0:T(2,128)S(1)} %copy-done.3, bf16[128,256]{1,0:T(8,128)(2,1)} %shard_map.187.refs_1_.q_ref, bf16[8,128,384]{2,1,0:T(8,128)(2,1)S(1)} %shard_map.188.same_ref.refs_0_, bf16[8,128,384]{2,1,0:T(8,128)(2,1)S(1)} %collective-permute-done.other_ref), custom_call_target="tpu_custom_call" | custom-call | flops 1000 | bytes 1000 | tf_op jit(solution)/shard_map/pallas_call | solution.py:106
  29.2 7.2 %all-to-all-start.1 = ((bf16[8,128,256]{2,1,0:T(8,128)(2,1)}), bf16[8,128,256]{2,1,0:T(8,128)(2,1)S(1)}, u32[]{:S(2)}, u32[]{:S(2)}) async-start(bf16[8,128,256]{2,1,0:T(8,128)(2,1)} %shard_map.189), calls=%async_computation.1 | async-start | bytes 1048576 | tf_op jit(solution)/shard_map/all_to_all | solution.py:627
  37.8 9.4 %all-to-all-done.1.mixed_ref = bf16[8,128,256]{2,1,0:T(8,128)(2,1)S(1)} async-done(((bf16[8,128,256]{2,1,0:T(8,128)(2,1)}), bf16[8,128,256]{2,1,0:T(8,128)(2,1)S(1)}, u32[]{:S(2)}, u32[]{:S(2)}) %all-to-all-start.1) | async-done | bytes 524320 | tf_op jit(solution)/shard_map/all_to_all | solution.py:627
  47.1 4.2 %shard_map.190 = (bf16[8,64,768]{2,1,0:T(8,128)(2,1)}, f32[32,768]{1,0:T(8,128)}, bf16[256,768]{1,0:T(8,128)(2,1)S(1)}, bf16[256,384]{1,0:T(8,128)(2,1)S(1)}, bf16[256,384]{1,0:T(8,128)(2,1)S(1)}) custom-call(bf16[8,128,256]{2,1,0:T(8,128)(2,1)S(1)} %all-to-all-done.1.mixed_ref, bf16[2,128,768]{2,1,0:T(8,128)(2,1)} %tok_ref.7, bf16[2,128,768]{2,1,0:T(8,128)(2,1)} %og_ref.5, ...), custom_call_target="tpu_custom_call" | custom-call | flops 1000 | bytes 1000 | tf_op jit(solution)/shard_map/pallas_call | solution.py:106
  51.3 2.8 %shard_map.194 = (bf16[8,48,768]{2,1,0:T(8,128)(2,1)S(1)}, bf16[8,48,768]{2,1,0:T(8,128)(2,1)}) custom-call(bf16[256,768]{1,0:T(8,128)(2,1)S(1)} %get-tuple-element.57.normed_ref, bf16[256,384]{1,0:T(8,128)(2,1)S(1)} %get-tuple-element.58.act_ref, bf16[256,384]{1,0:T(8,128)(2,1)S(1)} %get-tuple-element.59.gpre_ref, bf16[2,128,768]{2,1,0:T(8,128)(2,1)} %og_ref.5), custom_call_target="tpu_custom_call" | custom-call | flops 1000 | bytes 1000 | tf_op jit(solution)/shard_map/pallas_call | solution.py:106
  55.8 3.5 %all-to-all-start.2 = ((bf16[8,64,768]{2,1,0:T(8,128)(2,1)}), bf16[8,64,768]{2,1,0:T(8,128)(2,1)S(1)}, u32[]{:S(2)}, u32[]{:S(2)}) async-start(bf16[8,64,768]{2,1,0:T(8,128)(2,1)} %get-tuple-element.53), calls=%async_computation.2 | async-start | bytes 1572864 | tf_op jit(solution)/shard_map/all_to_all | solution.py:627
  61.3 2.6 %collective-permute-start.4 = (bf16[2,48,768]{2,1,0:T(8,128)(2,1)}, bf16[2,48,768]{2,1,0:T(8,128)(2,1)S(1)}, u32[]{:S(2)}, u32[]{:S(2)}) collective-permute-start(bf16[2,48,768]{2,1,0:T(8,128)(2,1)} %get-tuple-element.63), channel_id=1, source_target_pairs={{0,64},{32,96},{64,0},{96,32},{1,65},{33,97},{65,1},{97,33},{2,66}... | collective-permute-start | bytes 442376 | tf_op jit(solution)/shard_map/ppermute | solution.py:647
  65.2 2.3 %shard_map.191.query_ref = bf16[4,32,256]{2,1,0:T(8,128)(2,1)} custom-call(bf16[128,768]{1,0:T(8,128)(2,1)} %get-tuple-element.52.normed_ref, bf16[768,2304]{1,0:T(8,128)(2,1)} %w_ref.7), custom_call_target="tpu_custom_call" | custom-call | flops 1000 | bytes 1000 | tf_op jit(solution)/shard_map/pallas_call | solution.py:106
  67.5 6.4 %all-to-all-done.2.sums_ref = bf16[8,64,768]{2,1,0:T(8,128)(2,1)S(1)} async-done(((bf16[8,64,768]{2,1,0:T(8,128)(2,1)}), bf16[8,64,768]{2,1,0:T(8,128)(2,1)S(1)}, u32[]{:S(2)}, u32[]{:S(2)}) %all-to-all-start.2) | async-done | bytes 786464 | tf_op jit(solution)/shard_map/all_to_all | solution.py:627
  73.9 3.0 %shard_map.192 = (bf16[8,4,32,512]{3,2,1,0:T(8,128)(2,1)}, bf16[32,768]{1,0:T(8,128)(2,1)}, f32[32,768]{1,0:T(8,128)}, bf16[32,768]{1,0:T(8,128)(2,1)}, f32[8,768]{1,0:T(8,128)}) custom-call(bf16[8,64,768]{2,1,0:T(8,128)(2,1)S(1)} %all-to-all-done.2.sums_ref, f32[32,768]{1,0:T(8,128)} %get-tuple-element.54.middle_ref, bf16[2,128,768]{2,1,0:T(8,128)(2,1)} %og_ref.5, ...), custom_call_target="tpu_custom_call" | custom-call | flops 1000 | bytes 1000 | tf_op jit(solution)/shard_map/pallas_call | solution.py:106
  76.9 3.9 %all-to-all-start.3 = ((bf16[32,32,512]{2,1,0:T(8,128)(2,1)}), bf16[32,32,512]{2,1,0:T(8,128)(2,1)S(1)}, u32[]{:S(2)}, u32[]{:S(2)}) async-start(bf16[32,32,512]{2,1,0:T(8,128)(2,1)} %bitcast.8), calls=%async_computation.3 | async-start | bytes 2097152 | tf_op jit(solution)/shard_map/all_to_all | solution.py:627
  81.7 2.9 %collective-permute-start.6 = (bf16[32,768]{1,0:T(8,128)(2,1)S(1)}, bf16[32,768]{1,0:T(8,128)(2,1)S(1)}, u32[]{:S(2)}, u32[]{:S(2)}) collective-permute-start(bf16[32,768]{1,0:T(8,128)(2,1)S(1)} %copy-done.2), channel_id=1, source_target_pairs={{0,1},{1,0},{2,3},{3,2},{4,5},{5,4},{6,7},{7,6},{8,9},{9,8},{10,11... | collective-permute-start | bytes 147464 | tf_op jit(solution)/shard_map/ppermute | solution.py:647
  87.6 8.3 %collective-permute-done.6.refs_1_.low1_ref = bf16[32,768]{1,0:T(8,128)(2,1)S(1)} collective-permute-done((bf16[32,768]{1,0:T(8,128)(2,1)S(1)}, bf16[32,768]{1,0:T(8,128)(2,1)S(1)}, u32[]{:S(2)}, u32[]{:S(2)}) %collective-permute-start.6) | collective-permute-done | bytes 49184 | tf_op jit(solution)/shard_map/ppermute | solution.py:647
  95.8 2.4 %collective-permute-done.8.refs_3_.low3_ref = bf16[32,768]{1,0:T(8,128)(2,1)S(1)} collective-permute-done((bf16[32,768]{1,0:T(8,128)(2,1)S(1)}, bf16[32,768]{1,0:T(8,128)(2,1)S(1)}, u32[]{:S(2)}, u32[]{:S(2)}) %collective-permute-start.8) | collective-permute-done | bytes 49184 | tf_op jit(solution)/shard_map/ppermute | solution.py:647
  102.8 4.3 %shard_map.199 = (bf16[128,640]{1,0:T(8,128)(2,1)S(1)}, bf16[3,768,384]{2,1,0:T(8,128)(2,1)S(1)}, bf16[16,48,384]{2,1,0:T(8,128)(2,1)S(1)}, bf16[16,48,384]{2,1,0:T(8,128)(2,1)S(1)}) custom-call(s32[2,32]{1,0:T(2,128)S(1)} %copy-done.3, bf16[8,128,384]{2,1,0:T(8,128)(2,1)} %shard_map.193.kvs_ref, ...), custom_call_target="tpu_custom_call" | custom-call | flops 1000 | bytes 1000 | tf_op jit(solution)/shard_map/pallas_call | solution.py:106
  109.0 2.5 %shard_map.201 = (f32[32,768]{1,0:T(8,128)}, bf16[32,768]{1,0:T(8,128)(2,1)}, bf16[32,768]{1,0:T(8,128)(2,1)}, bf16[32,768]{1,0:T(8,128)(2,1)}, f32[8,768]{1,0:T(8,128)}, /*index=5*/bf16[2,48,768]{2,1,0:T(8,128)(2,1)}) custom-call(bf16[128,640]{1,0:T(8,128)(2,1)S(1)} %get-tuple-element.66.gqkv_ref, bf16[3,768,384]{2,1,0:T(8,128)(2,1)S(1)} %get-tuple-element.67.w_ref, ...), custom_call_target="tpu_custom_call" | custom-call | flops 1000 | bytes 1000 | tf_op jit(solution)/shard_map/pallas_call | solution.py:106
  112.5 6.0 %all-to-all-start.4 = ((bf16[16,48,384]{2,1,0:T(8,128)(2,1)}), bf16[16,48,384]{2,1,0:T(8,128)(2,1)S(1)}, u32[]{:S(2)}, u32[]{:S(2)}) async-start(bf16[16,48,384]{2,1,0:T(8,128)(2,1)} %shard_map.203), calls=%async_computation.4 | async-start | bytes 1179648 | tf_op jit(solution)/shard_map/all_to_all | solution.py:627
  119.4 3.3 %collective-permute-start.13 = (bf16[32,768]{1,0:T(8,128)(2,1)S(1)}, bf16[32,768]{1,0:T(8,128)(2,1)S(1)}, u32[]{:S(2)}, u32[]{:S(2)}) collective-permute-start(bf16[32,768]{1,0:T(8,128)(2,1)S(1)} %copy-done.4), channel_id=1, source_target_pairs={{0,3},{1,2},{2,1},{3,0},{4,7},{5,6},{6,5},{7,4},{8,11},{9,10},{10,... | collective-permute-start | bytes 147464 | tf_op jit(solution)/shard_map/ppermute | solution.py:647
  122.7 4.9 %collective-permute-done.11.refs_2_.one_ref = bf16[32,768]{1,0:T(8,128)(2,1)S(1)} collective-permute-done((bf16[32,768]{1,0:T(8,128)(2,1)S(1)}, bf16[32,768]{1,0:T(8,128)(2,1)S(1)}, u32[]{:S(2)}, u32[]{:S(2)}) %collective-permute-start.11) | collective-permute-done | bytes 49184 | tf_op jit(solution)/shard_map/ppermute | solution.py:647
  130.0 2.4 %shard_map.205.unused_ref = bf16[8,8,56,384]{3,2,1,0:T(8,128)(2,1)} custom-call(bf16[16,48,384]{2,1,0:T(8,128)(2,1)S(1)} %shard_map.204.in_ref, f32[8,768]{1,0:T(8,128)} %get-tuple-element.77.refs_1_.vec_ref), custom_call_target="tpu_custom_call" | custom-call | flops 1000 | bytes 1000 | tf_op jit(solution)/shard_map/pallas_call | solution.py:106
  132.4 8.2 %all-to-all-start.5 = ((bf16[64,56,384]{2,1,0:T(8,128)(2,1)}), bf16[64,56,384]{2,1,0:T(8,128)(2,1)S(1)}, u32[]{:S(2)}, u32[]{:S(2)}) async-start(bf16[64,56,384]{2,1,0:T(8,128)(2,1)} %bitcast.7), calls=%async_computation.5 | async-start | bytes 5505024 | tf_op jit(solution)/shard_map/all_to_all | solution.py:627
  140.6 3.0 %shard_map.206.refs_1_.refs_0_ = bf16[8,64,768]{2,1,0:T(8,128)(2,1)} custom-call(f32[32,768]{1,0:T(8,128)} %get-tuple-element.69.unused_ref.own_ref, bf16[32,768]{1,0:T(8,128)(2,1)S(1)} %collective-permute-done.11.refs_2_.one_ref, bf16[32,768]{1,0:T(8,128)(2,1)S(1)} %collective-permute-done.12.refs_3_.two_ref, ...), custom_call_target="tpu_custom_call" | custom-call | flops 1000 | bytes 1000 | tf_op jit(solution)/shard_map/pallas_call | solution.py:106
  143.6 30.7 %all-to-all-done.5 = bf16[64,56,384]{2,1,0:T(8,128)(2,1)S(1)} async-done(((bf16[64,56,384]{2,1,0:T(8,128)(2,1)}), bf16[64,56,384]{2,1,0:T(8,128)(2,1)S(1)}, u32[]{:S(2)}, u32[]{:S(2)}) %all-to-all-start.5) | async-done | bytes 2752544 | tf_op jit(solution)/shard_map/all_to_all | solution.py:627
  174.3 3.6 %collective-permute-start.15 = (bf16[8,8,56,384]{3,2,1,0:T(8,128)(2,1)S(1)}, bf16[8,8,56,384]{3,2,1,0:T(8,128)(2,1)}, u32[]{:S(2)}, u32[]{:S(2)}) collective-permute-start(bf16[8,8,56,384]{3,2,1,0:T(8,128)(2,1)S(1)} %shard_map.207.refs_1_.in_ref), channel_id=1, source_target_pairs={{0,8},{8,0},{1,9},{9,1},{2,10},{10,2},{3,11},{11,3},{4,12},{12,4},... | collective-permute-start | bytes 8257544 | tf_op jit(solution)/shard_map/ppermute | solution.py:631
  177.9 3.7 %all-to-all-start.6 = ((bf16[8,64,768]{2,1,0:T(8,128)(2,1)}), bf16[8,64,768]{2,1,0:T(8,128)(2,1)S(1)}, u32[]{:S(2)}, u32[]{:S(2)}) async-start(bf16[8,64,768]{2,1,0:T(8,128)(2,1)} %shard_map.208), calls=%async_computation.6 | async-start | bytes 1572864 | tf_op jit(solution)/shard_map/all_to_all | solution.py:627
  186.6 2.4 %shard_map.209 = (f32[768,2304]{1,0:T(8,128)}, f32[768,768]{1,0:T(8,128)}, f32[8,384]{1,0:T(8,128)S(1)}) custom-call(bf16[8,8,56,384]{3,2,1,0:T(8,128)(2,1)S(1)} %shard_map.207.refs_1_.in_ref), custom_call_target="tpu_custom_call" | custom-call | flops 1000 | bytes 1000 | tf_op jit(solution)/shard_map/pallas_call | solution.py:106
  189.0 4.1 %shard_map.210 = (f32[768,2304]{1,0:T(8,128)}, f32[768,768]{1,0:T(8,128)}, f32[768]{0:T(1024)}, f32[768]{0:T(1024)}, f32[768]{0:T(1024)}, /*index=5*/f32[768]{0:T(1024)}) custom-call(bf16[8,8,56,384]{3,2,1,0:T(8,128)(2,1)} %collective-permute-done.15.in_ref, f32[8,384]{1,0:T(8,128)S(1)} %get-tuple-element.78.refs_0_, ...), custom_call_target="tpu_custom_call", output_to_operand_aliasing={{0}: (2, {}), {1}: (3, {})} | custom-call | flops 1000 | bytes 1000 | tf_op jit(solution)/shard_map/pallas_call | solution.py:106
  195.8 2.5 %shard_map.214 = (f32[768,384]{1,0:T(8,128)}, f32[384,768]{1,0:T(8,128)}) custom-call(bf16[2,48,768]{2,1,0:T(8,128)(2,1)} %get-tuple-element.82.refs_0_, bf16[2,48,768]{2,1,0:T(8,128)(2,1)S(1)} %shard_map.211.refs_1_, bf16[2,48,768]{2,1,0:T(8,128)(2,1)S(1)} %shard_map.212.refs_2_, bf16[2,48,768]{2,1,0:T(8,128)(2,1)S(1)} %shard_map.213.refs_3_, ...), custom_call_target="tpu_custom_call" | custom-call | flops 1000 | bytes 1000 | tf_op jit(solution)/shard_map/pallas_call | solution.py:106
  (73 shorter events, 33.4 us)
Async XLA Ops:
  4.3 17.6 %all-to-all-start = ((bf16[8,128,384]{2,1,0:T(8,128)(2,1)}), bf16[8,128,384]{2,1,0:T(8,128)(2,1)S(1)}, u32[]{:S(2)}, u32[]{:S(2)}) async-start(bf16[8,128,384]{2,1,0:T(8,128)(2,1)} %get-tuple-element.51), calls=%async_computation | async-start | bytes 1572864 | tf_op jit(solution)/shard_map/all_to_all | solution.py:627
  10.3 15.8 %copy-start.3 = (s32[2,32]{1,0:T(2,128)S(1)}, s32[2,32]{1,0:T(2,128)}, u32[]{:S(2)}) copy-start(s32[2,32]{1,0:T(2,128)} %scene_ref.3) | copy-start | bytes 772
  22.0 15.8 %copy-start = (bf16[8,128,384]{2,1,0:T(8,128)(2,1)}, bf16[8,128,384]{2,1,0:T(8,128)(2,1)S(1)}, u32[]{:S(2)}) copy-start(bf16[8,128,384]{2,1,0:T(8,128)(2,1)S(1)} %shard_map.188.same_ref.refs_0_) | copy-start | bytes 2359300
  22.0 4.1 %collective-permute-start = (bf16[8,128,384]{2,1,0:T(8,128)(2,1)S(1)}, bf16[8,128,384]{2,1,0:T(8,128)(2,1)S(1)}, u32[]{:S(2)}, u32[]{:S(2)}) collective-permute-start(bf16[8,128,384]{2,1,0:T(8,128)(2,1)S(1)} %shard_map.188.same_ref.refs_0_), channel_id=1, source_target_pairs={{0,8},{8,0},{1,9},{9,1},{2,10},{10,2},{3,11},{11,3},{4,12},{12,4},... | collective-permute-start | bytes 2359304 | tf_op jit(solution)/shard_map/ppermute | solution.py:631
  29.2 18.0 %all-to-all-start.1 = ((bf16[8,128,256]{2,1,0:T(8,128)(2,1)}), bf16[8,128,256]{2,1,0:T(8,128)(2,1)S(1)}, u32[]{:S(2)}, u32[]{:S(2)}) async-start(bf16[8,128,256]{2,1,0:T(8,128)(2,1)} %shard_map.189), calls=%async_computation.1 | async-start | bytes 1048576 | tf_op jit(solution)/shard_map/all_to_all | solution.py:627
  54.1 5.3 %collective-permute-start.2 = (bf16[8,48,768]{2,1,0:T(8,128)(2,1)}, bf16[8,48,768]{2,1,0:T(8,128)(2,1)}, u32[]{:S(2)}, u32[]{:S(2)}) collective-permute-start(bf16[8,48,768]{2,1,0:T(8,128)(2,1)} %get-tuple-element.61), channel_id=1, source_target_pairs={{0,8},{8,0},{1,9},{9,1},{2,10},{10,2},{3,11},{11,3},{4,12},{12,4},... | collective-permute-start | bytes 1769480 | tf_op jit(solution)/shard_map/ppermute | solution.py:631
  55.8 18.1 %all-to-all-start.2 = ((bf16[8,64,768]{2,1,0:T(8,128)(2,1)}), bf16[8,64,768]{2,1,0:T(8,128)(2,1)S(1)}, u32[]{:S(2)}, u32[]{:S(2)}) async-start(bf16[8,64,768]{2,1,0:T(8,128)(2,1)} %get-tuple-element.53), calls=%async_computation.2 | async-start | bytes 1572864 | tf_op jit(solution)/shard_map/all_to_all | solution.py:627
  61.3 15.5 %collective-permute-start.3 = (bf16[2,48,768]{2,1,0:T(8,128)(2,1)}, bf16[2,48,768]{2,1,0:T(8,128)(2,1)S(1)}, u32[]{:S(2)}, u32[]{:S(2)}) collective-permute-start(bf16[2,48,768]{2,1,0:T(8,128)(2,1)} %get-tuple-element.62), channel_id=1, source_target_pairs={{0,32},{32,0},{64,96},{96,64},{1,33},{33,1},{65,97},{97,65},{2,34}... | collective-permute-start | bytes 442376 | tf_op jit(solution)/shard_map/ppermute | solution.py:647
  61.3 15.6 %collective-permute-start.4 = (bf16[2,48,768]{2,1,0:T(8,128)(2,1)}, bf16[2,48,768]{2,1,0:T(8,128)(2,1)S(1)}, u32[]{:S(2)}, u32[]{:S(2)}) collective-permute-start(bf16[2,48,768]{2,1,0:T(8,128)(2,1)} %get-tuple-element.63), channel_id=1, source_target_pairs={{0,64},{32,96},{64,0},{96,32},{1,65},{33,97},{65,1},{97,33},{2,66}... | collective-permute-start | bytes 442376 | tf_op jit(solution)/shard_map/ppermute | solution.py:647
  64.0 12.9 %collective-permute-start.5 = (bf16[2,48,768]{2,1,0:T(8,128)(2,1)}, bf16[2,48,768]{2,1,0:T(8,128)(2,1)S(1)}, u32[]{:S(2)}, u32[]{:S(2)}) collective-permute-start(bf16[2,48,768]{2,1,0:T(8,128)(2,1)} %get-tuple-element.64), channel_id=1, source_target_pairs={{0,96},{32,64},{64,32},{96,0},{1,97},{33,65},{65,33},{97,1},{2,98}... | collective-permute-start | bytes 442376 | tf_op jit(solution)/shard_map/ppermute | solution.py:647
  76.9 21.4 %all-to-all-start.3 = ((bf16[32,32,512]{2,1,0:T(8,128)(2,1)}), bf16[32,32,512]{2,1,0:T(8,128)(2,1)S(1)}, u32[]{:S(2)}, u32[]{:S(2)}) async-start(bf16[32,32,512]{2,1,0:T(8,128)(2,1)} %bitcast.8), calls=%async_computation.3 | async-start | bytes 2097152 | tf_op jit(solution)/shard_map/all_to_all | solution.py:627
  80.9 17.4 %collective-permute-start.1 = (bf16[8,128,384]{2,1,0:T(8,128)(2,1)}, bf16[8,128,384]{2,1,0:T(8,128)(2,1)S(1)}, u32[]{:S(2)}, u32[]{:S(2)}) collective-permute-start(bf16[8,128,384]{2,1,0:T(8,128)(2,1)} %shard_map.193.kvs_ref), channel_id=1, source_target_pairs={{0,8},{8,0},{1,9},{9,1},{2,10},{10,2},{3,11},{11,3},{4,12},{12,4},... | collective-permute-start | bytes 2359304 | tf_op jit(solution)/shard_map/ppermute | solution.py:631
  81.7 14.1 %collective-permute-start.6 = (bf16[32,768]{1,0:T(8,128)(2,1)S(1)}, bf16[32,768]{1,0:T(8,128)(2,1)S(1)}, u32[]{:S(2)}, u32[]{:S(2)}) collective-permute-start(bf16[32,768]{1,0:T(8,128)(2,1)S(1)} %copy-done.2), channel_id=1, source_target_pairs={{0,1},{1,0},{2,3},{3,2},{4,5},{5,4},{6,7},{7,6},{8,9},{9,8},{10,11... | collective-permute-start | bytes 147464 | tf_op jit(solution)/shard_map/ppermute | solution.py:647
  84.7 11.2 %collective-permute-start.7 = (bf16[32,768]{1,0:T(8,128)(2,1)S(1)}, bf16[32,768]{1,0:T(8,128)(2,1)S(1)}, u32[]{:S(2)}, u32[]{:S(2)}) collective-permute-start(bf16[32,768]{1,0:T(8,128)(2,1)S(1)} %copy-done.2), channel_id=1, source_target_pairs={{0,2},{1,3},{2,0},{3,1},{4,6},{5,7},{6,4},{7,5},{8,10},{9,11},{10,... | collective-permute-start | bytes 147464 | tf_op jit(solution)/shard_map/ppermute | solution.py:647
  85.9 12.4 %collective-permute-start.8 = (bf16[32,768]{1,0:T(8,128)(2,1)S(1)}, bf16[32,768]{1,0:T(8,128)(2,1)S(1)}, u32[]{:S(2)}, u32[]{:S(2)}) collective-permute-start(bf16[32,768]{1,0:T(8,128)(2,1)S(1)} %copy-done.2), channel_id=1, source_target_pairs={{0,3},{1,2},{2,1},{3,0},{4,7},{5,6},{6,5},{7,4},{8,11},{9,10},{10,... | collective-permute-start | bytes 147464 | tf_op jit(solution)/shard_map/ppermute | solution.py:647
  98.3 4.2 %collective-permute-start.9 = (bf16[8,128,512]{2,1,0:T(8,128)(2,1)S(1)}, bf16[8,128,512]{2,1,0:T(8,128)(2,1)S(1)}, u32[]{:S(2)}, u32[]{:S(2)}) collective-permute-start(bf16[8,128,512]{2,1,0:T(8,128)(2,1)S(1)} %shard_map.198.gs_ref), channel_id=1, source_target_pairs={{0,8},{8,0},{1,9},{9,1},{2,10},{10,2},{3,11},{11,3},{4,12},{12,4},... | collective-permute-start | bytes 3145736 | tf_op jit(solution)/shard_map/ppermute | solution.py:631
  102.5 5.3 %collective-permute-start.10 = (bf16[2,48,768]{2,1,0:T(8,128)(2,1)}, bf16[2,48,768]{2,1,0:T(8,128)(2,1)S(1)}, u32[]{:S(2)}, u32[]{:S(2)}) collective-permute-start(bf16[2,48,768]{2,1,0:T(8,128)(2,1)} %shard_map.200.near_ref), channel_id=1, source_target_pairs={{0,16},{16,0},{1,17},{17,1},{2,18},{18,2},{3,19},{19,3},{4,20},{20... | collective-permute-start | bytes 442376 | tf_op jit(solution)/shard_map/ppermute | solution.py:647
  107.8 3.8 %collective-permute-start.14 = (bf16[16,48,384]{2,1,0:T(8,128)(2,1)S(1)}, bf16[16,48,384]{2,1,0:T(8,128)(2,1)S(1)}, u32[]{:S(2)}, u32[]{:S(2)}) collective-permute-start(bf16[16,48,384]{2,1,0:T(8,128)(2,1)S(1)} %shard_map.202), channel_id=1, source_target_pairs={{0,8},{8,0},{1,9},{9,1},{2,10},{10,2},{3,11},{11,3},{4,12},{12,4},... | collective-permute-start | bytes 1769480 | tf_op jit(solution)/shard_map/ppermute | solution.py:631
  112.5 17.5 %all-to-all-start.4 = ((bf16[16,48,384]{2,1,0:T(8,128)(2,1)}), bf16[16,48,384]{2,1,0:T(8,128)(2,1)S(1)}, u32[]{:S(2)}, u32[]{:S(2)}) async-start(bf16[16,48,384]{2,1,0:T(8,128)(2,1)} %shard_map.203), calls=%async_computation.4 | async-start | bytes 1179648 | tf_op jit(solution)/shard_map/all_to_all | solution.py:627
  118.5 9.1 %collective-permute-start.11 = (bf16[32,768]{1,0:T(8,128)(2,1)S(1)}, bf16[32,768]{1,0:T(8,128)(2,1)S(1)}, u32[]{:S(2)}, u32[]{:S(2)}) collective-permute-start(bf16[32,768]{1,0:T(8,128)(2,1)S(1)} %copy-done.6), channel_id=1, source_target_pairs={{0,1},{1,0},{2,3},{3,2},{4,5},{5,4},{6,7},{7,6},{8,9},{9,8},{10,11... | collective-permute-start | bytes 147464 | tf_op jit(solution)/shard_map/ppermute | solution.py:647
  119.4 8.2 %collective-permute-start.12 = (bf16[32,768]{1,0:T(8,128)(2,1)S(1)}, bf16[32,768]{1,0:T(8,128)(2,1)S(1)}, u32[]{:S(2)}, u32[]{:S(2)}) collective-permute-start(bf16[32,768]{1,0:T(8,128)(2,1)S(1)} %copy-done.5), channel_id=1, source_target_pairs={{0,2},{1,3},{2,0},{3,1},{4,6},{5,7},{6,4},{7,5},{8,10},{9,11},{10,... | collective-permute-start | bytes 147464 | tf_op jit(solution)/shard_map/ppermute | solution.py:647
  119.4 10.1 %collective-permute-start.13 = (bf16[32,768]{1,0:T(8,128)(2,1)S(1)}, bf16[32,768]{1,0:T(8,128)(2,1)S(1)}, u32[]{:S(2)}, u32[]{:S(2)}) collective-permute-start(bf16[32,768]{1,0:T(8,128)(2,1)S(1)} %copy-done.4), channel_id=1, source_target_pairs={{0,3},{1,2},{2,1},{3,0},{4,7},{5,6},{6,5},{7,4},{8,11},{9,10},{10,... | collective-permute-start | bytes 147464 | tf_op jit(solution)/shard_map/ppermute | solution.py:647
  132.4 41.9 %all-to-all-start.5 = ((bf16[64,56,384]{2,1,0:T(8,128)(2,1)}), bf16[64,56,384]{2,1,0:T(8,128)(2,1)S(1)}, u32[]{:S(2)}, u32[]{:S(2)}) async-start(bf16[64,56,384]{2,1,0:T(8,128)(2,1)} %bitcast.7), calls=%async_computation.5 | async-start | bytes 5505024 | tf_op jit(solution)/shard_map/all_to_all | solution.py:627
  174.3 14.7 %collective-permute-start.15 = (bf16[8,8,56,384]{3,2,1,0:T(8,128)(2,1)S(1)}, bf16[8,8,56,384]{3,2,1,0:T(8,128)(2,1)}, u32[]{:S(2)}, u32[]{:S(2)}) collective-permute-start(bf16[8,8,56,384]{3,2,1,0:T(8,128)(2,1)S(1)} %shard_map.207.refs_1_.in_ref), channel_id=1, source_target_pairs={{0,8},{8,0},{1,9},{9,1},{2,10},{10,2},{3,11},{11,3},{4,12},{12,4},... | collective-permute-start | bytes 8257544 | tf_op jit(solution)/shard_map/ppermute | solution.py:631
  177.9 20.3 %all-to-all-start.6 = ((bf16[8,64,768]{2,1,0:T(8,128)(2,1)}), bf16[8,64,768]{2,1,0:T(8,128)(2,1)S(1)}, u32[]{:S(2)}, u32[]{:S(2)}) async-start(bf16[8,64,768]{2,1,0:T(8,128)(2,1)} %shard_map.208), calls=%async_computation.6 | async-start | bytes 1572864 | tf_op jit(solution)/shard_map/all_to_all | solution.py:627
  181.6 11.5 %collective-permute-start.16 = (bf16[2,48,768]{2,1,0:T(8,128)(2,1)}, bf16[2,48,768]{2,1,0:T(8,128)(2,1)S(1)}, u32[]{:S(2)}, u32[]{:S(2)}) collective-permute-start(bf16[2,48,768]{2,1,0:T(8,128)(2,1)} %get-tuple-element.82.refs_0_), channel_id=1, source_target_pairs={{0,32},{32,0},{64,96},{96,64},{1,33},{33,1},{65,97},{97,65},{2,34}... | collective-permute-start | bytes 442376 | tf_op jit(solution)/shard_map/ppermute | solution.py:647
  181.9 11.3 %collective-permute-start.17 = (bf16[2,48,768]{2,1,0:T(8,128)(2,1)}, bf16[2,48,768]{2,1,0:T(8,128)(2,1)S(1)}, u32[]{:S(2)}, u32[]{:S(2)}) collective-permute-start(bf16[2,48,768]{2,1,0:T(8,128)(2,1)} %get-tuple-element.82.refs_0_), channel_id=1, source_target_pairs={{0,64},{32,96},{64,0},{96,32},{1,65},{33,97},{65,1},{97,33},{2,66}... | collective-permute-start | bytes 442376 | tf_op jit(solution)/shard_map/ppermute | solution.py:647
  183.9 9.9 %collective-permute-start.18 = (bf16[2,48,768]{2,1,0:T(8,128)(2,1)}, bf16[2,48,768]{2,1,0:T(8,128)(2,1)S(1)}, u32[]{:S(2)}, u32[]{:S(2)}) collective-permute-start(bf16[2,48,768]{2,1,0:T(8,128)(2,1)} %get-tuple-element.82.refs_0_), channel_id=1, source_target_pairs={{0,96},{32,64},{64,32},{96,0},{1,97},{33,65},{65,33},{97,1},{2,98}... | collective-permute-start | bytes 442376 | tf_op jit(solution)/shard_map/ppermute | solution.py:647
  185.4 9.3 %collective-permute-start.19 = (bf16[2,48,768]{2,1,0:T(8,128)(2,1)}, bf16[2,48,768]{2,1,0:T(8,128)(2,1)S(1)}, u32[]{:S(2)}, u32[]{:S(2)}) collective-permute-start(bf16[2,48,768]{2,1,0:T(8,128)(2,1)} %get-tuple-element.82.refs_0_), channel_id=1, source_target_pairs={{0,8},{8,0},{1,9},{9,1},{2,10},{10,2},{3,11},{11,3},{4,12},{12,4},... | collective-permute-start | bytes 442376 | tf_op jit(solution)/shard_map/ppermute | solution.py:631
  193.1 1.6 collective-permute-start.20
  193.2 1.5 collective-permute-start.21
  193.8 2.0 collective-permute-start.22
  (5 other events, 35.4 us)

commit v18 on v17

--- a/solution.py
+++ b/solution.py
@@ -102,7 +102,7 @@
 
 
 def call(kernel, outs, ins, cost, scratch=(), vmem=16, aliases=None):
-    places = {"V": pltpu.VMEM, "H": pltpu.HBM, "S": pltpu.SMEM, "L": pltpu.VMEM}
+    places = {"V": pltpu.VMEM, "H": pltpu.HBM, "S": pltpu.SMEM, "L": pltpu.VMEM, "A": pl.ANY}
     return pl.pallas_call(
         kernel,
         out_shape=[
@@ -467,7 +467,7 @@
 
 def normed_grad_kernel(
     gqkv_ref, w_ref, tok_ref, vec_ref, near_ref, far_ref, own_ref, one_ref, two_ref, three_ref, sums_ref, ff_ref,
-    x_buf, vec_buf, near_buf, part_buf, low_buf, sums_buf, ff_buf, in_sem, out_sem,
+    x_buf, vec_buf, near_buf, part_buf, low_buf, sums_buf, ff_buf, rows_buf, in_sem, out_sem, row_sem,
 ):
     loads = [
         pltpu.make_async_copy(tok_ref.at[lax.axis_index(MICRO)], x_buf, in_sem.at[0]),
@@ -491,7 +491,8 @@
     stores = []
     for k, ref in enumerate((own_ref, one_ref, two_ref, three_ref)):
         rows = pl.ds(pl.multiple_of((group ^ k) * BLK, BLK), BLK)
-        stores.append(pltpu.make_async_copy((low_buf if k else part_buf).at[rows], ref, out_sem.at[k]))
+        target = ref.at[pl.ds(0, BLK)] if k else ref
+        stores.append(pltpu.make_async_copy((low_buf if k else part_buf).at[rows], target, out_sem.at[k]))
         stores[-1].start()
     wait_all(loads)
     ff_buf[...] = (near_buf[...].astype(F32) + far_ref[...].astype(F32)).astype(BF)
@@ -500,7 +501,17 @@
     unit, _ = normalized(x_buf[...].astype(F32))
     gain1 = jnp.sum(total * unit, axis=0, keepdims=True)
     shift1 = jnp.sum(total, axis=0, keepdims=True)
-    sums_buf[...] = jnp.concatenate([gain1, shift1, vec_buf[...][:2], jnp.zeros((4, D), F32)], axis=0)
+    vectors = jnp.concatenate([gain1, shift1, vec_buf[...][:2], jnp.zeros((4, D), F32)], axis=0)
+    sums_buf[...] = vectors
+    for index in range(4):
+        rows_buf[index] = jnp.concatenate(
+            [vectors[index:index + 1], jnp.zeros((15, D), F32)], axis=0
+        ).astype(BF)
+    for k, ref in enumerate((one_ref, two_ref, three_ref)):
+        stores.append(
+            pltpu.make_async_copy(rows_buf.at[group ^ (k + 1)], ref.at[pl.ds(BLK, 16)], row_sem.at[k])
+        )
+        stores[-1].start()
     stores.append(pltpu.make_async_copy(sums_buf, sums_ref, out_sem.at[4]))
     stores[-1].start()
     wait_all(stores)
@@ -513,15 +524,23 @@
     copy.wait()
 
 
-def sum_kernel(in_ref, vec_ref, out_ref, buf, vec_buf, sem, vec_sem):
-    load = pltpu.make_async_copy(vec_ref, vec_buf, vec_sem)
-    load.start()
+def sum_kernel(in_ref, vec_ref, one_ref, two_ref, three_ref, out_ref, buf, vec_buf, row_buf, sem, vec_sem, row_sem):
+    loads = [pltpu.make_async_copy(vec_ref, vec_buf, vec_sem)] + [
+        pltpu.make_async_copy(ref.at[pl.ds(BLK, 16)], row_buf.at[k], row_sem.at[k])
+        for k, ref in enumerate((one_ref, two_ref, three_ref))
+    ]
+    for load in loads:
+        load.start()
     total = in_ref[0].astype(F32)
     for index in range(1, 16):
         total = total + in_ref[index].astype(F32)
-    load.wait()
-    vectors = vec_buf[...][:4]
-    block = jnp.concatenate([total, vectors[:, :384], vectors[:, 384:]], axis=0).astype(BF)
+    wait_all(loads)
+    vector = vec_buf[pl.ds(group_index(), 1)]
+    for k in range(3):
+        vector = vector + row_buf[k].astype(F32)[:1]
+    rows = [vector[:, at:at + 128] for at in range(0, D, 128)] + [jnp.zeros((2, 128), F32)]
+    pieces = [total[at:at + 8] for at in range(0, 48, 8)] + [jnp.concatenate(rows, axis=0)]
+    block = jnp.concatenate(pieces, axis=1).astype(BF)
     for index in range(8):
         buf[index] = block
     wait_all(send_copies(buf, out_ref, range(8), sem))
@@ -541,14 +560,15 @@
     owner = lax.axis_index(CORE)
     owner = 1 - owner if turn else owner
     copies = []
-    vectors = jnp.zeros((8, 384), F32)
+    vectors = [jnp.zeros((8, 128), F32)] * 4
     for tile in range(8):
         if turn:
             loads[tile].wait()
         whole = [in_buf[tile, index].astype(F32) for index in range(8)]
-        block = [value[:48] for value in whole]
-        for value in whole:
-            vectors = vectors + value[48:]
+        block = [
+            jnp.concatenate([value[:, at:at + 384] for at in range(0, 2304, 384)], axis=0) for value in whole
+        ]
+        vectors = [total + whole[k][:, 2304:] + whole[4 + k][:, 2304:] for k, total in enumerate(vectors)]
         for part, half, at in ((1, 0, 0), (2, 0, 192), (0, 4, 0)):
             qkv_buf[tile, :, part * D:(part + 1) * D] = jnp.concatenate(
                 [block[half + group][:, at:at + 192] for group in range(4)], axis=1
@@ -568,11 +588,12 @@
             copy.start()
             copies.append(copy)
     if turn:
-        vectors = vectors + refs[0][...]
         for k, ref in enumerate(vec_refs):
-            ref[...] = jnp.concatenate([vectors[k:k + 1], vectors[4 + k:5 + k]], axis=1).reshape(D)
+            total = vectors[k] + refs[0][k]
+            ref[...] = jnp.concatenate([total[row:row + 1] for row in range(6)], axis=1).reshape(D)
     else:
-        vec_refs[0][...] = vectors
+        for k, total in enumerate(vectors):
+            vec_refs[0][k] = total
     wait_all(copies)
 
 
@@ -608,7 +629,7 @@
     load.wait()
     total = own_ref[...]
     for ref in (one_ref, two_ref, three_ref):
-        total = total + ref[...].astype(F32)
+        total = total + ref[:BLK].astype(F32)
     unit, inverse = normalized(x_buf[...].astype(F32))
     grad = grad_ref[...] + norm_back(total, unit, inverse, gain_ref[...].reshape(1, D))
     buf[:BLK] = grad.astype(BF)
@@ -764,12 +785,13 @@
     )
     own, *sends, sums, ff_part = call(
         normed_grad_kernel,
-        [((BLK, D), F32, "H")] + [((BLK, D), BF, "H")] * 3 + [((8, D), F32, "H"), ((2, 48, D), BF, "H")],
+        [((BLK, D), F32, "H")] + [((BLK + 16, D), BF, "H")] * 3 + [((8, D), F32, "H"), ((2, 48, D), BF, "H")],
         [(gqkv, "V"), (w_own, "V"), (tokens, "H"), (vec2, "H"), (ff_near, "H"), (ff_far, "V")],
         1000,
         [
             pltpu.VMEM((TOK, D), BF), pltpu.VMEM((8, D), F32), pltpu.VMEM((2, 48, D), BF), pltpu.VMEM((TOK, D), F32),
-            pltpu.VMEM((TOK, D), BF), pltpu.VMEM((8, D), F32), pltpu.VMEM((2, 48, D), BF), DMA((3,)), DMA((6,)),
+            pltpu.VMEM((TOK, D), BF), pltpu.VMEM((8, D), F32), pltpu.VMEM((2, 48, D), BF), pltpu.VMEM((4, 16, D), BF),
+            DMA((3,)), DMA((6,)), DMA((3,)),
         ],
     )
     (weight_send,) = call(
@@ -785,10 +807,13 @@
     ff_parts = [flip(ff_part, "y", 4, k) for k in (1, 2, 3)]
     (weight_total,) = call(
         sum_kernel,
-        [((8, 8, 56, 384), BF, "H")],
-        [(weight_parts, "V"), (sums, "H")],
-        1000,
-        [pltpu.VMEM((8, 56, 384), BF), pltpu.VMEM((8, D), F32), DMA((8,)), DMA],
+        [((8, 8, 8, 2432), BF, "H")],
+        [(weight_parts, "V"), (sums, "H"), *[(value, "A") for value in parts]],
+        1000,
+        [
+            pltpu.VMEM((8, 8, 2432), BF), pltpu.VMEM((8, D), F32), pltpu.VMEM((3, 16, D), BF), DMA((8,)), DMA,
+            DMA((3,)),
+        ],
     )
     (packed,) = call(
         input_kernel,
@@ -800,7 +825,7 @@
         1000,
         [pltpu.VMEM((2 * BLK, D), BF), pltpu.VMEM((BLK, D), BF), DMA((8,)), DMA],
     )
-    weight_same = exchange(weight_total.reshape(64, 56, 384), (*CHIP, *NARROW)).reshape(8, 8, 56, 384)
+    weight_same = exchange(weight_total.reshape(64, 8, 2432), (*CHIP, *NARROW)).reshape(8, 8, 8, 2432)
     weight_same = after(weight_same, pin(packed))
     everyone = exchange(after(pin(packed), weight_same), NARROW)
     weight_other = swap(weight_same)
@@ -810,7 +835,7 @@
     grads = [((D, 3 * D), F32, "H"), ((D, D), F32, "H")]
     half = call(
         functools.partial(spread_kernel, False),
-        grads + [((8, 384), F32, "V")],
+        grads + [((4, 8, 128), F32, "V")],
         [(weight_same, "V")],
         1000,
         scratch,
@@ -820,7 +845,7 @@
         grads + [((D,), F32, "L")] * 4,
         [(weight_other, "H"), (half[2], "V"), (half[0], "H"), (half[1], "H")],
         1000,
-        [pltpu.VMEM((8, 8, 56, 384), BF), DMA((8,))] + scratch,
+        [pltpu.VMEM((8, 8, 8, 2432), BF), DMA((8,))] + scratch,
         aliases={2: 0, 3: 1},
     )
     ff_parts = [after(value, pin(vectors[0])) for value in ff_parts]

time: 201 us -> 199 us (0.990)
  waiting for transfers between devices: 79 us -> 76.5 us
    all_to_all x7, waiting for transfers between devices: 55.6 us -> 52.6 us  [exchange(): return lax.all_to_all(value, axes, 0, 0, tiled=True)]
  transfers between devices with their start and end apart: 30 -> 30, of which waited for: 13 -> 14; matrix products, arithmetic and copies ran while one was open for 1% -> 1% of each run, Pallas kernels for 15% -> 16%
where the time goes in v18:
time: 199 us; the launch traced here: 198 us
  waiting for transfers between devices  76.5 us (38%)
  starting transfers between devices  69.8 us (35%)
  Pallas kernels  48.9 us (25%)
    all_to_all x7, waiting for transfers between devices, exchange(): return lax.all_to_all(value, axes, 0, 0, tiled=True)  52.6 us
    pallas_call x18, Pallas kernels, call(): pl.pallas_call(kernel, out_shape=[(pltpu.HBM if place in 'HL' else jax.Sh...  48.8 us
    all_to_all x7, starting transfers between devices, exchange(): return lax.all_to_all(value, axes, 0, 0, tiled=True)  39.7 us
    ppermute x13, waiting for transfers between devices, flip(): lax.ppermute(value, axes, [(index, index ^ bits) for index in range(count)])  18.7 us
    ppermute x13, starting transfers between devices, flip(): lax.ppermute(value, axes, [(index, index ^ bits) for index in range(count)])  16.5 us
    ppermute x10, starting transfers between devices, swap(): return lax.ppermute(value, CORE, [(0, 1), (1, 0)])  13.6 us
    ppermute x10, waiting for transfers between devices, swap(): return lax.ppermute(value, CORE, [(0, 1), (1, 0)])  5.22 us
  transfers between devices with their start and end apart: 30, of which 14 were waited for; matrix products, arithmetic and copies ran while one was open for 1% of the time, Pallas kernels for 16%

profile of v18, /device:TPU:1, one launch (start us, length us, event | category | flops | bytes accessed | tf_op | source)
XLA Modules:
  0.0 197.6 jit_solution(15570283936989347021)
XLA Ops:
  0.6 3.7 %shard_map.186 = (bf16[8,128,384]{2,1,0:T(8,128)(2,1)}, bf16[128,768]{1,0:T(8,128)(2,1)}) custom-call(bf16[2,128,768]{2,1,0:T(8,128)(2,1)} %tok_ref.7, f32[768]{0:T(1024)} %gain_ref.7, f32[768]{0:T(1024)} %shift_ref.2, bf16[768,2304]{1,0:T(8,128)(2,1)} %w_ref.7), custom_call_target="tpu_custom_call" | custom-call | flops 1000 | bytes 1000 | tf_op jit(solution)/shard_map/pallas_call | solution.py:106
  4.3 6.0 %all-to-all-start = ((bf16[8,128,384]{2,1,0:T(8,128)(2,1)}), bf16[8,128,384]{2,1,0:T(8,128)(2,1)S(1)}, u32[]{:S(2)}, u32[]{:S(2)}) async-start(bf16[8,128,384]{2,1,0:T(8,128)(2,1)} %get-tuple-element.51), calls=%async_computation | async-start | bytes 1572864 | tf_op jit(solution)/shard_map/all_to_all | solution.py:648
  10.3 3.0 %shard_map.187.refs_1_.q_ref = bf16[128,256]{1,0:T(8,128)(2,1)} custom-call(bf16[128,768]{1,0:T(8,128)(2,1)} %get-tuple-element.52.normed_ref, bf16[768,2304]{1,0:T(8,128)(2,1)} %w_ref.7), custom_call_target="tpu_custom_call" | custom-call | flops 1000 | bytes 1000 | tf_op jit(solution)/shard_map/pallas_call | solution.py:106
  13.4 8.6 %all-to-all-done.refs_0_ = bf16[8,128,384]{2,1,0:T(8,128)(2,1)S(1)} async-done(((bf16[8,128,384]{2,1,0:T(8,128)(2,1)}), bf16[8,128,384]{2,1,0:T(8,128)(2,1)S(1)}, u32[]{:S(2)}, u32[]{:S(2)}) %all-to-all-start) | async-done | bytes 786464 | tf_op jit(solution)/shard_map/all_to_all | solution.py:648
  26.1 3.1 %shard_map.189 = bf16[8,128,256]{2,1,0:T(8,128)(2,1)} custom-call(s32[2,32]{1,0:T(2,128)S(1)} %copy-done.3, bf16[128,256]{1,0:T(8,128)(2,1)} %shard_map.187.refs_1_.q_ref, bf16[8,128,384]{2,1,0:T(8,128)(2,1)S(1)} %shard_map.188.same_ref.refs_0_, bf16[8,128,384]{2,1,0:T(8,128)(2,1)S(1)} %collective-permute-done.other_ref), custom_call_target="tpu_custom_call" | custom-call | flops 1000 | bytes 1000 | tf_op jit(solution)/shard_map/pallas_call | solution.py:106
  29.2 7.2 %all-to-all-start.1 = ((bf16[8,128,256]{2,1,0:T(8,128)(2,1)}), bf16[8,128,256]{2,1,0:T(8,128)(2,1)S(1)}, u32[]{:S(2)}, u32[]{:S(2)}) async-start(bf16[8,128,256]{2,1,0:T(8,128)(2,1)} %shard_map.189), calls=%async_computation.1 | async-start | bytes 1048576 | tf_op jit(solution)/shard_map/all_to_all | solution.py:648
  37.8 9.4 %all-to-all-done.1.mixed_ref = bf16[8,128,256]{2,1,0:T(8,128)(2,1)S(1)} async-done(((bf16[8,128,256]{2,1,0:T(8,128)(2,1)}), bf16[8,128,256]{2,1,0:T(8,128)(2,1)S(1)}, u32[]{:S(2)}, u32[]{:S(2)}) %all-to-all-start.1) | async-done | bytes 524320 | tf_op jit(solution)/shard_map/all_to_all | solution.py:648
  47.1 4.2 %shard_map.190 = (bf16[8,64,768]{2,1,0:T(8,128)(2,1)}, f32[32,768]{1,0:T(8,128)}, bf16[256,768]{1,0:T(8,128)(2,1)S(1)}, bf16[256,384]{1,0:T(8,128)(2,1)S(1)}, bf16[256,384]{1,0:T(8,128)(2,1)S(1)}) custom-call(bf16[8,128,256]{2,1,0:T(8,128)(2,1)S(1)} %all-to-all-done.1.mixed_ref, bf16[2,128,768]{2,1,0:T(8,128)(2,1)} %tok_ref.7, bf16[2,128,768]{2,1,0:T(8,128)(2,1)} %og_ref.5, ...), custom_call_target="tpu_custom_call" | custom-call | flops 1000 | bytes 1000 | tf_op jit(solution)/shard_map/pallas_call | solution.py:106
  51.3 2.8 %shard_map.194 = (bf16[8,48,768]{2,1,0:T(8,128)(2,1)S(1)}, bf16[8,48,768]{2,1,0:T(8,128)(2,1)}) custom-call(bf16[256,768]{1,0:T(8,128)(2,1)S(1)} %get-tuple-element.57.normed_ref, bf16[256,384]{1,0:T(8,128)(2,1)S(1)} %get-tuple-element.58.act_ref, bf16[256,384]{1,0:T(8,128)(2,1)S(1)} %get-tuple-element.59.gpre_ref, bf16[2,128,768]{2,1,0:T(8,128)(2,1)} %og_ref.5), custom_call_target="tpu_custom_call" | custom-call | flops 1000 | bytes 1000 | tf_op jit(solution)/shard_map/pallas_call | solution.py:106
  55.8 3.5 %all-to-all-start.2 = ((bf16[8,64,768]{2,1,0:T(8,128)(2,1)}), bf16[8,64,768]{2,1,0:T(8,128)(2,1)S(1)}, u32[]{:S(2)}, u32[]{:S(2)}) async-start(bf16[8,64,768]{2,1,0:T(8,128)(2,1)} %get-tuple-element.53), calls=%async_computation.2 | async-start | bytes 1572864 | tf_op jit(solution)/shard_map/all_to_all | solution.py:648
  65.2 2.3 %shard_map.191.query_ref = bf16[4,32,256]{2,1,0:T(8,128)(2,1)} custom-call(bf16[128,768]{1,0:T(8,128)(2,1)} %get-tuple-element.52.normed_ref, bf16[768,2304]{1,0:T(8,128)(2,1)} %w_ref.7), custom_call_target="tpu_custom_call" | custom-call | flops 1000 | bytes 1000 | tf_op jit(solution)/shard_map/pallas_call | solution.py:106
  67.5 6.4 %all-to-all-done.2.sums_ref = bf16[8,64,768]{2,1,0:T(8,128)(2,1)S(1)} async-done(((bf16[8,64,768]{2,1,0:T(8,128)(2,1)}), bf16[8,64,768]{2,1,0:T(8,128)(2,1)S(1)}, u32[]{:S(2)}, u32[]{:S(2)}) %all-to-all-start.2) | async-done | bytes 786464 | tf_op jit(solution)/shard_map/all_to_all | solution.py:648
  73.9 3.0 %shard_map.192 = (bf16[8,4,32,512]{3,2,1,0:T(8,128)(2,1)}, bf16[32,768]{1,0:T(8,128)(2,1)}, f32[32,768]{1,0:T(8,128)}, bf16[32,768]{1,0:T(8,128)(2,1)}, f32[8,768]{1,0:T(8,128)}) custom-call(bf16[8,64,768]{2,1,0:T(8,128)(2,1)S(1)} %all-to-all-done.2.sums_ref, f32[32,768]{1,0:T(8,128)} %get-tuple-element.54.middle_ref, bf16[2,128,768]{2,1,0:T(8,128)(2,1)} %og_ref.5, ...), custom_call_target="tpu_custom_call" | custom-call | flops 1000 | bytes 1000 | tf_op jit(solution)/shard_map/pallas_call | solution.py:106
  76.9 3.9 %all-to-all-start.3 = ((bf16[32,32,512]{2,1,0:T(8,128)(2,1)}), bf16[32,32,512]{2,1,0:T(8,128)(2,1)S(1)}, u32[]{:S(2)}, u32[]{:S(2)}) async-start(bf16[32,32,512]{2,1,0:T(8,128)(2,1)} %bitcast.8), calls=%async_computation.3 | async-start | bytes 2097152 | tf_op jit(solution)/shard_map/all_to_all | solution.py:648
  81.7 2.9 %collective-permute-start.6 = (bf16[32,768]{1,0:T(8,128)(2,1)S(1)}, bf16[32,768]{1,0:T(8,128)(2,1)S(1)}, u32[]{:S(2)}, u32[]{:S(2)}) collective-permute-start(bf16[32,768]{1,0:T(8,128)(2,1)S(1)} %copy-done.2), channel_id=1, source_target_pairs={{0,1},{1,0},{2,3},{3,2},{4,5},{5,4},{6,7},{7,6},{8,9},{9,8},{10,11... | collective-permute-start | bytes 147464 | tf_op jit(solution)/shard_map/ppermute | solution.py:668
  87.6 8.3 %collective-permute-done.6.refs_1_.low1_ref = bf16[32,768]{1,0:T(8,128)(2,1)S(1)} collective-permute-done((bf16[32,768]{1,0:T(8,128)(2,1)S(1)}, bf16[32,768]{1,0:T(8,128)(2,1)S(1)}, u32[]{:S(2)}, u32[]{:S(2)}) %collective-permute-start.6) | collective-permute-done | bytes 49184 | tf_op jit(solution)/shard_map/ppermute | solution.py:668
  95.8 2.5 %collective-permute-done.8.refs_3_.low3_ref = bf16[32,768]{1,0:T(8,128)(2,1)S(1)} collective-permute-done((bf16[32,768]{1,0:T(8,128)(2,1)S(1)}, bf16[32,768]{1,0:T(8,128)(2,1)S(1)}, u32[]{:S(2)}, u32[]{:S(2)}) %collective-permute-start.8) | collective-permute-done | bytes 49184 | tf_op jit(solution)/shard_map/ppermute | solution.py:668
  100.2 2.3 %collective-permute-done.9.go_ref.refs_1_ = bf16[8,128,512]{2,1,0:T(8,128)(2,1)S(1)} collective-permute-done((bf16[8,128,512]{2,1,0:T(8,128)(2,1)S(1)}, bf16[8,128,512]{2,1,0:T(8,128)(2,1)S(1)}, u32[]{:S(2)}, u32[]{:S(2)}) %collective-permute-start.9) | collective-permute-done | bytes 1048608 | tf_op jit(solution)/shard_map/ppermute | solution.py:652
  102.8 4.3 %shard_map.199 = (bf16[128,640]{1,0:T(8,128)(2,1)S(1)}, bf16[3,768,384]{2,1,0:T(8,128)(2,1)S(1)}, bf16[16,48,384]{2,1,0:T(8,128)(2,1)S(1)}, bf16[16,48,384]{2,1,0:T(8,128)(2,1)S(1)}) custom-call(s32[2,32]{1,0:T(2,128)S(1)} %copy-done.3, bf16[8,128,384]{2,1,0:T(8,128)(2,1)} %shard_map.193.kvs_ref, ...), custom_call_target="tpu_custom_call" | custom-call | flops 1000 | bytes 1000 | tf_op jit(solution)/shard_map/pallas_call | solution.py:106
  109.0 2.6 %shard_map.201 = (f32[32,768]{1,0:T(8,128)}, bf16[48,768]{1,0:T(8,128)(2,1)}, bf16[48,768]{1,0:T(8,128)(2,1)}, bf16[48,768]{1,0:T(8,128)(2,1)}, f32[8,768]{1,0:T(8,128)}, /*index=5*/bf16[2,48,768]{2,1,0:T(8,128)(2,1)}) custom-call(bf16[128,640]{1,0:T(8,128)(2,1)S(1)} %get-tuple-element.66.gqkv_ref, bf16[3,768,384]{2,1,0:T(8,128)(2,1)S(1)} %get-tuple-element.67.w_ref, ...), custom_call_target="tpu_custom_call" | custom-call | flops 1000 | bytes 1000 | tf_op jit(solution)/shard_map/pallas_call | solution.py:106
  112.6 5.9 %all-to-all-start.4 = ((bf16[16,48,384]{2,1,0:T(8,128)(2,1)}), bf16[16,48,384]{2,1,0:T(8,128)(2,1)S(1)}, u32[]{:S(2)}, u32[]{:S(2)}) async-start(bf16[16,48,384]{2,1,0:T(8,128)(2,1)} %shard_map.203), calls=%async_computation.4 | async-start | bytes 1179648 | tf_op jit(solution)/shard_map/all_to_all | solution.py:648
  119.5 3.4 %collective-permute-start.13 = (bf16[48,768]{1,0:T(8,128)(2,1)S(1)}, bf16[48,768]{1,0:T(8,128)(2,1)S(1)}, u32[]{:S(2)}, u32[]{:S(2)}) collective-permute-start(bf16[48,768]{1,0:T(8,128)(2,1)S(1)} %copy-done.5), channel_id=1, source_target_pairs={{0,3},{1,2},{2,1},{3,0},{4,7},{5,6},{6,5},{7,4},{8,11},{9,10},{10,... | collective-permute-start | bytes 221192 | tf_op jit(solution)/shard_map/ppermute | solution.py:668
  122.8 5.4 %collective-permute-done.11.refs_2_.one_ref = bf16[48,768]{1,0:T(8,128)(2,1)S(1)} collective-permute-done((bf16[48,768]{1,0:T(8,128)(2,1)S(1)}, bf16[48,768]{1,0:T(8,128)(2,1)S(1)}, u32[]{:S(2)}, u32[]{:S(2)}) %collective-permute-start.11) | collective-permute-done | bytes 73760 | tf_op jit(solution)/shard_map/ppermute | solution.py:668
  130.1 2.3 %shard_map.205.unused_ref = bf16[8,8,8,2432]{3,2,1,0:T(8,128)(2,1)} custom-call(bf16[16,48,384]{2,1,0:T(8,128)(2,1)S(1)} %shard_map.204.in_ref, f32[8,768]{1,0:T(8,128)} %get-tuple-element.77.refs_1_.vec_ref, bf16[48,768]{1,0:T(8,128)(2,1)S(1)} %collective-permute-done.11.refs_2_.one_ref, bf16[48,768]{1,0:T(8,128)(2,1)S(1)} %collective-permute-done.12.refs_3_.two_ref, ...), custom_call_target="tpu_custom_call" | custom-call | flops 1000 | bytes 1000 | tf_op jit(solution)/shard_map/pallas_call | solution.py:106
  132.4 9.5 %all-to-all-start.5 = ((bf16[64,8,2432]{2,1,0:T(8,128)(2,1)}), bf16[64,8,2432]{2,1,0:T(8,128)(2,1)S(1)}, u32[]{:S(2)}, u32[]{:S(2)}) async-start(bf16[64,8,2432]{2,1,0:T(8,128)(2,1)} %bitcast.7), calls=%async_computation.5 | async-start | bytes 4980736 | tf_op jit(solution)/shard_map/all_to_all | solution.py:648
  142.0 3.0 %shard_map.206.refs_1_.refs_0_ = bf16[8,64,768]{2,1,0:T(8,128)(2,1)} custom-call(f32[32,768]{1,0:T(8,128)} %get-tuple-element.69.unused_ref.own_ref, bf16[48,768]{1,0:T(8,128)(2,1)S(1)} %collective-permute-done.11.refs_2_.one_ref, bf16[48,768]{1,0:T(8,128)(2,1)S(1)} %collective-permute-done.12.refs_3_.two_ref, ...), custom_call_target="tpu_custom_call" | custom-call | flops 1000 | bytes 1000 | tf_op jit(solution)/shard_map/pallas_call | solution.py:106
  145.0 28.2 %all-to-all-done.5 = bf16[64,8,2432]{2,1,0:T(8,128)(2,1)S(1)} async-done(((bf16[64,8,2432]{2,1,0:T(8,128)(2,1)}), bf16[64,8,2432]{2,1,0:T(8,128)(2,1)S(1)}, u32[]{:S(2)}, u32[]{:S(2)}) %all-to-all-start.5) | async-done | bytes 2490400 | tf_op jit(solution)/shard_map/all_to_all | solution.py:648
  173.2 3.4 %collective-permute-start.15 = (bf16[8,8,8,2432]{3,2,1,0:T(8,128)(2,1)S(1)}, bf16[8,8,8,2432]{3,2,1,0:T(8,128)(2,1)}, u32[]{:S(2)}, u32[]{:S(2)}) collective-permute-start(bf16[8,8,8,2432]{3,2,1,0:T(8,128)(2,1)S(1)} %shard_map.207.refs_1_.in_ref), channel_id=1, source_target_pairs={{0,8},{8,0},{1,9},{9,1},{2,10},{10,2},{3,11},{11,3},{4,12},{12,4},... | collective-permute-start | bytes 7471112 | tf_op jit(solution)/shard_map/ppermute | solution.py:652
  176.5 3.6 %all-to-all-start.6 = ((bf16[8,64,768]{2,1,0:T(8,128)(2,1)}), bf16[8,64,768]{2,1,0:T(8,128)(2,1)S(1)}, u32[]{:S(2)}, u32[]{:S(2)}) async-start(bf16[8,64,768]{2,1,0:T(8,128)(2,1)} %shard_map.208), calls=%async_computation.6 | async-start | bytes 1572864 | tf_op jit(solution)/shard_map/all_to_all | solution.py:648
  185.4 2.4 %shard_map.209 = (f32[768,2304]{1,0:T(8,128)}, f32[768,768]{1,0:T(8,128)}, f32[4,8,128]{2,1,0:T(8,128)S(1)}) custom-call(bf16[8,8,8,2432]{3,2,1,0:T(8,128)(2,1)S(1)} %shard_map.207.refs_1_.in_ref), custom_call_target="tpu_custom_call" | custom-call | flops 1000 | bytes 1000 | tf_op jit(solution)/shard_map/pallas_call | solution.py:106
  187.8 4.1 %shard_map.210 = (f32[768,2304]{1,0:T(8,128)}, f32[768,768]{1,0:T(8,128)}, f32[768]{0:T(1024)}, f32[768]{0:T(1024)}, f32[768]{0:T(1024)}, /*index=5*/f32[768]{0:T(1024)}) custom-call(bf16[8,8,8,2432]{3,2,1,0:T(8,128)(2,1)} %collective-permute-done.15.in_ref, ...), custom_call_target="tpu_custom_call", output_to_operand_aliasing={{0}: (2, {}), {1}: (3, {})} | custom-call | flops 1000 | bytes 1000 | tf_op jit(solution)/shard_map/pallas_call | solution.py:106
  194.0 2.5 %shard_map.214 = (f32[768,384]{1,0:T(8,128)}, f32[384,768]{1,0:T(8,128)}) custom-call(bf16[2,48,768]{2,1,0:T(8,128)(2,1)} %get-tuple-element.82.refs_0_, bf16[2,48,768]{2,1,0:T(8,128)(2,1)S(1)} %shard_map.211.refs_1_, bf16[2,48,768]{2,1,0:T(8,128)(2,1)S(1)} %shard_map.212.refs_2_, bf16[2,48,768]{2,1,0:T(8,128)(2,1)S(1)} %shard_map.213.refs_3_, ...), custom_call_target="tpu_custom_call" | custom-call | flops 1000 | bytes 1000 | tf_op jit(solution)/shard_map/pallas_call | solution.py:106
  (75 shorter events, 33.0 us)
Async XLA Ops:
  4.3 17.6 %all-to-all-start = ((bf16[8,128,384]{2,1,0:T(8,128)(2,1)}), bf16[8,128,384]{2,1,0:T(8,128)(2,1)S(1)}, u32[]{:S(2)}, u32[]{:S(2)}) async-start(bf16[8,128,384]{2,1,0:T(8,128)(2,1)} %get-tuple-element.51), calls=%async_computation | async-start | bytes 1572864 | tf_op jit(solution)/shard_map/all_to_all | solution.py:648
  10.3 15.8 %copy-start.3 = (s32[2,32]{1,0:T(2,128)S(1)}, s32[2,32]{1,0:T(2,128)}, u32[]{:S(2)}) copy-start(s32[2,32]{1,0:T(2,128)} %scene_ref.3) | copy-start | bytes 772
  22.0 15.8 %copy-start = (bf16[8,128,384]{2,1,0:T(8,128)(2,1)}, bf16[8,128,384]{2,1,0:T(8,128)(2,1)S(1)}, u32[]{:S(2)}) copy-start(bf16[8,128,384]{2,1,0:T(8,128)(2,1)S(1)} %shard_map.188.same_ref.refs_0_) | copy-start | bytes 2359300
  22.0 4.1 %collective-permute-start = (bf16[8,128,384]{2,1,0:T(8,128)(2,1)S(1)}, bf16[8,128,384]{2,1,0:T(8,128)(2,1)S(1)}, u32[]{:S(2)}, u32[]{:S(2)}) collective-permute-start(bf16[8,128,384]{2,1,0:T(8,128)(2,1)S(1)} %shard_map.188.same_ref.refs_0_), channel_id=1, source_target_pairs={{0,8},{8,0},{1,9},{9,1},{2,10},{10,2},{3,11},{11,3},{4,12},{12,4},... | collective-permute-start | bytes 2359304 | tf_op jit(solution)/shard_map/ppermute | solution.py:652
  29.2 18.0 %all-to-all-start.1 = ((bf16[8,128,256]{2,1,0:T(8,128)(2,1)}), bf16[8,128,256]{2,1,0:T(8,128)(2,1)S(1)}, u32[]{:S(2)}, u32[]{:S(2)}) async-start(bf16[8,128,256]{2,1,0:T(8,128)(2,1)} %shard_map.189), calls=%async_computation.1 | async-start | bytes 1048576 | tf_op jit(solution)/shard_map/all_to_all | solution.py:648
  54.1 5.3 %collective-permute-start.2 = (bf16[8,48,768]{2,1,0:T(8,128)(2,1)}, bf16[8,48,768]{2,1,0:T(8,128)(2,1)}, u32[]{:S(2)}, u32[]{:S(2)}) collective-permute-start(bf16[8,48,768]{2,1,0:T(8,128)(2,1)} %get-tuple-element.61), channel_id=1, source_target_pairs={{0,8},{8,0},{1,9},{9,1},{2,10},{10,2},{3,11},{11,3},{4,12},{12,4},... | collective-permute-start | bytes 1769480 | tf_op jit(solution)/shard_map/ppermute | solution.py:652
  55.8 18.1 %all-to-all-start.2 = ((bf16[8,64,768]{2,1,0:T(8,128)(2,1)}), bf16[8,64,768]{2,1,0:T(8,128)(2,1)S(1)}, u32[]{:S(2)}, u32[]{:S(2)}) async-start(bf16[8,64,768]{2,1,0:T(8,128)(2,1)} %get-tuple-element.53), calls=%async_computation.2 | async-start | bytes 1572864 | tf_op jit(solution)/shard_map/all_to_all | solution.py:648
  61.3 15.6 %collective-permute-start.3 = (bf16[2,48,768]{2,1,0:T(8,128)(2,1)}, bf16[2,48,768]{2,1,0:T(8,128)(2,1)S(1)}, u32[]{:S(2)}, u32[]{:S(2)}) collective-permute-start(bf16[2,48,768]{2,1,0:T(8,128)(2,1)} %get-tuple-element.62), channel_id=1, source_target_pairs={{0,32},{32,0},{64,96},{96,64},{1,33},{33,1},{65,97},{97,65},{2,34}... | collective-permute-start | bytes 442376 | tf_op jit(solution)/shard_map/ppermute | solution.py:668
  61.9 15.0 %collective-permute-start.4 = (bf16[2,48,768]{2,1,0:T(8,128)(2,1)}, bf16[2,48,768]{2,1,0:T(8,128)(2,1)S(1)}, u32[]{:S(2)}, u32[]{:S(2)}) collective-permute-start(bf16[2,48,768]{2,1,0:T(8,128)(2,1)} %get-tuple-element.63), channel_id=1, source_target_pairs={{0,64},{32,96},{64,0},{96,32},{1,65},{33,97},{65,1},{97,33},{2,66}... | collective-permute-start | bytes 442376 | tf_op jit(solution)/shard_map/ppermute | solution.py:668
  63.9 12.9 %collective-permute-start.5 = (bf16[2,48,768]{2,1,0:T(8,128)(2,1)}, bf16[2,48,768]{2,1,0:T(8,128)(2,1)S(1)}, u32[]{:S(2)}, u32[]{:S(2)}) collective-permute-start(bf16[2,48,768]{2,1,0:T(8,128)(2,1)} %get-tuple-element.64), channel_id=1, source_target_pairs={{0,96},{32,64},{64,32},{96,0},{1,97},{33,65},{65,33},{97,1},{2,98}... | collective-permute-start | bytes 442376 | tf_op jit(solution)/shard_map/ppermute | solution.py:668
  76.9 21.4 %all-to-all-start.3 = ((bf16[32,32,512]{2,1,0:T(8,128)(2,1)}), bf16[32,32,512]{2,1,0:T(8,128)(2,1)S(1)}, u32[]{:S(2)}, u32[]{:S(2)}) async-start(bf16[32,32,512]{2,1,0:T(8,128)(2,1)} %bitcast.8), calls=%async_computation.3 | async-start | bytes 2097152 | tf_op jit(solution)/shard_map/all_to_all | solution.py:648
  80.9 17.4 %collective-permute-start.1 = (bf16[8,128,384]{2,1,0:T(8,128)(2,1)}, bf16[8,128,384]{2,1,0:T(8,128)(2,1)S(1)}, u32[]{:S(2)}, u32[]{:S(2)}) collective-permute-start(bf16[8,128,384]{2,1,0:T(8,128)(2,1)} %shard_map.193.kvs_ref), channel_id=1, source_target_pairs={{0,8},{8,0},{1,9},{9,1},{2,10},{10,2},{3,11},{11,3},{4,12},{12,4},... | collective-permute-start | bytes 2359304 | tf_op jit(solution)/shard_map/ppermute | solution.py:652
  81.7 14.1 %collective-permute-start.6 = (bf16[32,768]{1,0:T(8,128)(2,1)S(1)}, bf16[32,768]{1,0:T(8,128)(2,1)S(1)}, u32[]{:S(2)}, u32[]{:S(2)}) collective-permute-start(bf16[32,768]{1,0:T(8,128)(2,1)S(1)} %copy-done.2), channel_id=1, source_target_pairs={{0,1},{1,0},{2,3},{3,2},{4,5},{5,4},{6,7},{7,6},{8,9},{9,8},{10,11... | collective-permute-start | bytes 147464 | tf_op jit(solution)/shard_map/ppermute | solution.py:668
  84.7 11.2 %collective-permute-start.7 = (bf16[32,768]{1,0:T(8,128)(2,1)S(1)}, bf16[32,768]{1,0:T(8,128)(2,1)S(1)}, u32[]{:S(2)}, u32[]{:S(2)}) collective-permute-start(bf16[32,768]{1,0:T(8,128)(2,1)S(1)} %copy-done.2), channel_id=1, source_target_pairs={{0,2},{1,3},{2,0},{3,1},{4,6},{5,7},{6,4},{7,5},{8,10},{9,11},{10,... | collective-permute-start | bytes 147464 | tf_op jit(solution)/shard_map/ppermute | solution.py:668
  85.9 12.4 %collective-permute-start.8 = (bf16[32,768]{1,0:T(8,128)(2,1)S(1)}, bf16[32,768]{1,0:T(8,128)(2,1)S(1)}, u32[]{:S(2)}, u32[]{:S(2)}) collective-permute-start(bf16[32,768]{1,0:T(8,128)(2,1)S(1)} %copy-done.2), channel_id=1, source_target_pairs={{0,3},{1,2},{2,1},{3,0},{4,7},{5,6},{6,5},{7,4},{8,11},{9,10},{10,... | collective-permute-start | bytes 147464 | tf_op jit(solution)/shard_map/ppermute | solution.py:668
  98.3 4.2 %collective-permute-start.9 = (bf16[8,128,512]{2,1,0:T(8,128)(2,1)S(1)}, bf16[8,128,512]{2,1,0:T(8,128)(2,1)S(1)}, u32[]{:S(2)}, u32[]{:S(2)}) collective-permute-start(bf16[8,128,512]{2,1,0:T(8,128)(2,1)S(1)} %shard_map.198.gs_ref), channel_id=1, source_target_pairs={{0,8},{8,0},{1,9},{9,1},{2,10},{10,2},{3,11},{11,3},{4,12},{12,4},... | collective-permute-start | bytes 3145736 | tf_op jit(solution)/shard_map/ppermute | solution.py:652
  102.5 5.3 %collective-permute-start.10 = (bf16[2,48,768]{2,1,0:T(8,128)(2,1)}, bf16[2,48,768]{2,1,0:T(8,128)(2,1)S(1)}, u32[]{:S(2)}, u32[]{:S(2)}) collective-permute-start(bf16[2,48,768]{2,1,0:T(8,128)(2,1)} %shard_map.200.near_ref), channel_id=1, source_target_pairs={{0,16},{16,0},{1,17},{17,1},{2,18},{18,2},{3,19},{19,3},{4,20},{20... | collective-permute-start | bytes 442376 | tf_op jit(solution)/shard_map/ppermute | solution.py:668
  107.8 3.9 %collective-permute-start.14 = (bf16[16,48,384]{2,1,0:T(8,128)(2,1)S(1)}, bf16[16,48,384]{2,1,0:T(8,128)(2,1)S(1)}, u32[]{:S(2)}, u32[]{:S(2)}) collective-permute-start(bf16[16,48,384]{2,1,0:T(8,128)(2,1)S(1)} %shard_map.202), channel_id=1, source_target_pairs={{0,8},{8,0},{1,9},{9,1},{2,10},{10,2},{3,11},{11,3},{4,12},{12,4},... | collective-permute-start | bytes 1769480 | tf_op jit(solution)/shard_map/ppermute | solution.py:652
  112.6 17.5 %all-to-all-start.4 = ((bf16[16,48,384]{2,1,0:T(8,128)(2,1)}), bf16[16,48,384]{2,1,0:T(8,128)(2,1)S(1)}, u32[]{:S(2)}, u32[]{:S(2)}) async-start(bf16[16,48,384]{2,1,0:T(8,128)(2,1)} %shard_map.203), calls=%async_computation.4 | async-start | bytes 1179648 | tf_op jit(solution)/shard_map/all_to_all | solution.py:648
  118.6 9.6 %collective-permute-start.11 = (bf16[48,768]{1,0:T(8,128)(2,1)S(1)}, bf16[48,768]{1,0:T(8,128)(2,1)S(1)}, u32[]{:S(2)}, u32[]{:S(2)}) collective-permute-start(bf16[48,768]{1,0:T(8,128)(2,1)S(1)} %copy-done.7), channel_id=1, source_target_pairs={{0,1},{1,0},{2,3},{3,2},{4,5},{5,4},{6,7},{7,6},{8,9},{9,8},{10,11... | collective-permute-start | bytes 221192 | tf_op jit(solution)/shard_map/ppermute | solution.py:668
  119.4 8.8 %collective-permute-start.12 = (bf16[48,768]{1,0:T(8,128)(2,1)S(1)}, bf16[48,768]{1,0:T(8,128)(2,1)S(1)}, u32[]{:S(2)}, u32[]{:S(2)}) collective-permute-start(bf16[48,768]{1,0:T(8,128)(2,1)S(1)} %copy-done.6), channel_id=1, source_target_pairs={{0,2},{1,3},{2,0},{3,1},{4,6},{5,7},{6,4},{7,5},{8,10},{9,11},{10,... | collective-permute-start | bytes 221192 | tf_op jit(solution)/shard_map/ppermute | solution.py:668
  119.5 10.7 %collective-permute-start.13 = (bf16[48,768]{1,0:T(8,128)(2,1)S(1)}, bf16[48,768]{1,0:T(8,128)(2,1)S(1)}, u32[]{:S(2)}, u32[]{:S(2)}) collective-permute-start(bf16[48,768]{1,0:T(8,128)(2,1)S(1)} %copy-done.5), channel_id=1, source_target_pairs={{0,3},{1,2},{2,1},{3,0},{4,7},{5,6},{6,5},{7,4},{8,11},{9,10},{10,... | collective-permute-start | bytes 221192 | tf_op jit(solution)/shard_map/ppermute | solution.py:668
  132.4 40.7 %all-to-all-start.5 = ((bf16[64,8,2432]{2,1,0:T(8,128)(2,1)}), bf16[64,8,2432]{2,1,0:T(8,128)(2,1)S(1)}, u32[]{:S(2)}, u32[]{:S(2)}) async-start(bf16[64,8,2432]{2,1,0:T(8,128)(2,1)} %bitcast.7), calls=%async_computation.5 | async-start | bytes 4980736 | tf_op jit(solution)/shard_map/all_to_all | solution.py:648
  173.2 14.6 %collective-permute-start.15 = (bf16[8,8,8,2432]{3,2,1,0:T(8,128)(2,1)S(1)}, bf16[8,8,8,2432]{3,2,1,0:T(8,128)(2,1)}, u32[]{:S(2)}, u32[]{:S(2)}) collective-permute-start(bf16[8,8,8,2432]{3,2,1,0:T(8,128)(2,1)S(1)} %shard_map.207.refs_1_.in_ref), channel_id=1, source_target_pairs={{0,8},{8,0},{1,9},{9,1},{2,10},{10,2},{3,11},{11,3},{4,12},{12,4},... | collective-permute-start | bytes 7471112 | tf_op jit(solution)/shard_map/ppermute | solution.py:652
  176.5 20.0 %all-to-all-start.6 = ((bf16[8,64,768]{2,1,0:T(8,128)(2,1)}), bf16[8,64,768]{2,1,0:T(8,128)(2,1)S(1)}, u32[]{:S(2)}, u32[]{:S(2)}) async-start(bf16[8,64,768]{2,1,0:T(8,128)(2,1)} %shard_map.208), calls=%async_computation.6 | async-start | bytes 1572864 | tf_op jit(solution)/shard_map/all_to_all | solution.py:648
  180.1 11.7 %collective-permute-start.16 = (bf16[2,48,768]{2,1,0:T(8,128)(2,1)S(1)}, bf16[2,48,768]{2,1,0:T(8,128)(2,1)S(1)}, u32[]{:S(2)}, u32[]{:S(2)}) collective-permute-start(bf16[2,48,768]{2,1,0:T(8,128)(2,1)S(1)} %copy-done.4), channel_id=1, source_target_pairs={{0,32},{32,0},{64,96},{96,64},{1,33},{33,1},{65,97},{97,65},{2,34}... | collective-permute-start | bytes 442376 | tf_op jit(solution)/shard_map/ppermute | solution.py:668
  180.6 11.4 %collective-permute-start.17 = (bf16[2,48,768]{2,1,0:T(8,128)(2,1)S(1)}, bf16[2,48,768]{2,1,0:T(8,128)(2,1)S(1)}, u32[]{:S(2)}, u32[]{:S(2)}) collective-permute-start(bf16[2,48,768]{2,1,0:T(8,128)(2,1)S(1)} %copy-done.4), channel_id=1, source_target_pairs={{0,64},{32,96},{64,0},{96,32},{1,65},{33,97},{65,1},{97,33},{2,66}... | collective-permute-start | bytes 442376 | tf_op jit(solution)/shard_map/ppermute | solution.py:668
  182.4 10.1 %collective-permute-start.18 = (bf16[2,48,768]{2,1,0:T(8,128)(2,1)S(1)}, bf16[2,48,768]{2,1,0:T(8,128)(2,1)S(1)}, u32[]{:S(2)}, u32[]{:S(2)}) collective-permute-start(bf16[2,48,768]{2,1,0:T(8,128)(2,1)S(1)} %copy-done.4), channel_id=1, source_target_pairs={{0,96},{32,64},{64,32},{96,0},{1,97},{33,65},{65,33},{97,1},{2,98}... | collective-permute-start | bytes 442376 | tf_op jit(solution)/shard_map/ppermute | solution.py:668
  184.1 8.9 %collective-permute-start.19 = (bf16[2,48,768]{2,1,0:T(8,128)(2,1)S(1)}, bf16[2,48,768]{2,1,0:T(8,128)(2,1)S(1)}, u32[]{:S(2)}, u32[]{:S(2)}) collective-permute-start(bf16[2,48,768]{2,1,0:T(8,128)(2,1)S(1)} %copy-done.4), channel_id=1, source_target_pairs={{0,8},{8,0},{1,9},{9,1},{2,10},{10,2},{3,11},{11,3},{4,12},{12,4},... | collective-permute-start | bytes 442376 | tf_op jit(solution)/shard_map/ppermute | solution.py:652
  191.9 1.5 collective-permute-start.20
  192.0 1.5 collective-permute-start.21
  192.5 1.5 collective-permute-start.22
  (6 other events, 40.5 us)

commit v19 on v18

--- a/solution.py
+++ b/solution.py
@@ -597,26 +597,26 @@
     wait_all(copies)
 
 
-def spread_ff_kernel(*refs):
-    up_ref, down_ref, up_buf, down_buf, up_sem, down_sem = refs[8:]
+def spread_ff_kernel(turn, *refs):
+    up_ref, down_ref, up_buf, down_buf, up_sem, down_sem = refs[-6:]
     y, core = lax.axis_index("y"), lax.axis_index(CORE)
+    owner = 1 - core if turn else core
     copies = []
     for near in range(4):
         for xl in range(2):
             chip = (y ^ near) * 2 + xl
-            for index in (near, near + 4):
-                owner = core ^ (index // 4)
-                block = refs[index][xl].astype(F32)
-                up_buf[near, xl, pl.ds(pl.multiple_of(owner * 48, 16), 48)] = block[:, :384]
-                down_buf[near, xl, :, pl.ds(pl.multiple_of(owner * 384, 128), 384)] = block[:, 384:]
-            for source, target, rows, sem in ((up_buf, up_ref, 96, up_sem), (down_buf, down_ref, 48, down_sem)):
-                copy = pltpu.make_async_copy(
-                    source.at[near, xl],
-                    target.at[pl.ds(pl.multiple_of(chip * rows, 16), rows)],
-                    sem.at[near, xl],
-                )
-                copy.start()
-                copies.append(copy)
+            block = refs[near][xl].astype(F32)
+            up_buf[near, xl] = block[:, :384]
+            down_buf[near, xl] = block[:, 384:]
+            up_rows = pl.ds(pl.multiple_of((chip * 2 + owner) * 48, 16), 48)
+            down_rows = pl.ds(pl.multiple_of(chip * 48, 16), 48)
+            columns = pl.ds(pl.multiple_of(owner * 384, 128), 384)
+            copies.append(pltpu.make_async_copy(up_buf.at[near, xl], up_ref.at[up_rows], up_sem.at[near, xl]))
+            copies.append(
+                pltpu.make_async_copy(down_buf.at[near, xl], down_ref.at[down_rows, columns], down_sem.at[near, xl])
+            )
+            copies[-2].start()
+            copies[-1].start()
     wait_all(copies)
 
 
@@ -850,12 +850,24 @@
     )
     ff_parts = [after(value, pin(vectors[0])) for value in ff_parts]
     ff_swapped = [swap(value) for value in (ff_part, *ff_parts)]
+    ff_grads = [((D, FFL), F32, "H"), ((FFL, D), F32, "H")]
+    ff_scratch = [
+        pltpu.VMEM((4, 2, 48, FFL), F32), pltpu.VMEM((4, 2, 48, FFL), F32), DMA((4, 2)), DMA((4, 2)),
+    ]
+    ff_half = call(
+        functools.partial(spread_ff_kernel, False),
+        ff_grads,
+        [(ff_part, "L"), *[(value, "V") for value in ff_parts]],
+        1000,
+        ff_scratch,
+    )
     up_grad, down_grad = call(
-        spread_ff_kernel,
-        [((D, FFL), F32, "H"), ((FFL, D), F32, "H")],
-        [(ff_part, "L"), *[(value, "V") for value in ff_parts], *[(value, "V") for value in ff_swapped]],
-        1000,
-        [pltpu.VMEM((4, 2, 96, FFL), F32), pltpu.VMEM((4, 2, 48, D), F32), DMA((4, 2)), DMA((4, 2))],
+        functools.partial(spread_ff_kernel, True),
+        ff_grads,
+        [*[(value, "V") for value in ff_swapped], (ff_half[0], "H"), (ff_half[1], "H")],
+        1000,
+        ff_scratch,
+        aliases={4: 0, 5: 1},
     )
     input_grad, result = call(
         unpack_kernel, [((2, TOK, D), F32, "L"), ((2, TOK, D), BF, "L")], [(everyone, "V"), (vectors[0], "H"), (up_grad, "H")], 1000

time: 199 us -> 199 us (level)
  Pallas kernels: 48.9 us -> 51.7 us
    pallas_call x18 -> x19, Pallas kernels: 48.8 us -> 51.7 us  [call(): pl.pallas_call(kernel, out_shape=[(pltpu.HBM if place in 'HL' else jax.Sh...]
  transfers between devices with their start and end apart: 30 -> 30, of which waited for: 14 -> 10; matrix products, arithmetic and copies ran while one was open for 1% -> 1% of each run, Pallas kernels for 16% -> 17%
where the time goes in v19:
time: 199 us; the launch traced here: 197 us
  waiting for transfers between devices  74.9 us (38%)
  starting transfers between devices  68.4 us (34%)
  Pallas kernels  51.7 us (26%)
    all_to_all x7, waiting for transfers between devices, exchange(): return lax.all_to_all(value, axes, 0, 0, tiled=True)  52.6 us
    pallas_call x19, Pallas kernels, call(): pl.pallas_call(kernel, out_shape=[(pltpu.HBM if place in 'HL' else jax.Sh...  51.7 us
    all_to_all x7, starting transfers between devices, exchange(): return lax.all_to_all(value, axes, 0, 0, tiled=True)  38.8 us
    ppermute x13, waiting for transfers between devices, flip(): lax.ppermute(value, axes, [(index, index ^ bits) for index in range(count)])  18.1 us
    ppermute x13, starting transfers between devices, flip(): lax.ppermute(value, axes, [(index, index ^ bits) for index in range(count)])  16.5 us
    ppermute x10, starting transfers between devices, swap(): return lax.ppermute(value, CORE, [(0, 1), (1, 0)])  13.1 us
    ppermute x10, waiting for transfers between devices, swap(): return lax.ppermute(value, CORE, [(0, 1), (1, 0)])  4.22 us
  transfers between devices with their start and end apart: 30, of which 10 were waited for; matrix products, arithmetic and copies ran while one was open for 1% of the time, Pallas kernels for 17%

profile of v19, /device:TPU:1, one launch (start us, length us, event | category | flops | bytes accessed | tf_op | source)
XLA Modules:
  0.0 197.4 jit_solution(5343362547657401835)
XLA Ops:
  0.6 3.7 %shard_map.186 = (bf16[8,128,384]{2,1,0:T(8,128)(2,1)}, bf16[128,768]{1,0:T(8,128)(2,1)}) custom-call(bf16[2,128,768]{2,1,0:T(8,128)(2,1)} %tok_ref.7, f32[768]{0:T(1024)} %gain_ref.7, f32[768]{0:T(1024)} %shift_ref.2, bf16[768,2304]{1,0:T(8,128)(2,1)} %w_ref.7), custom_call_target="tpu_custom_call" | custom-call | flops 1000 | bytes 1000 | tf_op jit(solution)/shard_map/pallas_call | solution.py:106
  4.3 6.0 %all-to-all-start = ((bf16[8,128,384]{2,1,0:T(8,128)(2,1)}), bf16[8,128,384]{2,1,0:T(8,128)(2,1)S(1)}, u32[]{:S(2)}, u32[]{:S(2)}) async-start(bf16[8,128,384]{2,1,0:T(8,128)(2,1)} %get-tuple-element.53), calls=%async_computation | async-start | bytes 1572864 | tf_op jit(solution)/shard_map/all_to_all | solution.py:648
  10.3 3.0 %shard_map.187.refs_1_.q_ref = bf16[128,256]{1,0:T(8,128)(2,1)} custom-call(bf16[128,768]{1,0:T(8,128)(2,1)} %get-tuple-element.54.normed_ref, bf16[768,2304]{1,0:T(8,128)(2,1)} %w_ref.7), custom_call_target="tpu_custom_call" | custom-call | flops 1000 | bytes 1000 | tf_op jit(solution)/shard_map/pallas_call | solution.py:106
  13.4 8.6 %all-to-all-done.refs_0_ = bf16[8,128,384]{2,1,0:T(8,128)(2,1)S(1)} async-done(((bf16[8,128,384]{2,1,0:T(8,128)(2,1)}), bf16[8,128,384]{2,1,0:T(8,128)(2,1)S(1)}, u32[]{:S(2)}, u32[]{:S(2)}) %all-to-all-start) | async-done | bytes 786464 | tf_op jit(solution)/shard_map/all_to_all | solution.py:648
  22.0 2.2 %collective-permute-start = (bf16[8,128,384]{2,1,0:T(8,128)(2,1)S(1)}, bf16[8,128,384]{2,1,0:T(8,128)(2,1)S(1)}, u32[]{:S(2)}, u32[]{:S(2)}) collective-permute-start(bf16[8,128,384]{2,1,0:T(8,128)(2,1)S(1)} %shard_map.188.same_ref.refs_0_), channel_id=1, source_target_pairs={{0,8},{8,0},{1,9},{9,1},{2,10},{10,2},{3,11},{11,3},{4,12},{12,4},... | collective-permute-start | bytes 2359304 | tf_op jit(solution)/shard_map/ppermute | solution.py:652
  26.1 4.0 %shard_map.189 = bf16[8,128,256]{2,1,0:T(8,128)(2,1)} custom-call(s32[2,32]{1,0:T(2,128)S(1)} %copy-done.3, bf16[128,256]{1,0:T(8,128)(2,1)} %shard_map.187.refs_1_.q_ref, bf16[8,128,384]{2,1,0:T(8,128)(2,1)S(1)} %shard_map.188.same_ref.refs_0_, bf16[8,128,384]{2,1,0:T(8,128)(2,1)S(1)} %collective-permute-done.other_ref), custom_call_target="tpu_custom_call" | custom-call | flops 1000 | bytes 1000 | tf_op jit(solution)/shard_map/pallas_call | solution.py:106
  30.1 6.3 %all-to-all-start.1 = ((bf16[8,128,256]{2,1,0:T(8,128)(2,1)}), bf16[8,128,256]{2,1,0:T(8,128)(2,1)S(1)}, u32[]{:S(2)}, u32[]{:S(2)}) async-start(bf16[8,128,256]{2,1,0:T(8,128)(2,1)} %shard_map.189), calls=%async_computation.1 | async-start | bytes 1048576 | tf_op jit(solution)/shard_map/all_to_all | solution.py:648
  37.8 9.4 %all-to-all-done.1.mixed_ref = bf16[8,128,256]{2,1,0:T(8,128)(2,1)S(1)} async-done(((bf16[8,128,256]{2,1,0:T(8,128)(2,1)}), bf16[8,128,256]{2,1,0:T(8,128)(2,1)S(1)}, u32[]{:S(2)}, u32[]{:S(2)}) %all-to-all-start.1) | async-done | bytes 524320 | tf_op jit(solution)/shard_map/all_to_all | solution.py:648
  47.1 4.2 %shard_map.190 = (bf16[8,64,768]{2,1,0:T(8,128)(2,1)}, f32[32,768]{1,0:T(8,128)}, bf16[256,768]{1,0:T(8,128)(2,1)S(1)}, bf16[256,384]{1,0:T(8,128)(2,1)S(1)}, bf16[256,384]{1,0:T(8,128)(2,1)S(1)}) custom-call(bf16[8,128,256]{2,1,0:T(8,128)(2,1)S(1)} %all-to-all-done.1.mixed_ref, bf16[2,128,768]{2,1,0:T(8,128)(2,1)} %tok_ref.7, bf16[2,128,768]{2,1,0:T(8,128)(2,1)} %og_ref.5, ...), custom_call_target="tpu_custom_call" | custom-call | flops 1000 | bytes 1000 | tf_op jit(solution)/shard_map/pallas_call | solution.py:106
  51.3 2.8 %shard_map.194 = (bf16[8,48,768]{2,1,0:T(8,128)(2,1)S(1)}, bf16[8,48,768]{2,1,0:T(8,128)(2,1)}) custom-call(bf16[256,768]{1,0:T(8,128)(2,1)S(1)} %get-tuple-element.59.normed_ref, bf16[256,384]{1,0:T(8,128)(2,1)S(1)} %get-tuple-element.60.act_ref, bf16[256,384]{1,0:T(8,128)(2,1)S(1)} %get-tuple-element.61.gpre_ref, bf16[2,128,768]{2,1,0:T(8,128)(2,1)} %og_ref.5), custom_call_target="tpu_custom_call" | custom-call | flops 1000 | bytes 1000 | tf_op jit(solution)/shard_map/pallas_call | solution.py:106
  55.8 3.5 %all-to-all-start.2 = ((bf16[8,64,768]{2,1,0:T(8,128)(2,1)}), bf16[8,64,768]{2,1,0:T(8,128)(2,1)S(1)}, u32[]{:S(2)}, u32[]{:S(2)}) async-start(bf16[8,64,768]{2,1,0:T(8,128)(2,1)} %get-tuple-element.55), calls=%async_computation.2 | async-start | bytes 1572864 | tf_op jit(solution)/shard_map/all_to_all | solution.py:648
  65.2 2.3 %shard_map.191.query_ref = bf16[4,32,256]{2,1,0:T(8,128)(2,1)} custom-call(bf16[128,768]{1,0:T(8,128)(2,1)} %get-tuple-element.54.normed_ref, bf16[768,2304]{1,0:T(8,128)(2,1)} %w_ref.7), custom_call_target="tpu_custom_call" | custom-call | flops 1000 | bytes 1000 | tf_op jit(solution)/shard_map/pallas_call | solution.py:106
  67.5 6.4 %all-to-all-done.2.sums_ref = bf16[8,64,768]{2,1,0:T(8,128)(2,1)S(1)} async-done(((bf16[8,64,768]{2,1,0:T(8,128)(2,1)}), bf16[8,64,768]{2,1,0:T(8,128)(2,1)S(1)}, u32[]{:S(2)}, u32[]{:S(2)}) %all-to-all-start.2) | async-done | bytes 786464 | tf_op jit(solution)/shard_map/all_to_all | solution.py:648
  73.9 3.0 %shard_map.192 = (bf16[8,4,32,512]{3,2,1,0:T(8,128)(2,1)}, bf16[32,768]{1,0:T(8,128)(2,1)}, f32[32,768]{1,0:T(8,128)}, bf16[32,768]{1,0:T(8,128)(2,1)}, f32[8,768]{1,0:T(8,128)}) custom-call(bf16[8,64,768]{2,1,0:T(8,128)(2,1)S(1)} %all-to-all-done.2.sums_ref, f32[32,768]{1,0:T(8,128)} %get-tuple-element.56.middle_ref, bf16[2,128,768]{2,1,0:T(8,128)(2,1)} %og_ref.5, ...), custom_call_target="tpu_custom_call" | custom-call | flops 1000 | bytes 1000 | tf_op jit(solution)/shard_map/pallas_call | solution.py:106
  76.9 3.9 %all-to-all-start.3 = ((bf16[32,32,512]{2,1,0:T(8,128)(2,1)}), bf16[32,32,512]{2,1,0:T(8,128)(2,1)S(1)}, u32[]{:S(2)}, u32[]{:S(2)}) async-start(bf16[32,32,512]{2,1,0:T(8,128)(2,1)} %bitcast.8), calls=%async_computation.3 | async-start | bytes 2097152 | tf_op jit(solution)/shard_map/all_to_all | solution.py:648
  81.7 2.9 %collective-permute-start.6 = (bf16[32,768]{1,0:T(8,128)(2,1)S(1)}, bf16[32,768]{1,0:T(8,128)(2,1)S(1)}, u32[]{:S(2)}, u32[]{:S(2)}) collective-permute-start(bf16[32,768]{1,0:T(8,128)(2,1)S(1)} %copy-done.2), channel_id=1, source_target_pairs={{0,1},{1,0},{2,3},{3,2},{4,5},{5,4},{6,7},{7,6},{8,9},{9,8},{10,11... | collective-permute-start | bytes 147464 | tf_op jit(solution)/shard_map/ppermute | solution.py:668
  87.6 8.3 %collective-permute-done.6.refs_1_.low1_ref = bf16[32,768]{1,0:T(8,128)(2,1)S(1)} collective-permute-done((bf16[32,768]{1,0:T(8,128)(2,1)S(1)}, bf16[32,768]{1,0:T(8,128)(2,1)S(1)}, u32[]{:S(2)}, u32[]{:S(2)}) %collective-permute-start.6) | collective-permute-done | bytes 49184 | tf_op jit(solution)/shard_map/ppermute | solution.py:668
  95.8 2.5 %collective-permute-done.8.refs_3_.low3_ref = bf16[32,768]{1,0:T(8,128)(2,1)S(1)} collective-permute-done((bf16[32,768]{1,0:T(8,128)(2,1)S(1)}, bf16[32,768]{1,0:T(8,128)(2,1)S(1)}, u32[]{:S(2)}, u32[]{:S(2)}) %collective-permute-start.8) | collective-permute-done | bytes 49184 | tf_op jit(solution)/shard_map/ppermute | solution.py:668
  100.2 2.3 %collective-permute-done.9.go_ref.refs_1_ = bf16[8,128,512]{2,1,0:T(8,128)(2,1)S(1)} collective-permute-done((bf16[8,128,512]{2,1,0:T(8,128)(2,1)S(1)}, bf16[8,128,512]{2,1,0:T(8,128)(2,1)S(1)}, u32[]{:S(2)}, u32[]{:S(2)}) %collective-permute-start.9) | collective-permute-done | bytes 1048608 | tf_op jit(solution)/shard_map/ppermute | solution.py:652
  102.8 5.5 %shard_map.199 = (bf16[128,640]{1,0:T(8,128)(2,1)S(1)}, bf16[3,768,384]{2,1,0:T(8,128)(2,1)S(1)}, bf16[16,48,384]{2,1,0:T(8,128)(2,1)S(1)}, bf16[16,48,384]{2,1,0:T(8,128)(2,1)S(1)}) custom-call(s32[2,32]{1,0:T(2,128)S(1)} %copy-done.3, bf16[8,128,384]{2,1,0:T(8,128)(2,1)} %shard_map.193.kvs_ref, ...), custom_call_target="tpu_custom_call" | custom-call | flops 1000 | bytes 1000 | tf_op jit(solution)/shard_map/pallas_call | solution.py:106
  109.0 2.6 %shard_map.201 = (f32[32,768]{1,0:T(8,128)}, bf16[48,768]{1,0:T(8,128)(2,1)}, bf16[48,768]{1,0:T(8,128)(2,1)}, bf16[48,768]{1,0:T(8,128)(2,1)}, f32[8,768]{1,0:T(8,128)}, /*index=5*/bf16[2,48,768]{2,1,0:T(8,128)(2,1)}) custom-call(bf16[128,640]{1,0:T(8,128)(2,1)S(1)} %get-tuple-element.68.gqkv_ref, bf16[3,768,384]{2,1,0:T(8,128)(2,1)S(1)} %get-tuple-element.69.w_ref, ...), custom_call_target="tpu_custom_call" | custom-call | flops 1000 | bytes 1000 | tf_op jit(solution)/shard_map/pallas_call | solution.py:106
  112.7 5.9 %all-to-all-start.4 = ((bf16[16,48,384]{2,1,0:T(8,128)(2,1)}), bf16[16,48,384]{2,1,0:T(8,128)(2,1)S(1)}, u32[]{:S(2)}, u32[]{:S(2)}) async-start(bf16[16,48,384]{2,1,0:T(8,128)(2,1)} %shard_map.203), calls=%async_computation.4 | async-start | bytes 1179648 | tf_op jit(solution)/shard_map/all_to_all | solution.py:648
  119.5 3.4 %collective-permute-start.13 = (bf16[48,768]{1,0:T(8,128)(2,1)S(1)}, bf16[48,768]{1,0:T(8,128)(2,1)S(1)}, u32[]{:S(2)}, u32[]{:S(2)}) collective-permute-start(bf16[48,768]{1,0:T(8,128)(2,1)S(1)} %copy-done.5), channel_id=1, source_target_pairs={{0,3},{1,2},{2,1},{3,0},{4,7},{5,6},{6,5},{7,4},{8,11},{9,10},{10,... | collective-permute-start | bytes 221192 | tf_op jit(solution)/shard_map/ppermute | solution.py:668
  122.8 5.4 %collective-permute-done.11.refs_2_.one_ref = bf16[48,768]{1,0:T(8,128)(2,1)S(1)} collective-permute-done((bf16[48,768]{1,0:T(8,128)(2,1)S(1)}, bf16[48,768]{1,0:T(8,128)(2,1)S(1)}, u32[]{:S(2)}, u32[]{:S(2)}) %collective-permute-start.11) | collective-permute-done | bytes 73760 | tf_op jit(solution)/shard_map/ppermute | solution.py:668
  130.1 2.3 %shard_map.205.unused_ref = bf16[8,8,8,2432]{3,2,1,0:T(8,128)(2,1)} custom-call(bf16[16,48,384]{2,1,0:T(8,128)(2,1)S(1)} %shard_map.204.in_ref, f32[8,768]{1,0:T(8,128)} %get-tuple-element.79.refs_1_.vec_ref, bf16[48,768]{1,0:T(8,128)(2,1)S(1)} %collective-permute-done.11.refs_2_.one_ref, bf16[48,768]{1,0:T(8,128)(2,1)S(1)} %collective-permute-done.12.refs_3_.two_ref, ...), custom_call_target="tpu_custom_call" | custom-call | flops 1000 | bytes 1000 | tf_op jit(solution)/shard_map/pallas_call | solution.py:106
  132.4 9.5 %all-to-all-start.5 = ((bf16[64,8,2432]{2,1,0:T(8,128)(2,1)}), bf16[64,8,2432]{2,1,0:T(8,128)(2,1)S(1)}, u32[]{:S(2)}, u32[]{:S(2)}) async-start(bf16[64,8,2432]{2,1,0:T(8,128)(2,1)} %bitcast.7), calls=%async_computation.5 | async-start | bytes 4980736 | tf_op jit(solution)/shard_map/all_to_all | solution.py:648
  142.0 3.0 %shard_map.206.refs_1_.refs_0_ = bf16[8,64,768]{2,1,0:T(8,128)(2,1)} custom-call(f32[32,768]{1,0:T(8,128)} %get-tuple-element.71.unused_ref.own_ref, bf16[48,768]{1,0:T(8,128)(2,1)S(1)} %collective-permute-done.11.refs_2_.one_ref, bf16[48,768]{1,0:T(8,128)(2,1)S(1)} %collective-permute-done.12.refs_3_.two_ref, ...), custom_call_target="tpu_custom_call" | custom-call | flops 1000 | bytes 1000 | tf_op jit(solution)/shard_map/pallas_call | solution.py:106
  145.0 28.2 %all-to-all-done.5 = bf16[64,8,2432]{2,1,0:T(8,128)(2,1)S(1)} async-done(((bf16[64,8,2432]{2,1,0:T(8,128)(2,1)}), bf16[64,8,2432]{2,1,0:T(8,128)(2,1)S(1)}, u32[]{:S(2)}, u32[]{:S(2)}) %all-to-all-start.5) | async-done | bytes 2490400 | tf_op jit(solution)/shard_map/all_to_all | solution.py:648
  173.2 3.4 %collective-permute-start.15 = (bf16[8,8,8,2432]{3,2,1,0:T(8,128)(2,1)S(1)}, bf16[8,8,8,2432]{3,2,1,0:T(8,128)(2,1)}, u32[]{:S(2)}, u32[]{:S(2)}) collective-permute-start(bf16[8,8,8,2432]{3,2,1,0:T(8,128)(2,1)S(1)} %shard_map.207.refs_1_.in_ref), channel_id=1, source_target_pairs={{0,8},{8,0},{1,9},{9,1},{2,10},{10,2},{3,11},{11,3},{4,12},{12,4},... | collective-permute-start | bytes 7471112 | tf_op jit(solution)/shard_map/ppermute | solution.py:652
  176.5 3.6 %all-to-all-start.6 = ((bf16[8,64,768]{2,1,0:T(8,128)(2,1)}), bf16[8,64,768]{2,1,0:T(8,128)(2,1)S(1)}, u32[]{:S(2)}, u32[]{:S(2)}) async-start(bf16[8,64,768]{2,1,0:T(8,128)(2,1)} %shard_map.208), calls=%async_computation.6 | async-start | bytes 1572864 | tf_op jit(solution)/shard_map/all_to_all | solution.py:648
  185.4 2.4 %shard_map.209 = (f32[768,2304]{1,0:T(8,128)}, f32[768,768]{1,0:T(8,128)}, f32[4,8,128]{2,1,0:T(8,128)S(1)}) custom-call(bf16[8,8,8,2432]{3,2,1,0:T(8,128)(2,1)S(1)} %shard_map.207.refs_1_.in_ref), custom_call_target="tpu_custom_call" | custom-call | flops 1000 | bytes 1000 | tf_op jit(solution)/shard_map/pallas_call | solution.py:106
  187.8 4.1 %shard_map.210 = (f32[768,2304]{1,0:T(8,128)}, f32[768,768]{1,0:T(8,128)}, f32[768]{0:T(1024)}, f32[768]{0:T(1024)}, f32[768]{0:T(1024)}, /*index=5*/f32[768]{0:T(1024)}) custom-call(bf16[8,8,8,2432]{3,2,1,0:T(8,128)(2,1)} %collective-permute-done.15.in_ref, ...), custom_call_target="tpu_custom_call", output_to_operand_aliasing={{0}: (2, {}), {1}: (3, {})} | custom-call | flops 1000 | bytes 1000 | tf_op jit(solution)/shard_map/pallas_call | solution.py:106
  (76 shorter events, 31.9 us)
Async XLA Ops:
  4.3 17.6 %all-to-all-start = ((bf16[8,128,384]{2,1,0:T(8,128)(2,1)}), bf16[8,128,384]{2,1,0:T(8,128)(2,1)S(1)}, u32[]{:S(2)}, u32[]{:S(2)}) async-start(bf16[8,128,384]{2,1,0:T(8,128)(2,1)} %get-tuple-element.53), calls=%async_computation | async-start | bytes 1572864 | tf_op jit(solution)/shard_map/all_to_all | solution.py:648
  10.3 15.8 %copy-start.3 = (s32[2,32]{1,0:T(2,128)S(1)}, s32[2,32]{1,0:T(2,128)}, u32[]{:S(2)}) copy-start(s32[2,32]{1,0:T(2,128)} %scene_ref.3) | copy-start | bytes 772
  22.0 15.8 %copy-start = (bf16[8,128,384]{2,1,0:T(8,128)(2,1)}, bf16[8,128,384]{2,1,0:T(8,128)(2,1)S(1)}, u32[]{:S(2)}) copy-start(bf16[8,128,384]{2,1,0:T(8,128)(2,1)S(1)} %shard_map.188.same_ref.refs_0_) | copy-start | bytes 2359300
  22.0 4.1 %collective-permute-start = (bf16[8,128,384]{2,1,0:T(8,128)(2,1)S(1)}, bf16[8,128,384]{2,1,0:T(8,128)(2,1)S(1)}, u32[]{:S(2)}, u32[]{:S(2)}) collective-permute-start(bf16[8,128,384]{2,1,0:T(8,128)(2,1)S(1)} %shard_map.188.same_ref.refs_0_), channel_id=1, source_target_pairs={{0,8},{8,0},{1,9},{9,1},{2,10},{10,2},{3,11},{11,3},{4,12},{12,4},... | collective-permute-start | bytes 2359304 | tf_op jit(solution)/shard_map/ppermute | solution.py:652
  30.1 17.1 %all-to-all-start.1 = ((bf16[8,128,256]{2,1,0:T(8,128)(2,1)}), bf16[8,128,256]{2,1,0:T(8,128)(2,1)S(1)}, u32[]{:S(2)}, u32[]{:S(2)}) async-start(bf16[8,128,256]{2,1,0:T(8,128)(2,1)} %shard_map.189), calls=%async_computation.1 | async-start | bytes 1048576 | tf_op jit(solution)/shard_map/all_to_all | solution.py:648
  54.1 5.3 %collective-permute-start.2 = (bf16[8,48,768]{2,1,0:T(8,128)(2,1)}, bf16[8,48,768]{2,1,0:T(8,128)(2,1)}, u32[]{:S(2)}, u32[]{:S(2)}) collective-permute-start(bf16[8,48,768]{2,1,0:T(8,128)(2,1)} %get-tuple-element.63), channel_id=1, source_target_pairs={{0,8},{8,0},{1,9},{9,1},{2,10},{10,2},{3,11},{11,3},{4,12},{12,4},... | collective-permute-start | bytes 1769480 | tf_op jit(solution)/shard_map/ppermute | solution.py:652
  55.8 18.1 %all-to-all-start.2 = ((bf16[8,64,768]{2,1,0:T(8,128)(2,1)}), bf16[8,64,768]{2,1,0:T(8,128)(2,1)S(1)}, u32[]{:S(2)}, u32[]{:S(2)}) async-start(bf16[8,64,768]{2,1,0:T(8,128)(2,1)} %get-tuple-element.55), calls=%async_computation.2 | async-start | bytes 1572864 | tf_op jit(solution)/shard_map/all_to_all | solution.py:648
  61.3 15.6 %collective-permute-start.3 = (bf16[2,48,768]{2,1,0:T(8,128)(2,1)}, bf16[2,48,768]{2,1,0:T(8,128)(2,1)S(1)}, u32[]{:S(2)}, u32[]{:S(2)}) collective-permute-start(bf16[2,48,768]{2,1,0:T(8,128)(2,1)} %get-tuple-element.64), channel_id=1, source_target_pairs={{0,32},{32,0},{64,96},{96,64},{1,33},{33,1},{65,97},{97,65},{2,34}... | collective-permute-start | bytes 442376 | tf_op jit(solution)/shard_map/ppermute | solution.py:668
  61.9 15.0 %collective-permute-start.4 = (bf16[2,48,768]{2,1,0:T(8,128)(2,1)}, bf16[2,48,768]{2,1,0:T(8,128)(2,1)S(1)}, u32[]{:S(2)}, u32[]{:S(2)}) collective-permute-start(bf16[2,48,768]{2,1,0:T(8,128)(2,1)} %get-tuple-element.65), channel_id=1, source_target_pairs={{0,64},{32,96},{64,0},{96,32},{1,65},{33,97},{65,1},{97,33},{2,66}... | collective-permute-start | bytes 442376 | tf_op jit(solution)/shard_map/ppermute | solution.py:668
  63.9 12.9 %collective-permute-start.5 = (bf16[2,48,768]{2,1,0:T(8,128)(2,1)}, bf16[2,48,768]{2,1,0:T(8,128)(2,1)S(1)}, u32[]{:S(2)}, u32[]{:S(2)}) collective-permute-start(bf16[2,48,768]{2,1,0:T(8,128)(2,1)} %get-tuple-element.66), channel_id=1, source_target_pairs={{0,96},{32,64},{64,32},{96,0},{1,97},{33,65},{65,33},{97,1},{2,98}... | collective-permute-start | bytes 442376 | tf_op jit(solution)/shard_map/ppermute | solution.py:668
  76.9 21.4 %all-to-all-start.3 = ((bf16[32,32,512]{2,1,0:T(8,128)(2,1)}), bf16[32,32,512]{2,1,0:T(8,128)(2,1)S(1)}, u32[]{:S(2)}, u32[]{:S(2)}) async-start(bf16[32,32,512]{2,1,0:T(8,128)(2,1)} %bitcast.8), calls=%async_computation.3 | async-start | bytes 2097152 | tf_op jit(solution)/shard_map/all_to_all | solution.py:648
  80.9 17.4 %collective-permute-start.1 = (bf16[8,128,384]{2,1,0:T(8,128)(2,1)}, bf16[8,128,384]{2,1,0:T(8,128)(2,1)S(1)}, u32[]{:S(2)}, u32[]{:S(2)}) collective-permute-start(bf16[8,128,384]{2,1,0:T(8,128)(2,1)} %shard_map.193.kvs_ref), channel_id=1, source_target_pairs={{0,8},{8,0},{1,9},{9,1},{2,10},{10,2},{3,11},{11,3},{4,12},{12,4},... | collective-permute-start | bytes 2359304 | tf_op jit(solution)/shard_map/ppermute | solution.py:652
  81.7 14.1 %collective-permute-start.6 = (bf16[32,768]{1,0:T(8,128)(2,1)S(1)}, bf16[32,768]{1,0:T(8,128)(2,1)S(1)}, u32[]{:S(2)}, u32[]{:S(2)}) collective-permute-start(bf16[32,768]{1,0:T(8,128)(2,1)S(1)} %copy-done.2), channel_id=1, source_target_pairs={{0,1},{1,0},{2,3},{3,2},{4,5},{5,4},{6,7},{7,6},{8,9},{9,8},{10,11... | collective-permute-start | bytes 147464 | tf_op jit(solution)/shard_map/ppermute | solution.py:668
  84.7 11.2 %collective-permute-start.7 = (bf16[32,768]{1,0:T(8,128)(2,1)S(1)}, bf16[32,768]{1,0:T(8,128)(2,1)S(1)}, u32[]{:S(2)}, u32[]{:S(2)}) collective-permute-start(bf16[32,768]{1,0:T(8,128)(2,1)S(1)} %copy-done.2), channel_id=1, source_target_pairs={{0,2},{1,3},{2,0},{3,1},{4,6},{5,7},{6,4},{7,5},{8,10},{9,11},{10,... | collective-permute-start | bytes 147464 | tf_op jit(solution)/shard_map/ppermute | solution.py:668
  85.9 12.4 %collective-permute-start.8 = (bf16[32,768]{1,0:T(8,128)(2,1)S(1)}, bf16[32,768]{1,0:T(8,128)(2,1)S(1)}, u32[]{:S(2)}, u32[]{:S(2)}) collective-permute-start(bf16[32,768]{1,0:T(8,128)(2,1)S(1)} %copy-done.2), channel_id=1, source_target_pairs={{0,3},{1,2},{2,1},{3,0},{4,7},{5,6},{6,5},{7,4},{8,11},{9,10},{10,... | collective-permute-start | bytes 147464 | tf_op jit(solution)/shard_map/ppermute | solution.py:668
  98.3 4.2 %collective-permute-start.9 = (bf16[8,128,512]{2,1,0:T(8,128)(2,1)S(1)}, bf16[8,128,512]{2,1,0:T(8,128)(2,1)S(1)}, u32[]{:S(2)}, u32[]{:S(2)}) collective-permute-start(bf16[8,128,512]{2,1,0:T(8,128)(2,1)S(1)} %shard_map.198.gs_ref), channel_id=1, source_target_pairs={{0,8},{8,0},{1,9},{9,1},{2,10},{10,2},{3,11},{11,3},{4,12},{12,4},... | collective-permute-start | bytes 3145736 | tf_op jit(solution)/shard_map/ppermute | solution.py:652
  102.5 5.8 %collective-permute-start.10 = (bf16[2,48,768]{2,1,0:T(8,128)(2,1)}, bf16[2,48,768]{2,1,0:T(8,128)(2,1)S(1)}, u32[]{:S(2)}, u32[]{:S(2)}) collective-permute-start(bf16[2,48,768]{2,1,0:T(8,128)(2,1)} %shard_map.200.near_ref), channel_id=1, source_target_pairs={{0,16},{16,0},{1,17},{17,1},{2,18},{18,2},{3,19},{19,3},{4,20},{20... | collective-permute-start | bytes 442376 | tf_op jit(solution)/shard_map/ppermute | solution.py:668
  108.3 3.4 %collective-permute-start.14 = (bf16[16,48,384]{2,1,0:T(8,128)(2,1)S(1)}, bf16[16,48,384]{2,1,0:T(8,128)(2,1)S(1)}, u32[]{:S(2)}, u32[]{:S(2)}) collective-permute-start(bf16[16,48,384]{2,1,0:T(8,128)(2,1)S(1)} %shard_map.202), channel_id=1, source_target_pairs={{0,8},{8,0},{1,9},{9,1},{2,10},{10,2},{3,11},{11,3},{4,12},{12,4},... | collective-permute-start | bytes 1769480 | tf_op jit(solution)/shard_map/ppermute | solution.py:652
  112.7 17.4 %all-to-all-start.4 = ((bf16[16,48,384]{2,1,0:T(8,128)(2,1)}), bf16[16,48,384]{2,1,0:T(8,128)(2,1)S(1)}, u32[]{:S(2)}, u32[]{:S(2)}) async-start(bf16[16,48,384]{2,1,0:T(8,128)(2,1)} %shard_map.203), calls=%async_computation.4 | async-start | bytes 1179648 | tf_op jit(solution)/shard_map/all_to_all | solution.py:648
  118.6 9.6 %collective-permute-start.11 = (bf16[48,768]{1,0:T(8,128)(2,1)S(1)}, bf16[48,768]{1,0:T(8,128)(2,1)S(1)}, u32[]{:S(2)}, u32[]{:S(2)}) collective-permute-start(bf16[48,768]{1,0:T(8,128)(2,1)S(1)} %copy-done.7), channel_id=1, source_target_pairs={{0,1},{1,0},{2,3},{3,2},{4,5},{5,4},{6,7},{7,6},{8,9},{9,8},{10,11... | collective-permute-start | bytes 221192 | tf_op jit(solution)/shard_map/ppermute | solution.py:668
  119.4 8.8 %collective-permute-start.12 = (bf16[48,768]{1,0:T(8,128)(2,1)S(1)}, bf16[48,768]{1,0:T(8,128)(2,1)S(1)}, u32[]{:S(2)}, u32[]{:S(2)}) collective-permute-start(bf16[48,768]{1,0:T(8,128)(2,1)S(1)} %copy-done.6), channel_id=1, source_target_pairs={{0,2},{1,3},{2,0},{3,1},{4,6},{5,7},{6,4},{7,5},{8,10},{9,11},{10,... | collective-permute-start | bytes 221192 | tf_op jit(solution)/shard_map/ppermute | solution.py:668
  119.5 10.7 %collective-permute-start.13 = (bf16[48,768]{1,0:T(8,128)(2,1)S(1)}, bf16[48,768]{1,0:T(8,128)(2,1)S(1)}, u32[]{:S(2)}, u32[]{:S(2)}) collective-permute-start(bf16[48,768]{1,0:T(8,128)(2,1)S(1)} %copy-done.5), channel_id=1, source_target_pairs={{0,3},{1,2},{2,1},{3,0},{4,7},{5,6},{6,5},{7,4},{8,11},{9,10},{10,... | collective-permute-start | bytes 221192 | tf_op jit(solution)/shard_map/ppermute | solution.py:668
  132.4 40.7 %all-to-all-start.5 = ((bf16[64,8,2432]{2,1,0:T(8,128)(2,1)}), bf16[64,8,2432]{2,1,0:T(8,128)(2,1)S(1)}, u32[]{:S(2)}, u32[]{:S(2)}) async-start(bf16[64,8,2432]{2,1,0:T(8,128)(2,1)} %bitcast.7), calls=%async_computation.5 | async-start | bytes 4980736 | tf_op jit(solution)/shard_map/all_to_all | solution.py:648
  173.2 14.6 %collective-permute-start.15 = (bf16[8,8,8,2432]{3,2,1,0:T(8,128)(2,1)S(1)}, bf16[8,8,8,2432]{3,2,1,0:T(8,128)(2,1)}, u32[]{:S(2)}, u32[]{:S(2)}) collective-permute-start(bf16[8,8,8,2432]{3,2,1,0:T(8,128)(2,1)S(1)} %shard_map.207.refs_1_.in_ref), channel_id=1, source_target_pairs={{0,8},{8,0},{1,9},{9,1},{2,10},{10,2},{3,11},{11,3},{4,12},{12,4},... | collective-permute-start | bytes 7471112 | tf_op jit(solution)/shard_map/ppermute | solution.py:652
  176.5 19.8 %all-to-all-start.6 = ((bf16[8,64,768]{2,1,0:T(8,128)(2,1)}), bf16[8,64,768]{2,1,0:T(8,128)(2,1)S(1)}, u32[]{:S(2)}, u32[]{:S(2)}) async-start(bf16[8,64,768]{2,1,0:T(8,128)(2,1)} %shard_map.208), calls=%async_computation.6 | async-start | bytes 1572864 | tf_op jit(solution)/shard_map/all_to_all | solution.py:648
  180.1 11.7 %collective-permute-start.17 = (bf16[2,48,768]{2,1,0:T(8,128)(2,1)S(1)}, bf16[2,48,768]{2,1,0:T(8,128)(2,1)S(1)}, u32[]{:S(2)}, u32[]{:S(2)}) collective-permute-start(bf16[2,48,768]{2,1,0:T(8,128)(2,1)S(1)} %copy-done.4), channel_id=1, source_target_pairs={{0,32},{32,0},{64,96},{96,64},{1,33},{33,1},{65,97},{97,65},{2,34}... | collective-permute-start | bytes 442376 | tf_op jit(solution)/shard_map/ppermute | solution.py:668
  180.6 11.4 %collective-permute-start.19 = (bf16[2,48,768]{2,1,0:T(8,128)(2,1)S(1)}, bf16[2,48,768]{2,1,0:T(8,128)(2,1)S(1)}, u32[]{:S(2)}, u32[]{:S(2)}) collective-permute-start(bf16[2,48,768]{2,1,0:T(8,128)(2,1)S(1)} %copy-done.4), channel_id=1, source_target_pairs={{0,64},{32,96},{64,0},{96,32},{1,65},{33,97},{65,1},{97,33},{2,66}... | collective-permute-start | bytes 442376 | tf_op jit(solution)/shard_map/ppermute | solution.py:668
  182.4 10.1 %collective-permute-start.21 = (bf16[2,48,768]{2,1,0:T(8,128)(2,1)S(1)}, bf16[2,48,768]{2,1,0:T(8,128)(2,1)S(1)}, u32[]{:S(2)}, u32[]{:S(2)}) collective-permute-start(bf16[2,48,768]{2,1,0:T(8,128)(2,1)S(1)} %copy-done.4), channel_id=1, source_target_pairs={{0,96},{32,64},{64,32},{96,0},{1,97},{33,65},{65,33},{97,1},{2,98}... | collective-permute-start | bytes 442376 | tf_op jit(solution)/shard_map/ppermute | solution.py:668
  184.1 11.0 %collective-permute-start.16 = (bf16[2,48,768]{2,1,0:T(8,128)(2,1)S(1)}, bf16[2,48,768]{2,1,0:T(8,128)(2,1)S(1)}, u32[]{:S(2)}, u32[]{:S(2)}) collective-permute-start(bf16[2,48,768]{2,1,0:T(8,128)(2,1)S(1)} %copy-done.4), channel_id=1, source_target_pairs={{0,8},{8,0},{1,9},{9,1},{2,10},{10,2},{3,11},{11,3},{4,12},{12,4},... | collective-permute-start | bytes 442376 | tf_op jit(solution)/shard_map/ppermute | solution.py:652
  191.9 3.2 %collective-permute-start.18 = (bf16[2,48,768]{2,1,0:T(8,128)(2,1)S(1)}, bf16[2,48,768]{2,1,0:T(8,128)(2,1)S(1)}, u32[]{:S(2)}, u32[]{:S(2)}) collective-permute-start(bf16[2,48,768]{2,1,0:T(8,128)(2,1)S(1)} %shard_map.211.refs_1_), channel_id=1, source_target_pairs={{0,8},{8,0},{1,9},{9,1},{2,10},{10,2},{3,11},{11,3},{4,12},{12,4},... | collective-permute-start | bytes 442376 | tf_op jit(solution)/shard_map/ppermute | solution.py:652
  192.0 3.1 %collective-permute-start.20 = (bf16[2,48,768]{2,1,0:T(8,128)(2,1)S(1)}, bf16[2,48,768]{2,1,0:T(8,128)(2,1)S(1)}, u32[]{:S(2)}, u32[]{:S(2)}) collective-permute-start(bf16[2,48,768]{2,1,0:T(8,128)(2,1)S(1)} %shard_map.212.refs_2_), channel_id=1, source_target_pairs={{0,8},{8,0},{1,9},{9,1},{2,10},{10,2},{3,11},{11,3},{4,12},{12,4},... | collective-permute-start | bytes 442376 | tf_op jit(solution)/shard_map/ppermute | solution.py:652
  192.5 2.6 %collective-permute-start.22 = (bf16[2,48,768]{2,1,0:T(8,128)(2,1)S(1)}, bf16[2,48,768]{2,1,0:T(8,128)(2,1)S(1)}, u32[]{:S(2)}, u32[]{:S(2)}) collective-permute-start(bf16[2,48,768]{2,1,0:T(8,128)(2,1)S(1)} %shard_map.213.refs_3_), channel_id=1, source_target_pairs={{0,8},{8,0},{1,9},{9,1},{2,10},{10,2},{3,11},{11,3},{4,12},{12,4},... | collective-permute-start | bytes 442376 | tf_op jit(solution)/shard_map/ppermute | solution.py:652
  (6 other events, 40.3 us)

commit v20 on v19

--- a/solution.py
+++ b/solution.py
@@ -359,8 +359,13 @@
             inside = (lane >= (head + 1) * HD) & (lane < (head + 2) * HD)
             columns += three(jnp.sum(jnp.where(inside, product, 0.0), axis=-1, keepdims=True))
         stats = put_columns(256, BLK, 9, columns)
-        buf[head_group, :, :256] = jnp.where(lane < 9, mixed, jnp.where(lane < HD, stats, back)).astype(BF)
-        buf[head_group, :, 256:] = query_buf[head_group]
+        packed = jnp.where(lane < 9, mixed, jnp.where(lane < HD, stats, back)).astype(BF)
+        query = query_buf[head_group]
+        last = query[:, 128:192]
+        buf[head_group, :32] = packed[:, :128]
+        buf[head_group, 32:64] = packed[:, 128:]
+        buf[head_group, 64:96] = query[:, :128]
+        buf[head_group, 96:] = jnp.concatenate([last[:16], last[16:]], axis=1)
     sends = send_copies(buf, out_ref, range(8), sem)
     wait_all(stores)
     wait_all(sends)
@@ -394,11 +399,19 @@
         def cut(value):
             return [value[:, at:at + 128] for at in range(0, value.shape[1], 128)]
 
-        every = cut(jnp.concatenate(
-            [ref[pl.ds(first, count)].reshape(rows, 512) for ref in (gs_ref, go_ref)], axis=0
-        ))
+        def unpacked(ref, start, tiles):
+            blocks = [ref[pl.ds(start, tiles), :, at:at + 32] for at in (0, 32, 64)]
+            last = ref[pl.ds(start, tiles), :, 96:]
+            turned = jnp.concatenate([last[..., HD:], last[..., :HD]], axis=-1)
+            blocks.append(jnp.concatenate([last, turned], axis=2))
+            return [block.reshape(tiles * TOK, 128) for block in blocks]
+
+        every = [
+            jnp.concatenate(pair, axis=0)
+            for pair in zip(*[unpacked(ref, first, count) for ref in (gs_ref, go_ref)])
+        ]
         grad, query = every[:2], every[2:]
-        g_own = cut(gs_ref[chip])
+        g_own = unpacked(gs_ref, chip, 1)
         g_heads = [halves(g_own[0])[1], *halves(g_own[1])]
         own_stats = g_own[0].astype(F32)
         all_stats = grad[0].astype(F32).T
@@ -407,7 +420,7 @@
             [kv_buf[:count].reshape(rows, 384), kvo_ref[pl.ds(first, count)].reshape(rows, 384)], axis=0
         ))
         own = cut(kv_buf[chip - first]) + g_own[2:]
-        q_heads = [*halves(own[3]), own[4]]
+        q_heads = [*halves(own[3]), halves(own[4])[0]]
         k_heads = [*halves(own[0]), halves(own[1])[0]]
         v_heads = [halves(own[1])[1], *halves(own[2])]
 
@@ -745,7 +758,7 @@
     grad_send, low, grad_mid, result_part, vec2 = call(
         middle_kernel,
         [
-            ((8, 4, BLK, 512), BF, "H"), ((BLK, D), BF, "H"), ((BLK, D), F32, "H"), ((BLK, D), BF, "H"),
+            ((8, 4, 112, 128), BF, "H"), ((BLK, D), BF, "H"), ((BLK, D), F32, "H"), ((BLK, D), BF, "H"),
             ((8, D), F32, "H"),
         ],
         [
@@ -754,13 +767,13 @@
         ],
         1000,
         [
-            pltpu.VMEM((4, BLK, 512), BF), pltpu.VMEM((BLK, D), F32), pltpu.VMEM((BLK, D), BF),
+            pltpu.VMEM((4, 112, 128), BF), pltpu.VMEM((BLK, D), F32), pltpu.VMEM((BLK, D), BF),
             pltpu.VMEM((4, BLK, 256), BF), pltpu.VMEM((D,), F32), pltpu.VMEM((4, BLK, 256), BF), pltpu.VMEM((BLK, D), BF), pltpu.VMEM((BLK, D), F32),
             pltpu.VMEM((BLK, D), BF), pltpu.VMEM((8, D), F32), DMA((5,)), DMA((8,)), DMA((4,)),
         ],
     )
     grad_send = after(pin(grad_send), *pieces[1:])
-    grad_same = exchange(grad_send.reshape(32, BLK, 512), (*CHIP, *GROUP)).reshape(8, TOK, 512)
+    grad_same = exchange(grad_send.reshape(32, 112, 128), (*CHIP, *GROUP)).reshape(8, 4, 112, 128)
     lows = [flip(low, GROUP, 4, k) for k in (1, 2, 3)]
     kv_same = after(pin(kv_same), low)
     kv_other = swap(kv_same)

time: 199 us -> 197 us (0.990)
  no operation moved by 1% of the time
where the time goes in v20:
time: 197 us; the launch traced here: 196 us
  waiting for transfers between devices  73.1 us (37%)
  starting transfers between devices  68.6 us (35%)
  Pallas kernels  51.7 us (26%)
    all_to_all x7, waiting for transfers between devices, exchange(): return lax.all_to_all(value, axes, 0, 0, tiled=True)  52.6 us
    pallas_call x19, Pallas kernels, call(): pl.pallas_call(kernel, out_shape=[(pltpu.HBM if place in 'HL' else jax.Sh...  51.6 us
    all_to_all x7, starting transfers between devices, exchange(): return lax.all_to_all(value, axes, 0, 0, tiled=True)  38.9 us
    ppermute x13, starting transfers between devices, flip(): lax.ppermute(value, axes, [(index, index ^ bits) for index in range(count)])  16.5 us
    ppermute x13, waiting for transfers between devices, flip(): lax.ppermute(value, axes, [(index, index ^ bits) for index in range(count)])  16.5 us
    ppermute x10, starting transfers between devices, swap(): return lax.ppermute(value, CORE, [(0, 1), (1, 0)])  13.2 us
    ppermute x10, waiting for transfers between devices, swap(): return lax.ppermute(value, CORE, [(0, 1), (1, 0)])  4.03 us
  transfers between devices with their start and end apart: 30, of which 10 were waited for; matrix products, arithmetic and copies ran while one was open for 1% of the time, Pallas kernels for 17%

profile of v20, /device:TPU:1, one launch (start us, length us, event | category | flops | bytes accessed | tf_op | source)
XLA Modules:
  0.0 195.8 jit_solution(10069457259422393110)
XLA Ops:
  0.6 3.7 %shard_map.186 = (bf16[8,128,384]{2,1,0:T(8,128)(2,1)}, bf16[128,768]{1,0:T(8,128)(2,1)}) custom-call(bf16[2,128,768]{2,1,0:T(8,128)(2,1)} %tok_ref.7, f32[768]{0:T(1024)} %gain_ref.7, f32[768]{0:T(1024)} %shift_ref.2, bf16[768,2304]{1,0:T(8,128)(2,1)} %w_ref.7), custom_call_target="tpu_custom_call" | custom-call | flops 1000 | bytes 1000 | tf_op jit(solution)/shard_map/pallas_call | solution.py:106
  4.3 6.0 %all-to-all-start = ((bf16[8,128,384]{2,1,0:T(8,128)(2,1)}), bf16[8,128,384]{2,1,0:T(8,128)(2,1)S(1)}, u32[]{:S(2)}, u32[]{:S(2)}) async-start(bf16[8,128,384]{2,1,0:T(8,128)(2,1)} %get-tuple-element.53), calls=%async_computation | async-start | bytes 1572864 | tf_op jit(solution)/shard_map/all_to_all | solution.py:661
  10.3 3.0 %shard_map.187.refs_1_.q_ref = bf16[128,256]{1,0:T(8,128)(2,1)} custom-call(bf16[128,768]{1,0:T(8,128)(2,1)} %get-tuple-element.54.normed_ref, bf16[768,2304]{1,0:T(8,128)(2,1)} %w_ref.7), custom_call_target="tpu_custom_call" | custom-call | flops 1000 | bytes 1000 | tf_op jit(solution)/shard_map/pallas_call | solution.py:106
  13.4 8.6 %all-to-all-done.refs_0_ = bf16[8,128,384]{2,1,0:T(8,128)(2,1)S(1)} async-done(((bf16[8,128,384]{2,1,0:T(8,128)(2,1)}), bf16[8,128,384]{2,1,0:T(8,128)(2,1)S(1)}, u32[]{:S(2)}, u32[]{:S(2)}) %all-to-all-start) | async-done | bytes 786464 | tf_op jit(solution)/shard_map/all_to_all | solution.py:661
  22.0 2.2 %collective-permute-start = (bf16[8,128,384]{2,1,0:T(8,128)(2,1)S(1)}, bf16[8,128,384]{2,1,0:T(8,128)(2,1)S(1)}, u32[]{:S(2)}, u32[]{:S(2)}) collective-permute-start(bf16[8,128,384]{2,1,0:T(8,128)(2,1)S(1)} %shard_map.188.same_ref.refs_0_), channel_id=1, source_target_pairs={{0,8},{8,0},{1,9},{9,1},{2,10},{10,2},{3,11},{11,3},{4,12},{12,4},... | collective-permute-start | bytes 2359304 | tf_op jit(solution)/shard_map/ppermute | solution.py:665
  26.1 4.0 %shard_map.189 = bf16[8,128,256]{2,1,0:T(8,128)(2,1)} custom-call(s32[2,32]{1,0:T(2,128)S(1)} %copy-done.3, bf16[128,256]{1,0:T(8,128)(2,1)} %shard_map.187.refs_1_.q_ref, bf16[8,128,384]{2,1,0:T(8,128)(2,1)S(1)} %shard_map.188.same_ref.refs_0_, bf16[8,128,384]{2,1,0:T(8,128)(2,1)S(1)} %collective-permute-done.other_ref), custom_call_target="tpu_custom_call" | custom-call | flops 1000 | bytes 1000 | tf_op jit(solution)/shard_map/pallas_call | solution.py:106
  30.1 6.3 %all-to-all-start.1 = ((bf16[8,128,256]{2,1,0:T(8,128)(2,1)}), bf16[8,128,256]{2,1,0:T(8,128)(2,1)S(1)}, u32[]{:S(2)}, u32[]{:S(2)}) async-start(bf16[8,128,256]{2,1,0:T(8,128)(2,1)} %shard_map.189), calls=%async_computation.1 | async-start | bytes 1048576 | tf_op jit(solution)/shard_map/all_to_all | solution.py:661
  37.8 9.4 %all-to-all-done.1.mixed_ref = bf16[8,128,256]{2,1,0:T(8,128)(2,1)S(1)} async-done(((bf16[8,128,256]{2,1,0:T(8,128)(2,1)}), bf16[8,128,256]{2,1,0:T(8,128)(2,1)S(1)}, u32[]{:S(2)}, u32[]{:S(2)}) %all-to-all-start.1) | async-done | bytes 524320 | tf_op jit(solution)/shard_map/all_to_all | solution.py:661
  47.1 4.2 %shard_map.190 = (bf16[8,64,768]{2,1,0:T(8,128)(2,1)}, f32[32,768]{1,0:T(8,128)}, bf16[256,768]{1,0:T(8,128)(2,1)S(1)}, bf16[256,384]{1,0:T(8,128)(2,1)S(1)}, bf16[256,384]{1,0:T(8,128)(2,1)S(1)}) custom-call(bf16[8,128,256]{2,1,0:T(8,128)(2,1)S(1)} %all-to-all-done.1.mixed_ref, bf16[2,128,768]{2,1,0:T(8,128)(2,1)} %tok_ref.7, bf16[2,128,768]{2,1,0:T(8,128)(2,1)} %og_ref.5, ...), custom_call_target="tpu_custom_call" | custom-call | flops 1000 | bytes 1000 | tf_op jit(solution)/shard_map/pallas_call | solution.py:106
  51.3 2.8 %shard_map.194 = (bf16[8,48,768]{2,1,0:T(8,128)(2,1)S(1)}, bf16[8,48,768]{2,1,0:T(8,128)(2,1)}) custom-call(bf16[256,768]{1,0:T(8,128)(2,1)S(1)} %get-tuple-element.59.normed_ref, bf16[256,384]{1,0:T(8,128)(2,1)S(1)} %get-tuple-element.60.act_ref, bf16[256,384]{1,0:T(8,128)(2,1)S(1)} %get-tuple-element.61.gpre_ref, bf16[2,128,768]{2,1,0:T(8,128)(2,1)} %og_ref.5), custom_call_target="tpu_custom_call" | custom-call | flops 1000 | bytes 1000 | tf_op jit(solution)/shard_map/pallas_call | solution.py:106
  55.8 3.5 %all-to-all-start.2 = ((bf16[8,64,768]{2,1,0:T(8,128)(2,1)}), bf16[8,64,768]{2,1,0:T(8,128)(2,1)S(1)}, u32[]{:S(2)}, u32[]{:S(2)}) async-start(bf16[8,64,768]{2,1,0:T(8,128)(2,1)} %get-tuple-element.55), calls=%async_computation.2 | async-start | bytes 1572864 | tf_op jit(solution)/shard_map/all_to_all | solution.py:661
  61.3 2.6 %collective-permute-start.4 = (bf16[2,48,768]{2,1,0:T(8,128)(2,1)}, bf16[2,48,768]{2,1,0:T(8,128)(2,1)S(1)}, u32[]{:S(2)}, u32[]{:S(2)}) collective-permute-start(bf16[2,48,768]{2,1,0:T(8,128)(2,1)} %get-tuple-element.65), channel_id=1, source_target_pairs={{0,64},{32,96},{64,0},{96,32},{1,65},{33,97},{65,1},{97,33},{2,66}... | collective-permute-start | bytes 442376 | tf_op jit(solution)/shard_map/ppermute | solution.py:681
  65.2 2.3 %shard_map.191.query_ref = bf16[4,32,256]{2,1,0:T(8,128)(2,1)} custom-call(bf16[128,768]{1,0:T(8,128)(2,1)} %get-tuple-element.54.normed_ref, bf16[768,2304]{1,0:T(8,128)(2,1)} %w_ref.7), custom_call_target="tpu_custom_call" | custom-call | flops 1000 | bytes 1000 | tf_op jit(solution)/shard_map/pallas_call | solution.py:106
  67.5 6.4 %all-to-all-done.2.sums_ref = bf16[8,64,768]{2,1,0:T(8,128)(2,1)S(1)} async-done(((bf16[8,64,768]{2,1,0:T(8,128)(2,1)}), bf16[8,64,768]{2,1,0:T(8,128)(2,1)S(1)}, u32[]{:S(2)}, u32[]{:S(2)}) %all-to-all-start.2) | async-done | bytes 786464 | tf_op jit(solution)/shard_map/all_to_all | solution.py:661
  73.9 2.9 %shard_map.192 = (bf16[8,4,112,128]{3,2,1,0:T(8,128)(2,1)}, bf16[32,768]{1,0:T(8,128)(2,1)}, f32[32,768]{1,0:T(8,128)}, bf16[32,768]{1,0:T(8,128)(2,1)}, f32[8,768]{1,0:T(8,128)}) custom-call(bf16[8,64,768]{2,1,0:T(8,128)(2,1)S(1)} %all-to-all-done.2.sums_ref, f32[32,768]{1,0:T(8,128)} %get-tuple-element.56.middle_ref, bf16[2,128,768]{2,1,0:T(8,128)(2,1)} %og_ref.5, ...), custom_call_target="tpu_custom_call" | custom-call | flops 1000 | bytes 1000 | tf_op jit(solution)/shard_map/pallas_call | solution.py:106
  76.9 3.9 %all-to-all-start.3 = ((bf16[32,112,128]{2,1,0:T(8,128)(2,1)}), bf16[32,112,128]{2,1,0:T(8,128)(2,1)S(1)}, u32[]{:S(2)}, u32[]{:S(2)}) async-start(bf16[32,112,128]{2,1,0:T(8,128)(2,1)} %bitcast.8), calls=%async_computation.3 | async-start | bytes 1835008 | tf_op jit(solution)/shard_map/all_to_all | solution.py:661
  81.7 2.9 %collective-permute-start.6 = (bf16[32,768]{1,0:T(8,128)(2,1)S(1)}, bf16[32,768]{1,0:T(8,128)(2,1)S(1)}, u32[]{:S(2)}, u32[]{:S(2)}) collective-permute-start(bf16[32,768]{1,0:T(8,128)(2,1)S(1)} %copy-done.2), channel_id=1, source_target_pairs={{0,1},{1,0},{2,3},{3,2},{4,5},{5,4},{6,7},{7,6},{8,9},{9,8},{10,11... | collective-permute-start | bytes 147464 | tf_op jit(solution)/shard_map/ppermute | solution.py:681
  87.5 6.9 %collective-permute-done.6.refs_1_.low1_ref = bf16[32,768]{1,0:T(8,128)(2,1)S(1)} collective-permute-done((bf16[32,768]{1,0:T(8,128)(2,1)S(1)}, bf16[32,768]{1,0:T(8,128)(2,1)S(1)}, u32[]{:S(2)}, u32[]{:S(2)}) %collective-permute-start.6) | collective-permute-done | bytes 49184 | tf_op jit(solution)/shard_map/ppermute | solution.py:681
  94.4 2.3 %collective-permute-done.8.refs_3_.low3_ref = bf16[32,768]{1,0:T(8,128)(2,1)S(1)} collective-permute-done((bf16[32,768]{1,0:T(8,128)(2,1)S(1)}, bf16[32,768]{1,0:T(8,128)(2,1)S(1)}, u32[]{:S(2)}, u32[]{:S(2)}) %collective-permute-start.8) | collective-permute-done | bytes 49184 | tf_op jit(solution)/shard_map/ppermute | solution.py:681
  101.0 5.5 %shard_map.199 = (bf16[128,640]{1,0:T(8,128)(2,1)S(1)}, bf16[3,768,384]{2,1,0:T(8,128)(2,1)S(1)}, bf16[16,48,384]{2,1,0:T(8,128)(2,1)S(1)}, bf16[16,48,384]{2,1,0:T(8,128)(2,1)S(1)}) custom-call(s32[2,32]{1,0:T(2,128)S(1)} %copy-done.3, bf16[8,128,384]{2,1,0:T(8,128)(2,1)} %shard_map.193.kvs_ref, ...), custom_call_target="tpu_custom_call" | custom-call | flops 1000 | bytes 1000 | tf_op jit(solution)/shard_map/pallas_call | solution.py:106
  107.3 2.6 %shard_map.201 = (f32[32,768]{1,0:T(8,128)}, bf16[48,768]{1,0:T(8,128)(2,1)}, bf16[48,768]{1,0:T(8,128)(2,1)}, bf16[48,768]{1,0:T(8,128)(2,1)}, f32[8,768]{1,0:T(8,128)}, /*index=5*/bf16[2,48,768]{2,1,0:T(8,128)(2,1)}) custom-call(bf16[128,640]{1,0:T(8,128)(2,1)S(1)} %get-tuple-element.68.gqkv_ref, bf16[3,768,384]{2,1,0:T(8,128)(2,1)S(1)} %get-tuple-element.69.w_ref, ...), custom_call_target="tpu_custom_call" | custom-call | flops 1000 | bytes 1000 | tf_op jit(solution)/shard_map/pallas_call | solution.py:106
  111.0 6.0 %all-to-all-start.4 = ((bf16[16,48,384]{2,1,0:T(8,128)(2,1)}), bf16[16,48,384]{2,1,0:T(8,128)(2,1)S(1)}, u32[]{:S(2)}, u32[]{:S(2)}) async-start(bf16[16,48,384]{2,1,0:T(8,128)(2,1)} %shard_map.203), calls=%async_computation.4 | async-start | bytes 1179648 | tf_op jit(solution)/shard_map/all_to_all | solution.py:661
  117.8 3.4 %collective-permute-start.13 = (bf16[48,768]{1,0:T(8,128)(2,1)S(1)}, bf16[48,768]{1,0:T(8,128)(2,1)S(1)}, u32[]{:S(2)}, u32[]{:S(2)}) collective-permute-start(bf16[48,768]{1,0:T(8,128)(2,1)S(1)} %copy-done.5), channel_id=1, source_target_pairs={{0,3},{1,2},{2,1},{3,0},{4,7},{5,6},{6,5},{7,4},{8,11},{9,10},{10,... | collective-permute-start | bytes 221192 | tf_op jit(solution)/shard_map/ppermute | solution.py:681
  121.2 5.4 %collective-permute-done.11.refs_2_.one_ref = bf16[48,768]{1,0:T(8,128)(2,1)S(1)} collective-permute-done((bf16[48,768]{1,0:T(8,128)(2,1)S(1)}, bf16[48,768]{1,0:T(8,128)(2,1)S(1)}, u32[]{:S(2)}, u32[]{:S(2)}) %collective-permute-start.11) | collective-permute-done | bytes 73760 | tf_op jit(solution)/shard_map/ppermute | solution.py:681
  128.5 2.3 %shard_map.205.unused_ref = bf16[8,8,8,2432]{3,2,1,0:T(8,128)(2,1)} custom-call(bf16[16,48,384]{2,1,0:T(8,128)(2,1)S(1)} %shard_map.204.in_ref, f32[8,768]{1,0:T(8,128)} %get-tuple-element.79.refs_1_.vec_ref, bf16[48,768]{1,0:T(8,128)(2,1)S(1)} %collective-permute-done.11.refs_2_.one_ref, bf16[48,768]{1,0:T(8,128)(2,1)S(1)} %collective-permute-done.12.refs_3_.two_ref, ...), custom_call_target="tpu_custom_call" | custom-call | flops 1000 | bytes 1000 | tf_op jit(solution)/shard_map/pallas_call | solution.py:106
  130.8 9.5 %all-to-all-start.5 = ((bf16[64,8,2432]{2,1,0:T(8,128)(2,1)}), bf16[64,8,2432]{2,1,0:T(8,128)(2,1)S(1)}, u32[]{:S(2)}, u32[]{:S(2)}) async-start(bf16[64,8,2432]{2,1,0:T(8,128)(2,1)} %bitcast.7), calls=%async_computation.5 | async-start | bytes 4980736 | tf_op jit(solution)/shard_map/all_to_all | solution.py:661
  140.4 3.0 %shard_map.206.refs_1_.refs_0_ = bf16[8,64,768]{2,1,0:T(8,128)(2,1)} custom-call(f32[32,768]{1,0:T(8,128)} %get-tuple-element.71.unused_ref.own_ref, bf16[48,768]{1,0:T(8,128)(2,1)S(1)} %collective-permute-done.11.refs_2_.one_ref, bf16[48,768]{1,0:T(8,128)(2,1)S(1)} %collective-permute-done.12.refs_3_.two_ref, ...), custom_call_target="tpu_custom_call" | custom-call | flops 1000 | bytes 1000 | tf_op jit(solution)/shard_map/pallas_call | solution.py:106
  143.3 28.2 %all-to-all-done.5 = bf16[64,8,2432]{2,1,0:T(8,128)(2,1)S(1)} async-done(((bf16[64,8,2432]{2,1,0:T(8,128)(2,1)}), bf16[64,8,2432]{2,1,0:T(8,128)(2,1)S(1)}, u32[]{:S(2)}, u32[]{:S(2)}) %all-to-all-start.5) | async-done | bytes 2490400 | tf_op jit(solution)/shard_map/all_to_all | solution.py:661
  171.6 3.4 %collective-permute-start.15 = (bf16[8,8,8,2432]{3,2,1,0:T(8,128)(2,1)S(1)}, bf16[8,8,8,2432]{3,2,1,0:T(8,128)(2,1)}, u32[]{:S(2)}, u32[]{:S(2)}) collective-permute-start(bf16[8,8,8,2432]{3,2,1,0:T(8,128)(2,1)S(1)} %shard_map.207.refs_1_.in_ref), channel_id=1, source_target_pairs={{0,8},{8,0},{1,9},{9,1},{2,10},{10,2},{3,11},{11,3},{4,12},{12,4},... | collective-permute-start | bytes 7471112 | tf_op jit(solution)/shard_map/ppermute | solution.py:665
  174.9 3.6 %all-to-all-start.6 = ((bf16[8,64,768]{2,1,0:T(8,128)(2,1)}), bf16[8,64,768]{2,1,0:T(8,128)(2,1)S(1)}, u32[]{:S(2)}, u32[]{:S(2)}) async-start(bf16[8,64,768]{2,1,0:T(8,128)(2,1)} %shard_map.208), calls=%async_computation.6 | async-start | bytes 1572864 | tf_op jit(solution)/shard_map/all_to_all | solution.py:661
  183.7 2.4 %shard_map.209 = (f32[768,2304]{1,0:T(8,128)}, f32[768,768]{1,0:T(8,128)}, f32[4,8,128]{2,1,0:T(8,128)S(1)}) custom-call(bf16[8,8,8,2432]{3,2,1,0:T(8,128)(2,1)S(1)} %shard_map.207.refs_1_.in_ref), custom_call_target="tpu_custom_call" | custom-call | flops 1000 | bytes 1000 | tf_op jit(solution)/shard_map/pallas_call | solution.py:106
  186.2 4.1 %shard_map.210 = (f32[768,2304]{1,0:T(8,128)}, f32[768,768]{1,0:T(8,128)}, f32[768]{0:T(1024)}, f32[768]{0:T(1024)}, f32[768]{0:T(1024)}, /*index=5*/f32[768]{0:T(1024)}) custom-call(bf16[8,8,8,2432]{3,2,1,0:T(8,128)(2,1)} %collective-permute-done.15.in_ref, ...), custom_call_target="tpu_custom_call", output_to_operand_aliasing={{0}: (2, {}), {1}: (3, {})} | custom-call | flops 1000 | bytes 1000 | tf_op jit(solution)/shard_map/pallas_call | solution.py:106
  (76 shorter events, 31.5 us)
Async XLA Ops:
  4.3 17.6 %all-to-all-start = ((bf16[8,128,384]{2,1,0:T(8,128)(2,1)}), bf16[8,128,384]{2,1,0:T(8,128)(2,1)S(1)}, u32[]{:S(2)}, u32[]{:S(2)}) async-start(bf16[8,128,384]{2,1,0:T(8,128)(2,1)} %get-tuple-element.53), calls=%async_computation | async-start | bytes 1572864 | tf_op jit(solution)/shard_map/all_to_all | solution.py:661
  10.3 15.8 %copy-start.3 = (s32[2,32]{1,0:T(2,128)S(1)}, s32[2,32]{1,0:T(2,128)}, u32[]{:S(2)}) copy-start(s32[2,32]{1,0:T(2,128)} %scene_ref.3) | copy-start | bytes 772
  22.0 15.8 %copy-start = (bf16[8,128,384]{2,1,0:T(8,128)(2,1)}, bf16[8,128,384]{2,1,0:T(8,128)(2,1)S(1)}, u32[]{:S(2)}) copy-start(bf16[8,128,384]{2,1,0:T(8,128)(2,1)S(1)} %shard_map.188.same_ref.refs_0_) | copy-start | bytes 2359300
  22.0 4.1 %collective-permute-start = (bf16[8,128,384]{2,1,0:T(8,128)(2,1)S(1)}, bf16[8,128,384]{2,1,0:T(8,128)(2,1)S(1)}, u32[]{:S(2)}, u32[]{:S(2)}) collective-permute-start(bf16[8,128,384]{2,1,0:T(8,128)(2,1)S(1)} %shard_map.188.same_ref.refs_0_), channel_id=1, source_target_pairs={{0,8},{8,0},{1,9},{9,1},{2,10},{10,2},{3,11},{11,3},{4,12},{12,4},... | collective-permute-start | bytes 2359304 | tf_op jit(solution)/shard_map/ppermute | solution.py:665
  30.1 17.1 %all-to-all-start.1 = ((bf16[8,128,256]{2,1,0:T(8,128)(2,1)}), bf16[8,128,256]{2,1,0:T(8,128)(2,1)S(1)}, u32[]{:S(2)}, u32[]{:S(2)}) async-start(bf16[8,128,256]{2,1,0:T(8,128)(2,1)} %shard_map.189), calls=%async_computation.1 | async-start | bytes 1048576 | tf_op jit(solution)/shard_map/all_to_all | solution.py:661
  54.1 5.3 %collective-permute-start.2 = (bf16[8,48,768]{2,1,0:T(8,128)(2,1)}, bf16[8,48,768]{2,1,0:T(8,128)(2,1)}, u32[]{:S(2)}, u32[]{:S(2)}) collective-permute-start(bf16[8,48,768]{2,1,0:T(8,128)(2,1)} %get-tuple-element.63), channel_id=1, source_target_pairs={{0,8},{8,0},{1,9},{9,1},{2,10},{10,2},{3,11},{11,3},{4,12},{12,4},... | collective-permute-start | bytes 1769480 | tf_op jit(solution)/shard_map/ppermute | solution.py:665
  55.8 18.1 %all-to-all-start.2 = ((bf16[8,64,768]{2,1,0:T(8,128)(2,1)}), bf16[8,64,768]{2,1,0:T(8,128)(2,1)S(1)}, u32[]{:S(2)}, u32[]{:S(2)}) async-start(bf16[8,64,768]{2,1,0:T(8,128)(2,1)} %get-tuple-element.55), calls=%async_computation.2 | async-start | bytes 1572864 | tf_op jit(solution)/shard_map/all_to_all | solution.py:661
  61.3 15.5 %collective-permute-start.3 = (bf16[2,48,768]{2,1,0:T(8,128)(2,1)}, bf16[2,48,768]{2,1,0:T(8,128)(2,1)S(1)}, u32[]{:S(2)}, u32[]{:S(2)}) collective-permute-start(bf16[2,48,768]{2,1,0:T(8,128)(2,1)} %get-tuple-element.64), channel_id=1, source_target_pairs={{0,32},{32,0},{64,96},{96,64},{1,33},{33,1},{65,97},{97,65},{2,34}... | collective-permute-start | bytes 442376 | tf_op jit(solution)/shard_map/ppermute | solution.py:681
  61.3 15.5 %collective-permute-start.4 = (bf16[2,48,768]{2,1,0:T(8,128)(2,1)}, bf16[2,48,768]{2,1,0:T(8,128)(2,1)S(1)}, u32[]{:S(2)}, u32[]{:S(2)}) collective-permute-start(bf16[2,48,768]{2,1,0:T(8,128)(2,1)} %get-tuple-element.65), channel_id=1, source_target_pairs={{0,64},{32,96},{64,0},{96,32},{1,65},{33,97},{65,1},{97,33},{2,66}... | collective-permute-start | bytes 442376 | tf_op jit(solution)/shard_map/ppermute | solution.py:681
  63.9 12.9 %collective-permute-start.5 = (bf16[2,48,768]{2,1,0:T(8,128)(2,1)}, bf16[2,48,768]{2,1,0:T(8,128)(2,1)S(1)}, u32[]{:S(2)}, u32[]{:S(2)}) collective-permute-start(bf16[2,48,768]{2,1,0:T(8,128)(2,1)} %get-tuple-element.66), channel_id=1, source_target_pairs={{0,96},{32,64},{64,32},{96,0},{1,97},{33,65},{65,33},{97,1},{2,98}... | collective-permute-start | bytes 442376 | tf_op jit(solution)/shard_map/ppermute | solution.py:681
  76.9 19.8 %all-to-all-start.3 = ((bf16[32,112,128]{2,1,0:T(8,128)(2,1)}), bf16[32,112,128]{2,1,0:T(8,128)(2,1)S(1)}, u32[]{:S(2)}, u32[]{:S(2)}) async-start(bf16[32,112,128]{2,1,0:T(8,128)(2,1)} %bitcast.8), calls=%async_computation.3 | async-start | bytes 1835008 | tf_op jit(solution)/shard_map/all_to_all | solution.py:661
  80.8 15.8 %collective-permute-start.1 = (bf16[8,128,384]{2,1,0:T(8,128)(2,1)}, bf16[8,128,384]{2,1,0:T(8,128)(2,1)S(1)}, u32[]{:S(2)}, u32[]{:S(2)}) collective-permute-start(bf16[8,128,384]{2,1,0:T(8,128)(2,1)} %shard_map.193.kvs_ref), channel_id=1, source_target_pairs={{0,8},{8,0},{1,9},{9,1},{2,10},{10,2},{3,11},{11,3},{4,12},{12,4},... | collective-permute-start | bytes 2359304 | tf_op jit(solution)/shard_map/ppermute | solution.py:665
  81.7 12.7 %collective-permute-start.6 = (bf16[32,768]{1,0:T(8,128)(2,1)S(1)}, bf16[32,768]{1,0:T(8,128)(2,1)S(1)}, u32[]{:S(2)}, u32[]{:S(2)}) collective-permute-start(bf16[32,768]{1,0:T(8,128)(2,1)S(1)} %copy-done.2), channel_id=1, source_target_pairs={{0,1},{1,0},{2,3},{3,2},{4,5},{5,4},{6,7},{7,6},{8,9},{9,8},{10,11... | collective-permute-start | bytes 147464 | tf_op jit(solution)/shard_map/ppermute | solution.py:681
  84.6 9.8 %collective-permute-start.7 = (bf16[32,768]{1,0:T(8,128)(2,1)S(1)}, bf16[32,768]{1,0:T(8,128)(2,1)S(1)}, u32[]{:S(2)}, u32[]{:S(2)}) collective-permute-start(bf16[32,768]{1,0:T(8,128)(2,1)S(1)} %copy-done.2), channel_id=1, source_target_pairs={{0,2},{1,3},{2,0},{3,1},{4,6},{5,7},{6,4},{7,5},{8,10},{9,11},{10,... | collective-permute-start | bytes 147464 | tf_op jit(solution)/shard_map/ppermute | solution.py:681
  85.8 10.8 %collective-permute-start.8 = (bf16[32,768]{1,0:T(8,128)(2,1)S(1)}, bf16[32,768]{1,0:T(8,128)(2,1)S(1)}, u32[]{:S(2)}, u32[]{:S(2)}) collective-permute-start(bf16[32,768]{1,0:T(8,128)(2,1)S(1)} %copy-done.2), channel_id=1, source_target_pairs={{0,3},{1,2},{2,1},{3,0},{4,7},{5,6},{6,5},{7,4},{8,11},{9,10},{10,... | collective-permute-start | bytes 147464 | tf_op jit(solution)/shard_map/ppermute | solution.py:681
  96.7 4.1 %collective-permute-start.9 = (bf16[8,4,112,128]{3,2,1,0:T(8,128)(2,1)S(1)}, bf16[8,4,112,128]{3,2,1,0:T(8,128)(2,1)S(1)}, u32[]{:S(2)}, u32[]{:S(2)}) collective-permute-start(bf16[8,4,112,128]{3,2,1,0:T(8,128)(2,1)S(1)} %shard_map.198.gs_ref), channel_id=1, source_target_pairs={{0,8},{8,0},{1,9},{9,1},{2,10},{10,2},{3,11},{11,3},{4,12},{12,4},... | collective-permute-start | bytes 2752520 | tf_op jit(solution)/shard_map/ppermute | solution.py:665
  100.7 5.8 %collective-permute-start.10 = (bf16[2,48,768]{2,1,0:T(8,128)(2,1)}, bf16[2,48,768]{2,1,0:T(8,128)(2,1)S(1)}, u32[]{:S(2)}, u32[]{:S(2)}) collective-permute-start(bf16[2,48,768]{2,1,0:T(8,128)(2,1)} %shard_map.200.near_ref), channel_id=1, source_target_pairs={{0,16},{16,0},{1,17},{17,1},{2,18},{18,2},{3,19},{19,3},{4,20},{20... | collective-permute-start | bytes 442376 | tf_op jit(solution)/shard_map/ppermute | solution.py:681
  106.6 3.4 %collective-permute-start.14 = (bf16[16,48,384]{2,1,0:T(8,128)(2,1)S(1)}, bf16[16,48,384]{2,1,0:T(8,128)(2,1)S(1)}, u32[]{:S(2)}, u32[]{:S(2)}) collective-permute-start(bf16[16,48,384]{2,1,0:T(8,128)(2,1)S(1)} %shard_map.202), channel_id=1, source_target_pairs={{0,8},{8,0},{1,9},{9,1},{2,10},{10,2},{3,11},{11,3},{4,12},{12,4},... | collective-permute-start | bytes 1769480 | tf_op jit(solution)/shard_map/ppermute | solution.py:665
  111.0 17.5 %all-to-all-start.4 = ((bf16[16,48,384]{2,1,0:T(8,128)(2,1)}), bf16[16,48,384]{2,1,0:T(8,128)(2,1)S(1)}, u32[]{:S(2)}, u32[]{:S(2)}) async-start(bf16[16,48,384]{2,1,0:T(8,128)(2,1)} %shard_map.203), calls=%async_computation.4 | async-start | bytes 1179648 | tf_op jit(solution)/shard_map/all_to_all | solution.py:661
  117.0 9.6 %collective-permute-start.11 = (bf16[48,768]{1,0:T(8,128)(2,1)S(1)}, bf16[48,768]{1,0:T(8,128)(2,1)S(1)}, u32[]{:S(2)}, u32[]{:S(2)}) collective-permute-start(bf16[48,768]{1,0:T(8,128)(2,1)S(1)} %copy-done.7), channel_id=1, source_target_pairs={{0,1},{1,0},{2,3},{3,2},{4,5},{5,4},{6,7},{7,6},{8,9},{9,8},{10,11... | collective-permute-start | bytes 221192 | tf_op jit(solution)/shard_map/ppermute | solution.py:681
  117.8 8.8 %collective-permute-start.12 = (bf16[48,768]{1,0:T(8,128)(2,1)S(1)}, bf16[48,768]{1,0:T(8,128)(2,1)S(1)}, u32[]{:S(2)}, u32[]{:S(2)}) collective-permute-start(bf16[48,768]{1,0:T(8,128)(2,1)S(1)} %copy-done.6), channel_id=1, source_target_pairs={{0,2},{1,3},{2,0},{3,1},{4,6},{5,7},{6,4},{7,5},{8,10},{9,11},{10,... | collective-permute-start | bytes 221192 | tf_op jit(solution)/shard_map/ppermute | solution.py:681
  117.8 10.7 %collective-permute-start.13 = (bf16[48,768]{1,0:T(8,128)(2,1)S(1)}, bf16[48,768]{1,0:T(8,128)(2,1)S(1)}, u32[]{:S(2)}, u32[]{:S(2)}) collective-permute-start(bf16[48,768]{1,0:T(8,128)(2,1)S(1)} %copy-done.5), channel_id=1, source_target_pairs={{0,3},{1,2},{2,1},{3,0},{4,7},{5,6},{6,5},{7,4},{8,11},{9,10},{10,... | collective-permute-start | bytes 221192 | tf_op jit(solution)/shard_map/ppermute | solution.py:681
  130.8 40.7 %all-to-all-start.5 = ((bf16[64,8,2432]{2,1,0:T(8,128)(2,1)}), bf16[64,8,2432]{2,1,0:T(8,128)(2,1)S(1)}, u32[]{:S(2)}, u32[]{:S(2)}) async-start(bf16[64,8,2432]{2,1,0:T(8,128)(2,1)} %bitcast.7), calls=%async_computation.5 | async-start | bytes 4980736 | tf_op jit(solution)/shard_map/all_to_all | solution.py:661
  171.6 14.6 %collective-permute-start.15 = (bf16[8,8,8,2432]{3,2,1,0:T(8,128)(2,1)S(1)}, bf16[8,8,8,2432]{3,2,1,0:T(8,128)(2,1)}, u32[]{:S(2)}, u32[]{:S(2)}) collective-permute-start(bf16[8,8,8,2432]{3,2,1,0:T(8,128)(2,1)S(1)} %shard_map.207.refs_1_.in_ref), channel_id=1, source_target_pairs={{0,8},{8,0},{1,9},{9,1},{2,10},{10,2},{3,11},{11,3},{4,12},{12,4},... | collective-permute-start | bytes 7471112 | tf_op jit(solution)/shard_map/ppermute | solution.py:665
  174.9 19.8 %all-to-all-start.6 = ((bf16[8,64,768]{2,1,0:T(8,128)(2,1)}), bf16[8,64,768]{2,1,0:T(8,128)(2,1)S(1)}, u32[]{:S(2)}, u32[]{:S(2)}) async-start(bf16[8,64,768]{2,1,0:T(8,128)(2,1)} %shard_map.208), calls=%async_computation.6 | async-start | bytes 1572864 | tf_op jit(solution)/shard_map/all_to_all | solution.py:661
  178.5 11.7 %collective-permute-start.17 = (bf16[2,48,768]{2,1,0:T(8,128)(2,1)S(1)}, bf16[2,48,768]{2,1,0:T(8,128)(2,1)S(1)}, u32[]{:S(2)}, u32[]{:S(2)}) collective-permute-start(bf16[2,48,768]{2,1,0:T(8,128)(2,1)S(1)} %copy-done.4), channel_id=1, source_target_pairs={{0,32},{32,0},{64,96},{96,64},{1,33},{33,1},{65,97},{97,65},{2,34}... | collective-permute-start | bytes 442376 | tf_op jit(solution)/shard_map/ppermute | solution.py:681
  178.9 11.4 %collective-permute-start.19 = (bf16[2,48,768]{2,1,0:T(8,128)(2,1)S(1)}, bf16[2,48,768]{2,1,0:T(8,128)(2,1)S(1)}, u32[]{:S(2)}, u32[]{:S(2)}) collective-permute-start(bf16[2,48,768]{2,1,0:T(8,128)(2,1)S(1)} %copy-done.4), channel_id=1, source_target_pairs={{0,64},{32,96},{64,0},{96,32},{1,65},{33,97},{65,1},{97,33},{2,66}... | collective-permute-start | bytes 442376 | tf_op jit(solution)/shard_map/ppermute | solution.py:681
  180.8 10.1 %collective-permute-start.21 = (bf16[2,48,768]{2,1,0:T(8,128)(2,1)S(1)}, bf16[2,48,768]{2,1,0:T(8,128)(2,1)S(1)}, u32[]{:S(2)}, u32[]{:S(2)}) collective-permute-start(bf16[2,48,768]{2,1,0:T(8,128)(2,1)S(1)} %copy-done.4), channel_id=1, source_target_pairs={{0,96},{32,64},{64,32},{96,0},{1,97},{33,65},{65,33},{97,1},{2,98}... | collective-permute-start | bytes 442376 | tf_op jit(solution)/shard_map/ppermute | solution.py:681
  182.5 11.0 %collective-permute-start.16 = (bf16[2,48,768]{2,1,0:T(8,128)(2,1)S(1)}, bf16[2,48,768]{2,1,0:T(8,128)(2,1)S(1)}, u32[]{:S(2)}, u32[]{:S(2)}) collective-permute-start(bf16[2,48,768]{2,1,0:T(8,128)(2,1)S(1)} %copy-done.4), channel_id=1, source_target_pairs={{0,8},{8,0},{1,9},{9,1},{2,10},{10,2},{3,11},{11,3},{4,12},{12,4},... | collective-permute-start | bytes 442376 | tf_op jit(solution)/shard_map/ppermute | solution.py:665
  190.3 3.2 %collective-permute-start.18 = (bf16[2,48,768]{2,1,0:T(8,128)(2,1)S(1)}, bf16[2,48,768]{2,1,0:T(8,128)(2,1)S(1)}, u32[]{:S(2)}, u32[]{:S(2)}) collective-permute-start(bf16[2,48,768]{2,1,0:T(8,128)(2,1)S(1)} %shard_map.211.refs_1_), channel_id=1, source_target_pairs={{0,8},{8,0},{1,9},{9,1},{2,10},{10,2},{3,11},{11,3},{4,12},{12,4},... | collective-permute-start | bytes 442376 | tf_op jit(solution)/shard_map/ppermute | solution.py:665
  190.4 3.1 %collective-permute-start.20 = (bf16[2,48,768]{2,1,0:T(8,128)(2,1)S(1)}, bf16[2,48,768]{2,1,0:T(8,128)(2,1)S(1)}, u32[]{:S(2)}, u32[]{:S(2)}) collective-permute-start(bf16[2,48,768]{2,1,0:T(8,128)(2,1)S(1)} %shard_map.212.refs_2_), channel_id=1, source_target_pairs={{0,8},{8,0},{1,9},{9,1},{2,10},{10,2},{3,11},{11,3},{4,12},{12,4},... | collective-permute-start | bytes 442376 | tf_op jit(solution)/shard_map/ppermute | solution.py:665
  190.9 2.6 %collective-permute-start.22 = (bf16[2,48,768]{2,1,0:T(8,128)(2,1)S(1)}, bf16[2,48,768]{2,1,0:T(8,128)(2,1)S(1)}, u32[]{:S(2)}, u32[]{:S(2)}) collective-permute-start(bf16[2,48,768]{2,1,0:T(8,128)(2,1)S(1)} %shard_map.213.refs_3_), channel_id=1, source_target_pairs={{0,8},{8,0},{1,9},{9,1},{2,10},{10,2},{3,11},{11,3},{4,12},{12,4},... | collective-permute-start | bytes 442376 | tf_op jit(solution)/shard_map/ppermute | solution.py:665
  (6 other events, 40.6 us)

commit v21 on v20

--- a/solution.py
+++ b/solution.py
@@ -204,13 +204,13 @@
             [ref[pl.ds(first, count)].reshape(rows, 384) for ref in (same_ref, other_ref)], axis=0
         )
         load.wait()
-        query = q_buf[...]
+        query = q_buf[...] * jnp.asarray(HD**-0.5, BF)
         q0, q1 = halves(query[:, :128])
         blocks = [keys[:, :128], keys[:, 128:256], keys[:, 256:]]
         mixed = []
         columns = []
         for qh, kb, vb in ((q0, 0, 1), (q1, 0, 2), (query[:, 128:], 1, 2)):
-            scores = mm_nt(qh, blocks[kb]) * (HD**-0.5)
+            scores = mm_nt(qh, blocks[kb])
             top = jnp.max(scores, axis=-1, keepdims=True)
             weights = jnp.exp(scores - top)
             total = jnp.sum(weights, axis=-1, keepdims=True)
@@ -420,8 +420,9 @@
             [kv_buf[:count].reshape(rows, 384), kvo_ref[pl.ds(first, count)].reshape(rows, 384)], axis=0
         ))
         own = cut(kv_buf[chip - first]) + g_own[2:]
-        q_heads = [*halves(own[3]), halves(own[4])[0]]
-        k_heads = [*halves(own[0]), halves(own[1])[0]]
+        small = jnp.asarray(scale, BF)
+        q_heads = [*halves(own[3] * small), halves(own[4] * small)[0]]
+        k_heads = [*halves(own[0] * small), halves(own[1] * small)[0]]
         v_heads = [halves(own[1])[1], *halves(own[2])]
 
         def column(at):
@@ -433,10 +434,10 @@
         dq, dk, dv = [], [], []
         for head, (kb, vb) in enumerate(((0, 1), (0, 2), (1, 2))):
             qb, gb = (0, 0, 1)[head], (0, 1, 1)[head]
-            probs = jnp.exp(mm_nt(q_heads[head], kv[kb]) * scale - column(3 * head))
+            probs = jnp.exp(mm_nt(q_heads[head], kv[kb]) - column(3 * head))
             gap = mm_nt(g_heads[head], kv[vb]) - column(9 + 3 * head)
             dq.append(mm((probs * gap).astype(BF), kv[kb]) * scale)
-            probs = jnp.exp(mm_nt(k_heads[head], query[qb]) * scale - row(3 * head))
+            probs = jnp.exp(mm_nt(k_heads[head], query[qb]) - row(3 * head))
             gap = mm_nt(v_heads[head], grad[gb]) - row(9 + 3 * head)
             dv.append(mm(probs.astype(BF), grad[gb]))
             dk.append(mm((probs * gap).astype(BF), query[qb]) * scale)

time: 197 us -> 197 us (level)
  Pallas kernels: 51.7 us -> 49.6 us
    pallas_call x19, Pallas kernels: 51.6 us -> 49.6 us  [call(): pl.pallas_call(kernel, out_shape=[(pltpu.HBM if place in 'HL' else jax.Sh...]
  transfers between devices with their start and end apart: 30 -> 30, of which waited for: 10 -> 11; matrix products, arithmetic and copies ran while one was open for 1% -> 1% of each run, Pallas kernels for 17% -> 16%
where the time goes in v21:
time: 197 us; the launch traced here: 196 us
  waiting for transfers between devices  73.7 us (37%)
  starting transfers between devices  70 us (36%)
  Pallas kernels  49.6 us (25%)
    all_to_all x7, waiting for transfers between devices, exchange(): return lax.all_to_all(value, axes, 0, 0, tiled=True)  52.6 us
    pallas_call x19, Pallas kernels, call(): pl.pallas_call(kernel, out_shape=[(pltpu.HBM if place in 'HL' else jax.Sh...  49.6 us
    all_to_all x7, starting transfers between devices, exchange(): return lax.all_to_all(value, axes, 0, 0, tiled=True)  39.8 us
    ppermute x13, waiting for transfers between devices, flip(): lax.ppermute(value, axes, [(index, index ^ bits) for index in range(count)])  17.1 us
    ppermute x13, starting transfers between devices, flip(): lax.ppermute(value, axes, [(index, index ^ bits) for index in range(count)])  16.5 us
    ppermute x10, starting transfers between devices, swap(): return lax.ppermute(value, CORE, [(0, 1), (1, 0)])  13.7 us
    ppermute x10, waiting for transfers between devices, swap(): return lax.ppermute(value, CORE, [(0, 1), (1, 0)])  4.03 us
  transfers between devices with their start and end apart: 30, of which 11 were waited for; matrix products, arithmetic and copies ran while one was open for 1% of the time, Pallas kernels for 16%

profile of v21, /device:TPU:1, one launch (start us, length us, event | category | flops | bytes accessed | tf_op | source)
XLA Modules:
  0.0 195.7 jit_solution(17652780030911329388)
XLA Ops:
  0.6 3.7 %shard_map.186 = (bf16[8,128,384]{2,1,0:T(8,128)(2,1)}, bf16[128,768]{1,0:T(8,128)(2,1)}) custom-call(bf16[2,128,768]{2,1,0:T(8,128)(2,1)} %tok_ref.7, f32[768]{0:T(1024)} %gain_ref.7, f32[768]{0:T(1024)} %shift_ref.2, bf16[768,2304]{1,0:T(8,128)(2,1)} %w_ref.7), custom_call_target="tpu_custom_call" | custom-call | flops 1000 | bytes 1000 | tf_op jit(solution)/shard_map/pallas_call | solution.py:106
  4.3 6.0 %all-to-all-start = ((bf16[8,128,384]{2,1,0:T(8,128)(2,1)}), bf16[8,128,384]{2,1,0:T(8,128)(2,1)S(1)}, u32[]{:S(2)}, u32[]{:S(2)}) async-start(bf16[8,128,384]{2,1,0:T(8,128)(2,1)} %get-tuple-element.53), calls=%async_computation | async-start | bytes 1572864 | tf_op jit(solution)/shard_map/all_to_all | solution.py:662
  10.3 3.0 %shard_map.187.refs_1_.q_ref = bf16[128,256]{1,0:T(8,128)(2,1)} custom-call(bf16[128,768]{1,0:T(8,128)(2,1)} %get-tuple-element.54.normed_ref, bf16[768,2304]{1,0:T(8,128)(2,1)} %w_ref.7), custom_call_target="tpu_custom_call" | custom-call | flops 1000 | bytes 1000 | tf_op jit(solution)/shard_map/pallas_call | solution.py:106
  13.4 8.6 %all-to-all-done.refs_0_ = bf16[8,128,384]{2,1,0:T(8,128)(2,1)S(1)} async-done(((bf16[8,128,384]{2,1,0:T(8,128)(2,1)}), bf16[8,128,384]{2,1,0:T(8,128)(2,1)S(1)}, u32[]{:S(2)}, u32[]{:S(2)}) %all-to-all-start) | async-done | bytes 786464 | tf_op jit(solution)/shard_map/all_to_all | solution.py:662
  22.0 2.2 %collective-permute-start = (bf16[8,128,384]{2,1,0:T(8,128)(2,1)S(1)}, bf16[8,128,384]{2,1,0:T(8,128)(2,1)S(1)}, u32[]{:S(2)}, u32[]{:S(2)}) collective-permute-start(bf16[8,128,384]{2,1,0:T(8,128)(2,1)S(1)} %shard_map.188.same_ref.refs_0_), channel_id=1, source_target_pairs={{0,8},{8,0},{1,9},{9,1},{2,10},{10,2},{3,11},{11,3},{4,12},{12,4},... | collective-permute-start | bytes 2359304 | tf_op jit(solution)/shard_map/ppermute | solution.py:666
  26.1 3.1 %shard_map.189 = bf16[8,128,256]{2,1,0:T(8,128)(2,1)} custom-call(s32[2,32]{1,0:T(2,128)S(1)} %copy-done.3, bf16[128,256]{1,0:T(8,128)(2,1)} %shard_map.187.refs_1_.q_ref, bf16[8,128,384]{2,1,0:T(8,128)(2,1)S(1)} %shard_map.188.same_ref.refs_0_, bf16[8,128,384]{2,1,0:T(8,128)(2,1)S(1)} %collective-permute-done.other_ref), custom_call_target="tpu_custom_call" | custom-call | flops 1000 | bytes 1000 | tf_op jit(solution)/shard_map/pallas_call | solution.py:106
  29.2 7.2 %all-to-all-start.1 = ((bf16[8,128,256]{2,1,0:T(8,128)(2,1)}), bf16[8,128,256]{2,1,0:T(8,128)(2,1)S(1)}, u32[]{:S(2)}, u32[]{:S(2)}) async-start(bf16[8,128,256]{2,1,0:T(8,128)(2,1)} %shard_map.189), calls=%async_computation.1 | async-start | bytes 1048576 | tf_op jit(solution)/shard_map/all_to_all | solution.py:662
  37.8 9.4 %all-to-all-done.1.mixed_ref = bf16[8,128,256]{2,1,0:T(8,128)(2,1)S(1)} async-done(((bf16[8,128,256]{2,1,0:T(8,128)(2,1)}), bf16[8,128,256]{2,1,0:T(8,128)(2,1)S(1)}, u32[]{:S(2)}, u32[]{:S(2)}) %all-to-all-start.1) | async-done | bytes 524320 | tf_op jit(solution)/shard_map/all_to_all | solution.py:662
  47.1 4.1 %shard_map.190 = (bf16[8,64,768]{2,1,0:T(8,128)(2,1)}, f32[32,768]{1,0:T(8,128)}, bf16[256,768]{1,0:T(8,128)(2,1)S(1)}, bf16[256,384]{1,0:T(8,128)(2,1)S(1)}, bf16[256,384]{1,0:T(8,128)(2,1)S(1)}) custom-call(bf16[8,128,256]{2,1,0:T(8,128)(2,1)S(1)} %all-to-all-done.1.mixed_ref, bf16[2,128,768]{2,1,0:T(8,128)(2,1)} %tok_ref.7, bf16[2,128,768]{2,1,0:T(8,128)(2,1)} %og_ref.5, ...), custom_call_target="tpu_custom_call" | custom-call | flops 1000 | bytes 1000 | tf_op jit(solution)/shard_map/pallas_call | solution.py:106
  51.3 2.8 %shard_map.194 = (bf16[8,48,768]{2,1,0:T(8,128)(2,1)S(1)}, bf16[8,48,768]{2,1,0:T(8,128)(2,1)}) custom-call(bf16[256,768]{1,0:T(8,128)(2,1)S(1)} %get-tuple-element.59.normed_ref, bf16[256,384]{1,0:T(8,128)(2,1)S(1)} %get-tuple-element.60.act_ref, bf16[256,384]{1,0:T(8,128)(2,1)S(1)} %get-tuple-element.61.gpre_ref, bf16[2,128,768]{2,1,0:T(8,128)(2,1)} %og_ref.5), custom_call_target="tpu_custom_call" | custom-call | flops 1000 | bytes 1000 | tf_op jit(solution)/shard_map/pallas_call | solution.py:106
  55.8 3.5 %all-to-all-start.2 = ((bf16[8,64,768]{2,1,0:T(8,128)(2,1)}), bf16[8,64,768]{2,1,0:T(8,128)(2,1)S(1)}, u32[]{:S(2)}, u32[]{:S(2)}) async-start(bf16[8,64,768]{2,1,0:T(8,128)(2,1)} %get-tuple-element.55), calls=%async_computation.2 | async-start | bytes 1572864 | tf_op jit(solution)/shard_map/all_to_all | solution.py:662
  61.3 2.6 %collective-permute-start.4 = (bf16[2,48,768]{2,1,0:T(8,128)(2,1)}, bf16[2,48,768]{2,1,0:T(8,128)(2,1)S(1)}, u32[]{:S(2)}, u32[]{:S(2)}) collective-permute-start(bf16[2,48,768]{2,1,0:T(8,128)(2,1)} %get-tuple-element.65), channel_id=1, source_target_pairs={{0,64},{32,96},{64,0},{96,32},{1,65},{33,97},{65,1},{97,33},{2,66}... | collective-permute-start | bytes 442376 | tf_op jit(solution)/shard_map/ppermute | solution.py:682
  65.2 2.3 %shard_map.191.query_ref = bf16[4,32,256]{2,1,0:T(8,128)(2,1)} custom-call(bf16[128,768]{1,0:T(8,128)(2,1)} %get-tuple-element.54.normed_ref, bf16[768,2304]{1,0:T(8,128)(2,1)} %w_ref.7), custom_call_target="tpu_custom_call" | custom-call | flops 1000 | bytes 1000 | tf_op jit(solution)/shard_map/pallas_call | solution.py:106
  67.5 6.4 %all-to-all-done.2.sums_ref = bf16[8,64,768]{2,1,0:T(8,128)(2,1)S(1)} async-done(((bf16[8,64,768]{2,1,0:T(8,128)(2,1)}), bf16[8,64,768]{2,1,0:T(8,128)(2,1)S(1)}, u32[]{:S(2)}, u32[]{:S(2)}) %all-to-all-start.2) | async-done | bytes 786464 | tf_op jit(solution)/shard_map/all_to_all | solution.py:662
  73.9 2.9 %shard_map.192 = (bf16[8,4,112,128]{3,2,1,0:T(8,128)(2,1)}, bf16[32,768]{1,0:T(8,128)(2,1)}, f32[32,768]{1,0:T(8,128)}, bf16[32,768]{1,0:T(8,128)(2,1)}, f32[8,768]{1,0:T(8,128)}) custom-call(bf16[8,64,768]{2,1,0:T(8,128)(2,1)S(1)} %all-to-all-done.2.sums_ref, f32[32,768]{1,0:T(8,128)} %get-tuple-element.56.middle_ref, bf16[2,128,768]{2,1,0:T(8,128)(2,1)} %og_ref.5, ...), custom_call_target="tpu_custom_call" | custom-call | flops 1000 | bytes 1000 | tf_op jit(solution)/shard_map/pallas_call | solution.py:106
  76.8 3.9 %all-to-all-start.3 = ((bf16[32,112,128]{2,1,0:T(8,128)(2,1)}), bf16[32,112,128]{2,1,0:T(8,128)(2,1)S(1)}, u32[]{:S(2)}, u32[]{:S(2)}) async-start(bf16[32,112,128]{2,1,0:T(8,128)(2,1)} %bitcast.8), calls=%async_computation.3 | async-start | bytes 1835008 | tf_op jit(solution)/shard_map/all_to_all | solution.py:662
  81.7 2.9 %collective-permute-start.6 = (bf16[32,768]{1,0:T(8,128)(2,1)S(1)}, bf16[32,768]{1,0:T(8,128)(2,1)S(1)}, u32[]{:S(2)}, u32[]{:S(2)}) collective-permute-start(bf16[32,768]{1,0:T(8,128)(2,1)S(1)} %copy-done.2), channel_id=1, source_target_pairs={{0,1},{1,0},{2,3},{3,2},{4,5},{5,4},{6,7},{7,6},{8,9},{9,8},{10,11... | collective-permute-start | bytes 147464 | tf_op jit(solution)/shard_map/ppermute | solution.py:682
  87.5 6.9 %collective-permute-done.6.refs_1_.low1_ref = bf16[32,768]{1,0:T(8,128)(2,1)S(1)} collective-permute-done((bf16[32,768]{1,0:T(8,128)(2,1)S(1)}, bf16[32,768]{1,0:T(8,128)(2,1)S(1)}, u32[]{:S(2)}, u32[]{:S(2)}) %collective-permute-start.6) | collective-permute-done | bytes 49184 | tf_op jit(solution)/shard_map/ppermute | solution.py:682
  94.4 2.3 %collective-permute-done.8.refs_3_.low3_ref = bf16[32,768]{1,0:T(8,128)(2,1)S(1)} collective-permute-done((bf16[32,768]{1,0:T(8,128)(2,1)S(1)}, bf16[32,768]{1,0:T(8,128)(2,1)S(1)}, u32[]{:S(2)}, u32[]{:S(2)}) %collective-permute-start.8) | collective-permute-done | bytes 49184 | tf_op jit(solution)/shard_map/ppermute | solution.py:682
  101.0 4.3 %shard_map.199 = (bf16[128,640]{1,0:T(8,128)(2,1)S(1)}, bf16[3,768,384]{2,1,0:T(8,128)(2,1)S(1)}, bf16[16,48,384]{2,1,0:T(8,128)(2,1)S(1)}, bf16[16,48,384]{2,1,0:T(8,128)(2,1)S(1)}) custom-call(s32[2,32]{1,0:T(2,128)S(1)} %copy-done.3, bf16[8,128,384]{2,1,0:T(8,128)(2,1)} %shard_map.193.kvs_ref, ...), custom_call_target="tpu_custom_call" | custom-call | flops 1000 | bytes 1000 | tf_op jit(solution)/shard_map/pallas_call | solution.py:106
  107.2 2.6 %shard_map.201 = (f32[32,768]{1,0:T(8,128)}, bf16[48,768]{1,0:T(8,128)(2,1)}, bf16[48,768]{1,0:T(8,128)(2,1)}, bf16[48,768]{1,0:T(8,128)(2,1)}, f32[8,768]{1,0:T(8,128)}, /*index=5*/bf16[2,48,768]{2,1,0:T(8,128)(2,1)}) custom-call(bf16[128,640]{1,0:T(8,128)(2,1)S(1)} %get-tuple-element.68.gqkv_ref, bf16[3,768,384]{2,1,0:T(8,128)(2,1)S(1)} %get-tuple-element.69.w_ref, ...), custom_call_target="tpu_custom_call" | custom-call | flops 1000 | bytes 1000 | tf_op jit(solution)/shard_map/pallas_call | solution.py:106
  110.9 6.1 %all-to-all-start.4 = ((bf16[16,48,384]{2,1,0:T(8,128)(2,1)}), bf16[16,48,384]{2,1,0:T(8,128)(2,1)S(1)}, u32[]{:S(2)}, u32[]{:S(2)}) async-start(bf16[16,48,384]{2,1,0:T(8,128)(2,1)} %shard_map.203), calls=%async_computation.4 | async-start | bytes 1179648 | tf_op jit(solution)/shard_map/all_to_all | solution.py:662
  117.8 3.4 %collective-permute-start.13 = (bf16[48,768]{1,0:T(8,128)(2,1)S(1)}, bf16[48,768]{1,0:T(8,128)(2,1)S(1)}, u32[]{:S(2)}, u32[]{:S(2)}) collective-permute-start(bf16[48,768]{1,0:T(8,128)(2,1)S(1)} %copy-done.5), channel_id=1, source_target_pairs={{0,3},{1,2},{2,1},{3,0},{4,7},{5,6},{6,5},{7,4},{8,11},{9,10},{10,... | collective-permute-start | bytes 221192 | tf_op jit(solution)/shard_map/ppermute | solution.py:682
  121.2 5.4 %collective-permute-done.11.refs_2_.one_ref = bf16[48,768]{1,0:T(8,128)(2,1)S(1)} collective-permute-done((bf16[48,768]{1,0:T(8,128)(2,1)S(1)}, bf16[48,768]{1,0:T(8,128)(2,1)S(1)}, u32[]{:S(2)}, u32[]{:S(2)}) %collective-permute-start.11) | collective-permute-done | bytes 73760 | tf_op jit(solution)/shard_map/ppermute | solution.py:682
  128.5 2.3 %shard_map.205.unused_ref = bf16[8,8,8,2432]{3,2,1,0:T(8,128)(2,1)} custom-call(bf16[16,48,384]{2,1,0:T(8,128)(2,1)S(1)} %shard_map.204.in_ref, f32[8,768]{1,0:T(8,128)} %get-tuple-element.79.refs_1_.vec_ref, bf16[48,768]{1,0:T(8,128)(2,1)S(1)} %collective-permute-done.11.refs_2_.one_ref, bf16[48,768]{1,0:T(8,128)(2,1)S(1)} %collective-permute-done.12.refs_3_.two_ref, ...), custom_call_target="tpu_custom_call" | custom-call | flops 1000 | bytes 1000 | tf_op jit(solution)/shard_map/pallas_call | solution.py:106
  130.8 9.5 %all-to-all-start.5 = ((bf16[64,8,2432]{2,1,0:T(8,128)(2,1)}), bf16[64,8,2432]{2,1,0:T(8,128)(2,1)S(1)}, u32[]{:S(2)}, u32[]{:S(2)}) async-start(bf16[64,8,2432]{2,1,0:T(8,128)(2,1)} %bitcast.7), calls=%async_computation.5 | async-start | bytes 4980736 | tf_op jit(solution)/shard_map/all_to_all | solution.py:662
  140.3 3.0 %shard_map.206.refs_1_.refs_0_ = bf16[8,64,768]{2,1,0:T(8,128)(2,1)} custom-call(f32[32,768]{1,0:T(8,128)} %get-tuple-element.71.unused_ref.own_ref, bf16[48,768]{1,0:T(8,128)(2,1)S(1)} %collective-permute-done.11.refs_2_.one_ref, bf16[48,768]{1,0:T(8,128)(2,1)S(1)} %collective-permute-done.12.refs_3_.two_ref, ...), custom_call_target="tpu_custom_call" | custom-call | flops 1000 | bytes 1000 | tf_op jit(solution)/shard_map/pallas_call | solution.py:106
  143.3 28.2 %all-to-all-done.5 = bf16[64,8,2432]{2,1,0:T(8,128)(2,1)S(1)} async-done(((bf16[64,8,2432]{2,1,0:T(8,128)(2,1)}), bf16[64,8,2432]{2,1,0:T(8,128)(2,1)S(1)}, u32[]{:S(2)}, u32[]{:S(2)}) %all-to-all-start.5) | async-done | bytes 2490400 | tf_op jit(solution)/shard_map/all_to_all | solution.py:662
  171.5 3.4 %collective-permute-start.15 = (bf16[8,8,8,2432]{3,2,1,0:T(8,128)(2,1)S(1)}, bf16[8,8,8,2432]{3,2,1,0:T(8,128)(2,1)}, u32[]{:S(2)}, u32[]{:S(2)}) collective-permute-start(bf16[8,8,8,2432]{3,2,1,0:T(8,128)(2,1)S(1)} %shard_map.207.refs_1_.in_ref), channel_id=1, source_target_pairs={{0,8},{8,0},{1,9},{9,1},{2,10},{10,2},{3,11},{11,3},{4,12},{12,4},... | collective-permute-start | bytes 7471112 | tf_op jit(solution)/shard_map/ppermute | solution.py:666
  174.9 3.6 %all-to-all-start.6 = ((bf16[8,64,768]{2,1,0:T(8,128)(2,1)}), bf16[8,64,768]{2,1,0:T(8,128)(2,1)S(1)}, u32[]{:S(2)}, u32[]{:S(2)}) async-start(bf16[8,64,768]{2,1,0:T(8,128)(2,1)} %shard_map.208), calls=%async_computation.6 | async-start | bytes 1572864 | tf_op jit(solution)/shard_map/all_to_all | solution.py:662
  183.7 2.4 %shard_map.209 = (f32[768,2304]{1,0:T(8,128)}, f32[768,768]{1,0:T(8,128)}, f32[4,8,128]{2,1,0:T(8,128)S(1)}) custom-call(bf16[8,8,8,2432]{3,2,1,0:T(8,128)(2,1)S(1)} %shard_map.207.refs_1_.in_ref), custom_call_target="tpu_custom_call" | custom-call | flops 1000 | bytes 1000 | tf_op jit(solution)/shard_map/pallas_call | solution.py:106
  186.2 4.1 %shard_map.210 = (f32[768,2304]{1,0:T(8,128)}, f32[768,768]{1,0:T(8,128)}, f32[768]{0:T(1024)}, f32[768]{0:T(1024)}, f32[768]{0:T(1024)}, /*index=5*/f32[768]{0:T(1024)}) custom-call(bf16[8,8,8,2432]{3,2,1,0:T(8,128)(2,1)} %collective-permute-done.15.in_ref, ...), custom_call_target="tpu_custom_call", output_to_operand_aliasing={{0}: (2, {}), {1}: (3, {})} | custom-call | flops 1000 | bytes 1000 | tf_op jit(solution)/shard_map/pallas_call | solution.py:106
  (76 shorter events, 32.6 us)
Async XLA Ops:
  4.3 17.6 %all-to-all-start = ((bf16[8,128,384]{2,1,0:T(8,128)(2,1)}), bf16[8,128,384]{2,1,0:T(8,128)(2,1)S(1)}, u32[]{:S(2)}, u32[]{:S(2)}) async-start(bf16[8,128,384]{2,1,0:T(8,128)(2,1)} %get-tuple-element.53), calls=%async_computation | async-start | bytes 1572864 | tf_op jit(solution)/shard_map/all_to_all | solution.py:662
  10.3 15.8 %copy-start.3 = (s32[2,32]{1,0:T(2,128)S(1)}, s32[2,32]{1,0:T(2,128)}, u32[]{:S(2)}) copy-start(s32[2,32]{1,0:T(2,128)} %scene_ref.3) | copy-start | bytes 772
  22.0 15.8 %copy-start = (bf16[8,128,384]{2,1,0:T(8,128)(2,1)}, bf16[8,128,384]{2,1,0:T(8,128)(2,1)S(1)}, u32[]{:S(2)}) copy-start(bf16[8,128,384]{2,1,0:T(8,128)(2,1)S(1)} %shard_map.188.same_ref.refs_0_) | copy-start | bytes 2359300
  22.0 4.1 %collective-permute-start = (bf16[8,128,384]{2,1,0:T(8,128)(2,1)S(1)}, bf16[8,128,384]{2,1,0:T(8,128)(2,1)S(1)}, u32[]{:S(2)}, u32[]{:S(2)}) collective-permute-start(bf16[8,128,384]{2,1,0:T(8,128)(2,1)S(1)} %shard_map.188.same_ref.refs_0_), channel_id=1, source_target_pairs={{0,8},{8,0},{1,9},{9,1},{2,10},{10,2},{3,11},{11,3},{4,12},{12,4},... | collective-permute-start | bytes 2359304 | tf_op jit(solution)/shard_map/ppermute | solution.py:666
  29.2 18.0 %all-to-all-start.1 = ((bf16[8,128,256]{2,1,0:T(8,128)(2,1)}), bf16[8,128,256]{2,1,0:T(8,128)(2,1)S(1)}, u32[]{:S(2)}, u32[]{:S(2)}) async-start(bf16[8,128,256]{2,1,0:T(8,128)(2,1)} %shard_map.189), calls=%async_computation.1 | async-start | bytes 1048576 | tf_op jit(solution)/shard_map/all_to_all | solution.py:662
  54.1 5.3 %collective-permute-start.2 = (bf16[8,48,768]{2,1,0:T(8,128)(2,1)}, bf16[8,48,768]{2,1,0:T(8,128)(2,1)}, u32[]{:S(2)}, u32[]{:S(2)}) collective-permute-start(bf16[8,48,768]{2,1,0:T(8,128)(2,1)} %get-tuple-element.63), channel_id=1, source_target_pairs={{0,8},{8,0},{1,9},{9,1},{2,10},{10,2},{3,11},{11,3},{4,12},{12,4},... | collective-permute-start | bytes 1769480 | tf_op jit(solution)/shard_map/ppermute | solution.py:666
  55.8 18.1 %all-to-all-start.2 = ((bf16[8,64,768]{2,1,0:T(8,128)(2,1)}), bf16[8,64,768]{2,1,0:T(8,128)(2,1)S(1)}, u32[]{:S(2)}, u32[]{:S(2)}) async-start(bf16[8,64,768]{2,1,0:T(8,128)(2,1)} %get-tuple-element.55), calls=%async_computation.2 | async-start | bytes 1572864 | tf_op jit(solution)/shard_map/all_to_all | solution.py:662
  61.3 15.5 %collective-permute-start.3 = (bf16[2,48,768]{2,1,0:T(8,128)(2,1)}, bf16[2,48,768]{2,1,0:T(8,128)(2,1)S(1)}, u32[]{:S(2)}, u32[]{:S(2)}) collective-permute-start(bf16[2,48,768]{2,1,0:T(8,128)(2,1)} %get-tuple-element.64), channel_id=1, source_target_pairs={{0,32},{32,0},{64,96},{96,64},{1,33},{33,1},{65,97},{97,65},{2,34}... | collective-permute-start | bytes 442376 | tf_op jit(solution)/shard_map/ppermute | solution.py:682
  61.3 15.5 %collective-permute-start.4 = (bf16[2,48,768]{2,1,0:T(8,128)(2,1)}, bf16[2,48,768]{2,1,0:T(8,128)(2,1)S(1)}, u32[]{:S(2)}, u32[]{:S(2)}) collective-permute-start(bf16[2,48,768]{2,1,0:T(8,128)(2,1)} %get-tuple-element.65), channel_id=1, source_target_pairs={{0,64},{32,96},{64,0},{96,32},{1,65},{33,97},{65,1},{97,33},{2,66}... | collective-permute-start | bytes 442376 | tf_op jit(solution)/shard_map/ppermute | solution.py:682
  63.9 12.9 %collective-permute-start.5 = (bf16[2,48,768]{2,1,0:T(8,128)(2,1)}, bf16[2,48,768]{2,1,0:T(8,128)(2,1)S(1)}, u32[]{:S(2)}, u32[]{:S(2)}) collective-permute-start(bf16[2,48,768]{2,1,0:T(8,128)(2,1)} %get-tuple-element.66), channel_id=1, source_target_pairs={{0,96},{32,64},{64,32},{96,0},{1,97},{33,65},{65,33},{97,1},{2,98}... | collective-permute-start | bytes 442376 | tf_op jit(solution)/shard_map/ppermute | solution.py:682
  76.8 19.8 %all-to-all-start.3 = ((bf16[32,112,128]{2,1,0:T(8,128)(2,1)}), bf16[32,112,128]{2,1,0:T(8,128)(2,1)S(1)}, u32[]{:S(2)}, u32[]{:S(2)}) async-start(bf16[32,112,128]{2,1,0:T(8,128)(2,1)} %bitcast.8), calls=%async_computation.3 | async-start | bytes 1835008 | tf_op jit(solution)/shard_map/all_to_all | solution.py:662
  80.8 15.8 %collective-permute-start.1 = (bf16[8,128,384]{2,1,0:T(8,128)(2,1)}, bf16[8,128,384]{2,1,0:T(8,128)(2,1)S(1)}, u32[]{:S(2)}, u32[]{:S(2)}) collective-permute-start(bf16[8,128,384]{2,1,0:T(8,128)(2,1)} %shard_map.193.kvs_ref), channel_id=1, source_target_pairs={{0,8},{8,0},{1,9},{9,1},{2,10},{10,2},{3,11},{11,3},{4,12},{12,4},... | collective-permute-start | bytes 2359304 | tf_op jit(solution)/shard_map/ppermute | solution.py:666
  81.7 12.7 %collective-permute-start.6 = (bf16[32,768]{1,0:T(8,128)(2,1)S(1)}, bf16[32,768]{1,0:T(8,128)(2,1)S(1)}, u32[]{:S(2)}, u32[]{:S(2)}) collective-permute-start(bf16[32,768]{1,0:T(8,128)(2,1)S(1)} %copy-done.2), channel_id=1, source_target_pairs={{0,1},{1,0},{2,3},{3,2},{4,5},{5,4},{6,7},{7,6},{8,9},{9,8},{10,11... | collective-permute-start | bytes 147464 | tf_op jit(solution)/shard_map/ppermute | solution.py:682
  84.6 9.8 %collective-permute-start.7 = (bf16[32,768]{1,0:T(8,128)(2,1)S(1)}, bf16[32,768]{1,0:T(8,128)(2,1)S(1)}, u32[]{:S(2)}, u32[]{:S(2)}) collective-permute-start(bf16[32,768]{1,0:T(8,128)(2,1)S(1)} %copy-done.2), channel_id=1, source_target_pairs={{0,2},{1,3},{2,0},{3,1},{4,6},{5,7},{6,4},{7,5},{8,10},{9,11},{10,... | collective-permute-start | bytes 147464 | tf_op jit(solution)/shard_map/ppermute | solution.py:682
  85.8 10.8 %collective-permute-start.8 = (bf16[32,768]{1,0:T(8,128)(2,1)S(1)}, bf16[32,768]{1,0:T(8,128)(2,1)S(1)}, u32[]{:S(2)}, u32[]{:S(2)}) collective-permute-start(bf16[32,768]{1,0:T(8,128)(2,1)S(1)} %copy-done.2), channel_id=1, source_target_pairs={{0,3},{1,2},{2,1},{3,0},{4,7},{5,6},{6,5},{7,4},{8,11},{9,10},{10,... | collective-permute-start | bytes 147464 | tf_op jit(solution)/shard_map/ppermute | solution.py:682
  96.6 4.1 %collective-permute-start.9 = (bf16[8,4,112,128]{3,2,1,0:T(8,128)(2,1)S(1)}, bf16[8,4,112,128]{3,2,1,0:T(8,128)(2,1)S(1)}, u32[]{:S(2)}, u32[]{:S(2)}) collective-permute-start(bf16[8,4,112,128]{3,2,1,0:T(8,128)(2,1)S(1)} %shard_map.198.gs_ref), channel_id=1, source_target_pairs={{0,8},{8,0},{1,9},{9,1},{2,10},{10,2},{3,11},{11,3},{4,12},{12,4},... | collective-permute-start | bytes 2752520 | tf_op jit(solution)/shard_map/ppermute | solution.py:666
  100.7 5.3 %collective-permute-start.10 = (bf16[2,48,768]{2,1,0:T(8,128)(2,1)}, bf16[2,48,768]{2,1,0:T(8,128)(2,1)S(1)}, u32[]{:S(2)}, u32[]{:S(2)}) collective-permute-start(bf16[2,48,768]{2,1,0:T(8,128)(2,1)} %shard_map.200.near_ref), channel_id=1, source_target_pairs={{0,16},{16,0},{1,17},{17,1},{2,18},{18,2},{3,19},{19,3},{4,20},{20... | collective-permute-start | bytes 442376 | tf_op jit(solution)/shard_map/ppermute | solution.py:682
  106.0 3.9 %collective-permute-start.14 = (bf16[16,48,384]{2,1,0:T(8,128)(2,1)S(1)}, bf16[16,48,384]{2,1,0:T(8,128)(2,1)S(1)}, u32[]{:S(2)}, u32[]{:S(2)}) collective-permute-start(bf16[16,48,384]{2,1,0:T(8,128)(2,1)S(1)} %shard_map.202), channel_id=1, source_target_pairs={{0,8},{8,0},{1,9},{9,1},{2,10},{10,2},{3,11},{11,3},{4,12},{12,4},... | collective-permute-start | bytes 1769480 | tf_op jit(solution)/shard_map/ppermute | solution.py:666
  110.9 17.6 %all-to-all-start.4 = ((bf16[16,48,384]{2,1,0:T(8,128)(2,1)}), bf16[16,48,384]{2,1,0:T(8,128)(2,1)S(1)}, u32[]{:S(2)}, u32[]{:S(2)}) async-start(bf16[16,48,384]{2,1,0:T(8,128)(2,1)} %shard_map.203), calls=%async_computation.4 | async-start | bytes 1179648 | tf_op jit(solution)/shard_map/all_to_all | solution.py:662
  116.9 9.6 %collective-permute-start.11 = (bf16[48,768]{1,0:T(8,128)(2,1)S(1)}, bf16[48,768]{1,0:T(8,128)(2,1)S(1)}, u32[]{:S(2)}, u32[]{:S(2)}) collective-permute-start(bf16[48,768]{1,0:T(8,128)(2,1)S(1)} %copy-done.7), channel_id=1, source_target_pairs={{0,1},{1,0},{2,3},{3,2},{4,5},{5,4},{6,7},{7,6},{8,9},{9,8},{10,11... | collective-permute-start | bytes 221192 | tf_op jit(solution)/shard_map/ppermute | solution.py:682
  117.8 8.8 %collective-permute-start.12 = (bf16[48,768]{1,0:T(8,128)(2,1)S(1)}, bf16[48,768]{1,0:T(8,128)(2,1)S(1)}, u32[]{:S(2)}, u32[]{:S(2)}) collective-permute-start(bf16[48,768]{1,0:T(8,128)(2,1)S(1)} %copy-done.6), channel_id=1, source_target_pairs={{0,2},{1,3},{2,0},{3,1},{4,6},{5,7},{6,4},{7,5},{8,10},{9,11},{10,... | collective-permute-start | bytes 221192 | tf_op jit(solution)/shard_map/ppermute | solution.py:682
  117.8 10.7 %collective-permute-start.13 = (bf16[48,768]{1,0:T(8,128)(2,1)S(1)}, bf16[48,768]{1,0:T(8,128)(2,1)S(1)}, u32[]{:S(2)}, u32[]{:S(2)}) collective-permute-start(bf16[48,768]{1,0:T(8,128)(2,1)S(1)} %copy-done.5), channel_id=1, source_target_pairs={{0,3},{1,2},{2,1},{3,0},{4,7},{5,6},{6,5},{7,4},{8,11},{9,10},{10,... | collective-permute-start | bytes 221192 | tf_op jit(solution)/shard_map/ppermute | solution.py:682
  130.8 40.7 %all-to-all-start.5 = ((bf16[64,8,2432]{2,1,0:T(8,128)(2,1)}), bf16[64,8,2432]{2,1,0:T(8,128)(2,1)S(1)}, u32[]{:S(2)}, u32[]{:S(2)}) async-start(bf16[64,8,2432]{2,1,0:T(8,128)(2,1)} %bitcast.7), calls=%async_computation.5 | async-start | bytes 4980736 | tf_op jit(solution)/shard_map/all_to_all | solution.py:662
  171.5 14.6 %collective-permute-start.15 = (bf16[8,8,8,2432]{3,2,1,0:T(8,128)(2,1)S(1)}, bf16[8,8,8,2432]{3,2,1,0:T(8,128)(2,1)}, u32[]{:S(2)}, u32[]{:S(2)}) collective-permute-start(bf16[8,8,8,2432]{3,2,1,0:T(8,128)(2,1)S(1)} %shard_map.207.refs_1_.in_ref), channel_id=1, source_target_pairs={{0,8},{8,0},{1,9},{9,1},{2,10},{10,2},{3,11},{11,3},{4,12},{12,4},... | collective-permute-start | bytes 7471112 | tf_op jit(solution)/shard_map/ppermute | solution.py:666
  174.9 19.8 %all-to-all-start.6 = ((bf16[8,64,768]{2,1,0:T(8,128)(2,1)}), bf16[8,64,768]{2,1,0:T(8,128)(2,1)S(1)}, u32[]{:S(2)}, u32[]{:S(2)}) async-start(bf16[8,64,768]{2,1,0:T(8,128)(2,1)} %shard_map.208), calls=%async_computation.6 | async-start | bytes 1572864 | tf_op jit(solution)/shard_map/all_to_all | solution.py:662
  178.5 11.7 %collective-permute-start.17 = (bf16[2,48,768]{2,1,0:T(8,128)(2,1)S(1)}, bf16[2,48,768]{2,1,0:T(8,128)(2,1)S(1)}, u32[]{:S(2)}, u32[]{:S(2)}) collective-permute-start(bf16[2,48,768]{2,1,0:T(8,128)(2,1)S(1)} %copy-done.4), channel_id=1, source_target_pairs={{0,32},{32,0},{64,96},{96,64},{1,33},{33,1},{65,97},{97,65},{2,34}... | collective-permute-start | bytes 442376 | tf_op jit(solution)/shard_map/ppermute | solution.py:682
  178.9 11.4 %collective-permute-start.19 = (bf16[2,48,768]{2,1,0:T(8,128)(2,1)S(1)}, bf16[2,48,768]{2,1,0:T(8,128)(2,1)S(1)}, u32[]{:S(2)}, u32[]{:S(2)}) collective-permute-start(bf16[2,48,768]{2,1,0:T(8,128)(2,1)S(1)} %copy-done.4), channel_id=1, source_target_pairs={{0,64},{32,96},{64,0},{96,32},{1,65},{33,97},{65,1},{97,33},{2,66}... | collective-permute-start | bytes 442376 | tf_op jit(solution)/shard_map/ppermute | solution.py:682
  180.8 10.1 %collective-permute-start.21 = (bf16[2,48,768]{2,1,0:T(8,128)(2,1)S(1)}, bf16[2,48,768]{2,1,0:T(8,128)(2,1)S(1)}, u32[]{:S(2)}, u32[]{:S(2)}) collective-permute-start(bf16[2,48,768]{2,1,0:T(8,128)(2,1)S(1)} %copy-done.4), channel_id=1, source_target_pairs={{0,96},{32,64},{64,32},{96,0},{1,97},{33,65},{65,33},{97,1},{2,98}... | collective-permute-start | bytes 442376 | tf_op jit(solution)/shard_map/ppermute | solution.py:682
  182.4 11.0 %collective-permute-start.16 = (bf16[2,48,768]{2,1,0:T(8,128)(2,1)S(1)}, bf16[2,48,768]{2,1,0:T(8,128)(2,1)S(1)}, u32[]{:S(2)}, u32[]{:S(2)}) collective-permute-start(bf16[2,48,768]{2,1,0:T(8,128)(2,1)S(1)} %copy-done.4), channel_id=1, source_target_pairs={{0,8},{8,0},{1,9},{9,1},{2,10},{10,2},{3,11},{11,3},{4,12},{12,4},... | collective-permute-start | bytes 442376 | tf_op jit(solution)/shard_map/ppermute | solution.py:666
  190.3 3.2 %collective-permute-start.18 = (bf16[2,48,768]{2,1,0:T(8,128)(2,1)S(1)}, bf16[2,48,768]{2,1,0:T(8,128)(2,1)S(1)}, u32[]{:S(2)}, u32[]{:S(2)}) collective-permute-start(bf16[2,48,768]{2,1,0:T(8,128)(2,1)S(1)} %shard_map.211.refs_1_), channel_id=1, source_target_pairs={{0,8},{8,0},{1,9},{9,1},{2,10},{10,2},{3,11},{11,3},{4,12},{12,4},... | collective-permute-start | bytes 442376 | tf_op jit(solution)/shard_map/ppermute | solution.py:666
  190.4 3.1 %collective-permute-start.20 = (bf16[2,48,768]{2,1,0:T(8,128)(2,1)S(1)}, bf16[2,48,768]{2,1,0:T(8,128)(2,1)S(1)}, u32[]{:S(2)}, u32[]{:S(2)}) collective-permute-start(bf16[2,48,768]{2,1,0:T(8,128)(2,1)S(1)} %shard_map.212.refs_2_), channel_id=1, source_target_pairs={{0,8},{8,0},{1,9},{9,1},{2,10},{10,2},{3,11},{11,3},{4,12},{12,4},... | collective-permute-start | bytes 442376 | tf_op jit(solution)/shard_map/ppermute | solution.py:666
  190.9 2.6 %collective-permute-start.22 = (bf16[2,48,768]{2,1,0:T(8,128)(2,1)S(1)}, bf16[2,48,768]{2,1,0:T(8,128)(2,1)S(1)}, u32[]{:S(2)}, u32[]{:S(2)}) collective-permute-start(bf16[2,48,768]{2,1,0:T(8,128)(2,1)S(1)} %shard_map.213.refs_3_), channel_id=1, source_target_pairs={{0,8},{8,0},{1,9},{9,1},{2,10},{10,2},{3,11},{11,3},{4,12},{12,4},... | collective-permute-start | bytes 442376 | tf_op jit(solution)/shard_map/ppermute | solution.py:666
  (6 other events, 40.9 us)

commit v22 on v20

--- a/solution.py
+++ b/solution.py
@@ -840,7 +840,6 @@
     )
     weight_same = exchange(weight_total.reshape(64, 8, 2432), (*CHIP, *NARROW)).reshape(8, 8, 8, 2432)
     weight_same = after(weight_same, pin(packed))
-    everyone = exchange(after(pin(packed), weight_same), NARROW)
     weight_other = swap(weight_same)
     scratch = [
         pltpu.VMEM((8, 48, 3 * D), F32), pltpu.VMEM((4, 2, 48, D), F32), DMA((8,)), DMA((4, 2)),
@@ -853,6 +852,7 @@
         1000,
         scratch,
     )
+    everyone = exchange(after(pin(packed), half[2]), NARROW)
     qkv_grad, out_proj_grad, *vectors = call(
         functools.partial(spread_kernel, True),
         grads + [((D,), F32, "L")] * 4,

time: 197 us -> 198 us (level)
  Pallas kernels: 51.7 us -> 49.6 us
    pallas_call x19, Pallas kernels: 51.6 us -> 49.6 us  [call(): pl.pallas_call(kernel, out_shape=[(pltpu.HBM if place in 'HL' else jax.Sh...]
  transfers between devices with their start and end apart: 30 -> 30, of which waited for: 10 -> 12; matrix products, arithmetic and copies ran while one was open for 1% -> 1% of each run, Pallas kernels for 17% -> 16%
where the time goes in v22:
time: 198 us; the launch traced here: 197 us
  waiting for transfers between devices  75 us (38%)
  starting transfers between devices  69.7 us (35%)
  Pallas kernels  49.6 us (25%)
    all_to_all x7, waiting for transfers between devices, exchange(): return lax.all_to_all(value, axes, 0, 0, tiled=True)  52.6 us
    pallas_call x19, Pallas kernels, call(): pl.pallas_call(kernel, out_shape=[(pltpu.HBM if place in 'HL' else jax.Sh...  49.6 us
    all_to_all x7, starting transfers between devices, exchange(): return lax.all_to_all(value, axes, 0, 0, tiled=True)  39.7 us
    ppermute x13, waiting for transfers between devices, flip(): lax.ppermute(value, axes, [(index, index ^ bits) for index in range(count)])  18.4 us
    ppermute x13, starting transfers between devices, flip(): lax.ppermute(value, axes, [(index, index ^ bits) for index in range(count)])  15.9 us
    ppermute x10, starting transfers between devices, swap(): return lax.ppermute(value, CORE, [(0, 1), (1, 0)])  14.1 us
    ppermute x10, waiting for transfers between devices, swap(): return lax.ppermute(value, CORE, [(0, 1), (1, 0)])  4.03 us
  transfers between devices with their start and end apart: 30, of which 12 were waited for; matrix products, arithmetic and copies ran while one was open for 1% of the time, Pallas kernels for 16%

profile of v22, /device:TPU:1, one launch (start us, length us, event | category | flops | bytes accessed | tf_op | source)
XLA Modules:
  0.0 196.7 jit_solution(3600433951033145879)
XLA Ops:
  0.6 3.7 %shard_map.186 = (bf16[8,128,384]{2,1,0:T(8,128)(2,1)}, bf16[128,768]{1,0:T(8,128)(2,1)}) custom-call(bf16[2,128,768]{2,1,0:T(8,128)(2,1)} %tok_ref.7, f32[768]{0:T(1024)} %gain_ref.7, f32[768]{0:T(1024)} %shift_ref.2, bf16[768,2304]{1,0:T(8,128)(2,1)} %w_ref.7), custom_call_target="tpu_custom_call" | custom-call | flops 1000 | bytes 1000 | tf_op jit(solution)/shard_map/pallas_call | solution.py:106
  4.3 6.0 %all-to-all-start = ((bf16[8,128,384]{2,1,0:T(8,128)(2,1)}), bf16[8,128,384]{2,1,0:T(8,128)(2,1)S(1)}, u32[]{:S(2)}, u32[]{:S(2)}) async-start(bf16[8,128,384]{2,1,0:T(8,128)(2,1)} %get-tuple-element.53), calls=%async_computation | async-start | bytes 1572864 | tf_op jit(solution)/shard_map/all_to_all | solution.py:661
  10.3 3.0 %shard_map.187.refs_1_.q_ref = bf16[128,256]{1,0:T(8,128)(2,1)} custom-call(bf16[128,768]{1,0:T(8,128)(2,1)} %get-tuple-element.54.normed_ref, bf16[768,2304]{1,0:T(8,128)(2,1)} %w_ref.7), custom_call_target="tpu_custom_call" | custom-call | flops 1000 | bytes 1000 | tf_op jit(solution)/shard_map/pallas_call | solution.py:106
  13.4 8.6 %all-to-all-done.refs_0_ = bf16[8,128,384]{2,1,0:T(8,128)(2,1)S(1)} async-done(((bf16[8,128,384]{2,1,0:T(8,128)(2,1)}), bf16[8,128,384]{2,1,0:T(8,128)(2,1)S(1)}, u32[]{:S(2)}, u32[]{:S(2)}) %all-to-all-start) | async-done | bytes 786464 | tf_op jit(solution)/shard_map/all_to_all | solution.py:661
  22.0 2.2 %collective-permute-start = (bf16[8,128,384]{2,1,0:T(8,128)(2,1)S(1)}, bf16[8,128,384]{2,1,0:T(8,128)(2,1)S(1)}, u32[]{:S(2)}, u32[]{:S(2)}) collective-permute-start(bf16[8,128,384]{2,1,0:T(8,128)(2,1)S(1)} %shard_map.188.same_ref.refs_0_), channel_id=1, source_target_pairs={{0,8},{8,0},{1,9},{9,1},{2,10},{10,2},{3,11},{11,3},{4,12},{12,4},... | collective-permute-start | bytes 2359304 | tf_op jit(solution)/shard_map/ppermute | solution.py:665
  26.1 3.1 %shard_map.189 = bf16[8,128,256]{2,1,0:T(8,128)(2,1)} custom-call(s32[2,32]{1,0:T(2,128)S(1)} %copy-done.3, bf16[128,256]{1,0:T(8,128)(2,1)} %shard_map.187.refs_1_.q_ref, bf16[8,128,384]{2,1,0:T(8,128)(2,1)S(1)} %shard_map.188.same_ref.refs_0_, bf16[8,128,384]{2,1,0:T(8,128)(2,1)S(1)} %collective-permute-done.other_ref), custom_call_target="tpu_custom_call" | custom-call | flops 1000 | bytes 1000 | tf_op jit(solution)/shard_map/pallas_call | solution.py:106
  29.2 8.1 %all-to-all-start.1 = ((bf16[8,128,256]{2,1,0:T(8,128)(2,1)}), bf16[8,128,256]{2,1,0:T(8,128)(2,1)S(1)}, u32[]{:S(2)}, u32[]{:S(2)}) async-start(bf16[8,128,256]{2,1,0:T(8,128)(2,1)} %shard_map.189), calls=%async_computation.1 | async-start | bytes 1048576 | tf_op jit(solution)/shard_map/all_to_all | solution.py:661
  38.7 9.4 %all-to-all-done.1.mixed_ref = bf16[8,128,256]{2,1,0:T(8,128)(2,1)S(1)} async-done(((bf16[8,128,256]{2,1,0:T(8,128)(2,1)}), bf16[8,128,256]{2,1,0:T(8,128)(2,1)S(1)}, u32[]{:S(2)}, u32[]{:S(2)}) %all-to-all-start.1) | async-done | bytes 524320 | tf_op jit(solution)/shard_map/all_to_all | solution.py:661
  48.0 4.2 %shard_map.190 = (bf16[8,64,768]{2,1,0:T(8,128)(2,1)}, f32[32,768]{1,0:T(8,128)}, bf16[256,768]{1,0:T(8,128)(2,1)S(1)}, bf16[256,384]{1,0:T(8,128)(2,1)S(1)}, bf16[256,384]{1,0:T(8,128)(2,1)S(1)}) custom-call(bf16[8,128,256]{2,1,0:T(8,128)(2,1)S(1)} %all-to-all-done.1.mixed_ref, bf16[2,128,768]{2,1,0:T(8,128)(2,1)} %tok_ref.7, bf16[2,128,768]{2,1,0:T(8,128)(2,1)} %og_ref.5, ...), custom_call_target="tpu_custom_call" | custom-call | flops 1000 | bytes 1000 | tf_op jit(solution)/shard_map/pallas_call | solution.py:106
  52.2 2.8 %shard_map.194 = (bf16[8,48,768]{2,1,0:T(8,128)(2,1)S(1)}, bf16[8,48,768]{2,1,0:T(8,128)(2,1)}) custom-call(bf16[256,768]{1,0:T(8,128)(2,1)S(1)} %get-tuple-element.59.normed_ref, bf16[256,384]{1,0:T(8,128)(2,1)S(1)} %get-tuple-element.60.act_ref, bf16[256,384]{1,0:T(8,128)(2,1)S(1)} %get-tuple-element.61.gpre_ref, bf16[2,128,768]{2,1,0:T(8,128)(2,1)} %og_ref.5), custom_call_target="tpu_custom_call" | custom-call | flops 1000 | bytes 1000 | tf_op jit(solution)/shard_map/pallas_call | solution.py:106
  56.7 3.5 %all-to-all-start.2 = ((bf16[8,64,768]{2,1,0:T(8,128)(2,1)}), bf16[8,64,768]{2,1,0:T(8,128)(2,1)S(1)}, u32[]{:S(2)}, u32[]{:S(2)}) async-start(bf16[8,64,768]{2,1,0:T(8,128)(2,1)} %get-tuple-element.55), calls=%async_computation.2 | async-start | bytes 1572864 | tf_op jit(solution)/shard_map/all_to_all | solution.py:661
  63.1 3.0 %collective-permute-start.5 = (bf16[2,48,768]{2,1,0:T(8,128)(2,1)}, bf16[2,48,768]{2,1,0:T(8,128)(2,1)S(1)}, u32[]{:S(2)}, u32[]{:S(2)}) collective-permute-start(bf16[2,48,768]{2,1,0:T(8,128)(2,1)} %get-tuple-element.66), channel_id=1, source_target_pairs={{0,96},{32,64},{64,32},{96,0},{1,97},{33,65},{65,33},{97,1},{2,98}... | collective-permute-start | bytes 442376 | tf_op jit(solution)/shard_map/ppermute | solution.py:681
  66.0 2.3 %shard_map.191.query_ref = bf16[4,32,256]{2,1,0:T(8,128)(2,1)} custom-call(bf16[128,768]{1,0:T(8,128)(2,1)} %get-tuple-element.54.normed_ref, bf16[768,2304]{1,0:T(8,128)(2,1)} %w_ref.7), custom_call_target="tpu_custom_call" | custom-call | flops 1000 | bytes 1000 | tf_op jit(solution)/shard_map/pallas_call | solution.py:106
  68.4 6.4 %all-to-all-done.2.sums_ref = bf16[8,64,768]{2,1,0:T(8,128)(2,1)S(1)} async-done(((bf16[8,64,768]{2,1,0:T(8,128)(2,1)}), bf16[8,64,768]{2,1,0:T(8,128)(2,1)S(1)}, u32[]{:S(2)}, u32[]{:S(2)}) %all-to-all-start.2) | async-done | bytes 786464 | tf_op jit(solution)/shard_map/all_to_all | solution.py:661
  74.8 2.9 %shard_map.192 = (bf16[8,4,112,128]{3,2,1,0:T(8,128)(2,1)}, bf16[32,768]{1,0:T(8,128)(2,1)}, f32[32,768]{1,0:T(8,128)}, bf16[32,768]{1,0:T(8,128)(2,1)}, f32[8,768]{1,0:T(8,128)}) custom-call(bf16[8,64,768]{2,1,0:T(8,128)(2,1)S(1)} %all-to-all-done.2.sums_ref, f32[32,768]{1,0:T(8,128)} %get-tuple-element.56.middle_ref, bf16[2,128,768]{2,1,0:T(8,128)(2,1)} %og_ref.5, ...), custom_call_target="tpu_custom_call" | custom-call | flops 1000 | bytes 1000 | tf_op jit(solution)/shard_map/pallas_call | solution.py:106
  77.7 3.9 %all-to-all-start.3 = ((bf16[32,112,128]{2,1,0:T(8,128)(2,1)}), bf16[32,112,128]{2,1,0:T(8,128)(2,1)S(1)}, u32[]{:S(2)}, u32[]{:S(2)}) async-start(bf16[32,112,128]{2,1,0:T(8,128)(2,1)} %bitcast.8), calls=%async_computation.3 | async-start | bytes 1835008 | tf_op jit(solution)/shard_map/all_to_all | solution.py:661
  82.6 2.9 %collective-permute-start.6 = (bf16[32,768]{1,0:T(8,128)(2,1)S(1)}, bf16[32,768]{1,0:T(8,128)(2,1)S(1)}, u32[]{:S(2)}, u32[]{:S(2)}) collective-permute-start(bf16[32,768]{1,0:T(8,128)(2,1)S(1)} %copy-done.2), channel_id=1, source_target_pairs={{0,1},{1,0},{2,3},{3,2},{4,5},{5,4},{6,7},{7,6},{8,9},{9,8},{10,11... | collective-permute-start | bytes 147464 | tf_op jit(solution)/shard_map/ppermute | solution.py:681
  88.4 6.9 %collective-permute-done.6.refs_1_.low1_ref = bf16[32,768]{1,0:T(8,128)(2,1)S(1)} collective-permute-done((bf16[32,768]{1,0:T(8,128)(2,1)S(1)}, bf16[32,768]{1,0:T(8,128)(2,1)S(1)}, u32[]{:S(2)}, u32[]{:S(2)}) %collective-permute-start.6) | collective-permute-done | bytes 49184 | tf_op jit(solution)/shard_map/ppermute | solution.py:681
  95.3 2.3 %collective-permute-done.8.refs_3_.low3_ref = bf16[32,768]{1,0:T(8,128)(2,1)S(1)} collective-permute-done((bf16[32,768]{1,0:T(8,128)(2,1)S(1)}, bf16[32,768]{1,0:T(8,128)(2,1)S(1)}, u32[]{:S(2)}, u32[]{:S(2)}) %collective-permute-start.8) | collective-permute-done | bytes 49184 | tf_op jit(solution)/shard_map/ppermute | solution.py:681
  101.9 4.3 %shard_map.199 = (bf16[128,640]{1,0:T(8,128)(2,1)S(1)}, bf16[3,768,384]{2,1,0:T(8,128)(2,1)S(1)}, bf16[16,48,384]{2,1,0:T(8,128)(2,1)S(1)}, bf16[16,48,384]{2,1,0:T(8,128)(2,1)S(1)}) custom-call(s32[2,32]{1,0:T(2,128)S(1)} %copy-done.3, bf16[8,128,384]{2,1,0:T(8,128)(2,1)} %shard_map.193.kvs_ref, ...), custom_call_target="tpu_custom_call" | custom-call | flops 1000 | bytes 1000 | tf_op jit(solution)/shard_map/pallas_call | solution.py:106
  108.1 2.6 %shard_map.201 = (f32[32,768]{1,0:T(8,128)}, bf16[48,768]{1,0:T(8,128)(2,1)}, bf16[48,768]{1,0:T(8,128)(2,1)}, bf16[48,768]{1,0:T(8,128)(2,1)}, f32[8,768]{1,0:T(8,128)}, /*index=5*/bf16[2,48,768]{2,1,0:T(8,128)(2,1)}) custom-call(bf16[128,640]{1,0:T(8,128)(2,1)S(1)} %get-tuple-element.68.gqkv_ref, bf16[3,768,384]{2,1,0:T(8,128)(2,1)S(1)} %get-tuple-element.69.w_ref, ...), custom_call_target="tpu_custom_call" | custom-call | flops 1000 | bytes 1000 | tf_op jit(solution)/shard_map/pallas_call | solution.py:106
  111.7 5.2 %all-to-all-start.4 = ((bf16[16,48,384]{2,1,0:T(8,128)(2,1)}), bf16[16,48,384]{2,1,0:T(8,128)(2,1)S(1)}, u32[]{:S(2)}, u32[]{:S(2)}) async-start(bf16[16,48,384]{2,1,0:T(8,128)(2,1)} %shard_map.203), calls=%async_computation.4 | async-start | bytes 1179648 | tf_op jit(solution)/shard_map/all_to_all | solution.py:661
  118.7 2.5 %collective-permute-start.13 = (bf16[48,768]{1,0:T(8,128)(2,1)S(1)}, bf16[48,768]{1,0:T(8,128)(2,1)S(1)}, u32[]{:S(2)}, u32[]{:S(2)}) collective-permute-start(bf16[48,768]{1,0:T(8,128)(2,1)S(1)} %copy-done.5), channel_id=1, source_target_pairs={{0,3},{1,2},{2,1},{3,0},{4,7},{5,6},{6,5},{7,4},{8,11},{9,10},{10,... | collective-permute-start | bytes 221192 | tf_op jit(solution)/shard_map/ppermute | solution.py:681
  121.2 6.2 %collective-permute-done.11.refs_2_.one_ref = bf16[48,768]{1,0:T(8,128)(2,1)S(1)} collective-permute-done((bf16[48,768]{1,0:T(8,128)(2,1)S(1)}, bf16[48,768]{1,0:T(8,128)(2,1)S(1)}, u32[]{:S(2)}, u32[]{:S(2)}) %collective-permute-start.11) | collective-permute-done | bytes 73760 | tf_op jit(solution)/shard_map/ppermute | solution.py:681
  128.7 2.3 %shard_map.205.unused_ref = bf16[8,8,8,2432]{3,2,1,0:T(8,128)(2,1)} custom-call(bf16[16,48,384]{2,1,0:T(8,128)(2,1)S(1)} %shard_map.204.in_ref, f32[8,768]{1,0:T(8,128)} %get-tuple-element.79.refs_1_.vec_ref, bf16[48,768]{1,0:T(8,128)(2,1)S(1)} %collective-permute-done.11.refs_2_.one_ref, bf16[48,768]{1,0:T(8,128)(2,1)S(1)} %collective-permute-done.12.refs_3_.two_ref, ...), custom_call_target="tpu_custom_call" | custom-call | flops 1000 | bytes 1000 | tf_op jit(solution)/shard_map/pallas_call | solution.py:106
  131.0 9.4 %all-to-all-start.5 = ((bf16[64,8,2432]{2,1,0:T(8,128)(2,1)}), bf16[64,8,2432]{2,1,0:T(8,128)(2,1)S(1)}, u32[]{:S(2)}, u32[]{:S(2)}) async-start(bf16[64,8,2432]{2,1,0:T(8,128)(2,1)} %bitcast.7), calls=%async_computation.5 | async-start | bytes 4980736 | tf_op jit(solution)/shard_map/all_to_all | solution.py:661
  140.4 3.0 %shard_map.206.refs_1_.refs_0_ = bf16[8,64,768]{2,1,0:T(8,128)(2,1)} custom-call(f32[32,768]{1,0:T(8,128)} %get-tuple-element.71.unused_ref.own_ref, bf16[48,768]{1,0:T(8,128)(2,1)S(1)} %collective-permute-done.11.refs_2_.one_ref, bf16[48,768]{1,0:T(8,128)(2,1)S(1)} %collective-permute-done.12.refs_3_.two_ref, ...), custom_call_target="tpu_custom_call" | custom-call | flops 1000 | bytes 1000 | tf_op jit(solution)/shard_map/pallas_call | solution.py:106
  143.4 28.2 %all-to-all-done.5 = bf16[64,8,2432]{2,1,0:T(8,128)(2,1)S(1)} async-done(((bf16[64,8,2432]{2,1,0:T(8,128)(2,1)}), bf16[64,8,2432]{2,1,0:T(8,128)(2,1)S(1)}, u32[]{:S(2)}, u32[]{:S(2)}) %all-to-all-start.5) | async-done | bytes 2490400 | tf_op jit(solution)/shard_map/all_to_all | solution.py:661
  171.6 3.4 %collective-permute-start.15 = (bf16[8,8,8,2432]{3,2,1,0:T(8,128)(2,1)S(1)}, bf16[8,8,8,2432]{3,2,1,0:T(8,128)(2,1)}, u32[]{:S(2)}, u32[]{:S(2)}) collective-permute-start(bf16[8,8,8,2432]{3,2,1,0:T(8,128)(2,1)S(1)} %shard_map.207.in_ref), channel_id=1, source_target_pairs={{0,8},{8,0},{1,9},{9,1},{2,10},{10,2},{3,11},{11,3},{4,12},{12,4},... | collective-permute-start | bytes 7471112 | tf_op jit(solution)/shard_map/ppermute | solution.py:665
  174.9 2.4 %shard_map.208 = (f32[768,2304]{1,0:T(8,128)}, f32[768,768]{1,0:T(8,128)}, f32[4,8,128]{2,1,0:T(8,128)S(1)}) custom-call(bf16[8,8,8,2432]{3,2,1,0:T(8,128)(2,1)S(1)} %shard_map.207.in_ref), custom_call_target="tpu_custom_call" | custom-call | flops 1000 | bytes 1000 | tf_op jit(solution)/shard_map/pallas_call | solution.py:106
  177.4 3.6 %all-to-all-start.6 = ((bf16[8,64,768]{2,1,0:T(8,128)(2,1)}), bf16[8,64,768]{2,1,0:T(8,128)(2,1)S(1)}, u32[]{:S(2)}, u32[]{:S(2)}) async-start(bf16[8,64,768]{2,1,0:T(8,128)(2,1)} %shard_map.209), calls=%async_computation.6 | async-start | bytes 1572864 | tf_op jit(solution)/shard_map/all_to_all | solution.py:661
  185.5 4.1 %shard_map.210 = (f32[768,2304]{1,0:T(8,128)}, f32[768,768]{1,0:T(8,128)}, f32[768]{0:T(1024)}, f32[768]{0:T(1024)}, f32[768]{0:T(1024)}, /*index=5*/f32[768]{0:T(1024)}) custom-call(bf16[8,8,8,2432]{3,2,1,0:T(8,128)(2,1)} %collective-permute-done.15.in_ref, ...), custom_call_target="tpu_custom_call", output_to_operand_aliasing={{0}: (2, {}), {1}: (3, {})} | custom-call | flops 1000 | bytes 1000 | tf_op jit(solution)/shard_map/pallas_call | solution.py:106
  (76 shorter events, 33.4 us)
Async XLA Ops:
  4.3 17.6 %all-to-all-start = ((bf16[8,128,384]{2,1,0:T(8,128)(2,1)}), bf16[8,128,384]{2,1,0:T(8,128)(2,1)S(1)}, u32[]{:S(2)}, u32[]{:S(2)}) async-start(bf16[8,128,384]{2,1,0:T(8,128)(2,1)} %get-tuple-element.53), calls=%async_computation | async-start | bytes 1572864 | tf_op jit(solution)/shard_map/all_to_all | solution.py:661
  10.3 15.8 %copy-start.3 = (s32[2,32]{1,0:T(2,128)S(1)}, s32[2,32]{1,0:T(2,128)}, u32[]{:S(2)}) copy-start(s32[2,32]{1,0:T(2,128)} %scene_ref.3) | copy-start | bytes 772
  22.0 16.7 %copy-start = (bf16[8,128,384]{2,1,0:T(8,128)(2,1)}, bf16[8,128,384]{2,1,0:T(8,128)(2,1)S(1)}, u32[]{:S(2)}) copy-start(bf16[8,128,384]{2,1,0:T(8,128)(2,1)S(1)} %shard_map.188.same_ref.refs_0_) | copy-start | bytes 2359300
  22.0 4.1 %collective-permute-start = (bf16[8,128,384]{2,1,0:T(8,128)(2,1)S(1)}, bf16[8,128,384]{2,1,0:T(8,128)(2,1)S(1)}, u32[]{:S(2)}, u32[]{:S(2)}) collective-permute-start(bf16[8,128,384]{2,1,0:T(8,128)(2,1)S(1)} %shard_map.188.same_ref.refs_0_), channel_id=1, source_target_pairs={{0,8},{8,0},{1,9},{9,1},{2,10},{10,2},{3,11},{11,3},{4,12},{12,4},... | collective-permute-start | bytes 2359304 | tf_op jit(solution)/shard_map/ppermute | solution.py:665
  29.2 18.9 %all-to-all-start.1 = ((bf16[8,128,256]{2,1,0:T(8,128)(2,1)}), bf16[8,128,256]{2,1,0:T(8,128)(2,1)S(1)}, u32[]{:S(2)}, u32[]{:S(2)}) async-start(bf16[8,128,256]{2,1,0:T(8,128)(2,1)} %shard_map.189), calls=%async_computation.1 | async-start | bytes 1048576 | tf_op jit(solution)/shard_map/all_to_all | solution.py:661
  55.0 5.3 %collective-permute-start.2 = (bf16[8,48,768]{2,1,0:T(8,128)(2,1)}, bf16[8,48,768]{2,1,0:T(8,128)(2,1)}, u32[]{:S(2)}, u32[]{:S(2)}) collective-permute-start(bf16[8,48,768]{2,1,0:T(8,128)(2,1)} %get-tuple-element.63), channel_id=1, source_target_pairs={{0,8},{8,0},{1,9},{9,1},{2,10},{10,2},{3,11},{11,3},{4,12},{12,4},... | collective-permute-start | bytes 1769480 | tf_op jit(solution)/shard_map/ppermute | solution.py:665
  56.7 18.1 %all-to-all-start.2 = ((bf16[8,64,768]{2,1,0:T(8,128)(2,1)}), bf16[8,64,768]{2,1,0:T(8,128)(2,1)S(1)}, u32[]{:S(2)}, u32[]{:S(2)}) async-start(bf16[8,64,768]{2,1,0:T(8,128)(2,1)} %get-tuple-element.55), calls=%async_computation.2 | async-start | bytes 1572864 | tf_op jit(solution)/shard_map/all_to_all | solution.py:661
  62.2 15.5 %collective-permute-start.3 = (bf16[2,48,768]{2,1,0:T(8,128)(2,1)}, bf16[2,48,768]{2,1,0:T(8,128)(2,1)S(1)}, u32[]{:S(2)}, u32[]{:S(2)}) collective-permute-start(bf16[2,48,768]{2,1,0:T(8,128)(2,1)} %get-tuple-element.64), channel_id=1, source_target_pairs={{0,32},{32,0},{64,96},{96,64},{1,33},{33,1},{65,97},{97,65},{2,34}... | collective-permute-start | bytes 442376 | tf_op jit(solution)/shard_map/ppermute | solution.py:681
  62.2 15.5 %collective-permute-start.4 = (bf16[2,48,768]{2,1,0:T(8,128)(2,1)}, bf16[2,48,768]{2,1,0:T(8,128)(2,1)S(1)}, u32[]{:S(2)}, u32[]{:S(2)}) collective-permute-start(bf16[2,48,768]{2,1,0:T(8,128)(2,1)} %get-tuple-element.65), channel_id=1, source_target_pairs={{0,64},{32,96},{64,0},{96,32},{1,65},{33,97},{65,1},{97,33},{2,66}... | collective-permute-start | bytes 442376 | tf_op jit(solution)/shard_map/ppermute | solution.py:681
  63.1 14.7 %collective-permute-start.5 = (bf16[2,48,768]{2,1,0:T(8,128)(2,1)}, bf16[2,48,768]{2,1,0:T(8,128)(2,1)S(1)}, u32[]{:S(2)}, u32[]{:S(2)}) collective-permute-start(bf16[2,48,768]{2,1,0:T(8,128)(2,1)} %get-tuple-element.66), channel_id=1, source_target_pairs={{0,96},{32,64},{64,32},{96,0},{1,97},{33,65},{65,33},{97,1},{2,98}... | collective-permute-start | bytes 442376 | tf_op jit(solution)/shard_map/ppermute | solution.py:681
  77.7 19.8 %all-to-all-start.3 = ((bf16[32,112,128]{2,1,0:T(8,128)(2,1)}), bf16[32,112,128]{2,1,0:T(8,128)(2,1)S(1)}, u32[]{:S(2)}, u32[]{:S(2)}) async-start(bf16[32,112,128]{2,1,0:T(8,128)(2,1)} %bitcast.8), calls=%async_computation.3 | async-start | bytes 1835008 | tf_op jit(solution)/shard_map/all_to_all | solution.py:661
  81.7 15.8 %collective-permute-start.1 = (bf16[8,128,384]{2,1,0:T(8,128)(2,1)}, bf16[8,128,384]{2,1,0:T(8,128)(2,1)S(1)}, u32[]{:S(2)}, u32[]{:S(2)}) collective-permute-start(bf16[8,128,384]{2,1,0:T(8,128)(2,1)} %shard_map.193.kvs_ref), channel_id=1, source_target_pairs={{0,8},{8,0},{1,9},{9,1},{2,10},{10,2},{3,11},{11,3},{4,12},{12,4},... | collective-permute-start | bytes 2359304 | tf_op jit(solution)/shard_map/ppermute | solution.py:665
  82.6 12.7 %collective-permute-start.6 = (bf16[32,768]{1,0:T(8,128)(2,1)S(1)}, bf16[32,768]{1,0:T(8,128)(2,1)S(1)}, u32[]{:S(2)}, u32[]{:S(2)}) collective-permute-start(bf16[32,768]{1,0:T(8,128)(2,1)S(1)} %copy-done.2), channel_id=1, source_target_pairs={{0,1},{1,0},{2,3},{3,2},{4,5},{5,4},{6,7},{7,6},{8,9},{9,8},{10,11... | collective-permute-start | bytes 147464 | tf_op jit(solution)/shard_map/ppermute | solution.py:681
  85.5 9.8 %collective-permute-start.7 = (bf16[32,768]{1,0:T(8,128)(2,1)S(1)}, bf16[32,768]{1,0:T(8,128)(2,1)S(1)}, u32[]{:S(2)}, u32[]{:S(2)}) collective-permute-start(bf16[32,768]{1,0:T(8,128)(2,1)S(1)} %copy-done.2), channel_id=1, source_target_pairs={{0,2},{1,3},{2,0},{3,1},{4,6},{5,7},{6,4},{7,5},{8,10},{9,11},{10,... | collective-permute-start | bytes 147464 | tf_op jit(solution)/shard_map/ppermute | solution.py:681
  86.7 10.8 %collective-permute-start.8 = (bf16[32,768]{1,0:T(8,128)(2,1)S(1)}, bf16[32,768]{1,0:T(8,128)(2,1)S(1)}, u32[]{:S(2)}, u32[]{:S(2)}) collective-permute-start(bf16[32,768]{1,0:T(8,128)(2,1)S(1)} %copy-done.2), channel_id=1, source_target_pairs={{0,3},{1,2},{2,1},{3,0},{4,7},{5,6},{6,5},{7,4},{8,11},{9,10},{10,... | collective-permute-start | bytes 147464 | tf_op jit(solution)/shard_map/ppermute | solution.py:681
  97.5 4.1 %collective-permute-start.9 = (bf16[8,4,112,128]{3,2,1,0:T(8,128)(2,1)S(1)}, bf16[8,4,112,128]{3,2,1,0:T(8,128)(2,1)S(1)}, u32[]{:S(2)}, u32[]{:S(2)}) collective-permute-start(bf16[8,4,112,128]{3,2,1,0:T(8,128)(2,1)S(1)} %shard_map.198.gs_ref), channel_id=1, source_target_pairs={{0,8},{8,0},{1,9},{9,1},{2,10},{10,2},{3,11},{11,3},{4,12},{12,4},... | collective-permute-start | bytes 2752520 | tf_op jit(solution)/shard_map/ppermute | solution.py:665
  101.6 5.3 %collective-permute-start.10 = (bf16[2,48,768]{2,1,0:T(8,128)(2,1)}, bf16[2,48,768]{2,1,0:T(8,128)(2,1)S(1)}, u32[]{:S(2)}, u32[]{:S(2)}) collective-permute-start(bf16[2,48,768]{2,1,0:T(8,128)(2,1)} %shard_map.200.near_ref), channel_id=1, source_target_pairs={{0,16},{16,0},{1,17},{17,1},{2,18},{18,2},{3,19},{19,3},{4,20},{20... | collective-permute-start | bytes 442376 | tf_op jit(solution)/shard_map/ppermute | solution.py:681
  106.9 3.9 %collective-permute-start.14 = (bf16[16,48,384]{2,1,0:T(8,128)(2,1)S(1)}, bf16[16,48,384]{2,1,0:T(8,128)(2,1)S(1)}, u32[]{:S(2)}, u32[]{:S(2)}) collective-permute-start(bf16[16,48,384]{2,1,0:T(8,128)(2,1)S(1)} %shard_map.202), channel_id=1, source_target_pairs={{0,8},{8,0},{1,9},{9,1},{2,10},{10,2},{3,11},{11,3},{4,12},{12,4},... | collective-permute-start | bytes 1769480 | tf_op jit(solution)/shard_map/ppermute | solution.py:665
  111.7 16.9 %all-to-all-start.4 = ((bf16[16,48,384]{2,1,0:T(8,128)(2,1)}), bf16[16,48,384]{2,1,0:T(8,128)(2,1)S(1)}, u32[]{:S(2)}, u32[]{:S(2)}) async-start(bf16[16,48,384]{2,1,0:T(8,128)(2,1)} %shard_map.203), calls=%async_computation.4 | async-start | bytes 1179648 | tf_op jit(solution)/shard_map/all_to_all | solution.py:661
  116.9 10.5 %collective-permute-start.11 = (bf16[48,768]{1,0:T(8,128)(2,1)S(1)}, bf16[48,768]{1,0:T(8,128)(2,1)S(1)}, u32[]{:S(2)}, u32[]{:S(2)}) collective-permute-start(bf16[48,768]{1,0:T(8,128)(2,1)S(1)} %copy-done.7), channel_id=1, source_target_pairs={{0,1},{1,0},{2,3},{3,2},{4,5},{5,4},{6,7},{7,6},{8,9},{9,8},{10,11... | collective-permute-start | bytes 221192 | tf_op jit(solution)/shard_map/ppermute | solution.py:681
  118.7 8.8 %collective-permute-start.12 = (bf16[48,768]{1,0:T(8,128)(2,1)S(1)}, bf16[48,768]{1,0:T(8,128)(2,1)S(1)}, u32[]{:S(2)}, u32[]{:S(2)}) collective-permute-start(bf16[48,768]{1,0:T(8,128)(2,1)S(1)} %copy-done.6), channel_id=1, source_target_pairs={{0,2},{1,3},{2,0},{3,1},{4,6},{5,7},{6,4},{7,5},{8,10},{9,11},{10,... | collective-permute-start | bytes 221192 | tf_op jit(solution)/shard_map/ppermute | solution.py:681
  118.7 10.0 %collective-permute-start.13 = (bf16[48,768]{1,0:T(8,128)(2,1)S(1)}, bf16[48,768]{1,0:T(8,128)(2,1)S(1)}, u32[]{:S(2)}, u32[]{:S(2)}) collective-permute-start(bf16[48,768]{1,0:T(8,128)(2,1)S(1)} %copy-done.5), channel_id=1, source_target_pairs={{0,3},{1,2},{2,1},{3,0},{4,7},{5,6},{6,5},{7,4},{8,11},{9,10},{10,... | collective-permute-start | bytes 221192 | tf_op jit(solution)/shard_map/ppermute | solution.py:681
  131.0 40.6 %all-to-all-start.5 = ((bf16[64,8,2432]{2,1,0:T(8,128)(2,1)}), bf16[64,8,2432]{2,1,0:T(8,128)(2,1)S(1)}, u32[]{:S(2)}, u32[]{:S(2)}) async-start(bf16[64,8,2432]{2,1,0:T(8,128)(2,1)} %bitcast.7), calls=%async_computation.5 | async-start | bytes 4980736 | tf_op jit(solution)/shard_map/all_to_all | solution.py:661
  171.6 13.9 %collective-permute-start.15 = (bf16[8,8,8,2432]{3,2,1,0:T(8,128)(2,1)S(1)}, bf16[8,8,8,2432]{3,2,1,0:T(8,128)(2,1)}, u32[]{:S(2)}, u32[]{:S(2)}) collective-permute-start(bf16[8,8,8,2432]{3,2,1,0:T(8,128)(2,1)S(1)} %shard_map.207.in_ref), channel_id=1, source_target_pairs={{0,8},{8,0},{1,9},{9,1},{2,10},{10,2},{3,11},{11,3},{4,12},{12,4},... | collective-permute-start | bytes 7471112 | tf_op jit(solution)/shard_map/ppermute | solution.py:665
  177.4 18.2 %all-to-all-start.6 = ((bf16[8,64,768]{2,1,0:T(8,128)(2,1)}), bf16[8,64,768]{2,1,0:T(8,128)(2,1)S(1)}, u32[]{:S(2)}, u32[]{:S(2)}) async-start(bf16[8,64,768]{2,1,0:T(8,128)(2,1)} %shard_map.209), calls=%async_computation.6 | async-start | bytes 1572864 | tf_op jit(solution)/shard_map/all_to_all | solution.py:661
  181.0 9.6 %collective-permute-start.21 = (bf16[2,48,768]{2,1,0:T(8,128)(2,1)S(1)}, bf16[2,48,768]{2,1,0:T(8,128)(2,1)S(1)}, u32[]{:S(2)}, u32[]{:S(2)}) collective-permute-start(bf16[2,48,768]{2,1,0:T(8,128)(2,1)S(1)} %copy-done.4), channel_id=1, source_target_pairs={{0,96},{32,64},{64,32},{96,0},{1,97},{33,65},{65,33},{97,1},{2,98}... | collective-permute-start | bytes 442376 | tf_op jit(solution)/shard_map/ppermute | solution.py:681
  182.1 9.6 %collective-permute-start.19 = (bf16[2,48,768]{2,1,0:T(8,128)(2,1)S(1)}, bf16[2,48,768]{2,1,0:T(8,128)(2,1)S(1)}, u32[]{:S(2)}, u32[]{:S(2)}) collective-permute-start(bf16[2,48,768]{2,1,0:T(8,128)(2,1)S(1)} %copy-done.4), channel_id=1, source_target_pairs={{0,64},{32,96},{64,0},{96,32},{1,65},{33,97},{65,1},{97,33},{2,66}... | collective-permute-start | bytes 442376 | tf_op jit(solution)/shard_map/ppermute | solution.py:681
  183.2 8.6 %collective-permute-start.17 = (bf16[2,48,768]{2,1,0:T(8,128)(2,1)S(1)}, bf16[2,48,768]{2,1,0:T(8,128)(2,1)S(1)}, u32[]{:S(2)}, u32[]{:S(2)}) collective-permute-start(bf16[2,48,768]{2,1,0:T(8,128)(2,1)S(1)} %copy-done.4), channel_id=1, source_target_pairs={{0,32},{32,0},{64,96},{96,64},{1,33},{33,1},{65,97},{97,65},{2,34}... | collective-permute-start | bytes 442376 | tf_op jit(solution)/shard_map/ppermute | solution.py:681
  184.3 10.1 %collective-permute-start.16 = (bf16[2,48,768]{2,1,0:T(8,128)(2,1)S(1)}, bf16[2,48,768]{2,1,0:T(8,128)(2,1)S(1)}, u32[]{:S(2)}, u32[]{:S(2)}) collective-permute-start(bf16[2,48,768]{2,1,0:T(8,128)(2,1)S(1)} %copy-done.4), channel_id=1, source_target_pairs={{0,8},{8,0},{1,9},{9,1},{2,10},{10,2},{3,11},{11,3},{4,12},{12,4},... | collective-permute-start | bytes 442376 | tf_op jit(solution)/shard_map/ppermute | solution.py:665
  190.6 3.8 %collective-permute-start.22 = (bf16[2,48,768]{2,1,0:T(8,128)(2,1)S(1)}, bf16[2,48,768]{2,1,0:T(8,128)(2,1)S(1)}, u32[]{:S(2)}, u32[]{:S(2)}) collective-permute-start(bf16[2,48,768]{2,1,0:T(8,128)(2,1)S(1)} %shard_map.213.refs_3_), channel_id=1, source_target_pairs={{0,8},{8,0},{1,9},{9,1},{2,10},{10,2},{3,11},{11,3},{4,12},{12,4},... | collective-permute-start | bytes 442376 | tf_op jit(solution)/shard_map/ppermute | solution.py:665
  191.7 2.7 %collective-permute-start.20 = (bf16[2,48,768]{2,1,0:T(8,128)(2,1)S(1)}, bf16[2,48,768]{2,1,0:T(8,128)(2,1)S(1)}, u32[]{:S(2)}, u32[]{:S(2)}) collective-permute-start(bf16[2,48,768]{2,1,0:T(8,128)(2,1)S(1)} %shard_map.212.refs_2_), channel_id=1, source_target_pairs={{0,8},{8,0},{1,9},{9,1},{2,10},{10,2},{3,11},{11,3},{4,12},{12,4},... | collective-permute-start | bytes 442376 | tf_op jit(solution)/shard_map/ppermute | solution.py:665
  191.8 2.6 %collective-permute-start.18 = (bf16[2,48,768]{2,1,0:T(8,128)(2,1)S(1)}, bf16[2,48,768]{2,1,0:T(8,128)(2,1)S(1)}, u32[]{:S(2)}, u32[]{:S(2)}) collective-permute-start(bf16[2,48,768]{2,1,0:T(8,128)(2,1)S(1)} %shard_map.211.refs_1_), channel_id=1, source_target_pairs={{0,8},{8,0},{1,9},{9,1},{2,10},{10,2},{3,11},{11,3},{4,12},{12,4},... | collective-permute-start | bytes 442376 | tf_op jit(solution)/shard_map/ppermute | solution.py:665
  (6 other events, 42.4 us)

commit v23 on v18

--- a/solution.py
+++ b/solution.py
@@ -359,8 +359,13 @@
             inside = (lane >= (head + 1) * HD) & (lane < (head + 2) * HD)
             columns += three(jnp.sum(jnp.where(inside, product, 0.0), axis=-1, keepdims=True))
         stats = put_columns(256, BLK, 9, columns)
-        buf[head_group, :, :256] = jnp.where(lane < 9, mixed, jnp.where(lane < HD, stats, back)).astype(BF)
-        buf[head_group, :, 256:] = query_buf[head_group]
+        packed = jnp.where(lane < 9, mixed, jnp.where(lane < HD, stats, back)).astype(BF)
+        query = query_buf[head_group]
+        last = query[:, 128:192]
+        buf[head_group, :32] = packed[:, :128]
+        buf[head_group, 32:64] = packed[:, 128:]
+        buf[head_group, 64:96] = query[:, :128]
+        buf[head_group, 96:] = jnp.concatenate([last[:16], last[16:]], axis=1)
     sends = send_copies(buf, out_ref, range(8), sem)
     wait_all(stores)
     wait_all(sends)
@@ -394,11 +399,19 @@
         def cut(value):
             return [value[:, at:at + 128] for at in range(0, value.shape[1], 128)]
 
-        every = cut(jnp.concatenate(
-            [ref[pl.ds(first, count)].reshape(rows, 512) for ref in (gs_ref, go_ref)], axis=0
-        ))
+        def unpacked(ref, start, tiles):
+            blocks = [ref[pl.ds(start, tiles), :, at:at + 32] for at in (0, 32, 64)]
+            last = ref[pl.ds(start, tiles), :, 96:]
+            turned = jnp.concatenate([last[..., HD:], last[..., :HD]], axis=-1)
+            blocks.append(jnp.concatenate([last, turned], axis=2))
+            return [block.reshape(tiles * TOK, 128) for block in blocks]
+
+        every = [
+            jnp.concatenate(pair, axis=0)
+            for pair in zip(*[unpacked(ref, first, count) for ref in (gs_ref, go_ref)])
+        ]
         grad, query = every[:2], every[2:]
-        g_own = cut(gs_ref[chip])
+        g_own = unpacked(gs_ref, chip, 1)
         g_heads = [halves(g_own[0])[1], *halves(g_own[1])]
         own_stats = g_own[0].astype(F32)
         all_stats = grad[0].astype(F32).T
@@ -407,7 +420,7 @@
             [kv_buf[:count].reshape(rows, 384), kvo_ref[pl.ds(first, count)].reshape(rows, 384)], axis=0
         ))
         own = cut(kv_buf[chip - first]) + g_own[2:]
-        q_heads = [*halves(own[3]), own[4]]
+        q_heads = [*halves(own[3]), halves(own[4])[0]]
         k_heads = [*halves(own[0]), halves(own[1])[0]]
         v_heads = [halves(own[1])[1], *halves(own[2])]
 
@@ -745,7 +758,7 @@
     grad_send, low, grad_mid, result_part, vec2 = call(
         middle_kernel,
         [
-            ((8, 4, BLK, 512), BF, "H"), ((BLK, D), BF, "H"), ((BLK, D), F32, "H"), ((BLK, D), BF, "H"),
+            ((8, 4, 112, 128), BF, "H"), ((BLK, D), BF, "H"), ((BLK, D), F32, "H"), ((BLK, D), BF, "H"),
             ((8, D), F32, "H"),
         ],
         [
@@ -754,13 +767,13 @@
         ],
         1000,
         [
-            pltpu.VMEM((4, BLK, 512), BF), pltpu.VMEM((BLK, D), F32), pltpu.VMEM((BLK, D), BF),
+            pltpu.VMEM((4, 112, 128), BF), pltpu.VMEM((BLK, D), F32), pltpu.VMEM((BLK, D), BF),
             pltpu.VMEM((4, BLK, 256), BF), pltpu.VMEM((D,), F32), pltpu.VMEM((4, BLK, 256), BF), pltpu.VMEM((BLK, D), BF), pltpu.VMEM((BLK, D), F32),
             pltpu.VMEM((BLK, D), BF), pltpu.VMEM((8, D), F32), DMA((5,)), DMA((8,)), DMA((4,)),
         ],
     )
     grad_send = after(pin(grad_send), *pieces[1:])
-    grad_same = exchange(grad_send.reshape(32, BLK, 512), (*CHIP, *GROUP)).reshape(8, TOK, 512)
+    grad_same = exchange(grad_send.reshape(32, 112, 128), (*CHIP, *GROUP)).reshape(8, 4, 112, 128)
     lows = [flip(low, GROUP, 4, k) for k in (1, 2, 3)]
     kv_same = after(pin(kv_same), low)
     kv_other = swap(kv_same)

time: 199 us -> 197 us (0.990)
  no operation moved by 1% of the time
where the time goes in v23:
time: 197 us; the launch traced here: 196 us
  waiting for transfers between devices  74.6 us (38%)
  starting transfers between devices  70.3 us (36%)
  Pallas kernels  48.8 us (25%)
    all_to_all x7, waiting for transfers between devices, exchange(): return lax.all_to_all(value, axes, 0, 0, tiled=True)  52.6 us
    pallas_call x18, Pallas kernels, call(): pl.pallas_call(kernel, out_shape=[(pltpu.HBM if place in 'HL' else jax.Sh...  48.8 us
    all_to_all x7, starting transfers between devices, exchange(): return lax.all_to_all(value, axes, 0, 0, tiled=True)  40.1 us
    ppermute x13, waiting for transfers between devices, flip(): lax.ppermute(value, axes, [(index, index ^ bits) for index in range(count)])  17 us
    ppermute x13, starting transfers between devices, flip(): lax.ppermute(value, axes, [(index, index ^ bits) for index in range(count)])  16.6 us
    ppermute x10, starting transfers between devices, swap(): return lax.ppermute(value, CORE, [(0, 1), (1, 0)])  13.7 us
    ppermute x10, waiting for transfers between devices, swap(): return lax.ppermute(value, CORE, [(0, 1), (1, 0)])  5.03 us
  transfers between devices with their start and end apart: 30, of which 14 were waited for; matrix products, arithmetic and copies ran while one was open for 1% of the time, Pallas kernels for 16%

profile of v23, /device:TPU:1, one launch (start us, length us, event | category | flops | bytes accessed | tf_op | source)
XLA Modules:
  0.0 196.2 jit_solution(11441623994755256667)
XLA Ops:
  0.6 3.7 %shard_map.186 = (bf16[8,128,384]{2,1,0:T(8,128)(2,1)}, bf16[128,768]{1,0:T(8,128)(2,1)}) custom-call(bf16[2,128,768]{2,1,0:T(8,128)(2,1)} %tok_ref.7, f32[768]{0:T(1024)} %gain_ref.7, f32[768]{0:T(1024)} %shift_ref.2, bf16[768,2304]{1,0:T(8,128)(2,1)} %w_ref.7), custom_call_target="tpu_custom_call" | custom-call | flops 1000 | bytes 1000 | tf_op jit(solution)/shard_map/pallas_call | solution.py:106
  4.3 6.0 %all-to-all-start = ((bf16[8,128,384]{2,1,0:T(8,128)(2,1)}), bf16[8,128,384]{2,1,0:T(8,128)(2,1)S(1)}, u32[]{:S(2)}, u32[]{:S(2)}) async-start(bf16[8,128,384]{2,1,0:T(8,128)(2,1)} %get-tuple-element.51), calls=%async_computation | async-start | bytes 1572864 | tf_op jit(solution)/shard_map/all_to_all | solution.py:661
  10.3 3.0 %shard_map.187.refs_1_.q_ref = bf16[128,256]{1,0:T(8,128)(2,1)} custom-call(bf16[128,768]{1,0:T(8,128)(2,1)} %get-tuple-element.52.normed_ref, bf16[768,2304]{1,0:T(8,128)(2,1)} %w_ref.7), custom_call_target="tpu_custom_call" | custom-call | flops 1000 | bytes 1000 | tf_op jit(solution)/shard_map/pallas_call | solution.py:106
  13.4 8.6 %all-to-all-done.refs_0_ = bf16[8,128,384]{2,1,0:T(8,128)(2,1)S(1)} async-done(((bf16[8,128,384]{2,1,0:T(8,128)(2,1)}), bf16[8,128,384]{2,1,0:T(8,128)(2,1)S(1)}, u32[]{:S(2)}, u32[]{:S(2)}) %all-to-all-start) | async-done | bytes 786464 | tf_op jit(solution)/shard_map/all_to_all | solution.py:661
  22.0 2.2 %collective-permute-start = (bf16[8,128,384]{2,1,0:T(8,128)(2,1)S(1)}, bf16[8,128,384]{2,1,0:T(8,128)(2,1)S(1)}, u32[]{:S(2)}, u32[]{:S(2)}) collective-permute-start(bf16[8,128,384]{2,1,0:T(8,128)(2,1)S(1)} %shard_map.188.same_ref.refs_0_), channel_id=1, source_target_pairs={{0,8},{8,0},{1,9},{9,1},{2,10},{10,2},{3,11},{11,3},{4,12},{12,4},... | collective-permute-start | bytes 2359304 | tf_op jit(solution)/shard_map/ppermute | solution.py:665
  26.1 3.1 %shard_map.189 = bf16[8,128,256]{2,1,0:T(8,128)(2,1)} custom-call(s32[2,32]{1,0:T(2,128)S(1)} %copy-done.3, bf16[128,256]{1,0:T(8,128)(2,1)} %shard_map.187.refs_1_.q_ref, bf16[8,128,384]{2,1,0:T(8,128)(2,1)S(1)} %shard_map.188.same_ref.refs_0_, bf16[8,128,384]{2,1,0:T(8,128)(2,1)S(1)} %collective-permute-done.other_ref), custom_call_target="tpu_custom_call" | custom-call | flops 1000 | bytes 1000 | tf_op jit(solution)/shard_map/pallas_call | solution.py:106
  29.2 7.2 %all-to-all-start.1 = ((bf16[8,128,256]{2,1,0:T(8,128)(2,1)}), bf16[8,128,256]{2,1,0:T(8,128)(2,1)S(1)}, u32[]{:S(2)}, u32[]{:S(2)}) async-start(bf16[8,128,256]{2,1,0:T(8,128)(2,1)} %shard_map.189), calls=%async_computation.1 | async-start | bytes 1048576 | tf_op jit(solution)/shard_map/all_to_all | solution.py:661
  37.8 9.4 %all-to-all-done.1.mixed_ref = bf16[8,128,256]{2,1,0:T(8,128)(2,1)S(1)} async-done(((bf16[8,128,256]{2,1,0:T(8,128)(2,1)}), bf16[8,128,256]{2,1,0:T(8,128)(2,1)S(1)}, u32[]{:S(2)}, u32[]{:S(2)}) %all-to-all-start.1) | async-done | bytes 524320 | tf_op jit(solution)/shard_map/all_to_all | solution.py:661
  47.1 4.2 %shard_map.190 = (bf16[8,64,768]{2,1,0:T(8,128)(2,1)}, f32[32,768]{1,0:T(8,128)}, bf16[256,768]{1,0:T(8,128)(2,1)S(1)}, bf16[256,384]{1,0:T(8,128)(2,1)S(1)}, bf16[256,384]{1,0:T(8,128)(2,1)S(1)}) custom-call(bf16[8,128,256]{2,1,0:T(8,128)(2,1)S(1)} %all-to-all-done.1.mixed_ref, bf16[2,128,768]{2,1,0:T(8,128)(2,1)} %tok_ref.7, bf16[2,128,768]{2,1,0:T(8,128)(2,1)} %og_ref.5, ...), custom_call_target="tpu_custom_call" | custom-call | flops 1000 | bytes 1000 | tf_op jit(solution)/shard_map/pallas_call | solution.py:106
  51.3 2.8 %shard_map.194 = (bf16[8,48,768]{2,1,0:T(8,128)(2,1)S(1)}, bf16[8,48,768]{2,1,0:T(8,128)(2,1)}) custom-call(bf16[256,768]{1,0:T(8,128)(2,1)S(1)} %get-tuple-element.57.normed_ref, bf16[256,384]{1,0:T(8,128)(2,1)S(1)} %get-tuple-element.58.act_ref, bf16[256,384]{1,0:T(8,128)(2,1)S(1)} %get-tuple-element.59.gpre_ref, bf16[2,128,768]{2,1,0:T(8,128)(2,1)} %og_ref.5), custom_call_target="tpu_custom_call" | custom-call | flops 1000 | bytes 1000 | tf_op jit(solution)/shard_map/pallas_call | solution.py:106
  55.8 3.5 %all-to-all-start.2 = ((bf16[8,64,768]{2,1,0:T(8,128)(2,1)}), bf16[8,64,768]{2,1,0:T(8,128)(2,1)S(1)}, u32[]{:S(2)}, u32[]{:S(2)}) async-start(bf16[8,64,768]{2,1,0:T(8,128)(2,1)} %get-tuple-element.53), calls=%async_computation.2 | async-start | bytes 1572864 | tf_op jit(solution)/shard_map/all_to_all | solution.py:661
  65.2 2.3 %shard_map.191.query_ref = bf16[4,32,256]{2,1,0:T(8,128)(2,1)} custom-call(bf16[128,768]{1,0:T(8,128)(2,1)} %get-tuple-element.52.normed_ref, bf16[768,2304]{1,0:T(8,128)(2,1)} %w_ref.7), custom_call_target="tpu_custom_call" | custom-call | flops 1000 | bytes 1000 | tf_op jit(solution)/shard_map/pallas_call | solution.py:106
  67.5 6.4 %all-to-all-done.2.sums_ref = bf16[8,64,768]{2,1,0:T(8,128)(2,1)S(1)} async-done(((bf16[8,64,768]{2,1,0:T(8,128)(2,1)}), bf16[8,64,768]{2,1,0:T(8,128)(2,1)S(1)}, u32[]{:S(2)}, u32[]{:S(2)}) %all-to-all-start.2) | async-done | bytes 786464 | tf_op jit(solution)/shard_map/all_to_all | solution.py:661
  73.9 2.9 %shard_map.192 = (bf16[8,4,112,128]{3,2,1,0:T(8,128)(2,1)}, bf16[32,768]{1,0:T(8,128)(2,1)}, f32[32,768]{1,0:T(8,128)}, bf16[32,768]{1,0:T(8,128)(2,1)}, f32[8,768]{1,0:T(8,128)}) custom-call(bf16[8,64,768]{2,1,0:T(8,128)(2,1)S(1)} %all-to-all-done.2.sums_ref, f32[32,768]{1,0:T(8,128)} %get-tuple-element.54.middle_ref, bf16[2,128,768]{2,1,0:T(8,128)(2,1)} %og_ref.5, ...), custom_call_target="tpu_custom_call" | custom-call | flops 1000 | bytes 1000 | tf_op jit(solution)/shard_map/pallas_call | solution.py:106
  76.9 3.9 %all-to-all-start.3 = ((bf16[32,112,128]{2,1,0:T(8,128)(2,1)}), bf16[32,112,128]{2,1,0:T(8,128)(2,1)S(1)}, u32[]{:S(2)}, u32[]{:S(2)}) async-start(bf16[32,112,128]{2,1,0:T(8,128)(2,1)} %bitcast.8), calls=%async_computation.3 | async-start | bytes 1835008 | tf_op jit(solution)/shard_map/all_to_all | solution.py:661
  81.7 3.0 %collective-permute-start.6 = (bf16[32,768]{1,0:T(8,128)(2,1)S(1)}, bf16[32,768]{1,0:T(8,128)(2,1)S(1)}, u32[]{:S(2)}, u32[]{:S(2)}) collective-permute-start(bf16[32,768]{1,0:T(8,128)(2,1)S(1)} %copy-done.2), channel_id=1, source_target_pairs={{0,1},{1,0},{2,3},{3,2},{4,5},{5,4},{6,7},{7,6},{8,9},{9,8},{10,11... | collective-permute-start | bytes 147464 | tf_op jit(solution)/shard_map/ppermute | solution.py:681
  87.6 6.7 %collective-permute-done.6.refs_1_.low1_ref = bf16[32,768]{1,0:T(8,128)(2,1)S(1)} collective-permute-done((bf16[32,768]{1,0:T(8,128)(2,1)S(1)}, bf16[32,768]{1,0:T(8,128)(2,1)S(1)}, u32[]{:S(2)}, u32[]{:S(2)}) %collective-permute-start.6) | collective-permute-done | bytes 49184 | tf_op jit(solution)/shard_map/ppermute | solution.py:681
  94.2 2.4 %collective-permute-done.8.refs_3_.low3_ref = bf16[32,768]{1,0:T(8,128)(2,1)S(1)} collective-permute-done((bf16[32,768]{1,0:T(8,128)(2,1)S(1)}, bf16[32,768]{1,0:T(8,128)(2,1)S(1)}, u32[]{:S(2)}, u32[]{:S(2)}) %collective-permute-start.8) | collective-permute-done | bytes 49184 | tf_op jit(solution)/shard_map/ppermute | solution.py:681
  101.0 4.3 %shard_map.199 = (bf16[128,640]{1,0:T(8,128)(2,1)S(1)}, bf16[3,768,384]{2,1,0:T(8,128)(2,1)S(1)}, bf16[16,48,384]{2,1,0:T(8,128)(2,1)S(1)}, bf16[16,48,384]{2,1,0:T(8,128)(2,1)S(1)}) custom-call(s32[2,32]{1,0:T(2,128)S(1)} %copy-done.3, bf16[8,128,384]{2,1,0:T(8,128)(2,1)} %shard_map.193.kvs_ref, ...), custom_call_target="tpu_custom_call" | custom-call | flops 1000 | bytes 1000 | tf_op jit(solution)/shard_map/pallas_call | solution.py:106
  107.2 2.6 %shard_map.201 = (f32[32,768]{1,0:T(8,128)}, bf16[48,768]{1,0:T(8,128)(2,1)}, bf16[48,768]{1,0:T(8,128)(2,1)}, bf16[48,768]{1,0:T(8,128)(2,1)}, f32[8,768]{1,0:T(8,128)}, /*index=5*/bf16[2,48,768]{2,1,0:T(8,128)(2,1)}) custom-call(bf16[128,640]{1,0:T(8,128)(2,1)S(1)} %get-tuple-element.66.gqkv_ref, bf16[3,768,384]{2,1,0:T(8,128)(2,1)S(1)} %get-tuple-element.67.w_ref, ...), custom_call_target="tpu_custom_call" | custom-call | flops 1000 | bytes 1000 | tf_op jit(solution)/shard_map/pallas_call | solution.py:106
  110.9 6.3 %all-to-all-start.4 = ((bf16[16,48,384]{2,1,0:T(8,128)(2,1)}), bf16[16,48,384]{2,1,0:T(8,128)(2,1)S(1)}, u32[]{:S(2)}, u32[]{:S(2)}) async-start(bf16[16,48,384]{2,1,0:T(8,128)(2,1)} %shard_map.203), calls=%async_computation.4 | async-start | bytes 1179648 | tf_op jit(solution)/shard_map/all_to_all | solution.py:661
  118.1 3.4 %collective-permute-start.13 = (bf16[48,768]{1,0:T(8,128)(2,1)S(1)}, bf16[48,768]{1,0:T(8,128)(2,1)S(1)}, u32[]{:S(2)}, u32[]{:S(2)}) collective-permute-start(bf16[48,768]{1,0:T(8,128)(2,1)S(1)} %copy-done.5), channel_id=1, source_target_pairs={{0,3},{1,2},{2,1},{3,0},{4,7},{5,6},{6,5},{7,4},{8,11},{9,10},{10,... | collective-permute-start | bytes 221192 | tf_op jit(solution)/shard_map/ppermute | solution.py:681
  121.4 5.4 %collective-permute-done.11.refs_2_.one_ref = bf16[48,768]{1,0:T(8,128)(2,1)S(1)} collective-permute-done((bf16[48,768]{1,0:T(8,128)(2,1)S(1)}, bf16[48,768]{1,0:T(8,128)(2,1)S(1)}, u32[]{:S(2)}, u32[]{:S(2)}) %collective-permute-start.11) | collective-permute-done | bytes 73760 | tf_op jit(solution)/shard_map/ppermute | solution.py:681
  128.7 2.3 %shard_map.205.unused_ref = bf16[8,8,8,2432]{3,2,1,0:T(8,128)(2,1)} custom-call(bf16[16,48,384]{2,1,0:T(8,128)(2,1)S(1)} %shard_map.204.in_ref, f32[8,768]{1,0:T(8,128)} %get-tuple-element.77.refs_1_.vec_ref, bf16[48,768]{1,0:T(8,128)(2,1)S(1)} %collective-permute-done.11.refs_2_.one_ref, bf16[48,768]{1,0:T(8,128)(2,1)S(1)} %collective-permute-done.12.refs_3_.two_ref, ...), custom_call_target="tpu_custom_call" | custom-call | flops 1000 | bytes 1000 | tf_op jit(solution)/shard_map/pallas_call | solution.py:106
  131.0 9.5 %all-to-all-start.5 = ((bf16[64,8,2432]{2,1,0:T(8,128)(2,1)}), bf16[64,8,2432]{2,1,0:T(8,128)(2,1)S(1)}, u32[]{:S(2)}, u32[]{:S(2)}) async-start(bf16[64,8,2432]{2,1,0:T(8,128)(2,1)} %bitcast.7), calls=%async_computation.5 | async-start | bytes 4980736 | tf_op jit(solution)/shard_map/all_to_all | solution.py:661
  140.6 3.0 %shard_map.206.refs_1_.refs_0_ = bf16[8,64,768]{2,1,0:T(8,128)(2,1)} custom-call(f32[32,768]{1,0:T(8,128)} %get-tuple-element.69.unused_ref.own_ref, bf16[48,768]{1,0:T(8,128)(2,1)S(1)} %collective-permute-done.11.refs_2_.one_ref, bf16[48,768]{1,0:T(8,128)(2,1)S(1)} %collective-permute-done.12.refs_3_.two_ref, ...), custom_call_target="tpu_custom_call" | custom-call | flops 1000 | bytes 1000 | tf_op jit(solution)/shard_map/pallas_call | solution.py:106
  143.6 28.2 %all-to-all-done.5 = bf16[64,8,2432]{2,1,0:T(8,128)(2,1)S(1)} async-done(((bf16[64,8,2432]{2,1,0:T(8,128)(2,1)}), bf16[64,8,2432]{2,1,0:T(8,128)(2,1)S(1)}, u32[]{:S(2)}, u32[]{:S(2)}) %all-to-all-start.5) | async-done | bytes 2490400 | tf_op jit(solution)/shard_map/all_to_all | solution.py:661
  171.8 3.4 %collective-permute-start.15 = (bf16[8,8,8,2432]{3,2,1,0:T(8,128)(2,1)S(1)}, bf16[8,8,8,2432]{3,2,1,0:T(8,128)(2,1)}, u32[]{:S(2)}, u32[]{:S(2)}) collective-permute-start(bf16[8,8,8,2432]{3,2,1,0:T(8,128)(2,1)S(1)} %shard_map.207.refs_1_.in_ref), channel_id=1, source_target_pairs={{0,8},{8,0},{1,9},{9,1},{2,10},{10,2},{3,11},{11,3},{4,12},{12,4},... | collective-permute-start | bytes 7471112 | tf_op jit(solution)/shard_map/ppermute | solution.py:665
  175.1 3.6 %all-to-all-start.6 = ((bf16[8,64,768]{2,1,0:T(8,128)(2,1)}), bf16[8,64,768]{2,1,0:T(8,128)(2,1)S(1)}, u32[]{:S(2)}, u32[]{:S(2)}) async-start(bf16[8,64,768]{2,1,0:T(8,128)(2,1)} %shard_map.208), calls=%async_computation.6 | async-start | bytes 1572864 | tf_op jit(solution)/shard_map/all_to_all | solution.py:661
  184.0 2.4 %shard_map.209 = (f32[768,2304]{1,0:T(8,128)}, f32[768,768]{1,0:T(8,128)}, f32[4,8,128]{2,1,0:T(8,128)S(1)}) custom-call(bf16[8,8,8,2432]{3,2,1,0:T(8,128)(2,1)S(1)} %shard_map.207.refs_1_.in_ref), custom_call_target="tpu_custom_call" | custom-call | flops 1000 | bytes 1000 | tf_op jit(solution)/shard_map/pallas_call | solution.py:106
  186.4 4.1 %shard_map.210 = (f32[768,2304]{1,0:T(8,128)}, f32[768,768]{1,0:T(8,128)}, f32[768]{0:T(1024)}, f32[768]{0:T(1024)}, f32[768]{0:T(1024)}, /*index=5*/f32[768]{0:T(1024)}) custom-call(bf16[8,8,8,2432]{3,2,1,0:T(8,128)(2,1)} %collective-permute-done.15.in_ref, ...), custom_call_target="tpu_custom_call", output_to_operand_aliasing={{0}: (2, {}), {1}: (3, {})} | custom-call | flops 1000 | bytes 1000 | tf_op jit(solution)/shard_map/pallas_call | solution.py:106
  192.6 2.5 %shard_map.214 = (f32[768,384]{1,0:T(8,128)}, f32[384,768]{1,0:T(8,128)}) custom-call(bf16[2,48,768]{2,1,0:T(8,128)(2,1)} %get-tuple-element.82.refs_0_, bf16[2,48,768]{2,1,0:T(8,128)(2,1)S(1)} %shard_map.211.refs_1_, bf16[2,48,768]{2,1,0:T(8,128)(2,1)S(1)} %shard_map.212.refs_2_, bf16[2,48,768]{2,1,0:T(8,128)(2,1)S(1)} %shard_map.213.refs_3_, ...), custom_call_target="tpu_custom_call" | custom-call | flops 1000 | bytes 1000 | tf_op jit(solution)/shard_map/pallas_call | solution.py:106
  (75 shorter events, 33.0 us)
Async XLA Ops:
  4.3 17.6 %all-to-all-start = ((bf16[8,128,384]{2,1,0:T(8,128)(2,1)}), bf16[8,128,384]{2,1,0:T(8,128)(2,1)S(1)}, u32[]{:S(2)}, u32[]{:S(2)}) async-start(bf16[8,128,384]{2,1,0:T(8,128)(2,1)} %get-tuple-element.51), calls=%async_computation | async-start | bytes 1572864 | tf_op jit(solution)/shard_map/all_to_all | solution.py:661
  10.3 15.8 %copy-start.3 = (s32[2,32]{1,0:T(2,128)S(1)}, s32[2,32]{1,0:T(2,128)}, u32[]{:S(2)}) copy-start(s32[2,32]{1,0:T(2,128)} %scene_ref.3) | copy-start | bytes 772
  22.0 15.8 %copy-start = (bf16[8,128,384]{2,1,0:T(8,128)(2,1)}, bf16[8,128,384]{2,1,0:T(8,128)(2,1)S(1)}, u32[]{:S(2)}) copy-start(bf16[8,128,384]{2,1,0:T(8,128)(2,1)S(1)} %shard_map.188.same_ref.refs_0_) | copy-start | bytes 2359300
  22.0 4.1 %collective-permute-start = (bf16[8,128,384]{2,1,0:T(8,128)(2,1)S(1)}, bf16[8,128,384]{2,1,0:T(8,128)(2,1)S(1)}, u32[]{:S(2)}, u32[]{:S(2)}) collective-permute-start(bf16[8,128,384]{2,1,0:T(8,128)(2,1)S(1)} %shard_map.188.same_ref.refs_0_), channel_id=1, source_target_pairs={{0,8},{8,0},{1,9},{9,1},{2,10},{10,2},{3,11},{11,3},{4,12},{12,4},... | collective-permute-start | bytes 2359304 | tf_op jit(solution)/shard_map/ppermute | solution.py:665
  29.2 18.0 %all-to-all-start.1 = ((bf16[8,128,256]{2,1,0:T(8,128)(2,1)}), bf16[8,128,256]{2,1,0:T(8,128)(2,1)S(1)}, u32[]{:S(2)}, u32[]{:S(2)}) async-start(bf16[8,128,256]{2,1,0:T(8,128)(2,1)} %shard_map.189), calls=%async_computation.1 | async-start | bytes 1048576 | tf_op jit(solution)/shard_map/all_to_all | solution.py:661
  54.1 5.3 %collective-permute-start.2 = (bf16[8,48,768]{2,1,0:T(8,128)(2,1)}, bf16[8,48,768]{2,1,0:T(8,128)(2,1)}, u32[]{:S(2)}, u32[]{:S(2)}) collective-permute-start(bf16[8,48,768]{2,1,0:T(8,128)(2,1)} %get-tuple-element.61), channel_id=1, source_target_pairs={{0,8},{8,0},{1,9},{9,1},{2,10},{10,2},{3,11},{11,3},{4,12},{12,4},... | collective-permute-start | bytes 1769480 | tf_op jit(solution)/shard_map/ppermute | solution.py:665
  55.8 18.1 %all-to-all-start.2 = ((bf16[8,64,768]{2,1,0:T(8,128)(2,1)}), bf16[8,64,768]{2,1,0:T(8,128)(2,1)S(1)}, u32[]{:S(2)}, u32[]{:S(2)}) async-start(bf16[8,64,768]{2,1,0:T(8,128)(2,1)} %get-tuple-element.53), calls=%async_computation.2 | async-start | bytes 1572864 | tf_op jit(solution)/shard_map/all_to_all | solution.py:661
  61.3 15.5 %collective-permute-start.3 = (bf16[2,48,768]{2,1,0:T(8,128)(2,1)}, bf16[2,48,768]{2,1,0:T(8,128)(2,1)S(1)}, u32[]{:S(2)}, u32[]{:S(2)}) collective-permute-start(bf16[2,48,768]{2,1,0:T(8,128)(2,1)} %get-tuple-element.62), channel_id=1, source_target_pairs={{0,32},{32,0},{64,96},{96,64},{1,33},{33,1},{65,97},{97,65},{2,34}... | collective-permute-start | bytes 442376 | tf_op jit(solution)/shard_map/ppermute | solution.py:681
  61.9 15.0 %collective-permute-start.4 = (bf16[2,48,768]{2,1,0:T(8,128)(2,1)}, bf16[2,48,768]{2,1,0:T(8,128)(2,1)S(1)}, u32[]{:S(2)}, u32[]{:S(2)}) collective-permute-start(bf16[2,48,768]{2,1,0:T(8,128)(2,1)} %get-tuple-element.63), channel_id=1, source_target_pairs={{0,64},{32,96},{64,0},{96,32},{1,65},{33,97},{65,1},{97,33},{2,66}... | collective-permute-start | bytes 442376 | tf_op jit(solution)/shard_map/ppermute | solution.py:681
  63.1 13.8 %collective-permute-start.5 = (bf16[2,48,768]{2,1,0:T(8,128)(2,1)}, bf16[2,48,768]{2,1,0:T(8,128)(2,1)S(1)}, u32[]{:S(2)}, u32[]{:S(2)}) collective-permute-start(bf16[2,48,768]{2,1,0:T(8,128)(2,1)} %get-tuple-element.64), channel_id=1, source_target_pairs={{0,96},{32,64},{64,32},{96,0},{1,97},{33,65},{65,33},{97,1},{2,98}... | collective-permute-start | bytes 442376 | tf_op jit(solution)/shard_map/ppermute | solution.py:681
  76.9 19.7 %all-to-all-start.3 = ((bf16[32,112,128]{2,1,0:T(8,128)(2,1)}), bf16[32,112,128]{2,1,0:T(8,128)(2,1)S(1)}, u32[]{:S(2)}, u32[]{:S(2)}) async-start(bf16[32,112,128]{2,1,0:T(8,128)(2,1)} %bitcast.8), calls=%async_computation.3 | async-start | bytes 1835008 | tf_op jit(solution)/shard_map/all_to_all | solution.py:661
  80.8 15.8 %collective-permute-start.1 = (bf16[8,128,384]{2,1,0:T(8,128)(2,1)}, bf16[8,128,384]{2,1,0:T(8,128)(2,1)S(1)}, u32[]{:S(2)}, u32[]{:S(2)}) collective-permute-start(bf16[8,128,384]{2,1,0:T(8,128)(2,1)} %shard_map.193.kvs_ref), channel_id=1, source_target_pairs={{0,8},{8,0},{1,9},{9,1},{2,10},{10,2},{3,11},{11,3},{4,12},{12,4},... | collective-permute-start | bytes 2359304 | tf_op jit(solution)/shard_map/ppermute | solution.py:665
  81.7 12.5 %collective-permute-start.6 = (bf16[32,768]{1,0:T(8,128)(2,1)S(1)}, bf16[32,768]{1,0:T(8,128)(2,1)S(1)}, u32[]{:S(2)}, u32[]{:S(2)}) collective-permute-start(bf16[32,768]{1,0:T(8,128)(2,1)S(1)} %copy-done.2), channel_id=1, source_target_pairs={{0,1},{1,0},{2,3},{3,2},{4,5},{5,4},{6,7},{7,6},{8,9},{9,8},{10,11... | collective-permute-start | bytes 147464 | tf_op jit(solution)/shard_map/ppermute | solution.py:681
  84.7 9.5 %collective-permute-start.7 = (bf16[32,768]{1,0:T(8,128)(2,1)S(1)}, bf16[32,768]{1,0:T(8,128)(2,1)S(1)}, u32[]{:S(2)}, u32[]{:S(2)}) collective-permute-start(bf16[32,768]{1,0:T(8,128)(2,1)S(1)} %copy-done.2), channel_id=1, source_target_pairs={{0,2},{1,3},{2,0},{3,1},{4,6},{5,7},{6,4},{7,5},{8,10},{9,11},{10,... | collective-permute-start | bytes 147464 | tf_op jit(solution)/shard_map/ppermute | solution.py:681
  85.9 10.7 %collective-permute-start.8 = (bf16[32,768]{1,0:T(8,128)(2,1)S(1)}, bf16[32,768]{1,0:T(8,128)(2,1)S(1)}, u32[]{:S(2)}, u32[]{:S(2)}) collective-permute-start(bf16[32,768]{1,0:T(8,128)(2,1)S(1)} %copy-done.2), channel_id=1, source_target_pairs={{0,3},{1,2},{2,1},{3,0},{4,7},{5,6},{6,5},{7,4},{8,11},{9,10},{10,... | collective-permute-start | bytes 147464 | tf_op jit(solution)/shard_map/ppermute | solution.py:681
  96.6 4.1 %collective-permute-start.9 = (bf16[8,4,112,128]{3,2,1,0:T(8,128)(2,1)S(1)}, bf16[8,4,112,128]{3,2,1,0:T(8,128)(2,1)S(1)}, u32[]{:S(2)}, u32[]{:S(2)}) collective-permute-start(bf16[8,4,112,128]{3,2,1,0:T(8,128)(2,1)S(1)} %shard_map.198.gs_ref), channel_id=1, source_target_pairs={{0,8},{8,0},{1,9},{9,1},{2,10},{10,2},{3,11},{11,3},{4,12},{12,4},... | collective-permute-start | bytes 2752520 | tf_op jit(solution)/shard_map/ppermute | solution.py:665
  100.7 5.3 %collective-permute-start.10 = (bf16[2,48,768]{2,1,0:T(8,128)(2,1)}, bf16[2,48,768]{2,1,0:T(8,128)(2,1)S(1)}, u32[]{:S(2)}, u32[]{:S(2)}) collective-permute-start(bf16[2,48,768]{2,1,0:T(8,128)(2,1)} %shard_map.200.near_ref), channel_id=1, source_target_pairs={{0,16},{16,0},{1,17},{17,1},{2,18},{18,2},{3,19},{19,3},{4,20},{20... | collective-permute-start | bytes 442376 | tf_op jit(solution)/shard_map/ppermute | solution.py:681
  106.0 3.9 %collective-permute-start.14 = (bf16[16,48,384]{2,1,0:T(8,128)(2,1)S(1)}, bf16[16,48,384]{2,1,0:T(8,128)(2,1)S(1)}, u32[]{:S(2)}, u32[]{:S(2)}) collective-permute-start(bf16[16,48,384]{2,1,0:T(8,128)(2,1)S(1)} %shard_map.202), channel_id=1, source_target_pairs={{0,8},{8,0},{1,9},{9,1},{2,10},{10,2},{3,11},{11,3},{4,12},{12,4},... | collective-permute-start | bytes 1769480 | tf_op jit(solution)/shard_map/ppermute | solution.py:665
  110.9 17.9 %all-to-all-start.4 = ((bf16[16,48,384]{2,1,0:T(8,128)(2,1)}), bf16[16,48,384]{2,1,0:T(8,128)(2,1)S(1)}, u32[]{:S(2)}, u32[]{:S(2)}) async-start(bf16[16,48,384]{2,1,0:T(8,128)(2,1)} %shard_map.203), calls=%async_computation.4 | async-start | bytes 1179648 | tf_op jit(solution)/shard_map/all_to_all | solution.py:661
  117.2 9.6 %collective-permute-start.11 = (bf16[48,768]{1,0:T(8,128)(2,1)S(1)}, bf16[48,768]{1,0:T(8,128)(2,1)S(1)}, u32[]{:S(2)}, u32[]{:S(2)}) collective-permute-start(bf16[48,768]{1,0:T(8,128)(2,1)S(1)} %copy-done.7), channel_id=1, source_target_pairs={{0,1},{1,0},{2,3},{3,2},{4,5},{5,4},{6,7},{7,6},{8,9},{9,8},{10,11... | collective-permute-start | bytes 221192 | tf_op jit(solution)/shard_map/ppermute | solution.py:681
  118.0 8.8 %collective-permute-start.12 = (bf16[48,768]{1,0:T(8,128)(2,1)S(1)}, bf16[48,768]{1,0:T(8,128)(2,1)S(1)}, u32[]{:S(2)}, u32[]{:S(2)}) collective-permute-start(bf16[48,768]{1,0:T(8,128)(2,1)S(1)} %copy-done.6), channel_id=1, source_target_pairs={{0,2},{1,3},{2,0},{3,1},{4,6},{5,7},{6,4},{7,5},{8,10},{9,11},{10,... | collective-permute-start | bytes 221192 | tf_op jit(solution)/shard_map/ppermute | solution.py:681
  118.1 10.7 %collective-permute-start.13 = (bf16[48,768]{1,0:T(8,128)(2,1)S(1)}, bf16[48,768]{1,0:T(8,128)(2,1)S(1)}, u32[]{:S(2)}, u32[]{:S(2)}) collective-permute-start(bf16[48,768]{1,0:T(8,128)(2,1)S(1)} %copy-done.5), channel_id=1, source_target_pairs={{0,3},{1,2},{2,1},{3,0},{4,7},{5,6},{6,5},{7,4},{8,11},{9,10},{10,... | collective-permute-start | bytes 221192 | tf_op jit(solution)/shard_map/ppermute | solution.py:681
  131.0 40.7 %all-to-all-start.5 = ((bf16[64,8,2432]{2,1,0:T(8,128)(2,1)}), bf16[64,8,2432]{2,1,0:T(8,128)(2,1)S(1)}, u32[]{:S(2)}, u32[]{:S(2)}) async-start(bf16[64,8,2432]{2,1,0:T(8,128)(2,1)} %bitcast.7), calls=%async_computation.5 | async-start | bytes 4980736 | tf_op jit(solution)/shard_map/all_to_all | solution.py:661
  171.8 14.6 %collective-permute-start.15 = (bf16[8,8,8,2432]{3,2,1,0:T(8,128)(2,1)S(1)}, bf16[8,8,8,2432]{3,2,1,0:T(8,128)(2,1)}, u32[]{:S(2)}, u32[]{:S(2)}) collective-permute-start(bf16[8,8,8,2432]{3,2,1,0:T(8,128)(2,1)S(1)} %shard_map.207.refs_1_.in_ref), channel_id=1, source_target_pairs={{0,8},{8,0},{1,9},{9,1},{2,10},{10,2},{3,11},{11,3},{4,12},{12,4},... | collective-permute-start | bytes 7471112 | tf_op jit(solution)/shard_map/ppermute | solution.py:665
  175.1 20.0 %all-to-all-start.6 = ((bf16[8,64,768]{2,1,0:T(8,128)(2,1)}), bf16[8,64,768]{2,1,0:T(8,128)(2,1)S(1)}, u32[]{:S(2)}, u32[]{:S(2)}) async-start(bf16[8,64,768]{2,1,0:T(8,128)(2,1)} %shard_map.208), calls=%async_computation.6 | async-start | bytes 1572864 | tf_op jit(solution)/shard_map/all_to_all | solution.py:661
  178.7 11.7 %collective-permute-start.16 = (bf16[2,48,768]{2,1,0:T(8,128)(2,1)S(1)}, bf16[2,48,768]{2,1,0:T(8,128)(2,1)S(1)}, u32[]{:S(2)}, u32[]{:S(2)}) collective-permute-start(bf16[2,48,768]{2,1,0:T(8,128)(2,1)S(1)} %copy-done.4), channel_id=1, source_target_pairs={{0,32},{32,0},{64,96},{96,64},{1,33},{33,1},{65,97},{97,65},{2,34}... | collective-permute-start | bytes 442376 | tf_op jit(solution)/shard_map/ppermute | solution.py:681
  179.2 11.4 %collective-permute-start.17 = (bf16[2,48,768]{2,1,0:T(8,128)(2,1)S(1)}, bf16[2,48,768]{2,1,0:T(8,128)(2,1)S(1)}, u32[]{:S(2)}, u32[]{:S(2)}) collective-permute-start(bf16[2,48,768]{2,1,0:T(8,128)(2,1)S(1)} %copy-done.4), channel_id=1, source_target_pairs={{0,64},{32,96},{64,0},{96,32},{1,65},{33,97},{65,1},{97,33},{2,66}... | collective-permute-start | bytes 442376 | tf_op jit(solution)/shard_map/ppermute | solution.py:681
  181.0 10.1 %collective-permute-start.18 = (bf16[2,48,768]{2,1,0:T(8,128)(2,1)S(1)}, bf16[2,48,768]{2,1,0:T(8,128)(2,1)S(1)}, u32[]{:S(2)}, u32[]{:S(2)}) collective-permute-start(bf16[2,48,768]{2,1,0:T(8,128)(2,1)S(1)} %copy-done.4), channel_id=1, source_target_pairs={{0,96},{32,64},{64,32},{96,0},{1,97},{33,65},{65,33},{97,1},{2,98}... | collective-permute-start | bytes 442376 | tf_op jit(solution)/shard_map/ppermute | solution.py:681
  182.7 8.9 %collective-permute-start.19 = (bf16[2,48,768]{2,1,0:T(8,128)(2,1)S(1)}, bf16[2,48,768]{2,1,0:T(8,128)(2,1)S(1)}, u32[]{:S(2)}, u32[]{:S(2)}) collective-permute-start(bf16[2,48,768]{2,1,0:T(8,128)(2,1)S(1)} %copy-done.4), channel_id=1, source_target_pairs={{0,8},{8,0},{1,9},{9,1},{2,10},{10,2},{3,11},{11,3},{4,12},{12,4},... | collective-permute-start | bytes 442376 | tf_op jit(solution)/shard_map/ppermute | solution.py:665
  190.5 1.5 collective-permute-start.20
  190.6 1.5 collective-permute-start.21
  191.1 1.5 collective-permute-start.22
  (6 other events, 41.6 us)
